TPU v7x, 32 devices: a whole 2x2x4 slice. The times are simulated.
32 devices in a mesh: section: 4 (over y, x), row: 4 (over z), col: 2 (over core).
Axes of the slice: x: 2, y: 2, z: 4, core: 2. Of those that a mesh axis runs over, the one named last changes fastest.
Arguments:
- inputs: bfloat16 [4, 3, 128, 2048], P('section', None, 'row', 'col'), may hold values from -6 to 6
- sample_ids: int32 [6], replicated, may hold values from 0 to 15
- send_base: bfloat16 [4, 16, 128, 2048], P('section', None, 'row', 'col'), may hold values from -1.796875 to 1.796875
- recv_base: bfloat16 [4, 16, 128, 2048], P('section', None, 'row', 'col'), may hold values from -1.796875 to 1.796875
- w_up: bfloat16 [4, 2048, 8192], P('section', 'col', 'row'), may hold values from -0.125 to 0.125
- w_down: bfloat16 [4, 8192, 2048], P('section', 'row', 'col'), may hold values from -0.0625 to 0.0625
- cotangent: bfloat16 [4, 3, 128, 2048], P('section', None, 'row', 'col'), may hold values from -6 to 6
Outputs:
- section_input: bfloat16 [4, 3, 128, 2048], P('section', None, 'row', 'col')
- section_output: bfloat16 [4, 3, 128, 2048], P('section', None, 'row', 'col')
- input_grad: bfloat16 [4, 3, 128, 2048], P('section', None, 'row', 'col')
- grad_up: bfloat16 [4, 2048, 8192], P('section', 'col', 'row')
- grad_down: bfloat16 [4, 8192, 2048], P('section', 'row', 'col')
All inputs are finite; a program needn't handle non-finite values.
Results may differ from a plain program's by a relative error of at most 0.04.
Values may be sent and summed in bfloat16 or wider, within the bound.
No kernel may reach another device: no remote copies, remote signals or barrier semaphores. Data moves between devices by JAX's collectives and lax.ppermute only.
A program may use at most 64 MiB of HBM per device.

v0:
```python
import jax
import jax.numpy as jnp
from jax import lax
from jax.sharding import PartitionSpec as P


def from_behind(block, axis, distance):
    devices = range(lax.axis_size(axis))
    route = [(i - distance, i) for i in devices if i - distance in devices]
    return lax.ppermute(block, axis, route)


def silu_slope(value):
    sig = jax.nn.sigmoid(value)
    return sig * (1.0 + value * (1.0 - sig))


def pick(table, index):
    return lax.dynamic_index_in_dim(table, index, 0, keepdims=False)


def per_device(inputs, sample_ids, send_base, recv_base, w_up, w_down, cotangent):
    section = lax.axis_index("section")
    sections = lax.axis_size("section")
    ticks = inputs.shape[1]
    piece_rows = inputs.shape[2]
    up_block = w_up[0]
    down_block = w_down[0]
    contract_last = (((1,), (1,)), ((), ()))
    contract_first = (((0,), (0,)), ((), ()))
    gathered_in = []
    hidden_pre = []
    hidden_act = []
    seen_in = []
    seen_out = []
    sending = None
    for tick in range(ticks):
        sample = pick(sample_ids, tick - section + sections - 1)
        if tick == 0:
            act_in = inputs[0, tick]
        else:
            arrived = from_behind(sending, "section", 1)
            rebuilt = (
                pick(recv_base[0], sample).astype(jnp.float32) + arrived.astype(jnp.float32)
            ).astype(jnp.bfloat16)
            act_in = jnp.where(section == 0, inputs[0, tick], rebuilt)
        full_in = lax.all_gather(act_in, "row", axis=0, tiled=True)
        partial_value = jnp.dot(full_in, up_block, preferred_element_type=jnp.float32)
        pre_keep = lax.psum(partial_value.astype(jnp.bfloat16), "col").astype(jnp.float32)
        act_full = jax.nn.silu(pre_keep).astype(jnp.bfloat16)

        def down_term(start, count, act_full=act_full):
            return jnp.dot(act_full, down_block, preferred_element_type=jnp.float32)

        mixed = lax.psum_scatter(
            down_term(jnp.int32(0), piece_rows * lax.axis_size("row")).astype(jnp.bfloat16),
            "row",
            scatter_dimension=0,
            tiled=True,
        ).astype(jnp.float32)
        act_out = (act_in.astype(jnp.float32) + mixed).astype(jnp.bfloat16)
        stored = pick(send_base[0], sample)
        sending = (act_out.astype(jnp.float32) - stored.astype(jnp.float32)).astype(jnp.bfloat16)
        gathered_in.append(full_in)
        hidden_pre.append(pre_keep)
        hidden_act.append(act_full)
        seen_in.append(act_in)
        seen_out.append(act_out)
    grads_full = [None] * ticks
    pre_grads = [None] * ticks
    seen_grad = [None] * ticks
    sending = None
    for turn in range(ticks):
        tick = ticks - 1 - turn
        if turn == 0:
            grad_out = cotangent[0, tick]
        else:
            arrived = from_behind(sending, "section", -1)
            grad_out = jnp.where(section == sections - 1, cotangent[0, tick], arrived)
        full_grad = lax.all_gather(grad_out, "row", axis=0, tiled=True)
        partial_value = lax.dot_general(
            full_grad, down_block, contract_last, preferred_element_type=jnp.float32
        )
        pre_keep = hidden_pre[tick]
        grad_act = lax.psum(partial_value.astype(jnp.bfloat16), "col").astype(jnp.float32)
        grad_pre = (grad_act * silu_slope(pre_keep)).astype(jnp.bfloat16)

        def feature_term(start, count, grad_pre=grad_pre):
            return lax.dot_general(
                grad_pre, up_block, contract_last, preferred_element_type=jnp.float32
            )

        returned = lax.psum_scatter(
            feature_term(jnp.int32(0), piece_rows * lax.axis_size("row")).astype(jnp.bfloat16),
            "row",
            scatter_dimension=0,
            tiled=True,
        ).astype(jnp.float32)
        grad_in = (grad_out.astype(jnp.float32) + returned).astype(jnp.bfloat16)
        sending = grad_in
        grads_full[tick] = full_grad
        pre_grads[tick] = grad_pre
        seen_grad[tick] = grad_in
    flat_in = jnp.concatenate(gathered_in, axis=0)
    flat_act = jnp.concatenate(hidden_act, axis=0)
    flat_grad = jnp.concatenate(grads_full, axis=0)
    flat_pre = jnp.concatenate(pre_grads, axis=0)
    grad_up = lax.dot_general(flat_in, flat_pre, contract_first, preferred_element_type=jnp.float32)
    grad_down = lax.dot_general(
        flat_act, flat_grad, contract_first, preferred_element_type=jnp.float32
    )
    return (
        jnp.stack(seen_in)[None],
        jnp.stack(seen_out)[None],
        jnp.stack(seen_grad)[None],
        grad_up.astype(jnp.bfloat16)[None],
        grad_down.astype(jnp.bfloat16)[None],
    )


def solution(mesh):
    placed = (
        P("section", None, "row", "col"),
        P(),
        P("section", None, "row", "col"),
        P("section", None, "row", "col"),
        P("section", "col", "row"),
        P("section", "row", "col"),
        P("section", None, "row", "col"),
    )
    return jax.shard_map(
        per_device,
        mesh=mesh,
        in_specs=placed,
        out_specs=(
            P("section", None, "row", "col"),
            P("section", None, "row", "col"),
            P("section", None, "row", "col"),
            P("section", "col", "row"),
            P("section", "row", "col"),
        ),
        check_vma=False,
    )
```

profile of v0, /device:TPU:3, one launch (start us, length us, event | category | flops | bytes accessed | tf_op | source)
XLA Modules:
  0.0 366.2 jit_solution(12115476629288019705)
XLA Ops:
  7.2 0.0 all-reduce.7.cloned.1.call-start
  7.2 0.9 slice_bitcast_fusion
  8.1 12.5 %all-gather = bf16[1,1,128,1024]{3,2,1,0:T(8,128)(2,1)S(1)} all-gather(bf16[1,1,32,1024]{3,2,1,0:T(8,128)(2,1)S(1)} %get-tuple-element.16), channel_id=2, replica_groups=mesh['section'=4,'row'=4,'col'=2] {'row'}, dimensions={2}, use_global_device_ids=true | all-gather | bytes 327680 | tf_op jit(solution)/shard_map/all_gather | solution.py:47
  20.6 3.7 %fusion.24 = bf16[128,2048]{1,0:T(8,128)(2,1)} fusion(bf16[1,1024,2048]{2,1,0:T(8,128)(2,1)} %param.11, bf16[1,1,128,1024]{3,2,1,0:T(8,128)(2,1)S(1)} %all-gather), kind=kOutput, calls=%fused_computation.26 | convolution fusion | flops 537133056 | bytes 4980736 | tf_op jit(solution)/shard_map/dot_general | solution.py:48
  24.3 0.0 reduce-scatter.7.cloned.1.call-start
  24.3 22.7 %all-reduce.7.cloned.1.call-done = bf16[128,2048]{1,0:T(8,128)(2,1)} async-done(((bf16[128,2048]{1,0:T(8,128)(2,1)}), bf16[128,2048]{1,0:T(8,128)(2,1)}) %all-reduce.7.cloned.1.call-update) | async-done | bytes 524304 | tf_op jit(solution)/shard_map/psum | solution.py:49
  47.1 3.8 %fusion.61 = bf16[128,1024]{1,0:T(8,128)(2,1)} fusion(bf16[1,2048,1024]{2,1,0:T(8,128)(2,1)} %param.12, bf16[128,2048]{1,0:T(8,128)(2,1)} %all-reduce.7.cloned.1.call-done), kind=kOutput, calls=%fused_computation.54 | convolution fusion | flops 538574848 | bytes 4980736 | tf_op jit(solution)/shard_map/dot_general | solution.py:53
  50.9 0.0 all-reduce.9.cloned.1.call-start
  51.0 0.6 fusion.123
  53.6 16.0 %reduce-scatter.7.cloned.1.call-done = bf16[32,1024]{1,0:T(8,128)(2,1)} async-done(((bf16[128,1024]{1,0:T(8,128)(2,1)}), bf16[32,1024]{1,0:T(8,128)(2,1)}) %reduce-scatter.7.cloned.1.call-update) | async-done | bytes 65552 | tf_op jit(solution)/shard_map/reduce_scatter | solution.py:55
  69.6 0.9 fusion.115
  70.5 3.1 collective-permute-start
  75.6 0.9 fusion.112
  76.5 12.2 %all_gather.19 = bf16[128,1024]{1,0:T(8,128)(2,1)S(1)} all-gather(bf16[32,1024]{1,0:T(8,128)(2,1)S(1)} %fusion.112), channel_id=1, replica_groups=mesh['section'=4,'row'=4,'col'=2] {'row'}, dimensions={0}, use_global_device_ids=true | all-gather | bytes 327680 | tf_op jit(solution)/shard_map/all_gather | solution.py:47
  88.7 3.7 %fusion.27 = bf16[128,2048]{1,0:T(8,128)(2,1)} fusion(bf16[128,1024]{1,0:T(8,128)(2,1)S(1)} %all_gather.19, bf16[1,1024,2048]{2,1,0:T(8,128)(2,1)} %param.11), kind=kOutput, calls=%fused_computation.27 | convolution fusion | flops 537133056 | bytes 4980736 | tf_op jit(solution)/shard_map/dot_general | solution.py:48
  92.4 0.0 reduce-scatter.9.cloned.1.call-start
  92.5 22.6 %all-reduce.9.cloned.1.call-done = bf16[128,2048]{1,0:T(8,128)(2,1)} async-done(((bf16[128,2048]{1,0:T(8,128)(2,1)}), bf16[128,2048]{1,0:T(8,128)(2,1)}) %all-reduce.9.cloned.1.call-update) | async-done | bytes 524304 | tf_op jit(solution)/shard_map/psum | solution.py:49
  115.1 3.8 %fusion.64 = bf16[128,1024]{1,0:T(8,128)(2,1)} fusion(bf16[1,2048,1024]{2,1,0:T(8,128)(2,1)} %param.12, bf16[128,2048]{1,0:T(8,128)(2,1)} %all-reduce.9.cloned.1.call-done), kind=kOutput, calls=%fused_computation.55 | convolution fusion | flops 538574848 | bytes 4980736 | tf_op jit(solution)/shard_map/dot_general | solution.py:53
  119.0 0.0 all-reduce.15.cloned.1.call-start
  119.0 13.2 %all-gather.1 = bf16[1,1,128,1024]{3,2,1,0:T(8,128)(2,1)S(1)} all-gather(bf16[1,1,32,1024]{3,2,1,0:T(8,128)(2,1)S(1)} %slice-done), channel_id=3, replica_groups=mesh['section'=4,'row'=4,'col'=2] {'row'}, dimensions={2}, use_global_device_ids=true | all-gather | bytes 327680 | tf_op jit(solution)/shard_map/all_gather | solution.py:80
  132.2 7.1 %reduce-scatter.9.cloned.1.call-done = bf16[32,1024]{1,0:T(8,128)(2,1)} async-done(((bf16[128,1024]{1,0:T(8,128)(2,1)}), bf16[32,1024]{1,0:T(8,128)(2,1)}) %reduce-scatter.9.cloned.1.call-update) | async-done | bytes 65552 | tf_op jit(solution)/shard_map/reduce_scatter | solution.py:55
  139.3 0.9 fusion.114
  140.2 3.1 collective-permute-start.1
  143.3 4.5 %fusion.33 = bf16[128,2048]{1,0:T(8,128)(2,1)} fusion(bf16[1,2048,1024]{2,1,0:T(8,128)(2,1)} %param.12, bf16[1,1,128,1024]{3,2,1,0:T(8,128)(2,1)S(1)} %all-gather.1), kind=kOutput, calls=%fused_computation.29 | convolution fusion | flops 537133056 | bytes 4980736 | tf_op jit(solution)/shard_map/dot_general | solution.py:81
  149.8 0.9 fusion.113
  150.6 11.0 %all_gather.20 = bf16[128,1024]{1,0:T(8,128)(2,1)S(1)} all-gather(bf16[32,1024]{1,0:T(8,128)(2,1)S(1)} %fusion.113), channel_id=1, replica_groups=mesh['section'=4,'row'=4,'col'=2] {'row'}, dimensions={0}, use_global_device_ids=true | all-gather | bytes 327680 | tf_op jit(solution)/shard_map/all_gather | solution.py:47
  161.6 3.7 %fusion.30 = bf16[128,2048]{1,0:T(8,128)(2,1)} fusion(bf16[128,1024]{1,0:T(8,128)(2,1)S(1)} %all_gather.20, bf16[1,1024,2048]{2,1,0:T(8,128)(2,1)} %param.11), kind=kOutput, calls=%fused_computation.28 | convolution fusion | flops 537133056 | bytes 4980736 | tf_op jit(solution)/shard_map/dot_general | solution.py:48
  165.3 0.0 reduce-scatter.13.cloned.1.call-start
  165.4 22.0 %all-reduce.15.cloned.1.call-done = (bf16[128,2048]{1,0:T(8,128)(2,1)}, bf16[128,2048]{1,0:T(8,128)(2,1)}) async-done(((bf16[128,2048]{1,0:T(8,128)(2,1)}, bf16[128,2048]{1,0:T(8,128)(2,1)}), (bf16[128,2048]{1,0:T(8,128)(2,1)}, bf16[128,2048]{1,0:T(8,128)(2,1)})) %all-reduce.15.cloned.1.call-update) | async-done | bytes 1048592 | tf_op jit(solution)/shard_map/psum | solution.py:49
  187.4 2.5 fusion.89
  189.9 4.4 %fusion.52 = bf16[128,1024]{1,0:T(8,128)(2,1)} fusion(bf16[128,2048]{1,0:T(8,128)(2,1)S(1)} %get-tuple-element.12, bf16[1,1024,2048]{2,1,0:T(8,128)(2,1)} %param.11), kind=kOutput, calls=%fused_computation.51 | convolution fusion | flops 537001984 | bytes 4980736 | tf_op jit(solution)/shard_map/dot_general | solution.py:89
  194.3 0.0 all-reduce.11.cloned.1.call-start
  194.4 18.6 %reduce-scatter.13.cloned.1.call-done = bf16[32,1024]{1,0:T(8,128)(2,1)} async-done(((bf16[128,1024]{1,0:T(8,128)(2,1)}), bf16[32,1024]{1,0:T(8,128)(2,1)}) %reduce-scatter.13.cloned.1.call-update) | async-done | bytes 65552 | tf_op jit(solution)/shard_map/reduce_scatter | solution.py:93
  213.0 0.9 fusion.104
  213.8 2.2 collective-permute-start.2
  216.0 3.7 %collective-permute-done.2 = bf16[32,1024]{1,0:T(8,128)(2,1)S(1)} collective-permute-done((bf16[32,1024]{1,0:T(8,128)(2,1)S(1)}, bf16[32,1024]{1,0:T(8,128)(2,1)S(1)}, u32[]{:S(2)}, u32[]{:S(2)}) %collective-permute-start.2) | collective-permute-done | bytes 65568 | tf_op jit(solution)/shard_map/ppermute | solution.py:10
  219.8 12.3 %all_gather.22 = bf16[128,1024]{1,0:T(8,128)(2,1)S(1)} all-gather(bf16[32,1024]{1,0:T(8,128)(2,1)S(1)} %bitcast_select_fusion), channel_id=1, replica_groups=mesh['section'=4,'row'=4,'col'=2] {'row'}, dimensions={0}, use_global_device_ids=true | all-gather | bytes 327680 | tf_op jit(solution)/shard_map/all_gather | solution.py:80
  232.0 4.5 %fusion.36 = bf16[128,2048]{1,0:T(8,128)(2,1)} fusion(bf16[128,1024]{1,0:T(8,128)(2,1)S(1)} %all_gather.22, bf16[1,2048,1024]{2,1,0:T(8,128)(2,1)} %param.12), kind=kOutput, calls=%fused_computation.30 | convolution fusion | flops 537133056 | bytes 4980736 | tf_op jit(solution)/shard_map/dot_general | solution.py:81
  236.6 0.0 reduce-scatter.15.cloned.1.call-start
  236.6 21.8 %all-reduce.11.cloned.1.call-done = bf16[128,2048]{1,0:T(8,128)(2,1)} async-done(((bf16[128,2048]{1,0:T(8,128)(2,1)}), bf16[128,2048]{1,0:T(8,128)(2,1)}) %all-reduce.11.cloned.1.call-update) | async-done | bytes 524304 | tf_op jit(solution)/shard_map/psum | solution.py:85
  258.4 2.3 fusion.81
  260.7 4.4 %fusion.55 = bf16[128,1024]{1,0:T(8,128)(2,1)} fusion(bf16[128,2048]{1,0:T(8,128)(2,1)S(1)} %get-tuple-element.10, bf16[1,1024,2048]{2,1,0:T(8,128)(2,1)} %param.11), kind=kOutput, calls=%fused_computation.52 | convolution fusion | flops 537001984 | bytes 4980736 | tf_op jit(solution)/shard_map/dot_general | solution.py:89
  265.1 0.0 reduce-scatter.11.cloned.1.call-start
  265.2 18.6 %reduce-scatter.15.cloned.1.call-done = bf16[32,1024]{1,0:T(8,128)(2,1)} async-done(((bf16[128,1024]{1,0:T(8,128)(2,1)}), bf16[32,1024]{1,0:T(8,128)(2,1)}) %reduce-scatter.15.cloned.1.call-update) | async-done | bytes 65552 | tf_op jit(solution)/shard_map/reduce_scatter | solution.py:93
  283.8 0.9 add_convert_fusion.1
  284.6 2.2 collective-permute-start.3
  286.9 3.8 %fusion.67 = bf16[128,1024]{1,0:T(8,128)(2,1)} fusion(bf16[1,2048,1024]{2,1,0:T(8,128)(2,1)} %param.12, bf16[128,2048]{1,0:T(8,128)(2,1)} %get-tuple-element.5), kind=kOutput, calls=%fused_computation.56 | convolution fusion | flops 538574848 | bytes 4980736 | tf_op jit(solution)/shard_map/dot_general | solution.py:53
  290.7 0.0 reduce-scatter.11.cloned.1.call-update
  290.7 0.0 all-reduce.13.cloned.1.call-start
  290.8 12.9 %all_gather.23 = bf16[128,1024]{1,0:T(8,128)(2,1)S(1)} all-gather(bf16[32,1024]{1,0:T(8,128)(2,1)S(1)} %bitcast_select_fusion.1), channel_id=1, replica_groups=mesh['section'=4,'row'=4,'col'=2] {'row'}, dimensions={0}, use_global_device_ids=true | all-gather | bytes 327680 | tf_op jit(solution)/shard_map/all_gather | solution.py:80
  303.7 4.5 %fusion.39 = bf16[128,2048]{1,0:T(8,128)(2,1)} fusion(bf16[128,1024]{1,0:T(8,128)(2,1)S(1)} %all_gather.23, bf16[1,2048,1024]{2,1,0:T(8,128)(2,1)} %param.12), kind=kOutput, calls=%fused_computation.31 | convolution fusion | flops 537133056 | bytes 4980736 | tf_op jit(solution)/shard_map/dot_general | solution.py:81
  308.2 0.0 reduce-scatter.17.cloned.1.call-start
  308.3 0.7 maximum_bitcast_fusion
  309.0 0.9 reduce-scatter.11.cloned.1.call-done
  309.8 0.9 fusion.110
  310.7 0.7 maximum_bitcast_fusion.1
  311.4 21.1 %all-reduce.13.cloned.1.call-done = bf16[128,2048]{1,0:T(8,128)(2,1)} async-done(((bf16[128,2048]{1,0:T(8,128)(2,1)}), bf16[128,2048]{1,0:T(8,128)(2,1)}) %all-reduce.13.cloned.1.call-update) | async-done | bytes 524304 | tf_op jit(solution)/shard_map/psum | solution.py:85
  332.5 2.5 fusion.73
  335.0 4.4 %fusion.58 = bf16[128,1024]{1,0:T(8,128)(2,1)} fusion(bf16[128,2048]{1,0:T(8,128)(2,1)S(1)} %get-tuple-element.8, bf16[1,1024,2048]{2,1,0:T(8,128)(2,1)} %param.11), kind=kOutput, calls=%fused_computation.53 | convolution fusion | flops 537001984 | bytes 4980736 | tf_op jit(solution)/shard_map/dot_general | solution.py:89
  339.4 4.4 %convert_bitcast_fusion.1 = bf16[1,1024,2048]{2,1,0:T(8,128)(2,1)} fusion(bf16[128,2048]{1,0:T(8,128)(2,1)S(1)} %get-tuple-element.12, bf16[128,2048]{1,0:T(8,128)(2,1)S(1)} %get-tuple-element.10, bf16[128,2048]{1,0:T(8,128)(2,1)S(1)} %get-tuple-element.8, bf16[128,1024]{1,0:T(8,128)(2,1)S(1)} %all_gather.20, bf16[128,1024]{1,0:T(8,128)(2,1)S(1)} %all_gather.19, ...), kind=kOutput, calls=%fused_computation.25 | convolution fusion | flops 1619787776 | bytes 6553600 | tf_op jit(solution)/shard_map/dot_general | solution.py:108
  343.9 4.4 %convert_bitcast_fusion = bf16[1,2048,1024]{2,1,0:T(8,128)(2,1)} fusion(bf16[128,2048]{1,0:T(8,128)(2,1)S(1)} %copy-done, bf16[128,2048]{1,0:T(8,128)(2,1)S(1)} %copy-done.2, bf16[128,2048]{1,0:T(8,128)(2,1)S(1)} %copy-done.3, bf16[128,1024]{1,0:T(8,128)(2,1)S(1)} %bitcast.121, bf16[128,1024]{1,0:T(8,128)(2,1)S(1)} %all_gather.22, ...), kind=kOutput, calls=%fused_computation.24 | convolution fusion | flops 1619787776 | bytes 6553600 | tf_op jit(solution)/shard_map/dot_general | solution.py:109
  348.3 9.8 %reduce-scatter.17.cloned.1.call-done = bf16[32,1024]{1,0:T(8,128)(2,1)} async-done(((bf16[128,1024]{1,0:T(8,128)(2,1)}), bf16[32,1024]{1,0:T(8,128)(2,1)}) %reduce-scatter.17.cloned.1.call-update) | async-done | bytes 65552 | tf_op jit(solution)/shard_map/reduce_scatter | solution.py:93
  358.1 0.9 fusion.111
  358.9 0.7 maximum_bitcast_fusion.2
  (35 shorter events, 0.2 us)
Async XLA Ops:
  7.2 39.9 %all-reduce.7.cloned.1.call-start = ((), (), s32[]{:S(2)}) async-start(), calls=%async_computation.6 | async-start | bytes 1048576 | tf_op jit(solution)/shard_map/psum | solution.py:49
  24.3 26.7 %copy-start.8 = (s32[6]{0:T(128)S(1)}, s32[6]{0:T(128)}, u32[]{:S(2)}) copy-start(s32[6]{0:T(128)} %param.8) | copy-start | bytes 76
  24.3 45.3 %copy-start.5 = (bf16[1,3,32,1024]{3,2,1,0:T(8,128)(2,1)S(1)}, bf16[1,3,32,1024]{3,2,1,0:T(8,128)(2,1)}, u32[]{:S(2)}) copy-start(bf16[1,3,32,1024]{3,2,1,0:T(8,128)(2,1)} %param.7) | copy-start | bytes 589828
  24.3 45.3 %reduce-scatter.7.cloned.1.call-start = ((), (), s32[]{:S(2)}) async-start(), calls=%async_computation.7 | async-start | bytes 327680 | tf_op jit(solution)/shard_map/reduce_scatter | solution.py:55
  50.9 64.2 %all-reduce.9.cloned.1.call-start = ((), (), s32[]{:S(2)}) async-start(), calls=%async_computation.8 | async-start | bytes 1048576 | tf_op jit(solution)/shard_map/psum | solution.py:49
  70.5 5.1 %collective-permute-start = (bf16[32,1024]{1,0:T(8,128)(2,1)S(1)}, bf16[32,1024]{1,0:T(8,128)(2,1)S(1)}, u32[]{:S(2)}, u32[]{:S(2)}) collective-permute-start(bf16[32,1024]{1,0:T(8,128)(2,1)S(1)} %get-tuple-element.14), channel_id=1, source_target_pairs={{0,8},{8,16},{16,24},{1,9},{9,17},{17,25},{2,10},{10,18},{18,26},{... | collective-permute-start | bytes 196616 | tf_op jit(solution)/shard_map/ppermute | solution.py:10
  92.4 26.6 %slice-start = ((bf16[1,3,32,1024]{3,2,1,0:T(8,128)(2,1)}), bf16[1,1,32,1024]{3,2,1,0:T(8,128)(2,1)S(1)}, s32[]{:S(2)}) async-start(bf16[1,3,32,1024]{3,2,1,0:T(8,128)(2,1)} %param.13), calls=%async_computation.17 | async-start | bytes 131072 | tf_op jit(solution)/shard_map/slice | solution.py:76
  92.4 46.9 %reduce-scatter.9.cloned.1.call-start = ((), (), s32[]{:S(2)}) async-start(), calls=%async_computation.9 | async-start | bytes 327680 | tf_op jit(solution)/shard_map/reduce_scatter | solution.py:55
  119.0 68.4 %all-reduce.15.cloned.1.call-start = ((), (), s32[]{:S(2)}) async-start(), calls=%async_computation.16 | async-start | bytes 2097152 | tf_op jit(solution)/shard_map/psum | solution.py:49
  140.2 9.5 %collective-permute-start.1 = (bf16[32,1024]{1,0:T(8,128)(2,1)S(1)}, bf16[32,1024]{1,0:T(8,128)(2,1)S(1)}, u32[]{:S(2)}, u32[]{:S(2)}) collective-permute-start(bf16[32,1024]{1,0:T(8,128)(2,1)S(1)} %get-tuple-element.18), channel_id=1, source_target_pairs={{0,8},{8,16},{16,24},{1,9},{9,17},{17,25},{2,10},{10,18},{18,26},{... | collective-permute-start | bytes 196616 | tf_op jit(solution)/shard_map/ppermute | solution.py:10
  165.3 47.7 %copy-start.4 = (bf16[1,3,32,1024]{3,2,1,0:T(8,128)(2,1)S(1)}, bf16[1,3,32,1024]{3,2,1,0:T(8,128)(2,1)}, u32[]{:S(2)}) copy-start(bf16[1,3,32,1024]{3,2,1,0:T(8,128)(2,1)} %param.13) | copy-start | bytes 589828
  165.3 47.7 %reduce-scatter.13.cloned.1.call-start = ((), (), s32[]{:S(2)}) async-start(), calls=%async_computation.11 | async-start | bytes 327680 | tf_op jit(solution)/shard_map/reduce_scatter | solution.py:93
  194.3 64.1 %copy-start.1 = (bf16[128,2048]{1,0:T(8,128)(2,1)S(1)}, bf16[128,2048]{1,0:T(8,128)(2,1)}, u32[]{:S(2)}) copy-start(bf16[128,2048]{1,0:T(8,128)(2,1)} %all-reduce.9.cloned.1.call-done) | copy-start | bytes 1572868
  194.3 64.0 %all-reduce.11.cloned.1.call-start = ((), (), s32[]{:S(2)}) async-start(), calls=%async_computation.12 | async-start | bytes 1048576 | tf_op jit(solution)/shard_map/psum | solution.py:85
  213.8 5.9 %collective-permute-start.2 = (bf16[32,1024]{1,0:T(8,128)(2,1)S(1)}, bf16[32,1024]{1,0:T(8,128)(2,1)S(1)}, u32[]{:S(2)}, u32[]{:S(2)}) collective-permute-start(bf16[32,1024]{1,0:T(8,128)(2,1)S(1)} %fusion.104), channel_id=1, source_target_pairs={{8,0},{16,8},{24,16},{9,1},{17,9},{25,17},{10,2},{18,10},{26,18},{... | collective-permute-start | bytes 196616 | tf_op jit(solution)/shard_map/ppermute | solution.py:10
  236.6 47.2 %reduce-scatter.15.cloned.1.call-start = ((), (), s32[]{:S(2)}) async-start(), calls=%async_computation.13 | async-start | bytes 327680 | tf_op jit(solution)/shard_map/reduce_scatter | solution.py:93
  265.1 44.7 %reduce-scatter.11.cloned.1.call-start = ((), (), s32[]{:S(2)}) async-start(), calls=%async_computation.10 | async-start | bytes 327680 | tf_op jit(solution)/shard_map/reduce_scatter | solution.py:55
  284.6 6.1 %copy-start.6 = (bf16[32,1024]{1,0:T(8,128)(2,1)}, bf16[32,1024]{1,0:T(8,128)(2,1)S(1)}, u32[]{:S(2)}) copy-start(bf16[32,1024]{1,0:T(8,128)(2,1)S(1)} %add_convert_fusion.1) | copy-start | bytes 196612
  284.6 6.1 %collective-permute-start.3 = (bf16[32,1024]{1,0:T(8,128)(2,1)S(1)}, bf16[32,1024]{1,0:T(8,128)(2,1)S(1)}, u32[]{:S(2)}, u32[]{:S(2)}) collective-permute-start(bf16[32,1024]{1,0:T(8,128)(2,1)S(1)} %add_convert_fusion.1), channel_id=1, source_target_pairs={{8,0},{16,8},{24,16},{9,1},{17,9},{25,17},{10,2},{18,10},{26,18},{... | collective-permute-start | bytes 196616 | tf_op jit(solution)/shard_map/ppermute | solution.py:10
  290.7 41.8 %all-reduce.13.cloned.1.call-start = ((), (), s32[]{:S(2)}) async-start(), calls=%async_computation.14 | async-start | bytes 1048576 | tf_op jit(solution)/shard_map/psum | solution.py:85
  308.2 49.9 %reduce-scatter.17.cloned.1.call-start = ((), (), s32[]{:S(2)}) async-start(), calls=%async_computation.15 | async-start | bytes 327680 | tf_op jit(solution)/shard_map/reduce_scatter | solution.py:93
  339.4 4.4 %copy-start = (bf16[128,2048]{1,0:T(8,128)(2,1)S(1)}, bf16[128,2048]{1,0:T(8,128)(2,1)}, u32[]{:S(2)}) copy-start(bf16[128,2048]{1,0:T(8,128)(2,1)} %get-tuple-element.11) | copy-start | bytes 1572868
  339.4 4.4 %copy-start.2 = (bf16[128,2048]{1,0:T(8,128)(2,1)S(1)}, bf16[128,2048]{1,0:T(8,128)(2,1)}, u32[]{:S(2)}) copy-start(bf16[128,2048]{1,0:T(8,128)(2,1)} %get-tuple-element.9) | copy-start | bytes 1572868
  339.4 4.4 %copy-start.3 = (bf16[128,2048]{1,0:T(8,128)(2,1)S(1)}, bf16[128,2048]{1,0:T(8,128)(2,1)}, u32[]{:S(2)}) copy-start(bf16[128,2048]{1,0:T(8,128)(2,1)} %get-tuple-element.7) | copy-start | bytes 1572868
  343.9 15.1 %copy-start.7 = (bf16[32,1024]{1,0:T(8,128)(2,1)S(1)}, bf16[32,1024]{1,0:T(8,128)(2,1)}, u32[]{:S(2)}) copy-start(bf16[32,1024]{1,0:T(8,128)(2,1)} %copy-done.6) | copy-start | bytes 196612
Sparse Core Ops, SparseCore 0:
  24.4 22.6 all-reduce.6
  51.1 18.4 reduce-scatter.6
  92.5 22.5 all-reduce.8
  119.1 20.1 reduce-scatter.8
  165.4 21.9 all-reduce.14
  194.4 18.4 reduce-scatter.12
  236.7 21.6 all-reduce.10
  265.2 18.4 reduce-scatter.14
  290.8 18.9 reduce-scatter.10
  312.7 19.7 all-reduce.12
  339.5 18.4 reduce-scatter.16
where the time goes:
time: 370 us; the launch traced here: 366 us
  waiting for transfers between devices  185 us (50%)
  blocking collectives  74 us (20%)
  matrix products  58.1 us (16%)
  between operations  19.9 us (5%)
  other arithmetic  16.3 us (4%)
  starting transfers between devices  11.1 us (3%)
    psum x5, waiting for transfers between devices, per_device(): lax.psum(partial_value.astype(jnp.bfloat16), 'col').astype(jnp.float32)  110 us
    reduce_scatter x3, waiting for transfers between devices, per_device(): lax.psum_scatter(feature_term(jnp.int32(0), piece_rows * lax.axis_size('r...  47 us
    all_gather x3, blocking collectives, per_device(): full_grad = lax.all_gather(grad_out, 'row', axis=0, tiled=True)  38.3 us
    all_gather x3, blocking collectives, per_device(): full_in = lax.all_gather(act_in, 'row', axis=0, tiled=True)  35.7 us
    reduce_scatter x3, waiting for transfers between devices, per_device(): lax.psum_scatter(down_term(jnp.int32(0), piece_rows * lax.axis_size('row'...  24 us
    dot_general x3, matrix products, per_device(): lax.dot_general(full_grad, down_block, contract_last, preferred_element_t...  13.5 us
    dot_general x3, matrix products, feature_term(): lax.dot_general(grad_pre, up_block, contract_last, preferred_element_type...  13.2 us
    dot_general x3, matrix products, down_term(): return jnp.dot(act_full, down_block, preferred_element_type=jnp.float32)  11.5 us
  transfers between devices with their start and end apart: 15, of which 12 were waited for; matrix products, arithmetic and copies ran while one was open for 7% of the time, Pallas kernels for 0%

commit v1 on v0

v1 whole, which is shorter than its diff:
```python
import jax
import jax.numpy as jnp
from jax import lax
from jax.sharding import PartitionSpec as P

BF = jnp.bfloat16
F32 = jnp.float32
LAST = (((1,), (1,)), ((), ()))
FIRST = (((0,), (0,)), ((), ()))


def from_behind(block, axis, distance):
    devices = range(lax.axis_size(axis))
    route = [(i - distance, i) for i in devices if i - distance in devices]
    return lax.ppermute(block, axis, route)


def turn(block, axis, distance):
    size = lax.axis_size(axis)
    return lax.ppermute(block, axis, [(i, (i + distance) % size) for i in range(size)])


def gather_rows(block):
    size = lax.axis_size("row")
    return jnp.concatenate([block] + [turn(block, "row", -j) for j in range(1, size)], axis=0)


def scatter_rows(partial):
    size = lax.axis_size("row")
    pieces = jnp.split(partial, size, axis=0)
    total = pieces[0].astype(F32)
    for j in range(1, size):
        total = total + turn(pieces[j], "row", j).astype(F32)
    return total


def sum_cols(partial):
    size = lax.axis_size("col")
    if size > 2:
        return lax.psum(partial, "col").astype(F32)
    total = partial.astype(F32)
    for j in range(1, size):
        total = total + turn(partial, "col", j).astype(F32)
    return total


def silu_slope(value):
    sig = jax.nn.sigmoid(value)
    return sig * (1.0 + value * (1.0 - sig))


def pick(table, index):
    return lax.dynamic_index_in_dim(table, index, 0, keepdims=False)


def matmul(a, b, dims=(((1,), (0,)), ((), ()))):
    return lax.dot_general(a, b, dims, preferred_element_type=F32)


def per_device(inputs, sample_ids, send_base, recv_base, w_up, w_down, cotangent):
    section = lax.axis_index("section")
    sections = lax.axis_size("section")
    ticks = inputs.shape[1]
    up_block = w_up[0]
    down_block = w_down[0]
    full_ins, pres, acts, seen_in, seen_out = [], [], [], [], []
    sending = None
    for tick in range(ticks):
        sample = pick(sample_ids, tick - section + sections - 1)
        if tick == 0:
            act_in = inputs[0, tick]
        else:
            arrived = from_behind(sending, "section", 1)
            rebuilt = (pick(recv_base[0], sample).astype(F32) + arrived.astype(F32)).astype(BF)
            act_in = jnp.where(section == 0, inputs[0, tick], rebuilt)
        full_in = gather_rows(act_in)
        pre = sum_cols(matmul(full_in, up_block).astype(BF))
        act = jax.nn.silu(pre).astype(BF)
        mixed = scatter_rows(matmul(act, down_block).astype(BF))
        act_out = (act_in.astype(F32) + mixed).astype(BF)
        stored = pick(send_base[0], sample)
        sending = (act_out.astype(F32) - stored.astype(F32)).astype(BF)
        full_ins.append(full_in)
        pres.append(pre)
        acts.append(act)
        seen_in.append(act_in)
        seen_out.append(act_out)
    full_grads = [None] * ticks
    pre_grads = [None] * ticks
    seen_grad = [None] * ticks
    for step in range(ticks):
        tick = ticks - 1 - step
        if step == 0:
            grad_out = cotangent[0, tick]
        else:
            arrived = from_behind(sending, "section", -1)
            grad_out = jnp.where(section == sections - 1, cotangent[0, tick], arrived)
        full_grad = gather_rows(grad_out)
        grad_act = sum_cols(matmul(full_grad, down_block, LAST).astype(BF))
        grad_pre = (grad_act * silu_slope(pres[tick])).astype(BF)
        returned = scatter_rows(matmul(grad_pre, up_block, LAST).astype(BF))
        sending = (grad_out.astype(F32) + returned).astype(BF)
        full_grads[tick] = full_grad
        pre_grads[tick] = grad_pre
        seen_grad[tick] = sending
    grad_up = matmul(jnp.concatenate(full_ins, axis=0), jnp.concatenate(pre_grads, axis=0), FIRST)
    grad_down = matmul(jnp.concatenate(acts, axis=0), jnp.concatenate(full_grads, axis=0), FIRST)
    return (
        jnp.stack(seen_in)[None],
        jnp.stack(seen_out)[None],
        jnp.stack(seen_grad)[None],
        grad_up.astype(BF)[None],
        grad_down.astype(BF)[None],
    )


def solution(mesh):
    placed = (
        P("section", None, "row", "col"),
        P(),
        P("section", None, "row", "col"),
        P("section", None, "row", "col"),
        P("section", "col", "row"),
        P("section", "row", "col"),
        P("section", None, "row", "col"),
    )
    return jax.shard_map(
        per_device,
        mesh=mesh,
        in_specs=placed,
        out_specs=(
            P("section", None, "row", "col"),
            P("section", None, "row", "col"),
            P("section", None, "row", "col"),
            P("section", "col", "row"),
            P("section", "row", "col"),
        ),
        check_vma=False,
    )
```

time: 370 us -> 178 us (0.48)
  waiting for transfers between devices: 185 us -> 44.8 us
  blocking collectives: 74 us -> 0 us
  starting transfers between devices: 11.1 us -> 70.8 us
  matrix products: 58.1 us -> 32.2 us
  between operations: 19.9 us -> 6.76 us
  local copies, waits for them, and re-layouts: 1.5 us -> 8.78 us
    psum x5 -> x0, waiting for transfers between devices: 110 us -> none  [per_device(): lax.psum(partial_value.astype(jnp.bfloat16), 'col').astype(jnp.float32)]
    all_gather x6 -> x0, blocking collectives: 74 us -> none  [the longest x3 38.3 us: per_device(): full_grad = lax.all_gather(grad_out, 'row', axis=0, tiled=True)]
    reduce_scatter x6 -> x0, waiting for transfers between devices: 71 us -> none  [the longest x3 47 us: per_device(): lax.psum_scatter(feature_term(jnp.int32(0), piece_rows * lax.axis_size('r...]
    ppermute x0 -> x42, starting transfers between devices: none -> 59.8 us  [turn(): lax.ppermute(block, axis, [(i, (i + distance) % size) for i in range(size)])]
    ppermute x0 -> x42, waiting for transfers between devices: none -> 38.3 us  [turn(): lax.ppermute(block, axis, [(i, (i + distance) % size) for i in range(size)])]
    dot_general x14, matrix products: 58.1 us -> 32.2 us  [matmul(): return lax.dot_general(a, b, dims, preferred_element_type=F32)]
    unnamed x18 -> x71, local copies, waits for them, and re-layouts: 0.04 us -> 4.43 us
    convert_element_type x5 -> x9, other arithmetic: 8.96 us -> 7.16 us  [the longest x2 3.04 us: per_device(): sending = (act_out.astype(F32) - stored.astype(F32)).astype(BF)]
  transfers between devices with their start and end apart: 15 -> 46, of which waited for: 12 -> 29; matrix products, arithmetic and copies ran while one was open for 7% -> 16% of each run, Pallas kernels for 0% -> 0%
where the time goes in v1:
time: 178 us; the launch traced here: 177 us
  starting transfers between devices  70.8 us (40%)
  waiting for transfers between devices  44.8 us (25%)
  matrix products  32.2 us (18%)
  other arithmetic  13.4 us (8%)
  local copies, waits for them, and re-layouts  8.78 us (5%)
  between operations  6.76 us (4%)
    ppermute x42, starting transfers between devices, turn(): lax.ppermute(block, axis, [(i, (i + distance) % size) for i in range(size)])  59.8 us
    ppermute x42, waiting for transfers between devices, turn(): lax.ppermute(block, axis, [(i, (i + distance) % size) for i in range(size)])  38.3 us
    dot_general x14, matrix products, matmul(): return lax.dot_general(a, b, dims, preferred_element_type=F32)  32.2 us
    ppermute x4, starting transfers between devices, from_behind(): return lax.ppermute(block, axis, route)  11 us
    ppermute x4, waiting for transfers between devices, from_behind(): return lax.ppermute(block, axis, route)  6.58 us
    unnamed x71, local copies, waits for them, and re-layouts  4.43 us
  transfers between devices with their start and end apart: 46, of which 29 were waited for; matrix products, arithmetic and copies ran while one was open for 16% of the time, Pallas kernels for 0%

profile of v1, /device:TPU:3, one launch (start us, length us, event | category | flops | bytes accessed | tf_op | source)
XLA Modules:
  0.0 176.8 jit_solution(918827185829455958)
XLA Ops:
  0.7 1.5 slice_bitcast_fusion.2
  2.2 1.3 collective-permute-start.2
  3.5 2.3 %collective-permute-start.1 = (bf16[32,1024]{1,0:T(8,128)(2,1)S(1)}, bf16[32,1024]{1,0:T(8,128)(2,1)S(1)}, u32[]{:S(2)}, u32[]{:S(2)}) collective-permute-start(bf16[32,1024]{1,0:T(8,128)(2,1)S(1)} %get-tuple-element.36), channel_id=1, source_target_pairs={{0,4},{2,6},{4,0},{6,2},{1,5},{3,7},{5,1},{7,3},{8,12},{10,14},{12... | collective-permute-start | bytes 196616 | tf_op jit(solution)/shard_map/ppermute | solution.py:20
  5.8 1.1 collective-permute-start
  7.2 2.9 %collective-permute-done.1 = bf16[32,1024]{1,0:T(8,128)(2,1)S(1)} collective-permute-done((bf16[32,1024]{1,0:T(8,128)(2,1)S(1)}, bf16[32,1024]{1,0:T(8,128)(2,1)S(1)}, u32[]{:S(2)}, u32[]{:S(2)}) %collective-permute-start.1) | collective-permute-done | bytes 65568 | tf_op jit(solution)/shard_map/ppermute | solution.py:20
  10.1 2.9 %fusion.24 = bf16[128,2048]{1,0:T(8,128)(2,1)S(1)} fusion(bf16[1,1024,2048]{2,1,0:T(8,128)(2,1)} %param.11, bf16[32,1024]{1,0:T(8,128)(2,1)S(1)} %collective-permute-done.2, bf16[32,1024]{1,0:T(8,128)(2,1)S(1)} %collective-permute-done.1, bf16[32,1024]{1,0:T(8,128)(2,1)S(1)} %collective-permute-done, bf16[32,1024]{1,0:T(8,128)(2,1)S(1)} %get-tuple-element.36), kind=kOutput, calls=%fused_computation.26 | convolution fusion | flops 538181632 | bytes 4980736 | tf_op jit(solution)/shard_map/dot_general | solution.py:57
  13.0 1.8 collective-permute-start.3
  19.6 3.1 %fusion.61 = bf16[128,1024]{1,0:T(8,128)(2,1)S(1)} fusion(bf16[128,2048]{1,0:T(8,128)(2,1)S(1)} %multiply_convert_fusion.5, bf16[1,2048,1024]{2,1,0:T(8,128)(2,1)} %param.12), kind=kOutput, calls=%fused_computation.45 | convolution fusion | flops 537001984 | bytes 4980736 | tf_op jit(solution)/shard_map/dot_general | solution.py:57
  22.7 1.3 collective-permute-start.4
  24.0 2.0 %collective-permute-start.6 = (bf16[32,1024]{1,0:T(8,128)(2,1)S(1)}, bf16[32,1024]{1,0:T(8,128)(2,1)S(1)}, u32[]{:S(2)}, u32[]{:S(2)}) collective-permute-start(bf16[32,1024]{1,0:T(8,128)(2,1)S(1)} %get-tuple-element.33), channel_id=1, source_target_pairs={{0,6},{2,0},{4,2},{6,4},{1,7},{3,1},{5,3},{7,5},{8,14},{10,8},{12,... | collective-permute-start | bytes 196616 | tf_op jit(solution)/shard_map/ppermute | solution.py:20
  26.1 2.3 %collective-permute-done.4 = bf16[32,1024]{1,0:T(8,128)(2,1)S(1)} collective-permute-done((bf16[32,1024]{1,0:T(8,128)(2,1)S(1)}, bf16[32,1024]{1,0:T(8,128)(2,1)S(1)}, u32[]{:S(2)}, u32[]{:S(2)}) %collective-permute-start.4) | collective-permute-done | bytes 65568 | tf_op jit(solution)/shard_map/ppermute | solution.py:20
  28.7 3.4 %collective-permute-done.5 = bf16[32,1024]{1,0:T(8,128)(2,1)S(1)} collective-permute-done((bf16[32,1024]{1,0:T(8,128)(2,1)S(1)}, bf16[32,1024]{1,0:T(8,128)(2,1)S(1)}, u32[]{:S(2)}, u32[]{:S(2)}) %collective-permute-start.5) | collective-permute-done | bytes 65568 | tf_op jit(solution)/shard_map/ppermute | solution.py:20
  32.1 1.5 fusion.114
  33.6 3.1 %collective-permute-start.7 = (bf16[32,1024]{1,0:T(8,128)(2,1)S(1)}, bf16[32,1024]{1,0:T(8,128)(2,1)S(1)}, u32[]{:S(2)}, u32[]{:S(2)}) collective-permute-start(bf16[32,1024]{1,0:T(8,128)(2,1)S(1)} %get-tuple-element.13), channel_id=1, source_target_pairs={{0,8},{8,16},{16,24},{1,9},{9,17},{17,25},{2,10},{10,18},{18,26},{... | collective-permute-start | bytes 196616 | tf_op jit(solution)/shard_map/ppermute | solution.py:15
  36.7 1.9 %collective-permute-done.7 = bf16[32,1024]{1,0:T(8,128)(2,1)S(1)} collective-permute-done((bf16[32,1024]{1,0:T(8,128)(2,1)S(1)}, bf16[32,1024]{1,0:T(8,128)(2,1)S(1)}, u32[]{:S(2)}, u32[]{:S(2)}) %collective-permute-start.7) | collective-permute-done | bytes 65568 | tf_op jit(solution)/shard_map/ppermute | solution.py:15
  39.6 2.7 %collective-permute-start.9 = (bf16[32,1024]{1,0:T(8,128)(2,1)S(1)}, bf16[32,1024]{1,0:T(8,128)(2,1)S(1)}, u32[]{:S(2)}, u32[]{:S(2)}) collective-permute-start(bf16[32,1024]{1,0:T(8,128)(2,1)S(1)} %get-tuple-element.10), channel_id=1, source_target_pairs={{0,4},{2,6},{4,0},{6,2},{1,5},{3,7},{5,1},{7,3},{8,12},{10,14},{12... | collective-permute-start | bytes 196616 | tf_op jit(solution)/shard_map/ppermute | solution.py:20
  42.8 1.7 collective-permute-done.10
  46.6 3.3 %collective-permute-start.11 = (bf16[128,2048]{1,0:T(8,128)(2,1)S(1)}, bf16[128,2048]{1,0:T(8,128)(2,1)S(1)}, u32[]{:S(2)}, u32[]{:S(2)}) collective-permute-start(bf16[128,2048]{1,0:T(8,128)(2,1)S(1)} %fusion.27), channel_id=1, source_target_pairs={{0,1},{1,0},{2,3},{3,2},{4,5},{5,4},{6,7},{7,6},{8,9},{9,8},{10,11... | collective-permute-start | bytes 1572872 | tf_op jit(solution)/shard_map/ppermute | solution.py:20
  49.9 1.5 slice_bitcast_fusion
  52.2 2.0 %collective-permute-start.24 = (bf16[32,1024]{1,0:T(8,128)(2,1)}, bf16[32,1024]{1,0:T(8,128)(2,1)}, u32[]{:S(2)}, u32[]{:S(2)}) collective-permute-start(bf16[32,1024]{1,0:T(8,128)(2,1)} %slice_bitcast_fusion), channel_id=1, source_target_pairs={{0,4},{2,6},{4,0},{6,2},{1,5},{3,7},{5,1},{7,3},{8,12},{10,14},{12... | collective-permute-start | bytes 196616 | tf_op jit(solution)/shard_map/ppermute | solution.py:20
  56.9 3.0 %fusion.64 = bf16[128,1024]{1,0:T(8,128)(2,1)S(1)} fusion(bf16[128,2048]{1,0:T(8,128)(2,1)S(1)} %multiply_convert_fusion.4, bf16[1,2048,1024]{2,1,0:T(8,128)(2,1)} %param.12), kind=kOutput, calls=%fused_computation.46 | convolution fusion | flops 537001984 | bytes 4980736 | tf_op jit(solution)/shard_map/dot_general | solution.py:57
  60.6 2.6 %collective-permute-start.14 = (bf16[32,1024]{1,0:T(8,128)(2,1)S(1)}, bf16[32,1024]{1,0:T(8,128)(2,1)S(1)}, u32[]{:S(2)}, u32[]{:S(2)}) collective-permute-start(bf16[32,1024]{1,0:T(8,128)(2,1)S(1)} %get-tuple-element.30), channel_id=1, source_target_pairs={{0,6},{2,0},{4,2},{6,4},{1,7},{3,1},{5,3},{7,5},{8,14},{10,8},{12,... | collective-permute-start | bytes 196616 | tf_op jit(solution)/shard_map/ppermute | solution.py:20
  63.9 1.2 collective-permute-done.12
  65.1 2.6 %collective-permute-done.13 = bf16[32,1024]{1,0:T(8,128)(2,1)S(1)} collective-permute-done((bf16[32,1024]{1,0:T(8,128)(2,1)S(1)}, bf16[32,1024]{1,0:T(8,128)(2,1)S(1)}, u32[]{:S(2)}, u32[]{:S(2)}) %collective-permute-start.13) | collective-permute-done | bytes 65568 | tf_op jit(solution)/shard_map/ppermute | solution.py:20
  67.7 1.5 fusion.112
  69.2 4.0 %collective-permute-start.15 = (bf16[32,1024]{1,0:T(8,128)(2,1)S(1)}, bf16[32,1024]{1,0:T(8,128)(2,1)S(1)}, u32[]{:S(2)}, u32[]{:S(2)}) collective-permute-start(bf16[32,1024]{1,0:T(8,128)(2,1)S(1)} %get-tuple-element.11), channel_id=1, source_target_pairs={{0,8},{8,16},{16,24},{1,9},{9,17},{17,25},{2,10},{10,18},{18,26},{... | collective-permute-start | bytes 196616 | tf_op jit(solution)/shard_map/ppermute | solution.py:15
  74.5 1.5 constant_dynamic-update-slice_fusion.3
  76.8 2.6 %collective-permute-start.16 = (bf16[32,1024]{1,0:T(8,128)(2,1)S(1)}, bf16[32,1024]{1,0:T(8,128)(2,1)S(1)}, u32[]{:S(2)}, u32[]{:S(2)}) collective-permute-start(bf16[32,1024]{1,0:T(8,128)(2,1)S(1)} %get-tuple-element.8), channel_id=1, source_target_pairs={{0,6},{2,0},{4,2},{6,4},{1,7},{3,1},{5,3},{7,5},{8,14},{10,8},{12,... | collective-permute-start | bytes 196616 | tf_op jit(solution)/shard_map/ppermute | solution.py:20
  79.4 2.4 %fusion.33 = bf16[128,2048]{1,0:T(8,128)(2,1)S(1)} fusion(bf16[1,2048,1024]{2,1,0:T(8,128)(2,1)S(1)} %copy-done, bf16[32,1024]{1,0:T(8,128)(2,1)S(1)} %collective-permute-done.25, bf16[32,1024]{1,0:T(8,128)(2,1)} %collective-permute-done.24, bf16[32,1024]{1,0:T(8,128)(2,1)S(1)} %collective-permute-done.23, bf16[32,1024]{1,0:T(8,128)(2,1)} %slice_bitcast_fusion), kind=kOutput, calls=%fused_computation.29 | convolution fusion | flops 538181632 | bytes 4980736 | tf_op jit(solution)/shard_map/dot_general | solution.py:57
  81.8 4.3 %collective-permute-start.26 = (bf16[128,2048]{1,0:T(8,128)(2,1)S(1)}, bf16[128,2048]{1,0:T(8,128)(2,1)S(1)}, u32[]{:S(2)}, u32[]{:S(2)}) collective-permute-start(bf16[128,2048]{1,0:T(8,128)(2,1)S(1)} %fusion.33), channel_id=1, source_target_pairs={{0,1},{1,0},{2,3},{3,2},{4,5},{5,4},{6,7},{7,6},{8,9},{9,8},{10,11... | collective-permute-start | bytes 1572872 | tf_op jit(solution)/shard_map/ppermute | solution.py:20
  87.6 1.4 collective-permute-done.19
  89.0 1.4 multiply_convert_fusion.2
  90.4 1.5 fusion.52
  92.6 1.4 collective-permute-start.27
  94.0 1.9 %collective-permute-start.29 = (bf16[32,1024]{1,0:T(8,128)(2,1)}, bf16[32,1024]{1,0:T(8,128)(2,1)}, u32[]{:S(2)}, u32[]{:S(2)}) collective-permute-start(bf16[32,1024]{1,0:T(8,128)(2,1)} %get-tuple-element.24), channel_id=1, source_target_pairs={{0,6},{2,0},{4,2},{6,4},{1,7},{3,1},{5,3},{7,5},{8,14},{10,8},{12,... | collective-permute-start | bytes 196616 | tf_op jit(solution)/shard_map/ppermute | solution.py:20
  95.9 2.1 %collective-permute-done.27 = bf16[32,1024]{1,0:T(8,128)(2,1)} collective-permute-done((bf16[32,1024]{1,0:T(8,128)(2,1)}, bf16[32,1024]{1,0:T(8,128)(2,1)}, u32[]{:S(2)}, u32[]{:S(2)}) %collective-permute-start.27) | collective-permute-done | bytes 65568 | tf_op jit(solution)/shard_map/ppermute | solution.py:20
  98.0 1.2 collective-permute-done.29
  99.2 3.5 %collective-permute-done.28 = bf16[32,1024]{1,0:T(8,128)(2,1)} collective-permute-done((bf16[32,1024]{1,0:T(8,128)(2,1)}, bf16[32,1024]{1,0:T(8,128)(2,1)}, u32[]{:S(2)}, u32[]{:S(2)}) %collective-permute-start.28) | collective-permute-done | bytes 65568 | tf_op jit(solution)/shard_map/ppermute | solution.py:20
  102.8 1.0 add_convert_fusion.2
  103.8 1.9 %collective-permute-start.30 = (bf16[32,1024]{1,0:T(8,128)(2,1)S(1)}, bf16[32,1024]{1,0:T(8,128)(2,1)S(1)}, u32[]{:S(2)}, u32[]{:S(2)}) collective-permute-start(bf16[32,1024]{1,0:T(8,128)(2,1)S(1)} %add_convert_fusion.2), channel_id=1, source_target_pairs={{8,0},{16,8},{24,16},{9,1},{17,9},{25,17},{10,2},{18,10},{26,18},{... | collective-permute-start | bytes 196616 | tf_op jit(solution)/shard_map/ppermute | solution.py:15
  105.7 1.5 maximum_bitcast_fusion
  107.2 3.1 %collective-permute-done.30 = bf16[32,1024]{1,0:T(8,128)(2,1)S(1)} collective-permute-done((bf16[32,1024]{1,0:T(8,128)(2,1)S(1)}, bf16[32,1024]{1,0:T(8,128)(2,1)S(1)}, u32[]{:S(2)}, u32[]{:S(2)}) %collective-permute-start.30) | collective-permute-done | bytes 65568 | tf_op jit(solution)/shard_map/ppermute | solution.py:15
  111.2 2.7 %collective-permute-start.32 = (bf16[32,1024]{1,0:T(8,128)(2,1)S(1)}, bf16[32,1024]{1,0:T(8,128)(2,1)S(1)}, u32[]{:S(2)}, u32[]{:S(2)}) collective-permute-start(bf16[32,1024]{1,0:T(8,128)(2,1)S(1)} %bitcast_select_fusion), channel_id=1, source_target_pairs={{0,4},{2,6},{4,0},{6,2},{1,5},{3,7},{5,1},{7,3},{8,12},{10,14},{12... | collective-permute-start | bytes 196616 | tf_op jit(solution)/shard_map/ppermute | solution.py:20
  114.5 1.5 constant_dynamic-update-slice_fusion.2
  117.5 3.7 %fusion.36 = bf16[128,2048]{1,0:T(8,128)(2,1)S(1)} fusion(bf16[1,2048,1024]{2,1,0:T(8,128)(2,1)} %param.12, bf16[32,1024]{1,0:T(8,128)(2,1)S(1)} %collective-permute-done.33, bf16[32,1024]{1,0:T(8,128)(2,1)S(1)} %collective-permute-done.32, bf16[32,1024]{1,0:T(8,128)(2,1)S(1)} %collective-permute-done.31, bf16[32,1024]{1,0:T(8,128)(2,1)S(1)} %bitcast_select_fusion), kind=kOutput, calls=%fused_computation.30 | convolution fusion | flops 538181632 | bytes 4980736 | tf_op jit(solution)/shard_map/dot_general | solution.py:57
  121.2 3.1 %collective-permute-start.34 = (bf16[128,2048]{1,0:T(8,128)(2,1)S(1)}, bf16[128,2048]{1,0:T(8,128)(2,1)S(1)}, u32[]{:S(2)}, u32[]{:S(2)}) collective-permute-start(bf16[128,2048]{1,0:T(8,128)(2,1)S(1)} %fusion.36), channel_id=1, source_target_pairs={{0,1},{1,0},{2,3},{3,2},{4,5},{5,4},{6,7},{7,6},{8,9},{9,8},{10,11... | collective-permute-start | bytes 1572872 | tf_op jit(solution)/shard_map/ppermute | solution.py:20
  126.4 1.5 fusion.55
  127.9 1.0 collective-permute-start.35
  129.0 2.3 %collective-permute-start.37 = (bf16[32,1024]{1,0:T(8,128)(2,1)S(1)}, bf16[32,1024]{1,0:T(8,128)(2,1)S(1)}, u32[]{:S(2)}, u32[]{:S(2)}) collective-permute-start(bf16[32,1024]{1,0:T(8,128)(2,1)S(1)} %get-tuple-element.21), channel_id=1, source_target_pairs={{0,6},{2,0},{4,2},{6,4},{1,7},{3,1},{5,3},{7,5},{8,14},{10,8},{12,... | collective-permute-start | bytes 196616 | tf_op jit(solution)/shard_map/ppermute | solution.py:20
  132.0 2.6 %collective-permute-start.22 = (bf16[32,1024]{1,0:T(8,128)(2,1)S(1)}, bf16[32,1024]{1,0:T(8,128)(2,1)S(1)}, u32[]{:S(2)}, u32[]{:S(2)}) collective-permute-start(bf16[32,1024]{1,0:T(8,128)(2,1)S(1)} %get-tuple-element.27), channel_id=1, source_target_pairs={{0,6},{2,0},{4,2},{6,4},{1,7},{3,1},{5,3},{7,5},{8,14},{10,8},{12,... | collective-permute-start | bytes 196616 | tf_op jit(solution)/shard_map/ppermute | solution.py:20
  135.2 2.3 %collective-permute-done.36 = bf16[32,1024]{1,0:T(8,128)(2,1)S(1)} collective-permute-done((bf16[32,1024]{1,0:T(8,128)(2,1)S(1)}, bf16[32,1024]{1,0:T(8,128)(2,1)S(1)}, u32[]{:S(2)}, u32[]{:S(2)}) %collective-permute-start.36) | collective-permute-done | bytes 65568 | tf_op jit(solution)/shard_map/ppermute | solution.py:20
  137.5 1.9 %collective-permute-start.38 = (bf16[32,1024]{1,0:T(8,128)(2,1)S(1)}, bf16[32,1024]{1,0:T(8,128)(2,1)S(1)}, u32[]{:S(2)}, u32[]{:S(2)}) collective-permute-start(bf16[32,1024]{1,0:T(8,128)(2,1)S(1)} %add_convert_fusion.1), channel_id=1, source_target_pairs={{8,0},{16,8},{24,16},{9,1},{17,9},{25,17},{10,2},{18,10},{26,18},{... | collective-permute-start | bytes 196616 | tf_op jit(solution)/shard_map/ppermute | solution.py:15
  139.5 2.9 %collective-permute-done.21 = bf16[32,1024]{1,0:T(8,128)(2,1)S(1)} collective-permute-done((bf16[32,1024]{1,0:T(8,128)(2,1)S(1)}, bf16[32,1024]{1,0:T(8,128)(2,1)S(1)}, u32[]{:S(2)}, u32[]{:S(2)}) %collective-permute-start.21) | collective-permute-done | bytes 65568 | tf_op jit(solution)/shard_map/ppermute | solution.py:20
  142.5 1.0 collective-permute-done.38
  143.5 1.8 %collective-permute-start.39 = (bf16[32,1024]{1,0:T(8,128)(2,1)S(1)}, bf16[32,1024]{1,0:T(8,128)(2,1)S(1)}, u32[]{:S(2)}, u32[]{:S(2)}) collective-permute-start(bf16[32,1024]{1,0:T(8,128)(2,1)S(1)} %get-tuple-element.6), channel_id=1, source_target_pairs={{0,6},{2,0},{4,2},{6,4},{1,7},{3,1},{5,3},{7,5},{8,14},{10,8},{12,... | collective-permute-start | bytes 196616 | tf_op jit(solution)/shard_map/ppermute | solution.py:20
  146.7 3.4 %collective-permute-done.40 = bf16[32,1024]{1,0:T(8,128)(2,1)S(1)} collective-permute-done((bf16[32,1024]{1,0:T(8,128)(2,1)S(1)}, bf16[32,1024]{1,0:T(8,128)(2,1)S(1)}, u32[]{:S(2)}, u32[]{:S(2)}) %collective-permute-start.40) | collective-permute-done | bytes 65568 | tf_op jit(solution)/shard_map/ppermute | solution.py:20
  151.0 1.5 fusion.39
  152.5 6.7 %collective-permute-start.42 = (bf16[128,2048]{1,0:T(8,128)(2,1)S(1)}, bf16[128,2048]{1,0:T(8,128)(2,1)S(1)}, u32[]{:S(2)}, u32[]{:S(2)}) collective-permute-start(bf16[128,2048]{1,0:T(8,128)(2,1)S(1)} %fusion.39), channel_id=1, source_target_pairs={{0,1},{1,0},{2,3},{3,2},{4,5},{5,4},{6,7},{7,6},{8,9},{9,8},{10,11... | collective-permute-start | bytes 1572872 | tf_op jit(solution)/shard_map/ppermute | solution.py:20
  160.1 4.4 %convert_bitcast_fusion = bf16[1,2048,1024]{2,1,0:T(8,128)(2,1)} fusion(bf16[384,1024]{1,0:T(8,128)(2,1)S(1)} %constant_dynamic-update-slice_fusion.12, bf16[128,2048]{1,0:T(8,128)(2,1)S(1)} %copy-done.7, bf16[128,2048]{1,0:T(8,128)(2,1)S(1)} %multiply_convert_fusion.4, bf16[128,2048]{1,0:T(8,128)(2,1)S(1)} %multiply_convert_fusion.5), kind=kOutput, calls=%fused_computation.24 | convolution fusion | flops 1617428480 | bytes 6553600 | tf_op jit(solution)/shard_map/dot_general | solution.py:57
  165.0 1.5 fusion.58
  166.6 1.1 collective-permute-start.43
  167.7 2.3 %collective-permute-start.45 = (bf16[32,1024]{1,0:T(8,128)(2,1)S(1)}, bf16[32,1024]{1,0:T(8,128)(2,1)S(1)}, u32[]{:S(2)}, u32[]{:S(2)}) collective-permute-start(bf16[32,1024]{1,0:T(8,128)(2,1)S(1)} %get-tuple-element.18), channel_id=1, source_target_pairs={{0,6},{2,0},{4,2},{6,4},{1,7},{3,1},{5,3},{7,5},{8,14},{10,8},{12,... | collective-permute-start | bytes 196616 | tf_op jit(solution)/shard_map/ppermute | solution.py:20
  169.9 4.4 %convert_bitcast_fusion.1 = bf16[1,1024,2048]{2,1,0:T(8,128)(2,1)} fusion(bf16[384,1024]{1,0:T(8,128)(2,1)S(1)} %constant_dynamic-update-slice_fusion, bf16[128,2048]{1,0:T(8,128)(2,1)S(1)} %copy-done.6, bf16[128,2048]{1,0:T(8,128)(2,1)S(1)} %multiply_convert_fusion.1, bf16[128,2048]{1,0:T(8,128)(2,1)S(1)} %multiply_convert_fusion), kind=kOutput, calls=%fused_computation.25 | convolution fusion | flops 1617428480 | bytes 6553600 | tf_op jit(solution)/shard_map/dot_general | solution.py:57
  174.3 1.7 collective-permute-done.44
  (142 shorter events, 23.5 us)
Async XLA Ops:
  0.6 18.6 %copy-start.8 = (bf16[1,3,32,1024]{3,2,1,0:T(8,128)(2,1)S(1)}, bf16[1,3,32,1024]{3,2,1,0:T(8,128)(2,1)}, u32[]{:S(2)}) copy-start(bf16[1,3,32,1024]{3,2,1,0:T(8,128)(2,1)} %param.7) | copy-start | bytes 589828
  0.6 14.1 %copy-start.25 = (s32[6]{0:T(128)S(1)}, s32[6]{0:T(128)}, u32[]{:S(2)}) copy-start(s32[6]{0:T(128)} %param.8) | copy-start | bytes 76
  2.2 5.0 %collective-permute-start.2 = (bf16[32,1024]{1,0:T(8,128)(2,1)S(1)}, bf16[32,1024]{1,0:T(8,128)(2,1)S(1)}, u32[]{:S(2)}, u32[]{:S(2)}) collective-permute-start(bf16[32,1024]{1,0:T(8,128)(2,1)S(1)} %get-tuple-element.36), channel_id=1, source_target_pairs={{0,2},{2,4},{4,6},{6,0},{1,3},{3,5},{5,7},{7,1},{8,10},{10,12},{12... | collective-permute-start | bytes 196616 | tf_op jit(solution)/shard_map/ppermute | solution.py:20
  3.5 6.6 %collective-permute-start.1 = (bf16[32,1024]{1,0:T(8,128)(2,1)S(1)}, bf16[32,1024]{1,0:T(8,128)(2,1)S(1)}, u32[]{:S(2)}, u32[]{:S(2)}) collective-permute-start(bf16[32,1024]{1,0:T(8,128)(2,1)S(1)} %get-tuple-element.36), channel_id=1, source_target_pairs={{0,4},{2,6},{4,0},{6,2},{1,5},{3,7},{5,1},{7,3},{8,12},{10,14},{12... | collective-permute-start | bytes 196616 | tf_op jit(solution)/shard_map/ppermute | solution.py:20
  5.8 4.3 %collective-permute-start = (bf16[32,1024]{1,0:T(8,128)(2,1)S(1)}, bf16[32,1024]{1,0:T(8,128)(2,1)S(1)}, u32[]{:S(2)}, u32[]{:S(2)}) collective-permute-start(bf16[32,1024]{1,0:T(8,128)(2,1)S(1)} %get-tuple-element.36), channel_id=1, source_target_pairs={{0,6},{2,0},{4,2},{6,4},{1,7},{3,1},{5,3},{7,5},{8,14},{10,8},{12,... | collective-permute-start | bytes 196616 | tf_op jit(solution)/shard_map/ppermute | solution.py:20
  13.0 6.3 %collective-permute-start.3 = (bf16[128,2048]{1,0:T(8,128)(2,1)S(1)}, bf16[128,2048]{1,0:T(8,128)(2,1)S(1)}, u32[]{:S(2)}, u32[]{:S(2)}) collective-permute-start(bf16[128,2048]{1,0:T(8,128)(2,1)S(1)} %fusion.24), channel_id=1, source_target_pairs={{0,1},{1,0},{2,3},{3,2},{4,5},{5,4},{6,7},{7,6},{8,9},{9,8},{10,11... | collective-permute-start | bytes 1572872 | tf_op jit(solution)/shard_map/ppermute | solution.py:20
  19.2 26.6 %copy-start.2 = (bf16[1,1024,2048]{2,1,0:T(8,128)(2,1)S(1)}, bf16[1,1024,2048]{2,1,0:T(8,128)(2,1)}, u32[]{:S(2)}) copy-start(bf16[1,1024,2048]{2,1,0:T(8,128)(2,1)} %param.11) | copy-start | bytes 12582916
  22.7 5.6 %collective-permute-start.4 = (bf16[32,1024]{1,0:T(8,128)(2,1)S(1)}, bf16[32,1024]{1,0:T(8,128)(2,1)S(1)}, u32[]{:S(2)}, u32[]{:S(2)}) collective-permute-start(bf16[32,1024]{1,0:T(8,128)(2,1)S(1)} %get-tuple-element.32), channel_id=1, source_target_pairs={{0,2},{2,4},{4,6},{6,0},{1,3},{3,5},{5,7},{7,1},{8,10},{10,12},{12... | collective-permute-start | bytes 196616 | tf_op jit(solution)/shard_map/ppermute | solution.py:20
  24.0 4.7 %collective-permute-start.6 = (bf16[32,1024]{1,0:T(8,128)(2,1)S(1)}, bf16[32,1024]{1,0:T(8,128)(2,1)S(1)}, u32[]{:S(2)}, u32[]{:S(2)}) collective-permute-start(bf16[32,1024]{1,0:T(8,128)(2,1)S(1)} %get-tuple-element.33), channel_id=1, source_target_pairs={{0,6},{2,0},{4,2},{6,4},{1,7},{3,1},{5,3},{7,5},{8,14},{10,8},{12,... | collective-permute-start | bytes 196616 | tf_op jit(solution)/shard_map/ppermute | solution.py:20
  26.0 6.0 %collective-permute-start.5 = (bf16[32,1024]{1,0:T(8,128)(2,1)S(1)}, bf16[32,1024]{1,0:T(8,128)(2,1)S(1)}, u32[]{:S(2)}, u32[]{:S(2)}) collective-permute-start(bf16[32,1024]{1,0:T(8,128)(2,1)S(1)} %get-tuple-element.34), channel_id=1, source_target_pairs={{0,4},{2,6},{4,0},{6,2},{1,5},{3,7},{5,1},{7,3},{8,12},{10,14},{12... | collective-permute-start | bytes 196616 | tf_op jit(solution)/shard_map/ppermute | solution.py:20
  33.6 5.0 %collective-permute-start.7 = (bf16[32,1024]{1,0:T(8,128)(2,1)S(1)}, bf16[32,1024]{1,0:T(8,128)(2,1)S(1)}, u32[]{:S(2)}, u32[]{:S(2)}) collective-permute-start(bf16[32,1024]{1,0:T(8,128)(2,1)S(1)} %get-tuple-element.13), channel_id=1, source_target_pairs={{0,8},{8,16},{16,24},{1,9},{9,17},{17,25},{2,10},{10,18},{18,26},{... | collective-permute-start | bytes 196616 | tf_op jit(solution)/shard_map/ppermute | solution.py:15
  39.5 5.1 %collective-permute-start.10 = (bf16[32,1024]{1,0:T(8,128)(2,1)S(1)}, bf16[32,1024]{1,0:T(8,128)(2,1)S(1)}, u32[]{:S(2)}, u32[]{:S(2)}) collective-permute-start(bf16[32,1024]{1,0:T(8,128)(2,1)S(1)} %get-tuple-element.10), channel_id=1, source_target_pairs={{0,2},{2,4},{4,6},{6,0},{1,3},{3,5},{5,7},{7,1},{8,10},{10,12},{12... | collective-permute-start | bytes 196616 | tf_op jit(solution)/shard_map/ppermute | solution.py:20
  39.6 5.9 %collective-permute-start.9 = (bf16[32,1024]{1,0:T(8,128)(2,1)S(1)}, bf16[32,1024]{1,0:T(8,128)(2,1)S(1)}, u32[]{:S(2)}, u32[]{:S(2)}) collective-permute-start(bf16[32,1024]{1,0:T(8,128)(2,1)S(1)} %get-tuple-element.10), channel_id=1, source_target_pairs={{0,4},{2,6},{4,0},{6,2},{1,5},{3,7},{5,1},{7,3},{8,12},{10,14},{12... | collective-permute-start | bytes 196616 | tf_op jit(solution)/shard_map/ppermute | solution.py:20
  42.3 3.5 %collective-permute-start.8 = (bf16[32,1024]{1,0:T(8,128)(2,1)S(1)}, bf16[32,1024]{1,0:T(8,128)(2,1)S(1)}, u32[]{:S(2)}, u32[]{:S(2)}) collective-permute-start(bf16[32,1024]{1,0:T(8,128)(2,1)S(1)} %get-tuple-element.10), channel_id=1, source_target_pairs={{0,6},{2,0},{4,2},{6,4},{1,7},{3,1},{5,3},{7,5},{8,14},{10,8},{12,... | collective-permute-start | bytes 196616 | tf_op jit(solution)/shard_map/ppermute | solution.py:20
  45.5 11.1 %copy-start.19 = (bf16[32,1024]{1,0:T(8,128)(2,1)}, bf16[32,1024]{1,0:T(8,128)(2,1)S(1)}, u32[]{:S(2)}) copy-start(bf16[32,1024]{1,0:T(8,128)(2,1)S(1)} %collective-permute-done.9) | copy-start | bytes 196612
  46.6 10.0 %collective-permute-start.11 = (bf16[128,2048]{1,0:T(8,128)(2,1)S(1)}, bf16[128,2048]{1,0:T(8,128)(2,1)S(1)}, u32[]{:S(2)}, u32[]{:S(2)}) collective-permute-start(bf16[128,2048]{1,0:T(8,128)(2,1)S(1)} %fusion.27), channel_id=1, source_target_pairs={{0,1},{1,0},{2,3},{3,2},{4,5},{5,4},{6,7},{7,6},{8,9},{9,8},{10,11... | collective-permute-start | bytes 1572872 | tf_op jit(solution)/shard_map/ppermute | solution.py:20
  51.4 25.4 %collective-permute-start.25 = (bf16[32,1024]{1,0:T(8,128)(2,1)}, bf16[32,1024]{1,0:T(8,128)(2,1)S(1)}, u32[]{:S(2)}, u32[]{:S(2)}) collective-permute-start(bf16[32,1024]{1,0:T(8,128)(2,1)} %slice_bitcast_fusion), channel_id=1, source_target_pairs={{0,2},{2,4},{4,6},{6,0},{1,3},{3,5},{5,7},{7,1},{8,10},{10,12},{12... | collective-permute-start | bytes 196616 | tf_op jit(solution)/shard_map/ppermute | solution.py:20
  52.2 27.1 %collective-permute-start.24 = (bf16[32,1024]{1,0:T(8,128)(2,1)}, bf16[32,1024]{1,0:T(8,128)(2,1)}, u32[]{:S(2)}, u32[]{:S(2)}) collective-permute-start(bf16[32,1024]{1,0:T(8,128)(2,1)} %slice_bitcast_fusion), channel_id=1, source_target_pairs={{0,4},{2,6},{4,0},{6,2},{1,5},{3,7},{5,1},{7,3},{8,12},{10,14},{12... | collective-permute-start | bytes 196616 | tf_op jit(solution)/shard_map/ppermute | solution.py:20
  55.9 23.5 %copy-start = (bf16[1,2048,1024]{2,1,0:T(8,128)(2,1)S(1)}, bf16[1,2048,1024]{2,1,0:T(8,128)(2,1)}, u32[]{:S(2)}) copy-start(bf16[1,2048,1024]{2,1,0:T(8,128)(2,1)} %param.12) | copy-start | bytes 12582916
  59.9 26.2 %copy-start.3 = (bf16[1,1024,2048]{2,1,0:T(8,128)(2,1)S(1)}, bf16[1,1024,2048]{2,1,0:T(8,128)(2,1)}, u32[]{:S(2)}) copy-start(bf16[1,1024,2048]{2,1,0:T(8,128)(2,1)} %param.11) | copy-start | bytes 12582916
  59.9 5.1 %collective-permute-start.12 = (bf16[32,1024]{1,0:T(8,128)(2,1)S(1)}, bf16[32,1024]{1,0:T(8,128)(2,1)S(1)}, u32[]{:S(2)}, u32[]{:S(2)}) collective-permute-start(bf16[32,1024]{1,0:T(8,128)(2,1)S(1)} %get-tuple-element.29), channel_id=1, source_target_pairs={{0,2},{2,4},{4,6},{6,0},{1,3},{3,5},{5,7},{7,1},{8,10},{10,12},{12... | collective-permute-start | bytes 196616 | tf_op jit(solution)/shard_map/ppermute | solution.py:20
  60.6 4.4 %collective-permute-start.14 = (bf16[32,1024]{1,0:T(8,128)(2,1)S(1)}, bf16[32,1024]{1,0:T(8,128)(2,1)S(1)}, u32[]{:S(2)}, u32[]{:S(2)}) collective-permute-start(bf16[32,1024]{1,0:T(8,128)(2,1)S(1)} %get-tuple-element.30), channel_id=1, source_target_pairs={{0,6},{2,0},{4,2},{6,4},{1,7},{3,1},{5,3},{7,5},{8,14},{10,8},{12,... | collective-permute-start | bytes 196616 | tf_op jit(solution)/shard_map/ppermute | solution.py:20
  63.2 4.5 %collective-permute-start.13 = (bf16[32,1024]{1,0:T(8,128)(2,1)S(1)}, bf16[32,1024]{1,0:T(8,128)(2,1)S(1)}, u32[]{:S(2)}, u32[]{:S(2)}) collective-permute-start(bf16[32,1024]{1,0:T(8,128)(2,1)S(1)} %get-tuple-element.31), channel_id=1, source_target_pairs={{0,4},{2,6},{4,0},{6,2},{1,5},{3,7},{5,1},{7,3},{8,12},{10,14},{12... | collective-permute-start | bytes 196616 | tf_op jit(solution)/shard_map/ppermute | solution.py:20
  65.1 14.3 %collective-permute-start.23 = (bf16[32,1024]{1,0:T(8,128)(2,1)}, bf16[32,1024]{1,0:T(8,128)(2,1)S(1)}, u32[]{:S(2)}, u32[]{:S(2)}) collective-permute-start(bf16[32,1024]{1,0:T(8,128)(2,1)} %slice_bitcast_fusion), channel_id=1, source_target_pairs={{0,6},{2,0},{4,2},{6,4},{1,7},{3,1},{5,3},{7,5},{8,14},{10,8},{12,... | collective-permute-start | bytes 196616 | tf_op jit(solution)/shard_map/ppermute | solution.py:20
  69.2 5.3 %collective-permute-start.15 = (bf16[32,1024]{1,0:T(8,128)(2,1)S(1)}, bf16[32,1024]{1,0:T(8,128)(2,1)S(1)}, u32[]{:S(2)}, u32[]{:S(2)}) collective-permute-start(bf16[32,1024]{1,0:T(8,128)(2,1)S(1)} %get-tuple-element.11), channel_id=1, source_target_pairs={{0,8},{8,16},{16,24},{1,9},{9,17},{17,25},{2,10},{10,18},{18,26},{... | collective-permute-start | bytes 196616 | tf_op jit(solution)/shard_map/ppermute | solution.py:15
  76.0 10.0 %collective-permute-start.18 = (bf16[32,1024]{1,0:T(8,128)(2,1)S(1)}, bf16[32,1024]{1,0:T(8,128)(2,1)S(1)}, u32[]{:S(2)}, u32[]{:S(2)}) collective-permute-start(bf16[32,1024]{1,0:T(8,128)(2,1)S(1)} %get-tuple-element.8), channel_id=1, source_target_pairs={{0,2},{2,4},{4,6},{6,0},{1,3},{3,5},{5,7},{7,1},{8,10},{10,12},{12... | collective-permute-start | bytes 196616 | tf_op jit(solution)/shard_map/ppermute | solution.py:20
  76.0 10.0 %collective-permute-start.17 = (bf16[32,1024]{1,0:T(8,128)(2,1)S(1)}, bf16[32,1024]{1,0:T(8,128)(2,1)S(1)}, u32[]{:S(2)}, u32[]{:S(2)}) collective-permute-start(bf16[32,1024]{1,0:T(8,128)(2,1)S(1)} %get-tuple-element.8), channel_id=1, source_target_pairs={{0,4},{2,6},{4,0},{6,2},{1,5},{3,7},{5,1},{7,3},{8,12},{10,14},{12... | collective-permute-start | bytes 196616 | tf_op jit(solution)/shard_map/ppermute | solution.py:20
  76.8 10.1 %copy-start.10 = (bf16[32,1024]{1,0:T(8,128)(2,1)}, bf16[32,1024]{1,0:T(8,128)(2,1)S(1)}, u32[]{:S(2)}) copy-start(bf16[32,1024]{1,0:T(8,128)(2,1)S(1)} %collective-permute-done.25) | copy-start | bytes 196612
  76.8 9.3 %collective-permute-start.16 = (bf16[32,1024]{1,0:T(8,128)(2,1)S(1)}, bf16[32,1024]{1,0:T(8,128)(2,1)S(1)}, u32[]{:S(2)}, u32[]{:S(2)}) collective-permute-start(bf16[32,1024]{1,0:T(8,128)(2,1)S(1)} %get-tuple-element.8), channel_id=1, source_target_pairs={{0,6},{2,0},{4,2},{6,4},{1,7},{3,1},{5,3},{7,5},{8,14},{10,8},{12,... | collective-permute-start | bytes 196616 | tf_op jit(solution)/shard_map/ppermute | solution.py:20
  79.4 7.5 %copy-start.12 = (bf16[32,1024]{1,0:T(8,128)(2,1)}, bf16[32,1024]{1,0:T(8,128)(2,1)S(1)}, u32[]{:S(2)}) copy-start(bf16[32,1024]{1,0:T(8,128)(2,1)S(1)} %collective-permute-done.23) | copy-start | bytes 196612
  81.8 5.8 %collective-permute-start.26 = (bf16[128,2048]{1,0:T(8,128)(2,1)S(1)}, bf16[128,2048]{1,0:T(8,128)(2,1)S(1)}, u32[]{:S(2)}, u32[]{:S(2)}) collective-permute-start(bf16[128,2048]{1,0:T(8,128)(2,1)S(1)} %fusion.33), channel_id=1, source_target_pairs={{0,1},{1,0},{2,3},{3,2},{4,5},{5,4},{6,7},{7,6},{8,9},{9,8},{10,11... | collective-permute-start | bytes 1572872 | tf_op jit(solution)/shard_map/ppermute | solution.py:20
  86.9 2.1 %collective-permute-start.19 = (bf16[128,2048]{1,0:T(8,128)(2,1)S(1)}, bf16[128,2048]{1,0:T(8,128)(2,1)S(1)}, u32[]{:S(2)}, u32[]{:S(2)}) collective-permute-start(bf16[128,2048]{1,0:T(8,128)(2,1)S(1)} %fusion.30), channel_id=1, source_target_pairs={{0,1},{1,0},{2,3},{3,2},{4,5},{5,4},{6,7},{7,6},{8,9},{9,8},{10,11... | collective-permute-start | bytes 1572872 | tf_op jit(solution)/shard_map/ppermute | solution.py:20
  92.6 5.4 %collective-permute-start.27 = (bf16[32,1024]{1,0:T(8,128)(2,1)}, bf16[32,1024]{1,0:T(8,128)(2,1)}, u32[]{:S(2)}, u32[]{:S(2)}) collective-permute-start(bf16[32,1024]{1,0:T(8,128)(2,1)} %get-tuple-element.23), channel_id=1, source_target_pairs={{0,2},{2,4},{4,6},{6,0},{1,3},{3,5},{5,7},{7,1},{8,10},{10,12},{12... | collective-permute-start | bytes 196616 | tf_op jit(solution)/shard_map/ppermute | solution.py:20
  94.0 5.2 %collective-permute-start.29 = (bf16[32,1024]{1,0:T(8,128)(2,1)}, bf16[32,1024]{1,0:T(8,128)(2,1)}, u32[]{:S(2)}, u32[]{:S(2)}) collective-permute-start(bf16[32,1024]{1,0:T(8,128)(2,1)} %get-tuple-element.24), channel_id=1, source_target_pairs={{0,6},{2,0},{4,2},{6,4},{1,7},{3,1},{5,3},{7,5},{8,14},{10,8},{12,... | collective-permute-start | bytes 196616 | tf_op jit(solution)/shard_map/ppermute | solution.py:20
  95.9 6.9 %collective-permute-start.28 = (bf16[32,1024]{1,0:T(8,128)(2,1)}, bf16[32,1024]{1,0:T(8,128)(2,1)}, u32[]{:S(2)}, u32[]{:S(2)}) collective-permute-start(bf16[32,1024]{1,0:T(8,128)(2,1)} %get-tuple-element.25), channel_id=1, source_target_pairs={{0,4},{2,6},{4,0},{6,2},{1,5},{3,7},{5,1},{7,3},{8,12},{10,14},{12... | collective-permute-start | bytes 196616 | tf_op jit(solution)/shard_map/ppermute | solution.py:20
  95.9 28.4 %copy-start.17 = (bf16[32,1024]{1,0:T(8,128)(2,1)S(1)}, bf16[32,1024]{1,0:T(8,128)(2,1)}, u32[]{:S(2)}) copy-start(bf16[32,1024]{1,0:T(8,128)(2,1)} %copy-done.16) | copy-start | bytes 196612
  95.9 28.4 %copy-start.15 = (bf16[32,1024]{1,0:T(8,128)(2,1)S(1)}, bf16[32,1024]{1,0:T(8,128)(2,1)}, u32[]{:S(2)}) copy-start(bf16[32,1024]{1,0:T(8,128)(2,1)} %copy-done.14) | copy-start | bytes 196612
  95.9 28.4 %copy-start.1 = (bf16[1,2048,1024]{2,1,0:T(8,128)(2,1)S(1)}, bf16[1,2048,1024]{2,1,0:T(8,128)(2,1)}, u32[]{:S(2)}) copy-start(bf16[1,2048,1024]{2,1,0:T(8,128)(2,1)} %param.12) | copy-start | bytes 12582916
  95.9 28.4 %copy-start.7 = (bf16[128,2048]{1,0:T(8,128)(2,1)S(1)}, bf16[128,2048]{1,0:T(8,128)(2,1)}, u32[]{:S(2)}) copy-start(bf16[128,2048]{1,0:T(8,128)(2,1)} %get-tuple-element.16) | copy-start | bytes 1572868
  103.8 6.5 %collective-permute-start.30 = (bf16[32,1024]{1,0:T(8,128)(2,1)S(1)}, bf16[32,1024]{1,0:T(8,128)(2,1)S(1)}, u32[]{:S(2)}, u32[]{:S(2)}) collective-permute-start(bf16[32,1024]{1,0:T(8,128)(2,1)S(1)} %add_convert_fusion.2), channel_id=1, source_target_pairs={{8,0},{16,8},{24,16},{9,1},{17,9},{25,17},{10,2},{18,10},{26,18},{... | collective-permute-start | bytes 196616 | tf_op jit(solution)/shard_map/ppermute | solution.py:15
  111.2 5.1 %collective-permute-start.33 = (bf16[32,1024]{1,0:T(8,128)(2,1)S(1)}, bf16[32,1024]{1,0:T(8,128)(2,1)S(1)}, u32[]{:S(2)}, u32[]{:S(2)}) collective-permute-start(bf16[32,1024]{1,0:T(8,128)(2,1)S(1)} %bitcast_select_fusion), channel_id=1, source_target_pairs={{0,2},{2,4},{4,6},{6,0},{1,3},{3,5},{5,7},{7,1},{8,10},{10,12},{12... | collective-permute-start | bytes 196616 | tf_op jit(solution)/shard_map/ppermute | solution.py:20
  111.2 5.9 %collective-permute-start.32 = (bf16[32,1024]{1,0:T(8,128)(2,1)S(1)}, bf16[32,1024]{1,0:T(8,128)(2,1)S(1)}, u32[]{:S(2)}, u32[]{:S(2)}) collective-permute-start(bf16[32,1024]{1,0:T(8,128)(2,1)S(1)} %bitcast_select_fusion), channel_id=1, source_target_pairs={{0,4},{2,6},{4,0},{6,2},{1,5},{3,7},{5,1},{7,3},{8,12},{10,14},{12... | collective-permute-start | bytes 196616 | tf_op jit(solution)/shard_map/ppermute | solution.py:20
  113.9 3.6 %collective-permute-start.31 = (bf16[32,1024]{1,0:T(8,128)(2,1)S(1)}, bf16[32,1024]{1,0:T(8,128)(2,1)S(1)}, u32[]{:S(2)}, u32[]{:S(2)}) collective-permute-start(bf16[32,1024]{1,0:T(8,128)(2,1)S(1)} %bitcast_select_fusion), channel_id=1, source_target_pairs={{0,6},{2,0},{4,2},{6,4},{1,7},{3,1},{5,3},{7,5},{8,14},{10,8},{12,... | collective-permute-start | bytes 196616 | tf_op jit(solution)/shard_map/ppermute | solution.py:20
  115.9 8.3 %copy-start.24 = (bf16[384,1024]{1,0:T(8,128)(2,1)S(1)}, bf16[384,1024]{1,0:T(8,128)(2,1)}, u32[]{:S(2)}) copy-start(bf16[384,1024]{1,0:T(8,128)(2,1)} %constant_dynamic-update-slice_fusion.2) | copy-start | bytes 2359300
  121.2 4.6 %collective-permute-start.34 = (bf16[128,2048]{1,0:T(8,128)(2,1)S(1)}, bf16[128,2048]{1,0:T(8,128)(2,1)S(1)}, u32[]{:S(2)}, u32[]{:S(2)}) collective-permute-start(bf16[128,2048]{1,0:T(8,128)(2,1)S(1)} %fusion.36), channel_id=1, source_target_pairs={{0,1},{1,0},{2,3},{3,2},{4,5},{5,4},{6,7},{7,6},{8,9},{9,8},{10,11... | collective-permute-start | bytes 1572872 | tf_op jit(solution)/shard_map/ppermute | solution.py:20
  125.1 18.4 %copy-start.9 = (bf16[1,3,32,1024]{3,2,1,0:T(8,128)(2,1)S(1)}, bf16[1,3,32,1024]{3,2,1,0:T(8,128)(2,1)}, u32[]{:S(2)}) copy-start(bf16[1,3,32,1024]{3,2,1,0:T(8,128)(2,1)} %param.13) | copy-start | bytes 589828
  125.1 20.2 %copy-start.21 = (bf16[32,1024]{1,0:T(8,128)(2,1)S(1)}, bf16[32,1024]{1,0:T(8,128)(2,1)}, u32[]{:S(2)}) copy-start(bf16[32,1024]{1,0:T(8,128)(2,1)} %get-tuple-element.14) | copy-start | bytes 196612
  125.1 20.2 %copy-start.22 = (bf16[32,1024]{1,0:T(8,128)(2,1)S(1)}, bf16[32,1024]{1,0:T(8,128)(2,1)}, u32[]{:S(2)}) copy-start(bf16[32,1024]{1,0:T(8,128)(2,1)} %get-tuple-element.12) | copy-start | bytes 196612
  127.9 31.3 %copy-start.13 = (bf16[32,1024]{1,0:T(8,128)(2,1)S(1)}, bf16[32,1024]{1,0:T(8,128)(2,1)}, u32[]{:S(2)}) copy-start(bf16[32,1024]{1,0:T(8,128)(2,1)} %copy-done.12) | copy-start | bytes 196612
  127.9 32.2 %copy-start.11 = (bf16[32,1024]{1,0:T(8,128)(2,1)S(1)}, bf16[32,1024]{1,0:T(8,128)(2,1)}, u32[]{:S(2)}) copy-start(bf16[32,1024]{1,0:T(8,128)(2,1)} %copy-done.10) | copy-start | bytes 196612
  127.9 6.7 %collective-permute-start.35 = (bf16[32,1024]{1,0:T(8,128)(2,1)S(1)}, bf16[32,1024]{1,0:T(8,128)(2,1)S(1)}, u32[]{:S(2)}, u32[]{:S(2)}) collective-permute-start(bf16[32,1024]{1,0:T(8,128)(2,1)S(1)} %get-tuple-element.20), channel_id=1, source_target_pairs={{0,2},{2,4},{4,6},{6,0},{1,3},{3,5},{5,7},{7,1},{8,10},{10,12},{12... | collective-permute-start | bytes 196616 | tf_op jit(solution)/shard_map/ppermute | solution.py:20
  129.0 6.2 %collective-permute-start.37 = (bf16[32,1024]{1,0:T(8,128)(2,1)S(1)}, bf16[32,1024]{1,0:T(8,128)(2,1)S(1)}, u32[]{:S(2)}, u32[]{:S(2)}) collective-permute-start(bf16[32,1024]{1,0:T(8,128)(2,1)S(1)} %get-tuple-element.21), channel_id=1, source_target_pairs={{0,6},{2,0},{4,2},{6,4},{1,7},{3,1},{5,3},{7,5},{8,14},{10,8},{12,... | collective-permute-start | bytes 196616 | tf_op jit(solution)/shard_map/ppermute | solution.py:20
  131.2 6.2 %collective-permute-start.36 = (bf16[32,1024]{1,0:T(8,128)(2,1)S(1)}, bf16[32,1024]{1,0:T(8,128)(2,1)S(1)}, u32[]{:S(2)}, u32[]{:S(2)}) collective-permute-start(bf16[32,1024]{1,0:T(8,128)(2,1)S(1)} %get-tuple-element.22), channel_id=1, source_target_pairs={{0,4},{2,6},{4,0},{6,2},{1,5},{3,7},{5,1},{7,3},{8,12},{10,14},{12... | collective-permute-start | bytes 196616 | tf_op jit(solution)/shard_map/ppermute | solution.py:20
  131.3 8.2 %collective-permute-start.20 = (bf16[32,1024]{1,0:T(8,128)(2,1)S(1)}, bf16[32,1024]{1,0:T(8,128)(2,1)S(1)}, u32[]{:S(2)}, u32[]{:S(2)}) collective-permute-start(bf16[32,1024]{1,0:T(8,128)(2,1)S(1)} %get-tuple-element.26), channel_id=1, source_target_pairs={{0,2},{2,4},{4,6},{6,0},{1,3},{3,5},{5,7},{7,1},{8,10},{10,12},{12... | collective-permute-start | bytes 196616 | tf_op jit(solution)/shard_map/ppermute | solution.py:20
  132.0 7.5 %collective-permute-start.22 = (bf16[32,1024]{1,0:T(8,128)(2,1)S(1)}, bf16[32,1024]{1,0:T(8,128)(2,1)S(1)}, u32[]{:S(2)}, u32[]{:S(2)}) collective-permute-start(bf16[32,1024]{1,0:T(8,128)(2,1)S(1)} %get-tuple-element.27), channel_id=1, source_target_pairs={{0,6},{2,0},{4,2},{6,4},{1,7},{3,1},{5,3},{7,5},{8,14},{10,8},{12,... | collective-permute-start | bytes 196616 | tf_op jit(solution)/shard_map/ppermute | solution.py:20
  134.6 7.8 %collective-permute-start.21 = (bf16[32,1024]{1,0:T(8,128)(2,1)S(1)}, bf16[32,1024]{1,0:T(8,128)(2,1)S(1)}, u32[]{:S(2)}, u32[]{:S(2)}) collective-permute-start(bf16[32,1024]{1,0:T(8,128)(2,1)S(1)} %get-tuple-element.28), channel_id=1, source_target_pairs={{0,4},{2,6},{4,0},{6,2},{1,5},{3,7},{5,1},{7,3},{8,12},{10,14},{12... | collective-permute-start | bytes 196616 | tf_op jit(solution)/shard_map/ppermute | solution.py:20
  137.5 5.9 %collective-permute-start.38 = (bf16[32,1024]{1,0:T(8,128)(2,1)S(1)}, bf16[32,1024]{1,0:T(8,128)(2,1)S(1)}, u32[]{:S(2)}, u32[]{:S(2)}) collective-permute-start(bf16[32,1024]{1,0:T(8,128)(2,1)S(1)} %add_convert_fusion.1), channel_id=1, source_target_pairs={{8,0},{16,8},{24,16},{9,1},{17,9},{25,17},{10,2},{18,10},{26,18},{... | collective-permute-start | bytes 196616 | tf_op jit(solution)/shard_map/ppermute | solution.py:15
  143.5 3.2 %collective-permute-start.39 = (bf16[32,1024]{1,0:T(8,128)(2,1)S(1)}, bf16[32,1024]{1,0:T(8,128)(2,1)S(1)}, u32[]{:S(2)}, u32[]{:S(2)}) collective-permute-start(bf16[32,1024]{1,0:T(8,128)(2,1)S(1)} %get-tuple-element.6), channel_id=1, source_target_pairs={{0,6},{2,0},{4,2},{6,4},{1,7},{3,1},{5,3},{7,5},{8,14},{10,8},{12,... | collective-permute-start | bytes 196616 | tf_op jit(solution)/shard_map/ppermute | solution.py:20
  146.0 4.9 %collective-permute-start.41 = (bf16[32,1024]{1,0:T(8,128)(2,1)S(1)}, bf16[32,1024]{1,0:T(8,128)(2,1)S(1)}, u32[]{:S(2)}, u32[]{:S(2)}) collective-permute-start(bf16[32,1024]{1,0:T(8,128)(2,1)S(1)} %get-tuple-element.6), channel_id=1, source_target_pairs={{0,2},{2,4},{4,6},{6,0},{1,3},{3,5},{5,7},{7,1},{8,10},{10,12},{12... | collective-permute-start | bytes 196616 | tf_op jit(solution)/shard_map/ppermute | solution.py:20
  146.0 4.0 %collective-permute-start.40 = (bf16[32,1024]{1,0:T(8,128)(2,1)S(1)}, bf16[32,1024]{1,0:T(8,128)(2,1)S(1)}, u32[]{:S(2)}, u32[]{:S(2)}) collective-permute-start(bf16[32,1024]{1,0:T(8,128)(2,1)S(1)} %get-tuple-element.6), channel_id=1, source_target_pairs={{0,4},{2,6},{4,0},{6,2},{1,5},{3,7},{5,1},{7,3},{8,12},{10,14},{12... | collective-permute-start | bytes 196616 | tf_op jit(solution)/shard_map/ppermute | solution.py:20
  152.5 12.0 %collective-permute-start.42 = (bf16[128,2048]{1,0:T(8,128)(2,1)S(1)}, bf16[128,2048]{1,0:T(8,128)(2,1)S(1)}, u32[]{:S(2)}, u32[]{:S(2)}) collective-permute-start(bf16[128,2048]{1,0:T(8,128)(2,1)S(1)} %fusion.39), channel_id=1, source_target_pairs={{0,1},{1,0},{2,3},{3,2},{4,5},{5,4},{6,7},{7,6},{8,9},{9,8},{10,11... | collective-permute-start | bytes 1572872 | tf_op jit(solution)/shard_map/ppermute | solution.py:20
  166.6 7.7 %collective-permute-start.43 = (bf16[32,1024]{1,0:T(8,128)(2,1)S(1)}, bf16[32,1024]{1,0:T(8,128)(2,1)S(1)}, u32[]{:S(2)}, u32[]{:S(2)}) collective-permute-start(bf16[32,1024]{1,0:T(8,128)(2,1)S(1)} %get-tuple-element.17), channel_id=1, source_target_pairs={{0,2},{2,4},{4,6},{6,0},{1,3},{3,5},{5,7},{7,1},{8,10},{10,12},{12... | collective-permute-start | bytes 196616 | tf_op jit(solution)/shard_map/ppermute | solution.py:20
  167.7 6.7 %collective-permute-start.45 = (bf16[32,1024]{1,0:T(8,128)(2,1)S(1)}, bf16[32,1024]{1,0:T(8,128)(2,1)S(1)}, u32[]{:S(2)}, u32[]{:S(2)}) collective-permute-start(bf16[32,1024]{1,0:T(8,128)(2,1)S(1)} %get-tuple-element.18), channel_id=1, source_target_pairs={{0,6},{2,0},{4,2},{6,4},{1,7},{3,1},{5,3},{7,5},{8,14},{10,8},{12,... | collective-permute-start | bytes 196616 | tf_op jit(solution)/shard_map/ppermute | solution.py:20
  169.9 6.1 %collective-permute-start.44 = (bf16[32,1024]{1,0:T(8,128)(2,1)S(1)}, bf16[32,1024]{1,0:T(8,128)(2,1)S(1)}, u32[]{:S(2)}, u32[]{:S(2)}) collective-permute-start(bf16[32,1024]{1,0:T(8,128)(2,1)S(1)} %get-tuple-element.19), channel_id=1, source_target_pairs={{0,4},{2,6},{4,0},{6,2},{1,5},{3,7},{5,1},{7,3},{8,12},{10,14},{12... | collective-permute-start | bytes 196616 | tf_op jit(solution)/shard_map/ppermute | solution.py:20
  (8 other events, 38.2 us)

commit v2 on v1

--- a/solution.py
+++ b/solution.py
@@ -22,16 +22,15 @@
 
 def gather_rows(block):
     size = lax.axis_size("row")
-    return jnp.concatenate([block] + [turn(block, "row", -j) for j in range(1, size)], axis=0)
+    copies = jnp.broadcast_to(block[None], (size,) + block.shape)
+    full = lax.all_to_all(copies, "row", 0, 0)
+    return full.reshape((size * block.shape[0],) + block.shape[1:])
 
 
 def scatter_rows(partial):
     size = lax.axis_size("row")
-    pieces = jnp.split(partial, size, axis=0)
-    total = pieces[0].astype(F32)
-    for j in range(1, size):
-        total = total + turn(pieces[j], "row", j).astype(F32)
-    return total
+    pieces = partial.reshape((size, partial.shape[0] // size) + partial.shape[1:])
+    return lax.all_to_all(pieces, "row", 0, 0).astype(F32).sum(axis=0)
 
 
 def sum_cols(partial):

time: 178 us -> 217 us (1.22)
  blocking collectives: 0 us -> 40.8 us
  matrix products: 32.2 us -> 44.8 us
  waiting for transfers between devices: 44.8 us -> 33.3 us
  starting transfers between devices: 70.8 us -> 64 us
  other arithmetic: 13.4 us -> 16.2 us
    all_to_all x0 -> x4, blocking collectives: none -> 40.8 us  [the longest x3 30.8 us: gather_rows(): full = lax.all_to_all(copies, 'row', 0, 0)]
    ppermute x42 -> x6, starting transfers between devices: 59.8 us -> 22.7 us  [turn(): lax.ppermute(block, axis, [(i, (i + distance) % size) for i in range(size)])]
    ppermute x42 -> x6, waiting for transfers between devices: 38.3 us -> 6.91 us  [turn(): lax.ppermute(block, axis, [(i, (i + distance) % size) for i in range(size)])]
    all_to_all x0 -> x8, starting transfers between devices: none -> 30.6 us  [the longest x5 18.1 us: scatter_rows(): return lax.all_to_all(pieces, 'row', 0, 0).astype(F32).sum(axis=0)]
    all_to_all x0 -> x8, waiting for transfers between devices: none -> 18.1 us  [the longest x5 14.1 us: scatter_rows(): return lax.all_to_all(pieces, 'row', 0, 0).astype(F32).sum(axis=0)]
    dot_general x14, matrix products: 32.2 us -> 44.8 us  [matmul(): return lax.dot_general(a, b, dims, preferred_element_type=F32)]
    broadcast_in_dim x0 -> x6, local copies, waits for them, and re-layouts: none -> 4 us  [gather_rows(): copies = jnp.broadcast_to(block[None], (size,) + block.shape)]
    unnamed x71 -> x62, local copies, waits for them, and re-layouts: 4.43 us -> 0.76 us
  transfers between devices with their start and end apart: 46 -> 18, of which waited for: 29 -> 11; matrix products, arithmetic and copies ran while one was open for 16% -> 14% of each run, Pallas kernels for 0% -> 0%
where the time goes in v2:
time: 217 us; the launch traced here: 215 us
  starting transfers between devices  64 us (29%)
  matrix products  44.8 us (21%)
  blocking collectives  40.8 us (19%)
  waiting for transfers between devices  33.3 us (15%)
  other arithmetic  16.2 us (7%)
  local copies, waits for them, and re-layouts  8.53 us (4%)
  between operations  6.98 us (3%)
    dot_general x14, matrix products, matmul(): return lax.dot_general(a, b, dims, preferred_element_type=F32)  44.8 us
    all_to_all x3, blocking collectives, gather_rows(): full = lax.all_to_all(copies, 'row', 0, 0)  30.8 us
    ppermute x6, starting transfers between devices, turn(): lax.ppermute(block, axis, [(i, (i + distance) % size) for i in range(size)])  22.7 us
    all_to_all x5, starting transfers between devices, scatter_rows(): return lax.all_to_all(pieces, 'row', 0, 0).astype(F32).sum(axis=0)  18.1 us
    all_to_all x5, waiting for transfers between devices, scatter_rows(): return lax.all_to_all(pieces, 'row', 0, 0).astype(F32).sum(axis=0)  14.1 us
    all_to_all x3, starting transfers between devices, gather_rows(): full = lax.all_to_all(copies, 'row', 0, 0)  12.5 us
    ppermute x4, starting transfers between devices, from_behind(): return lax.ppermute(block, axis, route)  10.7 us
    all_to_all x1, blocking collectives, scatter_rows(): return lax.all_to_all(pieces, 'row', 0, 0).astype(F32).sum(axis=0)  9.97 us
  transfers between devices with their start and end apart: 18, of which 11 were waited for; matrix products, arithmetic and copies ran while one was open for 14% of the time, Pallas kernels for 0%

profile of v2, /device:TPU:3, one launch (start us, length us, event | category | flops | bytes accessed | tf_op | source)
XLA Modules:
  0.0 214.6 jit_solution(7857928495688921385)
XLA Ops:
  0.6 1.6 slice_bitcast_fusion.2
  2.3 11.3 %all_to_all.60 = bf16[4,32,1024]{2,1,0:T(8,128)(2,1)S(1)} all-to-all(bf16[4,32,1024]{2,1,0:T(8,128)(2,1)S(1)} %broadcast_in_dim.22), channel_id=1, replica_groups=mesh['section'=4,'row'=4,'col'=2] {'row'}, dimensions={0} | all-to-all | bytes 524288 | tf_op jit(solution)/shard_map/all_to_all | solution.py:26
  13.6 3.0 %fusion.24 = bf16[128,2048]{1,0:T(8,128)(2,1)S(1)} fusion(bf16[128,1024]{1,0:T(8,128)(2,1)S(1)} %bitcast.137, bf16[1,1024,2048]{2,1,0:T(8,128)(2,1)} %param.11), kind=kOutput, calls=%fused_computation.26 | convolution fusion | flops 537133056 | bytes 4980736 | tf_op jit(solution)/shard_map/dot_general | solution.py:56
  16.6 3.0 %collective-permute-start = (bf16[128,2048]{1,0:T(8,128)(2,1)S(1)}, bf16[128,2048]{1,0:T(8,128)(2,1)S(1)}, u32[]{:S(2)}, u32[]{:S(2)}) collective-permute-start(bf16[128,2048]{1,0:T(8,128)(2,1)S(1)} %fusion.24), channel_id=1, source_target_pairs={{0,1},{1,0},{2,3},{3,2},{4,5},{5,4},{6,7},{7,6},{8,9},{9,8},{10,11... | collective-permute-start | bytes 1572872 | tf_op jit(solution)/shard_map/ppermute | solution.py:20
  19.6 1.5 collective-permute-done
  21.5 1.4 fusion.61
  22.9 3.4 %all-to-all-start.1 = ((bf16[4,32,1024]{2,1,0:T(8,128)(2,1)}), bf16[4,32,1024]{2,1,0:T(8,128)(2,1)S(1)}, u32[]{:S(2)}, u32[]{:S(2)}) async-start(bf16[4,32,1024]{2,1,0:T(8,128)(2,1)} %bitcast.8), calls=%async_computation.1 | async-start | bytes 524288 | tf_op jit(solution)/shard_map/all_to_all | solution.py:33
  29.0 4.8 %all-to-all-done.1 = bf16[4,32,1024]{2,1,0:T(8,128)(2,1)S(1)} async-done(((bf16[4,32,1024]{2,1,0:T(8,128)(2,1)}), bf16[4,32,1024]{2,1,0:T(8,128)(2,1)S(1)}, u32[]{:S(2)}, u32[]{:S(2)}) %all-to-all-start.1) | async-done | bytes 262176 | tf_op jit(solution)/shard_map/all_to_all | solution.py:33
  33.8 0.9 fusion.83
  34.6 3.1 %collective-permute-start.1 = (bf16[32,1024]{1,0:T(8,128)(2,1)S(1)}, bf16[32,1024]{1,0:T(8,128)(2,1)S(1)}, u32[]{:S(2)}, u32[]{:S(2)}) collective-permute-start(bf16[32,1024]{1,0:T(8,128)(2,1)S(1)} %fusion.83), channel_id=1, source_target_pairs={{0,8},{8,16},{16,24},{1,9},{9,17},{17,25},{2,10},{10,18},{18,26},{... | collective-permute-start | bytes 196616 | tf_op jit(solution)/shard_map/ppermute | solution.py:15
  39.7 1.0 fusion.88
  41.4 9.2 %all_to_all.61 = bf16[4,32,1024]{2,1,0:T(8,128)(2,1)S(1)} all-to-all(bf16[4,32,1024]{2,1,0:T(8,128)(2,1)S(1)} %broadcast_in_dim.23), channel_id=1, replica_groups=mesh['section'=4,'row'=4,'col'=2] {'row'}, dimensions={0} | all-to-all | bytes 524288 | tf_op jit(solution)/shard_map/all_to_all | solution.py:26
  50.6 3.0 %fusion.27 = bf16[128,2048]{1,0:T(8,128)(2,1)S(1)} fusion(bf16[128,1024]{1,0:T(8,128)(2,1)S(1)} %bitcast.139, bf16[1,1024,2048]{2,1,0:T(8,128)(2,1)} %param.11), kind=kOutput, calls=%fused_computation.27 | convolution fusion | flops 537133056 | bytes 4980736 | tf_op jit(solution)/shard_map/dot_general | solution.py:56
  53.7 4.2 %collective-permute-start.2 = (bf16[128,2048]{1,0:T(8,128)(2,1)S(1)}, bf16[128,2048]{1,0:T(8,128)(2,1)S(1)}, u32[]{:S(2)}, u32[]{:S(2)}) collective-permute-start(bf16[128,2048]{1,0:T(8,128)(2,1)S(1)} %fusion.27), channel_id=1, source_target_pairs={{0,1},{1,0},{2,3},{3,2},{4,5},{5,4},{6,7},{7,6},{8,9},{9,8},{10,11... | collective-permute-start | bytes 1572872 | tf_op jit(solution)/shard_map/ppermute | solution.py:20
  57.9 1.5 collective-permute-done.2
  59.7 1.5 fusion.64
  61.2 3.4 %all-to-all-start.3 = ((bf16[4,32,1024]{2,1,0:T(8,128)(2,1)}), bf16[4,32,1024]{2,1,0:T(8,128)(2,1)S(1)}, u32[]{:S(2)}, u32[]{:S(2)}) async-start(bf16[4,32,1024]{2,1,0:T(8,128)(2,1)} %bitcast.16), calls=%async_computation.3 | async-start | bytes 524288 | tf_op jit(solution)/shard_map/all_to_all | solution.py:33
  64.6 1.5 slice_bitcast_fusion
  66.1 5.9 %all-to-all-done.3 = bf16[4,32,1024]{2,1,0:T(8,128)(2,1)S(1)} async-done(((bf16[4,32,1024]{2,1,0:T(8,128)(2,1)}), bf16[4,32,1024]{2,1,0:T(8,128)(2,1)S(1)}, u32[]{:S(2)}, u32[]{:S(2)}) %all-to-all-start.3) | async-done | bytes 262176 | tf_op jit(solution)/shard_map/all_to_all | solution.py:33
  72.0 1.6 broadcast_in_dim.54
  73.6 3.4 %all-to-all-start.6 = ((bf16[4,32,1024]{2,1,0:T(8,128)(2,1)}), bf16[4,32,1024]{2,1,0:T(8,128)(2,1)S(1)}, u32[]{:S(2)}, u32[]{:S(2)}) async-start(bf16[4,32,1024]{2,1,0:T(8,128)(2,1)} %broadcast_in_dim.54), calls=%async_computation.6 | async-start | bytes 524288 | tf_op jit(solution)/shard_map/all_to_all | solution.py:26
  77.0 1.0 convert_reduce_fusion.4
  78.0 1.6 fusion.92
  79.6 3.7 %collective-permute-start.3 = (bf16[32,1024]{1,0:T(8,128)(2,1)}, bf16[32,1024]{1,0:T(8,128)(2,1)}, u32[]{:S(2)}, u32[]{:S(2)}) collective-permute-start(bf16[32,1024]{1,0:T(8,128)(2,1)} %get-tuple-element.8), channel_id=1, source_target_pairs={{0,8},{8,16},{16,24},{1,9},{9,17},{17,25},{2,10},{10,18},{18,26},{... | collective-permute-start | bytes 196616 | tf_op jit(solution)/shard_map/ppermute | solution.py:15
  85.2 1.6 fusion.89
  86.8 1.6 broadcast_in_dim.25
  88.4 4.5 %all-to-all-start.4 = ((bf16[4,32,1024]{2,1,0:T(8,128)(2,1)}), bf16[4,32,1024]{2,1,0:T(8,128)(2,1)}, u32[]{:S(2)}, u32[]{:S(2)}) async-start(bf16[4,32,1024]{2,1,0:T(8,128)(2,1)} %broadcast_in_dim.25), calls=%async_computation.4 | async-start | bytes 524288 | tf_op jit(solution)/shard_map/all_to_all | solution.py:26
  92.9 4.5 %fusion.33 = bf16[128,2048]{1,0:T(8,128)(2,1)} fusion(bf16[128,1024]{1,0:T(8,128)(2,1)S(1)} %bitcast.141, bf16[1,2048,1024]{2,1,0:T(8,128)(2,1)} %param.12), kind=kOutput, calls=%fused_computation.29 | convolution fusion | flops 537133056 | bytes 4980736 | tf_op jit(solution)/shard_map/dot_general | solution.py:56
  97.4 3.7 %collective-permute-start.5 = (bf16[128,2048]{1,0:T(8,128)(2,1)}, bf16[128,2048]{1,0:T(8,128)(2,1)}, u32[]{:S(2)}, u32[]{:S(2)}) collective-permute-start(bf16[128,2048]{1,0:T(8,128)(2,1)} %fusion.33), channel_id=1, source_target_pairs={{0,1},{1,0},{2,3},{3,2},{4,5},{5,4},{6,7},{7,6},{8,9},{9,8},{10,11... | collective-permute-start | bytes 1572872 | tf_op jit(solution)/shard_map/ppermute | solution.py:20
  101.2 3.1 %fusion.30 = bf16[128,2048]{1,0:T(8,128)(2,1)S(1)} fusion(bf16[128,1024]{1,0:T(8,128)(2,1)} %bitcast.22, bf16[1,1024,2048]{2,1,0:T(8,128)(2,1)} %param.11), kind=kOutput, calls=%fused_computation.28 | convolution fusion | flops 537133056 | bytes 4980736 | tf_op jit(solution)/shard_map/dot_general | solution.py:56
  104.3 2.5 %collective-permute-start.4 = (bf16[128,2048]{1,0:T(8,128)(2,1)S(1)}, bf16[128,2048]{1,0:T(8,128)(2,1)S(1)}, u32[]{:S(2)}, u32[]{:S(2)}) collective-permute-start(bf16[128,2048]{1,0:T(8,128)(2,1)S(1)} %fusion.30), channel_id=1, source_target_pairs={{0,1},{1,0},{2,3},{3,2},{4,5},{5,4},{6,7},{7,6},{8,9},{9,8},{10,11... | collective-permute-start | bytes 1572872 | tf_op jit(solution)/shard_map/ppermute | solution.py:20
  106.8 1.5 collective-permute-done.4
  108.3 2.6 %multiply_convert_fusion.2 = (bf16[128,2048]{1,0:T(8,128)(2,1)S(1)}, bf16[128,2048]{1,0:T(8,128)(2,1)}) fusion(bf16[128,2048]{1,0:T(8,128)(2,1)} %collective-permute-done.5, bf16[128,2048]{1,0:T(8,128)(2,1)} %fusion.33, bf16[128,2048]{1,0:T(8,128)(2,1)S(1)} %collective-permute-done.4, bf16[128,2048]{1,0:T(8,128)(2,1)S(1)} %fusion.30), kind=kLoop, calls=%fused_computation.50 | loop fusion | flops 4456448 | bytes 3145728 | tf_op jit(solution)/shard_map/convert_element_type | solution.py:99
  110.9 1.5 fusion.52
  112.4 10.0 %all_to_all.62 = bf16[4,32,1024]{2,1,0:T(8,128)(2,1)S(1)} all-to-all(bf16[4,32,1024]{2,1,0:T(8,128)(2,1)S(1)} %bitcast.147), channel_id=1, replica_groups=mesh['section'=4,'row'=4,'col'=2] {'row'}, dimensions={0} | all-to-all | bytes 524288 | tf_op jit(solution)/shard_map/all_to_all | solution.py:33
  122.4 0.9 add_convert_fusion.2
  123.3 1.9 collective-permute-start.6
  125.2 4.3 %collective-permute-done.6 = bf16[32,1024]{1,0:T(8,128)(2,1)S(1)} collective-permute-done((bf16[32,1024]{1,0:T(8,128)(2,1)S(1)}, bf16[32,1024]{1,0:T(8,128)(2,1)S(1)}, u32[]{:S(2)}, u32[]{:S(2)}) %collective-permute-start.6) | collective-permute-done | bytes 65568 | tf_op jit(solution)/shard_map/ppermute | solution.py:15
  129.6 0.8 bitcast_select_fusion
  130.5 10.3 %all_to_all.63 = bf16[4,32,1024]{2,1,0:T(8,128)(2,1)S(1)} all-to-all(bf16[4,32,1024]{2,1,0:T(8,128)(2,1)S(1)} %broadcast_in_dim.55), channel_id=1, replica_groups=mesh['section'=4,'row'=4,'col'=2] {'row'}, dimensions={0} | all-to-all | bytes 524288 | tf_op jit(solution)/shard_map/all_to_all | solution.py:26
  140.8 3.8 %fusion.36 = bf16[128,2048]{1,0:T(8,128)(2,1)S(1)} fusion(bf16[128,1024]{1,0:T(8,128)(2,1)S(1)} %bitcast.143, bf16[1,2048,1024]{2,1,0:T(8,128)(2,1)} %param.12), kind=kOutput, calls=%fused_computation.30 | convolution fusion | flops 537133056 | bytes 4980736 | tf_op jit(solution)/shard_map/dot_general | solution.py:56
  144.6 4.0 %collective-permute-start.7 = (bf16[128,2048]{1,0:T(8,128)(2,1)S(1)}, bf16[128,2048]{1,0:T(8,128)(2,1)S(1)}, u32[]{:S(2)}, u32[]{:S(2)}) collective-permute-start(bf16[128,2048]{1,0:T(8,128)(2,1)S(1)} %fusion.36), channel_id=1, source_target_pairs={{0,1},{1,0},{2,3},{3,2},{4,5},{5,4},{6,7},{7,6},{8,9},{9,8},{10,11... | collective-permute-start | bytes 1572872 | tf_op jit(solution)/shard_map/ppermute | solution.py:20
  148.6 1.5 collective-permute-done.7
  150.7 2.2 %fusion.55 = bf16[128,1024]{1,0:T(8,128)(2,1)} fusion(bf16[128,2048]{1,0:T(8,128)(2,1)S(1)} %multiply_convert_fusion.1, bf16[1,1024,2048]{2,1,0:T(8,128)(2,1)S(1)} %copy-done.3), kind=kOutput, calls=%fused_computation.43 | convolution fusion | flops 537001984 | bytes 4980736 | tf_op jit(solution)/shard_map/dot_general | solution.py:56
  152.9 3.7 %all-to-all-start.9 = ((bf16[4,32,1024]{2,1,0:T(8,128)(2,1)}), bf16[4,32,1024]{2,1,0:T(8,128)(2,1)S(1)}, u32[]{:S(2)}, u32[]{:S(2)}) async-start(bf16[4,32,1024]{2,1,0:T(8,128)(2,1)} %bitcast.32), calls=%async_computation.9 | async-start | bytes 524288 | tf_op jit(solution)/shard_map/all_to_all | solution.py:33
  156.7 3.8 %fusion.67 = bf16[128,1024]{1,0:T(8,128)(2,1)} fusion(bf16[128,2048]{1,0:T(8,128)(2,1)} %get-tuple-element.6, bf16[1,2048,1024]{2,1,0:T(8,128)(2,1)} %param.12), kind=kOutput, calls=%fused_computation.47 | convolution fusion | flops 537001984 | bytes 4980736 | tf_op jit(solution)/shard_map/dot_general | solution.py:56
  160.5 3.4 %all-to-all-done.9 = bf16[4,32,1024]{2,1,0:T(8,128)(2,1)S(1)} async-done(((bf16[4,32,1024]{2,1,0:T(8,128)(2,1)}), bf16[4,32,1024]{2,1,0:T(8,128)(2,1)S(1)}, u32[]{:S(2)}, u32[]{:S(2)}) %all-to-all-start.9) | async-done | bytes 262176 | tf_op jit(solution)/shard_map/all_to_all | solution.py:33
  163.9 3.5 %all-to-all-start.5 = ((bf16[4,32,1024]{2,1,0:T(8,128)(2,1)}), bf16[4,32,1024]{2,1,0:T(8,128)(2,1)S(1)}, u32[]{:S(2)}, u32[]{:S(2)}) async-start(bf16[4,32,1024]{2,1,0:T(8,128)(2,1)} %bitcast.23), calls=%async_computation.5 | async-start | bytes 524288 | tf_op jit(solution)/shard_map/all_to_all | solution.py:33
  167.5 1.9 collective-permute-start.8
  169.4 4.0 %collective-permute-done.8 = bf16[32,1024]{1,0:T(8,128)(2,1)S(1)} collective-permute-done((bf16[32,1024]{1,0:T(8,128)(2,1)S(1)}, bf16[32,1024]{1,0:T(8,128)(2,1)S(1)}, u32[]{:S(2)}, u32[]{:S(2)}) %collective-permute-start.8) | collective-permute-done | bytes 65568 | tf_op jit(solution)/shard_map/ppermute | solution.py:15
  173.5 0.7 broadcast_in_dim.56
  174.2 4.5 %all-to-all-start.10 = ((bf16[4,32,1024]{2,1,0:T(8,128)(2,1)}), bf16[4,32,1024]{2,1,0:T(8,128)(2,1)S(1)}, u32[]{:S(2)}, u32[]{:S(2)}) async-start(bf16[4,32,1024]{2,1,0:T(8,128)(2,1)} %broadcast_in_dim.56), calls=%async_computation.10 | async-start | bytes 524288 | tf_op jit(solution)/shard_map/all_to_all | solution.py:26
  178.7 0.9 fusion.85
  179.6 0.7 maximum_bitcast_fusion
  180.3 4.0 %all-to-all-done.10 = bf16[4,32,1024]{2,1,0:T(8,128)(2,1)S(1)} async-done(((bf16[4,32,1024]{2,1,0:T(8,128)(2,1)}), bf16[4,32,1024]{2,1,0:T(8,128)(2,1)S(1)}, u32[]{:S(2)}, u32[]{:S(2)}) %all-to-all-start.10) | async-done | bytes 262176 | tf_op jit(solution)/shard_map/all_to_all | solution.py:26
  184.3 3.8 %fusion.39 = bf16[128,2048]{1,0:T(8,128)(2,1)S(1)} fusion(bf16[128,1024]{1,0:T(8,128)(2,1)S(1)} %bitcast.145, bf16[1,2048,1024]{2,1,0:T(8,128)(2,1)} %param.12), kind=kOutput, calls=%fused_computation.31 | convolution fusion | flops 537133056 | bytes 4980736 | tf_op jit(solution)/shard_map/dot_general | solution.py:56
  188.2 5.3 %collective-permute-start.9 = (bf16[128,2048]{1,0:T(8,128)(2,1)S(1)}, bf16[128,2048]{1,0:T(8,128)(2,1)S(1)}, u32[]{:S(2)}, u32[]{:S(2)}) collective-permute-start(bf16[128,2048]{1,0:T(8,128)(2,1)S(1)} %fusion.39), channel_id=1, source_target_pairs={{0,1},{1,0},{2,3},{3,2},{4,5},{5,4},{6,7},{7,6},{8,9},{9,8},{10,11... | collective-permute-start | bytes 1572872 | tf_op jit(solution)/shard_map/ppermute | solution.py:20
  193.5 0.7 maximum_bitcast_fusion.1
  194.3 0.8 collective-permute-done.9
  195.6 2.2 %fusion.58 = bf16[128,1024]{1,0:T(8,128)(2,1)} fusion(bf16[128,2048]{1,0:T(8,128)(2,1)S(1)} %multiply_convert_fusion, bf16[1,1024,2048]{2,1,0:T(8,128)(2,1)S(1)} %copy-done.4), kind=kOutput, calls=%fused_computation.44 | convolution fusion | flops 537001984 | bytes 4980736 | tf_op jit(solution)/shard_map/dot_general | solution.py:56
  197.8 4.0 %all-to-all-start.11 = ((bf16[4,32,1024]{2,1,0:T(8,128)(2,1)}), bf16[4,32,1024]{2,1,0:T(8,128)(2,1)}, u32[]{:S(2)}, u32[]{:S(2)}) async-start(bf16[4,32,1024]{2,1,0:T(8,128)(2,1)} %bitcast.34), calls=%async_computation.11 | async-start | bytes 524288 | tf_op jit(solution)/shard_map/all_to_all | solution.py:33
  201.9 5.5 %convert_bitcast_fusion = bf16[1,2048,1024]{2,1,0:T(8,128)(2,1)} fusion(bf16[128,2048]{1,0:T(8,128)(2,1)S(1)} %copy-done.9, bf16[128,2048]{1,0:T(8,128)(2,1)S(1)} %multiply_convert_fusion.4, bf16[128,2048]{1,0:T(8,128)(2,1)S(1)} %multiply_convert_fusion.5, bf16[128,1024]{1,0:T(8,128)(2,1)S(1)} %bitcast.142, bf16[128,1024]{1,0:T(8,128)(2,1)} %bitcast.144, ...), kind=kOutput, calls=%fused_computation.24 | convolution fusion | flops 1619787776 | bytes 6553600 | tf_op jit(solution)/shard_map/dot_general | solution.py:56
  207.5 5.4 %convert_bitcast_fusion.1 = bf16[1,1024,2048]{2,1,0:T(8,128)(2,1)} fusion(bf16[128,2048]{1,0:T(8,128)(2,1)S(1)} %copy-done.8, bf16[128,2048]{1,0:T(8,128)(2,1)S(1)} %copy-done.6, bf16[128,2048]{1,0:T(8,128)(2,1)S(1)} %multiply_convert_fusion, bf16[128,1024]{1,0:T(8,128)(2,1)} %bitcast.22, bf16[128,1024]{1,0:T(8,128)(2,1)S(1)} %bitcast.140, ...), kind=kOutput, calls=%fused_computation.25 | convolution fusion | flops 1619787776 | bytes 6553600 | tf_op jit(solution)/shard_map/dot_general | solution.py:56
  212.9 1.0 convert_reduce_fusion
  (87 shorter events, 4.1 us)
Async XLA Ops:
  0.6 20.8 %copy-start = (bf16[1,2048,1024]{2,1,0:T(8,128)(2,1)S(1)}, bf16[1,2048,1024]{2,1,0:T(8,128)(2,1)}, u32[]{:S(2)}) copy-start(bf16[1,2048,1024]{2,1,0:T(8,128)(2,1)} %param.12) | copy-start | bytes 12582916
  13.6 6.0 %copy-start.10 = (bf16[4,32,1024]{2,1,0:T(8,128)(2,1)}, bf16[4,32,1024]{2,1,0:T(8,128)(2,1)S(1)}, u32[]{:S(2)}) copy-start(bf16[4,32,1024]{2,1,0:T(8,128)(2,1)S(1)} %all_to_all.60) | copy-start | bytes 786436
  16.6 9.8 %copy-start.30 = (s32[6]{0:T(128)S(1)}, s32[6]{0:T(128)}, u32[]{:S(2)}) copy-start(s32[6]{0:T(128)} %param.8) | copy-start | bytes 76
  16.6 17.2 %copy-start.25 = (bf16[1,3,32,1024]{3,2,1,0:T(8,128)(2,1)S(1)}, bf16[1,3,32,1024]{3,2,1,0:T(8,128)(2,1)}, u32[]{:S(2)}) copy-start(bf16[1,3,32,1024]{3,2,1,0:T(8,128)(2,1)} %param.7) | copy-start | bytes 589828
  16.6 4.5 %collective-permute-start = (bf16[128,2048]{1,0:T(8,128)(2,1)S(1)}, bf16[128,2048]{1,0:T(8,128)(2,1)S(1)}, u32[]{:S(2)}, u32[]{:S(2)}) collective-permute-start(bf16[128,2048]{1,0:T(8,128)(2,1)S(1)} %fusion.24), channel_id=1, source_target_pairs={{0,1},{1,0},{2,3},{3,2},{4,5},{5,4},{6,7},{7,6},{8,9},{9,8},{10,11... | collective-permute-start | bytes 1572872 | tf_op jit(solution)/shard_map/ppermute | solution.py:20
  22.9 10.8 %all-to-all-start.1 = ((bf16[4,32,1024]{2,1,0:T(8,128)(2,1)}), bf16[4,32,1024]{2,1,0:T(8,128)(2,1)S(1)}, u32[]{:S(2)}, u32[]{:S(2)}) async-start(bf16[4,32,1024]{2,1,0:T(8,128)(2,1)} %bitcast.8), calls=%async_computation.1 | async-start | bytes 524288 | tf_op jit(solution)/shard_map/all_to_all | solution.py:33
  34.6 5.1 %collective-permute-start.1 = (bf16[32,1024]{1,0:T(8,128)(2,1)S(1)}, bf16[32,1024]{1,0:T(8,128)(2,1)S(1)}, u32[]{:S(2)}, u32[]{:S(2)}) collective-permute-start(bf16[32,1024]{1,0:T(8,128)(2,1)S(1)} %fusion.83), channel_id=1, source_target_pairs={{0,8},{8,16},{16,24},{1,9},{9,17},{17,25},{2,10},{10,18},{18,26},{... | collective-permute-start | bytes 196616 | tf_op jit(solution)/shard_map/ppermute | solution.py:15
  39.7 20.0 %copy-start.1 = (bf16[1,2048,1024]{2,1,0:T(8,128)(2,1)S(1)}, bf16[1,2048,1024]{2,1,0:T(8,128)(2,1)}, u32[]{:S(2)}) copy-start(bf16[1,2048,1024]{2,1,0:T(8,128)(2,1)} %param.12) | copy-start | bytes 12582916
  40.8 0.6 copy-start.19
  50.6 7.2 %copy-start.12 = (bf16[4,32,1024]{2,1,0:T(8,128)(2,1)}, bf16[4,32,1024]{2,1,0:T(8,128)(2,1)S(1)}, u32[]{:S(2)}) copy-start(bf16[4,32,1024]{2,1,0:T(8,128)(2,1)S(1)} %all_to_all.61) | copy-start | bytes 786436
  53.7 5.7 %collective-permute-start.2 = (bf16[128,2048]{1,0:T(8,128)(2,1)S(1)}, bf16[128,2048]{1,0:T(8,128)(2,1)S(1)}, u32[]{:S(2)}, u32[]{:S(2)}) collective-permute-start(bf16[128,2048]{1,0:T(8,128)(2,1)S(1)} %fusion.27), channel_id=1, source_target_pairs={{0,1},{1,0},{2,3},{3,2},{4,5},{5,4},{6,7},{7,6},{8,9},{9,8},{10,11... | collective-permute-start | bytes 1572872 | tf_op jit(solution)/shard_map/ppermute | solution.py:20
  61.2 10.8 %all-to-all-start.3 = ((bf16[4,32,1024]{2,1,0:T(8,128)(2,1)}), bf16[4,32,1024]{2,1,0:T(8,128)(2,1)S(1)}, u32[]{:S(2)}, u32[]{:S(2)}) async-start(bf16[4,32,1024]{2,1,0:T(8,128)(2,1)} %bitcast.16), calls=%async_computation.3 | async-start | bytes 524288 | tf_op jit(solution)/shard_map/all_to_all | solution.py:33
  72.0 1.6 copy-start.18
  73.6 13.2 %all-to-all-start.6 = ((bf16[4,32,1024]{2,1,0:T(8,128)(2,1)}), bf16[4,32,1024]{2,1,0:T(8,128)(2,1)S(1)}, u32[]{:S(2)}, u32[]{:S(2)}) async-start(bf16[4,32,1024]{2,1,0:T(8,128)(2,1)} %broadcast_in_dim.54), calls=%async_computation.6 | async-start | bytes 524288 | tf_op jit(solution)/shard_map/all_to_all | solution.py:26
  79.6 5.6 %collective-permute-start.3 = (bf16[32,1024]{1,0:T(8,128)(2,1)}, bf16[32,1024]{1,0:T(8,128)(2,1)}, u32[]{:S(2)}, u32[]{:S(2)}) collective-permute-start(bf16[32,1024]{1,0:T(8,128)(2,1)} %get-tuple-element.8), channel_id=1, source_target_pairs={{0,8},{8,16},{16,24},{1,9},{9,17},{17,25},{2,10},{10,18},{18,26},{... | collective-permute-start | bytes 196616 | tf_op jit(solution)/shard_map/ppermute | solution.py:15
  86.8 17.5 %copy-start.14 = (bf16[4,32,1024]{2,1,0:T(8,128)(2,1)}, bf16[4,32,1024]{2,1,0:T(8,128)(2,1)S(1)}, u32[]{:S(2)}) copy-start(bf16[4,32,1024]{2,1,0:T(8,128)(2,1)S(1)} %all-to-all-done.6) | copy-start | bytes 786436
  88.4 12.8 %all-to-all-start.4 = ((bf16[4,32,1024]{2,1,0:T(8,128)(2,1)}), bf16[4,32,1024]{2,1,0:T(8,128)(2,1)}, u32[]{:S(2)}, u32[]{:S(2)}) async-start(bf16[4,32,1024]{2,1,0:T(8,128)(2,1)} %broadcast_in_dim.25), calls=%async_computation.4 | async-start | bytes 524288 | tf_op jit(solution)/shard_map/all_to_all | solution.py:26
  97.4 9.3 %collective-permute-start.5 = (bf16[128,2048]{1,0:T(8,128)(2,1)}, bf16[128,2048]{1,0:T(8,128)(2,1)}, u32[]{:S(2)}, u32[]{:S(2)}) collective-permute-start(bf16[128,2048]{1,0:T(8,128)(2,1)} %fusion.33), channel_id=1, source_target_pairs={{0,1},{1,0},{2,3},{3,2},{4,5},{5,4},{6,7},{7,6},{8,9},{9,8},{10,11... | collective-permute-start | bytes 1572872 | tf_op jit(solution)/shard_map/ppermute | solution.py:20
  101.2 9.7 %copy-start.2 = (bf16[1,1024,2048]{2,1,0:T(8,128)(2,1)S(1)}, bf16[1,1024,2048]{2,1,0:T(8,128)(2,1)}, u32[]{:S(2)}) copy-start(bf16[1,1024,2048]{2,1,0:T(8,128)(2,1)} %param.11) | copy-start | bytes 12582916
  104.3 4.0 %collective-permute-start.4 = (bf16[128,2048]{1,0:T(8,128)(2,1)S(1)}, bf16[128,2048]{1,0:T(8,128)(2,1)S(1)}, u32[]{:S(2)}, u32[]{:S(2)}) collective-permute-start(bf16[128,2048]{1,0:T(8,128)(2,1)S(1)} %fusion.30), channel_id=1, source_target_pairs={{0,1},{1,0},{2,3},{3,2},{4,5},{5,4},{6,7},{7,6},{8,9},{9,8},{10,11... | collective-permute-start | bytes 1572872 | tf_op jit(solution)/shard_map/ppermute | solution.py:20
  110.9 1.5 copy-start.7
  123.3 6.3 %collective-permute-start.6 = (bf16[32,1024]{1,0:T(8,128)(2,1)S(1)}, bf16[32,1024]{1,0:T(8,128)(2,1)S(1)}, u32[]{:S(2)}, u32[]{:S(2)}) collective-permute-start(bf16[32,1024]{1,0:T(8,128)(2,1)S(1)} %add_convert_fusion.2), channel_id=1, source_target_pairs={{8,0},{16,8},{24,16},{9,1},{17,9},{25,17},{10,2},{18,10},{26,18},{... | collective-permute-start | bytes 196616 | tf_op jit(solution)/shard_map/ppermute | solution.py:15
  130.4 20.2 %copy-start.3 = (bf16[1,1024,2048]{2,1,0:T(8,128)(2,1)S(1)}, bf16[1,1024,2048]{2,1,0:T(8,128)(2,1)}, u32[]{:S(2)}) copy-start(bf16[1,1024,2048]{2,1,0:T(8,128)(2,1)} %param.11) | copy-start | bytes 12582916
  140.7 12.2 %copy-start.16 = (bf16[4,32,1024]{2,1,0:T(8,128)(2,1)}, bf16[4,32,1024]{2,1,0:T(8,128)(2,1)S(1)}, u32[]{:S(2)}) copy-start(bf16[4,32,1024]{2,1,0:T(8,128)(2,1)S(1)} %all_to_all.63) | copy-start | bytes 786436
  144.6 5.5 %collective-permute-start.7 = (bf16[128,2048]{1,0:T(8,128)(2,1)S(1)}, bf16[128,2048]{1,0:T(8,128)(2,1)S(1)}, u32[]{:S(2)}, u32[]{:S(2)}) collective-permute-start(bf16[128,2048]{1,0:T(8,128)(2,1)S(1)} %fusion.36), channel_id=1, source_target_pairs={{0,1},{1,0},{2,3},{3,2},{4,5},{5,4},{6,7},{7,6},{8,9},{9,8},{10,11... | collective-permute-start | bytes 1572872 | tf_op jit(solution)/shard_map/ppermute | solution.py:20
  150.7 2.2 %copy-start.5 = (bf16[128,2048]{1,0:T(8,128)(2,1)}, bf16[128,2048]{1,0:T(8,128)(2,1)S(1)}, u32[]{:S(2)}) copy-start(bf16[128,2048]{1,0:T(8,128)(2,1)S(1)} %multiply_convert_fusion.1) | copy-start | bytes 1572868
  152.9 20.5 %copy-start.24 = (bf16[1,3,32,1024]{3,2,1,0:T(8,128)(2,1)S(1)}, bf16[1,3,32,1024]{3,2,1,0:T(8,128)(2,1)}, u32[]{:S(2)}) copy-start(bf16[1,3,32,1024]{3,2,1,0:T(8,128)(2,1)} %param.13) | copy-start | bytes 589828
  152.9 26.6 %copy-start.20 = (bf16[32,1024]{1,0:T(8,128)(2,1)S(1)}, bf16[32,1024]{1,0:T(8,128)(2,1)}, u32[]{:S(2)}) copy-start(bf16[32,1024]{1,0:T(8,128)(2,1)} %copy-done.19) | copy-start | bytes 196612
  152.9 26.6 %copy-start.21 = (bf16[32,1024]{1,0:T(8,128)(2,1)S(1)}, bf16[32,1024]{1,0:T(8,128)(2,1)}, u32[]{:S(2)}) copy-start(bf16[32,1024]{1,0:T(8,128)(2,1)} %fusion.89) | copy-start | bytes 196612
  152.9 26.6 %copy-start.26 = (bf16[1,32,1024]{2,1,0:T(8,128)(2,1)S(1)}, bf16[1,32,1024]{2,1,0:T(8,128)(2,1)}, u32[]{:S(2)}) copy-start(bf16[1,32,1024]{2,1,0:T(8,128)(2,1)} %get-tuple-element.9) | copy-start | bytes 196612
  152.9 10.9 %all-to-all-start.9 = ((bf16[4,32,1024]{2,1,0:T(8,128)(2,1)}), bf16[4,32,1024]{2,1,0:T(8,128)(2,1)S(1)}, u32[]{:S(2)}, u32[]{:S(2)}) async-start(bf16[4,32,1024]{2,1,0:T(8,128)(2,1)} %bitcast.32), calls=%async_computation.9 | async-start | bytes 524288 | tf_op jit(solution)/shard_map/all_to_all | solution.py:33
  163.9 29.6 %copy-start.27 = (bf16[1,32,1024]{2,1,0:T(8,128)(2,1)S(1)}, bf16[1,32,1024]{2,1,0:T(8,128)(2,1)}, u32[]{:S(2)}) copy-start(bf16[1,32,1024]{2,1,0:T(8,128)(2,1)} %get-tuple-element.7) | copy-start | bytes 196612
  163.9 9.6 %all-to-all-start.5 = ((bf16[4,32,1024]{2,1,0:T(8,128)(2,1)}), bf16[4,32,1024]{2,1,0:T(8,128)(2,1)S(1)}, u32[]{:S(2)}, u32[]{:S(2)}) async-start(bf16[4,32,1024]{2,1,0:T(8,128)(2,1)} %bitcast.23), calls=%async_computation.5 | async-start | bytes 524288 | tf_op jit(solution)/shard_map/all_to_all | solution.py:33
  167.5 5.9 %copy-start.28 = (bf16[32,1024]{1,0:T(8,128)(2,1)}, bf16[32,1024]{1,0:T(8,128)(2,1)S(1)}, u32[]{:S(2)}) copy-start(bf16[32,1024]{1,0:T(8,128)(2,1)S(1)} %add_convert_fusion.1) | copy-start | bytes 196612
  167.5 5.9 %collective-permute-start.8 = (bf16[32,1024]{1,0:T(8,128)(2,1)S(1)}, bf16[32,1024]{1,0:T(8,128)(2,1)S(1)}, u32[]{:S(2)}, u32[]{:S(2)}) collective-permute-start(bf16[32,1024]{1,0:T(8,128)(2,1)S(1)} %add_convert_fusion.1), channel_id=1, source_target_pairs={{8,0},{16,8},{24,16},{9,1},{17,9},{25,17},{10,2},{18,10},{26,18},{... | collective-permute-start | bytes 196616 | tf_op jit(solution)/shard_map/ppermute | solution.py:15
  173.4 0.7 copy-start.22
  174.2 10.1 %all-to-all-start.10 = ((bf16[4,32,1024]{2,1,0:T(8,128)(2,1)}), bf16[4,32,1024]{2,1,0:T(8,128)(2,1)S(1)}, u32[]{:S(2)}, u32[]{:S(2)}) async-start(bf16[4,32,1024]{2,1,0:T(8,128)(2,1)} %broadcast_in_dim.56), calls=%async_computation.10 | async-start | bytes 524288 | tf_op jit(solution)/shard_map/all_to_all | solution.py:26
  184.3 9.2 %copy-start.17 = (bf16[4,32,1024]{2,1,0:T(8,128)(2,1)}, bf16[4,32,1024]{2,1,0:T(8,128)(2,1)S(1)}, u32[]{:S(2)}) copy-start(bf16[4,32,1024]{2,1,0:T(8,128)(2,1)S(1)} %all-to-all-done.10) | copy-start | bytes 786436
  184.3 11.3 %copy-start.4 = (bf16[1,1024,2048]{2,1,0:T(8,128)(2,1)S(1)}, bf16[1,1024,2048]{2,1,0:T(8,128)(2,1)}, u32[]{:S(2)}) copy-start(bf16[1,1024,2048]{2,1,0:T(8,128)(2,1)} %param.11) | copy-start | bytes 12582916
  188.2 6.9 %collective-permute-start.9 = (bf16[128,2048]{1,0:T(8,128)(2,1)S(1)}, bf16[128,2048]{1,0:T(8,128)(2,1)S(1)}, u32[]{:S(2)}, u32[]{:S(2)}) collective-permute-start(bf16[128,2048]{1,0:T(8,128)(2,1)S(1)} %fusion.39), channel_id=1, source_target_pairs={{0,1},{1,0},{2,3},{3,2},{4,5},{5,4},{6,7},{7,6},{8,9},{9,8},{10,11... | collective-permute-start | bytes 1572872 | tf_op jit(solution)/shard_map/ppermute | solution.py:20
  194.2 7.6 %copy-start.9 = (bf16[128,2048]{1,0:T(8,128)(2,1)S(1)}, bf16[128,2048]{1,0:T(8,128)(2,1)}, u32[]{:S(2)}) copy-start(bf16[128,2048]{1,0:T(8,128)(2,1)} %get-tuple-element.6) | copy-start | bytes 1572868
  194.3 7.6 %copy-start.15 = (bf16[4,32,1024]{2,1,0:T(8,128)(2,1)S(1)}, bf16[4,32,1024]{2,1,0:T(8,128)(2,1)}, u32[]{:S(2)}) copy-start(bf16[4,32,1024]{2,1,0:T(8,128)(2,1)} %copy-done.14) | copy-start | bytes 786436
  197.8 15.1 %all-to-all-start.11 = ((bf16[4,32,1024]{2,1,0:T(8,128)(2,1)}), bf16[4,32,1024]{2,1,0:T(8,128)(2,1)}, u32[]{:S(2)}, u32[]{:S(2)}) async-start(bf16[4,32,1024]{2,1,0:T(8,128)(2,1)} %bitcast.34), calls=%async_computation.11 | async-start | bytes 524288 | tf_op jit(solution)/shard_map/all_to_all | solution.py:33
  201.9 5.6 %copy-start.6 = (bf16[128,2048]{1,0:T(8,128)(2,1)S(1)}, bf16[128,2048]{1,0:T(8,128)(2,1)}, u32[]{:S(2)}) copy-start(bf16[128,2048]{1,0:T(8,128)(2,1)} %copy-done.5) | copy-start | bytes 1572868
  201.9 5.6 %copy-start.8 = (bf16[128,2048]{1,0:T(8,128)(2,1)S(1)}, bf16[128,2048]{1,0:T(8,128)(2,1)}, u32[]{:S(2)}) copy-start(bf16[128,2048]{1,0:T(8,128)(2,1)} %copy-done.7) | copy-start | bytes 1572868
  201.9 5.6 %copy-start.11 = (bf16[4,32,1024]{2,1,0:T(8,128)(2,1)S(1)}, bf16[4,32,1024]{2,1,0:T(8,128)(2,1)}, u32[]{:S(2)}) copy-start(bf16[4,32,1024]{2,1,0:T(8,128)(2,1)} %copy-done.10) | copy-start | bytes 786436
  201.9 5.6 %copy-start.13 = (bf16[4,32,1024]{2,1,0:T(8,128)(2,1)S(1)}, bf16[4,32,1024]{2,1,0:T(8,128)(2,1)}, u32[]{:S(2)}) copy-start(bf16[4,32,1024]{2,1,0:T(8,128)(2,1)} %copy-done.12) | copy-start | bytes 786436
  207.5 6.4 %copy-start.23 = (bf16[32,1024]{1,0:T(8,128)(2,1)S(1)}, bf16[32,1024]{1,0:T(8,128)(2,1)}, u32[]{:S(2)}) copy-start(bf16[32,1024]{1,0:T(8,128)(2,1)} %copy-done.22) | copy-start | bytes 196612
  207.5 6.4 %copy-start.29 = (bf16[32,1024]{1,0:T(8,128)(2,1)S(1)}, bf16[32,1024]{1,0:T(8,128)(2,1)}, u32[]{:S(2)}) copy-start(bf16[32,1024]{1,0:T(8,128)(2,1)} %copy-done.28) | copy-start | bytes 196612

commit v3 on v1

--- a/solution.py
+++ b/solution.py
@@ -9,10 +9,8 @@
 FIRST = (((0,), (0,)), ((), ()))
 
 
-def from_behind(block, axis, distance):
-    devices = range(lax.axis_size(axis))
-    route = [(i - distance, i) for i in devices if i - distance in devices]
-    return lax.ppermute(block, axis, route)
+def partner(row, j, size):
+    return row ^ j if size & (size - 1) == 0 else (j - row) % size
 
 
 def turn(block, axis, distance):
@@ -20,9 +18,42 @@
     return lax.ppermute(block, axis, [(i, (i + distance) % size) for i in range(size)])
 
 
+def swap_rows(block, j):
+    size = lax.axis_size("row")
+    return lax.ppermute(block, "row", [(i, partner(i, j, size)) for i in range(size)])
+
+
 def gather_rows(block):
-    size = lax.axis_size("row")
-    return jnp.concatenate([block] + [turn(block, "row", -j) for j in range(1, size)], axis=0)
+    return [swap_rows(block, j) if j else block for j in range(lax.axis_size("row"))]
+
+
+def spread(block, step):
+    sections, size = lax.axis_size("section"), lax.axis_size("row")
+    there = [s for s in range(sections) if 0 <= s + step < sections]
+    return [
+        lax.ppermute(
+            block,
+            ("section", "row"),
+            [(s * size + i, (s + step) * size + partner(i, j, size)) for s in there for i in range(size)],
+        )
+        for j in range(size)
+    ]
+
+
+def gather_last(block):
+    last, size = lax.axis_size("section") - 1, lax.axis_size("row")
+    return [block] + [
+        lax.ppermute(
+            block,
+            ("section", "row"),
+            [(last * size + i, last * size + partner(i, j, size)) for i in range(size)],
+        )
+        for j in range(1, size)
+    ]
+
+
+def after(block, other):
+    return lax.optimization_barrier((block, other))[0]
 
 
 def scatter_rows(partial):
@@ -30,7 +61,7 @@
     pieces = jnp.split(partial, size, axis=0)
     total = pieces[0].astype(F32)
     for j in range(1, size):
-        total = total + turn(pieces[j], "row", j).astype(F32)
+        total = total + swap_rows(pieces[j], j).astype(F32)
     return total
 
 
@@ -63,27 +94,42 @@
     ticks = inputs.shape[1]
     up_block = w_up[0]
     down_block = w_down[0]
-    full_ins, pres, acts, seen_in, seen_out = [], [], [], [], []
+    full_ins, pres, acts, seen_out = [], [], [], []
+    samples = [pick(sample_ids, tick - section + sections - 1) for tick in range(ticks)]
+    bases = [
+        jnp.where(section == 0, inputs[0, tick], pick(recv_base[0], samples[tick])) for tick in range(1, ticks)
+    ]
     sending = None
     for tick in range(ticks):
-        sample = pick(sample_ids, tick - section + sections - 1)
         if tick == 0:
-            act_in = inputs[0, tick]
+            pieces = gather_rows(inputs[0, tick])
         else:
-            arrived = from_behind(sending, "section", 1)
-            rebuilt = (pick(recv_base[0], sample).astype(F32) + arrived.astype(F32)).astype(BF)
-            act_in = jnp.where(section == 0, inputs[0, tick], rebuilt)
-        full_in = gather_rows(act_in)
-        pre = sum_cols(matmul(full_in, up_block).astype(BF))
+            pieces = [
+                (base[tick - 1].astype(F32) + arrived.astype(F32)).astype(BF)
+                for base, arrived in zip(full_bases, spread(sending, 1))
+            ]
+        full_in = jnp.concatenate(pieces, axis=0)
+        partial = matmul(full_in, up_block).astype(BF)
+        if tick == 0:
+            full_bases = gather_rows(after(jnp.stack(bases), partial))
+        elif tick == 1:
+            first_cots = gather_rows(after(cotangent[0, ticks - 1], partial))
+        else:
+            last_cots = gather_last(after(cotangent[0, : ticks - 1], partial))
+        pre = sum_cols(partial)
         act = jax.nn.silu(pre).astype(BF)
         mixed = scatter_rows(matmul(act, down_block).astype(BF))
-        act_out = (act_in.astype(F32) + mixed).astype(BF)
-        stored = pick(send_base[0], sample)
+        act_out = (pieces[0].astype(F32) + mixed).astype(BF)
+        stored = pick(send_base[0], samples[tick])
         sending = (act_out.astype(F32) - stored.astype(F32)).astype(BF)
+        if tick == 0:
+            sending = after(sending, full_bases)
+        elif tick == 1:
+            first_grads = matmul(jnp.concatenate(first_cots, axis=0), down_block, LAST).astype(BF)
+            sending = after(sending, first_grads)
         full_ins.append(full_in)
         pres.append(pre)
         acts.append(act)
-        seen_in.append(act_in)
         seen_out.append(act_out)
     full_grads = [None] * ticks
     pre_grads = [None] * ticks
@@ -91,18 +137,25 @@
     for step in range(ticks):
         tick = ticks - 1 - step
         if step == 0:
-            grad_out = cotangent[0, tick]
+            pieces = first_cots
         else:
-            arrived = from_behind(sending, "section", -1)
-            grad_out = jnp.where(section == sections - 1, cotangent[0, tick], arrived)
-        full_grad = gather_rows(grad_out)
-        grad_act = sum_cols(matmul(full_grad, down_block, LAST).astype(BF))
+            pieces = [
+                jnp.where(section == sections - 1, own[tick], arrived)
+                for own, arrived in zip(last_cots, spread(sending, -1))
+            ]
+        full_grad = jnp.concatenate(pieces, axis=0)
+        partial = matmul(full_grad, down_block, LAST).astype(BF) if step else first_grads
+        grad_act = sum_cols(partial)
         grad_pre = (grad_act * silu_slope(pres[tick])).astype(BF)
         returned = scatter_rows(matmul(grad_pre, up_block, LAST).astype(BF))
-        sending = (grad_out.astype(F32) + returned).astype(BF)
+        sending = (pieces[0].astype(F32) + returned).astype(BF)
+        if step == 0:
+            sending = after(sending, last_cots)
         full_grads[tick] = full_grad
         pre_grads[tick] = grad_pre
         seen_grad[tick] = sending
+    piece_rows = inputs.shape[2]
+    seen_in = [full[:piece_rows] for full in full_ins]
     grad_up = matmul(jnp.concatenate(full_ins, axis=0), jnp.concatenate(pre_grads, axis=0), FIRST)
     grad_down = matmul(jnp.concatenate(acts, axis=0), jnp.concatenate(full_grads, axis=0), FIRST)
     return (

time: 178 us -> 186 us (1.045)
  waiting for transfers between devices: 44.8 us -> 56.3 us
  local copies, waits for them, and re-layouts: 8.78 us -> 2.42 us
  starting transfers between devices: 70.8 us -> 76.3 us
  matrix products: 32.2 us -> 28.9 us
    ppermute x4 -> x46, starting transfers between devices: 11 us -> 68.9 us  [the longest x16 37.1 us: spread(): lax.ppermute(block, ('section', 'row'), [(s * size + i, (s + step) * size...]
    ppermute x42 -> x6, starting transfers between devices: 59.8 us -> 7.42 us  [turn(): lax.ppermute(block, axis, [(i, (i + distance) % size) for i in range(size)])]
    ppermute x4 -> x46, waiting for transfers between devices: 6.58 us -> 54.8 us  [the longest x27 32 us: swap_rows(): lax.ppermute(block, 'row', [(i, partner(i, j, size)) for i in range(size)])]
    ppermute x42 -> x6, waiting for transfers between devices: 38.3 us -> 1.55 us  [turn(): lax.ppermute(block, axis, [(i, (i + distance) % size) for i in range(size)])]
    unnamed x71 -> x47, local copies, waits for them, and re-layouts: 4.43 us -> 0.21 us
    dot_general x14, matrix products: 32.2 us -> 28.9 us  [matmul(): return lax.dot_general(a, b, dims, preferred_element_type=F32)]
    unnamed x3 -> x11, other arithmetic: 2.38 us -> 0.22 us
  transfers between devices with their start and end apart: 46 -> 52, of which waited for: 29 -> 23; matrix products, arithmetic and copies ran while one was open for 16% -> 13% of each run, Pallas kernels for 0% -> 0%
where the time goes in v3:
time: 186 us; the launch traced here: 183 us
  starting transfers between devices  76.3 us (41%)
  waiting for transfers between devices  56.3 us (30%)
  matrix products  28.9 us (16%)
  other arithmetic  12.1 us (7%)
  between operations  7.32 us (4%)
  local copies, waits for them, and re-layouts  2.42 us (1%)
    ppermute x16, starting transfers between devices, spread(): lax.ppermute(block, ('section', 'row'), [(s * size + i, (s + step) * size...  37.1 us
    ppermute x27, waiting for transfers between devices, swap_rows(): lax.ppermute(block, 'row', [(i, partner(i, j, size)) for i in range(size)])  32 us
    ppermute x27, starting transfers between devices, swap_rows(): lax.ppermute(block, 'row', [(i, partner(i, j, size)) for i in range(size)])  29.5 us
    dot_general x14, matrix products, matmul(): return lax.dot_general(a, b, dims, preferred_element_type=F32)  28.9 us
    ppermute x16, waiting for transfers between devices, spread(): lax.ppermute(block, ('section', 'row'), [(s * size + i, (s + step) * size...  22.8 us
    ppermute x6, starting transfers between devices, turn(): lax.ppermute(block, axis, [(i, (i + distance) % size) for i in range(size)])  7.42 us
  transfers between devices with their start and end apart: 52, of which 23 were waited for; matrix products, arithmetic and copies ran while one was open for 13% of the time, Pallas kernels for 0%

profile of v3, /device:TPU:3, one launch (start us, length us, event | category | flops | bytes accessed | tf_op | source)
XLA Modules:
  0.0 183.4 jit_solution(8079739965674350444)
XLA Ops:
  0.7 1.4 fusion.155
  5.9 1.6 slice_bitcast_fusion.15
  7.5 3.3 %collective-permute-start.2 = (bf16[32,1024]{1,0:T(8,128)(2,1)S(1)}, bf16[32,1024]{1,0:T(8,128)(2,1)S(1)}, u32[]{:S(2)}, u32[]{:S(2)}) collective-permute-start(bf16[32,1024]{1,0:T(8,128)(2,1)S(1)} %get-tuple-element.68), channel_id=1, source_target_pairs={{0,6},{2,4},{4,2},{6,0},{1,7},{3,5},{5,3},{7,1},{8,14},{10,12},{12... | collective-permute-start | bytes 196616 | tf_op jit(solution)/shard_map/ppermute | solution.py:23
  11.1 1.4 collective-permute-done.2
  12.5 4.2 %collective-permute-done.1 = bf16[32,1024]{1,0:T(8,128)(2,1)S(1)} collective-permute-done((bf16[32,1024]{1,0:T(8,128)(2,1)S(1)}, bf16[32,1024]{1,0:T(8,128)(2,1)S(1)}, u32[]{:S(2)}, u32[]{:S(2)}) %collective-permute-start.1) | collective-permute-done | bytes 65568 | tf_op jit(solution)/shard_map/ppermute | solution.py:23
  16.7 2.9 %fusion.24 = bf16[128,2048]{1,0:T(8,128)(2,1)S(1)} fusion(bf16[1,1024,2048]{2,1,0:T(8,128)(2,1)} %param.11, bf16[32,1024]{1,0:T(8,128)(2,1)S(1)} %collective-permute-done.2, bf16[32,1024]{1,0:T(8,128)(2,1)S(1)} %collective-permute-done.1, bf16[32,1024]{1,0:T(8,128)(2,1)S(1)} %collective-permute-done, bf16[32,1024]{1,0:T(8,128)(2,1)S(1)} %get-tuple-element.68), kind=kOutput, calls=%fused_computation.26 | convolution fusion | flops 538181632 | bytes 4980736 | tf_op jit(solution)/shard_map/dot_general | solution.py:88
  22.4 2.4 %collective-permute-start.9 = (bf16[2,32,1024]{2,1,0:T(8,128)(2,1)S(1)}, bf16[2,32,1024]{2,1,0:T(8,128)(2,1)S(1)}, u32[]{:S(2)}, u32[]{:S(2)}) collective-permute-start(bf16[2,32,1024]{2,1,0:T(8,128)(2,1)S(1)} %pad_maximum_fusion), channel_id=1, source_target_pairs={{0,6},{2,4},{4,2},{6,0},{1,7},{3,5},{5,3},{7,1},{8,14},{10,12},{12... | collective-permute-start | bytes 393224 | tf_op jit(solution)/shard_map/ppermute | solution.py:23
  25.2 3.1 %fusion.61 = bf16[128,1024]{1,0:T(8,128)(2,1)S(1)} fusion(bf16[128,2048]{1,0:T(8,128)(2,1)S(1)} %multiply_convert_fusion.5, bf16[1,2048,1024]{2,1,0:T(8,128)(2,1)} %param.12), kind=kOutput, calls=%fused_computation.45 | convolution fusion | flops 537001984 | bytes 4980736 | tf_op jit(solution)/shard_map/dot_general | solution.py:88
  29.5 2.4 %collective-permute-start.6 = (bf16[32,1024]{1,0:T(8,128)(2,1)S(1)}, bf16[32,1024]{1,0:T(8,128)(2,1)S(1)}, u32[]{:S(2)}, u32[]{:S(2)}) collective-permute-start(bf16[32,1024]{1,0:T(8,128)(2,1)S(1)} %get-tuple-element.65), channel_id=1, source_target_pairs={{0,6},{2,4},{4,2},{6,0},{1,7},{3,5},{5,3},{7,1},{8,14},{10,12},{12... | collective-permute-start | bytes 196616 | tf_op jit(solution)/shard_map/ppermute | solution.py:23
  32.0 2.2 %collective-permute-start.7 = (bf16[2,32,1024]{2,1,0:T(8,128)(2,1)S(1)}, bf16[2,32,1024]{2,1,0:T(8,128)(2,1)S(1)}, u32[]{:S(2)}, u32[]{:S(2)}) collective-permute-start(bf16[2,32,1024]{2,1,0:T(8,128)(2,1)S(1)} %pad_maximum_fusion), channel_id=1, source_target_pairs={{0,2},{2,0},{4,6},{6,4},{1,3},{3,1},{5,7},{7,5},{8,10},{10,8},{12,... | collective-permute-start | bytes 393224 | tf_op jit(solution)/shard_map/ppermute | solution.py:23
  35.0 7.1 %collective-permute-done.5 = bf16[32,1024]{1,0:T(8,128)(2,1)S(1)} collective-permute-done((bf16[32,1024]{1,0:T(8,128)(2,1)S(1)}, bf16[32,1024]{1,0:T(8,128)(2,1)S(1)}, u32[]{:S(2)}, u32[]{:S(2)}) %collective-permute-start.5) | collective-permute-done | bytes 65568 | tf_op jit(solution)/shard_map/ppermute | solution.py:23
  42.1 1.5 fusion.120
  43.7 3.1 %collective-permute-start.10 = (bf16[32,1024]{1,0:T(8,128)(2,1)S(1)}, bf16[32,1024]{1,0:T(8,128)(2,1)S(1)}, u32[]{:S(2)}, u32[]{:S(2)}) collective-permute-start(bf16[32,1024]{1,0:T(8,128)(2,1)S(1)} %get-tuple-element.12), channel_id=1, source_target_pairs={{0,8},{2,10},{4,12},{6,14},{8,16},{10,18},{12,20},{14,22},{16,24},... | collective-permute-start | bytes 196616 | tf_op jit(solution)/shard_map/ppermute | solution.py:34
  46.8 4.5 %collective-permute-start.13 = (bf16[32,1024]{1,0:T(8,128)(2,1)S(1)}, bf16[32,1024]{1,0:T(8,128)(2,1)S(1)}, u32[]{:S(2)}, u32[]{:S(2)}) collective-permute-start(bf16[32,1024]{1,0:T(8,128)(2,1)S(1)} %get-tuple-element.12), channel_id=1, source_target_pairs={{0,14},{2,12},{4,10},{6,8},{8,22},{10,20},{12,18},{14,16},{16,30},... | collective-permute-start | bytes 196616 | tf_op jit(solution)/shard_map/ppermute | solution.py:34
  51.3 1.9 %collective-permute-start.12 = (bf16[32,1024]{1,0:T(8,128)(2,1)S(1)}, bf16[32,1024]{1,0:T(8,128)(2,1)S(1)}, u32[]{:S(2)}, u32[]{:S(2)}) collective-permute-start(bf16[32,1024]{1,0:T(8,128)(2,1)S(1)} %get-tuple-element.12), channel_id=1, source_target_pairs={{0,12},{2,14},{4,8},{6,10},{8,20},{10,22},{12,16},{14,18},{16,28},... | collective-permute-start | bytes 196616 | tf_op jit(solution)/shard_map/ppermute | solution.py:34
  53.3 1.9 %collective-permute-start.11 = (bf16[32,1024]{1,0:T(8,128)(2,1)S(1)}, bf16[32,1024]{1,0:T(8,128)(2,1)S(1)}, u32[]{:S(2)}, u32[]{:S(2)}) collective-permute-start(bf16[32,1024]{1,0:T(8,128)(2,1)S(1)} %get-tuple-element.12), channel_id=1, source_target_pairs={{0,10},{2,8},{4,14},{6,12},{8,18},{10,16},{12,22},{14,20},{16,26},... | collective-permute-start | bytes 196616 | tf_op jit(solution)/shard_map/ppermute | solution.py:34
  55.2 5.0 %collective-permute-done.11 = bf16[32,1024]{1,0:T(8,128)(2,1)S(1)} collective-permute-done((bf16[32,1024]{1,0:T(8,128)(2,1)S(1)}, bf16[32,1024]{1,0:T(8,128)(2,1)S(1)}, u32[]{:S(2)}, u32[]{:S(2)}) %collective-permute-start.11) | collective-permute-done | bytes 65568 | tf_op jit(solution)/shard_map/ppermute | solution.py:34
  61.1 1.5 collective-permute-start.14
  62.6 1.7 collective-permute-start.20
  64.9 1.3 collective-permute-start.18
  67.5 1.6 collective-permute-start.17
  70.0 1.5 collective-permute-done.19
  71.6 1.5 fusion.33
  73.4 3.0 %collective-permute-done.16 = bf16[32,1024]{1,0:T(8,128)(2,1)S(1)} collective-permute-done((bf16[32,1024]{1,0:T(8,128)(2,1)S(1)}, bf16[32,1024]{1,0:T(8,128)(2,1)S(1)}, u32[]{:S(2)}, u32[]{:S(2)}) %collective-permute-start.16) | collective-permute-done | bytes 65568 | tf_op jit(solution)/shard_map/ppermute | solution.py:23
  76.4 1.5 fusion.115
  78.0 2.6 %collective-permute-start.21 = (bf16[32,1024]{1,0:T(8,128)(2,1)S(1)}, bf16[32,1024]{1,0:T(8,128)(2,1)S(1)}, u32[]{:S(2)}, u32[]{:S(2)}) collective-permute-start(bf16[32,1024]{1,0:T(8,128)(2,1)S(1)} %get-tuple-element.14), channel_id=1, source_target_pairs={{0,8},{2,10},{4,12},{6,14},{8,16},{10,18},{12,20},{14,22},{16,24},... | collective-permute-start | bytes 196616 | tf_op jit(solution)/shard_map/ppermute | solution.py:34
  80.6 1.8 %collective-permute-start.29 = (bf16[128,2048]{1,0:T(8,128)(2,1)S(1)}, bf16[128,2048]{1,0:T(8,128)(2,1)S(1)}, u32[]{:S(2)}, u32[]{:S(2)}) collective-permute-start(bf16[128,2048]{1,0:T(8,128)(2,1)S(1)} %fusion.33), channel_id=1, source_target_pairs={{0,1},{1,0},{2,3},{3,2},{4,5},{5,4},{6,7},{7,6},{8,9},{9,8},{10,11... | collective-permute-start | bytes 1572872 | tf_op jit(solution)/shard_map/ppermute | solution.py:18
  82.4 3.0 %collective-permute-start.24 = (bf16[32,1024]{1,0:T(8,128)(2,1)S(1)}, bf16[32,1024]{1,0:T(8,128)(2,1)S(1)}, u32[]{:S(2)}, u32[]{:S(2)}) collective-permute-start(bf16[32,1024]{1,0:T(8,128)(2,1)S(1)} %get-tuple-element.14), channel_id=1, source_target_pairs={{0,14},{2,12},{4,10},{6,8},{8,22},{10,20},{12,18},{14,16},{16,30},... | collective-permute-start | bytes 196616 | tf_op jit(solution)/shard_map/ppermute | solution.py:34
  85.4 1.9 %collective-permute-start.23 = (bf16[32,1024]{1,0:T(8,128)(2,1)S(1)}, bf16[32,1024]{1,0:T(8,128)(2,1)S(1)}, u32[]{:S(2)}, u32[]{:S(2)}) collective-permute-start(bf16[32,1024]{1,0:T(8,128)(2,1)S(1)} %get-tuple-element.14), channel_id=1, source_target_pairs={{0,12},{2,14},{4,8},{6,10},{8,20},{10,22},{12,16},{14,18},{16,28},... | collective-permute-start | bytes 196616 | tf_op jit(solution)/shard_map/ppermute | solution.py:34
  87.3 1.9 %collective-permute-start.22 = (bf16[32,1024]{1,0:T(8,128)(2,1)S(1)}, bf16[32,1024]{1,0:T(8,128)(2,1)S(1)}, u32[]{:S(2)}, u32[]{:S(2)}) collective-permute-start(bf16[32,1024]{1,0:T(8,128)(2,1)S(1)} %get-tuple-element.14), channel_id=1, source_target_pairs={{0,10},{2,8},{4,14},{6,12},{8,18},{10,16},{12,22},{14,20},{16,26},... | collective-permute-start | bytes 196616 | tf_op jit(solution)/shard_map/ppermute | solution.py:34
  89.3 5.9 %collective-permute-done.22 = bf16[32,1024]{1,0:T(8,128)(2,1)S(1)} collective-permute-done((bf16[32,1024]{1,0:T(8,128)(2,1)S(1)}, bf16[32,1024]{1,0:T(8,128)(2,1)S(1)}, u32[]{:S(2)}, u32[]{:S(2)}) %collective-permute-start.22) | collective-permute-done | bytes 65568 | tf_op jit(solution)/shard_map/ppermute | solution.py:34
  96.6 1.5 collective-permute-done.25
  98.2 1.4 multiply_convert_fusion.2
  99.5 1.5 fusion.52
  101.9 1.6 collective-permute-start.32
  107.2 3.8 %collective-permute-done.31 = bf16[32,1024]{1,0:T(8,128)(2,1)} collective-permute-done((bf16[32,1024]{1,0:T(8,128)(2,1)}, bf16[32,1024]{1,0:T(8,128)(2,1)}, u32[]{:S(2)}, u32[]{:S(2)}) %collective-permute-start.31) | collective-permute-done | bytes 65568 | tf_op jit(solution)/shard_map/ppermute | solution.py:23
  112.0 2.6 %collective-permute-start.39 = (bf16[32,1024]{1,0:T(8,128)(2,1)S(1)}, bf16[32,1024]{1,0:T(8,128)(2,1)S(1)}, u32[]{:S(2)}, u32[]{:S(2)}) collective-permute-start(bf16[32,1024]{1,0:T(8,128)(2,1)S(1)} %add_convert_fusion.2), channel_id=1, source_target_pairs={{8,6},{10,4},{12,2},{14,0},{16,14},{18,12},{20,10},{22,8},{24,22},... | collective-permute-start | bytes 196616 | tf_op jit(solution)/shard_map/ppermute | solution.py:34
  114.7 1.5 maximum_bitcast_fusion
  116.2 1.9 %collective-permute-start.38 = (bf16[32,1024]{1,0:T(8,128)(2,1)S(1)}, bf16[32,1024]{1,0:T(8,128)(2,1)S(1)}, u32[]{:S(2)}, u32[]{:S(2)}) collective-permute-start(bf16[32,1024]{1,0:T(8,128)(2,1)S(1)} %add_convert_fusion.2), channel_id=1, source_target_pairs={{8,4},{10,6},{12,0},{14,2},{16,12},{18,14},{20,8},{22,10},{24,20},... | collective-permute-start | bytes 196616 | tf_op jit(solution)/shard_map/ppermute | solution.py:34
  118.1 1.9 %collective-permute-start.37 = (bf16[32,1024]{1,0:T(8,128)(2,1)S(1)}, bf16[32,1024]{1,0:T(8,128)(2,1)S(1)}, u32[]{:S(2)}, u32[]{:S(2)}) collective-permute-start(bf16[32,1024]{1,0:T(8,128)(2,1)S(1)} %add_convert_fusion.2), channel_id=1, source_target_pairs={{8,2},{10,0},{12,6},{14,4},{16,10},{18,8},{20,14},{22,12},{24,18},... | collective-permute-start | bytes 196616 | tf_op jit(solution)/shard_map/ppermute | solution.py:34
  120.0 2.1 %collective-permute-start.36 = (bf16[32,1024]{1,0:T(8,128)(2,1)S(1)}, bf16[32,1024]{1,0:T(8,128)(2,1)S(1)}, u32[]{:S(2)}, u32[]{:S(2)}) collective-permute-start(bf16[32,1024]{1,0:T(8,128)(2,1)S(1)} %add_convert_fusion.2), channel_id=1, source_target_pairs={{8,0},{10,2},{12,4},{14,6},{16,8},{18,10},{20,12},{22,14},{24,16},... | collective-permute-start | bytes 196616 | tf_op jit(solution)/shard_map/ppermute | solution.py:34
  122.2 2.8 %collective-permute-done.38 = bf16[32,1024]{1,0:T(8,128)(2,1)S(1)} collective-permute-done((bf16[32,1024]{1,0:T(8,128)(2,1)S(1)}, bf16[32,1024]{1,0:T(8,128)(2,1)S(1)}, u32[]{:S(2)}, u32[]{:S(2)}) %collective-permute-start.38) | collective-permute-done | bytes 65568 | tf_op jit(solution)/shard_map/ppermute | solution.py:34
  125.0 1.3 collective-permute-done.37
  127.4 3.7 %fusion.36 = bf16[128,2048]{1,0:T(8,128)(2,1)S(1)} fusion(bf16[1,2048,1024]{2,1,0:T(8,128)(2,1)} %param.12, bf16[32,1024]{1,0:T(8,128)(2,1)S(1)} %fusion.127, bf16[32,1024]{1,0:T(8,128)(2,1)S(1)} %fusion.128, bf16[32,1024]{1,0:T(8,128)(2,1)S(1)} %fusion.129, bf16[32,1024]{1,0:T(8,128)(2,1)S(1)} %bitcast_select_fusion), kind=kOutput, calls=%fused_computation.30 | convolution fusion | flops 538181632 | bytes 4980736 | tf_op jit(solution)/shard_map/dot_general | solution.py:88
  131.1 1.5 collective-permute-start.40
  134.1 1.6 collective-permute-start.28
  136.7 1.5 fusion.55
  138.2 1.6 collective-permute-start.41
  139.9 1.6 collective-permute-start.43
  141.5 1.5 collective-permute-done.27
  143.3 2.0 %collective-permute-done.43 = bf16[32,1024]{1,0:T(8,128)(2,1)S(1)} collective-permute-done((bf16[32,1024]{1,0:T(8,128)(2,1)S(1)}, bf16[32,1024]{1,0:T(8,128)(2,1)S(1)}, u32[]{:S(2)}, u32[]{:S(2)}) %collective-permute-start.43) | collective-permute-done | bytes 65568 | tf_op jit(solution)/shard_map/ppermute | solution.py:23
  145.3 3.6 %collective-permute-done.42 = bf16[32,1024]{1,0:T(8,128)(2,1)S(1)} collective-permute-done((bf16[32,1024]{1,0:T(8,128)(2,1)S(1)}, bf16[32,1024]{1,0:T(8,128)(2,1)S(1)}, u32[]{:S(2)}, u32[]{:S(2)}) %collective-permute-start.42) | collective-permute-done | bytes 65568 | tf_op jit(solution)/shard_map/ppermute | solution.py:23
  148.9 1.9 %collective-permute-start.44 = (bf16[32,1024]{1,0:T(8,128)(2,1)S(1)}, bf16[32,1024]{1,0:T(8,128)(2,1)S(1)}, u32[]{:S(2)}, u32[]{:S(2)}) collective-permute-start(bf16[32,1024]{1,0:T(8,128)(2,1)S(1)} %add_convert_fusion.1), channel_id=1, source_target_pairs={{8,0},{10,2},{12,4},{14,6},{16,8},{18,10},{20,12},{22,14},{24,16},... | collective-permute-start | bytes 196616 | tf_op jit(solution)/shard_map/ppermute | solution.py:34
  151.5 1.9 %collective-permute-start.47 = (bf16[32,1024]{1,0:T(8,128)(2,1)S(1)}, bf16[32,1024]{1,0:T(8,128)(2,1)S(1)}, u32[]{:S(2)}, u32[]{:S(2)}) collective-permute-start(bf16[32,1024]{1,0:T(8,128)(2,1)S(1)} %add_convert_fusion.1), channel_id=1, source_target_pairs={{8,6},{10,4},{12,2},{14,0},{16,14},{18,12},{20,10},{22,8},{24,22},... | collective-permute-start | bytes 196616 | tf_op jit(solution)/shard_map/ppermute | solution.py:34
  153.5 1.9 %collective-permute-start.46 = (bf16[32,1024]{1,0:T(8,128)(2,1)S(1)}, bf16[32,1024]{1,0:T(8,128)(2,1)S(1)}, u32[]{:S(2)}, u32[]{:S(2)}) collective-permute-start(bf16[32,1024]{1,0:T(8,128)(2,1)S(1)} %add_convert_fusion.1), channel_id=1, source_target_pairs={{8,4},{10,6},{12,0},{14,2},{16,12},{18,14},{20,8},{22,10},{24,20},... | collective-permute-start | bytes 196616 | tf_op jit(solution)/shard_map/ppermute | solution.py:34
  155.4 1.9 %collective-permute-start.45 = (bf16[32,1024]{1,0:T(8,128)(2,1)S(1)}, bf16[32,1024]{1,0:T(8,128)(2,1)S(1)}, u32[]{:S(2)}, u32[]{:S(2)}) collective-permute-start(bf16[32,1024]{1,0:T(8,128)(2,1)S(1)} %add_convert_fusion.1), channel_id=1, source_target_pairs={{8,2},{10,0},{12,6},{14,4},{16,10},{18,8},{20,14},{22,12},{24,18},... | collective-permute-start | bytes 196616 | tf_op jit(solution)/shard_map/ppermute | solution.py:34
  157.4 5.9 %collective-permute-done.45 = bf16[32,1024]{1,0:T(8,128)(2,1)S(1)} collective-permute-done((bf16[32,1024]{1,0:T(8,128)(2,1)S(1)}, bf16[32,1024]{1,0:T(8,128)(2,1)S(1)}, u32[]{:S(2)}, u32[]{:S(2)}) %collective-permute-start.45) | collective-permute-done | bytes 65568 | tf_op jit(solution)/shard_map/ppermute | solution.py:34
  164.1 1.5 fusion.39
  165.6 1.3 collective-permute-start.48
  167.0 4.4 %convert_bitcast_fusion = bf16[1,2048,1024]{2,1,0:T(8,128)(2,1)} fusion(bf16[384,1024]{1,0:T(8,128)(2,1)S(1)} %constant_dynamic-update-slice_fusion.12, bf16[128,2048]{1,0:T(8,128)(2,1)S(1)} %copy-done.6, bf16[128,2048]{1,0:T(8,128)(2,1)S(1)} %multiply_convert_fusion.4, bf16[128,2048]{1,0:T(8,128)(2,1)S(1)} %multiply_convert_fusion.5), kind=kOutput, calls=%fused_computation.24 | convolution fusion | flops 1617428480 | bytes 6553600 | tf_op jit(solution)/shard_map/dot_general | solution.py:88
  172.0 1.5 fusion.58
  173.9 1.6 collective-permute-start.51
  176.2 4.4 %convert_bitcast_fusion.1 = bf16[1,1024,2048]{2,1,0:T(8,128)(2,1)} fusion(bf16[384,1024]{1,0:T(8,128)(2,1)S(1)} %copy-done.17, bf16[128,2048]{1,0:T(8,128)(2,1)S(1)} %copy-done.5, bf16[128,2048]{1,0:T(8,128)(2,1)S(1)} %multiply_convert_fusion.1, bf16[128,2048]{1,0:T(8,128)(2,1)S(1)} %multiply_convert_fusion), kind=kOutput, calls=%fused_computation.25 | convolution fusion | flops 1617428480 | bytes 6553600 | tf_op jit(solution)/shard_map/dot_general | solution.py:88
  180.6 2.1 %collective-permute-done.50 = bf16[32,1024]{1,0:T(8,128)(2,1)S(1)} collective-permute-done((bf16[32,1024]{1,0:T(8,128)(2,1)S(1)}, bf16[32,1024]{1,0:T(8,128)(2,1)S(1)}, u32[]{:S(2)}, u32[]{:S(2)}) %collective-permute-start.50) | collective-permute-done | bytes 65568 | tf_op jit(solution)/shard_map/ppermute | solution.py:23
  (143 shorter events, 22.0 us)
Async XLA Ops:
  0.6 21.7 %copy-start.8 = (bf16[1,3,32,1024]{3,2,1,0:T(8,128)(2,1)S(1)}, bf16[1,3,32,1024]{3,2,1,0:T(8,128)(2,1)}, u32[]{:S(2)}) copy-start(bf16[1,3,32,1024]{3,2,1,0:T(8,128)(2,1)} %param.7) | copy-start | bytes 589828
  7.5 5.0 %collective-permute-start.2 = (bf16[32,1024]{1,0:T(8,128)(2,1)S(1)}, bf16[32,1024]{1,0:T(8,128)(2,1)S(1)}, u32[]{:S(2)}, u32[]{:S(2)}) collective-permute-start(bf16[32,1024]{1,0:T(8,128)(2,1)S(1)} %get-tuple-element.68), channel_id=1, source_target_pairs={{0,6},{2,4},{4,2},{6,0},{1,7},{3,5},{5,3},{7,1},{8,14},{10,12},{12... | collective-permute-start | bytes 196616 | tf_op jit(solution)/shard_map/ppermute | solution.py:23
  10.8 5.9 %collective-permute-start.1 = (bf16[32,1024]{1,0:T(8,128)(2,1)S(1)}, bf16[32,1024]{1,0:T(8,128)(2,1)S(1)}, u32[]{:S(2)}, u32[]{:S(2)}) collective-permute-start(bf16[32,1024]{1,0:T(8,128)(2,1)S(1)} %get-tuple-element.68), channel_id=1, source_target_pairs={{0,4},{2,6},{4,0},{6,2},{1,5},{3,7},{5,1},{7,3},{8,12},{10,14},{12... | collective-permute-start | bytes 196616 | tf_op jit(solution)/shard_map/ppermute | solution.py:23
  10.8 5.9 %collective-permute-start = (bf16[32,1024]{1,0:T(8,128)(2,1)S(1)}, bf16[32,1024]{1,0:T(8,128)(2,1)S(1)}, u32[]{:S(2)}, u32[]{:S(2)}) collective-permute-start(bf16[32,1024]{1,0:T(8,128)(2,1)S(1)} %get-tuple-element.68), channel_id=1, source_target_pairs={{0,2},{2,0},{4,6},{6,4},{1,3},{3,1},{5,7},{7,5},{8,10},{10,8},{12,... | collective-permute-start | bytes 196616 | tf_op jit(solution)/shard_map/ppermute | solution.py:23
  19.7 5.2 %collective-permute-start.3 = (bf16[128,2048]{1,0:T(8,128)(2,1)S(1)}, bf16[128,2048]{1,0:T(8,128)(2,1)S(1)}, u32[]{:S(2)}, u32[]{:S(2)}) collective-permute-start(bf16[128,2048]{1,0:T(8,128)(2,1)S(1)} %fusion.24), channel_id=1, source_target_pairs={{0,1},{1,0},{2,3},{3,2},{4,5},{5,4},{6,7},{7,6},{8,9},{9,8},{10,11... | collective-permute-start | bytes 1572872 | tf_op jit(solution)/shard_map/ppermute | solution.py:18
  22.4 21.3 %collective-permute-start.9 = (bf16[2,32,1024]{2,1,0:T(8,128)(2,1)S(1)}, bf16[2,32,1024]{2,1,0:T(8,128)(2,1)S(1)}, u32[]{:S(2)}, u32[]{:S(2)}) collective-permute-start(bf16[2,32,1024]{2,1,0:T(8,128)(2,1)S(1)} %pad_maximum_fusion), channel_id=1, source_target_pairs={{0,6},{2,4},{4,2},{6,0},{1,7},{3,5},{5,3},{7,1},{8,14},{10,12},{12... | collective-permute-start | bytes 393224 | tf_op jit(solution)/shard_map/ppermute | solution.py:23
  24.8 18.9 %collective-permute-start.8 = (bf16[2,32,1024]{2,1,0:T(8,128)(2,1)S(1)}, bf16[2,32,1024]{2,1,0:T(8,128)(2,1)S(1)}, u32[]{:S(2)}, u32[]{:S(2)}) collective-permute-start(bf16[2,32,1024]{2,1,0:T(8,128)(2,1)S(1)} %pad_maximum_fusion), channel_id=1, source_target_pairs={{0,4},{2,6},{4,0},{6,2},{1,5},{3,7},{5,1},{7,3},{8,12},{10,14},{12... | collective-permute-start | bytes 393224 | tf_op jit(solution)/shard_map/ppermute | solution.py:23
  24.8 35.5 %copy-start.2 = (bf16[1,1024,2048]{2,1,0:T(8,128)(2,1)S(1)}, bf16[1,1024,2048]{2,1,0:T(8,128)(2,1)}, u32[]{:S(2)}) copy-start(bf16[1,1024,2048]{2,1,0:T(8,128)(2,1)} %param.11) | copy-start | bytes 12582916
  28.2 34.4 %copy-start.15 = (bf16[1,3,32,1024]{3,2,1,0:T(8,128)(2,1)S(1)}, bf16[1,3,32,1024]{3,2,1,0:T(8,128)(2,1)}, u32[]{:S(2)}) copy-start(bf16[1,3,32,1024]{3,2,1,0:T(8,128)(2,1)} %param.13) | copy-start | bytes 589828
  28.3 3.7 %collective-permute-start.4 = (bf16[32,1024]{1,0:T(8,128)(2,1)S(1)}, bf16[32,1024]{1,0:T(8,128)(2,1)S(1)}, u32[]{:S(2)}, u32[]{:S(2)}) collective-permute-start(bf16[32,1024]{1,0:T(8,128)(2,1)S(1)} %get-tuple-element.64), channel_id=1, source_target_pairs={{0,2},{2,0},{4,6},{6,4},{1,3},{3,1},{5,7},{7,5},{8,10},{10,8},{12,... | collective-permute-start | bytes 196616 | tf_op jit(solution)/shard_map/ppermute | solution.py:23
  29.5 5.5 %collective-permute-start.6 = (bf16[32,1024]{1,0:T(8,128)(2,1)S(1)}, bf16[32,1024]{1,0:T(8,128)(2,1)S(1)}, u32[]{:S(2)}, u32[]{:S(2)}) collective-permute-start(bf16[32,1024]{1,0:T(8,128)(2,1)S(1)} %get-tuple-element.65), channel_id=1, source_target_pairs={{0,6},{2,4},{4,2},{6,0},{1,7},{3,5},{5,3},{7,1},{8,14},{10,12},{12... | collective-permute-start | bytes 196616 | tf_op jit(solution)/shard_map/ppermute | solution.py:23
  31.9 10.3 %collective-permute-start.5 = (bf16[32,1024]{1,0:T(8,128)(2,1)S(1)}, bf16[32,1024]{1,0:T(8,128)(2,1)S(1)}, u32[]{:S(2)}, u32[]{:S(2)}) collective-permute-start(bf16[32,1024]{1,0:T(8,128)(2,1)S(1)} %get-tuple-element.66), channel_id=1, source_target_pairs={{0,4},{2,6},{4,0},{6,2},{1,5},{3,7},{5,1},{7,3},{8,12},{10,14},{12... | collective-permute-start | bytes 196616 | tf_op jit(solution)/shard_map/ppermute | solution.py:23
  31.9 34.7 %copy-start = (bf16[1,2048,1024]{2,1,0:T(8,128)(2,1)S(1)}, bf16[1,2048,1024]{2,1,0:T(8,128)(2,1)}, u32[]{:S(2)}) copy-start(bf16[1,2048,1024]{2,1,0:T(8,128)(2,1)} %param.12) | copy-start | bytes 12582916
  32.0 11.7 %collective-permute-start.7 = (bf16[2,32,1024]{2,1,0:T(8,128)(2,1)S(1)}, bf16[2,32,1024]{2,1,0:T(8,128)(2,1)S(1)}, u32[]{:S(2)}, u32[]{:S(2)}) collective-permute-start(bf16[2,32,1024]{2,1,0:T(8,128)(2,1)S(1)} %pad_maximum_fusion), channel_id=1, source_target_pairs={{0,2},{2,0},{4,6},{6,4},{1,3},{3,1},{5,7},{7,5},{8,10},{10,8},{12,... | collective-permute-start | bytes 393224 | tf_op jit(solution)/shard_map/ppermute | solution.py:23
  43.7 11.5 %collective-permute-start.10 = (bf16[32,1024]{1,0:T(8,128)(2,1)S(1)}, bf16[32,1024]{1,0:T(8,128)(2,1)S(1)}, u32[]{:S(2)}, u32[]{:S(2)}) collective-permute-start(bf16[32,1024]{1,0:T(8,128)(2,1)S(1)} %get-tuple-element.12), channel_id=1, source_target_pairs={{0,8},{2,10},{4,12},{6,14},{8,16},{10,18},{12,20},{14,22},{16,24},... | collective-permute-start | bytes 196616 | tf_op jit(solution)/shard_map/ppermute | solution.py:34
  46.8 13.5 %collective-permute-start.13 = (bf16[32,1024]{1,0:T(8,128)(2,1)S(1)}, bf16[32,1024]{1,0:T(8,128)(2,1)S(1)}, u32[]{:S(2)}, u32[]{:S(2)}) collective-permute-start(bf16[32,1024]{1,0:T(8,128)(2,1)S(1)} %get-tuple-element.12), channel_id=1, source_target_pairs={{0,14},{2,12},{4,10},{6,8},{8,22},{10,20},{12,18},{14,16},{16,30},... | collective-permute-start | bytes 196616 | tf_op jit(solution)/shard_map/ppermute | solution.py:34
  51.3 8.9 %collective-permute-start.12 = (bf16[32,1024]{1,0:T(8,128)(2,1)S(1)}, bf16[32,1024]{1,0:T(8,128)(2,1)S(1)}, u32[]{:S(2)}, u32[]{:S(2)}) collective-permute-start(bf16[32,1024]{1,0:T(8,128)(2,1)S(1)} %get-tuple-element.12), channel_id=1, source_target_pairs={{0,12},{2,14},{4,8},{6,10},{8,20},{10,22},{12,16},{14,18},{16,28},... | collective-permute-start | bytes 196616 | tf_op jit(solution)/shard_map/ppermute | solution.py:34
  53.3 7.0 %collective-permute-start.11 = (bf16[32,1024]{1,0:T(8,128)(2,1)S(1)}, bf16[32,1024]{1,0:T(8,128)(2,1)S(1)}, u32[]{:S(2)}, u32[]{:S(2)}) collective-permute-start(bf16[32,1024]{1,0:T(8,128)(2,1)S(1)} %get-tuple-element.12), channel_id=1, source_target_pairs={{0,10},{2,8},{4,14},{6,12},{8,18},{10,16},{12,22},{14,20},{16,26},... | collective-permute-start | bytes 196616 | tf_op jit(solution)/shard_map/ppermute | solution.py:34
  61.1 5.1 %collective-permute-start.14 = (bf16[128,2048]{1,0:T(8,128)(2,1)S(1)}, bf16[128,2048]{1,0:T(8,128)(2,1)S(1)}, u32[]{:S(2)}, u32[]{:S(2)}) collective-permute-start(bf16[128,2048]{1,0:T(8,128)(2,1)S(1)} %fusion.27), channel_id=1, source_target_pairs={{0,1},{1,0},{2,3},{3,2},{4,5},{5,4},{6,7},{7,6},{8,9},{9,8},{10,11... | collective-permute-start | bytes 1572872 | tf_op jit(solution)/shard_map/ppermute | solution.py:18
  62.6 6.5 %collective-permute-start.20 = (bf16[32,1024]{1,0:T(8,128)(2,1)S(1)}, bf16[32,1024]{1,0:T(8,128)(2,1)S(1)}, u32[]{:S(2)}, u32[]{:S(2)}) collective-permute-start(bf16[32,1024]{1,0:T(8,128)(2,1)S(1)} %slice_bitcast_fusion.13), channel_id=1, source_target_pairs={{0,6},{2,4},{4,2},{6,0},{1,7},{3,5},{5,3},{7,1},{8,14},{10,12},{12... | collective-permute-start | bytes 196616 | tf_op jit(solution)/shard_map/ppermute | solution.py:23
  64.3 7.2 %collective-permute-start.19 = (bf16[32,1024]{1,0:T(8,128)(2,1)S(1)}, bf16[32,1024]{1,0:T(8,128)(2,1)S(1)}, u32[]{:S(2)}, u32[]{:S(2)}) collective-permute-start(bf16[32,1024]{1,0:T(8,128)(2,1)S(1)} %slice_bitcast_fusion.13), channel_id=1, source_target_pairs={{0,4},{2,6},{4,0},{6,2},{1,5},{3,7},{5,1},{7,3},{8,12},{10,14},{12... | collective-permute-start | bytes 196616 | tf_op jit(solution)/shard_map/ppermute | solution.py:23
  64.9 6.7 %collective-permute-start.18 = (bf16[32,1024]{1,0:T(8,128)(2,1)S(1)}, bf16[32,1024]{1,0:T(8,128)(2,1)S(1)}, u32[]{:S(2)}, u32[]{:S(2)}) collective-permute-start(bf16[32,1024]{1,0:T(8,128)(2,1)S(1)} %slice_bitcast_fusion.13), channel_id=1, source_target_pairs={{0,2},{2,0},{4,6},{6,4},{1,3},{3,1},{5,7},{7,5},{8,10},{10,8},{12,... | collective-permute-start | bytes 196616 | tf_op jit(solution)/shard_map/ppermute | solution.py:23
  67.3 5.8 %collective-permute-start.15 = (bf16[32,1024]{1,0:T(8,128)(2,1)S(1)}, bf16[32,1024]{1,0:T(8,128)(2,1)S(1)}, u32[]{:S(2)}, u32[]{:S(2)}) collective-permute-start(bf16[32,1024]{1,0:T(8,128)(2,1)S(1)} %get-tuple-element.61), channel_id=1, source_target_pairs={{0,2},{2,0},{4,6},{6,4},{1,3},{3,1},{5,7},{7,5},{8,10},{10,8},{12,... | collective-permute-start | bytes 196616 | tf_op jit(solution)/shard_map/ppermute | solution.py:23
  67.5 5.9 %collective-permute-start.17 = (bf16[32,1024]{1,0:T(8,128)(2,1)S(1)}, bf16[32,1024]{1,0:T(8,128)(2,1)S(1)}, u32[]{:S(2)}, u32[]{:S(2)}) collective-permute-start(bf16[32,1024]{1,0:T(8,128)(2,1)S(1)} %get-tuple-element.62), channel_id=1, source_target_pairs={{0,6},{2,4},{4,2},{6,0},{1,7},{3,5},{5,3},{7,1},{8,14},{10,12},{12... | collective-permute-start | bytes 196616 | tf_op jit(solution)/shard_map/ppermute | solution.py:23
  69.1 7.3 %collective-permute-start.16 = (bf16[32,1024]{1,0:T(8,128)(2,1)S(1)}, bf16[32,1024]{1,0:T(8,128)(2,1)S(1)}, u32[]{:S(2)}, u32[]{:S(2)}) collective-permute-start(bf16[32,1024]{1,0:T(8,128)(2,1)S(1)} %get-tuple-element.63), channel_id=1, source_target_pairs={{0,4},{2,6},{4,0},{6,2},{1,5},{3,7},{5,1},{7,3},{8,12},{10,14},{12... | collective-permute-start | bytes 196616 | tf_op jit(solution)/shard_map/ppermute | solution.py:23
  71.6 17.7 %copy-start.9 = (bf16[32,1024]{1,0:T(8,128)(2,1)}, bf16[32,1024]{1,0:T(8,128)(2,1)S(1)}, u32[]{:S(2)}) copy-start(bf16[32,1024]{1,0:T(8,128)(2,1)S(1)} %collective-permute-done.19) | copy-start | bytes 196612
  71.6 24.5 %copy-start.11 = (bf16[32,1024]{1,0:T(8,128)(2,1)}, bf16[32,1024]{1,0:T(8,128)(2,1)S(1)}, u32[]{:S(2)}) copy-start(bf16[32,1024]{1,0:T(8,128)(2,1)S(1)} %collective-permute-done.18) | copy-start | bytes 196612
  78.0 11.3 %collective-permute-start.21 = (bf16[32,1024]{1,0:T(8,128)(2,1)S(1)}, bf16[32,1024]{1,0:T(8,128)(2,1)S(1)}, u32[]{:S(2)}, u32[]{:S(2)}) collective-permute-start(bf16[32,1024]{1,0:T(8,128)(2,1)S(1)} %get-tuple-element.14), channel_id=1, source_target_pairs={{0,8},{2,10},{4,12},{6,14},{8,16},{10,18},{12,20},{14,22},{16,24},... | collective-permute-start | bytes 196616 | tf_op jit(solution)/shard_map/ppermute | solution.py:34
  80.6 16.1 %collective-permute-start.29 = (bf16[128,2048]{1,0:T(8,128)(2,1)S(1)}, bf16[128,2048]{1,0:T(8,128)(2,1)S(1)}, u32[]{:S(2)}, u32[]{:S(2)}) collective-permute-start(bf16[128,2048]{1,0:T(8,128)(2,1)S(1)} %fusion.33), channel_id=1, source_target_pairs={{0,1},{1,0},{2,3},{3,2},{4,5},{5,4},{6,7},{7,6},{8,9},{9,8},{10,11... | collective-permute-start | bytes 1572872 | tf_op jit(solution)/shard_map/ppermute | solution.py:18
  82.4 12.9 %collective-permute-start.24 = (bf16[32,1024]{1,0:T(8,128)(2,1)S(1)}, bf16[32,1024]{1,0:T(8,128)(2,1)S(1)}, u32[]{:S(2)}, u32[]{:S(2)}) collective-permute-start(bf16[32,1024]{1,0:T(8,128)(2,1)S(1)} %get-tuple-element.14), channel_id=1, source_target_pairs={{0,14},{2,12},{4,10},{6,8},{8,22},{10,20},{12,18},{14,16},{16,30},... | collective-permute-start | bytes 196616 | tf_op jit(solution)/shard_map/ppermute | solution.py:34
  85.4 9.9 %collective-permute-start.23 = (bf16[32,1024]{1,0:T(8,128)(2,1)S(1)}, bf16[32,1024]{1,0:T(8,128)(2,1)S(1)}, u32[]{:S(2)}, u32[]{:S(2)}) collective-permute-start(bf16[32,1024]{1,0:T(8,128)(2,1)S(1)} %get-tuple-element.14), channel_id=1, source_target_pairs={{0,12},{2,14},{4,8},{6,10},{8,20},{10,22},{12,16},{14,18},{16,28},... | collective-permute-start | bytes 196616 | tf_op jit(solution)/shard_map/ppermute | solution.py:34
  87.3 7.9 %collective-permute-start.22 = (bf16[32,1024]{1,0:T(8,128)(2,1)S(1)}, bf16[32,1024]{1,0:T(8,128)(2,1)S(1)}, u32[]{:S(2)}, u32[]{:S(2)}) collective-permute-start(bf16[32,1024]{1,0:T(8,128)(2,1)S(1)} %get-tuple-element.14), channel_id=1, source_target_pairs={{0,10},{2,8},{4,14},{6,12},{8,18},{10,16},{12,22},{14,20},{16,26},... | collective-permute-start | bytes 196616 | tf_op jit(solution)/shard_map/ppermute | solution.py:34
  96.1 2.1 %collective-permute-start.25 = (bf16[128,2048]{1,0:T(8,128)(2,1)S(1)}, bf16[128,2048]{1,0:T(8,128)(2,1)S(1)}, u32[]{:S(2)}, u32[]{:S(2)}) collective-permute-start(bf16[128,2048]{1,0:T(8,128)(2,1)S(1)} %fusion.30), channel_id=1, source_target_pairs={{0,1},{1,0},{2,3},{3,2},{4,5},{5,4},{6,7},{7,6},{8,9},{9,8},{10,11... | collective-permute-start | bytes 1572872 | tf_op jit(solution)/shard_map/ppermute | solution.py:18
  101.9 4.3 %collective-permute-start.30 = (bf16[32,1024]{1,0:T(8,128)(2,1)}, bf16[32,1024]{1,0:T(8,128)(2,1)}, u32[]{:S(2)}, u32[]{:S(2)}) collective-permute-start(bf16[32,1024]{1,0:T(8,128)(2,1)} %get-tuple-element.55), channel_id=1, source_target_pairs={{0,2},{2,0},{4,6},{6,4},{1,3},{3,1},{5,7},{7,5},{8,10},{10,8},{12,... | collective-permute-start | bytes 196616 | tf_op jit(solution)/shard_map/ppermute | solution.py:23
  101.9 5.3 %collective-permute-start.32 = (bf16[32,1024]{1,0:T(8,128)(2,1)}, bf16[32,1024]{1,0:T(8,128)(2,1)}, u32[]{:S(2)}, u32[]{:S(2)}) collective-permute-start(bf16[32,1024]{1,0:T(8,128)(2,1)} %get-tuple-element.56), channel_id=1, source_target_pairs={{0,6},{2,4},{4,2},{6,0},{1,7},{3,5},{5,3},{7,1},{8,14},{10,12},{12... | collective-permute-start | bytes 196616 | tf_op jit(solution)/shard_map/ppermute | solution.py:23
  103.5 7.5 %collective-permute-start.31 = (bf16[32,1024]{1,0:T(8,128)(2,1)}, bf16[32,1024]{1,0:T(8,128)(2,1)}, u32[]{:S(2)}, u32[]{:S(2)}) collective-permute-start(bf16[32,1024]{1,0:T(8,128)(2,1)} %get-tuple-element.57), channel_id=1, source_target_pairs={{0,4},{2,6},{4,0},{6,2},{1,5},{3,7},{5,1},{7,3},{8,12},{10,14},{12... | collective-permute-start | bytes 196616 | tf_op jit(solution)/shard_map/ppermute | solution.py:23
  104.6 28.1 %copy-start.1 = (bf16[1,2048,1024]{2,1,0:T(8,128)(2,1)S(1)}, bf16[1,2048,1024]{2,1,0:T(8,128)(2,1)}, u32[]{:S(2)}) copy-start(bf16[1,2048,1024]{2,1,0:T(8,128)(2,1)} %param.12) | copy-start | bytes 12582916
  104.6 28.1 %copy-start.6 = (bf16[128,2048]{1,0:T(8,128)(2,1)S(1)}, bf16[128,2048]{1,0:T(8,128)(2,1)}, u32[]{:S(2)}) copy-start(bf16[128,2048]{1,0:T(8,128)(2,1)} %get-tuple-element.48) | copy-start | bytes 1572868
  104.6 7.4 %collective-permute-start.35 = (bf16[2,32,1024]{2,1,0:T(8,128)(2,1)S(1)}, bf16[2,32,1024]{2,1,0:T(8,128)(2,1)S(1)}, u32[]{:S(2)}, u32[]{:S(2)}) collective-permute-start(bf16[2,32,1024]{2,1,0:T(8,128)(2,1)S(1)} %slice_bitcast_fusion), channel_id=1, source_target_pairs={{24,30},{26,28},{28,26},{30,24},{25,31},{27,29},{29,27},{31,25}} | collective-permute-start | bytes 393224 | tf_op jit(solution)/shard_map/ppermute | solution.py:46
  105.4 6.6 %collective-permute-start.34 = (bf16[2,32,1024]{2,1,0:T(8,128)(2,1)S(1)}, bf16[2,32,1024]{2,1,0:T(8,128)(2,1)S(1)}, u32[]{:S(2)}, u32[]{:S(2)}) collective-permute-start(bf16[2,32,1024]{2,1,0:T(8,128)(2,1)S(1)} %slice_bitcast_fusion), channel_id=1, source_target_pairs={{24,28},{26,30},{28,24},{30,26},{25,29},{27,31},{29,25},{31,27}} | collective-permute-start | bytes 393224 | tf_op jit(solution)/shard_map/ppermute | solution.py:46
  106.2 5.8 %collective-permute-start.33 = (bf16[2,32,1024]{2,1,0:T(8,128)(2,1)S(1)}, bf16[2,32,1024]{2,1,0:T(8,128)(2,1)S(1)}, u32[]{:S(2)}, u32[]{:S(2)}) collective-permute-start(bf16[2,32,1024]{2,1,0:T(8,128)(2,1)S(1)} %slice_bitcast_fusion), channel_id=1, source_target_pairs={{24,26},{26,24},{28,30},{30,28},{25,27},{27,25},{29,31},{31,29}} | collective-permute-start | bytes 393224 | tf_op jit(solution)/shard_map/ppermute | solution.py:46
  112.0 10.1 %collective-permute-start.39 = (bf16[32,1024]{1,0:T(8,128)(2,1)S(1)}, bf16[32,1024]{1,0:T(8,128)(2,1)S(1)}, u32[]{:S(2)}, u32[]{:S(2)}) collective-permute-start(bf16[32,1024]{1,0:T(8,128)(2,1)S(1)} %add_convert_fusion.2), channel_id=1, source_target_pairs={{8,6},{10,4},{12,2},{14,0},{16,14},{18,12},{20,10},{22,8},{24,22},... | collective-permute-start | bytes 196616 | tf_op jit(solution)/shard_map/ppermute | solution.py:34
  116.2 8.8 %collective-permute-start.38 = (bf16[32,1024]{1,0:T(8,128)(2,1)S(1)}, bf16[32,1024]{1,0:T(8,128)(2,1)S(1)}, u32[]{:S(2)}, u32[]{:S(2)}) collective-permute-start(bf16[32,1024]{1,0:T(8,128)(2,1)S(1)} %add_convert_fusion.2), channel_id=1, source_target_pairs={{8,4},{10,6},{12,0},{14,2},{16,12},{18,14},{20,8},{22,10},{24,20},... | collective-permute-start | bytes 196616 | tf_op jit(solution)/shard_map/ppermute | solution.py:34
  118.1 8.2 %collective-permute-start.37 = (bf16[32,1024]{1,0:T(8,128)(2,1)S(1)}, bf16[32,1024]{1,0:T(8,128)(2,1)S(1)}, u32[]{:S(2)}, u32[]{:S(2)}) collective-permute-start(bf16[32,1024]{1,0:T(8,128)(2,1)S(1)} %add_convert_fusion.2), channel_id=1, source_target_pairs={{8,2},{10,0},{12,6},{14,4},{16,10},{18,8},{20,14},{22,12},{24,18},... | collective-permute-start | bytes 196616 | tf_op jit(solution)/shard_map/ppermute | solution.py:34
  120.0 7.4 %collective-permute-start.36 = (bf16[32,1024]{1,0:T(8,128)(2,1)S(1)}, bf16[32,1024]{1,0:T(8,128)(2,1)S(1)}, u32[]{:S(2)}, u32[]{:S(2)}) collective-permute-start(bf16[32,1024]{1,0:T(8,128)(2,1)S(1)} %add_convert_fusion.2), channel_id=1, source_target_pairs={{8,0},{10,2},{12,4},{14,6},{16,8},{18,10},{20,12},{22,14},{24,16},... | collective-permute-start | bytes 196616 | tf_op jit(solution)/shard_map/ppermute | solution.py:34
  131.1 5.0 %collective-permute-start.40 = (bf16[128,2048]{1,0:T(8,128)(2,1)S(1)}, bf16[128,2048]{1,0:T(8,128)(2,1)S(1)}, u32[]{:S(2)}, u32[]{:S(2)}) collective-permute-start(bf16[128,2048]{1,0:T(8,128)(2,1)S(1)} %fusion.36), channel_id=1, source_target_pairs={{0,1},{1,0},{2,3},{3,2},{4,5},{5,4},{6,7},{7,6},{8,9},{9,8},{10,11... | collective-permute-start | bytes 1572872 | tf_op jit(solution)/shard_map/ppermute | solution.py:18
  133.4 8.1 %collective-permute-start.26 = (bf16[32,1024]{1,0:T(8,128)(2,1)S(1)}, bf16[32,1024]{1,0:T(8,128)(2,1)S(1)}, u32[]{:S(2)}, u32[]{:S(2)}) collective-permute-start(bf16[32,1024]{1,0:T(8,128)(2,1)S(1)} %get-tuple-element.58), channel_id=1, source_target_pairs={{0,2},{2,0},{4,6},{6,4},{1,3},{3,1},{5,7},{7,5},{8,10},{10,8},{12,... | collective-permute-start | bytes 196616 | tf_op jit(solution)/shard_map/ppermute | solution.py:23
  134.1 7.4 %collective-permute-start.28 = (bf16[32,1024]{1,0:T(8,128)(2,1)S(1)}, bf16[32,1024]{1,0:T(8,128)(2,1)S(1)}, u32[]{:S(2)}, u32[]{:S(2)}) collective-permute-start(bf16[32,1024]{1,0:T(8,128)(2,1)S(1)} %get-tuple-element.59), channel_id=1, source_target_pairs={{0,6},{2,4},{4,2},{6,0},{1,7},{3,5},{5,3},{7,1},{8,14},{10,12},{12... | collective-permute-start | bytes 196616 | tf_op jit(solution)/shard_map/ppermute | solution.py:23
  135.8 15.1 %copy-start.13 = (bf16[32,1024]{1,0:T(8,128)(2,1)S(1)}, bf16[32,1024]{1,0:T(8,128)(2,1)}, u32[]{:S(2)}) copy-start(bf16[32,1024]{1,0:T(8,128)(2,1)} %get-tuple-element.44) | copy-start | bytes 196612
  135.8 15.1 %copy-start.14 = (bf16[32,1024]{1,0:T(8,128)(2,1)S(1)}, bf16[32,1024]{1,0:T(8,128)(2,1)}, u32[]{:S(2)}) copy-start(bf16[32,1024]{1,0:T(8,128)(2,1)} %get-tuple-element.42) | copy-start | bytes 196612
  135.8 7.3 %collective-permute-start.27 = (bf16[32,1024]{1,0:T(8,128)(2,1)S(1)}, bf16[32,1024]{1,0:T(8,128)(2,1)S(1)}, u32[]{:S(2)}, u32[]{:S(2)}) collective-permute-start(bf16[32,1024]{1,0:T(8,128)(2,1)S(1)} %get-tuple-element.60), channel_id=1, source_target_pairs={{0,4},{2,6},{4,0},{6,2},{1,5},{3,7},{5,1},{7,3},{8,12},{10,14},{12... | collective-permute-start | bytes 196616 | tf_op jit(solution)/shard_map/ppermute | solution.py:23
  138.2 28.8 %copy-start.12 = (bf16[32,1024]{1,0:T(8,128)(2,1)S(1)}, bf16[32,1024]{1,0:T(8,128)(2,1)}, u32[]{:S(2)}) copy-start(bf16[32,1024]{1,0:T(8,128)(2,1)} %copy-done.11) | copy-start | bytes 196612
  138.2 28.8 %copy-start.10 = (bf16[32,1024]{1,0:T(8,128)(2,1)S(1)}, bf16[32,1024]{1,0:T(8,128)(2,1)}, u32[]{:S(2)}) copy-start(bf16[32,1024]{1,0:T(8,128)(2,1)} %copy-done.9) | copy-start | bytes 196612
  138.2 5.0 %collective-permute-start.41 = (bf16[32,1024]{1,0:T(8,128)(2,1)S(1)}, bf16[32,1024]{1,0:T(8,128)(2,1)S(1)}, u32[]{:S(2)}, u32[]{:S(2)}) collective-permute-start(bf16[32,1024]{1,0:T(8,128)(2,1)S(1)} %get-tuple-element.52), channel_id=1, source_target_pairs={{0,2},{2,0},{4,6},{6,4},{1,3},{3,1},{5,7},{7,5},{8,10},{10,8},{12,... | collective-permute-start | bytes 196616 | tf_op jit(solution)/shard_map/ppermute | solution.py:23
  139.9 5.4 %collective-permute-start.43 = (bf16[32,1024]{1,0:T(8,128)(2,1)S(1)}, bf16[32,1024]{1,0:T(8,128)(2,1)S(1)}, u32[]{:S(2)}, u32[]{:S(2)}) collective-permute-start(bf16[32,1024]{1,0:T(8,128)(2,1)S(1)} %get-tuple-element.53), channel_id=1, source_target_pairs={{0,6},{2,4},{4,2},{6,0},{1,7},{3,5},{5,3},{7,1},{8,14},{10,12},{12... | collective-permute-start | bytes 196616 | tf_op jit(solution)/shard_map/ppermute | solution.py:23
  141.5 7.3 %collective-permute-start.42 = (bf16[32,1024]{1,0:T(8,128)(2,1)S(1)}, bf16[32,1024]{1,0:T(8,128)(2,1)S(1)}, u32[]{:S(2)}, u32[]{:S(2)}) collective-permute-start(bf16[32,1024]{1,0:T(8,128)(2,1)S(1)} %get-tuple-element.54), channel_id=1, source_target_pairs={{0,4},{2,6},{4,0},{6,2},{1,5},{3,7},{5,1},{7,3},{8,12},{10,14},{12... | collective-permute-start | bytes 196616 | tf_op jit(solution)/shard_map/ppermute | solution.py:23
  148.9 8.4 %collective-permute-start.44 = (bf16[32,1024]{1,0:T(8,128)(2,1)S(1)}, bf16[32,1024]{1,0:T(8,128)(2,1)S(1)}, u32[]{:S(2)}, u32[]{:S(2)}) collective-permute-start(bf16[32,1024]{1,0:T(8,128)(2,1)S(1)} %add_convert_fusion.1), channel_id=1, source_target_pairs={{8,0},{10,2},{12,4},{14,6},{16,8},{18,10},{20,12},{22,14},{24,16},... | collective-permute-start | bytes 196616 | tf_op jit(solution)/shard_map/ppermute | solution.py:34
  151.5 12.5 %collective-permute-start.47 = (bf16[32,1024]{1,0:T(8,128)(2,1)S(1)}, bf16[32,1024]{1,0:T(8,128)(2,1)S(1)}, u32[]{:S(2)}, u32[]{:S(2)}) collective-permute-start(bf16[32,1024]{1,0:T(8,128)(2,1)S(1)} %add_convert_fusion.1), channel_id=1, source_target_pairs={{8,6},{10,4},{12,2},{14,0},{16,14},{18,12},{20,10},{22,8},{24,22},... | collective-permute-start | bytes 196616 | tf_op jit(solution)/shard_map/ppermute | solution.py:34
  153.5 10.5 %collective-permute-start.46 = (bf16[32,1024]{1,0:T(8,128)(2,1)S(1)}, bf16[32,1024]{1,0:T(8,128)(2,1)S(1)}, u32[]{:S(2)}, u32[]{:S(2)}) collective-permute-start(bf16[32,1024]{1,0:T(8,128)(2,1)S(1)} %add_convert_fusion.1), channel_id=1, source_target_pairs={{8,4},{10,6},{12,0},{14,2},{16,12},{18,14},{20,8},{22,10},{24,20},... | collective-permute-start | bytes 196616 | tf_op jit(solution)/shard_map/ppermute | solution.py:34
  155.4 7.8 %collective-permute-start.45 = (bf16[32,1024]{1,0:T(8,128)(2,1)S(1)}, bf16[32,1024]{1,0:T(8,128)(2,1)S(1)}, u32[]{:S(2)}, u32[]{:S(2)}) collective-permute-start(bf16[32,1024]{1,0:T(8,128)(2,1)S(1)} %add_convert_fusion.1), channel_id=1, source_target_pairs={{8,2},{10,0},{12,6},{14,4},{16,10},{18,8},{20,14},{22,12},{24,18},... | collective-permute-start | bytes 196616 | tf_op jit(solution)/shard_map/ppermute | solution.py:34
  165.6 5.8 %collective-permute-start.48 = (bf16[128,2048]{1,0:T(8,128)(2,1)S(1)}, bf16[128,2048]{1,0:T(8,128)(2,1)S(1)}, u32[]{:S(2)}, u32[]{:S(2)}) collective-permute-start(bf16[128,2048]{1,0:T(8,128)(2,1)S(1)} %fusion.39), channel_id=1, source_target_pairs={{0,1},{1,0},{2,3},{3,2},{4,5},{5,4},{6,7},{7,6},{8,9},{9,8},{10,11... | collective-permute-start | bytes 1572872 | tf_op jit(solution)/shard_map/ppermute | solution.py:18
  173.5 7.1 %collective-permute-start.49 = (bf16[32,1024]{1,0:T(8,128)(2,1)S(1)}, bf16[32,1024]{1,0:T(8,128)(2,1)S(1)}, u32[]{:S(2)}, u32[]{:S(2)}) collective-permute-start(bf16[32,1024]{1,0:T(8,128)(2,1)S(1)} %get-tuple-element.49), channel_id=1, source_target_pairs={{0,2},{2,0},{4,6},{6,4},{1,3},{3,1},{5,7},{7,5},{8,10},{10,8},{12,... | collective-permute-start | bytes 196616 | tf_op jit(solution)/shard_map/ppermute | solution.py:23
  173.9 6.8 %collective-permute-start.51 = (bf16[32,1024]{1,0:T(8,128)(2,1)S(1)}, bf16[32,1024]{1,0:T(8,128)(2,1)S(1)}, u32[]{:S(2)}, u32[]{:S(2)}) collective-permute-start(bf16[32,1024]{1,0:T(8,128)(2,1)S(1)} %get-tuple-element.50), channel_id=1, source_target_pairs={{0,6},{2,4},{4,2},{6,0},{1,7},{3,5},{5,3},{7,1},{8,14},{10,12},{12... | collective-permute-start | bytes 196616 | tf_op jit(solution)/shard_map/ppermute | solution.py:23
  175.5 7.2 %collective-permute-start.50 = (bf16[32,1024]{1,0:T(8,128)(2,1)S(1)}, bf16[32,1024]{1,0:T(8,128)(2,1)S(1)}, u32[]{:S(2)}, u32[]{:S(2)}) collective-permute-start(bf16[32,1024]{1,0:T(8,128)(2,1)S(1)} %get-tuple-element.51), channel_id=1, source_target_pairs={{0,4},{2,6},{4,0},{6,2},{1,5},{3,7},{5,1},{7,3},{8,12},{10,14},{12... | collective-permute-start | bytes 196616 | tf_op jit(solution)/shard_map/ppermute | solution.py:23
  (6 other events, 23.3 us)

commit v4 on v2

v4 whole, which is shorter than its diff:
```python
import jax
import jax.numpy as jnp
from jax import lax
from jax.sharding import PartitionSpec as P

BF = jnp.bfloat16
F32 = jnp.float32
LAST = (((1,), (1,)), ((), ()))
FIRST = (((0,), (0,)), ((), ()))


def turn(block, axis, distance):
    size = lax.axis_size(axis)
    return lax.ppermute(block, axis, [(i, (i + distance) % size) for i in range(size)])


def near(block):
    size = lax.axis_size("row")
    return lax.ppermute(block, "row", [(i, i ^ 1) for i in range(size)])


def far(block, j):
    size = lax.axis_size("row")
    return lax.ppermute(block, "row", [(i, i ^ (2 * j)) for i in range(size)])


def far_count():
    return lax.axis_size("row") // 2


def half_of(block):
    return jnp.stack([far(block, j) if j else block for j in range(far_count())])


def hand_over(half, step):
    sections, size, count = lax.axis_size("section"), lax.axis_size("row"), far_count()
    there = [s for s in range(sections) if 0 <= s + step < sections]
    arrived = []
    for j in range(count):
        route = [(s * size + i, (s + step) * size + (i ^ (2 * j))) for s in there for i in range(size)]
        block = lax.ppermute(half, ("section", "row"), route)
        arrived.append(block if j == 0 else jnp.stack([block[k ^ j] for k in range(count)]))
    return arrived


def whole(half):
    rows = half.shape[0] * half.shape[1]
    half = half.reshape(rows, half.shape[2])
    return jnp.concatenate([half, near(half)], axis=0)


def near_sum(partial):
    rows = partial.shape[0] // 2
    total = partial[:rows].astype(F32) + near(partial[rows:]).astype(F32)
    return total.reshape(far_count(), rows // far_count(), partial.shape[1])


def after(block, other):
    return lax.optimization_barrier((block, other))[0]


def sum_cols(partial):
    size = lax.axis_size("col")
    if size > 2:
        return lax.psum(partial, "col").astype(F32)
    total = partial.astype(F32)
    for j in range(1, size):
        total = total + turn(partial, "col", j).astype(F32)
    return total


def silu_slope(value):
    sig = jax.nn.sigmoid(value)
    return sig * (1.0 + value * (1.0 - sig))


def pick(table, index):
    return lax.dynamic_index_in_dim(table, index, 0, keepdims=False)


def matmul(a, b, dims=(((1,), (0,)), ((), ()))):
    return lax.dot_general(a, b, dims, preferred_element_type=F32)


def per_device(inputs, sample_ids, send_base, recv_base, w_up, w_down, cotangent):
    section = lax.axis_index("section")
    sections = lax.axis_size("section")
    ticks = inputs.shape[1]
    up_block = w_up[0]
    down_block = w_down[0]
    samples = [pick(sample_ids, tick - section + sections - 1) for tick in range(ticks)]
    stored = [pick(send_base[0], samples[tick]).astype(F32) for tick in range(ticks - 1)]
    bases = [jnp.where(section == 0, inputs[0, t], pick(recv_base[0], samples[t])) for t in range(1, ticks)]
    cots = [cotangent[0, tick] for tick in range(ticks)]
    half = half_of(inputs[0, 0])
    known = half_of(after(jnp.stack(bases + cots), half))
    base_halves = [None] + [known[:, tick] for tick in range(ticks - 1)]
    cot_halves = [known[:, ticks - 1 + tick] for tick in range(ticks)]
    full_ins, pres, acts, seen_in, outs, out_rest = [], [], [], [], [], []
    for tick in range(ticks):
        if tick:
            half = base_halves[tick].astype(F32)
            for block in hand_over(sending, 1):
                half = half + block.astype(F32)
            half = half.astype(BF)
        full_in = whole(half)
        partial = matmul(full_in, up_block).astype(BF)
        if tick == 1:
            full_cot = whole(after(cot_halves[-1], partial))
        pre = sum_cols(partial)
        act = jax.nn.silu(pre).astype(BF)
        mixed = near_sum(matmul(act, down_block).astype(BF))
        out = half[0].astype(F32) + mixed[0]
        if tick < ticks - 1:
            sending = jnp.concatenate([(out - stored[tick])[None], mixed[1:]]).astype(BF)
        if tick == 1:
            first_grads = matmul(full_cot, down_block, LAST).astype(BF)
            sending = after(sending, first_grads)
        full_ins.append(full_in)
        pres.append(pre)
        acts.append(act)
        seen_in.append(half[0])
        outs.append(out)
        out_rest.append(mixed[1:].astype(BF))
    full_grads = [None] * ticks
    pre_grads = [None] * ticks
    grads = [None] * ticks
    grad_rest = [None] * ticks
    for step in range(ticks):
        tick = ticks - 1 - step
        if step == 0:
            half, full_grad, partial = cot_halves[tick], full_cot, first_grads
        else:
            half = sum(block.astype(F32) for block in hand_over(sending, -1)).astype(BF)
            half = jnp.where(section == sections - 1, cot_halves[tick], half)
            full_grad = whole(half)
            partial = matmul(full_grad, down_block, LAST).astype(BF)
        grad_act = sum_cols(partial)
        grad_pre = (grad_act * silu_slope(pres[tick])).astype(BF)
        back = matmul(grad_pre, up_block, LAST).astype(BF)
        returned = near_sum(back)
        grad = half[0].astype(F32) + returned[0]
        sending = jnp.concatenate([grad[None], returned[1:]]).astype(BF)
        full_grads[tick] = full_grad
        pre_grads[tick] = grad_pre
        grads[tick] = grad
        grad_rest[tick] = sending[1:]
        if step == 1:
            early = far_sum(outs, after(jnp.stack(out_rest), partial))
        if step == 2:
            late = far_sum(grads[1:], after(jnp.stack(grad_rest[1:]), partial))
    last = far_sum(grads[:1], jnp.stack(grad_rest[:1]))
    flat = [jnp.concatenate(parts, axis=0) for parts in (full_ins, pre_grads, acts, full_grads)]
    flat_in, flat_pre, flat_act, flat_grad = lax.optimization_barrier((*flat, back))[:4]
    grad_up = matmul(flat_in, flat_pre, FIRST)
    grad_down = matmul(flat_act, flat_grad, FIRST)
    return (
        jnp.stack(seen_in)[None],
        early[None],
        jnp.concatenate([last, late])[None],
        grad_up.astype(BF)[None],
        grad_down.astype(BF)[None],
    )


def far_sum(owns, rests):
    total = jnp.stack(owns)
    for j in range(1, far_count()):
        total = total + far(rests[:, j - 1], j).astype(F32)
    return total.astype(BF)


def solution(mesh):
    placed = (
        P("section", None, "row", "col"),
        P(),
        P("section", None, "row", "col"),
        P("section", None, "row", "col"),
        P("section", "col", "row"),
        P("section", "row", "col"),
        P("section", None, "row", "col"),
    )
    return jax.shard_map(
        per_device,
        mesh=mesh,
        in_specs=placed,
        out_specs=(
            P("section", None, "row", "col"),
            P("section", None, "row", "col"),
            P("section", None, "row", "col"),
            P("section", "col", "row"),
            P("section", "row", "col"),
        ),
        check_vma=False,
    )
```

time: 217 us -> 192 us (0.88)
  waiting for transfers between devices: 33.3 us -> 87.1 us
  blocking collectives: 40.8 us -> 0 us
  starting transfers between devices: 64 us -> 47.1 us
  matrix products: 44.8 us -> 30.7 us
  other arithmetic: 16.2 us -> 11.7 us
    ppermute x4 -> x25, waiting for transfers between devices: 8.32 us -> 84.5 us  [the longest x8 31.3 us: hand_over(): block = lax.ppermute(half, ('section', 'row'), route)]
    all_to_all x4 -> x0, blocking collectives: 40.8 us -> none  [the longest x3 30.8 us: gather_rows(): full = lax.all_to_all(copies, 'row', 0, 0)]
    all_to_all x8 -> x0, starting transfers between devices: 30.6 us -> none  [the longest x5 18.1 us: scatter_rows(): return lax.all_to_all(pieces, 'row', 0, 0).astype(F32).sum(axis=0)]
    ppermute x4 -> x25, starting transfers between devices: 10.7 us -> 33 us  [the longest x8 22.1 us: hand_over(): block = lax.ppermute(half, ('section', 'row'), route)]
    all_to_all x8 -> x0, waiting for transfers between devices: 18.1 us -> none  [the longest x5 14.1 us: scatter_rows(): return lax.all_to_all(pieces, 'row', 0, 0).astype(F32).sum(axis=0)]
    dot_general x14, matrix products: 44.8 us -> 30.7 us  [matmul(): return lax.dot_general(a, b, dims, preferred_element_type=F32)]
    ppermute x6, starting transfers between devices: 22.7 us -> 14.1 us  [turn(): lax.ppermute(block, axis, [(i, (i + distance) % size) for i in range(size)])]
    ppermute x6, waiting for transfers between devices: 6.91 us -> 2.69 us  [turn(): lax.ppermute(block, axis, [(i, (i + distance) % size) for i in range(size)])]
  transfers between devices with their start and end apart: 18 -> 31, of which waited for: 11 -> 22; matrix products, arithmetic and copies ran while one was open for 14% -> 12% of each run, Pallas kernels for 0% -> 0%
where the time goes in v4:
time: 192 us; the launch traced here: 191 us
  waiting for transfers between devices  87.1 us (45%)
  starting transfers between devices  47.1 us (25%)
  matrix products  30.7 us (16%)
  other arithmetic  11.7 us (6%)
  between operations  7.33 us (4%)
  local copies, waits for them, and re-layouts  7.18 us (4%)
    ppermute x8, waiting for transfers between devices, hand_over(): block = lax.ppermute(half, ('section', 'row'), route)  31.3 us
    dot_general x14, matrix products, matmul(): return lax.dot_general(a, b, dims, preferred_element_type=F32)  30.7 us
    ppermute x12, waiting for transfers between devices, near(): return lax.ppermute(block, 'row', [(i, i ^ 1) for i in range(size)])  30.4 us
    ppermute x5, waiting for transfers between devices, far(): return lax.ppermute(block, 'row', [(i, i ^ 2 * j) for i in range(size)])  22.8 us
    ppermute x8, starting transfers between devices, hand_over(): block = lax.ppermute(half, ('section', 'row'), route)  22.1 us
    ppermute x6, starting transfers between devices, turn(): lax.ppermute(block, axis, [(i, (i + distance) % size) for i in range(size)])  14.1 us
    ppermute x5, starting transfers between devices, far(): return lax.ppermute(block, 'row', [(i, i ^ 2 * j) for i in range(size)])  6.06 us
    ppermute x12, starting transfers between devices, near(): return lax.ppermute(block, 'row', [(i, i ^ 1) for i in range(size)])  4.82 us
  transfers between devices with their start and end apart: 31, of which 22 were waited for; matrix products, arithmetic and copies ran while one was open for 12% of the time, Pallas kernels for 0%

profile of v4, /device:TPU:3, one launch (start us, length us, event | category | flops | bytes accessed | tf_op | source)
XLA Modules:
  0.0 191.2 jit_solution(723704012428377370)
XLA Ops:
  0.7 0.9 slice_bitcast_fusion.6
  1.6 2.4 %collective-permute-start = (bf16[32,1024]{1,0:T(8,128)(2,1)S(1)}, bf16[32,1024]{1,0:T(8,128)(2,1)S(1)}, u32[]{:S(2)}, u32[]{:S(2)}) collective-permute-start(bf16[32,1024]{1,0:T(8,128)(2,1)S(1)} %get-tuple-element.42), channel_id=1, source_target_pairs={{0,4},{2,6},{4,0},{6,2},{1,5},{3,7},{5,1},{7,3},{8,12},{10,14},{12... | collective-permute-start | bytes 196616 | tf_op jit(solution)/shard_map/ppermute | solution.py:24
  3.9 1.7 collective-permute-done
  5.7 2.3 %collective-permute-start.2 = (bf16[64,1024]{1,0:T(8,128)(2,1)S(1)}, bf16[64,1024]{1,0:T(8,128)(2,1)S(1)}, u32[]{:S(2)}, u32[]{:S(2)}) collective-permute-start(bf16[64,1024]{1,0:T(8,128)(2,1)S(1)} %bitcast.210), channel_id=1, source_target_pairs={{0,2},{2,0},{4,6},{6,4},{1,3},{3,1},{5,7},{7,5},{8,10},{10,8},{12,... | collective-permute-start | bytes 393224 | tf_op jit(solution)/shard_map/ppermute | solution.py:19
  7.9 1.4 fusion.132
  11.9 2.9 %fusion.24 = bf16[128,2048]{1,0:T(8,128)(2,1)S(1)} fusion(bf16[1,1024,2048]{2,1,0:T(8,128)(2,1)} %param.11, bf16[64,1024]{1,0:T(8,128)(2,1)S(1)} %collective-permute-done.2, bf16[64,1024]{1,0:T(8,128)(2,1)S(1)} %bitcast.211), kind=kOutput, calls=%fused_computation.26 | convolution fusion | flops 537657344 | bytes 4980736 | tf_op jit(solution)/shard_map/dot_general | solution.py:82
  14.8 2.6 %collective-permute-start.3 = (bf16[128,2048]{1,0:T(8,128)(2,1)S(1)}, bf16[128,2048]{1,0:T(8,128)(2,1)S(1)}, u32[]{:S(2)}, u32[]{:S(2)}) collective-permute-start(bf16[128,2048]{1,0:T(8,128)(2,1)S(1)} %fusion.24), channel_id=1, source_target_pairs={{0,1},{1,0},{2,3},{3,2},{4,5},{5,4},{6,7},{7,6},{8,9},{9,8},{10,11... | collective-permute-start | bytes 1572872 | tf_op jit(solution)/shard_map/ppermute | solution.py:14
  17.5 0.9 bitcast_dynamic-update-slice_fusion.4
  22.2 0.9 bitcast_dynamic-update-slice_fusion.3
  23.4 3.1 %fusion.51 = bf16[128,1024]{1,0:T(8,128)(2,1)S(1)} fusion(bf16[128,2048]{1,0:T(8,128)(2,1)S(1)} %multiply_convert_fusion.5, bf16[1,2048,1024]{2,1,0:T(8,128)(2,1)} %param.12), kind=kOutput, calls=%fused_computation.37 | convolution fusion | flops 537001984 | bytes 4980736 | tf_op jit(solution)/shard_map/dot_general | solution.py:82
  26.7 5.0 %collective-permute-done.4 = bf16[64,1024]{1,0:T(8,128)(2,1)S(1)} collective-permute-done((bf16[64,1024]{1,0:T(8,128)(2,1)S(1)}, bf16[64,1024]{1,0:T(8,128)(2,1)S(1)}, u32[]{:S(2)}, u32[]{:S(2)}) %collective-permute-start.4) | collective-permute-done | bytes 131104 | tf_op jit(solution)/shard_map/ppermute | solution.py:19
  32.3 1.5 fusion.105
  33.9 4.7 %collective-permute-start.6 = (bf16[2,32,1024]{2,1,0:T(8,128)(2,1)S(1)}, bf16[2,32,1024]{2,1,0:T(8,128)(2,1)S(1)}, u32[]{:S(2)}, u32[]{:S(2)}) collective-permute-start(bf16[2,32,1024]{2,1,0:T(8,128)(2,1)S(1)} %pad_maximum_fusion.5), channel_id=1, source_target_pairs={{0,12},{2,14},{4,8},{6,10},{8,20},{10,22},{12,16},{14,18},{16,28},... | collective-permute-start | bytes 393224 | tf_op jit(solution)/shard_map/ppermute | solution.py:41
  39.2 3.1 %collective-permute-start.5 = (bf16[2,32,1024]{2,1,0:T(8,128)(2,1)S(1)}, bf16[2,32,1024]{2,1,0:T(8,128)(2,1)S(1)}, u32[]{:S(2)}, u32[]{:S(2)}) collective-permute-start(bf16[2,32,1024]{2,1,0:T(8,128)(2,1)S(1)} %pad_maximum_fusion.5), channel_id=1, source_target_pairs={{0,8},{2,10},{4,12},{6,14},{8,16},{10,18},{12,20},{14,22},{16,24},... | collective-permute-start | bytes 393224 | tf_op jit(solution)/shard_map/ppermute | solution.py:41
  42.3 10.4 %collective-permute-done.6 = bf16[2,32,1024]{2,1,0:T(8,128)(2,1)S(1)} collective-permute-done((bf16[2,32,1024]{2,1,0:T(8,128)(2,1)S(1)}, bf16[2,32,1024]{2,1,0:T(8,128)(2,1)S(1)}, u32[]{:S(2)}, u32[]{:S(2)}) %collective-permute-start.6) | collective-permute-done | bytes 131104 | tf_op jit(solution)/shard_map/ppermute | solution.py:41
  52.7 7.0 %collective-permute-done.1 = bf16[5,32,1024]{2,1,0:T(8,128)(2,1)S(1)} collective-permute-done((bf16[5,32,1024]{2,1,0:T(8,128)(2,1)S(1)}, bf16[5,32,1024]{2,1,0:T(8,128)(2,1)S(1)}, u32[]{:S(2)}, u32[]{:S(2)}) %collective-permute-start.1) | collective-permute-done | bytes 327712 | tf_op jit(solution)/shard_map/ppermute | solution.py:24
  59.9 4.5 %collective-permute-done.7 = bf16[64,1024]{1,0:T(8,128)(2,1)S(1)} collective-permute-done((bf16[64,1024]{1,0:T(8,128)(2,1)S(1)}, bf16[64,1024]{1,0:T(8,128)(2,1)S(1)}, u32[]{:S(2)}, u32[]{:S(2)}) %collective-permute-start.7) | collective-permute-done | bytes 131104 | tf_op jit(solution)/shard_map/ppermute | solution.py:19
  64.4 0.7 fusion.27
  65.1 1.4 collective-permute-start.8
  66.7 1.4 collective-permute-done.8
  68.1 0.8 copy-done.4
  69.2 0.7 fusion.54
  70.1 1.6 collective-permute-done.10
  71.8 2.3 %fusion.33 = bf16[128,2048]{1,0:T(8,128)(2,1)} fusion(bf16[1,2048,1024]{2,1,0:T(8,128)(2,1)S(1)} %copy-done, bf16[64,1024]{1,0:T(8,128)(2,1)S(1)} %collective-permute-done.10, bf16[64,1024]{1,0:T(8,128)(2,1)S(1)} %bitcast.214), kind=kOutput, calls=%fused_computation.29 | convolution fusion | flops 537657344 | bytes 4980736 | tf_op jit(solution)/shard_map/dot_general | solution.py:82
  75.4 1.5 fusion.103
  76.9 4.6 %collective-permute-start.12 = (bf16[2,32,1024]{2,1,0:T(8,128)(2,1)S(1)}, bf16[2,32,1024]{2,1,0:T(8,128)(2,1)S(1)}, u32[]{:S(2)}, u32[]{:S(2)}) collective-permute-start(bf16[2,32,1024]{2,1,0:T(8,128)(2,1)S(1)} %pad_maximum_fusion.6), channel_id=1, source_target_pairs={{0,12},{2,14},{4,8},{6,10},{8,20},{10,22},{12,16},{14,18},{16,28},... | collective-permute-start | bytes 393224 | tf_op jit(solution)/shard_map/ppermute | solution.py:41
  81.6 1.9 %collective-permute-start.11 = (bf16[2,32,1024]{2,1,0:T(8,128)(2,1)S(1)}, bf16[2,32,1024]{2,1,0:T(8,128)(2,1)S(1)}, u32[]{:S(2)}, u32[]{:S(2)}) collective-permute-start(bf16[2,32,1024]{2,1,0:T(8,128)(2,1)S(1)} %pad_maximum_fusion.6), channel_id=1, source_target_pairs={{0,8},{2,10},{4,12},{6,14},{8,16},{10,18},{12,20},{14,22},{16,24},... | collective-permute-start | bytes 393224 | tf_op jit(solution)/shard_map/ppermute | solution.py:41
  83.5 5.0 %collective-permute-done.12 = bf16[2,32,1024]{2,1,0:T(8,128)(2,1)S(1)} collective-permute-done((bf16[2,32,1024]{2,1,0:T(8,128)(2,1)S(1)}, bf16[2,32,1024]{2,1,0:T(8,128)(2,1)S(1)}, u32[]{:S(2)}, u32[]{:S(2)}) %collective-permute-start.12) | collective-permute-done | bytes 131104 | tf_op jit(solution)/shard_map/ppermute | solution.py:41
  88.5 2.9 %collective-permute-done.11 = bf16[2,32,1024]{2,1,0:T(8,128)(2,1)S(1)} collective-permute-done((bf16[2,32,1024]{2,1,0:T(8,128)(2,1)S(1)}, bf16[2,32,1024]{2,1,0:T(8,128)(2,1)S(1)}, u32[]{:S(2)}, u32[]{:S(2)}) %collective-permute-start.11) | collective-permute-done | bytes 131104 | tf_op jit(solution)/shard_map/ppermute | solution.py:41
  92.1 3.9 %collective-permute-done.13 = bf16[64,1024]{1,0:T(8,128)(2,1)S(1)} collective-permute-done((bf16[64,1024]{1,0:T(8,128)(2,1)S(1)}, bf16[64,1024]{1,0:T(8,128)(2,1)S(1)}, u32[]{:S(2)}, u32[]{:S(2)}) %collective-permute-start.13) | collective-permute-done | bytes 131104 | tf_op jit(solution)/shard_map/ppermute | solution.py:19
  96.0 1.5 fusion.30
  97.5 1.4 collective-permute-start.14
  98.9 0.9 constant_dynamic-update-slice_fusion.5
  99.9 0.9 constant_dynamic-update-slice_fusion.4
  100.8 2.2 %multiply_convert_fusion.2 = (bf16[128,2048]{1,0:T(8,128)(2,1)S(1)}, bf16[128,2048]{1,0:T(8,128)(2,1)S(1)}) fusion(bf16[128,2048]{1,0:T(8,128)(2,1)} %collective-permute-done.16, bf16[128,2048]{1,0:T(8,128)(2,1)} %fusion.33, bf16[128,2048]{1,0:T(8,128)(2,1)} %collective-permute-done.14, bf16[128,2048]{1,0:T(8,128)(2,1)} %fusion.30), kind=kLoop, calls=%fused_computation.42 | loop fusion | flops 4456448 | bytes 3145728 | tf_op jit(solution)/shard_map/convert_element_type | solution.py:139
  103.0 3.9 %fusion.42 = bf16[128,1024]{1,0:T(8,128)(2,1)S(1)} fusion(bf16[128,2048]{1,0:T(8,128)(2,1)S(1)} %get-tuple-element.29, bf16[1,1024,2048]{2,1,0:T(8,128)(2,1)} %param.11), kind=kOutput, calls=%fused_computation.34 | convolution fusion | flops 537001984 | bytes 4980736 | tf_op jit(solution)/shard_map/dot_general | solution.py:82
  107.1 0.7 maximum_bitcast_fusion
  107.8 4.0 %collective-permute-done.17 = bf16[64,1024]{1,0:T(8,128)(2,1)S(1)} collective-permute-done((bf16[64,1024]{1,0:T(8,128)(2,1)S(1)}, bf16[64,1024]{1,0:T(8,128)(2,1)S(1)}, u32[]{:S(2)}, u32[]{:S(2)}) %collective-permute-start.17) | collective-permute-done | bytes 131104 | tf_op jit(solution)/shard_map/ppermute | solution.py:19
  111.9 1.9 %collective-permute-start.19 = (bf16[2,32,1024]{2,1,0:T(8,128)(2,1)S(1)}, bf16[2,32,1024]{2,1,0:T(8,128)(2,1)S(1)}, u32[]{:S(2)}, u32[]{:S(2)}) collective-permute-start(bf16[2,32,1024]{2,1,0:T(8,128)(2,1)S(1)} %pad_maximum_fusion.7), channel_id=1, source_target_pairs={{8,4},{10,6},{12,0},{14,2},{16,12},{18,14},{20,8},{22,10},{24,20},... | collective-permute-start | bytes 393224 | tf_op jit(solution)/shard_map/ppermute | solution.py:41
  113.9 2.1 %collective-permute-start.18 = (bf16[2,32,1024]{2,1,0:T(8,128)(2,1)S(1)}, bf16[2,32,1024]{2,1,0:T(8,128)(2,1)S(1)}, u32[]{:S(2)}, u32[]{:S(2)}) collective-permute-start(bf16[2,32,1024]{2,1,0:T(8,128)(2,1)S(1)} %pad_maximum_fusion.7), channel_id=1, source_target_pairs={{8,0},{10,2},{12,4},{14,6},{16,8},{18,10},{20,12},{22,14},{24,16},... | collective-permute-start | bytes 393224 | tf_op jit(solution)/shard_map/ppermute | solution.py:41
  116.0 8.4 %collective-permute-done.19 = bf16[2,32,1024]{2,1,0:T(8,128)(2,1)S(1)} collective-permute-done((bf16[2,32,1024]{2,1,0:T(8,128)(2,1)S(1)}, bf16[2,32,1024]{2,1,0:T(8,128)(2,1)S(1)}, u32[]{:S(2)}, u32[]{:S(2)}) %collective-permute-start.19) | collective-permute-done | bytes 131104 | tf_op jit(solution)/shard_map/ppermute | solution.py:41
  124.9 0.7 fusion.57
  125.6 1.2 collective-permute-start.15
  126.8 1.5 collective-permute-done.20
  128.4 1.5 fusion.36
  129.9 3.6 %collective-permute-start.22 = (bf16[128,2048]{1,0:T(8,128)(2,1)S(1)}, bf16[128,2048]{1,0:T(8,128)(2,1)S(1)}, u32[]{:S(2)}, u32[]{:S(2)}) collective-permute-start(bf16[128,2048]{1,0:T(8,128)(2,1)S(1)} %fusion.36), channel_id=1, source_target_pairs={{0,1},{1,0},{2,3},{3,2},{4,5},{5,4},{6,7},{7,6},{8,9},{9,8},{10,11... | collective-permute-start | bytes 1572872 | tf_op jit(solution)/shard_map/ppermute | solution.py:14
  133.7 1.3 collective-permute-done.22
  135.6 1.5 fusion.45
  137.3 1.2 collective-permute-start.21
  138.5 5.1 %collective-permute-done.23 = bf16[64,1024]{1,0:T(8,128)(2,1)S(1)} collective-permute-done((bf16[64,1024]{1,0:T(8,128)(2,1)S(1)}, bf16[64,1024]{1,0:T(8,128)(2,1)S(1)}, u32[]{:S(2)}, u32[]{:S(2)}) %collective-permute-start.23) | collective-permute-done | bytes 131104 | tf_op jit(solution)/shard_map/ppermute | solution.py:19
  143.7 1.9 %collective-permute-start.25 = (bf16[2,32,1024]{2,1,0:T(8,128)(2,1)S(1)}, bf16[2,32,1024]{2,1,0:T(8,128)(2,1)S(1)}, u32[]{:S(2)}, u32[]{:S(2)}) collective-permute-start(bf16[2,32,1024]{2,1,0:T(8,128)(2,1)S(1)} %pad_maximum_fusion.8), channel_id=1, source_target_pairs={{8,4},{10,6},{12,0},{14,2},{16,12},{18,14},{20,8},{22,10},{24,20},... | collective-permute-start | bytes 393224 | tf_op jit(solution)/shard_map/ppermute | solution.py:41
  145.7 5.7 %collective-permute-done.21 = bf16[3,32,1024]{2,1,0:T(8,128)(2,1)S(1)} collective-permute-done((bf16[3,32,1024]{2,1,0:T(8,128)(2,1)S(1)}, bf16[3,32,1024]{2,1,0:T(8,128)(2,1)S(1)}, u32[]{:S(2)}, u32[]{:S(2)}) %collective-permute-start.21) | collective-permute-done | bytes 196640 | tf_op jit(solution)/shard_map/ppermute | solution.py:24
  151.4 0.7 fusion.84
  152.1 1.9 collective-permute-start.24
  154.0 1.0 collective-permute-done.25
  155.0 3.6 %collective-permute-done.24 = bf16[2,32,1024]{2,1,0:T(8,128)(2,1)S(1)} collective-permute-done((bf16[2,32,1024]{2,1,0:T(8,128)(2,1)S(1)}, bf16[2,32,1024]{2,1,0:T(8,128)(2,1)S(1)}, u32[]{:S(2)}, u32[]{:S(2)}) %collective-permute-start.24) | collective-permute-done | bytes 131104 | tf_op jit(solution)/shard_map/ppermute | solution.py:41
  158.9 3.8 %collective-permute-done.26 = bf16[64,1024]{1,0:T(8,128)(2,1)S(1)} collective-permute-done((bf16[64,1024]{1,0:T(8,128)(2,1)S(1)}, bf16[64,1024]{1,0:T(8,128)(2,1)S(1)}, u32[]{:S(2)}, u32[]{:S(2)}) %collective-permute-start.26) | collective-permute-done | bytes 131104 | tf_op jit(solution)/shard_map/ppermute | solution.py:19
  162.6 1.5 fusion.39
  164.1 4.5 %collective-permute-start.27 = (bf16[128,2048]{1,0:T(8,128)(2,1)S(1)}, bf16[128,2048]{1,0:T(8,128)(2,1)S(1)}, u32[]{:S(2)}, u32[]{:S(2)}) collective-permute-start(bf16[128,2048]{1,0:T(8,128)(2,1)S(1)} %fusion.39), channel_id=1, source_target_pairs={{0,1},{1,0},{2,3},{3,2},{4,5},{5,4},{6,7},{7,6},{8,9},{9,8},{10,11... | collective-permute-start | bytes 1572872 | tf_op jit(solution)/shard_map/ppermute | solution.py:14
  168.9 8.4 %collective-permute-done.30 = bf16[2,32,1024]{2,1,0:T(8,128)(2,1)S(1)} collective-permute-done((bf16[2,32,1024]{2,1,0:T(8,128)(2,1)S(1)}, bf16[2,32,1024]{2,1,0:T(8,128)(2,1)S(1)}, u32[]{:S(2)}, u32[]{:S(2)}) %collective-permute-start.30) | collective-permute-done | bytes 131104 | tf_op jit(solution)/shard_map/ppermute | solution.py:24
  177.9 1.5 fusion.48
  179.6 4.4 %convert_bitcast_fusion.1 = bf16[1,1024,2048]{2,1,0:T(8,128)(2,1)} fusion(bf16[384,1024]{1,0:T(8,128)(2,1)S(1)} %constant_dynamic-update-slice_fusion, bf16[384,2048]{1,0:T(8,128)(2,1)S(1)} %pad_maximum_fusion), kind=kOutput, calls=%fused_computation.25 | convolution fusion | flops 1612709888 | bytes 6553600 | tf_op jit(solution)/shard_map/dot_general | solution.py:82
  184.3 1.7 collective-permute-start.29
  186.0 4.4 %convert_bitcast_fusion = bf16[1,2048,1024]{2,1,0:T(8,128)(2,1)} fusion(bf16[384,2048]{1,0:T(8,128)(2,1)S(1)} %pad_maximum_fusion.1, bf16[384,1024]{1,0:T(8,128)(2,1)S(1)} %constant_dynamic-update-slice_fusion.6), kind=kOutput, calls=%fused_computation.24 | convolution fusion | flops 1612709888 | bytes 6553600 | tf_op jit(solution)/shard_map/dot_general | solution.py:82
  (132 shorter events, 9.2 us)
Async XLA Ops:
  0.6 16.8 %copy-start.20 = (bf16[1,3,32,1024]{3,2,1,0:T(8,128)(2,1)S(1)}, bf16[1,3,32,1024]{3,2,1,0:T(8,128)(2,1)}, u32[]{:S(2)}) copy-start(bf16[1,3,32,1024]{3,2,1,0:T(8,128)(2,1)} %param.7) | copy-start | bytes 589828
  0.6 22.4 %copy-start.23 = (bf16[1,3,32,1024]{3,2,1,0:T(8,128)(2,1)S(1)}, bf16[1,3,32,1024]{3,2,1,0:T(8,128)(2,1)}, u32[]{:S(2)}) copy-start(bf16[1,3,32,1024]{3,2,1,0:T(8,128)(2,1)} %param.13) | copy-start | bytes 589828
  1.6 9.7 %copy-start.9 = (bf16[1,32,1024]{2,1,0:T(8,128)(2,1)}, bf16[1,32,1024]{2,1,0:T(8,128)(2,1)S(1)}, u32[]{:S(2)}) copy-start(bf16[1,32,1024]{2,1,0:T(8,128)(2,1)S(1)} %get-tuple-element.41) | copy-start | bytes 196612
  1.6 4.1 %collective-permute-start = (bf16[32,1024]{1,0:T(8,128)(2,1)S(1)}, bf16[32,1024]{1,0:T(8,128)(2,1)S(1)}, u32[]{:S(2)}, u32[]{:S(2)}) collective-permute-start(bf16[32,1024]{1,0:T(8,128)(2,1)S(1)} %get-tuple-element.42), channel_id=1, source_target_pairs={{0,4},{2,6},{4,0},{6,2},{1,5},{3,7},{5,1},{7,3},{8,12},{10,14},{12... | collective-permute-start | bytes 196616 | tf_op jit(solution)/shard_map/ppermute | solution.py:24
  5.7 5.6 %copy-start.6 = (bf16[2,32,1024]{2,1,0:T(8,128)(2,1)}, bf16[2,32,1024]{2,1,0:T(8,128)(2,1)S(1)}, u32[]{:S(2)}) copy-start(bf16[2,32,1024]{2,1,0:T(8,128)(2,1)S(1)} %pad_maximum_fusion.4) | copy-start | bytes 393220
  5.7 5.6 %collective-permute-start.2 = (bf16[64,1024]{1,0:T(8,128)(2,1)S(1)}, bf16[64,1024]{1,0:T(8,128)(2,1)S(1)}, u32[]{:S(2)}, u32[]{:S(2)}) collective-permute-start(bf16[64,1024]{1,0:T(8,128)(2,1)S(1)} %bitcast.210), channel_id=1, source_target_pairs={{0,2},{2,0},{4,6},{6,4},{1,3},{3,1},{5,7},{7,5},{8,10},{10,8},{12,... | collective-permute-start | bytes 393224 | tf_op jit(solution)/shard_map/ppermute | solution.py:19
  11.3 0.6 copy-start.13
  14.8 8.2 %collective-permute-start.3 = (bf16[128,2048]{1,0:T(8,128)(2,1)S(1)}, bf16[128,2048]{1,0:T(8,128)(2,1)S(1)}, u32[]{:S(2)}, u32[]{:S(2)}) collective-permute-start(bf16[128,2048]{1,0:T(8,128)(2,1)S(1)} %fusion.24), channel_id=1, source_target_pairs={{0,1},{1,0},{2,3},{3,2},{4,5},{5,4},{6,7},{7,6},{8,9},{9,8},{10,11... | collective-permute-start | bytes 1572872 | tf_op jit(solution)/shard_map/ppermute | solution.py:14
  23.4 41.0 %copy-start.2 = (bf16[1,1024,2048]{2,1,0:T(8,128)(2,1)S(1)}, bf16[1,1024,2048]{2,1,0:T(8,128)(2,1)}, u32[]{:S(2)}) copy-start(bf16[1,1024,2048]{2,1,0:T(8,128)(2,1)} %param.11) | copy-start | bytes 12582916
  26.5 5.2 %collective-permute-start.4 = (bf16[64,1024]{1,0:T(8,128)(2,1)S(1)}, bf16[64,1024]{1,0:T(8,128)(2,1)S(1)}, u32[]{:S(2)}, u32[]{:S(2)}) collective-permute-start(bf16[64,1024]{1,0:T(8,128)(2,1)S(1)} %slice.236), channel_id=1, source_target_pairs={{0,2},{2,0},{4,6},{6,4},{1,3},{3,1},{5,7},{7,5},{8,10},{10,8},{12,... | collective-permute-start | bytes 393224 | tf_op jit(solution)/shard_map/ppermute | solution.py:19
  33.9 18.8 %collective-permute-start.6 = (bf16[2,32,1024]{2,1,0:T(8,128)(2,1)S(1)}, bf16[2,32,1024]{2,1,0:T(8,128)(2,1)S(1)}, u32[]{:S(2)}, u32[]{:S(2)}) collective-permute-start(bf16[2,32,1024]{2,1,0:T(8,128)(2,1)S(1)} %pad_maximum_fusion.5), channel_id=1, source_target_pairs={{0,12},{2,14},{4,8},{6,10},{8,20},{10,22},{12,16},{14,18},{16,28},... | collective-permute-start | bytes 393224 | tf_op jit(solution)/shard_map/ppermute | solution.py:41
  38.6 21.1 %collective-permute-start.1 = (bf16[5,32,1024]{2,1,0:T(8,128)(2,1)S(1)}, bf16[5,32,1024]{2,1,0:T(8,128)(2,1)S(1)}, u32[]{:S(2)}, u32[]{:S(2)}) collective-permute-start(bf16[5,32,1024]{2,1,0:T(8,128)(2,1)S(1)} %bitcast_dynamic-update-slice_fusion), channel_id=1, source_target_pairs={{0,4},{2,6},{4,0},{6,2},{1,5},{3,7},{5,1},{7,3},{8,12},{10,14},{12... | collective-permute-start | bytes 983048 | tf_op jit(solution)/shard_map/ppermute | solution.py:24
  39.2 20.5 %collective-permute-start.5 = (bf16[2,32,1024]{2,1,0:T(8,128)(2,1)S(1)}, bf16[2,32,1024]{2,1,0:T(8,128)(2,1)S(1)}, u32[]{:S(2)}, u32[]{:S(2)}) collective-permute-start(bf16[2,32,1024]{2,1,0:T(8,128)(2,1)S(1)} %pad_maximum_fusion.5), channel_id=1, source_target_pairs={{0,8},{2,10},{4,12},{6,14},{8,16},{10,18},{12,20},{14,22},{16,24},... | collective-permute-start | bytes 393224 | tf_op jit(solution)/shard_map/ppermute | solution.py:41
  59.7 9.5 %copy-start = (bf16[1,2048,1024]{2,1,0:T(8,128)(2,1)S(1)}, bf16[1,2048,1024]{2,1,0:T(8,128)(2,1)}, u32[]{:S(2)}) copy-start(bf16[1,2048,1024]{2,1,0:T(8,128)(2,1)} %param.12) | copy-start | bytes 12582916
  59.8 4.6 %collective-permute-start.7 = (bf16[64,1024]{1,0:T(8,128)(2,1)S(1)}, bf16[64,1024]{1,0:T(8,128)(2,1)S(1)}, u32[]{:S(2)}, u32[]{:S(2)}) collective-permute-start(bf16[64,1024]{1,0:T(8,128)(2,1)S(1)} %bitcast.201), channel_id=1, source_target_pairs={{0,2},{2,0},{4,6},{6,4},{1,3},{3,1},{5,7},{7,5},{8,10},{10,8},{12,... | collective-permute-start | bytes 393224 | tf_op jit(solution)/shard_map/ppermute | solution.py:19
  64.4 2.2 %copy-start.14 = (bf16[64,1024]{1,0:T(8,128)(2,1)}, bf16[64,1024]{1,0:T(8,128)(2,1)S(1)}, u32[]{:S(2)}) copy-start(bf16[64,1024]{1,0:T(8,128)(2,1)S(1)} %collective-permute-done.7) | copy-start | bytes 393220
  65.1 2.9 %collective-permute-start.8 = (bf16[128,2048]{1,0:T(8,128)(2,1)S(1)}, bf16[128,2048]{1,0:T(8,128)(2,1)S(1)}, u32[]{:S(2)}, u32[]{:S(2)}) collective-permute-start(bf16[128,2048]{1,0:T(8,128)(2,1)S(1)} %fusion.27), channel_id=1, source_target_pairs={{0,1},{1,0},{2,3},{3,2},{4,5},{5,4},{6,7},{7,6},{8,9},{9,8},{10,11... | collective-permute-start | bytes 1572872 | tf_op jit(solution)/shard_map/ppermute | solution.py:14
  66.6 24.8 %copy-start.7 = (bf16[2,32,1024]{2,1,0:T(8,128)(2,1)}, bf16[2,32,1024]{2,1,0:T(8,128)(2,1)S(1)}, u32[]{:S(2)}) copy-start(bf16[2,32,1024]{2,1,0:T(8,128)(2,1)S(1)} %fusion.94) | copy-start | bytes 393220
  66.6 5.2 %collective-permute-start.10 = (bf16[64,1024]{1,0:T(8,128)(2,1)S(1)}, bf16[64,1024]{1,0:T(8,128)(2,1)S(1)}, u32[]{:S(2)}, u32[]{:S(2)}) collective-permute-start(bf16[64,1024]{1,0:T(8,128)(2,1)S(1)} %bitcast.213), channel_id=1, source_target_pairs={{0,2},{2,0},{4,6},{6,4},{1,3},{3,1},{5,7},{7,5},{8,10},{10,8},{12,... | collective-permute-start | bytes 393224 | tf_op jit(solution)/shard_map/ppermute | solution.py:19
  68.1 0.8 copy-start.4
  70.0 4.8 %collective-permute-start.9 = (bf16[64,1024]{1,0:T(8,128)(2,1)S(1)}, bf16[64,1024]{1,0:T(8,128)(2,1)S(1)}, u32[]{:S(2)}, u32[]{:S(2)}) collective-permute-start(bf16[64,1024]{1,0:T(8,128)(2,1)S(1)} %slice.245), channel_id=1, source_target_pairs={{0,2},{2,0},{4,6},{6,4},{1,3},{3,1},{5,7},{7,5},{8,10},{10,8},{12,... | collective-permute-start | bytes 393224 | tf_op jit(solution)/shard_map/ppermute | solution.py:19
  71.8 25.8 %copy-start.11 = (bf16[64,1024]{1,0:T(8,128)(2,1)}, bf16[64,1024]{1,0:T(8,128)(2,1)S(1)}, u32[]{:S(2)}) copy-start(bf16[64,1024]{1,0:T(8,128)(2,1)S(1)} %collective-permute-done.10) | copy-start | bytes 393220
  76.9 11.5 %collective-permute-start.12 = (bf16[2,32,1024]{2,1,0:T(8,128)(2,1)S(1)}, bf16[2,32,1024]{2,1,0:T(8,128)(2,1)S(1)}, u32[]{:S(2)}, u32[]{:S(2)}) collective-permute-start(bf16[2,32,1024]{2,1,0:T(8,128)(2,1)S(1)} %pad_maximum_fusion.6), channel_id=1, source_target_pairs={{0,12},{2,14},{4,8},{6,10},{8,20},{10,22},{12,16},{14,18},{16,28},... | collective-permute-start | bytes 393224 | tf_op jit(solution)/shard_map/ppermute | solution.py:41
  81.6 9.8 %collective-permute-start.11 = (bf16[2,32,1024]{2,1,0:T(8,128)(2,1)S(1)}, bf16[2,32,1024]{2,1,0:T(8,128)(2,1)S(1)}, u32[]{:S(2)}, u32[]{:S(2)}) collective-permute-start(bf16[2,32,1024]{2,1,0:T(8,128)(2,1)S(1)} %pad_maximum_fusion.6), channel_id=1, source_target_pairs={{0,8},{2,10},{4,12},{6,14},{8,16},{10,18},{12,20},{14,22},{16,24},... | collective-permute-start | bytes 393224 | tf_op jit(solution)/shard_map/ppermute | solution.py:41
  91.4 4.6 %collective-permute-start.13 = (bf16[64,1024]{1,0:T(8,128)(2,1)S(1)}, bf16[64,1024]{1,0:T(8,128)(2,1)S(1)}, u32[]{:S(2)}, u32[]{:S(2)}) collective-permute-start(bf16[64,1024]{1,0:T(8,128)(2,1)S(1)} %bitcast.198), channel_id=1, source_target_pairs={{0,2},{2,0},{4,6},{6,4},{1,3},{3,1},{5,7},{7,5},{8,10},{10,8},{12,... | collective-permute-start | bytes 393224 | tf_op jit(solution)/shard_map/ppermute | solution.py:19
  91.5 9.3 %collective-permute-start.16 = (bf16[128,2048]{1,0:T(8,128)(2,1)}, bf16[128,2048]{1,0:T(8,128)(2,1)}, u32[]{:S(2)}, u32[]{:S(2)}) collective-permute-start(bf16[128,2048]{1,0:T(8,128)(2,1)} %fusion.33), channel_id=1, source_target_pairs={{0,1},{1,0},{2,3},{3,2},{4,5},{5,4},{6,7},{7,6},{8,9},{9,8},{10,11... | collective-permute-start | bytes 1572872 | tf_op jit(solution)/shard_map/ppermute | solution.py:14
  96.0 1.5 copy-start.16
  97.5 3.3 %collective-permute-start.14 = (bf16[128,2048]{1,0:T(8,128)(2,1)}, bf16[128,2048]{1,0:T(8,128)(2,1)}, u32[]{:S(2)}, u32[]{:S(2)}) collective-permute-start(bf16[128,2048]{1,0:T(8,128)(2,1)} %fusion.30), channel_id=1, source_target_pairs={{0,1},{1,0},{2,3},{3,2},{4,5},{5,4},{6,7},{7,6},{8,9},{9,8},{10,11... | collective-permute-start | bytes 1572872 | tf_op jit(solution)/shard_map/ppermute | solution.py:14
  100.8 6.2 %copy-start.15 = (bf16[64,1024]{1,0:T(8,128)(2,1)S(1)}, bf16[64,1024]{1,0:T(8,128)(2,1)}, u32[]{:S(2)}) copy-start(bf16[64,1024]{1,0:T(8,128)(2,1)} %copy-done.14) | copy-start | bytes 393220
  100.8 6.3 %copy-start.10 = (bf16[1,32,1024]{2,1,0:T(8,128)(2,1)S(1)}, bf16[1,32,1024]{2,1,0:T(8,128)(2,1)}, u32[]{:S(2)}) copy-start(bf16[1,32,1024]{2,1,0:T(8,128)(2,1)} %copy-done.9) | copy-start | bytes 196612
  103.0 10.8 %copy-start.17 = (bf16[64,1024]{1,0:T(8,128)(2,1)S(1)}, bf16[64,1024]{1,0:T(8,128)(2,1)}, u32[]{:S(2)}) copy-start(bf16[64,1024]{1,0:T(8,128)(2,1)} %copy-done.16) | copy-start | bytes 393220
  103.0 21.9 %copy-start.1 = (bf16[1,2048,1024]{2,1,0:T(8,128)(2,1)S(1)}, bf16[1,2048,1024]{2,1,0:T(8,128)(2,1)}, u32[]{:S(2)}) copy-start(bf16[1,2048,1024]{2,1,0:T(8,128)(2,1)} %param.12) | copy-start | bytes 12582916
  106.9 4.9 %collective-permute-start.17 = (bf16[64,1024]{1,0:T(8,128)(2,1)S(1)}, bf16[64,1024]{1,0:T(8,128)(2,1)S(1)}, u32[]{:S(2)}, u32[]{:S(2)}) collective-permute-start(bf16[64,1024]{1,0:T(8,128)(2,1)S(1)} %slice.261), channel_id=1, source_target_pairs={{0,2},{2,0},{4,6},{6,4},{1,3},{3,1},{5,7},{7,5},{8,10},{10,8},{12,... | collective-permute-start | bytes 393224 | tf_op jit(solution)/shard_map/ppermute | solution.py:19
  111.9 12.5 %collective-permute-start.19 = (bf16[2,32,1024]{2,1,0:T(8,128)(2,1)S(1)}, bf16[2,32,1024]{2,1,0:T(8,128)(2,1)S(1)}, u32[]{:S(2)}, u32[]{:S(2)}) collective-permute-start(bf16[2,32,1024]{2,1,0:T(8,128)(2,1)S(1)} %pad_maximum_fusion.7), channel_id=1, source_target_pairs={{8,4},{10,6},{12,0},{14,2},{16,12},{18,14},{20,8},{22,10},{24,20},... | collective-permute-start | bytes 393224 | tf_op jit(solution)/shard_map/ppermute | solution.py:41
  113.9 10.5 %collective-permute-start.18 = (bf16[2,32,1024]{2,1,0:T(8,128)(2,1)S(1)}, bf16[2,32,1024]{2,1,0:T(8,128)(2,1)S(1)}, u32[]{:S(2)}, u32[]{:S(2)}) collective-permute-start(bf16[2,32,1024]{2,1,0:T(8,128)(2,1)S(1)} %pad_maximum_fusion.7), channel_id=1, source_target_pairs={{8,0},{10,2},{12,4},{14,6},{16,8},{18,10},{20,12},{22,14},{24,16},... | collective-permute-start | bytes 393224 | tf_op jit(solution)/shard_map/ppermute | solution.py:41
  124.5 3.9 %collective-permute-start.20 = (bf16[64,1024]{1,0:T(8,128)(2,1)S(1)}, bf16[64,1024]{1,0:T(8,128)(2,1)S(1)}, u32[]{:S(2)}, u32[]{:S(2)}) collective-permute-start(bf16[64,1024]{1,0:T(8,128)(2,1)S(1)} %bitcast.204), channel_id=1, source_target_pairs={{0,2},{2,0},{4,6},{6,4},{1,3},{3,1},{5,7},{7,5},{8,10},{10,8},{12,... | collective-permute-start | bytes 393224 | tf_op jit(solution)/shard_map/ppermute | solution.py:19
  125.6 9.4 %copy-start.5 = (bf16[128,2048]{1,0:T(8,128)(2,1)S(1)}, bf16[128,2048]{1,0:T(8,128)(2,1)}, u32[]{:S(2)}) copy-start(bf16[128,2048]{1,0:T(8,128)(2,1)} %copy-done.4) | copy-start | bytes 1572868
  125.6 7.9 %collective-permute-start.15 = (bf16[64,1024]{1,0:T(8,128)(2,1)S(1)}, bf16[64,1024]{1,0:T(8,128)(2,1)S(1)}, u32[]{:S(2)}, u32[]{:S(2)}) collective-permute-start(bf16[64,1024]{1,0:T(8,128)(2,1)S(1)} %slice.254), channel_id=1, source_target_pairs={{0,2},{2,0},{4,6},{6,4},{1,3},{3,1},{5,7},{7,5},{8,10},{10,8},{12,... | collective-permute-start | bytes 393224 | tf_op jit(solution)/shard_map/ppermute | solution.py:19
  129.9 5.7 %copy-start.3 = (bf16[1,1024,2048]{2,1,0:T(8,128)(2,1)S(1)}, bf16[1,1024,2048]{2,1,0:T(8,128)(2,1)}, u32[]{:S(2)}) copy-start(bf16[1,1024,2048]{2,1,0:T(8,128)(2,1)} %param.11) | copy-start | bytes 12582916
  129.9 5.1 %collective-permute-start.22 = (bf16[128,2048]{1,0:T(8,128)(2,1)S(1)}, bf16[128,2048]{1,0:T(8,128)(2,1)S(1)}, u32[]{:S(2)}, u32[]{:S(2)}) collective-permute-start(bf16[128,2048]{1,0:T(8,128)(2,1)S(1)} %fusion.36), channel_id=1, source_target_pairs={{0,1},{1,0},{2,3},{3,2},{4,5},{5,4},{6,7},{7,6},{8,9},{9,8},{10,11... | collective-permute-start | bytes 1572872 | tf_op jit(solution)/shard_map/ppermute | solution.py:14
  133.6 3.6 %copy-start.21 = (bf16[1,1,32,1024]{3,2,1,0:T(8,128)(2,1)S(1)}, bf16[1,1,32,1024]{3,2,1,0:T(8,128)(2,1)}, u32[]{:S(2)}) copy-start(bf16[1,1,32,1024]{3,2,1,0:T(8,128)(2,1)} %get-tuple-element.37) | copy-start | bytes 196612
  133.6 3.6 %copy-start.22 = (bf16[1,1,32,1024]{3,2,1,0:T(8,128)(2,1)S(1)}, bf16[1,1,32,1024]{3,2,1,0:T(8,128)(2,1)}, u32[]{:S(2)}) copy-start(bf16[1,1,32,1024]{3,2,1,0:T(8,128)(2,1)} %get-tuple-element.39) | copy-start | bytes 196612
  135.5 15.8 %copy-start.18 = (f32[1,32,1024]{2,1,0:T(8,128)S(1)}, f32[1,32,1024]{2,1,0:T(8,128)}, u32[]{:S(2)}) copy-start(f32[1,32,1024]{2,1,0:T(8,128)} %get-tuple-element.31) | copy-start | bytes 393220
  135.6 15.8 %copy-start.19 = (f32[1,32,1024]{2,1,0:T(8,128)S(1)}, f32[1,32,1024]{2,1,0:T(8,128)}, u32[]{:S(2)}) copy-start(f32[1,32,1024]{2,1,0:T(8,128)} %get-tuple-element.28) | copy-start | bytes 393220
  137.1 6.5 %collective-permute-start.23 = (bf16[64,1024]{1,0:T(8,128)(2,1)S(1)}, bf16[64,1024]{1,0:T(8,128)(2,1)S(1)}, u32[]{:S(2)}, u32[]{:S(2)}) collective-permute-start(bf16[64,1024]{1,0:T(8,128)(2,1)S(1)} %slice.268), channel_id=1, source_target_pairs={{0,2},{2,0},{4,6},{6,4},{1,3},{3,1},{5,7},{7,5},{8,10},{10,8},{12,... | collective-permute-start | bytes 393224 | tf_op jit(solution)/shard_map/ppermute | solution.py:19
  137.3 14.1 %collective-permute-start.21 = (bf16[3,32,1024]{2,1,0:T(8,128)(2,1)S(1)}, bf16[3,32,1024]{2,1,0:T(8,128)(2,1)S(1)}, u32[]{:S(2)}, u32[]{:S(2)}) collective-permute-start(bf16[3,32,1024]{2,1,0:T(8,128)(2,1)S(1)} %bitcast.216), channel_id=1, source_target_pairs={{0,4},{2,6},{4,0},{6,2},{1,5},{3,7},{5,1},{7,3},{8,12},{10,14},{12... | collective-permute-start | bytes 589832 | tf_op jit(solution)/shard_map/ppermute | solution.py:24
  143.7 11.3 %collective-permute-start.25 = (bf16[2,32,1024]{2,1,0:T(8,128)(2,1)S(1)}, bf16[2,32,1024]{2,1,0:T(8,128)(2,1)S(1)}, u32[]{:S(2)}, u32[]{:S(2)}) collective-permute-start(bf16[2,32,1024]{2,1,0:T(8,128)(2,1)S(1)} %pad_maximum_fusion.8), channel_id=1, source_target_pairs={{8,4},{10,6},{12,0},{14,2},{16,12},{18,14},{20,8},{22,10},{24,20},... | collective-permute-start | bytes 393224 | tf_op jit(solution)/shard_map/ppermute | solution.py:41
  151.3 17.5 %copy-start.8 = (bf16[2,32,1024]{2,1,0:T(8,128)(2,1)S(1)}, bf16[2,32,1024]{2,1,0:T(8,128)(2,1)}, u32[]{:S(2)}) copy-start(bf16[2,32,1024]{2,1,0:T(8,128)(2,1)} %copy-done.7) | copy-start | bytes 393220
  151.4 17.5 %copy-start.12 = (bf16[64,1024]{1,0:T(8,128)(2,1)S(1)}, bf16[64,1024]{1,0:T(8,128)(2,1)}, u32[]{:S(2)}) copy-start(bf16[64,1024]{1,0:T(8,128)(2,1)} %copy-done.11) | copy-start | bytes 393220
  152.1 6.6 %collective-permute-start.24 = (bf16[2,32,1024]{2,1,0:T(8,128)(2,1)S(1)}, bf16[2,32,1024]{2,1,0:T(8,128)(2,1)S(1)}, u32[]{:S(2)}, u32[]{:S(2)}) collective-permute-start(bf16[2,32,1024]{2,1,0:T(8,128)(2,1)S(1)} %pad_maximum_fusion.8), channel_id=1, source_target_pairs={{8,0},{10,2},{12,4},{14,6},{16,8},{18,10},{20,12},{22,14},{24,16},... | collective-permute-start | bytes 393224 | tf_op jit(solution)/shard_map/ppermute | solution.py:41
  158.7 3.9 %collective-permute-start.26 = (bf16[64,1024]{1,0:T(8,128)(2,1)S(1)}, bf16[64,1024]{1,0:T(8,128)(2,1)S(1)}, u32[]{:S(2)}, u32[]{:S(2)}) collective-permute-start(bf16[64,1024]{1,0:T(8,128)(2,1)S(1)} %bitcast.207), channel_id=1, source_target_pairs={{0,2},{2,0},{4,6},{6,4},{1,3},{3,1},{5,7},{7,5},{8,10},{10,8},{12,... | collective-permute-start | bytes 393224 | tf_op jit(solution)/shard_map/ppermute | solution.py:19
  164.1 13.2 %collective-permute-start.27 = (bf16[128,2048]{1,0:T(8,128)(2,1)S(1)}, bf16[128,2048]{1,0:T(8,128)(2,1)S(1)}, u32[]{:S(2)}, u32[]{:S(2)}) collective-permute-start(bf16[128,2048]{1,0:T(8,128)(2,1)S(1)} %fusion.39), channel_id=1, source_target_pairs={{0,1},{1,0},{2,3},{3,2},{4,5},{5,4},{6,7},{7,6},{8,9},{9,8},{10,11... | collective-permute-start | bytes 1572872 | tf_op jit(solution)/shard_map/ppermute | solution.py:14
  168.6 8.6 %collective-permute-start.30 = (bf16[2,32,1024]{2,1,0:T(8,128)(2,1)S(1)}, bf16[2,32,1024]{2,1,0:T(8,128)(2,1)S(1)}, u32[]{:S(2)}, u32[]{:S(2)}) collective-permute-start(bf16[2,32,1024]{2,1,0:T(8,128)(2,1)S(1)} %bitcast.217), channel_id=1, source_target_pairs={{0,4},{2,6},{4,0},{6,2},{1,5},{3,7},{5,1},{7,3},{8,12},{10,14},{12... | collective-permute-start | bytes 393224 | tf_op jit(solution)/shard_map/ppermute | solution.py:24
  179.6 4.7 %collective-permute-start.28 = (bf16[64,1024]{1,0:T(8,128)(2,1)S(1)}, bf16[64,1024]{1,0:T(8,128)(2,1)S(1)}, u32[]{:S(2)}, u32[]{:S(2)}) collective-permute-start(bf16[64,1024]{1,0:T(8,128)(2,1)S(1)} %slice.275), channel_id=1, source_target_pairs={{0,2},{2,0},{4,6},{6,4},{1,3},{3,1},{5,7},{7,5},{8,10},{10,8},{12,... | collective-permute-start | bytes 393224 | tf_op jit(solution)/shard_map/ppermute | solution.py:19
  184.3 6.1 %collective-permute-start.29 = (bf16[1,32,1024]{2,1,0:T(8,128)(2,1)S(1)}, bf16[1,32,1024]{2,1,0:T(8,128)(2,1)S(1)}, u32[]{:S(2)}, u32[]{:S(2)}) collective-permute-start(bf16[1,32,1024]{2,1,0:T(8,128)(2,1)S(1)} %fusion.108), channel_id=1, source_target_pairs={{0,4},{2,6},{4,0},{6,2},{1,5},{3,7},{5,1},{7,3},{8,12},{10,14},{12... | collective-permute-start | bytes 196616 | tf_op jit(solution)/shard_map/ppermute | solution.py:24

commit v5 on v1

--- a/solution.py
+++ b/solution.py
@@ -1,6 +1,8 @@
 import jax
 import jax.numpy as jnp
 from jax import lax
+from jax.experimental import pallas as pl
+from jax.experimental.pallas import tpu as pltpu
 from jax.sharding import PartitionSpec as P
 
 BF = jnp.bfloat16
@@ -20,18 +22,59 @@
     return lax.ppermute(block, axis, [(i, (i + distance) % size) for i in range(size)])
 
 
+def partner(row, j, size):
+    return row ^ j if size & (size - 1) == 0 else (j - row) % size
+
+
+def swap_rows(block, j):
+    size = lax.axis_size("row")
+    return lax.ppermute(block, "row", [(i, partner(i, j, size)) for i in range(size)])
+
+
 def gather_rows(block):
-    size = lax.axis_size("row")
-    return jnp.concatenate([block] + [turn(block, "row", -j) for j in range(1, size)], axis=0)
+    return [swap_rows(block, j) if j else block for j in range(lax.axis_size("row"))]
 
 
 def scatter_rows(partial):
     size = lax.axis_size("row")
     pieces = jnp.split(partial, size, axis=0)
-    total = pieces[0].astype(F32)
-    for j in range(1, size):
-        total = total + turn(pieces[j], "row", j).astype(F32)
+    return [swap_rows(pieces[j], j) if j else pieces[0] for j in range(size)]
+
+
+def add_up(first, terms):
+    total = first.astype(F32)
+    for term in terms:
+        total = total + term.astype(F32)
     return total
+
+
+def after(block, other):
+    return lax.optimization_barrier((block, other))[0]
+
+
+def hold_kernel(up_hbm, down_hbm, up, down, sems):
+    copies = [
+        pltpu.make_async_copy(up_hbm, up, sems.at[0]),
+        pltpu.make_async_copy(down_hbm, down, sems.at[1]),
+    ]
+    for copy in copies:
+        copy.start()
+    for copy in copies:
+        copy.wait()
+
+
+def hold(up_block, down_block):
+    size = up_block.size * 2
+    return pl.pallas_call(
+        hold_kernel,
+        in_specs=[pl.BlockSpec(memory_space=pl.ANY)] * 2,
+        out_specs=[pl.BlockSpec(memory_space=pltpu.VMEM)] * 2,
+        out_shape=[pltpu.VMEM(up_block.shape, BF), pltpu.VMEM(down_block.shape, BF)],
+        scratch_shapes=[pltpu.SemaphoreType.DMA((2,))],
+        compiler_params=pltpu.CompilerParams(vmem_limit_bytes=4 * size),
+        cost_estimate=pl.CostEstimate(flops=0, bytes_accessed=4 * size, transcendentals=0),
+        name="hold",
+    )(up_block, down_block)
 
 
 def sum_cols(partial):
@@ -61,48 +104,67 @@
     section = lax.axis_index("section")
     sections = lax.axis_size("section")
     ticks = inputs.shape[1]
-    up_block = w_up[0]
-    down_block = w_down[0]
+    up_block, down_block = hold(w_up[0], w_down[0])
+    samples = [pick(sample_ids, tick - section + sections - 1) for tick in range(ticks)]
+    stored = [pick(send_base[0], samples[tick]) for tick in range(ticks - 1)]
+    bases = [jnp.where(section == 0, inputs[0, t], pick(recv_base[0], samples[t])) for t in range(1, ticks)]
+    stored, bases = lax.optimization_barrier((stored, [None] + bases))
     full_ins, pres, acts, seen_in, seen_out = [], [], [], [], []
-    sending = None
+    cot_pieces = [cotangent[0, ticks - 1]] + [None] * (lax.axis_size("row") - 1)
+    sending = inputs[0, 0]
     for tick in range(ticks):
-        sample = pick(sample_ids, tick - section + sections - 1)
         if tick == 0:
-            act_in = inputs[0, tick]
+            act_in = sending
         else:
             arrived = from_behind(sending, "section", 1)
-            rebuilt = (pick(recv_base[0], sample).astype(F32) + arrived.astype(F32)).astype(BF)
-            act_in = jnp.where(section == 0, inputs[0, tick], rebuilt)
-        full_in = gather_rows(act_in)
-        pre = sum_cols(matmul(full_in, up_block).astype(BF))
+            chosen = [j for j in range(1, len(cot_pieces)) if (j % 2 == 0) == (tick == 1)] if tick < 3 else []
+            for j in chosen:
+                cot_pieces[j] = swap_rows(after(cot_pieces[0], sending), j)
+            act_in = (bases[tick].astype(F32) + arrived.astype(F32)).astype(BF)
+            act_in = after(act_in, [cot_pieces[j] for j in chosen])
+        full_in = jnp.concatenate(gather_rows(act_in), axis=0)
+        partial = matmul(full_in, up_block).astype(BF)
+        if tick == ticks - 1:
+            full_cot = jnp.concatenate(cot_pieces, axis=0)
+            first_grads = matmul(full_cot, down_block, LAST).astype(BF)
+        pre = sum_cols(partial)
         act = jax.nn.silu(pre).astype(BF)
-        mixed = scatter_rows(matmul(act, down_block).astype(BF))
-        act_out = (act_in.astype(F32) + mixed).astype(BF)
-        stored = pick(send_base[0], sample)
-        sending = (act_out.astype(F32) - stored.astype(F32)).astype(BF)
+        if tick < ticks - 1:
+            terms = scatter_rows(matmul(act, down_block).astype(BF))
+            act_out = add_up(act_in, terms).astype(BF)
+            sending = (act_out.astype(F32) - stored[tick].astype(F32)).astype(BF)
+            seen_out.append(act_out)
         full_ins.append(full_in)
         pres.append(pre)
         acts.append(act)
         seen_in.append(act_in)
-        seen_out.append(act_out)
     full_grads = [None] * ticks
     pre_grads = [None] * ticks
     seen_grad = [None] * ticks
     for step in range(ticks):
         tick = ticks - 1 - step
         if step == 0:
-            grad_out = cotangent[0, tick]
+            grad_out, full_grad, partial = cot_pieces[0], full_cot, first_grads
         else:
             arrived = from_behind(sending, "section", -1)
+            if step == 1:
+                out_terms = jnp.split(matmul(after(acts[-1], sending), down_block).astype(BF), len(cot_pieces), axis=0)
+            chosen = [j for j in range(1, len(cot_pieces)) if (j % 2 == 0) == (step == 1)]
+            for j in chosen:
+                out_terms[j] = swap_rows(after(out_terms[j], sending), j)
             grad_out = jnp.where(section == sections - 1, cotangent[0, tick], arrived)
-        full_grad = gather_rows(grad_out)
-        grad_act = sum_cols(matmul(full_grad, down_block, LAST).astype(BF))
+            grad_out = after(grad_out, [out_terms[j] for j in chosen])
+            full_grad = jnp.concatenate(gather_rows(grad_out), axis=0)
+            partial = matmul(full_grad, down_block, LAST).astype(BF)
+        grad_act = sum_cols(partial)
         grad_pre = (grad_act * silu_slope(pres[tick])).astype(BF)
-        returned = scatter_rows(matmul(grad_pre, up_block, LAST).astype(BF))
-        sending = (grad_out.astype(F32) + returned).astype(BF)
+        back = matmul(grad_pre, up_block, LAST).astype(BF)
+        sending = add_up(grad_out, scatter_rows(back)).astype(BF)
         full_grads[tick] = full_grad
         pre_grads[tick] = grad_pre
         seen_grad[tick] = sending
+    seen_out.append(add_up(act_in, out_terms).astype(BF))
+    full_ins, pre_grads, acts, full_grads = lax.optimization_barrier(((full_ins, pre_grads, acts, full_grads), back))[0]
     grad_up = matmul(jnp.concatenate(full_ins, axis=0), jnp.concatenate(pre_grads, axis=0), FIRST)
     grad_down = matmul(jnp.concatenate(acts, axis=0), jnp.concatenate(full_grads, axis=0), FIRST)
     return (

time: 178 us -> 180 us (1.011)
  starting transfers between devices: 70.8 us -> 79.9 us
  matrix products: 32.2 us -> 27 us
  waiting for transfers between devices: 44.8 us -> 41.1 us
  other arithmetic: 13.4 us -> 10.3 us
  local copies, waits for them, and re-layouts: 8.78 us -> 11 us
    ppermute x0 -> x36, starting transfers between devices: none -> 46.5 us  [swap_rows(): lax.ppermute(block, 'row', [(i, partner(i, j, size)) for i in range(size)])]
    ppermute x42 -> x6, starting transfers between devices: 59.8 us -> 22.9 us  [turn(): lax.ppermute(block, axis, [(i, (i + distance) % size) for i in range(size)])]
    ppermute x0 -> x36, waiting for transfers between devices: none -> 35.3 us  [swap_rows(): lax.ppermute(block, 'row', [(i, partner(i, j, size)) for i in range(size)])]
    ppermute x42 -> x6, waiting for transfers between devices: 38.3 us -> 4.62 us  [turn(): lax.ppermute(block, axis, [(i, (i + distance) % size) for i in range(size)])]
    ppermute x4, waiting for transfers between devices: 6.58 us -> 1.17 us  [from_behind(): return lax.ppermute(block, axis, route)]
    dot_general x14, matrix products: 32.2 us -> 27 us  [matmul(): return lax.dot_general(a, b, dims, preferred_element_type=F32)]
    unnamed x71 -> x82, local copies, waits for them, and re-layouts: 4.43 us -> 7.15 us
    unnamed x3 -> x0, other arithmetic: 2.38 us -> none
  transfers between devices with their start and end apart: 46 -> 46, of which waited for: 29 -> 22; matrix products, arithmetic and copies ran while one was open for 16% -> 10% of each run, Pallas kernels for 0% -> 0%
where the time goes in v5:
time: 180 us; the launch traced here: 177 us
  starting transfers between devices  79.9 us (44%)
  waiting for transfers between devices  41.1 us (23%)
  matrix products  27 us (15%)
  local copies, waits for them, and re-layouts  11 us (6%)
  other arithmetic  10.3 us (6%)
  between operations  7.25 us (4%)
    ppermute x36, starting transfers between devices, swap_rows(): lax.ppermute(block, 'row', [(i, partner(i, j, size)) for i in range(size)])  46.5 us
    ppermute x36, waiting for transfers between devices, swap_rows(): lax.ppermute(block, 'row', [(i, partner(i, j, size)) for i in range(size)])  35.3 us
    dot_general x14, matrix products, matmul(): return lax.dot_general(a, b, dims, preferred_element_type=F32)  27 us
    ppermute x6, starting transfers between devices, turn(): lax.ppermute(block, axis, [(i, (i + distance) % size) for i in range(size)])  22.9 us
    ppermute x4, starting transfers between devices, from_behind(): return lax.ppermute(block, axis, route)  10.5 us
    unnamed x82, local copies, waits for them, and re-layouts  7.15 us
    ppermute x6, waiting for transfers between devices, turn(): lax.ppermute(block, axis, [(i, (i + distance) % size) for i in range(size)])  4.62 us
  transfers between devices with their start and end apart: 46, of which 22 were waited for; matrix products, arithmetic and copies ran while one was open for 10% of the time, Pallas kernels for 0%

profile of v5, /device:TPU:3, one launch (start us, length us, event | category | flops | bytes accessed | tf_op | source)
XLA Modules:
  0.0 177.0 jit_solution(9134542492068416829)
XLA Ops:
  0.6 1.4 fusion.30
  5.9 1.6 slice_bitcast_fusion.2
  7.5 1.3 collective-permute-start
  8.8 2.3 %collective-permute-start.1 = (bf16[32,1024]{1,0:T(8,128)(2,1)S(1)}, bf16[32,1024]{1,0:T(8,128)(2,1)S(1)}, u32[]{:S(2)}, u32[]{:S(2)}) collective-permute-start(bf16[32,1024]{1,0:T(8,128)(2,1)S(1)} %get-tuple-element.90), channel_id=1, source_target_pairs={{0,4},{2,6},{4,0},{6,2},{1,5},{3,7},{5,1},{7,3},{8,12},{10,14},{12... | collective-permute-start | bytes 196616 | tf_op jit(solution)/shard_map/ppermute | solution.py:31
  11.1 2.2 %copy-done.6 = bf16[1,1024,2048]{2,1,0:T(8,128)(2,1)S(1)} copy-done((bf16[1,1024,2048]{2,1,0:T(8,128)(2,1)S(1)}, bf16[1,1024,2048]{2,1,0:T(8,128)(2,1)}, u32[]{:S(2)}) %copy-start.6) | copy-done | bytes 4194328
  13.3 2.2 %copy-done.7 = bf16[1,2048,1024]{2,1,0:T(8,128)(2,1)S(1)} copy-done((bf16[1,2048,1024]{2,1,0:T(8,128)(2,1)S(1)}, bf16[1,2048,1024]{2,1,0:T(8,128)(2,1)}, u32[]{:S(2)}) %copy-start.7) | copy-done | bytes 4194328
  16.2 1.9 %copy-done = bf16[1024,2048]{1,0:T(8,128)(2,1)} copy-done((bf16[1024,2048]{1,0:T(8,128)(2,1)}, bf16[1024,2048]{1,0:T(8,128)(2,1)S(1)}, u32[]{:S(2)}) %copy-start) | copy-done | bytes 4194328
  19.5 1.5 collective-permute-start.3
  23.3 3.1 %convolution_convert_fusion.11 = bf16[128,1024]{1,0:T(8,128)(2,1)S(1)} fusion(bf16[128,2048]{1,0:T(8,128)(2,1)S(1)} %multiply_convert_fusion.5, bf16[2048,1024]{1,0:T(8,128)(2,1)} %copy-done.3), kind=kOutput, calls=%fused_computation.23 | convolution fusion | flops 537001984 | bytes 4980736 | tf_op jit(solution)/shard_map/dot_general | solution.py:100
  26.8 3.2 %collective-permute-start.5 = (bf16[32,1024]{1,0:T(8,128)(2,1)S(1)}, bf16[32,1024]{1,0:T(8,128)(2,1)S(1)}, u32[]{:S(2)}, u32[]{:S(2)}) collective-permute-start(bf16[32,1024]{1,0:T(8,128)(2,1)S(1)} %get-tuple-element.88), channel_id=1, source_target_pairs={{0,4},{2,6},{4,0},{6,2},{1,5},{3,7},{5,1},{7,3},{8,12},{10,14},{12... | collective-permute-start | bytes 196616 | tf_op jit(solution)/shard_map/ppermute | solution.py:31
  30.9 1.4 collective-permute-done.5
  32.4 2.7 %collective-permute-done.6 = bf16[32,1024]{1,0:T(8,128)(2,1)S(1)} collective-permute-done((bf16[32,1024]{1,0:T(8,128)(2,1)S(1)}, bf16[32,1024]{1,0:T(8,128)(2,1)S(1)}, u32[]{:S(2)}, u32[]{:S(2)}) %collective-permute-start.6) | collective-permute-done | bytes 65568 | tf_op jit(solution)/shard_map/ppermute | solution.py:31
  35.1 1.5 subtract_convert_fusion.1
  36.6 3.1 %collective-permute-start.7 = (bf16[32,1024]{1,0:T(8,128)(2,1)S(1)}, bf16[32,1024]{1,0:T(8,128)(2,1)S(1)}, u32[]{:S(2)}, u32[]{:S(2)}) collective-permute-start(bf16[32,1024]{1,0:T(8,128)(2,1)S(1)} %get-tuple-element.63), channel_id=1, source_target_pairs={{0,8},{8,16},{16,24},{1,9},{9,17},{17,25},{2,10},{10,18},{18,26},{... | collective-permute-start | bytes 196616 | tf_op jit(solution)/shard_map/ppermute | solution.py:17
  40.5 2.8 %collective-permute-start.8 = (bf16[32,1024]{1,0:T(8,128)(2,1)S(1)}, bf16[32,1024]{1,0:T(8,128)(2,1)S(1)}, u32[]{:S(2)}, u32[]{:S(2)}) collective-permute-start(bf16[32,1024]{1,0:T(8,128)(2,1)S(1)} %slice_bitcast_fusion), channel_id=1, source_target_pairs={{0,4},{2,6},{4,0},{6,2},{1,5},{3,7},{5,1},{7,3},{8,12},{10,14},{12... | collective-permute-start | bytes 196616 | tf_op jit(solution)/shard_map/ppermute | solution.py:31
  43.3 1.6 collective-permute-done.8
  45.0 1.4 collective-permute-start.9
  47.3 1.2 collective-permute-start.11
  48.6 2.5 %collective-permute-done.10 = bf16[32,1024]{1,0:T(8,128)(2,1)S(1)} collective-permute-done((bf16[32,1024]{1,0:T(8,128)(2,1)S(1)}, bf16[32,1024]{1,0:T(8,128)(2,1)S(1)}, u32[]{:S(2)}, u32[]{:S(2)}) %collective-permute-start.10) | collective-permute-done | bytes 65568 | tf_op jit(solution)/shard_map/ppermute | solution.py:31
  51.1 1.4 collective-permute-done.11
  53.2 4.1 %collective-permute-start.12 = (bf16[128,2048]{1,0:T(8,128)(2,1)S(1)}, bf16[128,2048]{1,0:T(8,128)(2,1)S(1)}, u32[]{:S(2)}, u32[]{:S(2)}) collective-permute-start(bf16[128,2048]{1,0:T(8,128)(2,1)S(1)} %convolution_convert_fusion.4), channel_id=1, source_target_pairs={{0,1},{1,0},{2,3},{3,2},{4,5},{5,4},{6,7},{7,6},{8,9},{9,8},{10,11... | collective-permute-start | bytes 1572872 | tf_op jit(solution)/shard_map/ppermute | solution.py:22
  57.4 1.5 collective-permute-done.12
  60.1 2.4 %collective-permute-start.14 = (bf16[32,1024]{1,0:T(8,128)(2,1)S(1)}, bf16[32,1024]{1,0:T(8,128)(2,1)S(1)}, u32[]{:S(2)}, u32[]{:S(2)}) collective-permute-start(bf16[32,1024]{1,0:T(8,128)(2,1)S(1)} %get-tuple-element.85), channel_id=1, source_target_pairs={{0,4},{2,6},{4,0},{6,2},{1,5},{3,7},{5,1},{7,3},{8,12},{10,14},{12... | collective-permute-start | bytes 196616 | tf_op jit(solution)/shard_map/ppermute | solution.py:31
  64.3 3.1 %collective-permute-done.15 = bf16[32,1024]{1,0:T(8,128)(2,1)S(1)} collective-permute-done((bf16[32,1024]{1,0:T(8,128)(2,1)S(1)}, bf16[32,1024]{1,0:T(8,128)(2,1)S(1)}, u32[]{:S(2)}, u32[]{:S(2)}) %collective-permute-start.15) | collective-permute-done | bytes 65568 | tf_op jit(solution)/shard_map/ppermute | solution.py:31
  68.0 3.1 %collective-permute-start.16 = (bf16[32,1024]{1,0:T(8,128)(2,1)S(1)}, bf16[32,1024]{1,0:T(8,128)(2,1)S(1)}, u32[]{:S(2)}, u32[]{:S(2)}) collective-permute-start(bf16[32,1024]{1,0:T(8,128)(2,1)S(1)} %get-tuple-element.61), channel_id=1, source_target_pairs={{0,8},{8,16},{16,24},{1,9},{9,17},{17,25},{2,10},{10,18},{18,26},{... | collective-permute-start | bytes 196616 | tf_op jit(solution)/shard_map/ppermute | solution.py:17
  71.2 1.4 collective-permute-start.17
  72.5 2.0 %collective-permute-start.18 = (bf16[32,1024]{1,0:T(8,128)(2,1)S(1)}, bf16[32,1024]{1,0:T(8,128)(2,1)S(1)}, u32[]{:S(2)}, u32[]{:S(2)}) collective-permute-start(bf16[32,1024]{1,0:T(8,128)(2,1)S(1)} %slice_bitcast_fusion), channel_id=1, source_target_pairs={{0,6},{2,4},{4,2},{6,0},{1,7},{3,5},{5,3},{7,1},{8,14},{10,12},{12... | collective-permute-start | bytes 196616 | tf_op jit(solution)/shard_map/ppermute | solution.py:31
  74.6 3.0 %collective-permute-done.18 = bf16[32,1024]{1,0:T(8,128)(2,1)S(1)} collective-permute-done((bf16[32,1024]{1,0:T(8,128)(2,1)S(1)}, bf16[32,1024]{1,0:T(8,128)(2,1)S(1)}, u32[]{:S(2)}, u32[]{:S(2)}) %collective-permute-start.18) | collective-permute-done | bytes 65568 | tf_op jit(solution)/shard_map/ppermute | solution.py:31
  77.5 2.6 %collective-permute-start.20 = (bf16[32,1024]{1,0:T(8,128)(2,1)S(1)}, bf16[32,1024]{1,0:T(8,128)(2,1)S(1)}, u32[]{:S(2)}, u32[]{:S(2)}) collective-permute-start(bf16[32,1024]{1,0:T(8,128)(2,1)S(1)} %add_convert_fusion.4), channel_id=1, source_target_pairs={{0,4},{2,6},{4,0},{6,2},{1,5},{3,7},{5,1},{7,3},{8,12},{10,14},{12... | collective-permute-start | bytes 196616 | tf_op jit(solution)/shard_map/ppermute | solution.py:31
  81.1 1.5 convolution_convert_fusion.2
  82.6 4.0 %collective-permute-start.23 = (bf16[128,2048]{1,0:T(8,128)(2,1)S(1)}, bf16[128,2048]{1,0:T(8,128)(2,1)S(1)}, u32[]{:S(2)}, u32[]{:S(2)}) collective-permute-start(bf16[128,2048]{1,0:T(8,128)(2,1)S(1)} %convolution_convert_fusion.2), channel_id=1, source_target_pairs={{0,1},{1,0},{2,3},{3,2},{4,5},{5,4},{6,7},{7,6},{8,9},{9,8},{10,11... | collective-permute-start | bytes 1572872 | tf_op jit(solution)/shard_map/ppermute | solution.py:22
  87.5 3.2 %collective-permute-start.22 = (bf16[128,2048]{1,0:T(8,128)(2,1)S(1)}, bf16[128,2048]{1,0:T(8,128)(2,1)S(1)}, u32[]{:S(2)}, u32[]{:S(2)}) collective-permute-start(bf16[128,2048]{1,0:T(8,128)(2,1)S(1)} %convolution_convert_fusion.3), channel_id=1, source_target_pairs={{0,1},{1,0},{2,3},{3,2},{4,5},{5,4},{6,7},{7,6},{8,9},{9,8},{10,11... | collective-permute-start | bytes 1572872 | tf_op jit(solution)/shard_map/ppermute | solution.py:22
  90.6 1.5 collective-permute-done.22
  92.2 1.4 multiply_convert_fusion.2
  93.6 1.5 convolution_convert_fusion.9
  95.8 1.3 collective-permute-start.25
  97.1 2.2 %collective-permute-start.26 = (bf16[32,1024]{1,0:T(8,128)(2,1)}, bf16[32,1024]{1,0:T(8,128)(2,1)}, u32[]{:S(2)}, u32[]{:S(2)}) collective-permute-start(bf16[32,1024]{1,0:T(8,128)(2,1)} %get-tuple-element.81), channel_id=1, source_target_pairs={{0,6},{2,4},{4,2},{6,0},{1,7},{3,5},{5,3},{7,1},{8,14},{10,12},{12... | collective-permute-start | bytes 196616 | tf_op jit(solution)/shard_map/ppermute | solution.py:31
  100.2 2.7 %collective-permute-done.26 = bf16[32,1024]{1,0:T(8,128)(2,1)} collective-permute-done((bf16[32,1024]{1,0:T(8,128)(2,1)}, bf16[32,1024]{1,0:T(8,128)(2,1)}, u32[]{:S(2)}, u32[]{:S(2)}) %collective-permute-start.26) | collective-permute-done | bytes 65568 | tf_op jit(solution)/shard_map/ppermute | solution.py:31
  103.9 2.4 %collective-permute-start.27 = (bf16[32,1024]{1,0:T(8,128)(2,1)S(1)}, bf16[32,1024]{1,0:T(8,128)(2,1)S(1)}, u32[]{:S(2)}, u32[]{:S(2)}) collective-permute-start(bf16[32,1024]{1,0:T(8,128)(2,1)S(1)} %add_convert_fusion.3), channel_id=1, source_target_pairs={{8,0},{16,8},{24,16},{9,1},{17,9},{25,17},{10,2},{18,10},{26,18},{... | collective-permute-start | bytes 196616 | tf_op jit(solution)/shard_map/ppermute | solution.py:17
  106.3 3.1 %convolution_convert_fusion.8 = bf16[128,1024]{1,0:T(8,128)(2,1)S(1)} fusion(bf16[128,2048]{1,0:T(8,128)(2,1)} %get-tuple-element.57, bf16[2048,1024]{1,0:T(8,128)(2,1)} %copy-done.3), kind=kOutput, calls=%fused_computation.20 | convolution fusion | flops 537001984 | bytes 4980736 | tf_op jit(solution)/shard_map/dot_general | solution.py:100
  109.4 1.7 collective-permute-start.28
  111.1 2.3 %collective-permute-done.28 = bf16[32,1024]{1,0:T(8,128)(2,1)S(1)} collective-permute-done((bf16[32,1024]{1,0:T(8,128)(2,1)S(1)}, bf16[32,1024]{1,0:T(8,128)(2,1)S(1)}, u32[]{:S(2)}, u32[]{:S(2)}) %collective-permute-start.28) | collective-permute-done | bytes 65568 | tf_op jit(solution)/shard_map/ppermute | solution.py:31
  113.5 1.6 collective-permute-start.29
  115.4 1.8 collective-permute-start.31
  117.1 2.3 %collective-permute-done.30 = bf16[32,1024]{1,0:T(8,128)(2,1)S(1)} collective-permute-done((bf16[32,1024]{1,0:T(8,128)(2,1)S(1)}, bf16[32,1024]{1,0:T(8,128)(2,1)S(1)}, u32[]{:S(2)}, u32[]{:S(2)}) %collective-permute-start.30) | collective-permute-done | bytes 65568 | tf_op jit(solution)/shard_map/ppermute | solution.py:31
  120.4 1.5 convolution_convert_fusion.1
  122.0 5.9 %collective-permute-start.32 = (bf16[128,2048]{1,0:T(8,128)(2,1)S(1)}, bf16[128,2048]{1,0:T(8,128)(2,1)S(1)}, u32[]{:S(2)}, u32[]{:S(2)}) collective-permute-start(bf16[128,2048]{1,0:T(8,128)(2,1)S(1)} %convolution_convert_fusion.1), channel_id=1, source_target_pairs={{0,1},{1,0},{2,3},{3,2},{4,5},{5,4},{6,7},{7,6},{8,9},{9,8},{10,11... | collective-permute-start | bytes 1572872 | tf_op jit(solution)/shard_map/ppermute | solution.py:22
  127.9 1.5 collective-permute-done.32
  130.0 1.5 convolution_convert_fusion.7
  131.7 1.2 collective-permute-start.34
  132.9 2.3 %collective-permute-start.35 = (bf16[32,1024]{1,0:T(8,128)(2,1)S(1)}, bf16[32,1024]{1,0:T(8,128)(2,1)S(1)}, u32[]{:S(2)}, u32[]{:S(2)}) collective-permute-start(bf16[32,1024]{1,0:T(8,128)(2,1)S(1)} %get-tuple-element.78), channel_id=1, source_target_pairs={{0,6},{2,4},{4,2},{6,0},{1,7},{3,5},{5,3},{7,1},{8,14},{10,12},{12... | collective-permute-start | bytes 196616 | tf_op jit(solution)/shard_map/ppermute | solution.py:31
  135.9 2.4 %collective-permute-done.35 = bf16[32,1024]{1,0:T(8,128)(2,1)S(1)} collective-permute-done((bf16[32,1024]{1,0:T(8,128)(2,1)S(1)}, bf16[32,1024]{1,0:T(8,128)(2,1)S(1)}, u32[]{:S(2)}, u32[]{:S(2)}) %collective-permute-start.35) | collective-permute-done | bytes 65568 | tf_op jit(solution)/shard_map/ppermute | solution.py:31
  138.4 1.9 %collective-permute-start.38 = (bf16[32,1024]{1,0:T(8,128)(2,1)S(1)}, bf16[32,1024]{1,0:T(8,128)(2,1)S(1)}, u32[]{:S(2)}, u32[]{:S(2)}) collective-permute-start(bf16[32,1024]{1,0:T(8,128)(2,1)S(1)} %add_convert_fusion.2), channel_id=1, source_target_pairs={{8,0},{16,8},{24,16},{9,1},{17,9},{25,17},{10,2},{18,10},{26,18},{... | collective-permute-start | bytes 196616 | tf_op jit(solution)/shard_map/ppermute | solution.py:17
  140.4 1.9 %collective-permute-start.36 = (bf16[32,1024]{1,0:T(8,128)(2,1)S(1)}, bf16[32,1024]{1,0:T(8,128)(2,1)S(1)}, u32[]{:S(2)}, u32[]{:S(2)}) collective-permute-start(bf16[32,1024]{1,0:T(8,128)(2,1)S(1)} %get-tuple-element.46), channel_id=1, source_target_pairs={{0,2},{2,0},{4,6},{6,4},{1,3},{3,1},{5,7},{7,5},{8,10},{10,8},{12,... | collective-permute-start | bytes 196616 | tf_op jit(solution)/shard_map/ppermute | solution.py:31
  143.1 1.2 collective-permute-done.38
  144.3 3.4 %collective-permute-done.37 = bf16[32,1024]{1,0:T(8,128)(2,1)S(1)} collective-permute-done((bf16[32,1024]{1,0:T(8,128)(2,1)S(1)}, bf16[32,1024]{1,0:T(8,128)(2,1)S(1)}, u32[]{:S(2)}, u32[]{:S(2)}) %collective-permute-start.37) | collective-permute-done | bytes 65568 | tf_op jit(solution)/shard_map/ppermute | solution.py:31
  148.4 2.9 %collective-permute-start.41 = (bf16[32,1024]{1,0:T(8,128)(2,1)S(1)}, bf16[32,1024]{1,0:T(8,128)(2,1)S(1)}, u32[]{:S(2)}, u32[]{:S(2)}) collective-permute-start(bf16[32,1024]{1,0:T(8,128)(2,1)S(1)} %bitcast_select_fusion), channel_id=1, source_target_pairs={{0,6},{2,4},{4,2},{6,0},{1,7},{3,5},{5,3},{7,1},{8,14},{10,12},{12... | collective-permute-start | bytes 196616 | tf_op jit(solution)/shard_map/ppermute | solution.py:31
  151.8 2.7 %collective-permute-done.41 = bf16[32,1024]{1,0:T(8,128)(2,1)S(1)} collective-permute-done((bf16[32,1024]{1,0:T(8,128)(2,1)S(1)}, bf16[32,1024]{1,0:T(8,128)(2,1)S(1)}, u32[]{:S(2)}, u32[]{:S(2)}) %collective-permute-start.41) | collective-permute-done | bytes 65568 | tf_op jit(solution)/shard_map/ppermute | solution.py:31
  154.5 1.5 convolution_convert_fusion
  156.0 4.2 %collective-permute-start.42 = (bf16[128,2048]{1,0:T(8,128)(2,1)S(1)}, bf16[128,2048]{1,0:T(8,128)(2,1)S(1)}, u32[]{:S(2)}, u32[]{:S(2)}) collective-permute-start(bf16[128,2048]{1,0:T(8,128)(2,1)S(1)} %convolution_convert_fusion), channel_id=1, source_target_pairs={{0,1},{1,0},{2,3},{3,2},{4,5},{5,4},{6,7},{7,6},{8,9},{9,8},{10,11... | collective-permute-start | bytes 1572872 | tf_op jit(solution)/shard_map/ppermute | solution.py:22
  162.2 1.5 convolution_convert_fusion.6
  163.9 2.5 %collective-permute-start.44 = (bf16[32,1024]{1,0:T(8,128)(2,1)S(1)}, bf16[32,1024]{1,0:T(8,128)(2,1)S(1)}, u32[]{:S(2)}, u32[]{:S(2)}) collective-permute-start(bf16[32,1024]{1,0:T(8,128)(2,1)S(1)} %get-tuple-element.73), channel_id=1, source_target_pairs={{0,4},{2,6},{4,0},{6,2},{1,5},{3,7},{5,1},{7,3},{8,12},{10,14},{12... | collective-permute-start | bytes 196616 | tf_op jit(solution)/shard_map/ppermute | solution.py:31
  167.4 4.4 %convert_bitcast_fusion = bf16[1,2048,1024]{2,1,0:T(8,128)(2,1)} fusion(bf16[128,2048]{1,0:T(8,128)(2,1)S(1)} %copy-done.10, bf16[128,2048]{1,0:T(8,128)(2,1)S(1)} %multiply_convert_fusion.4, bf16[128,2048]{1,0:T(8,128)(2,1)S(1)} %multiply_convert_fusion.5, bf16[128,1024]{1,0:T(8,128)(2,1)S(1)} %pad_maximum_fusion.1, ...), kind=kOutput, calls=%fused_computation | convolution fusion | flops 1619787776 | bytes 6553600 | tf_op jit(solution)/shard_map/dot_general | solution.py:100
  171.8 4.4 %convert_bitcast_fusion.1 = bf16[1,1024,2048]{2,1,0:T(8,128)(2,1)} fusion(bf16[128,2048]{1,0:T(8,128)(2,1)S(1)} %copy-done.9, bf16[128,2048]{1,0:T(8,128)(2,1)S(1)} %multiply_convert_fusion.1, bf16[128,2048]{1,0:T(8,128)(2,1)S(1)} %multiply_convert_fusion, bf16[128,1024]{1,0:T(8,128)(2,1)S(1)} %copy-done.18, bf16[128,1024]{1,0:T(8,128)(2,1)S(1)} %copy-done.16, ...), kind=kOutput, calls=%fused_computation.1 | convolution fusion | flops 1619787776 | bytes 6553600 | tf_op jit(solution)/shard_map/dot_general | solution.py:100
  (159 shorter events, 22.9 us)
Async XLA Ops:
  7.5 8.6 %collective-permute-start = (bf16[32,1024]{1,0:T(8,128)(2,1)S(1)}, bf16[32,1024]{1,0:T(8,128)(2,1)S(1)}, u32[]{:S(2)}, u32[]{:S(2)}) collective-permute-start(bf16[32,1024]{1,0:T(8,128)(2,1)S(1)} %get-tuple-element.90), channel_id=1, source_target_pairs={{0,2},{2,0},{4,6},{6,4},{1,3},{3,1},{5,7},{7,5},{8,10},{10,8},{12,... | collective-permute-start | bytes 196616 | tf_op jit(solution)/shard_map/ppermute | solution.py:31
  8.8 7.3 %collective-permute-start.1 = (bf16[32,1024]{1,0:T(8,128)(2,1)S(1)}, bf16[32,1024]{1,0:T(8,128)(2,1)S(1)}, u32[]{:S(2)}, u32[]{:S(2)}) collective-permute-start(bf16[32,1024]{1,0:T(8,128)(2,1)S(1)} %get-tuple-element.90), channel_id=1, source_target_pairs={{0,4},{2,6},{4,0},{6,2},{1,5},{3,7},{5,1},{7,3},{8,12},{10,14},{12... | collective-permute-start | bytes 196616 | tf_op jit(solution)/shard_map/ppermute | solution.py:31
  11.1 5.0 %collective-permute-start.2 = (bf16[32,1024]{1,0:T(8,128)(2,1)S(1)}, bf16[32,1024]{1,0:T(8,128)(2,1)S(1)}, u32[]{:S(2)}, u32[]{:S(2)}) collective-permute-start(bf16[32,1024]{1,0:T(8,128)(2,1)S(1)} %get-tuple-element.90), channel_id=1, source_target_pairs={{0,6},{2,4},{4,2},{6,0},{1,7},{3,5},{5,3},{7,1},{8,14},{10,12},{12... | collective-permute-start | bytes 196616 | tf_op jit(solution)/shard_map/ppermute | solution.py:31
  19.5 3.4 %collective-permute-start.3 = (bf16[128,2048]{1,0:T(8,128)(2,1)S(1)}, bf16[128,2048]{1,0:T(8,128)(2,1)S(1)}, u32[]{:S(2)}, u32[]{:S(2)}) collective-permute-start(bf16[128,2048]{1,0:T(8,128)(2,1)S(1)} %convolution_convert_fusion.5), channel_id=1, source_target_pairs={{0,1},{1,0},{2,3},{3,2},{4,5},{5,4},{6,7},{7,6},{8,9},{9,8},{10,11... | collective-permute-start | bytes 1572872 | tf_op jit(solution)/shard_map/ppermute | solution.py:22
  22.9 29.5 %copy-start.1 = (bf16[1024,2048]{1,0:T(8,128)(2,1)S(1)}, bf16[1024,2048]{1,0:T(8,128)(2,1)}, u32[]{:S(2)}) copy-start(bf16[1024,2048]{1,0:T(8,128)(2,1)} %copy-done) | copy-start | bytes 12582916
  26.4 32.8 %copy-start.4 = (bf16[2048,1024]{1,0:T(8,128)(2,1)S(1)}, bf16[2048,1024]{1,0:T(8,128)(2,1)}, u32[]{:S(2)}) copy-start(bf16[2048,1024]{1,0:T(8,128)(2,1)} %copy-done.3) | copy-start | bytes 12582916
  26.4 4.6 %collective-permute-start.4 = (bf16[32,1024]{1,0:T(8,128)(2,1)S(1)}, bf16[32,1024]{1,0:T(8,128)(2,1)S(1)}, u32[]{:S(2)}, u32[]{:S(2)}) collective-permute-start(bf16[32,1024]{1,0:T(8,128)(2,1)S(1)} %get-tuple-element.86), channel_id=1, source_target_pairs={{0,2},{2,0},{4,6},{6,4},{1,3},{3,1},{5,7},{7,5},{8,10},{10,8},{12,... | collective-permute-start | bytes 196616 | tf_op jit(solution)/shard_map/ppermute | solution.py:31
  26.8 5.5 %collective-permute-start.5 = (bf16[32,1024]{1,0:T(8,128)(2,1)S(1)}, bf16[32,1024]{1,0:T(8,128)(2,1)S(1)}, u32[]{:S(2)}, u32[]{:S(2)}) collective-permute-start(bf16[32,1024]{1,0:T(8,128)(2,1)S(1)} %get-tuple-element.88), channel_id=1, source_target_pairs={{0,4},{2,6},{4,0},{6,2},{1,5},{3,7},{5,1},{7,3},{8,12},{10,14},{12... | collective-permute-start | bytes 196616 | tf_op jit(solution)/shard_map/ppermute | solution.py:31
  30.0 5.0 %collective-permute-start.6 = (bf16[32,1024]{1,0:T(8,128)(2,1)S(1)}, bf16[32,1024]{1,0:T(8,128)(2,1)S(1)}, u32[]{:S(2)}, u32[]{:S(2)}) collective-permute-start(bf16[32,1024]{1,0:T(8,128)(2,1)S(1)} %get-tuple-element.87), channel_id=1, source_target_pairs={{0,6},{2,4},{4,2},{6,0},{1,7},{3,5},{5,3},{7,1},{8,14},{10,12},{12... | collective-permute-start | bytes 196616 | tf_op jit(solution)/shard_map/ppermute | solution.py:31
  36.6 6.7 %collective-permute-start.7 = (bf16[32,1024]{1,0:T(8,128)(2,1)S(1)}, bf16[32,1024]{1,0:T(8,128)(2,1)S(1)}, u32[]{:S(2)}, u32[]{:S(2)}) collective-permute-start(bf16[32,1024]{1,0:T(8,128)(2,1)S(1)} %get-tuple-element.63), channel_id=1, source_target_pairs={{0,8},{8,16},{16,24},{1,9},{9,17},{17,25},{2,10},{10,18},{18,26},{... | collective-permute-start | bytes 196616 | tf_op jit(solution)/shard_map/ppermute | solution.py:17
  40.5 40.5 %copy-start.11 = (bf16[32,1024]{1,0:T(8,128)(2,1)}, bf16[32,1024]{1,0:T(8,128)(2,1)S(1)}, u32[]{:S(2)}) copy-start(bf16[32,1024]{1,0:T(8,128)(2,1)S(1)} %slice_bitcast_fusion) | copy-start | bytes 196612
  40.5 4.4 %collective-permute-start.8 = (bf16[32,1024]{1,0:T(8,128)(2,1)S(1)}, bf16[32,1024]{1,0:T(8,128)(2,1)S(1)}, u32[]{:S(2)}, u32[]{:S(2)}) collective-permute-start(bf16[32,1024]{1,0:T(8,128)(2,1)S(1)} %slice_bitcast_fusion), channel_id=1, source_target_pairs={{0,4},{2,6},{4,0},{6,2},{1,5},{3,7},{5,1},{7,3},{8,12},{10,14},{12... | collective-permute-start | bytes 196616 | tf_op jit(solution)/shard_map/ppermute | solution.py:31
  45.0 36.1 %copy-start.26 = (bf16[32,1024]{1,0:T(8,128)(2,1)}, bf16[32,1024]{1,0:T(8,128)(2,1)S(1)}, u32[]{:S(2)}) copy-start(bf16[32,1024]{1,0:T(8,128)(2,1)S(1)} %collective-permute-done.8) | copy-start | bytes 196612
  45.0 3.6 %collective-permute-start.9 = (bf16[32,1024]{1,0:T(8,128)(2,1)S(1)}, bf16[32,1024]{1,0:T(8,128)(2,1)S(1)}, u32[]{:S(2)}, u32[]{:S(2)}) collective-permute-start(bf16[32,1024]{1,0:T(8,128)(2,1)S(1)} %add_convert_fusion.6), channel_id=1, source_target_pairs={{0,2},{2,0},{4,6},{6,4},{1,3},{3,1},{5,7},{7,5},{8,10},{10,8},{12,... | collective-permute-start | bytes 196616 | tf_op jit(solution)/shard_map/ppermute | solution.py:31
  46.4 4.7 %collective-permute-start.10 = (bf16[32,1024]{1,0:T(8,128)(2,1)S(1)}, bf16[32,1024]{1,0:T(8,128)(2,1)S(1)}, u32[]{:S(2)}, u32[]{:S(2)}) collective-permute-start(bf16[32,1024]{1,0:T(8,128)(2,1)S(1)} %add_convert_fusion.6), channel_id=1, source_target_pairs={{0,4},{2,6},{4,0},{6,2},{1,5},{3,7},{5,1},{7,3},{8,12},{10,14},{12... | collective-permute-start | bytes 196616 | tf_op jit(solution)/shard_map/ppermute | solution.py:31
  47.3 5.1 %collective-permute-start.11 = (bf16[32,1024]{1,0:T(8,128)(2,1)S(1)}, bf16[32,1024]{1,0:T(8,128)(2,1)S(1)}, u32[]{:S(2)}, u32[]{:S(2)}) collective-permute-start(bf16[32,1024]{1,0:T(8,128)(2,1)S(1)} %add_convert_fusion.6), channel_id=1, source_target_pairs={{0,6},{2,4},{4,2},{6,0},{1,7},{3,5},{5,3},{7,1},{8,14},{10,12},{12... | collective-permute-start | bytes 196616 | tf_op jit(solution)/shard_map/ppermute | solution.py:31
  53.2 5.7 %collective-permute-start.12 = (bf16[128,2048]{1,0:T(8,128)(2,1)S(1)}, bf16[128,2048]{1,0:T(8,128)(2,1)S(1)}, u32[]{:S(2)}, u32[]{:S(2)}) collective-permute-start(bf16[128,2048]{1,0:T(8,128)(2,1)S(1)} %convolution_convert_fusion.4), channel_id=1, source_target_pairs={{0,1},{1,0},{2,3},{3,2},{4,5},{5,4},{6,7},{7,6},{8,9},{9,8},{10,11... | collective-permute-start | bytes 1572872 | tf_op jit(solution)/shard_map/ppermute | solution.py:22
  60.0 3.6 %collective-permute-start.13 = (bf16[32,1024]{1,0:T(8,128)(2,1)S(1)}, bf16[32,1024]{1,0:T(8,128)(2,1)S(1)}, u32[]{:S(2)}, u32[]{:S(2)}) collective-permute-start(bf16[32,1024]{1,0:T(8,128)(2,1)S(1)} %get-tuple-element.83), channel_id=1, source_target_pairs={{0,2},{2,0},{4,6},{6,4},{1,3},{3,1},{5,7},{7,5},{8,10},{10,8},{12,... | collective-permute-start | bytes 196616 | tf_op jit(solution)/shard_map/ppermute | solution.py:31
  60.1 4.2 %collective-permute-start.14 = (bf16[32,1024]{1,0:T(8,128)(2,1)S(1)}, bf16[32,1024]{1,0:T(8,128)(2,1)S(1)}, u32[]{:S(2)}, u32[]{:S(2)}) collective-permute-start(bf16[32,1024]{1,0:T(8,128)(2,1)S(1)} %get-tuple-element.85), channel_id=1, source_target_pairs={{0,4},{2,6},{4,0},{6,2},{1,5},{3,7},{5,1},{7,3},{8,12},{10,14},{12... | collective-permute-start | bytes 196616 | tf_op jit(solution)/shard_map/ppermute | solution.py:31
  62.5 4.9 %collective-permute-start.15 = (bf16[32,1024]{1,0:T(8,128)(2,1)S(1)}, bf16[32,1024]{1,0:T(8,128)(2,1)S(1)}, u32[]{:S(2)}, u32[]{:S(2)}) collective-permute-start(bf16[32,1024]{1,0:T(8,128)(2,1)S(1)} %get-tuple-element.84), channel_id=1, source_target_pairs={{0,6},{2,4},{4,2},{6,0},{1,7},{3,5},{5,3},{7,1},{8,14},{10,12},{12... | collective-permute-start | bytes 196616 | tf_op jit(solution)/shard_map/ppermute | solution.py:31
  68.0 6.5 %collective-permute-start.16 = (bf16[32,1024]{1,0:T(8,128)(2,1)S(1)}, bf16[32,1024]{1,0:T(8,128)(2,1)S(1)}, u32[]{:S(2)}, u32[]{:S(2)}) collective-permute-start(bf16[32,1024]{1,0:T(8,128)(2,1)S(1)} %get-tuple-element.61), channel_id=1, source_target_pairs={{0,8},{8,16},{16,24},{1,9},{9,17},{17,25},{2,10},{10,18},{18,26},{... | collective-permute-start | bytes 196616 | tf_op jit(solution)/shard_map/ppermute | solution.py:17
  71.2 3.4 %collective-permute-start.17 = (bf16[32,1024]{1,0:T(8,128)(2,1)S(1)}, bf16[32,1024]{1,0:T(8,128)(2,1)S(1)}, u32[]{:S(2)}, u32[]{:S(2)}) collective-permute-start(bf16[32,1024]{1,0:T(8,128)(2,1)S(1)} %slice_bitcast_fusion), channel_id=1, source_target_pairs={{0,2},{2,0},{4,6},{6,4},{1,3},{3,1},{5,7},{7,5},{8,10},{10,8},{12,... | collective-permute-start | bytes 196616 | tf_op jit(solution)/shard_map/ppermute | solution.py:31
  72.5 5.0 %collective-permute-start.18 = (bf16[32,1024]{1,0:T(8,128)(2,1)S(1)}, bf16[32,1024]{1,0:T(8,128)(2,1)S(1)}, u32[]{:S(2)}, u32[]{:S(2)}) collective-permute-start(bf16[32,1024]{1,0:T(8,128)(2,1)S(1)} %slice_bitcast_fusion), channel_id=1, source_target_pairs={{0,6},{2,4},{4,2},{6,0},{1,7},{3,5},{5,3},{7,1},{8,14},{10,12},{12... | collective-permute-start | bytes 196616 | tf_op jit(solution)/shard_map/ppermute | solution.py:31
  74.5 12.9 %copy-start.28 = (bf16[32,1024]{1,0:T(8,128)(2,1)}, bf16[32,1024]{1,0:T(8,128)(2,1)S(1)}, u32[]{:S(2)}) copy-start(bf16[32,1024]{1,0:T(8,128)(2,1)S(1)} %collective-permute-done.17) | copy-start | bytes 196612
  77.5 9.1 %collective-permute-start.19 = (bf16[32,1024]{1,0:T(8,128)(2,1)S(1)}, bf16[32,1024]{1,0:T(8,128)(2,1)S(1)}, u32[]{:S(2)}, u32[]{:S(2)}) collective-permute-start(bf16[32,1024]{1,0:T(8,128)(2,1)S(1)} %add_convert_fusion.4), channel_id=1, source_target_pairs={{0,2},{2,0},{4,6},{6,4},{1,3},{3,1},{5,7},{7,5},{8,10},{10,8},{12,... | collective-permute-start | bytes 196616 | tf_op jit(solution)/shard_map/ppermute | solution.py:31
  77.5 9.1 %collective-permute-start.20 = (bf16[32,1024]{1,0:T(8,128)(2,1)S(1)}, bf16[32,1024]{1,0:T(8,128)(2,1)S(1)}, u32[]{:S(2)}, u32[]{:S(2)}) collective-permute-start(bf16[32,1024]{1,0:T(8,128)(2,1)S(1)} %add_convert_fusion.4), channel_id=1, source_target_pairs={{0,4},{2,6},{4,0},{6,2},{1,5},{3,7},{5,1},{7,3},{8,12},{10,14},{12... | collective-permute-start | bytes 196616 | tf_op jit(solution)/shard_map/ppermute | solution.py:31
  80.1 6.5 %collective-permute-start.21 = (bf16[32,1024]{1,0:T(8,128)(2,1)S(1)}, bf16[32,1024]{1,0:T(8,128)(2,1)S(1)}, u32[]{:S(2)}, u32[]{:S(2)}) collective-permute-start(bf16[32,1024]{1,0:T(8,128)(2,1)S(1)} %add_convert_fusion.4), channel_id=1, source_target_pairs={{0,6},{2,4},{4,2},{6,0},{1,7},{3,5},{5,3},{7,1},{8,14},{10,12},{12... | collective-permute-start | bytes 196616 | tf_op jit(solution)/shard_map/ppermute | solution.py:31
  82.6 8.0 %collective-permute-start.23 = (bf16[128,2048]{1,0:T(8,128)(2,1)S(1)}, bf16[128,2048]{1,0:T(8,128)(2,1)S(1)}, u32[]{:S(2)}, u32[]{:S(2)}) collective-permute-start(bf16[128,2048]{1,0:T(8,128)(2,1)S(1)} %convolution_convert_fusion.2), channel_id=1, source_target_pairs={{0,1},{1,0},{2,3},{3,2},{4,5},{5,4},{6,7},{7,6},{8,9},{9,8},{10,11... | collective-permute-start | bytes 1572872 | tf_op jit(solution)/shard_map/ppermute | solution.py:22
  87.5 4.7 %collective-permute-start.22 = (bf16[128,2048]{1,0:T(8,128)(2,1)S(1)}, bf16[128,2048]{1,0:T(8,128)(2,1)S(1)}, u32[]{:S(2)}, u32[]{:S(2)}) collective-permute-start(bf16[128,2048]{1,0:T(8,128)(2,1)S(1)} %convolution_convert_fusion.3), channel_id=1, source_target_pairs={{0,1},{1,0},{2,3},{3,2},{4,5},{5,4},{6,7},{7,6},{8,9},{9,8},{10,11... | collective-permute-start | bytes 1572872 | tf_op jit(solution)/shard_map/ppermute | solution.py:22
  95.8 3.6 %collective-permute-start.24 = (bf16[32,1024]{1,0:T(8,128)(2,1)}, bf16[32,1024]{1,0:T(8,128)(2,1)}, u32[]{:S(2)}, u32[]{:S(2)}) collective-permute-start(bf16[32,1024]{1,0:T(8,128)(2,1)} %get-tuple-element.80), channel_id=1, source_target_pairs={{0,2},{2,0},{4,6},{6,4},{1,3},{3,1},{5,7},{7,5},{8,10},{10,8},{12,... | collective-permute-start | bytes 196616 | tf_op jit(solution)/shard_map/ppermute | solution.py:31
  95.8 4.4 %collective-permute-start.25 = (bf16[32,1024]{1,0:T(8,128)(2,1)}, bf16[32,1024]{1,0:T(8,128)(2,1)}, u32[]{:S(2)}, u32[]{:S(2)}) collective-permute-start(bf16[32,1024]{1,0:T(8,128)(2,1)} %get-tuple-element.82), channel_id=1, source_target_pairs={{0,4},{2,6},{4,0},{6,2},{1,5},{3,7},{5,1},{7,3},{8,12},{10,14},{12... | collective-permute-start | bytes 196616 | tf_op jit(solution)/shard_map/ppermute | solution.py:31
  97.1 5.8 %collective-permute-start.26 = (bf16[32,1024]{1,0:T(8,128)(2,1)}, bf16[32,1024]{1,0:T(8,128)(2,1)}, u32[]{:S(2)}, u32[]{:S(2)}) collective-permute-start(bf16[32,1024]{1,0:T(8,128)(2,1)} %get-tuple-element.81), channel_id=1, source_target_pairs={{0,6},{2,4},{4,2},{6,0},{1,7},{3,5},{5,3},{7,1},{8,14},{10,12},{12... | collective-permute-start | bytes 196616 | tf_op jit(solution)/shard_map/ppermute | solution.py:31
  99.3 21.1 %copy-start.5 = (bf16[2048,1024]{1,0:T(8,128)(2,1)S(1)}, bf16[2048,1024]{1,0:T(8,128)(2,1)}, u32[]{:S(2)}) copy-start(bf16[2048,1024]{1,0:T(8,128)(2,1)} %copy-done.3) | copy-start | bytes 12582916
  103.9 7.2 %collective-permute-start.27 = (bf16[32,1024]{1,0:T(8,128)(2,1)S(1)}, bf16[32,1024]{1,0:T(8,128)(2,1)S(1)}, u32[]{:S(2)}, u32[]{:S(2)}) collective-permute-start(bf16[32,1024]{1,0:T(8,128)(2,1)S(1)} %add_convert_fusion.3), channel_id=1, source_target_pairs={{8,0},{16,8},{24,16},{9,1},{17,9},{25,17},{10,2},{18,10},{26,18},{... | collective-permute-start | bytes 196616 | tf_op jit(solution)/shard_map/ppermute | solution.py:17
  109.4 20.6 %copy-start.2 = (bf16[1024,2048]{1,0:T(8,128)(2,1)S(1)}, bf16[1024,2048]{1,0:T(8,128)(2,1)}, u32[]{:S(2)}) copy-start(bf16[1024,2048]{1,0:T(8,128)(2,1)} %copy-done) | copy-start | bytes 12582916
  109.4 4.1 %collective-permute-start.28 = (bf16[32,1024]{1,0:T(8,128)(2,1)S(1)}, bf16[32,1024]{1,0:T(8,128)(2,1)S(1)}, u32[]{:S(2)}, u32[]{:S(2)}) collective-permute-start(bf16[32,1024]{1,0:T(8,128)(2,1)S(1)} %get-tuple-element.44), channel_id=1, source_target_pairs={{0,4},{2,6},{4,0},{6,2},{1,5},{3,7},{5,1},{7,3},{8,12},{10,14},{12... | collective-permute-start | bytes 196616 | tf_op jit(solution)/shard_map/ppermute | solution.py:31
  113.5 3.7 %collective-permute-start.29 = (bf16[32,1024]{1,0:T(8,128)(2,1)S(1)}, bf16[32,1024]{1,0:T(8,128)(2,1)S(1)}, u32[]{:S(2)}, u32[]{:S(2)}) collective-permute-start(bf16[32,1024]{1,0:T(8,128)(2,1)S(1)} %bitcast_select_fusion.1), channel_id=1, source_target_pairs={{0,2},{2,0},{4,6},{6,4},{1,3},{3,1},{5,7},{7,5},{8,10},{10,8},{12,... | collective-permute-start | bytes 196616 | tf_op jit(solution)/shard_map/ppermute | solution.py:31
  115.0 4.4 %collective-permute-start.30 = (bf16[32,1024]{1,0:T(8,128)(2,1)S(1)}, bf16[32,1024]{1,0:T(8,128)(2,1)S(1)}, u32[]{:S(2)}, u32[]{:S(2)}) collective-permute-start(bf16[32,1024]{1,0:T(8,128)(2,1)S(1)} %bitcast_select_fusion.1), channel_id=1, source_target_pairs={{0,4},{2,6},{4,0},{6,2},{1,5},{3,7},{5,1},{7,3},{8,12},{10,14},{12... | collective-permute-start | bytes 196616 | tf_op jit(solution)/shard_map/ppermute | solution.py:31
  115.4 5.1 %collective-permute-start.31 = (bf16[32,1024]{1,0:T(8,128)(2,1)S(1)}, bf16[32,1024]{1,0:T(8,128)(2,1)S(1)}, u32[]{:S(2)}, u32[]{:S(2)}) collective-permute-start(bf16[32,1024]{1,0:T(8,128)(2,1)S(1)} %bitcast_select_fusion.1), channel_id=1, source_target_pairs={{0,6},{2,4},{4,2},{6,0},{1,7},{3,5},{5,3},{7,1},{8,14},{10,12},{12... | collective-permute-start | bytes 196616 | tf_op jit(solution)/shard_map/ppermute | solution.py:31
  122.0 18.4 %copy-start.14 = (bf16[32,1024]{1,0:T(8,128)(2,1)S(1)}, bf16[32,1024]{1,0:T(8,128)(2,1)}, u32[]{:S(2)}) copy-start(bf16[32,1024]{1,0:T(8,128)(2,1)} %copy-done.13) | copy-start | bytes 196612
  122.0 18.4 %copy-start.21 = (bf16[32,1024]{1,0:T(8,128)(2,1)S(1)}, bf16[32,1024]{1,0:T(8,128)(2,1)}, u32[]{:S(2)}) copy-start(bf16[32,1024]{1,0:T(8,128)(2,1)} %copy-done.20) | copy-start | bytes 196612
  122.0 18.4 %copy-start.23 = (bf16[32,1024]{1,0:T(8,128)(2,1)S(1)}, bf16[32,1024]{1,0:T(8,128)(2,1)}, u32[]{:S(2)}) copy-start(bf16[32,1024]{1,0:T(8,128)(2,1)} %copy-done.22) | copy-start | bytes 196612
  122.0 18.4 %copy-start.25 = (bf16[32,1024]{1,0:T(8,128)(2,1)S(1)}, bf16[32,1024]{1,0:T(8,128)(2,1)}, u32[]{:S(2)}) copy-start(bf16[32,1024]{1,0:T(8,128)(2,1)} %copy-done.24) | copy-start | bytes 196612
  122.0 7.5 %collective-permute-start.32 = (bf16[128,2048]{1,0:T(8,128)(2,1)S(1)}, bf16[128,2048]{1,0:T(8,128)(2,1)S(1)}, u32[]{:S(2)}, u32[]{:S(2)}) collective-permute-start(bf16[128,2048]{1,0:T(8,128)(2,1)S(1)} %convolution_convert_fusion.1), channel_id=1, source_target_pairs={{0,1},{1,0},{2,3},{3,2},{4,5},{5,4},{6,7},{7,6},{8,9},{9,8},{10,11... | collective-permute-start | bytes 1572872 | tf_op jit(solution)/shard_map/ppermute | solution.py:22
  131.5 28.6 %copy-start.32 = (bf16[1,32,1024]{2,1,0:T(8,128)(2,1)S(1)}, bf16[1,32,1024]{2,1,0:T(8,128)(2,1)}, u32[]{:S(2)}) copy-start(bf16[1,32,1024]{2,1,0:T(8,128)(2,1)} %get-tuple-element.89) | copy-start | bytes 196612
  131.6 29.3 %copy-start.12 = (bf16[32,1024]{1,0:T(8,128)(2,1)S(1)}, bf16[32,1024]{1,0:T(8,128)(2,1)}, u32[]{:S(2)}) copy-start(bf16[32,1024]{1,0:T(8,128)(2,1)} %copy-done.11) | copy-start | bytes 196612
  131.6 29.3 %copy-start.27 = (bf16[32,1024]{1,0:T(8,128)(2,1)S(1)}, bf16[32,1024]{1,0:T(8,128)(2,1)}, u32[]{:S(2)}) copy-start(bf16[32,1024]{1,0:T(8,128)(2,1)} %copy-done.26) | copy-start | bytes 196612
  131.6 29.3 %copy-start.29 = (bf16[32,1024]{1,0:T(8,128)(2,1)S(1)}, bf16[32,1024]{1,0:T(8,128)(2,1)}, u32[]{:S(2)}) copy-start(bf16[32,1024]{1,0:T(8,128)(2,1)} %copy-done.28) | copy-start | bytes 196612
  131.6 29.3 %copy-start.31 = (bf16[32,1024]{1,0:T(8,128)(2,1)S(1)}, bf16[32,1024]{1,0:T(8,128)(2,1)}, u32[]{:S(2)}) copy-start(bf16[32,1024]{1,0:T(8,128)(2,1)} %copy-done.30) | copy-start | bytes 196612
  131.6 29.4 %copy-start.33 = (bf16[32,1024]{1,0:T(8,128)(2,1)S(1)}, bf16[32,1024]{1,0:T(8,128)(2,1)}, u32[]{:S(2)}) copy-start(bf16[32,1024]{1,0:T(8,128)(2,1)} %get-tuple-element.64) | copy-start | bytes 196612
  131.6 29.4 %copy-start.34 = (bf16[32,1024]{1,0:T(8,128)(2,1)S(1)}, bf16[32,1024]{1,0:T(8,128)(2,1)}, u32[]{:S(2)}) copy-start(bf16[32,1024]{1,0:T(8,128)(2,1)} %get-tuple-element.62) | copy-start | bytes 196612
  131.6 3.6 %collective-permute-start.33 = (bf16[32,1024]{1,0:T(8,128)(2,1)S(1)}, bf16[32,1024]{1,0:T(8,128)(2,1)S(1)}, u32[]{:S(2)}, u32[]{:S(2)}) collective-permute-start(bf16[32,1024]{1,0:T(8,128)(2,1)S(1)} %get-tuple-element.77), channel_id=1, source_target_pairs={{0,2},{2,0},{4,6},{6,4},{1,3},{3,1},{5,7},{7,5},{8,10},{10,8},{12,... | collective-permute-start | bytes 196616 | tf_op jit(solution)/shard_map/ppermute | solution.py:31
  131.7 4.2 %collective-permute-start.34 = (bf16[32,1024]{1,0:T(8,128)(2,1)S(1)}, bf16[32,1024]{1,0:T(8,128)(2,1)S(1)}, u32[]{:S(2)}, u32[]{:S(2)}) collective-permute-start(bf16[32,1024]{1,0:T(8,128)(2,1)S(1)} %get-tuple-element.79), channel_id=1, source_target_pairs={{0,4},{2,6},{4,0},{6,2},{1,5},{3,7},{5,1},{7,3},{8,12},{10,14},{12... | collective-permute-start | bytes 196616 | tf_op jit(solution)/shard_map/ppermute | solution.py:31
  132.9 5.4 %collective-permute-start.35 = (bf16[32,1024]{1,0:T(8,128)(2,1)S(1)}, bf16[32,1024]{1,0:T(8,128)(2,1)S(1)}, u32[]{:S(2)}, u32[]{:S(2)}) collective-permute-start(bf16[32,1024]{1,0:T(8,128)(2,1)S(1)} %get-tuple-element.78), channel_id=1, source_target_pairs={{0,6},{2,4},{4,2},{6,0},{1,7},{3,5},{5,3},{7,1},{8,14},{10,12},{12... | collective-permute-start | bytes 196616 | tf_op jit(solution)/shard_map/ppermute | solution.py:31
  138.4 5.9 %collective-permute-start.38 = (bf16[32,1024]{1,0:T(8,128)(2,1)S(1)}, bf16[32,1024]{1,0:T(8,128)(2,1)S(1)}, u32[]{:S(2)}, u32[]{:S(2)}) collective-permute-start(bf16[32,1024]{1,0:T(8,128)(2,1)S(1)} %add_convert_fusion.2), channel_id=1, source_target_pairs={{8,0},{16,8},{24,16},{9,1},{17,9},{25,17},{10,2},{18,10},{26,18},{... | collective-permute-start | bytes 196616 | tf_op jit(solution)/shard_map/ppermute | solution.py:17
  140.4 3.9 %collective-permute-start.36 = (bf16[32,1024]{1,0:T(8,128)(2,1)S(1)}, bf16[32,1024]{1,0:T(8,128)(2,1)S(1)}, u32[]{:S(2)}, u32[]{:S(2)}) collective-permute-start(bf16[32,1024]{1,0:T(8,128)(2,1)S(1)} %get-tuple-element.46), channel_id=1, source_target_pairs={{0,2},{2,0},{4,6},{6,4},{1,3},{3,1},{5,7},{7,5},{8,10},{10,8},{12,... | collective-permute-start | bytes 196616 | tf_op jit(solution)/shard_map/ppermute | solution.py:31
  142.3 5.5 %collective-permute-start.37 = (bf16[32,1024]{1,0:T(8,128)(2,1)S(1)}, bf16[32,1024]{1,0:T(8,128)(2,1)S(1)}, u32[]{:S(2)}, u32[]{:S(2)}) collective-permute-start(bf16[32,1024]{1,0:T(8,128)(2,1)S(1)} %get-tuple-element.47), channel_id=1, source_target_pairs={{0,6},{2,4},{4,2},{6,0},{1,7},{3,5},{5,3},{7,1},{8,14},{10,12},{12... | collective-permute-start | bytes 196616 | tf_op jit(solution)/shard_map/ppermute | solution.py:31
  147.8 3.6 %collective-permute-start.39 = (bf16[32,1024]{1,0:T(8,128)(2,1)S(1)}, bf16[32,1024]{1,0:T(8,128)(2,1)S(1)}, u32[]{:S(2)}, u32[]{:S(2)}) collective-permute-start(bf16[32,1024]{1,0:T(8,128)(2,1)S(1)} %bitcast_select_fusion), channel_id=1, source_target_pairs={{0,2},{2,0},{4,6},{6,4},{1,3},{3,1},{5,7},{7,5},{8,10},{10,8},{12,... | collective-permute-start | bytes 196616 | tf_op jit(solution)/shard_map/ppermute | solution.py:31
  147.8 4.0 %collective-permute-start.40 = (bf16[32,1024]{1,0:T(8,128)(2,1)S(1)}, bf16[32,1024]{1,0:T(8,128)(2,1)S(1)}, u32[]{:S(2)}, u32[]{:S(2)}) collective-permute-start(bf16[32,1024]{1,0:T(8,128)(2,1)S(1)} %bitcast_select_fusion), channel_id=1, source_target_pairs={{0,4},{2,6},{4,0},{6,2},{1,5},{3,7},{5,1},{7,3},{8,12},{10,14},{12... | collective-permute-start | bytes 196616 | tf_op jit(solution)/shard_map/ppermute | solution.py:31
  148.4 6.0 %collective-permute-start.41 = (bf16[32,1024]{1,0:T(8,128)(2,1)S(1)}, bf16[32,1024]{1,0:T(8,128)(2,1)S(1)}, u32[]{:S(2)}, u32[]{:S(2)}) collective-permute-start(bf16[32,1024]{1,0:T(8,128)(2,1)S(1)} %bitcast_select_fusion), channel_id=1, source_target_pairs={{0,6},{2,4},{4,2},{6,0},{1,7},{3,5},{5,3},{7,1},{8,14},{10,12},{12... | collective-permute-start | bytes 196616 | tf_op jit(solution)/shard_map/ppermute | solution.py:31
  156.0 5.7 %collective-permute-start.42 = (bf16[128,2048]{1,0:T(8,128)(2,1)S(1)}, bf16[128,2048]{1,0:T(8,128)(2,1)S(1)}, u32[]{:S(2)}, u32[]{:S(2)}) collective-permute-start(bf16[128,2048]{1,0:T(8,128)(2,1)S(1)} %convolution_convert_fusion), channel_id=1, source_target_pairs={{0,1},{1,0},{2,3},{3,2},{4,5},{5,4},{6,7},{7,6},{8,9},{9,8},{10,11... | collective-permute-start | bytes 1572872 | tf_op jit(solution)/shard_map/ppermute | solution.py:22
  163.8 12.5 %collective-permute-start.43 = (bf16[32,1024]{1,0:T(8,128)(2,1)S(1)}, bf16[32,1024]{1,0:T(8,128)(2,1)S(1)}, u32[]{:S(2)}, u32[]{:S(2)}) collective-permute-start(bf16[32,1024]{1,0:T(8,128)(2,1)S(1)} %get-tuple-element.71), channel_id=1, source_target_pairs={{0,2},{2,0},{4,6},{6,4},{1,3},{3,1},{5,7},{7,5},{8,10},{10,8},{12,... | collective-permute-start | bytes 196616 | tf_op jit(solution)/shard_map/ppermute | solution.py:31
  163.9 12.4 %collective-permute-start.44 = (bf16[32,1024]{1,0:T(8,128)(2,1)S(1)}, bf16[32,1024]{1,0:T(8,128)(2,1)S(1)}, u32[]{:S(2)}, u32[]{:S(2)}) collective-permute-start(bf16[32,1024]{1,0:T(8,128)(2,1)S(1)} %get-tuple-element.73), channel_id=1, source_target_pairs={{0,4},{2,6},{4,0},{6,2},{1,5},{3,7},{5,1},{7,3},{8,12},{10,14},{12... | collective-permute-start | bytes 196616 | tf_op jit(solution)/shard_map/ppermute | solution.py:31
  166.3 9.9 %collective-permute-start.45 = (bf16[32,1024]{1,0:T(8,128)(2,1)S(1)}, bf16[32,1024]{1,0:T(8,128)(2,1)S(1)}, u32[]{:S(2)}, u32[]{:S(2)}) collective-permute-start(bf16[32,1024]{1,0:T(8,128)(2,1)S(1)} %get-tuple-element.72), channel_id=1, source_target_pairs={{0,6},{2,4},{4,2},{6,0},{1,7},{3,5},{5,3},{7,1},{8,14},{10,12},{12... | collective-permute-start | bytes 196616 | tf_op jit(solution)/shard_map/ppermute | solution.py:31
  (17 other events, 99.3 us)

commit v6 on v5

v6 whole, which is shorter than its diff:
```python
import jax
import jax.numpy as jnp
from jax import lax
from jax.experimental import pallas as pl
from jax.experimental.pallas import tpu as pltpu
from jax.sharding import PartitionSpec as P

BF = jnp.bfloat16
F32 = jnp.float32
LAST = (((1,), (1,)), ((), ()))
FIRST = (((0,), (0,)), ((), ()))


def from_behind(block, axis, distance):
    devices = range(lax.axis_size(axis))
    route = [(i - distance, i) for i in devices if i - distance in devices]
    return lax.ppermute(block, axis, route)


def turn(block, axis, distance):
    size = lax.axis_size(axis)
    return lax.ppermute(block, axis, [(i, (i + distance) % size) for i in range(size)])


def partner(row, j, size):
    return row ^ j if size & (size - 1) == 0 else (j - row) % size


def swap_rows(block, j):
    size = lax.axis_size("row")
    return lax.ppermute(block, "row", [(i, partner(i, j, size)) for i in range(size)])


def gather_rows(block):
    return [swap_rows(block, j) if j else block for j in range(lax.axis_size("row"))]


def scatter_rows(pieces):
    return [swap_rows(piece, j) if j else piece for j, piece in enumerate(pieces)]


def beside(turn):
    size = lax.axis_size("row")
    return [[1], [2], range(3, size)][turn] if size > 2 else [[], [], [1]][turn]


def add_up(first, terms):
    total = first.astype(F32)
    for term in terms:
        total = total + term.astype(F32)
    return total


def after(block, other):
    return lax.optimization_barrier((block, other))[0]


def run(kernel, outs, *ins, flops):
    ins = [pltpu.with_memory_space_constraint(block, pltpu.VMEM) for block in ins]
    size = sum(x.size * x.dtype.itemsize for x in [*ins, *outs])
    return pl.pallas_call(
        kernel,
        in_specs=[pl.BlockSpec(memory_space=pltpu.VMEM)] * len(ins),
        out_specs=[pl.BlockSpec(memory_space=pltpu.VMEM)] * len(outs),
        out_shape=[pltpu.VMEM(x.shape, x.dtype) for x in outs],
        compiler_params=pltpu.CompilerParams(vmem_limit_bytes=32 << 20),
        cost_estimate=pl.CostEstimate(flops=flops, bytes_accessed=size, transcendentals=0),
        name=kernel.__name__,
    )(*ins)


def hold_kernel(source, kept, sem):
    copy = pltpu.make_async_copy(source, kept, sem)
    copy.start()
    copy.wait()


def hold(weight, other):
    return pl.pallas_call(
        hold_kernel,
        in_specs=[pl.BlockSpec(memory_space=pltpu.HBM)],
        out_specs=pl.BlockSpec(memory_space=pltpu.VMEM),
        out_shape=pltpu.VMEM(weight.shape, weight.dtype),
        scratch_shapes=[pltpu.SemaphoreType.DMA],
        compiler_params=pltpu.CompilerParams(vmem_limit_bytes=32 << 20),
        cost_estimate=pl.CostEstimate(flops=0, bytes_accessed=4 * weight.size, transcendentals=0),
        name="hold",
    )(after(weight, other))


def columns(width, step=256):
    step = min(width, step)
    return [slice(n, n + step) for n in range(0, width, step)]


def up_product(*refs):
    *pieces, weight, whole, product = refs
    whole[...] = jnp.concatenate([piece[...] for piece in pieces], axis=0)
    for n in columns(product.shape[1]):
        product[:, n] = matmul(whole[...], weight[:, n]).astype(BF)


def back_product(*refs):
    *pieces, weight, whole, product = refs
    whole[...] = jnp.concatenate([piece[...] for piece in pieces], axis=0)
    for n in columns(product.shape[1]):
        product[:, n] = matmul(whole[...], weight[n, :], LAST).astype(BF)


def put_rows(pieces, n, product):
    rows = pieces[0].shape[0]
    for j, piece in enumerate(pieces):
        piece[:, n] = product[j * rows : (j + 1) * rows].astype(BF)


def down_product(mine, other, weight, act, *pieces):
    for n in columns(act.shape[1]):
        pre = mine[:, n].astype(F32) + other[:, n].astype(F32)
        act[:, n] = jax.nn.silu(pre).astype(BF)
    for n in columns(weight.shape[1]):
        put_rows(pieces, n, matmul(act[...], weight[:, n]))


def down_again(act, weight, *pieces):
    for n in columns(weight.shape[1]):
        put_rows(pieces, n, matmul(act[...], weight[:, n]))


def in_product(mine, other, pre_mine, pre_other, weight, grad_pre, *pieces):
    for n in columns(grad_pre.shape[1]):
        pre = pre_mine[:, n].astype(F32) + pre_other[:, n].astype(F32)
        grad = mine[:, n].astype(F32) + other[:, n].astype(F32)
        grad_pre[:, n] = (grad * silu_slope(pre)).astype(BF)
    for n in columns(weight.shape[0]):
        put_rows(pieces, n, matmul(grad_pre[...], weight[n, :], LAST))


def act_only(mine, other, act):
    for n in columns(act.shape[1]):
        pre = mine[:, n].astype(F32) + other[:, n].astype(F32)
        act[:, n] = jax.nn.silu(pre).astype(BF)


def weight_grad(*refs):
    count = len(refs) // 2
    left = jnp.concatenate([ref[...] for ref in refs[:count]], axis=0)
    right = jnp.concatenate([ref[...] for ref in refs[count:-1]], axis=0)
    refs[-1][...] = matmul(left, right, FIRST).astype(BF)


def weight_product(lefts, rights, step=256):
    rows, width, depth = lefts[0].shape[1], rights[0].shape[1], lefts[0].shape[0]
    step = min(rows, step)
    return pl.pallas_call(
        weight_grad,
        grid=(rows // step,),
        in_specs=[pl.BlockSpec((depth, step), lambda i: (0, i))] * len(lefts)
        + [pl.BlockSpec((depth, width), lambda i: (0, 0))] * len(rights),
        out_specs=pl.BlockSpec((step, width), lambda i: (i, 0)),
        out_shape=jax.ShapeDtypeStruct((rows, width), BF),
        compiler_params=pltpu.CompilerParams(vmem_limit_bytes=32 << 20),
        cost_estimate=pl.CostEstimate(
            flops=2 * rows * width * depth * len(lefts), bytes_accessed=2 * rows * width, transcendentals=0
        ),
        name="weight_grad",
    )(*lefts, *rights)


def other_cols(partial):
    size = lax.axis_size("col")
    if size == 2:
        return turn(partial, "col", 1)
    return (lax.psum(partial.astype(F32), "col") - partial.astype(F32)).astype(BF)


def silu_slope(value):
    sig = jax.nn.sigmoid(value)
    return sig * (1.0 + value * (1.0 - sig))


def pick(table, index):
    return lax.dynamic_index_in_dim(table, index, 0, keepdims=False)


def matmul(a, b, dims=(((1,), (0,)), ((), ()))):
    return lax.dot_general(a, b, dims, preferred_element_type=F32)


def per_device(inputs, sample_ids, send_base, recv_base, w_up, w_down, cotangent):
    section = lax.axis_index("section")
    sections = lax.axis_size("section")
    ticks = inputs.shape[1]
    up_block, down_block = w_up[0], w_down[0]
    rows = lax.axis_size("row")
    piece_rows, width = inputs.shape[2:]
    tokens, hidden = rows * piece_rows, up_block.shape[1]
    flops = 2 * tokens * width * hidden
    pieces_like = [jax.ShapeDtypeStruct((piece_rows, width), BF)] * rows
    whole_like = jax.ShapeDtypeStruct((tokens, width), BF)
    hidden_like = jax.ShapeDtypeStruct((tokens, hidden), BF)

    cot_pieces = [cotangent[0, ticks - 1]] + [None] * (rows - 1)
    full_ins, pres, acts, seen_in, seen_out = [], [], [], [], []
    sending = inputs[0, 0]
    for tick in range(ticks):
        if tick == 0:
            act_in = sending
        else:
            arrived = from_behind(sending, "section", 1)
            act_in = (bases[tick].astype(F32) + arrived.astype(F32)).astype(BF)
        pieces = gather_rows(act_in)
        if tick == 0:
            for j in beside(0):
                cot_pieces[j] = swap_rows(after(cot_pieces[0], act_in), j)
            pieces = after(pieces, [cot_pieces[j] for j in beside(0)])
        if tick == ticks - 1:
            full_cot, first_grads = run(
                back_product, [whole_like, hidden_like], *cot_pieces, hold(down_block, act_in), flops=flops
            )
            pieces = after(pieces, first_grads)
        full_in, partial = run(up_product, [whole_like, hidden_like], *pieces, hold(up_block, act_in), flops=flops)
        other = other_cols(partial)
        if tick == 0:
            samples = [pick(after(sample_ids, partial), t - section + sections - 1) for t in range(ticks)]
            stored = [pick(send_base[0], samples[t]) for t in range(ticks - 1)]
            bases = [jnp.where(section == 0, inputs[0, t], pick(recv_base[0], samples[t])) for t in range(1, ticks)]
            stored, bases, other = lax.optimization_barrier((stored, [None] + bases, other))
        if tick < ticks - 1:
            for j in beside(tick + 1):
                cot_pieces[j] = swap_rows(after(cot_pieces[0], partial), j)
            act, *terms = run(
                down_product, [hidden_like, *pieces_like], partial, other, hold(down_block, partial), flops=flops
            )
            terms = after(terms, [cot_pieces[j] for j in beside(tick + 1)])
            act_out = add_up(act_in, scatter_rows(terms)).astype(BF)
            sending = (act_out.astype(F32) - stored[tick].astype(F32)).astype(BF)
            seen_out.append(act_out)
            acts.append(act)
        full_ins.append(full_in)
        pres.append((partial, other))
        seen_in.append(act_in)
    full_grads = [None] * ticks
    pre_grads = [None] * ticks
    seen_grad = [None] * ticks
    for step in range(ticks):
        tick = ticks - 1 - step
        if step == 0:
            grad_out, full_grad, partial = cot_pieces[0], full_cot, first_grads
        else:
            arrived = from_behind(sending, "section", -1)
            grad_out = jnp.where(section == sections - 1, cotangent[0, tick], arrived)
            if step == 1:
                (act,) = run(act_only, [hidden_like], *after(pres[-1], sending), flops=0)
                acts.append(act)
                out_pieces = list(run(down_again, pieces_like, act, hold(down_block, sending), flops=flops))
                grad_out = after(grad_out, out_pieces)
            pieces = gather_rows(grad_out)
            full_grad, partial = run(
                back_product, [whole_like, hidden_like], *pieces, hold(down_block, grad_out), flops=flops
            )
        other = other_cols(partial)
        for j in beside(step) if step else []:
            out_pieces[j] = swap_rows(after(out_pieces[j], partial), j)
        up_kept = hold(up_block, pres[-1][0] if step == 0 else partial)
        grad_pre, *terms = run(
            in_product, [hidden_like, *pieces_like], partial, other, *pres[tick], up_kept, flops=flops
        )
        if step:
            terms = after(terms, [out_pieces[j] for j in beside(step)])
        sending = add_up(grad_out, scatter_rows(terms)).astype(BF)
        full_grads[tick] = full_grad
        pre_grads[tick] = grad_pre
        seen_grad[tick] = sending
    for j in beside(0):
        out_pieces[j] = swap_rows(after(out_pieces[j], terms), j)
    seen_out.append(add_up(act_in, out_pieces).astype(BF))
    acts, full_grads = after((acts, full_grads), terms)
    grad_up = weight_product(full_ins, pre_grads)
    grad_down = weight_product(acts, full_grads)
    return (
        jnp.stack(seen_in)[None],
        jnp.stack(seen_out)[None],
        jnp.stack(seen_grad)[None],
        grad_up[None],
        grad_down[None],
    )


def solution(mesh):
    placed = (
        P("section", None, "row", "col"),
        P(),
        P("section", None, "row", "col"),
        P("section", None, "row", "col"),
        P("section", "col", "row"),
        P("section", "row", "col"),
        P("section", None, "row", "col"),
    )
    return jax.shard_map(
        per_device,
        mesh=mesh,
        in_specs=placed,
        out_specs=(
            P("section", None, "row", "col"),
            P("section", None, "row", "col"),
            P("section", None, "row", "col"),
            P("section", "col", "row"),
            P("section", "row", "col"),
        ),
        check_vma=False,
    )
```

time: 180 us -> 175 us (0.972)
  matrix products: 27 us -> 0 us
  Pallas kernels: 0.58 us -> 27.2 us
  starting transfers between devices: 79.9 us -> 74.8 us
  other arithmetic: 10.3 us -> 7.82 us
  waiting for transfers between devices: 41.1 us -> 43.2 us
    dot_general x14 -> x0, matrix products: 27 us -> none  [matmul(): return lax.dot_general(a, b, dims, preferred_element_type=F32)]
    pallas_call x1 -> x27, Pallas kernels: 0.58 us -> 27.2 us  [the longest x13 13.8 us: run(): pl.pallas_call(kernel, in_specs=[pl.BlockSpec(memory_space=pltpu.VMEM)] *...]
    ppermute x4, waiting for transfers between devices: 1.17 us -> 8.43 us  [from_behind(): return lax.ppermute(block, axis, route)]
    ppermute x36, starting transfers between devices: 46.5 us -> 42.7 us  [swap_rows(): lax.ppermute(block, 'row', [(i, partner(i, j, size)) for i in range(size)])]
    ppermute x36, waiting for transfers between devices: 35.3 us -> 32.3 us  [swap_rows(): lax.ppermute(block, 'row', [(i, partner(i, j, size)) for i in range(size)])]
    convert_element_type x7 -> x2, other arithmetic: 4.13 us -> 1.56 us  [per_device(): sending = add_up(grad_out, scatter_rows(terms)).astype(BF)]
    unnamed x82 -> x50, local copies, waits for them, and re-layouts: 7.15 us -> 9.52 us
    ppermute x6, waiting for transfers between devices: 4.62 us -> 2.46 us  [turn(): lax.ppermute(block, axis, [(i, (i + distance) % size) for i in range(size)])]
  transfers between devices with their start and end apart: 46 -> 46, of which waited for: 22 -> 24; matrix products, arithmetic and copies ran while one was open for 10% -> 2% of each run, Pallas kernels for 0% -> 12%
where the time goes in v6:
time: 175 us; the launch traced here: 173 us
  starting transfers between devices  74.8 us (43%)
  waiting for transfers between devices  43.2 us (25%)
  Pallas kernels  27.2 us (16%)
  local copies, waits for them, and re-layouts  12.4 us (7%)
  other arithmetic  7.82 us (4%)
  between operations  7.1 us (4%)
    ppermute x36, starting transfers between devices, swap_rows(): lax.ppermute(block, 'row', [(i, partner(i, j, size)) for i in range(size)])  42.7 us
    ppermute x36, waiting for transfers between devices, swap_rows(): lax.ppermute(block, 'row', [(i, partner(i, j, size)) for i in range(size)])  32.3 us
    ppermute x6, starting transfers between devices, turn(): lax.ppermute(block, axis, [(i, (i + distance) % size) for i in range(size)])  21 us
    pallas_call x13, Pallas kernels, run(): pl.pallas_call(kernel, in_specs=[pl.BlockSpec(memory_space=pltpu.VMEM)] *...  13.8 us
    ppermute x4, starting transfers between devices, from_behind(): return lax.ppermute(block, axis, route)  11.1 us
    pallas_call x2, Pallas kernels, weight_product(): pl.pallas_call(weight_grad, grid=(rows // step,), in_specs=[pl.BlockSpec(...  9.93 us
    unnamed x50, local copies, waits for them, and re-layouts  9.52 us
    ppermute x4, waiting for transfers between devices, from_behind(): return lax.ppermute(block, axis, route)  8.43 us
  transfers between devices with their start and end apart: 46, of which 24 were waited for; matrix products, arithmetic and copies ran while one was open for 2% of the time, Pallas kernels for 12%

profile of v6, /device:TPU:3, one launch (start us, length us, event | category | flops | bytes accessed | tf_op | source)
XLA Modules:
  0.0 172.5 jit_solution(6783960935682932741)
XLA Ops:
  0.6 1.5 slice_bitcast_fusion.2
  3.0 1.3 collective-permute-start.3
  4.4 2.3 %collective-permute-start.1 = (bf16[32,1024]{1,0:T(8,128)(2,1)S(1)}, bf16[32,1024]{1,0:T(8,128)(2,1)S(1)}, u32[]{:S(2)}, u32[]{:S(2)}) collective-permute-start(bf16[32,1024]{1,0:T(8,128)(2,1)S(1)} %get-tuple-element.104.refs_0_), channel_id=1, source_target_pairs={{0,4},{2,6},{4,0},{6,2},{1,5},{3,7},{5,1},{7,3},{8,12},{10,14},{12... | collective-permute-start | bytes 196616 | tf_op jit(solution)/shard_map/ppermute | solution.py:31
  7.8 2.2 %copy-done.4 = bf16[1,1024,2048]{2,1,0:T(8,128)(2,1)S(1)} copy-done((bf16[1,1024,2048]{2,1,0:T(8,128)(2,1)S(1)}, bf16[1,1024,2048]{2,1,0:T(8,128)(2,1)}, u32[]{:S(2)}) %copy-start.4) | copy-done | bytes 4194328
  10.3 2.2 %collective-permute-done.2.refs_3_ = bf16[32,1024]{1,0:T(8,128)(2,1)S(1)} collective-permute-done((bf16[32,1024]{1,0:T(8,128)(2,1)S(1)}, bf16[32,1024]{1,0:T(8,128)(2,1)S(1)}, u32[]{:S(2)}, u32[]{:S(2)}) %collective-permute-start.2) | collective-permute-done | bytes 65568 | tf_op jit(solution)/shard_map/ppermute | solution.py:31
  13.3 1.9 %collective-permute-start.4 = (bf16[128,2048]{1,0:T(8,128)(2,1)S(1)}, bf16[128,2048]{1,0:T(8,128)(2,1)S(1)}, u32[]{:S(2)}, u32[]{:S(2)}) collective-permute-start(bf16[128,2048]{1,0:T(8,128)(2,1)S(1)} %get-tuple-element.109.mine.pre_mine), channel_id=1, source_target_pairs={{0,1},{1,0},{2,3},{3,2},{4,5},{5,4},{6,7},{7,6},{8,9},{9,8},{10,11... | collective-permute-start | bytes 1572872 | tf_op jit(solution)/shard_map/ppermute | solution.py:22
  19.6 2.1 %collective-permute-start.5 = (bf16[32,1024]{1,0:T(8,128)(2,1)S(1)}, bf16[32,1024]{1,0:T(8,128)(2,1)S(1)}, u32[]{:S(2)}, u32[]{:S(2)}) collective-permute-start(bf16[32,1024]{1,0:T(8,128)(2,1)S(1)} %slice_bitcast_fusion.refs_0_), channel_id=1, source_target_pairs={{0,4},{2,6},{4,0},{6,2},{1,5},{3,7},{5,1},{7,3},{8,12},{10,14},{12... | collective-permute-start | bytes 196616 | tf_op jit(solution)/shard_map/ppermute | solution.py:31
  24.7 2.2 %copy-done = bf16[1,2048,1024]{2,1,0:T(8,128)(2,1)S(1)} copy-done((bf16[1,2048,1024]{2,1,0:T(8,128)(2,1)S(1)}, bf16[1,2048,1024]{2,1,0:T(8,128)(2,1)}, u32[]{:S(2)}) %copy-start) | copy-done | bytes 4194328
  29.3 2.3 %collective-permute-start.8 = (bf16[32,1024]{1,0:T(8,128)(2,1)S(1)}, bf16[32,1024]{1,0:T(8,128)(2,1)S(1)}, u32[]{:S(2)}, u32[]{:S(2)}) collective-permute-start(bf16[32,1024]{1,0:T(8,128)(2,1)S(1)} %get-tuple-element.122), channel_id=1, source_target_pairs={{0,6},{2,4},{4,2},{6,0},{1,7},{3,5},{5,3},{7,1},{8,14},{10,12},{12... | collective-permute-start | bytes 196616 | tf_op jit(solution)/shard_map/ppermute | solution.py:31
  32.4 2.5 %collective-permute-done.8 = bf16[32,1024]{1,0:T(8,128)(2,1)S(1)} collective-permute-done((bf16[32,1024]{1,0:T(8,128)(2,1)S(1)}, bf16[32,1024]{1,0:T(8,128)(2,1)S(1)}, u32[]{:S(2)}, u32[]{:S(2)}) %collective-permute-start.8) | collective-permute-done | bytes 65568 | tf_op jit(solution)/shard_map/ppermute | solution.py:31
  35.5 3.1 %collective-permute-start.9 = (bf16[32,1024]{1,0:T(8,128)(2,1)S(1)}, bf16[32,1024]{1,0:T(8,128)(2,1)S(1)}, u32[]{:S(2)}, u32[]{:S(2)}) collective-permute-start(bf16[32,1024]{1,0:T(8,128)(2,1)S(1)} %get-tuple-element.203), channel_id=1, source_target_pairs={{0,8},{8,16},{16,24},{1,9},{9,17},{17,25},{2,10},{10,18},{18,26},{... | collective-permute-start | bytes 196616 | tf_op jit(solution)/shard_map/ppermute | solution.py:17
  38.6 1.9 %collective-permute-done.9 = bf16[32,1024]{1,0:T(8,128)(2,1)S(1)} collective-permute-done((bf16[32,1024]{1,0:T(8,128)(2,1)S(1)}, bf16[32,1024]{1,0:T(8,128)(2,1)S(1)}, u32[]{:S(2)}, u32[]{:S(2)}) %collective-permute-start.9) | collective-permute-done | bytes 65568 | tf_op jit(solution)/shard_map/ppermute | solution.py:17
  40.5 1.6 collective-permute-start.10
  42.6 1.8 %collective-permute-start.12 = (bf16[32,1024]{1,0:T(8,128)(2,1)S(1)}, bf16[32,1024]{1,0:T(8,128)(2,1)S(1)}, u32[]{:S(2)}, u32[]{:S(2)}) collective-permute-start(bf16[32,1024]{1,0:T(8,128)(2,1)S(1)} %add_convert_fusion.6.refs_0_), channel_id=1, source_target_pairs={{0,6},{2,4},{4,2},{6,0},{1,7},{3,5},{5,3},{7,1},{8,14},{10,12},{12... | collective-permute-start | bytes 196616 | tf_op jit(solution)/shard_map/ppermute | solution.py:31
  44.7 2.0 %collective-permute-done.11.refs_2_ = bf16[32,1024]{1,0:T(8,128)(2,1)S(1)} collective-permute-done((bf16[32,1024]{1,0:T(8,128)(2,1)S(1)}, bf16[32,1024]{1,0:T(8,128)(2,1)S(1)}, u32[]{:S(2)}, u32[]{:S(2)}) %collective-permute-start.11) | collective-permute-done | bytes 65568 | tf_op jit(solution)/shard_map/ppermute | solution.py:31
  49.1 4.9 %collective-permute-start.13 = (bf16[128,2048]{1,0:T(8,128)(2,1)S(1)}, bf16[128,2048]{1,0:T(8,128)(2,1)S(1)}, u32[]{:S(2)}, u32[]{:S(2)}) collective-permute-start(bf16[128,2048]{1,0:T(8,128)(2,1)S(1)} %get-tuple-element.126.mine.pre_mine), channel_id=1, source_target_pairs={{0,1},{1,0},{2,3},{3,2},{4,5},{5,4},{6,7},{7,6},{8,9},{9,8},{10,11... | collective-permute-start | bytes 1572872 | tf_op jit(solution)/shard_map/ppermute | solution.py:22
  54.0 1.7 collective-permute-start.14
  56.8 2.8 %collective-permute-done.14.refs_3_ = bf16[32,1024]{1,0:T(8,128)(2,1)S(1)} collective-permute-done((bf16[32,1024]{1,0:T(8,128)(2,1)S(1)}, bf16[32,1024]{1,0:T(8,128)(2,1)S(1)}, u32[]{:S(2)}, u32[]{:S(2)}) %collective-permute-start.14) | collective-permute-done | bytes 65568 | tf_op jit(solution)/shard_map/ppermute | solution.py:31
  59.5 2.0 %collective-permute-start.16 = (bf16[32,1024]{1,0:T(8,128)(2,1)S(1)}, bf16[32,1024]{1,0:T(8,128)(2,1)S(1)}, u32[]{:S(2)}, u32[]{:S(2)}) collective-permute-start(bf16[32,1024]{1,0:T(8,128)(2,1)S(1)} %get-tuple-element.135), channel_id=1, source_target_pairs={{0,4},{2,6},{4,0},{6,2},{1,5},{3,7},{5,1},{7,3},{8,12},{10,14},{12... | collective-permute-start | bytes 196616 | tf_op jit(solution)/shard_map/ppermute | solution.py:31
  61.5 1.6 collective-permute-start.17
  63.6 3.5 %collective-permute-done.17 = bf16[32,1024]{1,0:T(8,128)(2,1)S(1)} collective-permute-done((bf16[32,1024]{1,0:T(8,128)(2,1)S(1)}, bf16[32,1024]{1,0:T(8,128)(2,1)S(1)}, u32[]{:S(2)}, u32[]{:S(2)}) %collective-permute-start.17) | collective-permute-done | bytes 65568 | tf_op jit(solution)/shard_map/ppermute | solution.py:31
  67.7 4.0 %collective-permute-start.18 = (bf16[32,1024]{1,0:T(8,128)(2,1)S(1)}, bf16[32,1024]{1,0:T(8,128)(2,1)S(1)}, u32[]{:S(2)}, u32[]{:S(2)}) collective-permute-start(bf16[32,1024]{1,0:T(8,128)(2,1)S(1)} %get-tuple-element.201), channel_id=1, source_target_pairs={{0,8},{8,16},{16,24},{1,9},{9,17},{17,25},{2,10},{10,18},{18,26},{... | collective-permute-start | bytes 196616 | tf_op jit(solution)/shard_map/ppermute | solution.py:17
  71.7 1.3 collective-permute-done.18
  73.2 2.0 %collective-permute-start.20 = (bf16[32,1024]{1,0:T(8,128)(2,1)S(1)}, bf16[32,1024]{1,0:T(8,128)(2,1)S(1)}, u32[]{:S(2)}, u32[]{:S(2)}) collective-permute-start(bf16[32,1024]{1,0:T(8,128)(2,1)S(1)} %add_convert_fusion.4.refs_0_), channel_id=1, source_target_pairs={{0,4},{2,6},{4,0},{6,2},{1,5},{3,7},{5,1},{7,3},{8,12},{10,14},{12... | collective-permute-start | bytes 196616 | tf_op jit(solution)/shard_map/ppermute | solution.py:31
  75.1 1.6 collective-permute-start.21
  77.3 1.5 back_product.3
  79.5 3.7 %collective-permute-start.23 = (bf16[128,2048]{1,0:T(8,128)(2,1)S(1)}, bf16[128,2048]{1,0:T(8,128)(2,1)S(1)}, u32[]{:S(2)}, u32[]{:S(2)}) collective-permute-start(bf16[128,2048]{1,0:T(8,128)(2,1)S(1)} %get-tuple-element.139.mine), channel_id=1, source_target_pairs={{0,1},{1,0},{2,3},{3,2},{4,5},{5,4},{6,7},{7,6},{8,9},{9,8},{10,11... | collective-permute-start | bytes 1572872 | tf_op jit(solution)/shard_map/ppermute | solution.py:22
  84.6 1.2 collective-permute-start.22
  86.1 1.2 collective-permute-done.22.pre_other.other
  87.4 1.6 in_product.3
  89.7 2.0 %collective-permute-start.25 = (bf16[32,1024]{1,0:T(8,128)(2,1)S(1)}, bf16[32,1024]{1,0:T(8,128)(2,1)S(1)}, u32[]{:S(2)}, u32[]{:S(2)}) collective-permute-start(bf16[32,1024]{1,0:T(8,128)(2,1)S(1)} %get-tuple-element.149), channel_id=1, source_target_pairs={{0,4},{2,6},{4,0},{6,2},{1,5},{3,7},{5,1},{7,3},{8,12},{10,14},{12... | collective-permute-start | bytes 196616 | tf_op jit(solution)/shard_map/ppermute | solution.py:31
  91.7 1.5 collective-permute-start.26
  93.8 2.9 %collective-permute-done.26 = bf16[32,1024]{1,0:T(8,128)(2,1)S(1)} collective-permute-done((bf16[32,1024]{1,0:T(8,128)(2,1)S(1)}, bf16[32,1024]{1,0:T(8,128)(2,1)S(1)}, u32[]{:S(2)}, u32[]{:S(2)}) %collective-permute-start.26) | collective-permute-done | bytes 65568 | tf_op jit(solution)/shard_map/ppermute | solution.py:31
  96.7 1.5 add_convert_fusion.3
  98.3 1.9 %collective-permute-start.27 = (bf16[32,1024]{1,0:T(8,128)(2,1)}, bf16[32,1024]{1,0:T(8,128)(2,1)}, u32[]{:S(2)}, u32[]{:S(2)}) collective-permute-start(bf16[32,1024]{1,0:T(8,128)(2,1)} %add_convert_fusion.3), channel_id=1, source_target_pairs={{8,0},{16,8},{24,16},{9,1},{17,9},{25,17},{10,2},{18,10},{26,18},{... | collective-permute-start | bytes 196616 | tf_op jit(solution)/shard_map/ppermute | solution.py:17
  100.2 2.2 %copy-done.2 = bf16[1,2048,1024]{2,1,0:T(8,128)(2,1)S(1)} copy-done((bf16[1,2048,1024]{2,1,0:T(8,128)(2,1)S(1)}, bf16[1,2048,1024]{2,1,0:T(8,128)(2,1)}, u32[]{:S(2)}) %copy-start.2) | copy-done | bytes 4194328
  103.7 1.4 collective-permute-done.27
  106.9 1.1 collective-permute-start.29
  108.0 1.5 collective-permute-start.30
  109.9 1.8 %collective-permute-done.29.refs_2_ = bf16[32,1024]{1,0:T(8,128)(2,1)S(1)} collective-permute-done((bf16[32,1024]{1,0:T(8,128)(2,1)S(1)}, bf16[32,1024]{1,0:T(8,128)(2,1)S(1)}, u32[]{:S(2)}, u32[]{:S(2)}) %collective-permute-start.29) | collective-permute-done | bytes 65568 | tf_op jit(solution)/shard_map/ppermute | solution.py:31
  111.7 1.4 collective-permute-done.30.refs_3_
  113.1 1.5 back_product.4
  114.6 4.4 %collective-permute-start.31 = (bf16[128,2048]{1,0:T(8,128)(2,1)S(1)}, bf16[128,2048]{1,0:T(8,128)(2,1)S(1)}, u32[]{:S(2)}, u32[]{:S(2)}) collective-permute-start(bf16[128,2048]{1,0:T(8,128)(2,1)S(1)} %get-tuple-element.160.mine), channel_id=1, source_target_pairs={{0,1},{1,0},{2,3},{3,2},{4,5},{5,4},{6,7},{7,6},{8,9},{9,8},{10,11... | collective-permute-start | bytes 1572872 | tf_op jit(solution)/shard_map/ppermute | solution.py:22
  119.3 1.2 collective-permute-done.31.other
  120.6 1.5 in_product.4
  122.1 2.6 %collective-permute-done.32 = bf16[32,1024]{1,0:T(8,128)(2,1)S(1)} collective-permute-done((bf16[32,1024]{1,0:T(8,128)(2,1)S(1)}, bf16[32,1024]{1,0:T(8,128)(2,1)S(1)}, u32[]{:S(2)}, u32[]{:S(2)}) %collective-permute-start.32) | collective-permute-done | bytes 65568 | tf_op jit(solution)/shard_map/ppermute | solution.py:31
  124.7 1.9 %collective-permute-start.34 = (bf16[32,1024]{1,0:T(8,128)(2,1)S(1)}, bf16[32,1024]{1,0:T(8,128)(2,1)S(1)}, u32[]{:S(2)}, u32[]{:S(2)}) collective-permute-start(bf16[32,1024]{1,0:T(8,128)(2,1)S(1)} %get-tuple-element.169), channel_id=1, source_target_pairs={{0,4},{2,6},{4,0},{6,2},{1,5},{3,7},{5,1},{7,3},{8,12},{10,14},{12... | collective-permute-start | bytes 196616 | tf_op jit(solution)/shard_map/ppermute | solution.py:31
  126.6 1.7 collective-permute-start.35
  128.8 3.0 %collective-permute-done.35 = bf16[32,1024]{1,0:T(8,128)(2,1)S(1)} collective-permute-done((bf16[32,1024]{1,0:T(8,128)(2,1)S(1)}, bf16[32,1024]{1,0:T(8,128)(2,1)S(1)}, u32[]{:S(2)}, u32[]{:S(2)}) %collective-permute-start.35) | collective-permute-done | bytes 65568 | tf_op jit(solution)/shard_map/ppermute | solution.py:31
  131.9 2.1 %collective-permute-start.36 = (bf16[32,1024]{1,0:T(8,128)(2,1)S(1)}, bf16[32,1024]{1,0:T(8,128)(2,1)S(1)}, u32[]{:S(2)}, u32[]{:S(2)}) collective-permute-start(bf16[32,1024]{1,0:T(8,128)(2,1)S(1)} %add_convert_fusion.2), channel_id=1, source_target_pairs={{8,0},{16,8},{24,16},{9,1},{17,9},{25,17},{10,2},{18,10},{26,18},{... | collective-permute-start | bytes 196616 | tf_op jit(solution)/shard_map/ppermute | solution.py:17
  134.0 3.8 %collective-permute-done.36 = bf16[32,1024]{1,0:T(8,128)(2,1)S(1)} collective-permute-done((bf16[32,1024]{1,0:T(8,128)(2,1)S(1)}, bf16[32,1024]{1,0:T(8,128)(2,1)S(1)}, u32[]{:S(2)}, u32[]{:S(2)}) %collective-permute-start.36) | collective-permute-done | bytes 65568 | tf_op jit(solution)/shard_map/ppermute | solution.py:17
  138.4 1.3 collective-permute-start.38
  139.7 1.7 collective-permute-start.39
  142.4 2.3 %collective-permute-done.39.refs_3_ = bf16[32,1024]{1,0:T(8,128)(2,1)S(1)} collective-permute-done((bf16[32,1024]{1,0:T(8,128)(2,1)S(1)}, bf16[32,1024]{1,0:T(8,128)(2,1)S(1)}, u32[]{:S(2)}, u32[]{:S(2)}) %collective-permute-start.39) | collective-permute-done | bytes 65568 | tf_op jit(solution)/shard_map/ppermute | solution.py:31
  144.7 1.5 back_product.5
  146.3 4.9 %collective-permute-start.40 = (bf16[128,2048]{1,0:T(8,128)(2,1)S(1)}, bf16[128,2048]{1,0:T(8,128)(2,1)S(1)}, u32[]{:S(2)}, u32[]{:S(2)}) collective-permute-start(bf16[128,2048]{1,0:T(8,128)(2,1)S(1)} %get-tuple-element.172.mine), channel_id=1, source_target_pairs={{0,1},{1,0},{2,3},{3,2},{4,5},{5,4},{6,7},{7,6},{8,9},{9,8},{10,11... | collective-permute-start | bytes 1572872 | tf_op jit(solution)/shard_map/ppermute | solution.py:22
  151.1 1.6 collective-permute-start.41
  153.8 1.6 in_product.5
  155.4 1.2 collective-permute-done.41
  156.6 1.9 %collective-permute-start.44 = (bf16[32,1024]{1,0:T(8,128)(2,1)S(1)}, bf16[32,1024]{1,0:T(8,128)(2,1)S(1)}, u32[]{:S(2)}, u32[]{:S(2)}) collective-permute-start(bf16[32,1024]{1,0:T(8,128)(2,1)S(1)} %get-tuple-element.181), channel_id=1, source_target_pairs={{0,4},{2,6},{4,0},{6,2},{1,5},{3,7},{5,1},{7,3},{8,12},{10,14},{12... | collective-permute-start | bytes 196616 | tf_op jit(solution)/shard_map/ppermute | solution.py:31
  158.5 1.7 collective-permute-start.45
  160.2 5.7 %weight_grad.3 = bf16[2048,1024]{1,0:T(8,128)(2,1)} custom-call(bf16[128,2048]{1,0:T(8,128)(2,1)S(1)} %copy-done.8, bf16[128,2048]{1,0:T(8,128)(2,1)S(1)} %copy-done.10, bf16[128,2048]{1,0:T(8,128)(2,1)S(1)} %act_only.1.act.refs_2_, bf16[128,1024]{1,0:T(8,128)(2,1)S(1)} %get-tuple-element.198.refs_3_, bf16[128,1024]{1,0:T(8,128)(2,1)S(1)} %get-tuple-element.199.refs_4_, ...), custom_call_target="tpu_custom_call" | custom-call | flops 1610612736 | bytes 4194304 | tf_op jit(solution)/shard_map/weight_grad/pallas_call | solution.py:154
  165.9 4.3 %weight_grad.2 = bf16[1024,2048]{1,0:T(8,128)(2,1)} custom-call(bf16[128,1024]{1,0:T(8,128)(2,1)S(1)} %get-tuple-element.184.refs_0_, bf16[128,1024]{1,0:T(8,128)(2,1)S(1)} %copy-done.14, bf16[128,1024]{1,0:T(8,128)(2,1)S(1)} %copy-done.18, bf16[128,2048]{1,0:T(8,128)(2,1)S(1)} %get-tuple-element.187.refs_3_, ...), custom_call_target="tpu_custom_call" | custom-call | flops 1610612736 | bytes 4194304 | tf_op jit(solution)/shard_map/weight_grad/pallas_call | solution.py:154
  170.2 1.5 maximum_bitcast_fusion.2
  (122 shorter events, 26.0 us)
Async XLA Ops:
  3.0 7.4 %collective-permute-start.3 = (bf16[32,1024]{1,0:T(8,128)(2,1)S(1)}, bf16[32,1024]{1,0:T(8,128)(2,1)S(1)}, u32[]{:S(2)}, u32[]{:S(2)}) collective-permute-start(bf16[32,1024]{1,0:T(8,128)(2,1)S(1)} %slice_bitcast_fusion.refs_0_), channel_id=1, source_target_pairs={{0,2},{2,0},{4,6},{6,4},{1,3},{3,1},{5,7},{7,5},{8,10},{10,8},{12,... | collective-permute-start | bytes 196616 | tf_op jit(solution)/shard_map/ppermute | solution.py:31
  4.3 6.1 %collective-permute-start = (bf16[32,1024]{1,0:T(8,128)(2,1)S(1)}, bf16[32,1024]{1,0:T(8,128)(2,1)S(1)}, u32[]{:S(2)}, u32[]{:S(2)}) collective-permute-start(bf16[32,1024]{1,0:T(8,128)(2,1)S(1)} %get-tuple-element.104.refs_0_), channel_id=1, source_target_pairs={{0,2},{2,0},{4,6},{6,4},{1,3},{3,1},{5,7},{7,5},{8,10},{10,8},{12,... | collective-permute-start | bytes 196616 | tf_op jit(solution)/shard_map/ppermute | solution.py:31
  4.4 5.9 %collective-permute-start.1 = (bf16[32,1024]{1,0:T(8,128)(2,1)S(1)}, bf16[32,1024]{1,0:T(8,128)(2,1)S(1)}, u32[]{:S(2)}, u32[]{:S(2)}) collective-permute-start(bf16[32,1024]{1,0:T(8,128)(2,1)S(1)} %get-tuple-element.104.refs_0_), channel_id=1, source_target_pairs={{0,4},{2,6},{4,0},{6,2},{1,5},{3,7},{5,1},{7,3},{8,12},{10,14},{12... | collective-permute-start | bytes 196616 | tf_op jit(solution)/shard_map/ppermute | solution.py:31
  6.7 5.8 %collective-permute-start.2 = (bf16[32,1024]{1,0:T(8,128)(2,1)S(1)}, bf16[32,1024]{1,0:T(8,128)(2,1)S(1)}, u32[]{:S(2)}, u32[]{:S(2)}) collective-permute-start(bf16[32,1024]{1,0:T(8,128)(2,1)S(1)} %get-tuple-element.104.refs_0_), channel_id=1, source_target_pairs={{0,6},{2,4},{4,2},{6,0},{1,7},{3,5},{5,3},{7,1},{8,14},{10,12},{12... | collective-permute-start | bytes 196616 | tf_op jit(solution)/shard_map/ppermute | solution.py:31
  10.3 4.9 %copy-start.24 = (s32[6]{0:T(128)S(1)}, s32[6]{0:T(128)}, u32[]{:S(2)}) copy-start(s32[6]{0:T(128)} %param.8) | copy-start | bytes 76
  10.3 13.4 %copy-start.20 = (bf16[1,3,32,1024]{3,2,1,0:T(8,128)(2,1)S(1)}, bf16[1,3,32,1024]{3,2,1,0:T(8,128)(2,1)}, u32[]{:S(2)}) copy-start(bf16[1,3,32,1024]{3,2,1,0:T(8,128)(2,1)} %param.7) | copy-start | bytes 589828
  13.3 13.9 %collective-permute-start.4 = (bf16[128,2048]{1,0:T(8,128)(2,1)S(1)}, bf16[128,2048]{1,0:T(8,128)(2,1)S(1)}, u32[]{:S(2)}, u32[]{:S(2)}) collective-permute-start(bf16[128,2048]{1,0:T(8,128)(2,1)S(1)} %get-tuple-element.109.mine.pre_mine), channel_id=1, source_target_pairs={{0,1},{1,0},{2,3},{3,2},{4,5},{5,4},{6,7},{7,6},{8,9},{9,8},{10,11... | collective-permute-start | bytes 1572872 | tf_op jit(solution)/shard_map/ppermute | solution.py:22
  19.6 8.3 %collective-permute-start.5 = (bf16[32,1024]{1,0:T(8,128)(2,1)S(1)}, bf16[32,1024]{1,0:T(8,128)(2,1)S(1)}, u32[]{:S(2)}, u32[]{:S(2)}) collective-permute-start(bf16[32,1024]{1,0:T(8,128)(2,1)S(1)} %slice_bitcast_fusion.refs_0_), channel_id=1, source_target_pairs={{0,4},{2,6},{4,0},{6,2},{1,5},{3,7},{5,1},{7,3},{8,12},{10,14},{12... | collective-permute-start | bytes 196616 | tf_op jit(solution)/shard_map/ppermute | solution.py:31
  27.2 17.2 %copy-start.5 = (bf16[1,1024,2048]{2,1,0:T(8,128)(2,1)S(1)}, bf16[1,1024,2048]{2,1,0:T(8,128)(2,1)}, u32[]{:S(2)}) copy-start(bf16[1,1024,2048]{2,1,0:T(8,128)(2,1)} %param.11) | copy-start | bytes 12582916
  28.0 16.4 %copy-start.7 = (bf16[128,2048]{1,0:T(8,128)(2,1)}, bf16[128,2048]{1,0:T(8,128)(2,1)S(1)}, u32[]{:S(2)}) copy-start(bf16[128,2048]{1,0:T(8,128)(2,1)S(1)} %get-tuple-element.195.refs_0_) | copy-start | bytes 1572868
  28.0 3.6 %collective-permute-start.6 = (bf16[32,1024]{1,0:T(8,128)(2,1)S(1)}, bf16[32,1024]{1,0:T(8,128)(2,1)S(1)}, u32[]{:S(2)}, u32[]{:S(2)}) collective-permute-start(bf16[32,1024]{1,0:T(8,128)(2,1)S(1)} %get-tuple-element.120), channel_id=1, source_target_pairs={{0,2},{2,0},{4,6},{6,4},{1,3},{3,1},{5,7},{7,5},{8,10},{10,8},{12,... | collective-permute-start | bytes 196616 | tf_op jit(solution)/shard_map/ppermute | solution.py:31
  28.2 4.1 %collective-permute-start.7 = (bf16[32,1024]{1,0:T(8,128)(2,1)S(1)}, bf16[32,1024]{1,0:T(8,128)(2,1)S(1)}, u32[]{:S(2)}, u32[]{:S(2)}) collective-permute-start(bf16[32,1024]{1,0:T(8,128)(2,1)S(1)} %get-tuple-element.121), channel_id=1, source_target_pairs={{0,4},{2,6},{4,0},{6,2},{1,5},{3,7},{5,1},{7,3},{8,12},{10,14},{12... | collective-permute-start | bytes 196616 | tf_op jit(solution)/shard_map/ppermute | solution.py:31
  29.3 5.5 %collective-permute-start.8 = (bf16[32,1024]{1,0:T(8,128)(2,1)S(1)}, bf16[32,1024]{1,0:T(8,128)(2,1)S(1)}, u32[]{:S(2)}, u32[]{:S(2)}) collective-permute-start(bf16[32,1024]{1,0:T(8,128)(2,1)S(1)} %get-tuple-element.122), channel_id=1, source_target_pairs={{0,6},{2,4},{4,2},{6,0},{1,7},{3,5},{5,3},{7,1},{8,14},{10,12},{12... | collective-permute-start | bytes 196616 | tf_op jit(solution)/shard_map/ppermute | solution.py:31
  35.5 5.0 %collective-permute-start.9 = (bf16[32,1024]{1,0:T(8,128)(2,1)S(1)}, bf16[32,1024]{1,0:T(8,128)(2,1)S(1)}, u32[]{:S(2)}, u32[]{:S(2)}) collective-permute-start(bf16[32,1024]{1,0:T(8,128)(2,1)S(1)} %get-tuple-element.203), channel_id=1, source_target_pairs={{0,8},{8,16},{16,24},{1,9},{9,17},{17,25},{2,10},{10,18},{18,26},{... | collective-permute-start | bytes 196616 | tf_op jit(solution)/shard_map/ppermute | solution.py:17
  40.5 4.1 %collective-permute-start.10 = (bf16[32,1024]{1,0:T(8,128)(2,1)S(1)}, bf16[32,1024]{1,0:T(8,128)(2,1)S(1)}, u32[]{:S(2)}, u32[]{:S(2)}) collective-permute-start(bf16[32,1024]{1,0:T(8,128)(2,1)S(1)} %add_convert_fusion.6.refs_0_), channel_id=1, source_target_pairs={{0,2},{2,0},{4,6},{6,4},{1,3},{3,1},{5,7},{7,5},{8,10},{10,8},{12,... | collective-permute-start | bytes 196616 | tf_op jit(solution)/shard_map/ppermute | solution.py:31
  42.2 4.5 %collective-permute-start.11 = (bf16[32,1024]{1,0:T(8,128)(2,1)S(1)}, bf16[32,1024]{1,0:T(8,128)(2,1)S(1)}, u32[]{:S(2)}, u32[]{:S(2)}) collective-permute-start(bf16[32,1024]{1,0:T(8,128)(2,1)S(1)} %add_convert_fusion.6.refs_0_), channel_id=1, source_target_pairs={{0,4},{2,6},{4,0},{6,2},{1,5},{3,7},{5,1},{7,3},{8,12},{10,14},{12... | collective-permute-start | bytes 196616 | tf_op jit(solution)/shard_map/ppermute | solution.py:31
  42.6 5.1 %collective-permute-start.12 = (bf16[32,1024]{1,0:T(8,128)(2,1)S(1)}, bf16[32,1024]{1,0:T(8,128)(2,1)S(1)}, u32[]{:S(2)}, u32[]{:S(2)}) collective-permute-start(bf16[32,1024]{1,0:T(8,128)(2,1)S(1)} %add_convert_fusion.6.refs_0_), channel_id=1, source_target_pairs={{0,6},{2,4},{4,2},{6,0},{1,7},{3,5},{5,3},{7,1},{8,14},{10,12},{12... | collective-permute-start | bytes 196616 | tf_op jit(solution)/shard_map/ppermute | solution.py:31
  44.6 11.1 %copy-start.1 = (bf16[1,2048,1024]{2,1,0:T(8,128)(2,1)S(1)}, bf16[1,2048,1024]{2,1,0:T(8,128)(2,1)}, u32[]{:S(2)}) copy-start(bf16[1,2048,1024]{2,1,0:T(8,128)(2,1)} %param.12) | copy-start | bytes 12582916
  49.1 6.9 %collective-permute-start.13 = (bf16[128,2048]{1,0:T(8,128)(2,1)S(1)}, bf16[128,2048]{1,0:T(8,128)(2,1)S(1)}, u32[]{:S(2)}, u32[]{:S(2)}) collective-permute-start(bf16[128,2048]{1,0:T(8,128)(2,1)S(1)} %get-tuple-element.126.mine.pre_mine), channel_id=1, source_target_pairs={{0,1},{1,0},{2,3},{3,2},{4,5},{5,4},{6,7},{7,6},{8,9},{9,8},{10,11... | collective-permute-start | bytes 1572872 | tf_op jit(solution)/shard_map/ppermute | solution.py:22
  54.0 5.5 %collective-permute-start.14 = (bf16[32,1024]{1,0:T(8,128)(2,1)S(1)}, bf16[32,1024]{1,0:T(8,128)(2,1)S(1)}, u32[]{:S(2)}, u32[]{:S(2)}) collective-permute-start(bf16[32,1024]{1,0:T(8,128)(2,1)S(1)} %slice_bitcast_fusion.refs_0_), channel_id=1, source_target_pairs={{0,6},{2,4},{4,2},{6,0},{1,7},{3,5},{5,3},{7,1},{8,14},{10,12},{12... | collective-permute-start | bytes 196616 | tf_op jit(solution)/shard_map/ppermute | solution.py:31
  56.8 18.3 %copy-start.9 = (bf16[128,2048]{1,0:T(8,128)(2,1)}, bf16[128,2048]{1,0:T(8,128)(2,1)S(1)}, u32[]{:S(2)}) copy-start(bf16[128,2048]{1,0:T(8,128)(2,1)S(1)} %get-tuple-element.196.refs_1_) | copy-start | bytes 1572868
  59.5 3.6 %collective-permute-start.15 = (bf16[32,1024]{1,0:T(8,128)(2,1)S(1)}, bf16[32,1024]{1,0:T(8,128)(2,1)S(1)}, u32[]{:S(2)}, u32[]{:S(2)}) collective-permute-start(bf16[32,1024]{1,0:T(8,128)(2,1)S(1)} %get-tuple-element.134), channel_id=1, source_target_pairs={{0,2},{2,0},{4,6},{6,4},{1,3},{3,1},{5,7},{7,5},{8,10},{10,8},{12,... | collective-permute-start | bytes 196616 | tf_op jit(solution)/shard_map/ppermute | solution.py:31
  59.5 4.1 %collective-permute-start.16 = (bf16[32,1024]{1,0:T(8,128)(2,1)S(1)}, bf16[32,1024]{1,0:T(8,128)(2,1)S(1)}, u32[]{:S(2)}, u32[]{:S(2)}) collective-permute-start(bf16[32,1024]{1,0:T(8,128)(2,1)S(1)} %get-tuple-element.135), channel_id=1, source_target_pairs={{0,4},{2,6},{4,0},{6,2},{1,5},{3,7},{5,1},{7,3},{8,12},{10,14},{12... | collective-permute-start | bytes 196616 | tf_op jit(solution)/shard_map/ppermute | solution.py:31
  61.5 5.6 %collective-permute-start.17 = (bf16[32,1024]{1,0:T(8,128)(2,1)S(1)}, bf16[32,1024]{1,0:T(8,128)(2,1)S(1)}, u32[]{:S(2)}, u32[]{:S(2)}) collective-permute-start(bf16[32,1024]{1,0:T(8,128)(2,1)S(1)} %get-tuple-element.136), channel_id=1, source_target_pairs={{0,6},{2,4},{4,2},{6,0},{1,7},{3,5},{5,3},{7,1},{8,14},{10,12},{12... | collective-permute-start | bytes 196616 | tf_op jit(solution)/shard_map/ppermute | solution.py:31
  67.7 5.3 %collective-permute-start.18 = (bf16[32,1024]{1,0:T(8,128)(2,1)S(1)}, bf16[32,1024]{1,0:T(8,128)(2,1)S(1)}, u32[]{:S(2)}, u32[]{:S(2)}) collective-permute-start(bf16[32,1024]{1,0:T(8,128)(2,1)S(1)} %get-tuple-element.201), channel_id=1, source_target_pairs={{0,8},{8,16},{16,24},{1,9},{9,17},{17,25},{2,10},{10,18},{18,26},{... | collective-permute-start | bytes 196616 | tf_op jit(solution)/shard_map/ppermute | solution.py:17
  73.1 10.1 %collective-permute-start.19 = (bf16[32,1024]{1,0:T(8,128)(2,1)S(1)}, bf16[32,1024]{1,0:T(8,128)(2,1)S(1)}, u32[]{:S(2)}, u32[]{:S(2)}) collective-permute-start(bf16[32,1024]{1,0:T(8,128)(2,1)S(1)} %add_convert_fusion.4.refs_0_), channel_id=1, source_target_pairs={{0,2},{2,0},{4,6},{6,4},{1,3},{3,1},{5,7},{7,5},{8,10},{10,8},{12,... | collective-permute-start | bytes 196616 | tf_op jit(solution)/shard_map/ppermute | solution.py:31
  73.2 10.0 %collective-permute-start.20 = (bf16[32,1024]{1,0:T(8,128)(2,1)S(1)}, bf16[32,1024]{1,0:T(8,128)(2,1)S(1)}, u32[]{:S(2)}, u32[]{:S(2)}) collective-permute-start(bf16[32,1024]{1,0:T(8,128)(2,1)S(1)} %add_convert_fusion.4.refs_0_), channel_id=1, source_target_pairs={{0,4},{2,6},{4,0},{6,2},{1,5},{3,7},{5,1},{7,3},{8,12},{10,14},{12... | collective-permute-start | bytes 196616 | tf_op jit(solution)/shard_map/ppermute | solution.py:31
  75.1 8.1 %collective-permute-start.21 = (bf16[32,1024]{1,0:T(8,128)(2,1)S(1)}, bf16[32,1024]{1,0:T(8,128)(2,1)S(1)}, u32[]{:S(2)}, u32[]{:S(2)}) collective-permute-start(bf16[32,1024]{1,0:T(8,128)(2,1)S(1)} %add_convert_fusion.4.refs_0_), channel_id=1, source_target_pairs={{0,6},{2,4},{4,2},{6,0},{1,7},{3,5},{5,3},{7,1},{8,14},{10,12},{12... | collective-permute-start | bytes 196616 | tf_op jit(solution)/shard_map/ppermute | solution.py:31
  79.5 6.6 %collective-permute-start.23 = (bf16[128,2048]{1,0:T(8,128)(2,1)S(1)}, bf16[128,2048]{1,0:T(8,128)(2,1)S(1)}, u32[]{:S(2)}, u32[]{:S(2)}) collective-permute-start(bf16[128,2048]{1,0:T(8,128)(2,1)S(1)} %get-tuple-element.139.mine), channel_id=1, source_target_pairs={{0,1},{1,0},{2,3},{3,2},{4,5},{5,4},{6,7},{7,6},{8,9},{9,8},{10,11... | collective-permute-start | bytes 1572872 | tf_op jit(solution)/shard_map/ppermute | solution.py:22
  84.6 2.8 %collective-permute-start.22 = (bf16[128,2048]{1,0:T(8,128)(2,1)S(1)}, bf16[128,2048]{1,0:T(8,128)(2,1)S(1)}, u32[]{:S(2)}, u32[]{:S(2)}) collective-permute-start(bf16[128,2048]{1,0:T(8,128)(2,1)S(1)} %get-tuple-element.151.pre_mine.mine), channel_id=1, source_target_pairs={{0,1},{1,0},{2,3},{3,2},{4,5},{5,4},{6,7},{7,6},{8,9},{9,8},{10,11... | collective-permute-start | bytes 1572872 | tf_op jit(solution)/shard_map/ppermute | solution.py:22
  89.7 3.6 %collective-permute-start.24 = (bf16[32,1024]{1,0:T(8,128)(2,1)S(1)}, bf16[32,1024]{1,0:T(8,128)(2,1)S(1)}, u32[]{:S(2)}, u32[]{:S(2)}) collective-permute-start(bf16[32,1024]{1,0:T(8,128)(2,1)S(1)} %get-tuple-element.148), channel_id=1, source_target_pairs={{0,2},{2,0},{4,6},{6,4},{1,3},{3,1},{5,7},{7,5},{8,10},{10,8},{12,... | collective-permute-start | bytes 196616 | tf_op jit(solution)/shard_map/ppermute | solution.py:31
  89.7 4.1 %collective-permute-start.25 = (bf16[32,1024]{1,0:T(8,128)(2,1)S(1)}, bf16[32,1024]{1,0:T(8,128)(2,1)S(1)}, u32[]{:S(2)}, u32[]{:S(2)}) collective-permute-start(bf16[32,1024]{1,0:T(8,128)(2,1)S(1)} %get-tuple-element.149), channel_id=1, source_target_pairs={{0,4},{2,6},{4,0},{6,2},{1,5},{3,7},{5,1},{7,3},{8,12},{10,14},{12... | collective-permute-start | bytes 196616 | tf_op jit(solution)/shard_map/ppermute | solution.py:31
  91.7 5.0 %collective-permute-start.26 = (bf16[32,1024]{1,0:T(8,128)(2,1)S(1)}, bf16[32,1024]{1,0:T(8,128)(2,1)S(1)}, u32[]{:S(2)}, u32[]{:S(2)}) collective-permute-start(bf16[32,1024]{1,0:T(8,128)(2,1)S(1)} %get-tuple-element.150), channel_id=1, source_target_pairs={{0,6},{2,4},{4,2},{6,0},{1,7},{3,5},{5,3},{7,1},{8,14},{10,12},{12... | collective-permute-start | bytes 196616 | tf_op jit(solution)/shard_map/ppermute | solution.py:31
  98.3 6.8 %collective-permute-start.27 = (bf16[32,1024]{1,0:T(8,128)(2,1)}, bf16[32,1024]{1,0:T(8,128)(2,1)}, u32[]{:S(2)}, u32[]{:S(2)}) collective-permute-start(bf16[32,1024]{1,0:T(8,128)(2,1)} %add_convert_fusion.3), channel_id=1, source_target_pairs={{8,0},{16,8},{24,16},{9,1},{17,9},{25,17},{10,2},{18,10},{26,18},{... | collective-permute-start | bytes 196616 | tf_op jit(solution)/shard_map/ppermute | solution.py:17
  102.7 2.4 %copy-start.19 = (bf16[1,3,32,1024]{3,2,1,0:T(8,128)(2,1)S(1)}, bf16[1,3,32,1024]{3,2,1,0:T(8,128)(2,1)}, u32[]{:S(2)}) copy-start(bf16[1,3,32,1024]{3,2,1,0:T(8,128)(2,1)} %param.13) | copy-start | bytes 589828
  102.7 6.9 %copy-start.3 = (bf16[1,2048,1024]{2,1,0:T(8,128)(2,1)S(1)}, bf16[1,2048,1024]{2,1,0:T(8,128)(2,1)}, u32[]{:S(2)}) copy-start(bf16[1,2048,1024]{2,1,0:T(8,128)(2,1)} %param.12) | copy-start | bytes 12582916
  105.9 3.9 %collective-permute-start.28 = (bf16[32,1024]{1,0:T(8,128)(2,1)S(1)}, bf16[32,1024]{1,0:T(8,128)(2,1)S(1)}, u32[]{:S(2)}, u32[]{:S(2)}) collective-permute-start(bf16[32,1024]{1,0:T(8,128)(2,1)S(1)} %bitcast_select_fusion.refs_0_), channel_id=1, source_target_pairs={{0,2},{2,0},{4,6},{6,4},{1,3},{3,1},{5,7},{7,5},{8,10},{10,8},{12,... | collective-permute-start | bytes 196616 | tf_op jit(solution)/shard_map/ppermute | solution.py:31
  106.9 4.7 %collective-permute-start.29 = (bf16[32,1024]{1,0:T(8,128)(2,1)S(1)}, bf16[32,1024]{1,0:T(8,128)(2,1)S(1)}, u32[]{:S(2)}, u32[]{:S(2)}) collective-permute-start(bf16[32,1024]{1,0:T(8,128)(2,1)S(1)} %bitcast_select_fusion.refs_0_), channel_id=1, source_target_pairs={{0,4},{2,6},{4,0},{6,2},{1,5},{3,7},{5,1},{7,3},{8,12},{10,14},{12... | collective-permute-start | bytes 196616 | tf_op jit(solution)/shard_map/ppermute | solution.py:31
  108.0 5.1 %collective-permute-start.30 = (bf16[32,1024]{1,0:T(8,128)(2,1)S(1)}, bf16[32,1024]{1,0:T(8,128)(2,1)S(1)}, u32[]{:S(2)}, u32[]{:S(2)}) collective-permute-start(bf16[32,1024]{1,0:T(8,128)(2,1)S(1)} %bitcast_select_fusion.refs_0_), channel_id=1, source_target_pairs={{0,6},{2,4},{4,2},{6,0},{1,7},{3,5},{5,3},{7,1},{8,14},{10,12},{12... | collective-permute-start | bytes 196616 | tf_op jit(solution)/shard_map/ppermute | solution.py:31
  109.9 9.2 %copy-start.6 = (bf16[1,1024,2048]{2,1,0:T(8,128)(2,1)S(1)}, bf16[1,1024,2048]{2,1,0:T(8,128)(2,1)}, u32[]{:S(2)}) copy-start(bf16[1,1024,2048]{2,1,0:T(8,128)(2,1)} %param.11) | copy-start | bytes 12582916
  114.6 5.9 %collective-permute-start.31 = (bf16[128,2048]{1,0:T(8,128)(2,1)S(1)}, bf16[128,2048]{1,0:T(8,128)(2,1)S(1)}, u32[]{:S(2)}, u32[]{:S(2)}) collective-permute-start(bf16[128,2048]{1,0:T(8,128)(2,1)S(1)} %get-tuple-element.160.mine), channel_id=1, source_target_pairs={{0,1},{1,0},{2,3},{3,2},{4,5},{5,4},{6,7},{7,6},{8,9},{9,8},{10,11... | collective-permute-start | bytes 1572872 | tf_op jit(solution)/shard_map/ppermute | solution.py:22
  119.0 5.7 %collective-permute-start.32 = (bf16[32,1024]{1,0:T(8,128)(2,1)S(1)}, bf16[32,1024]{1,0:T(8,128)(2,1)S(1)}, u32[]{:S(2)}, u32[]{:S(2)}) collective-permute-start(bf16[32,1024]{1,0:T(8,128)(2,1)S(1)} %get-tuple-element.166), channel_id=1, source_target_pairs={{0,4},{2,6},{4,0},{6,2},{1,5},{3,7},{5,1},{7,3},{8,12},{10,14},{12... | collective-permute-start | bytes 196616 | tf_op jit(solution)/shard_map/ppermute | solution.py:31
  124.7 3.6 %collective-permute-start.33 = (bf16[32,1024]{1,0:T(8,128)(2,1)S(1)}, bf16[32,1024]{1,0:T(8,128)(2,1)S(1)}, u32[]{:S(2)}, u32[]{:S(2)}) collective-permute-start(bf16[32,1024]{1,0:T(8,128)(2,1)S(1)} %get-tuple-element.168), channel_id=1, source_target_pairs={{0,2},{2,0},{4,6},{6,4},{1,3},{3,1},{5,7},{7,5},{8,10},{10,8},{12,... | collective-permute-start | bytes 196616 | tf_op jit(solution)/shard_map/ppermute | solution.py:31
  124.7 4.1 %collective-permute-start.34 = (bf16[32,1024]{1,0:T(8,128)(2,1)S(1)}, bf16[32,1024]{1,0:T(8,128)(2,1)S(1)}, u32[]{:S(2)}, u32[]{:S(2)}) collective-permute-start(bf16[32,1024]{1,0:T(8,128)(2,1)S(1)} %get-tuple-element.169), channel_id=1, source_target_pairs={{0,4},{2,6},{4,0},{6,2},{1,5},{3,7},{5,1},{7,3},{8,12},{10,14},{12... | collective-permute-start | bytes 196616 | tf_op jit(solution)/shard_map/ppermute | solution.py:31
  126.6 5.2 %collective-permute-start.35 = (bf16[32,1024]{1,0:T(8,128)(2,1)S(1)}, bf16[32,1024]{1,0:T(8,128)(2,1)S(1)}, u32[]{:S(2)}, u32[]{:S(2)}) collective-permute-start(bf16[32,1024]{1,0:T(8,128)(2,1)S(1)} %get-tuple-element.170), channel_id=1, source_target_pairs={{0,6},{2,4},{4,2},{6,0},{1,7},{3,5},{5,3},{7,1},{8,14},{10,12},{12... | collective-permute-start | bytes 196616 | tf_op jit(solution)/shard_map/ppermute | solution.py:31
  131.9 5.9 %collective-permute-start.36 = (bf16[32,1024]{1,0:T(8,128)(2,1)S(1)}, bf16[32,1024]{1,0:T(8,128)(2,1)S(1)}, u32[]{:S(2)}, u32[]{:S(2)}) collective-permute-start(bf16[32,1024]{1,0:T(8,128)(2,1)S(1)} %add_convert_fusion.2), channel_id=1, source_target_pairs={{8,0},{16,8},{24,16},{9,1},{17,9},{25,17},{10,2},{18,10},{26,18},{... | collective-permute-start | bytes 196616 | tf_op jit(solution)/shard_map/ppermute | solution.py:17
  137.8 3.9 %collective-permute-start.37 = (bf16[32,1024]{1,0:T(8,128)(2,1)S(1)}, bf16[32,1024]{1,0:T(8,128)(2,1)S(1)}, u32[]{:S(2)}, u32[]{:S(2)}) collective-permute-start(bf16[32,1024]{1,0:T(8,128)(2,1)S(1)} %bitcast_select_fusion.1.refs_0_), channel_id=1, source_target_pairs={{0,2},{2,0},{4,6},{6,4},{1,3},{3,1},{5,7},{7,5},{8,10},{10,8},{12,... | collective-permute-start | bytes 196616 | tf_op jit(solution)/shard_map/ppermute | solution.py:31
  138.4 4.0 %collective-permute-start.38 = (bf16[32,1024]{1,0:T(8,128)(2,1)S(1)}, bf16[32,1024]{1,0:T(8,128)(2,1)S(1)}, u32[]{:S(2)}, u32[]{:S(2)}) collective-permute-start(bf16[32,1024]{1,0:T(8,128)(2,1)S(1)} %bitcast_select_fusion.1.refs_0_), channel_id=1, source_target_pairs={{0,4},{2,6},{4,0},{6,2},{1,5},{3,7},{5,1},{7,3},{8,12},{10,14},{12... | collective-permute-start | bytes 196616 | tf_op jit(solution)/shard_map/ppermute | solution.py:31
  139.7 5.0 %collective-permute-start.39 = (bf16[32,1024]{1,0:T(8,128)(2,1)S(1)}, bf16[32,1024]{1,0:T(8,128)(2,1)S(1)}, u32[]{:S(2)}, u32[]{:S(2)}) collective-permute-start(bf16[32,1024]{1,0:T(8,128)(2,1)S(1)} %bitcast_select_fusion.1.refs_0_), channel_id=1, source_target_pairs={{0,6},{2,4},{4,2},{6,0},{1,7},{3,5},{5,3},{7,1},{8,14},{10,12},{12... | collective-permute-start | bytes 196616 | tf_op jit(solution)/shard_map/ppermute | solution.py:31
  141.7 11.0 %copy-start.21 = (bf16[1,32,1024]{2,1,0:T(8,128)(2,1)S(1)}, bf16[1,32,1024]{2,1,0:T(8,128)(2,1)}, u32[]{:S(2)}) copy-start(bf16[1,32,1024]{2,1,0:T(8,128)(2,1)} %get-tuple-element.209) | copy-start | bytes 196612
  146.3 7.5 %collective-permute-start.40 = (bf16[128,2048]{1,0:T(8,128)(2,1)S(1)}, bf16[128,2048]{1,0:T(8,128)(2,1)S(1)}, u32[]{:S(2)}, u32[]{:S(2)}) collective-permute-start(bf16[128,2048]{1,0:T(8,128)(2,1)S(1)} %get-tuple-element.172.mine), channel_id=1, source_target_pairs={{0,1},{1,0},{2,3},{3,2},{4,5},{5,4},{6,7},{7,6},{8,9},{9,8},{10,11... | collective-permute-start | bytes 1572872 | tf_op jit(solution)/shard_map/ppermute | solution.py:22
  151.1 5.5 %collective-permute-start.41 = (bf16[32,1024]{1,0:T(8,128)(2,1)S(1)}, bf16[32,1024]{1,0:T(8,128)(2,1)S(1)}, u32[]{:S(2)}, u32[]{:S(2)}) collective-permute-start(bf16[32,1024]{1,0:T(8,128)(2,1)S(1)} %get-tuple-element.178), channel_id=1, source_target_pairs={{0,6},{2,4},{4,2},{6,0},{1,7},{3,5},{5,3},{7,1},{8,14},{10,12},{12... | collective-permute-start | bytes 196616 | tf_op jit(solution)/shard_map/ppermute | solution.py:31
  153.7 6.4 %copy-start.8 = (bf16[128,2048]{1,0:T(8,128)(2,1)S(1)}, bf16[128,2048]{1,0:T(8,128)(2,1)}, u32[]{:S(2)}) copy-start(bf16[128,2048]{1,0:T(8,128)(2,1)} %copy-done.7) | copy-start | bytes 1572868
  153.7 6.4 %copy-start.10 = (bf16[128,2048]{1,0:T(8,128)(2,1)S(1)}, bf16[128,2048]{1,0:T(8,128)(2,1)}, u32[]{:S(2)}) copy-start(bf16[128,2048]{1,0:T(8,128)(2,1)} %copy-done.9) | copy-start | bytes 1572868
  153.7 6.4 %copy-start.16 = (bf16[128,1024]{1,0:T(8,128)(2,1)S(1)}, bf16[128,1024]{1,0:T(8,128)(2,1)}, u32[]{:S(2)}) copy-start(bf16[128,1024]{1,0:T(8,128)(2,1)} %copy-done.15) | copy-start | bytes 786436
  155.3 10.5 %copy-start.12 = (bf16[128,2048]{1,0:T(8,128)(2,1)S(1)}, bf16[128,2048]{1,0:T(8,128)(2,1)}, u32[]{:S(2)}) copy-start(bf16[128,2048]{1,0:T(8,128)(2,1)} %copy-done.11) | copy-start | bytes 1572868
  155.3 10.5 %copy-start.14 = (bf16[128,1024]{1,0:T(8,128)(2,1)S(1)}, bf16[128,1024]{1,0:T(8,128)(2,1)}, u32[]{:S(2)}) copy-start(bf16[128,1024]{1,0:T(8,128)(2,1)} %copy-done.13) | copy-start | bytes 786436
  155.3 10.5 %copy-start.18 = (bf16[128,1024]{1,0:T(8,128)(2,1)S(1)}, bf16[128,1024]{1,0:T(8,128)(2,1)}, u32[]{:S(2)}) copy-start(bf16[128,1024]{1,0:T(8,128)(2,1)} %copy-done.17) | copy-start | bytes 786436
  156.6 13.5 %collective-permute-start.43 = (bf16[32,1024]{1,0:T(8,128)(2,1)S(1)}, bf16[32,1024]{1,0:T(8,128)(2,1)S(1)}, u32[]{:S(2)}, u32[]{:S(2)}) collective-permute-start(bf16[32,1024]{1,0:T(8,128)(2,1)S(1)} %get-tuple-element.180), channel_id=1, source_target_pairs={{0,2},{2,0},{4,6},{6,4},{1,3},{3,1},{5,7},{7,5},{8,10},{10,8},{12,... | collective-permute-start | bytes 196616 | tf_op jit(solution)/shard_map/ppermute | solution.py:31
  156.6 13.5 %collective-permute-start.44 = (bf16[32,1024]{1,0:T(8,128)(2,1)S(1)}, bf16[32,1024]{1,0:T(8,128)(2,1)S(1)}, u32[]{:S(2)}, u32[]{:S(2)}) collective-permute-start(bf16[32,1024]{1,0:T(8,128)(2,1)S(1)} %get-tuple-element.181), channel_id=1, source_target_pairs={{0,4},{2,6},{4,0},{6,2},{1,5},{3,7},{5,1},{7,3},{8,12},{10,14},{12... | collective-permute-start | bytes 196616 | tf_op jit(solution)/shard_map/ppermute | solution.py:31
  158.5 11.7 %collective-permute-start.45 = (bf16[32,1024]{1,0:T(8,128)(2,1)S(1)}, bf16[32,1024]{1,0:T(8,128)(2,1)S(1)}, u32[]{:S(2)}, u32[]{:S(2)}) collective-permute-start(bf16[32,1024]{1,0:T(8,128)(2,1)S(1)} %get-tuple-element.182), channel_id=1, source_target_pairs={{0,6},{2,4},{4,2},{6,0},{1,7},{3,5},{5,3},{7,1},{8,14},{10,12},{12... | collective-permute-start | bytes 196616 | tf_op jit(solution)/shard_map/ppermute | solution.py:31
  160.2 11.6 %collective-permute-start.42 = (bf16[32,1024]{1,0:T(8,128)(2,1)S(1)}, bf16[32,1024]{1,0:T(8,128)(2,1)S(1)}, u32[]{:S(2)}, u32[]{:S(2)}) collective-permute-start(bf16[32,1024]{1,0:T(8,128)(2,1)S(1)} %get-tuple-element.183), channel_id=1, source_target_pairs={{0,2},{2,0},{4,6},{6,4},{1,3},{3,1},{5,7},{7,5},{8,10},{10,8},{12,... | collective-permute-start | bytes 196616 | tf_op jit(solution)/shard_map/ppermute | solution.py:31
  165.8 6.0 %copy-start.22 = (bf16[32,1024]{1,0:T(8,128)(2,1)S(1)}, bf16[32,1024]{1,0:T(8,128)(2,1)}, u32[]{:S(2)}) copy-start(bf16[32,1024]{1,0:T(8,128)(2,1)} %get-tuple-element.204) | copy-start | bytes 196612
  165.8 6.0 %copy-start.23 = (bf16[32,1024]{1,0:T(8,128)(2,1)S(1)}, bf16[32,1024]{1,0:T(8,128)(2,1)}, u32[]{:S(2)}) copy-start(bf16[32,1024]{1,0:T(8,128)(2,1)} %get-tuple-element.202) | copy-start | bytes 196612
  (7 other events, 9.5 us)

commit v7 on v6

v7 whole, which is shorter than its diff:
```python
import jax
import jax.numpy as jnp
from jax import lax
from jax.experimental import pallas as pl
from jax.experimental.pallas import tpu as pltpu
from jax.sharding import PartitionSpec as P

BF = jnp.bfloat16
F32 = jnp.float32
LAST = (((1,), (1,)), ((), ()))
FIRST = (((0,), (0,)), ((), ()))


def from_behind(block, axis, distance):
    devices = range(lax.axis_size(axis))
    route = [(i - distance, i) for i in devices if i - distance in devices]
    return lax.ppermute(block, axis, route)


def turn(block, axis, distance):
    size = lax.axis_size(axis)
    return lax.ppermute(block, axis, [(i, (i + distance) % size) for i in range(size)])


def partner(row, j, size):
    return row ^ j if size & (size - 1) == 0 else (j - row) % size


def swap_rows(block, j):
    size = lax.axis_size("row")
    return lax.ppermute(block, "row", [(i, partner(i, j, size)) for i in range(size)])


def gather_rows(block):
    return [swap_rows(block, j) if j else block for j in range(lax.axis_size("row"))]


def scatter_rows(pieces):
    return [swap_rows(piece, j) if j else piece for j, piece in enumerate(pieces)]


def beside(turn):
    size = lax.axis_size("row")
    return [[1], [2], range(3, size)][turn] if size > 2 else [[], [], [1]][turn]


def after(block, other):
    return lax.optimization_barrier((block, other))[0]


def vmem(count):
    return [pl.BlockSpec(memory_space=pltpu.VMEM)] * count


def run(kernel, outs, *ins, flops=0, scratch=()):
    ins = [pltpu.with_memory_space_constraint(block, pltpu.VMEM) for block in ins]
    size = sum(x.size * x.dtype.itemsize for x in [*ins, *outs])
    return pl.pallas_call(
        kernel,
        in_specs=vmem(len(ins)),
        out_specs=vmem(len(outs)),
        out_shape=[pltpu.VMEM(x.shape, x.dtype) for x in outs],
        scratch_shapes=scratch,
        compiler_params=pltpu.CompilerParams(vmem_limit_bytes=6 << 20),
        cost_estimate=pl.CostEstimate(flops=flops, bytes_accessed=size, transcendentals=0),
        name=kernel.__name__,
    )(*ins)


def first_kernel(inputs, cotangent, first, last, sems):
    copies = [
        pltpu.make_async_copy(inputs.at[0, 0], first, sems.at[0]),
        pltpu.make_async_copy(cotangent.at[0, cotangent.shape[1] - 1], last, sems.at[1]),
    ]
    for copy in copies:
        copy.start()
    for copy in copies:
        copy.wait()


def fetch_kernel(sample_ids, inputs, send_base, recv_base, cotangent, *refs):
    ticks = inputs.shape[1]
    count = ticks - 1
    stored, bases, cots = refs[:count], refs[count : 2 * count], refs[2 * count : 3 * count]
    fresh, sems = refs[3 * count :]
    section, sections = lax.axis_index("section"), lax.axis_size("section")
    samples = [sample_ids[tick - section + sections - 1] for tick in range(ticks)]
    copies = []
    for t in range(count):
        copies += [
            pltpu.make_async_copy(send_base.at[0, samples[t]], stored[t], sems.at[4 * t]),
            pltpu.make_async_copy(recv_base.at[0, samples[t + 1]], bases[t], sems.at[4 * t + 1]),
            pltpu.make_async_copy(inputs.at[0, t + 1], fresh.at[t], sems.at[4 * t + 2]),
            pltpu.make_async_copy(cotangent.at[0, t], cots[t], sems.at[4 * t + 3]),
        ]
    for copy in copies:
        copy.start()
    for copy in copies:
        copy.wait()
    for t in range(count):
        bases[t][...] = jnp.where(section == 0, fresh[t], bases[t][...])
        cots[t][...] = jnp.where(section == sections - 1, cots[t][...], jnp.zeros_like(cots[t]))


def fetch(sample_ids, inputs, send_base, recv_base, cotangent):
    count = inputs.shape[1] - 1
    piece = inputs.shape[2:]
    outs = pl.pallas_call(
        fetch_kernel,
        in_specs=[pl.BlockSpec(memory_space=pltpu.SMEM)] + [pl.BlockSpec(memory_space=pltpu.HBM)] * 4,
        out_specs=vmem(3 * count),
        out_shape=[pltpu.VMEM(piece, BF)] * (3 * count),
        scratch_shapes=[pltpu.VMEM((count, *piece), BF), pltpu.SemaphoreType.DMA((4 * count,))],
        compiler_params=pltpu.CompilerParams(vmem_limit_bytes=4 << 20),
        cost_estimate=pl.CostEstimate(flops=0, bytes_accessed=2 << 20, transcendentals=0),
        name="fetch",
    )(sample_ids, *[pltpu.with_memory_space_constraint(x, pltpu.HBM) for x in (inputs, send_base, recv_base, cotangent)])
    return outs[:count], outs[count : 2 * count], outs[2 * count :]


def first_pieces(inputs, cotangent):
    piece = inputs.shape[2:]
    return pl.pallas_call(
        first_kernel,
        in_specs=[pl.BlockSpec(memory_space=pltpu.HBM)] * 2,
        out_specs=vmem(2),
        out_shape=[pltpu.VMEM(piece, BF)] * 2,
        scratch_shapes=[pltpu.SemaphoreType.DMA((2,))],
        compiler_params=pltpu.CompilerParams(vmem_limit_bytes=2 << 20),
        cost_estimate=pl.CostEstimate(flops=0, bytes_accessed=1 << 18, transcendentals=0),
        name="first",
    )(*[pltpu.with_memory_space_constraint(x, pltpu.HBM) for x in (inputs, cotangent)])


def added(first, terms):
    total = first[...].astype(F32)
    for term in terms:
        total = total + term[...].astype(F32)
    return total.astype(BF)


def arrive(base, arrived, out):
    out[...] = added(base, [arrived])


def leave(first, *refs):
    *terms, stored, out, delta = refs
    out[...] = added(first, terms)
    delta[...] = (out[...].astype(F32) - stored[...].astype(F32)).astype(BF)


def leave_back(first, *refs):
    *terms, out = refs
    out[...] = added(first, terms)


def finish(first_out, first_grad, *refs):
    *rest, outs, grads = refs
    count = outs.shape[1] - 1
    terms, known_outs, known_grads = rest[: -2 * count], rest[-2 * count : -count], rest[-count:]
    outs[0, count] = added(first_out, [term.at[1] for term in terms])
    grads[0, 0] = added(first_grad, [term.at[0] for term in terms])
    for t in range(count):
        outs[0, t] = known_outs[t][...]
        grads[0, t + 1] = known_grads[t][...]


def turned(*refs):
    *pieces, out = refs
    out[...] = jnp.concatenate([piece[...] for piece in pieces], axis=0).T


def hold_kernel(source, kept, sem):
    copy = pltpu.make_async_copy(source, kept, sem)
    copy.start()
    copy.wait()


def hold(weight, other):
    return pl.pallas_call(
        hold_kernel,
        in_specs=[pl.BlockSpec(memory_space=pltpu.HBM)],
        out_specs=pl.BlockSpec(memory_space=pltpu.VMEM),
        out_shape=pltpu.VMEM(weight.shape, weight.dtype),
        scratch_shapes=[pltpu.SemaphoreType.DMA],
        compiler_params=pltpu.CompilerParams(vmem_limit_bytes=2 << 20),
        cost_estimate=pl.CostEstimate(flops=0, bytes_accessed=4 * weight.size, transcendentals=0),
        name="hold",
    )(pltpu.with_memory_space_constraint(after(weight, other), pltpu.HBM))


def columns(width, step=256):
    step = min(width, step)
    return [slice(n, n + step) for n in range(0, width, step)]


def up_product(*refs):
    *pieces, weight, product, whole = refs
    whole[...] = jnp.concatenate([piece[...] for piece in pieces], axis=0)
    for n in columns(product.shape[1]):
        product[:, n] = matmul(whole[...], weight[:, n]).astype(BF)


def back_product(*refs):
    *pieces, weight, whole, product = refs
    whole[...] = jnp.concatenate([piece[...] for piece in pieces], axis=0)
    for n in columns(product.shape[1]):
        product[:, n] = matmul(whole[...], weight[n, :], LAST).astype(BF)


def put_rows(pieces, n, product):
    rows = pieces[0].shape[0]
    for j, piece in enumerate(pieces):
        piece[:, n] = product[j * rows : (j + 1) * rows].astype(BF)


def down_product(mine, other, weight, act, *pieces):
    for n in columns(act.shape[1]):
        pre = mine[:, n].astype(F32) + other[:, n].astype(F32)
        act[:, n] = jax.nn.silu(pre).astype(BF)
    for n in columns(weight.shape[1]):
        put_rows(pieces, n, matmul(act[...], weight[:, n]))


def down_again(act, weight, *pieces):
    for n in columns(weight.shape[1]):
        put_rows(pieces, n, matmul(act[...], weight[:, n]))


def in_product(mine, other, pre_mine, pre_other, weight, grad_pre, *pieces):
    for n in columns(grad_pre.shape[1]):
        pre = pre_mine[:, n].astype(F32) + pre_other[:, n].astype(F32)
        grad = mine[:, n].astype(F32) + other[:, n].astype(F32)
        grad_pre[:, n] = (grad * silu_slope(pre)).astype(BF)
    for n in columns(weight.shape[0]):
        put_rows(pieces, n, matmul(grad_pre[...], weight[n, :], LAST))


def in_product_last(*refs):
    *ins, grad_pre = refs[: 6 + (len(refs) - 6) // 2]
    pairs = refs[len(ins) + 1 :]
    for piece, pair in zip(ins[5:], pairs):
        pair[1] = piece[...]
    in_product(*ins[:5], grad_pre, *[pair.at[0] for pair in pairs])


def act_only(mine, other, act):
    for n in columns(act.shape[1]):
        pre = mine[:, n].astype(F32) + other[:, n].astype(F32)
        act[:, n] = jax.nn.silu(pre).astype(BF)


def weight_grad(*refs):
    count = len(refs) // 2
    left = jnp.concatenate([ref[...] for ref in refs[:count]], axis=1)
    for n in columns(refs[-1].shape[1], 512):
        right = jnp.concatenate([ref[:, n] for ref in refs[count:-1]], axis=0)
        refs[-1][:, n] = matmul(left, right).astype(BF)


def weight_product(lefts, rights, step=256):
    rows, width, depth = lefts[0].shape[0], rights[0].shape[1], rights[0].shape[0]
    step = min(rows, step)
    return pl.pallas_call(
        weight_grad,
        grid=(rows // step,),
        in_specs=[pl.BlockSpec((step, depth), lambda i: (i, 0))] * len(lefts)
        + [pl.BlockSpec((depth, width), lambda i: (0, 0))] * len(rights),
        out_specs=pl.BlockSpec((step, width), lambda i: (i, 0)),
        out_shape=jax.ShapeDtypeStruct((rows, width), BF),
        compiler_params=pltpu.CompilerParams(vmem_limit_bytes=16 << 20),
        cost_estimate=pl.CostEstimate(
            flops=2 * rows * width * depth * len(lefts), bytes_accessed=2 * rows * width, transcendentals=0
        ),
        name="weight_grad",
    )(*lefts, *rights)


def other_cols(partial):
    size = lax.axis_size("col")
    if size == 2:
        return turn(partial, "col", 1)
    return (lax.psum(partial.astype(F32), "col") - partial.astype(F32)).astype(BF)


def silu_slope(value):
    sig = jax.nn.sigmoid(value)
    return sig * (1.0 + value * (1.0 - sig))


def matmul(a, b, dims=(((1,), (0,)), ((), ()))):
    return lax.dot_general(a, b, dims, preferred_element_type=F32)


def per_device(inputs, sample_ids, send_base, recv_base, w_up, w_down, cotangent):
    ticks = inputs.shape[1]
    up_block, down_block = w_up[0], w_down[0]
    rows = lax.axis_size("row")
    piece_rows, width = inputs.shape[2:]
    tokens, hidden = rows * piece_rows, up_block.shape[1]
    flops = 2 * tokens * width * hidden
    piece_like = jax.ShapeDtypeStruct((piece_rows, width), BF)
    pair_like = jax.ShapeDtypeStruct((2, piece_rows, width), BF)
    whole_like = jax.ShapeDtypeStruct((tokens, width), BF)
    hidden_like = jax.ShapeDtypeStruct((tokens, hidden), BF)
    turned_like = jax.ShapeDtypeStruct((width, tokens), BF)
    turned_hidden = jax.ShapeDtypeStruct((hidden, tokens), BF)
    room = [pltpu.VMEM((tokens, width), BF)]

    act_in, last_cot = first_pieces(inputs, cotangent)
    cot_pieces = [last_cot] + [None] * (rows - 1)
    in_pieces, acts, pres, seen_in, seen_out = [], [], [], [], []
    turned_ins, turned_acts = [], []
    for tick in range(ticks):
        if tick:
            (act_in,) = run(arrive, [piece_like], bases[tick - 1], from_behind(sending, "section", 1))
        pieces = gather_rows(act_in)
        if tick == 0:
            for j in beside(0):
                cot_pieces[j] = swap_rows(after(cot_pieces[0], act_in), j)
            stored, bases, cots = fetch(after(sample_ids, act_in), inputs, send_base, recv_base, cotangent)
            pieces = after(pieces, ([cot_pieces[j] for j in beside(0)], stored))
        if tick == ticks - 1:
            full_cot, first_grads = run(
                back_product, [whole_like, hidden_like], *cot_pieces, hold(down_block, act_in), flops=flops
            )
            pieces = after(pieces, first_grads)
        (partial,) = run(up_product, [hidden_like], *pieces, hold(up_block, act_in), flops=flops, scratch=room)
        other = other_cols(partial)
        if tick < ticks - 1:
            for j in beside(tick + 1):
                cot_pieces[j] = swap_rows(after(cot_pieces[0], partial), j)
            act, *terms = run(
                down_product, [hidden_like] + [piece_like] * rows, partial, other, hold(down_block, partial), flops=flops
            )
            terms = after(terms, [cot_pieces[j] for j in beside(tick + 1)])
            acts.append(act)
            terms_in = scatter_rows(terms)
            if tick == 1:
                turned_ins += run(turned, [turned_like], *after(in_pieces[0], terms))
                turned_acts += run(turned, [turned_hidden], after(acts[0], terms))
                terms_in[0] = after(terms_in[0], (turned_ins, turned_acts))
            act_out, sending = run(leave, [piece_like] * 2, act_in, *terms_in, stored[tick])
            seen_out.append(act_out)
        in_pieces.append(pieces)
        pres.append((partial, other))
        seen_in.append(act_in)
    full_grads = [None] * ticks
    pre_grads = [None] * ticks
    seen_grad = [None] * ticks
    for step in range(ticks):
        tick = ticks - 1 - step
        if step == 0:
            grad_out, full_grad, partial = last_cot, full_cot, first_grads
        else:
            arrived = from_behind(sending, "section", -1)
            if step == 1:
                (act,) = run(act_only, [hidden_like], *after(pres[-1], sending))
                acts.append(act)
                out_pieces = run(down_again, [piece_like] * rows, act, hold(down_block, sending), flops=flops)
                arrived = after(arrived, out_pieces)
            (grad_out,) = run(arrive, [piece_like], cots[tick], arrived)
            pieces = gather_rows(grad_out)
            full_grad, partial = run(
                back_product, [whole_like, hidden_like], *pieces, hold(down_block, grad_out), flops=flops
            )
        other = other_cols(partial)
        up_kept = hold(up_block, pres[-1][0] if step == 0 else partial)
        if step < ticks - 1:
            grad_pre, *terms = run(
                in_product,
                [hidden_like] + [piece_like] * rows,
                partial, other, *pres[tick], up_kept,
                flops=flops,
            )
            terms_in = scatter_rows(terms)
            while len(turned_ins) < min(step + 2, ticks):
                turned_ins += run(turned, [turned_like], *after(in_pieces[len(turned_ins)], terms))
                turned_acts += run(turned, [turned_hidden], after(acts[len(turned_acts)], terms))
            terms_in[0] = after(terms_in[0], (turned_ins, turned_acts))
            (sending,) = run(leave_back, [piece_like], grad_out, *terms_in)
            seen_grad[tick] = sending
        else:
            grad_pre, *terms = run(
                in_product_last,
                [hidden_like] + [pair_like] * rows,
                partial, other, *pres[tick], up_kept, *out_pieces,
                flops=flops,
            )
            terms_in = scatter_rows(terms)
        full_grads[tick] = full_grad
        pre_grads[tick] = grad_pre
    lefts = after((turned_ins, turned_acts), terms)
    grad_up = weight_product(lefts[0], pre_grads)
    grad_down = weight_product(lefts[1], full_grads)
    stack_like = jax.ShapeDtypeStruct((1, ticks, piece_rows, width), BF)
    terms_in[0] = after(terms_in[0], (grad_up, grad_down))
    section_output, input_grad = pl.pallas_call(
        finish,
        in_specs=vmem(2 + rows + 2 * (ticks - 1)),
        out_specs=vmem(2),
        out_shape=[stack_like] * 2,
        compiler_params=pltpu.CompilerParams(vmem_limit_bytes=6 << 20),
        name="finish",
    )(act_in, grad_out, *terms_in, *seen_out, *seen_grad[1:])
    return (
        jnp.stack(seen_in)[None],
        section_output,
        input_grad,
        grad_up[None],
        grad_down[None],
    )


def solution(mesh):
    placed = (
        P("section", None, "row", "col"),
        P(),
        P("section", None, "row", "col"),
        P("section", None, "row", "col"),
        P("section", "col", "row"),
        P("section", "row", "col"),
        P("section", None, "row", "col"),
    )
    return jax.shard_map(
        per_device,
        mesh=mesh,
        in_specs=placed,
        out_specs=(
            P("section", None, "row", "col"),
            P("section", None, "row", "col"),
            P("section", None, "row", "col"),
            P("section", "col", "row"),
            P("section", "row", "col"),
        ),
        check_vma=False,
    )
```

time: 175 us -> 159 us (0.909)
  Pallas kernels: 27.2 us -> 54.2 us
  waiting for transfers between devices: 43.2 us -> 27.7 us
  local copies, waits for them, and re-layouts: 12.4 us -> 0.01 us
  other arithmetic: 7.82 us -> 0.7 us
  between operations: 7.1 us -> 1.11 us
  starting transfers between devices: 74.8 us -> 72.9 us
    pallas_call x12, Pallas kernels: 3.47 us -> 26.4 us  [hold(): pl.pallas_call(hold_kernel, in_specs=[pl.BlockSpec(memory_space=pltpu.HBM...]
    ppermute x36 -> x33, waiting for transfers between devices: 32.3 us -> 19.2 us  [swap_rows(): lax.ppermute(block, 'row', [(i, partner(i, j, size)) for i in range(size)])]
    unnamed x50 -> x2, local copies, waits for them, and re-layouts: 9.52 us -> 0.01 us
    pallas_call x13 -> x30, Pallas kernels: 13.8 us -> 18.4 us  [the longest x27 15 us: run(): pl.pallas_call(kernel, in_specs=vmem(len(ins)), out_specs=vmem(len(outs))...]
    convert_element_type x6 -> x0, other arithmetic: 2.96 us -> none  [the longest x2 1.56 us: per_device(): sending = add_up(grad_out, scatter_rows(terms)).astype(BF)]
    ppermute x6, waiting for transfers between devices: 2.46 us -> 0.02 us  [turn(): lax.ppermute(block, axis, [(i, (i + distance) % size) for i in range(size)])]
    broadcast_in_dim x2 -> x0, other arithmetic: 2.24 us -> none  [the longest x1 1.54 us: per_device(): jnp.stack(seen_grad)[None]]
    select_n x3 -> x0, other arithmetic: 1.83 us -> none  [the longest x1 0.97 us: per_device(): jnp.where(section == 0, inputs[0, t], pick(recv_base[0], samples[t]))]
  transfers between devices with their start and end apart: 46 -> 43, of which waited for: 24 -> 21; matrix products, arithmetic and copies ran while one was open for 2% -> 0% of each run, Pallas kernels for 12% -> 28%
where the time goes in v7:
time: 159 us; the launch traced here: 157 us
  starting transfers between devices  72.9 us (46%)
  Pallas kernels  54.2 us (34%)
  waiting for transfers between devices  27.7 us (17%)
    ppermute x33, starting transfers between devices, swap_rows(): lax.ppermute(block, 'row', [(i, partner(i, j, size)) for i in range(size)])  42.5 us
    pallas_call x12, Pallas kernels, hold(): pl.pallas_call(hold_kernel, in_specs=[pl.BlockSpec(memory_space=pltpu.HBM...  26.4 us
    ppermute x6, starting transfers between devices, turn(): lax.ppermute(block, axis, [(i, (i + distance) % size) for i in range(size)])  19.3 us
    ppermute x33, waiting for transfers between devices, swap_rows(): lax.ppermute(block, 'row', [(i, partner(i, j, size)) for i in range(size)])  19.2 us
    pallas_call x27, Pallas kernels, run(): pl.pallas_call(kernel, in_specs=vmem(len(ins)), out_specs=vmem(len(outs))...  15 us
    ppermute x4, starting transfers between devices, from_behind(): return lax.ppermute(block, axis, route)  11.2 us
    pallas_call x2, Pallas kernels, weight_product(): pl.pallas_call(weight_grad, grid=(rows // step,), in_specs=[pl.BlockSpec(...  9.44 us
    ppermute x4, waiting for transfers between devices, from_behind(): return lax.ppermute(block, axis, route)  8.43 us
  transfers between devices with their start and end apart: 43, of which 21 were waited for; matrix products, arithmetic and copies ran while one was open for 0% of the time, Pallas kernels for 28%

profile of v7, /device:TPU:3, one launch (start us, length us, event | category | flops | bytes accessed | tf_op | source)
XLA Modules:
  0.0 156.7 jit_solution(15170590580421367657)
XLA Ops:
  0.6 0.9 first.1
  1.5 1.4 collective-permute-start.3
  3.1 2.3 %collective-permute-start.1 = (bf16[32,1024]{1,0:T(8,128)(2,1)S(1)}, bf16[32,1024]{1,0:T(8,128)(2,1)S(1)}, u32[]{:S(2)}, u32[]{:S(2)}) collective-permute-start(bf16[32,1024]{1,0:T(8,128)(2,1)S(1)} %get-tuple-element.149.refs_0_.first), channel_id=1, source_target_pairs={{0,4},{2,6},{4,0},{6,2},{1,5},{3,7},{5,1},{7,3},{8,12},{10,14},{12... | collective-permute-start | bytes 196616 | tf_op jit(solution)/shard_map/ppermute | solution.py:31
  5.4 1.1 collective-permute-start.2
  6.4 2.2 %hold.12.refs_4_ = bf16[1024,2048]{1,0:T(8,128)(2,1)S(1)} custom-call(bf16[1024,2048]{1,0:T(8,128)(2,1)} %bitcast.18), custom_call_target="tpu_custom_call" | custom-call | bytes 8388608 | tf_op jit(solution)/shard_map/hold/pallas_call | solution.py:180
  8.7 1.7 %fetch.1 = (bf16[32,1024]{1,0:T(8,128)(2,1)S(1)}, bf16[32,1024]{1,0:T(8,128)(2,1)S(1)}, bf16[32,1024]{1,0:T(8,128)(2,1)S(1)}, bf16[32,1024]{1,0:T(8,128)(2,1)S(1...) custom-call(s32[6]{0:T(128)S(1)} %copy-done, bf16[1,3,32,1024]{3,2,1,0:T(8,128)(2,1)} %inputs.3, ...), custom_call_target="tpu_custom_call" | custom-call | bytes 2097152 | tf_op jit(solution)/shard_map/fetch/pallas_call | solution.py:108
  11.9 1.9 %collective-permute-start.4 = (bf16[128,2048]{1,0:T(8,128)(2,1)S(1)}, bf16[128,2048]{1,0:T(8,128)(2,1)S(1)}, u32[]{:S(2)}, u32[]{:S(2)}) collective-permute-start(bf16[128,2048]{1,0:T(8,128)(2,1)S(1)} %up_product.3.mine.refs_2_), channel_id=1, source_target_pairs={{0,1},{1,0},{2,3},{3,2},{4,5},{5,4},{6,7},{7,6},{8,9},{9,8},{10,11... | collective-permute-start | bytes 1572872 | tf_op jit(solution)/shard_map/ppermute | solution.py:22
  13.8 2.1 %collective-permute-start.5 = (bf16[32,1024]{1,0:T(8,128)(2,1)S(1)}, bf16[32,1024]{1,0:T(8,128)(2,1)S(1)}, u32[]{:S(2)}, u32[]{:S(2)}) collective-permute-start(bf16[32,1024]{1,0:T(8,128)(2,1)S(1)} %get-tuple-element.144.refs_0_.first), channel_id=1, source_target_pairs={{0,4},{2,6},{4,0},{6,2},{1,5},{3,7},{5,1},{7,3},{8,12},{10,14},{12... | collective-permute-start | bytes 196616 | tf_op jit(solution)/shard_map/ppermute | solution.py:31
  15.9 2.2 %hold.13.weight = bf16[2048,1024]{1,0:T(8,128)(2,1)S(1)} custom-call(bf16[2048,1024]{1,0:T(8,128)(2,1)} %bitcast.12), custom_call_target="tpu_custom_call" | custom-call | bytes 8388608 | tf_op jit(solution)/shard_map/hold/pallas_call | solution.py:180
  18.8 0.9 collective-permute-done.5.refs_2_
  20.6 2.7 %collective-permute-start.8 = (bf16[32,1024]{1,0:T(8,128)(2,1)S(1)}, bf16[32,1024]{1,0:T(8,128)(2,1)S(1)}, u32[]{:S(2)}, u32[]{:S(2)}) collective-permute-start(bf16[32,1024]{1,0:T(8,128)(2,1)S(1)} %get-tuple-element.135), channel_id=1, source_target_pairs={{0,6},{2,4},{4,2},{6,0},{1,7},{3,5},{5,3},{7,1},{8,14},{10,12},{12... | collective-permute-start | bytes 196616 | tf_op jit(solution)/shard_map/ppermute | solution.py:31
  23.8 2.5 %collective-permute-done.8.refs_3_ = bf16[32,1024]{1,0:T(8,128)(2,1)S(1)} collective-permute-done((bf16[32,1024]{1,0:T(8,128)(2,1)S(1)}, bf16[32,1024]{1,0:T(8,128)(2,1)S(1)}, u32[]{:S(2)}, u32[]{:S(2)}) %collective-permute-start.8) | collective-permute-done | bytes 65568 | tf_op jit(solution)/shard_map/ppermute | solution.py:31
  26.4 3.1 %collective-permute-start.9 = (bf16[32,1024]{1,0:T(8,128)(2,1)S(1)}, bf16[32,1024]{1,0:T(8,128)(2,1)S(1)}, u32[]{:S(2)}, u32[]{:S(2)}) collective-permute-start(bf16[32,1024]{1,0:T(8,128)(2,1)S(1)} %get-tuple-element.136), channel_id=1, source_target_pairs={{0,8},{8,16},{16,24},{1,9},{9,17},{17,25},{2,10},{10,18},{18,26},{... | collective-permute-start | bytes 196616 | tf_op jit(solution)/shard_map/ppermute | solution.py:17
  29.5 1.9 %collective-permute-done.9.arrived = bf16[32,1024]{1,0:T(8,128)(2,1)S(1)} collective-permute-done((bf16[32,1024]{1,0:T(8,128)(2,1)S(1)}, bf16[32,1024]{1,0:T(8,128)(2,1)S(1)}, u32[]{:S(2)}, u32[]{:S(2)}) %collective-permute-start.9) | collective-permute-done | bytes 65568 | tf_op jit(solution)/shard_map/ppermute | solution.py:17
  31.4 1.2 collective-permute-start.10
  32.7 1.5 collective-permute-start.11
  35.0 2.2 %hold.14.refs_4_ = bf16[1024,2048]{1,0:T(8,128)(2,1)S(1)} custom-call(bf16[1024,2048]{1,0:T(8,128)(2,1)} %bitcast.19), custom_call_target="tpu_custom_call" | custom-call | bytes 8388608 | tf_op jit(solution)/shard_map/hold/pallas_call | solution.py:180
  37.4 1.8 %collective-permute-done.12.refs_3_ = bf16[32,1024]{1,0:T(8,128)(2,1)S(1)} collective-permute-done((bf16[32,1024]{1,0:T(8,128)(2,1)S(1)}, bf16[32,1024]{1,0:T(8,128)(2,1)S(1)}, u32[]{:S(2)}, u32[]{:S(2)}) %collective-permute-start.12) | collective-permute-done | bytes 65568 | tf_op jit(solution)/shard_map/ppermute | solution.py:31
  39.9 5.0 %collective-permute-start.13 = (bf16[128,2048]{1,0:T(8,128)(2,1)S(1)}, bf16[128,2048]{1,0:T(8,128)(2,1)S(1)}, u32[]{:S(2)}, u32[]{:S(2)}) collective-permute-start(bf16[128,2048]{1,0:T(8,128)(2,1)S(1)} %up_product.4.mine.pre_mine), channel_id=1, source_target_pairs={{0,1},{1,0},{2,3},{3,2},{4,5},{5,4},{6,7},{7,6},{8,9},{9,8},{10,11... | collective-permute-start | bytes 1572872 | tf_op jit(solution)/shard_map/ppermute | solution.py:22
  44.9 2.0 %collective-permute-start.14 = (bf16[32,1024]{1,0:T(8,128)(2,1)S(1)}, bf16[32,1024]{1,0:T(8,128)(2,1)S(1)}, u32[]{:S(2)}, u32[]{:S(2)}) collective-permute-start(bf16[32,1024]{1,0:T(8,128)(2,1)S(1)} %get-tuple-element.144.refs_0_.first), channel_id=1, source_target_pairs={{0,6},{2,4},{4,2},{6,0},{1,7},{3,5},{5,3},{7,1},{8,14},{10,12},{12... | collective-permute-start | bytes 196616 | tf_op jit(solution)/shard_map/ppermute | solution.py:31
  46.9 2.2 %hold.15.weight = bf16[2048,1024]{1,0:T(8,128)(2,1)S(1)} custom-call(bf16[2048,1024]{1,0:T(8,128)(2,1)} %bitcast.13), custom_call_target="tpu_custom_call" | custom-call | bytes 8388608 | tf_op jit(solution)/shard_map/hold/pallas_call | solution.py:180
  50.3 2.3 %collective-permute-start.16 = (bf16[32,1024]{1,0:T(8,128)(2,1)S(1)}, bf16[32,1024]{1,0:T(8,128)(2,1)S(1)}, u32[]{:S(2)}, u32[]{:S(2)}) collective-permute-start(bf16[32,1024]{1,0:T(8,128)(2,1)S(1)} %get-tuple-element.147), channel_id=1, source_target_pairs={{0,4},{2,6},{4,0},{6,2},{1,5},{3,7},{5,1},{7,3},{8,12},{10,14},{12... | collective-permute-start | bytes 196616 | tf_op jit(solution)/shard_map/ppermute | solution.py:31
  52.6 1.2 collective-permute-start.17
  54.4 3.5 %collective-permute-done.17.refs_3_ = bf16[32,1024]{1,0:T(8,128)(2,1)S(1)} collective-permute-done((bf16[32,1024]{1,0:T(8,128)(2,1)S(1)}, bf16[32,1024]{1,0:T(8,128)(2,1)S(1)}, u32[]{:S(2)}, u32[]{:S(2)}) %collective-permute-start.17) | collective-permute-done | bytes 65568 | tf_op jit(solution)/shard_map/ppermute | solution.py:31
  58.0 4.0 %collective-permute-start.18 = (bf16[32,1024]{1,0:T(8,128)(2,1)S(1)}, bf16[32,1024]{1,0:T(8,128)(2,1)S(1)}, u32[]{:S(2)}, u32[]{:S(2)}) collective-permute-start(bf16[32,1024]{1,0:T(8,128)(2,1)S(1)} %get-tuple-element.156), channel_id=1, source_target_pairs={{0,8},{8,16},{16,24},{1,9},{9,17},{17,25},{2,10},{10,18},{18,26},{... | collective-permute-start | bytes 196616 | tf_op jit(solution)/shard_map/ppermute | solution.py:17
  62.0 1.3 collective-permute-done.18.arrived
  63.9 1.0 collective-permute-start.21
  64.9 2.0 %collective-permute-start.22 = (bf16[32,1024]{1,0:T(8,128)(2,1)S(1)}, bf16[32,1024]{1,0:T(8,128)(2,1)S(1)}, u32[]{:S(2)}, u32[]{:S(2)}) collective-permute-start(bf16[32,1024]{1,0:T(8,128)(2,1)S(1)} %arrive.5.refs_0_.first_out), channel_id=1, source_target_pairs={{0,6},{2,4},{4,2},{6,0},{1,7},{3,5},{5,3},{7,1},{8,14},{10,12},{12... | collective-permute-start | bytes 196616 | tf_op jit(solution)/shard_map/ppermute | solution.py:31
  67.0 2.2 %hold.16.refs_4_ = bf16[2048,1024]{1,0:T(8,128)(2,1)S(1)} custom-call(bf16[2048,1024]{1,0:T(8,128)(2,1)} %bitcast.14), custom_call_target="tpu_custom_call" | custom-call | bytes 8388608 | tf_op jit(solution)/shard_map/hold/pallas_call | solution.py:180
  69.2 2.2 %hold.17.refs_4_ = bf16[1024,2048]{1,0:T(8,128)(2,1)S(1)} custom-call(bf16[1024,2048]{1,0:T(8,128)(2,1)} %bitcast.20), custom_call_target="tpu_custom_call" | custom-call | bytes 8388608 | tf_op jit(solution)/shard_map/hold/pallas_call | solution.py:180
  71.4 1.5 back_product.3
  72.9 4.0 %collective-permute-start.19 = (bf16[128,2048]{1,0:T(8,128)(2,1)S(1)}, bf16[128,2048]{1,0:T(8,128)(2,1)S(1)}, u32[]{:S(2)}, u32[]{:S(2)}) collective-permute-start(bf16[128,2048]{1,0:T(8,128)(2,1)S(1)} %get-tuple-element.160.mine), channel_id=1, source_target_pairs={{0,1},{1,0},{2,3},{3,2},{4,5},{5,4},{6,7},{7,6},{8,9},{9,8},{10,11... | collective-permute-start | bytes 1572872 | tf_op jit(solution)/shard_map/ppermute | solution.py:22
  77.8 2.2 %hold.18.weight = bf16[1024,2048]{1,0:T(8,128)(2,1)S(1)} custom-call(bf16[1024,2048]{1,0:T(8,128)(2,1)} %bitcast.21), custom_call_target="tpu_custom_call" | custom-call | bytes 8388608 | tf_op jit(solution)/shard_map/hold/pallas_call | solution.py:180
  80.0 1.6 in_product.2
  81.7 1.5 collective-permute-start.25
  83.2 2.0 %collective-permute-start.26 = (bf16[32,1024]{1,0:T(8,128)(2,1)S(1)}, bf16[32,1024]{1,0:T(8,128)(2,1)S(1)}, u32[]{:S(2)}, u32[]{:S(2)}) collective-permute-start(bf16[32,1024]{1,0:T(8,128)(2,1)S(1)} %get-tuple-element.170), channel_id=1, source_target_pairs={{0,6},{2,4},{4,2},{6,0},{1,7},{3,5},{5,3},{7,1},{8,14},{10,12},{12... | collective-permute-start | bytes 196616 | tf_op jit(solution)/shard_map/ppermute | solution.py:31
  85.8 2.9 %collective-permute-done.26.refs_3_ = bf16[32,1024]{1,0:T(8,128)(2,1)S(1)} collective-permute-done((bf16[32,1024]{1,0:T(8,128)(2,1)S(1)}, bf16[32,1024]{1,0:T(8,128)(2,1)S(1)}, u32[]{:S(2)}, u32[]{:S(2)}) %collective-permute-start.26) | collective-permute-done | bytes 65568 | tf_op jit(solution)/shard_map/ppermute | solution.py:31
  88.8 2.1 %collective-permute-start.27 = (bf16[32,1024]{1,0:T(8,128)(2,1)S(1)}, bf16[32,1024]{1,0:T(8,128)(2,1)S(1)}, u32[]{:S(2)}, u32[]{:S(2)}) collective-permute-start(bf16[32,1024]{1,0:T(8,128)(2,1)S(1)} %leave_back.2.refs_7_), channel_id=1, source_target_pairs={{8,0},{16,8},{24,16},{9,1},{17,9},{25,17},{10,2},{18,10},{26,18},{... | collective-permute-start | bytes 196616 | tf_op jit(solution)/shard_map/ppermute | solution.py:17
  90.9 2.2 %hold.19.weight = bf16[2048,1024]{1,0:T(8,128)(2,1)S(1)} custom-call(bf16[2048,1024]{1,0:T(8,128)(2,1)} %bitcast.15), custom_call_target="tpu_custom_call" | custom-call | bytes 8388608 | tf_op jit(solution)/shard_map/hold/pallas_call | solution.py:180
  94.1 1.3 collective-permute-done.27.arrived
  95.4 1.3 collective-permute-start.28
  97.1 1.9 %collective-permute-start.30 = (bf16[32,1024]{1,0:T(8,128)(2,1)S(1)}, bf16[32,1024]{1,0:T(8,128)(2,1)S(1)}, u32[]{:S(2)}, u32[]{:S(2)}) collective-permute-start(bf16[32,1024]{1,0:T(8,128)(2,1)S(1)} %arrive.6.refs_0_.first), channel_id=1, source_target_pairs={{0,6},{2,4},{4,2},{6,0},{1,7},{3,5},{5,3},{7,1},{8,14},{10,12},{12... | collective-permute-start | bytes 196616 | tf_op jit(solution)/shard_map/ppermute | solution.py:31
  99.0 2.2 %hold.20.refs_4_ = bf16[2048,1024]{1,0:T(8,128)(2,1)S(1)} custom-call(bf16[2048,1024]{1,0:T(8,128)(2,1)} %bitcast.16), custom_call_target="tpu_custom_call" | custom-call | bytes 8388608 | tf_op jit(solution)/shard_map/hold/pallas_call | solution.py:180
  102.2 1.5 back_product.4
  103.7 4.8 %collective-permute-start.31 = (bf16[128,2048]{1,0:T(8,128)(2,1)S(1)}, bf16[128,2048]{1,0:T(8,128)(2,1)S(1)}, u32[]{:S(2)}, u32[]{:S(2)}) collective-permute-start(bf16[128,2048]{1,0:T(8,128)(2,1)S(1)} %get-tuple-element.187.mine), channel_id=1, source_target_pairs={{0,1},{1,0},{2,3},{3,2},{4,5},{5,4},{6,7},{7,6},{8,9},{9,8},{10,11... | collective-permute-start | bytes 1572872 | tf_op jit(solution)/shard_map/ppermute | solution.py:22
  108.4 2.2 %hold.21.weight = bf16[1024,2048]{1,0:T(8,128)(2,1)S(1)} custom-call(bf16[1024,2048]{1,0:T(8,128)(2,1)} %bitcast.22), custom_call_target="tpu_custom_call" | custom-call | bytes 8388608 | tf_op jit(solution)/shard_map/hold/pallas_call | solution.py:180
  110.7 1.6 in_product.3
  112.3 1.8 %collective-permute-start.33 = (bf16[32,1024]{1,0:T(8,128)(2,1)S(1)}, bf16[32,1024]{1,0:T(8,128)(2,1)S(1)}, u32[]{:S(2)}, u32[]{:S(2)}) collective-permute-start(bf16[32,1024]{1,0:T(8,128)(2,1)S(1)} %get-tuple-element.191), channel_id=1, source_target_pairs={{0,4},{2,6},{4,0},{6,2},{1,5},{3,7},{5,1},{7,3},{8,12},{10,14},{12... | collective-permute-start | bytes 196616 | tf_op jit(solution)/shard_map/ppermute | solution.py:31
  114.1 1.8 %collective-permute-start.34 = (bf16[32,1024]{1,0:T(8,128)(2,1)S(1)}, bf16[32,1024]{1,0:T(8,128)(2,1)S(1)}, u32[]{:S(2)}, u32[]{:S(2)}) collective-permute-start(bf16[32,1024]{1,0:T(8,128)(2,1)S(1)} %get-tuple-element.192), channel_id=1, source_target_pairs={{0,6},{2,4},{4,2},{6,0},{1,7},{3,5},{5,3},{7,1},{8,14},{10,12},{12... | collective-permute-start | bytes 196616 | tf_op jit(solution)/shard_map/ppermute | solution.py:31
  117.0 2.0 %collective-permute-done.34.refs_3_ = bf16[32,1024]{1,0:T(8,128)(2,1)S(1)} collective-permute-done((bf16[32,1024]{1,0:T(8,128)(2,1)S(1)}, bf16[32,1024]{1,0:T(8,128)(2,1)S(1)}, u32[]{:S(2)}, u32[]{:S(2)}) %collective-permute-start.34) | collective-permute-done | bytes 65568 | tf_op jit(solution)/shard_map/ppermute | solution.py:31
  119.0 1.9 %collective-permute-start.35 = (bf16[32,1024]{1,0:T(8,128)(2,1)S(1)}, bf16[32,1024]{1,0:T(8,128)(2,1)S(1)}, u32[]{:S(2)}, u32[]{:S(2)}) collective-permute-start(bf16[32,1024]{1,0:T(8,128)(2,1)S(1)} %leave_back.3.refs_6_), channel_id=1, source_target_pairs={{8,0},{16,8},{24,16},{9,1},{17,9},{25,17},{10,2},{18,10},{26,18},{... | collective-permute-start | bytes 196616 | tf_op jit(solution)/shard_map/ppermute | solution.py:17
  121.0 4.0 %collective-permute-done.35.arrived = bf16[32,1024]{1,0:T(8,128)(2,1)S(1)} collective-permute-done((bf16[32,1024]{1,0:T(8,128)(2,1)S(1)}, bf16[32,1024]{1,0:T(8,128)(2,1)S(1)}, u32[]{:S(2)}, u32[]{:S(2)}) %collective-permute-start.35) | collective-permute-done | bytes 65568 | tf_op jit(solution)/shard_map/ppermute | solution.py:17
  125.0 2.6 %collective-permute-start.36 = (bf16[32,1024]{1,0:T(8,128)(2,1)S(1)}, bf16[32,1024]{1,0:T(8,128)(2,1)S(1)}, u32[]{:S(2)}, u32[]{:S(2)}) collective-permute-start(bf16[32,1024]{1,0:T(8,128)(2,1)S(1)} %arrive.7.refs_0_.first_grad), channel_id=1, source_target_pairs={{0,2},{2,0},{4,6},{6,4},{1,3},{3,1},{5,7},{7,5},{8,10},{10,8},{12,... | collective-permute-start | bytes 196616 | tf_op jit(solution)/shard_map/ppermute | solution.py:31
  128.0 1.8 %collective-permute-start.38 = (bf16[32,1024]{1,0:T(8,128)(2,1)S(1)}, bf16[32,1024]{1,0:T(8,128)(2,1)S(1)}, u32[]{:S(2)}, u32[]{:S(2)}) collective-permute-start(bf16[32,1024]{1,0:T(8,128)(2,1)S(1)} %arrive.7.refs_0_.first_grad), channel_id=1, source_target_pairs={{0,6},{2,4},{4,2},{6,0},{1,7},{3,5},{5,3},{7,1},{8,14},{10,12},{12... | collective-permute-start | bytes 196616 | tf_op jit(solution)/shard_map/ppermute | solution.py:31
  129.7 2.2 %hold.22.refs_4_ = bf16[2048,1024]{1,0:T(8,128)(2,1)S(1)} custom-call(bf16[2048,1024]{1,0:T(8,128)(2,1)} %bitcast.17), custom_call_target="tpu_custom_call" | custom-call | bytes 8388608 | tf_op jit(solution)/shard_map/hold/pallas_call | solution.py:180
  132.2 1.1 collective-permute-done.38.refs_3_
  133.3 1.5 back_product.5
  134.8 3.5 %collective-permute-start.39 = (bf16[128,2048]{1,0:T(8,128)(2,1)S(1)}, bf16[128,2048]{1,0:T(8,128)(2,1)S(1)}, u32[]{:S(2)}, u32[]{:S(2)}) collective-permute-start(bf16[128,2048]{1,0:T(8,128)(2,1)S(1)} %get-tuple-element.200.refs_0_), channel_id=1, source_target_pairs={{0,1},{1,0},{2,3},{3,2},{4,5},{5,4},{6,7},{7,6},{8,9},{9,8},{10,11... | collective-permute-start | bytes 1572872 | tf_op jit(solution)/shard_map/ppermute | solution.py:22
  139.0 2.2 %hold.23.refs_4_ = bf16[1024,2048]{1,0:T(8,128)(2,1)S(1)} custom-call(bf16[1024,2048]{1,0:T(8,128)(2,1)} %bitcast.23), custom_call_target="tpu_custom_call" | custom-call | bytes 8388608 | tf_op jit(solution)/shard_map/hold/pallas_call | solution.py:180
  141.2 1.6 in_product_last.1
  143.5 1.4 collective-permute-start.41
  144.9 1.5 collective-permute-start.42
  146.4 5.4 %weight_grad.3 = bf16[2048,1024]{1,0:T(8,128)(2,1)} custom-call(bf16[2048,128]{1,0:T(8,128)(2,1)S(1)} %turned.7.refs_0_, bf16[2048,128]{1,0:T(8,128)(2,1)S(1)} %turned.9.refs_1_, bf16[2048,128]{1,0:T(8,128)(2,1)S(1)} %turned.11.refs_2_, bf16[128,1024]{1,0:T(8,128)(2,1)S(1)} %get-tuple-element.215.refs_3_, bf16[128,1024]{1,0:T(8,128)(2,1)S(1)} %get-tuple-element.216.refs_4_, ...), custom_call_target="tpu_custom_call" | custom-call | flops 1610612736 | bytes 4194304 | tf_op jit(solution)/shard_map/weight_grad/pallas_call | solution.py:264
  151.8 4.1 %weight_grad.2 = bf16[1024,2048]{1,0:T(8,128)(2,1)} custom-call(bf16[1024,128]{1,0:T(8,128)(2,1)S(1)} %turned.6.refs_0_, bf16[1024,128]{1,0:T(8,128)(2,1)S(1)} %turned.8.refs_1_, bf16[1024,128]{1,0:T(8,128)(2,1)S(1)} %turned.10.refs_2_, bf16[128,2048]{1,0:T(8,128)(2,1)S(1)} %get-tuple-element.209.refs_3_, bf16[128,2048]{1,0:T(8,128)(2,1)S(1)} %get-tuple-element.210.refs_4_, ...), custom_call_target="tpu_custom_call" | custom-call | flops 1610612736 | bytes 4194304 | tf_op jit(solution)/shard_map/weight_grad/pallas_call | solution.py:264
  (69 shorter events, 15.9 us)
Async XLA Ops:
  1.5 8.9 %collective-permute-start.3 = (bf16[32,1024]{1,0:T(8,128)(2,1)S(1)}, bf16[32,1024]{1,0:T(8,128)(2,1)S(1)}, u32[]{:S(2)}, u32[]{:S(2)}) collective-permute-start(bf16[32,1024]{1,0:T(8,128)(2,1)S(1)} %get-tuple-element.144.refs_0_.first), channel_id=1, source_target_pairs={{0,2},{2,0},{4,6},{6,4},{1,3},{3,1},{5,7},{7,5},{8,10},{10,8},{12,... | collective-permute-start | bytes 196616 | tf_op jit(solution)/shard_map/ppermute | solution.py:31
  2.9 7.5 %collective-permute-start = (bf16[32,1024]{1,0:T(8,128)(2,1)S(1)}, bf16[32,1024]{1,0:T(8,128)(2,1)S(1)}, u32[]{:S(2)}, u32[]{:S(2)}) collective-permute-start(bf16[32,1024]{1,0:T(8,128)(2,1)S(1)} %get-tuple-element.149.refs_0_.first), channel_id=1, source_target_pairs={{0,2},{2,0},{4,6},{6,4},{1,3},{3,1},{5,7},{7,5},{8,10},{10,8},{12,... | collective-permute-start | bytes 196616 | tf_op jit(solution)/shard_map/ppermute | solution.py:31
  3.1 7.4 %collective-permute-start.1 = (bf16[32,1024]{1,0:T(8,128)(2,1)S(1)}, bf16[32,1024]{1,0:T(8,128)(2,1)S(1)}, u32[]{:S(2)}, u32[]{:S(2)}) collective-permute-start(bf16[32,1024]{1,0:T(8,128)(2,1)S(1)} %get-tuple-element.149.refs_0_.first), channel_id=1, source_target_pairs={{0,4},{2,6},{4,0},{6,2},{1,5},{3,7},{5,1},{7,3},{8,12},{10,14},{12... | collective-permute-start | bytes 196616 | tf_op jit(solution)/shard_map/ppermute | solution.py:31
  5.4 5.8 %collective-permute-start.2 = (bf16[32,1024]{1,0:T(8,128)(2,1)S(1)}, bf16[32,1024]{1,0:T(8,128)(2,1)S(1)}, u32[]{:S(2)}, u32[]{:S(2)}) collective-permute-start(bf16[32,1024]{1,0:T(8,128)(2,1)S(1)} %get-tuple-element.149.refs_0_.first), channel_id=1, source_target_pairs={{0,6},{2,4},{4,2},{6,0},{1,7},{3,5},{5,3},{7,1},{8,14},{10,12},{12... | collective-permute-start | bytes 196616 | tf_op jit(solution)/shard_map/ppermute | solution.py:31
  6.4 2.2 %copy-start = (s32[6]{0:T(128)S(1)}, s32[6]{0:T(128)}, u32[]{:S(2)}) copy-start(s32[6]{0:T(128)} %sample_ids) | copy-start | bytes 76
  11.9 6.1 %collective-permute-start.4 = (bf16[128,2048]{1,0:T(8,128)(2,1)S(1)}, bf16[128,2048]{1,0:T(8,128)(2,1)S(1)}, u32[]{:S(2)}, u32[]{:S(2)}) collective-permute-start(bf16[128,2048]{1,0:T(8,128)(2,1)S(1)} %up_product.3.mine.refs_2_), channel_id=1, source_target_pairs={{0,1},{1,0},{2,3},{3,2},{4,5},{5,4},{6,7},{7,6},{8,9},{9,8},{10,11... | collective-permute-start | bytes 1572872 | tf_op jit(solution)/shard_map/ppermute | solution.py:22
  13.8 6.0 %collective-permute-start.5 = (bf16[32,1024]{1,0:T(8,128)(2,1)S(1)}, bf16[32,1024]{1,0:T(8,128)(2,1)S(1)}, u32[]{:S(2)}, u32[]{:S(2)}) collective-permute-start(bf16[32,1024]{1,0:T(8,128)(2,1)S(1)} %get-tuple-element.144.refs_0_.first), channel_id=1, source_target_pairs={{0,4},{2,6},{4,0},{6,2},{1,5},{3,7},{5,1},{7,3},{8,12},{10,14},{12... | collective-permute-start | bytes 196616 | tf_op jit(solution)/shard_map/ppermute | solution.py:31
  19.8 3.6 %collective-permute-start.6 = (bf16[32,1024]{1,0:T(8,128)(2,1)S(1)}, bf16[32,1024]{1,0:T(8,128)(2,1)S(1)}, u32[]{:S(2)}, u32[]{:S(2)}) collective-permute-start(bf16[32,1024]{1,0:T(8,128)(2,1)S(1)} %get-tuple-element.133), channel_id=1, source_target_pairs={{0,2},{2,0},{4,6},{6,4},{1,3},{3,1},{5,7},{7,5},{8,10},{10,8},{12,... | collective-permute-start | bytes 196616 | tf_op jit(solution)/shard_map/ppermute | solution.py:31
  19.8 4.0 %collective-permute-start.7 = (bf16[32,1024]{1,0:T(8,128)(2,1)S(1)}, bf16[32,1024]{1,0:T(8,128)(2,1)S(1)}, u32[]{:S(2)}, u32[]{:S(2)}) collective-permute-start(bf16[32,1024]{1,0:T(8,128)(2,1)S(1)} %get-tuple-element.134), channel_id=1, source_target_pairs={{0,4},{2,6},{4,0},{6,2},{1,5},{3,7},{5,1},{7,3},{8,12},{10,14},{12... | collective-permute-start | bytes 196616 | tf_op jit(solution)/shard_map/ppermute | solution.py:31
  20.6 5.7 %collective-permute-start.8 = (bf16[32,1024]{1,0:T(8,128)(2,1)S(1)}, bf16[32,1024]{1,0:T(8,128)(2,1)S(1)}, u32[]{:S(2)}, u32[]{:S(2)}) collective-permute-start(bf16[32,1024]{1,0:T(8,128)(2,1)S(1)} %get-tuple-element.135), channel_id=1, source_target_pairs={{0,6},{2,4},{4,2},{6,0},{1,7},{3,5},{5,3},{7,1},{8,14},{10,12},{12... | collective-permute-start | bytes 196616 | tf_op jit(solution)/shard_map/ppermute | solution.py:31
  26.4 5.0 %collective-permute-start.9 = (bf16[32,1024]{1,0:T(8,128)(2,1)S(1)}, bf16[32,1024]{1,0:T(8,128)(2,1)S(1)}, u32[]{:S(2)}, u32[]{:S(2)}) collective-permute-start(bf16[32,1024]{1,0:T(8,128)(2,1)S(1)} %get-tuple-element.136), channel_id=1, source_target_pairs={{0,8},{8,16},{16,24},{1,9},{9,17},{17,25},{2,10},{10,18},{18,26},{... | collective-permute-start | bytes 196616 | tf_op jit(solution)/shard_map/ppermute | solution.py:17
  31.4 5.8 %collective-permute-start.10 = (bf16[32,1024]{1,0:T(8,128)(2,1)S(1)}, bf16[32,1024]{1,0:T(8,128)(2,1)S(1)}, u32[]{:S(2)}, u32[]{:S(2)}) collective-permute-start(bf16[32,1024]{1,0:T(8,128)(2,1)S(1)} %arrive.4.refs_0_.first), channel_id=1, source_target_pairs={{0,2},{2,0},{4,6},{6,4},{1,3},{3,1},{5,7},{7,5},{8,10},{10,8},{12,... | collective-permute-start | bytes 196616 | tf_op jit(solution)/shard_map/ppermute | solution.py:31
  32.7 4.7 %collective-permute-start.11 = (bf16[32,1024]{1,0:T(8,128)(2,1)S(1)}, bf16[32,1024]{1,0:T(8,128)(2,1)S(1)}, u32[]{:S(2)}, u32[]{:S(2)}) collective-permute-start(bf16[32,1024]{1,0:T(8,128)(2,1)S(1)} %arrive.4.refs_0_.first), channel_id=1, source_target_pairs={{0,4},{2,6},{4,0},{6,2},{1,5},{3,7},{5,1},{7,3},{8,12},{10,14},{12... | collective-permute-start | bytes 196616 | tf_op jit(solution)/shard_map/ppermute | solution.py:31
  34.2 4.9 %collective-permute-start.12 = (bf16[32,1024]{1,0:T(8,128)(2,1)S(1)}, bf16[32,1024]{1,0:T(8,128)(2,1)S(1)}, u32[]{:S(2)}, u32[]{:S(2)}) collective-permute-start(bf16[32,1024]{1,0:T(8,128)(2,1)S(1)} %arrive.4.refs_0_.first), channel_id=1, source_target_pairs={{0,6},{2,4},{4,2},{6,0},{1,7},{3,5},{5,3},{7,1},{8,14},{10,12},{12... | collective-permute-start | bytes 196616 | tf_op jit(solution)/shard_map/ppermute | solution.py:31
  39.9 9.2 %collective-permute-start.13 = (bf16[128,2048]{1,0:T(8,128)(2,1)S(1)}, bf16[128,2048]{1,0:T(8,128)(2,1)S(1)}, u32[]{:S(2)}, u32[]{:S(2)}) collective-permute-start(bf16[128,2048]{1,0:T(8,128)(2,1)S(1)} %up_product.4.mine.pre_mine), channel_id=1, source_target_pairs={{0,1},{1,0},{2,3},{3,2},{4,5},{5,4},{6,7},{7,6},{8,9},{9,8},{10,11... | collective-permute-start | bytes 1572872 | tf_op jit(solution)/shard_map/ppermute | solution.py:22
  44.9 5.5 %collective-permute-start.14 = (bf16[32,1024]{1,0:T(8,128)(2,1)S(1)}, bf16[32,1024]{1,0:T(8,128)(2,1)S(1)}, u32[]{:S(2)}, u32[]{:S(2)}) collective-permute-start(bf16[32,1024]{1,0:T(8,128)(2,1)S(1)} %get-tuple-element.144.refs_0_.first), channel_id=1, source_target_pairs={{0,6},{2,4},{4,2},{6,0},{1,7},{3,5},{5,3},{7,1},{8,14},{10,12},{12... | collective-permute-start | bytes 196616 | tf_op jit(solution)/shard_map/ppermute | solution.py:31
  50.3 3.9 %collective-permute-start.15 = (bf16[32,1024]{1,0:T(8,128)(2,1)S(1)}, bf16[32,1024]{1,0:T(8,128)(2,1)S(1)}, u32[]{:S(2)}, u32[]{:S(2)}) collective-permute-start(bf16[32,1024]{1,0:T(8,128)(2,1)S(1)} %get-tuple-element.146), channel_id=1, source_target_pairs={{0,2},{2,0},{4,6},{6,4},{1,3},{3,1},{5,7},{7,5},{8,10},{10,8},{12,... | collective-permute-start | bytes 196616 | tf_op jit(solution)/shard_map/ppermute | solution.py:31
  50.3 4.0 %collective-permute-start.16 = (bf16[32,1024]{1,0:T(8,128)(2,1)S(1)}, bf16[32,1024]{1,0:T(8,128)(2,1)S(1)}, u32[]{:S(2)}, u32[]{:S(2)}) collective-permute-start(bf16[32,1024]{1,0:T(8,128)(2,1)S(1)} %get-tuple-element.147), channel_id=1, source_target_pairs={{0,4},{2,6},{4,0},{6,2},{1,5},{3,7},{5,1},{7,3},{8,12},{10,14},{12... | collective-permute-start | bytes 196616 | tf_op jit(solution)/shard_map/ppermute | solution.py:31
  52.6 5.3 %collective-permute-start.17 = (bf16[32,1024]{1,0:T(8,128)(2,1)S(1)}, bf16[32,1024]{1,0:T(8,128)(2,1)S(1)}, u32[]{:S(2)}, u32[]{:S(2)}) collective-permute-start(bf16[32,1024]{1,0:T(8,128)(2,1)S(1)} %get-tuple-element.148), channel_id=1, source_target_pairs={{0,6},{2,4},{4,2},{6,0},{1,7},{3,5},{5,3},{7,1},{8,14},{10,12},{12... | collective-permute-start | bytes 196616 | tf_op jit(solution)/shard_map/ppermute | solution.py:31
  58.0 5.3 %collective-permute-start.18 = (bf16[32,1024]{1,0:T(8,128)(2,1)S(1)}, bf16[32,1024]{1,0:T(8,128)(2,1)S(1)}, u32[]{:S(2)}, u32[]{:S(2)}) collective-permute-start(bf16[32,1024]{1,0:T(8,128)(2,1)S(1)} %get-tuple-element.156), channel_id=1, source_target_pairs={{0,8},{8,16},{16,24},{1,9},{9,17},{17,25},{2,10},{10,18},{18,26},{... | collective-permute-start | bytes 196616 | tf_op jit(solution)/shard_map/ppermute | solution.py:17
  63.4 13.6 %collective-permute-start.20 = (bf16[32,1024]{1,0:T(8,128)(2,1)S(1)}, bf16[32,1024]{1,0:T(8,128)(2,1)S(1)}, u32[]{:S(2)}, u32[]{:S(2)}) collective-permute-start(bf16[32,1024]{1,0:T(8,128)(2,1)S(1)} %arrive.5.refs_0_.first_out), channel_id=1, source_target_pairs={{0,2},{2,0},{4,6},{6,4},{1,3},{3,1},{5,7},{7,5},{8,10},{10,8},{12,... | collective-permute-start | bytes 196616 | tf_op jit(solution)/shard_map/ppermute | solution.py:31
  63.9 13.1 %collective-permute-start.21 = (bf16[32,1024]{1,0:T(8,128)(2,1)S(1)}, bf16[32,1024]{1,0:T(8,128)(2,1)S(1)}, u32[]{:S(2)}, u32[]{:S(2)}) collective-permute-start(bf16[32,1024]{1,0:T(8,128)(2,1)S(1)} %arrive.5.refs_0_.first_out), channel_id=1, source_target_pairs={{0,4},{2,6},{4,0},{6,2},{1,5},{3,7},{5,1},{7,3},{8,12},{10,14},{12... | collective-permute-start | bytes 196616 | tf_op jit(solution)/shard_map/ppermute | solution.py:31
  64.9 12.0 %collective-permute-start.22 = (bf16[32,1024]{1,0:T(8,128)(2,1)S(1)}, bf16[32,1024]{1,0:T(8,128)(2,1)S(1)}, u32[]{:S(2)}, u32[]{:S(2)}) collective-permute-start(bf16[32,1024]{1,0:T(8,128)(2,1)S(1)} %arrive.5.refs_0_.first_out), channel_id=1, source_target_pairs={{0,6},{2,4},{4,2},{6,0},{1,7},{3,5},{5,3},{7,1},{8,14},{10,12},{12... | collective-permute-start | bytes 196616 | tf_op jit(solution)/shard_map/ppermute | solution.py:31
  72.9 7.1 %collective-permute-start.19 = (bf16[128,2048]{1,0:T(8,128)(2,1)S(1)}, bf16[128,2048]{1,0:T(8,128)(2,1)S(1)}, u32[]{:S(2)}, u32[]{:S(2)}) collective-permute-start(bf16[128,2048]{1,0:T(8,128)(2,1)S(1)} %get-tuple-element.160.mine), channel_id=1, source_target_pairs={{0,1},{1,0},{2,3},{3,2},{4,5},{5,4},{6,7},{7,6},{8,9},{9,8},{10,11... | collective-permute-start | bytes 1572872 | tf_op jit(solution)/shard_map/ppermute | solution.py:22
  77.7 2.3 %collective-permute-start.23 = (bf16[128,2048]{1,0:T(8,128)(2,1)S(1)}, bf16[128,2048]{1,0:T(8,128)(2,1)S(1)}, u32[]{:S(2)}, u32[]{:S(2)}) collective-permute-start(bf16[128,2048]{1,0:T(8,128)(2,1)S(1)} %up_product.5.pre_mine.mine), channel_id=1, source_target_pairs={{0,1},{1,0},{2,3},{3,2},{4,5},{5,4},{6,7},{7,6},{8,9},{9,8},{10,11... | collective-permute-start | bytes 1572872 | tf_op jit(solution)/shard_map/ppermute | solution.py:22
  81.6 3.9 %collective-permute-start.24 = (bf16[32,1024]{1,0:T(8,128)(2,1)S(1)}, bf16[32,1024]{1,0:T(8,128)(2,1)S(1)}, u32[]{:S(2)}, u32[]{:S(2)}) collective-permute-start(bf16[32,1024]{1,0:T(8,128)(2,1)S(1)} %get-tuple-element.168), channel_id=1, source_target_pairs={{0,2},{2,0},{4,6},{6,4},{1,3},{3,1},{5,7},{7,5},{8,10},{10,8},{12,... | collective-permute-start | bytes 196616 | tf_op jit(solution)/shard_map/ppermute | solution.py:31
  81.7 4.2 %collective-permute-start.25 = (bf16[32,1024]{1,0:T(8,128)(2,1)S(1)}, bf16[32,1024]{1,0:T(8,128)(2,1)S(1)}, u32[]{:S(2)}, u32[]{:S(2)}) collective-permute-start(bf16[32,1024]{1,0:T(8,128)(2,1)S(1)} %get-tuple-element.169), channel_id=1, source_target_pairs={{0,4},{2,6},{4,0},{6,2},{1,5},{3,7},{5,1},{7,3},{8,12},{10,14},{12... | collective-permute-start | bytes 196616 | tf_op jit(solution)/shard_map/ppermute | solution.py:31
  83.2 5.6 %collective-permute-start.26 = (bf16[32,1024]{1,0:T(8,128)(2,1)S(1)}, bf16[32,1024]{1,0:T(8,128)(2,1)S(1)}, u32[]{:S(2)}, u32[]{:S(2)}) collective-permute-start(bf16[32,1024]{1,0:T(8,128)(2,1)S(1)} %get-tuple-element.170), channel_id=1, source_target_pairs={{0,6},{2,4},{4,2},{6,0},{1,7},{3,5},{5,3},{7,1},{8,14},{10,12},{12... | collective-permute-start | bytes 196616 | tf_op jit(solution)/shard_map/ppermute | solution.py:31
  88.8 6.5 %collective-permute-start.27 = (bf16[32,1024]{1,0:T(8,128)(2,1)S(1)}, bf16[32,1024]{1,0:T(8,128)(2,1)S(1)}, u32[]{:S(2)}, u32[]{:S(2)}) collective-permute-start(bf16[32,1024]{1,0:T(8,128)(2,1)S(1)} %leave_back.2.refs_7_), channel_id=1, source_target_pairs={{8,0},{16,8},{24,16},{9,1},{17,9},{25,17},{10,2},{18,10},{26,18},{... | collective-permute-start | bytes 196616 | tf_op jit(solution)/shard_map/ppermute | solution.py:17
  95.4 5.8 %collective-permute-start.28 = (bf16[32,1024]{1,0:T(8,128)(2,1)S(1)}, bf16[32,1024]{1,0:T(8,128)(2,1)S(1)}, u32[]{:S(2)}, u32[]{:S(2)}) collective-permute-start(bf16[32,1024]{1,0:T(8,128)(2,1)S(1)} %arrive.6.refs_0_.first), channel_id=1, source_target_pairs={{0,2},{2,0},{4,6},{6,4},{1,3},{3,1},{5,7},{7,5},{8,10},{10,8},{12,... | collective-permute-start | bytes 196616 | tf_op jit(solution)/shard_map/ppermute | solution.py:31
  96.7 4.7 %collective-permute-start.29 = (bf16[32,1024]{1,0:T(8,128)(2,1)S(1)}, bf16[32,1024]{1,0:T(8,128)(2,1)S(1)}, u32[]{:S(2)}, u32[]{:S(2)}) collective-permute-start(bf16[32,1024]{1,0:T(8,128)(2,1)S(1)} %arrive.6.refs_0_.first), channel_id=1, source_target_pairs={{0,4},{2,6},{4,0},{6,2},{1,5},{3,7},{5,1},{7,3},{8,12},{10,14},{12... | collective-permute-start | bytes 196616 | tf_op jit(solution)/shard_map/ppermute | solution.py:31
  97.1 5.1 %collective-permute-start.30 = (bf16[32,1024]{1,0:T(8,128)(2,1)S(1)}, bf16[32,1024]{1,0:T(8,128)(2,1)S(1)}, u32[]{:S(2)}, u32[]{:S(2)}) collective-permute-start(bf16[32,1024]{1,0:T(8,128)(2,1)S(1)} %arrive.6.refs_0_.first), channel_id=1, source_target_pairs={{0,6},{2,4},{4,2},{6,0},{1,7},{3,5},{5,3},{7,1},{8,14},{10,12},{12... | collective-permute-start | bytes 196616 | tf_op jit(solution)/shard_map/ppermute | solution.py:31
  103.7 7.0 %collective-permute-start.31 = (bf16[128,2048]{1,0:T(8,128)(2,1)S(1)}, bf16[128,2048]{1,0:T(8,128)(2,1)S(1)}, u32[]{:S(2)}, u32[]{:S(2)}) collective-permute-start(bf16[128,2048]{1,0:T(8,128)(2,1)S(1)} %get-tuple-element.187.mine), channel_id=1, source_target_pairs={{0,1},{1,0},{2,3},{3,2},{4,5},{5,4},{6,7},{7,6},{8,9},{9,8},{10,11... | collective-permute-start | bytes 1572872 | tf_op jit(solution)/shard_map/ppermute | solution.py:22
  112.2 3.9 %collective-permute-start.32 = (bf16[32,1024]{1,0:T(8,128)(2,1)S(1)}, bf16[32,1024]{1,0:T(8,128)(2,1)S(1)}, u32[]{:S(2)}, u32[]{:S(2)}) collective-permute-start(bf16[32,1024]{1,0:T(8,128)(2,1)S(1)} %get-tuple-element.190), channel_id=1, source_target_pairs={{0,2},{2,0},{4,6},{6,4},{1,3},{3,1},{5,7},{7,5},{8,10},{10,8},{12,... | collective-permute-start | bytes 196616 | tf_op jit(solution)/shard_map/ppermute | solution.py:31
  112.3 4.7 %collective-permute-start.33 = (bf16[32,1024]{1,0:T(8,128)(2,1)S(1)}, bf16[32,1024]{1,0:T(8,128)(2,1)S(1)}, u32[]{:S(2)}, u32[]{:S(2)}) collective-permute-start(bf16[32,1024]{1,0:T(8,128)(2,1)S(1)} %get-tuple-element.191), channel_id=1, source_target_pairs={{0,4},{2,6},{4,0},{6,2},{1,5},{3,7},{5,1},{7,3},{8,12},{10,14},{12... | collective-permute-start | bytes 196616 | tf_op jit(solution)/shard_map/ppermute | solution.py:31
  114.1 4.9 %collective-permute-start.34 = (bf16[32,1024]{1,0:T(8,128)(2,1)S(1)}, bf16[32,1024]{1,0:T(8,128)(2,1)S(1)}, u32[]{:S(2)}, u32[]{:S(2)}) collective-permute-start(bf16[32,1024]{1,0:T(8,128)(2,1)S(1)} %get-tuple-element.192), channel_id=1, source_target_pairs={{0,6},{2,4},{4,2},{6,0},{1,7},{3,5},{5,3},{7,1},{8,14},{10,12},{12... | collective-permute-start | bytes 196616 | tf_op jit(solution)/shard_map/ppermute | solution.py:31
  119.0 5.9 %collective-permute-start.35 = (bf16[32,1024]{1,0:T(8,128)(2,1)S(1)}, bf16[32,1024]{1,0:T(8,128)(2,1)S(1)}, u32[]{:S(2)}, u32[]{:S(2)}) collective-permute-start(bf16[32,1024]{1,0:T(8,128)(2,1)S(1)} %leave_back.3.refs_6_), channel_id=1, source_target_pairs={{8,0},{16,8},{24,16},{9,1},{17,9},{25,17},{10,2},{18,10},{26,18},{... | collective-permute-start | bytes 196616 | tf_op jit(solution)/shard_map/ppermute | solution.py:17
  125.0 7.0 %collective-permute-start.36 = (bf16[32,1024]{1,0:T(8,128)(2,1)S(1)}, bf16[32,1024]{1,0:T(8,128)(2,1)S(1)}, u32[]{:S(2)}, u32[]{:S(2)}) collective-permute-start(bf16[32,1024]{1,0:T(8,128)(2,1)S(1)} %arrive.7.refs_0_.first_grad), channel_id=1, source_target_pairs={{0,2},{2,0},{4,6},{6,4},{1,3},{3,1},{5,7},{7,5},{8,10},{10,8},{12,... | collective-permute-start | bytes 196616 | tf_op jit(solution)/shard_map/ppermute | solution.py:31
  127.6 4.7 %collective-permute-start.37 = (bf16[32,1024]{1,0:T(8,128)(2,1)S(1)}, bf16[32,1024]{1,0:T(8,128)(2,1)S(1)}, u32[]{:S(2)}, u32[]{:S(2)}) collective-permute-start(bf16[32,1024]{1,0:T(8,128)(2,1)S(1)} %arrive.7.refs_0_.first_grad), channel_id=1, source_target_pairs={{0,4},{2,6},{4,0},{6,2},{1,5},{3,7},{5,1},{7,3},{8,12},{10,14},{12... | collective-permute-start | bytes 196616 | tf_op jit(solution)/shard_map/ppermute | solution.py:31
  128.0 5.4 %collective-permute-start.38 = (bf16[32,1024]{1,0:T(8,128)(2,1)S(1)}, bf16[32,1024]{1,0:T(8,128)(2,1)S(1)}, u32[]{:S(2)}, u32[]{:S(2)}) collective-permute-start(bf16[32,1024]{1,0:T(8,128)(2,1)S(1)} %arrive.7.refs_0_.first_grad), channel_id=1, source_target_pairs={{0,6},{2,4},{4,2},{6,0},{1,7},{3,5},{5,3},{7,1},{8,14},{10,12},{12... | collective-permute-start | bytes 196616 | tf_op jit(solution)/shard_map/ppermute | solution.py:31
  134.8 6.4 %collective-permute-start.39 = (bf16[128,2048]{1,0:T(8,128)(2,1)S(1)}, bf16[128,2048]{1,0:T(8,128)(2,1)S(1)}, u32[]{:S(2)}, u32[]{:S(2)}) collective-permute-start(bf16[128,2048]{1,0:T(8,128)(2,1)S(1)} %get-tuple-element.200.refs_0_), channel_id=1, source_target_pairs={{0,1},{1,0},{2,3},{3,2},{4,5},{5,4},{6,7},{7,6},{8,9},{9,8},{10,11... | collective-permute-start | bytes 1572872 | tf_op jit(solution)/shard_map/ppermute | solution.py:22
  142.8 13.1 %collective-permute-start.40 = (bf16[2,32,1024]{2,1,0:T(8,128)(2,1)S(1)}, bf16[2,32,1024]{2,1,0:T(8,128)(2,1)S(1)}, u32[]{:S(2)}, u32[]{:S(2)}) collective-permute-start(bf16[2,32,1024]{2,1,0:T(8,128)(2,1)S(1)} %get-tuple-element.203), channel_id=1, source_target_pairs={{0,2},{2,0},{4,6},{6,4},{1,3},{3,1},{5,7},{7,5},{8,10},{10,8},{12,... | collective-permute-start | bytes 393224 | tf_op jit(solution)/shard_map/ppermute | solution.py:31
  143.5 12.4 %collective-permute-start.41 = (bf16[2,32,1024]{2,1,0:T(8,128)(2,1)S(1)}, bf16[2,32,1024]{2,1,0:T(8,128)(2,1)S(1)}, u32[]{:S(2)}, u32[]{:S(2)}) collective-permute-start(bf16[2,32,1024]{2,1,0:T(8,128)(2,1)S(1)} %get-tuple-element.204), channel_id=1, source_target_pairs={{0,4},{2,6},{4,0},{6,2},{1,5},{3,7},{5,1},{7,3},{8,12},{10,14},{12... | collective-permute-start | bytes 393224 | tf_op jit(solution)/shard_map/ppermute | solution.py:31
  144.9 11.0 %collective-permute-start.42 = (bf16[2,32,1024]{2,1,0:T(8,128)(2,1)S(1)}, bf16[2,32,1024]{2,1,0:T(8,128)(2,1)S(1)}, u32[]{:S(2)}, u32[]{:S(2)}) collective-permute-start(bf16[2,32,1024]{2,1,0:T(8,128)(2,1)S(1)} %get-tuple-element.205), channel_id=1, source_target_pairs={{0,6},{2,4},{4,2},{6,0},{1,7},{3,5},{5,3},{7,1},{8,14},{10,12},{12... | collective-permute-start | bytes 393224 | tf_op jit(solution)/shard_map/ppermute | solution.py:31

commit v8 on v7

--- a/solution.py
+++ b/solution.py
@@ -7,8 +7,7 @@
 
 BF = jnp.bfloat16
 F32 = jnp.float32
-LAST = (((1,), (1,)), ((), ()))
-FIRST = (((0,), (0,)), ((), ()))
+WEIGHT_CUTS = 8
 
 
 def from_behind(block, axis, distance):
@@ -23,7 +22,7 @@
 
 
 def partner(row, j, size):
-    return row ^ j if size & (size - 1) == 0 else (j - row) % size
+    return row ^ ((size - j) % size) if size & (size - 1) == 0 else (j - row) % size
 
 
 def swap_rows(block, j):
@@ -41,7 +40,7 @@
 
 def beside(turn):
     size = lax.axis_size("row")
-    return [[1], [2], range(3, size)][turn] if size > 2 else [[], [], [1]][turn]
+    return [[size - 1], [size - 2], range(1, size - 2)][turn] if size > 2 else [[], [], [1]][turn]
 
 
 def after(block, other):
@@ -81,8 +80,9 @@
 def fetch_kernel(sample_ids, inputs, send_base, recv_base, cotangent, *refs):
     ticks = inputs.shape[1]
     count = ticks - 1
+    weights, refs = refs[:2], refs[2:]
     stored, bases, cots = refs[:count], refs[count : 2 * count], refs[2 * count : 3 * count]
-    fresh, sems = refs[3 * count :]
+    *kept, fresh, sems, weight_sems = refs[3 * count :]
     section, sections = lax.axis_index("section"), lax.axis_size("section")
     samples = [sample_ids[tick - section + sections - 1] for tick in range(ticks)]
     copies = []
@@ -93,6 +93,11 @@
             pltpu.make_async_copy(inputs.at[0, t + 1], fresh.at[t], sems.at[4 * t + 2]),
             pltpu.make_async_copy(cotangent.at[0, t], cots[t], sems.at[4 * t + 3]),
         ]
+    for k, (weight, room) in enumerate(zip(weights, kept)):
+        step = weight.shape[0] // WEIGHT_CUTS
+        for i in range(WEIGHT_CUTS):
+            part = pl.ds(i * step, step)
+            copies.append(pltpu.make_async_copy(weight.at[part], room.at[part], weight_sems.at[k, i]))
     for copy in copies:
         copy.start()
     for copy in copies:
@@ -102,20 +107,25 @@
         cots[t][...] = jnp.where(section == sections - 1, cots[t][...], jnp.zeros_like(cots[t]))
 
 
-def fetch(sample_ids, inputs, send_base, recv_base, cotangent):
+def fetch(sample_ids, inputs, send_base, recv_base, cotangent, *weights):
     count = inputs.shape[1] - 1
     piece = inputs.shape[2:]
-    outs = pl.pallas_call(
+    large = [pltpu.with_memory_space_constraint(x, pltpu.HBM) for x in (inputs, send_base, recv_base, cotangent, *weights)]
+    *outs, up_kept, down_kept = pl.pallas_call(
         fetch_kernel,
-        in_specs=[pl.BlockSpec(memory_space=pltpu.SMEM)] + [pl.BlockSpec(memory_space=pltpu.HBM)] * 4,
-        out_specs=vmem(3 * count),
-        out_shape=[pltpu.VMEM(piece, BF)] * (3 * count),
-        scratch_shapes=[pltpu.VMEM((count, *piece), BF), pltpu.SemaphoreType.DMA((4 * count,))],
+        in_specs=[pl.BlockSpec(memory_space=pltpu.SMEM)] + [pl.BlockSpec(memory_space=pltpu.HBM)] * len(large),
+        out_specs=vmem(3 * count + 2),
+        out_shape=[pltpu.VMEM(piece, BF)] * (3 * count) + [pltpu.VMEM(x.shape, BF) for x in weights],
+        scratch_shapes=[
+            pltpu.VMEM((count, *piece), BF),
+            pltpu.SemaphoreType.DMA((4 * count,)),
+            pltpu.SemaphoreType.DMA((2, WEIGHT_CUTS)),
+        ],
         compiler_params=pltpu.CompilerParams(vmem_limit_bytes=4 << 20),
-        cost_estimate=pl.CostEstimate(flops=0, bytes_accessed=2 << 20, transcendentals=0),
+        cost_estimate=pl.CostEstimate(flops=0, bytes_accessed=10 << 20, transcendentals=0),
         name="fetch",
-    )(sample_ids, *[pltpu.with_memory_space_constraint(x, pltpu.HBM) for x in (inputs, send_base, recv_base, cotangent)])
-    return outs[:count], outs[count : 2 * count], outs[2 * count :]
+    )(sample_ids, *large)
+    return outs[:count], outs[count : 2 * count], outs[2 * count :], up_kept, down_kept
 
 
 def first_pieces(inputs, cotangent):
@@ -157,12 +167,13 @@
 def finish(first_out, first_grad, *refs):
     *rest, outs, grads = refs
     count = outs.shape[1] - 1
-    terms, known_outs, known_grads = rest[: -2 * count], rest[-2 * count : -count], rest[-count:]
-    outs[0, count] = added(first_out, [term.at[1] for term in terms])
-    grads[0, 0] = added(first_grad, [term.at[0] for term in terms])
+    terms, known = rest[: -2 * count], rest[-2 * count :]
+    half = len(terms) // 2
+    outs[0, count] = added(first_out, terms[:half])
+    grads[0, 0] = added(first_grad, terms[half:])
     for t in range(count):
-        outs[0, t] = known_outs[t][...]
-        grads[0, t + 1] = known_grads[t][...]
+        outs[0, t] = known[t][...]
+        grads[0, t + 1] = known[count + t][...]
 
 
 def turned(*refs):
@@ -170,23 +181,9 @@
     out[...] = jnp.concatenate([piece[...] for piece in pieces], axis=0).T
 
 
-def hold_kernel(source, kept, sem):
-    copy = pltpu.make_async_copy(source, kept, sem)
-    copy.start()
-    copy.wait()
-
-
-def hold(weight, other):
-    return pl.pallas_call(
-        hold_kernel,
-        in_specs=[pl.BlockSpec(memory_space=pltpu.HBM)],
-        out_specs=pl.BlockSpec(memory_space=pltpu.VMEM),
-        out_shape=pltpu.VMEM(weight.shape, weight.dtype),
-        scratch_shapes=[pltpu.SemaphoreType.DMA],
-        compiler_params=pltpu.CompilerParams(vmem_limit_bytes=2 << 20),
-        cost_estimate=pl.CostEstimate(flops=0, bytes_accessed=4 * weight.size, transcendentals=0),
-        name="hold",
-    )(pltpu.with_memory_space_constraint(after(weight, other), pltpu.HBM))
+def turned_weight(weight, out):
+    for n in columns(out.shape[0]):
+        out[n, :] = weight[:, n].T
 
 
 def columns(width, step=256):
@@ -202,10 +199,8 @@
 
 
 def back_product(*refs):
-    *pieces, weight, whole, product = refs
-    whole[...] = jnp.concatenate([piece[...] for piece in pieces], axis=0)
-    for n in columns(product.shape[1]):
-        product[:, n] = matmul(whole[...], weight[n, :], LAST).astype(BF)
+    *ins, whole, product = refs
+    up_product(*ins, product, whole)
 
 
 def put_rows(pieces, n, product):
@@ -232,16 +227,8 @@
         pre = pre_mine[:, n].astype(F32) + pre_other[:, n].astype(F32)
         grad = mine[:, n].astype(F32) + other[:, n].astype(F32)
         grad_pre[:, n] = (grad * silu_slope(pre)).astype(BF)
-    for n in columns(weight.shape[0]):
-        put_rows(pieces, n, matmul(grad_pre[...], weight[n, :], LAST))
-
-
-def in_product_last(*refs):
-    *ins, grad_pre = refs[: 6 + (len(refs) - 6) // 2]
-    pairs = refs[len(ins) + 1 :]
-    for piece, pair in zip(ins[5:], pairs):
-        pair[1] = piece[...]
-    in_product(*ins[:5], grad_pre, *[pair.at[0] for pair in pairs])
+    for n in columns(weight.shape[1]):
+        put_rows(pieces, n, matmul(grad_pre[...], weight[:, n]))
 
 
 def act_only(mine, other, act):
@@ -251,29 +238,42 @@
 
 
 def weight_grad(*refs):
-    count = len(refs) // 2
-    left = jnp.concatenate([ref[...] for ref in refs[:count]], axis=1)
-    for n in columns(refs[-1].shape[1], 512):
-        right = jnp.concatenate([ref[:, n] for ref in refs[count:-1]], axis=0)
-        refs[-1][:, n] = matmul(left, right).astype(BF)
-
-
-def weight_product(lefts, rights, step=256):
-    rows, width, depth = lefts[0].shape[0], rights[0].shape[1], rights[0].shape[0]
-    step = min(rows, step)
+    *blocks, out, left, right, room, sems = refs
+    count = len(blocks) // 2
+    depth = blocks[-1].shape[0]
+    for t in range(count):
+        left[:, t * depth : (t + 1) * depth] = blocks[t][...]
+        right[t * depth : (t + 1) * depth, :] = blocks[count + t][...]
+    copies = []
+    for i, m in enumerate(columns(out.shape[0])):
+        for n in columns(out.shape[1]):
+            room[m, n] = matmul(left[m, :], right[:, n]).astype(BF)
+        part = pl.ds(m.start, m.stop - m.start)
+        copies.append(pltpu.make_async_copy(room.at[part], out.at[part], sems.at[i]))
+        copies[-1].start()
+    for copy in copies:
+        copy.wait()
+
+
+def weight_product(lefts, rights):
+    rows, width, depth = lefts[0].shape[0], rights[0].shape[1], rights[0].shape[0] * len(rights)
     return pl.pallas_call(
         weight_grad,
-        grid=(rows // step,),
-        in_specs=[pl.BlockSpec((step, depth), lambda i: (i, 0))] * len(lefts)
-        + [pl.BlockSpec((depth, width), lambda i: (0, 0))] * len(rights),
-        out_specs=pl.BlockSpec((step, width), lambda i: (i, 0)),
+        in_specs=vmem(len(lefts) + len(rights)),
+        out_specs=pl.BlockSpec(memory_space=pl.ANY),
         out_shape=jax.ShapeDtypeStruct((rows, width), BF),
-        compiler_params=pltpu.CompilerParams(vmem_limit_bytes=16 << 20),
+        scratch_shapes=[
+            pltpu.VMEM((rows, depth), BF),
+            pltpu.VMEM((depth, width), BF),
+            pltpu.VMEM((rows, width), BF),
+            pltpu.SemaphoreType.DMA((len(columns(rows)),)),
+        ],
+        compiler_params=pltpu.CompilerParams(vmem_limit_bytes=12 << 20),
         cost_estimate=pl.CostEstimate(
-            flops=2 * rows * width * depth * len(lefts), bytes_accessed=2 * rows * width, transcendentals=0
+            flops=2 * rows * width * depth, bytes_accessed=2 * rows * width, transcendentals=0
         ),
         name="weight_grad",
-    )(*lefts, *rights)
+    )(*[pltpu.with_memory_space_constraint(x, pltpu.VMEM) for x in (*lefts, *rights)])
 
 
 def other_cols(partial):
@@ -294,17 +294,16 @@
 
 def per_device(inputs, sample_ids, send_base, recv_base, w_up, w_down, cotangent):
     ticks = inputs.shape[1]
-    up_block, down_block = w_up[0], w_down[0]
     rows = lax.axis_size("row")
     piece_rows, width = inputs.shape[2:]
-    tokens, hidden = rows * piece_rows, up_block.shape[1]
+    tokens, hidden = rows * piece_rows, w_up.shape[2]
     flops = 2 * tokens * width * hidden
     piece_like = jax.ShapeDtypeStruct((piece_rows, width), BF)
-    pair_like = jax.ShapeDtypeStruct((2, piece_rows, width), BF)
     whole_like = jax.ShapeDtypeStruct((tokens, width), BF)
     hidden_like = jax.ShapeDtypeStruct((tokens, hidden), BF)
     turned_like = jax.ShapeDtypeStruct((width, tokens), BF)
     turned_hidden = jax.ShapeDtypeStruct((hidden, tokens), BF)
+    split_like = [hidden_like] + [piece_like] * rows
     room = [pltpu.VMEM((tokens, width), BF)]
 
     act_in, last_cot = first_pieces(inputs, cotangent)
@@ -318,28 +317,34 @@
         if tick == 0:
             for j in beside(0):
                 cot_pieces[j] = swap_rows(after(cot_pieces[0], act_in), j)
-            stored, bases, cots = fetch(after(sample_ids, act_in), inputs, send_base, recv_base, cotangent)
+            stored, bases, cots, up_kept, down_kept = fetch(
+                after(sample_ids, act_in), inputs, send_base, recv_base, cotangent, w_up[0], w_down[0]
+            )
             pieces = after(pieces, ([cot_pieces[j] for j in beside(0)], stored))
         if tick == ticks - 1:
             full_cot, first_grads = run(
-                back_product, [whole_like, hidden_like], *cot_pieces, hold(down_block, act_in), flops=flops
+                back_product, [whole_like, hidden_like], *cot_pieces, after(down_turned, act_in), flops=flops
             )
             pieces = after(pieces, first_grads)
-        (partial,) = run(up_product, [hidden_like], *pieces, hold(up_block, act_in), flops=flops, scratch=room)
+        (partial,) = run(up_product, [hidden_like], *pieces, up_kept, flops=flops, scratch=room)
         other = other_cols(partial)
         if tick < ticks - 1:
             for j in beside(tick + 1):
                 cot_pieces[j] = swap_rows(after(cot_pieces[0], partial), j)
-            act, *terms = run(
-                down_product, [hidden_like] + [piece_like] * rows, partial, other, hold(down_block, partial), flops=flops
-            )
+            act, *terms = run(down_product, split_like, partial, other, down_kept, flops=flops)
             terms = after(terms, [cot_pieces[j] for j in beside(tick + 1)])
             acts.append(act)
             terms_in = scatter_rows(terms)
+            if tick == 0:
+                (down_turned,) = run(
+                    turned_weight, [jax.ShapeDtypeStruct((width, hidden), BF)], after(down_kept, terms)
+                )
+                terms_in[0] = after(terms_in[0], down_turned)
             if tick == 1:
+                (up_turned,) = run(turned_weight, [jax.ShapeDtypeStruct((hidden, width), BF)], after(up_kept, terms))
                 turned_ins += run(turned, [turned_like], *after(in_pieces[0], terms))
                 turned_acts += run(turned, [turned_hidden], after(acts[0], terms))
-                terms_in[0] = after(terms_in[0], (turned_ins, turned_acts))
+                terms_in[0] = after(terms_in[0], (up_turned, turned_ins, turned_acts))
             act_out, sending = run(leave, [piece_like] * 2, act_in, *terms_in, stored[tick])
             seen_out.append(act_out)
         in_pieces.append(pieces)
@@ -357,39 +362,30 @@
             if step == 1:
                 (act,) = run(act_only, [hidden_like], *after(pres[-1], sending))
                 acts.append(act)
-                out_pieces = run(down_again, [piece_like] * rows, act, hold(down_block, sending), flops=flops)
+                out_pieces = run(down_again, [piece_like] * rows, act, down_kept, flops=flops)
                 arrived = after(arrived, out_pieces)
+                out_terms = list(out_pieces)
             (grad_out,) = run(arrive, [piece_like], cots[tick], arrived)
             pieces = gather_rows(grad_out)
-            full_grad, partial = run(
-                back_product, [whole_like, hidden_like], *pieces, hold(down_block, grad_out), flops=flops
-            )
+            full_grad, partial = run(back_product, [whole_like, hidden_like], *pieces, down_turned, flops=flops)
         other = other_cols(partial)
-        up_kept = hold(up_block, pres[-1][0] if step == 0 else partial)
+        for j in beside(step) if step else []:
+            out_terms[j] = swap_rows(after(out_pieces[j], partial), j)
+        grad_pre, *terms = run(in_product, split_like, partial, other, *pres[tick], up_turned, flops=flops)
+        if step:
+            terms = after(terms, [out_terms[j] for j in beside(step)])
+        terms_in = scatter_rows(terms)
         if step < ticks - 1:
-            grad_pre, *terms = run(
-                in_product,
-                [hidden_like] + [piece_like] * rows,
-                partial, other, *pres[tick], up_kept,
-                flops=flops,
-            )
-            terms_in = scatter_rows(terms)
             while len(turned_ins) < min(step + 2, ticks):
                 turned_ins += run(turned, [turned_like], *after(in_pieces[len(turned_ins)], terms))
                 turned_acts += run(turned, [turned_hidden], after(acts[len(turned_acts)], terms))
             terms_in[0] = after(terms_in[0], (turned_ins, turned_acts))
             (sending,) = run(leave_back, [piece_like], grad_out, *terms_in)
             seen_grad[tick] = sending
-        else:
-            grad_pre, *terms = run(
-                in_product_last,
-                [hidden_like] + [pair_like] * rows,
-                partial, other, *pres[tick], up_kept, *out_pieces,
-                flops=flops,
-            )
-            terms_in = scatter_rows(terms)
         full_grads[tick] = full_grad
         pre_grads[tick] = grad_pre
+    for j in beside(0):
+        out_terms[j] = swap_rows(after(out_pieces[j], terms), j)
     lefts = after((turned_ins, turned_acts), terms)
     grad_up = weight_product(lefts[0], pre_grads)
     grad_down = weight_product(lefts[1], full_grads)
@@ -397,12 +393,12 @@
     terms_in[0] = after(terms_in[0], (grad_up, grad_down))
     section_output, input_grad = pl.pallas_call(
         finish,
-        in_specs=vmem(2 + rows + 2 * (ticks - 1)),
+        in_specs=vmem(2 + 2 * rows + 2 * (ticks - 1)),
         out_specs=vmem(2),
         out_shape=[stack_like] * 2,
         compiler_params=pltpu.CompilerParams(vmem_limit_bytes=6 << 20),
         name="finish",
-    )(act_in, grad_out, *terms_in, *seen_out, *seen_grad[1:])
+    )(act_in, grad_out, *out_terms, *terms_in, *seen_out, *seen_grad[1:])
     return (
         jnp.stack(seen_in)[None],
         section_output,

time: 159 us -> 153 us (0.962)
  waiting for transfers between devices: 27.7 us -> 60 us
  Pallas kernels: 54.2 us -> 26 us
  starting transfers between devices: 72.9 us -> 62.6 us
    pallas_call x15 -> x3, Pallas kernels: 36.6 us -> 7.36 us  [the longest x2 6.57 us: weight_product(): pl.pallas_call(weight_grad, in_specs=vmem(len(lefts) + len(rights)), out_...]
    ppermute x33 -> x36, waiting for transfers between devices: 19.2 us -> 46.9 us  [swap_rows(): lax.ppermute(block, 'row', [(i, partner(i, j, size)) for i in range(size)])]
    ppermute x6, starting transfers between devices: 19.3 us -> 8.06 us  [turn(): lax.ppermute(block, axis, [(i, (i + distance) % size) for i in range(size)])]
    pallas_call x1, Pallas kernels: 1.72 us -> 4.31 us  [fetch(): pl.pallas_call(fetch_kernel, in_specs=[pl.BlockSpec(memory_space=pltpu.SM...]
    ppermute x6, waiting for transfers between devices: 0.02 us -> 2.37 us  [turn(): lax.ppermute(block, axis, [(i, (i + distance) % size) for i in range(size)])]
    ppermute x4, waiting for transfers between devices: 8.43 us -> 10.7 us  [from_behind(): return lax.ppermute(block, axis, route)]
    pallas_call x27 -> x29, Pallas kernels: 15 us -> 13.5 us  [run(): pl.pallas_call(kernel, in_specs=vmem(len(ins)), out_specs=vmem(len(outs))...]
    ppermute x33 -> x36, starting transfers between devices: 42.5 us -> 43.3 us  [swap_rows(): lax.ppermute(block, 'row', [(i, partner(i, j, size)) for i in range(size)])]
  transfers between devices with their start and end apart: 43 -> 46, of which waited for: 21 -> 26; matrix products, arithmetic and copies ran while one was open for 0% -> 0% of each run, Pallas kernels for 28% -> 13%
where the time goes in v8:
time: 153 us; the launch traced here: 151 us
  starting transfers between devices  62.6 us (41%)
  waiting for transfers between devices  60 us (39%)
  Pallas kernels  26 us (17%)
    ppermute x36, waiting for transfers between devices, swap_rows(): lax.ppermute(block, 'row', [(i, partner(i, j, size)) for i in range(size)])  46.9 us
    ppermute x36, starting transfers between devices, swap_rows(): lax.ppermute(block, 'row', [(i, partner(i, j, size)) for i in range(size)])  43.3 us
    pallas_call x29, Pallas kernels, run(): pl.pallas_call(kernel, in_specs=vmem(len(ins)), out_specs=vmem(len(outs))...  13.5 us
    ppermute x4, starting transfers between devices, from_behind(): return lax.ppermute(block, axis, route)  11.2 us
    ppermute x4, waiting for transfers between devices, from_behind(): return lax.ppermute(block, axis, route)  10.7 us
    ppermute x6, starting transfers between devices, turn(): lax.ppermute(block, axis, [(i, (i + distance) % size) for i in range(size)])  8.06 us
    pallas_call x2, Pallas kernels, weight_product(): pl.pallas_call(weight_grad, in_specs=vmem(len(lefts) + len(rights)), out_...  6.57 us
    pallas_call x1, Pallas kernels, fetch(): pl.pallas_call(fetch_kernel, in_specs=[pl.BlockSpec(memory_space=pltpu.SM...  4.31 us
  transfers between devices with their start and end apart: 46, of which 26 were waited for; matrix products, arithmetic and copies ran while one was open for 0% of the time, Pallas kernels for 13%

profile of v8, /device:TPU:3, one launch (start us, length us, event | category | flops | bytes accessed | tf_op | source)
XLA Modules:
  0.0 150.9 jit_solution(6430197469619227457)
XLA Ops:
  0.6 0.9 first.1
  1.5 1.4 collective-permute-start.3
  2.9 2.2 %collective-permute-start = (bf16[32,1024]{1,0:T(8,128)(2,1)S(1)}, bf16[32,1024]{1,0:T(8,128)(2,1)S(1)}, u32[]{:S(2)}, u32[]{:S(2)}) collective-permute-start(bf16[32,1024]{1,0:T(8,128)(2,1)S(1)} %get-tuple-element.155.refs_0_.first), channel_id=1, source_target_pairs={{0,6},{2,4},{4,2},{6,0},{1,7},{3,5},{5,3},{7,1},{8,14},{10,12},{12... | collective-permute-start | bytes 196616 | tf_op jit(solution)/shard_map/ppermute | solution.py:30
  5.2 1.2 collective-permute-start.2
  7.1 4.3 %fetch.1 = (bf16[32,1024]{1,0:T(8,128)(2,1)S(1)}, bf16[32,1024]{1,0:T(8,128)(2,1)S(1)}, bf16[32,1024]{1,0:T(8,128)(2,1)S(1)}, bf16[32,1024]{1,0:T(8,128)(2,1)S(1...) custom-call(s32[6]{0:T(128)S(1)} %copy-done, ...), custom_call_target="tpu_custom_call" | custom-call | bytes 10485760 | tf_op jit(solution)/shard_map/fetch/pallas_call | solution.py:114
  13.0 1.1 collective-permute-start.4
  14.0 1.4 collective-permute-start.5
  16.3 3.9 %collective-permute-done.5.refs_2_ = bf16[32,1024]{1,0:T(8,128)(2,1)S(1)} collective-permute-done((bf16[32,1024]{1,0:T(8,128)(2,1)S(1)}, bf16[32,1024]{1,0:T(8,128)(2,1)S(1)}, u32[]{:S(2)}, u32[]{:S(2)}) %collective-permute-start.5) | collective-permute-done | bytes 65568 | tf_op jit(solution)/shard_map/ppermute | solution.py:30
  20.2 2.2 %collective-permute-start.6 = (bf16[32,1024]{1,0:T(8,128)(2,1)S(1)}, bf16[32,1024]{1,0:T(8,128)(2,1)S(1)}, u32[]{:S(2)}, u32[]{:S(2)}) collective-permute-start(bf16[32,1024]{1,0:T(8,128)(2,1)S(1)} %get-tuple-element.138), channel_id=1, source_target_pairs={{0,6},{2,4},{4,2},{6,0},{1,7},{3,5},{5,3},{7,1},{8,14},{10,12},{12... | collective-permute-start | bytes 196616 | tf_op jit(solution)/shard_map/ppermute | solution.py:30
  22.5 1.3 collective-permute-start.8
  23.8 1.2 turned_weight.2.refs_4_
  25.2 3.7 %collective-permute-done.7.refs_2_ = bf16[32,1024]{1,0:T(8,128)(2,1)S(1)} collective-permute-done((bf16[32,1024]{1,0:T(8,128)(2,1)S(1)}, bf16[32,1024]{1,0:T(8,128)(2,1)S(1)}, u32[]{:S(2)}, u32[]{:S(2)}) %collective-permute-start.7) | collective-permute-done | bytes 65568 | tf_op jit(solution)/shard_map/ppermute | solution.py:30
  28.9 3.1 %collective-permute-start.9 = (bf16[32,1024]{1,0:T(8,128)(2,1)S(1)}, bf16[32,1024]{1,0:T(8,128)(2,1)S(1)}, u32[]{:S(2)}, u32[]{:S(2)}) collective-permute-start(bf16[32,1024]{1,0:T(8,128)(2,1)S(1)} %get-tuple-element.143), channel_id=1, source_target_pairs={{0,8},{8,16},{16,24},{1,9},{9,17},{17,25},{2,10},{10,18},{18,26},{... | collective-permute-start | bytes 196616 | tf_op jit(solution)/shard_map/ppermute | solution.py:16
  32.1 1.9 %collective-permute-done.9.arrived = bf16[32,1024]{1,0:T(8,128)(2,1)S(1)} collective-permute-done((bf16[32,1024]{1,0:T(8,128)(2,1)S(1)}, bf16[32,1024]{1,0:T(8,128)(2,1)S(1)}, u32[]{:S(2)}, u32[]{:S(2)}) %collective-permute-start.9) | collective-permute-done | bytes 65568 | tf_op jit(solution)/shard_map/ppermute | solution.py:16
  34.0 2.3 %collective-permute-start.10 = (bf16[32,1024]{1,0:T(8,128)(2,1)S(1)}, bf16[32,1024]{1,0:T(8,128)(2,1)S(1)}, u32[]{:S(2)}, u32[]{:S(2)}) collective-permute-start(bf16[32,1024]{1,0:T(8,128)(2,1)S(1)} %arrive.4.refs_0_.first), channel_id=1, source_target_pairs={{0,6},{2,4},{4,2},{6,0},{1,7},{3,5},{5,3},{7,1},{8,14},{10,12},{12... | collective-permute-start | bytes 196616 | tf_op jit(solution)/shard_map/ppermute | solution.py:30
  36.2 1.3 collective-permute-start.12
  37.6 1.4 collective-permute-done.10.refs_1_
  39.0 3.1 %collective-permute-done.11.refs_2_ = bf16[32,1024]{1,0:T(8,128)(2,1)S(1)} collective-permute-done((bf16[32,1024]{1,0:T(8,128)(2,1)S(1)}, bf16[32,1024]{1,0:T(8,128)(2,1)S(1)}, u32[]{:S(2)}, u32[]{:S(2)}) %collective-permute-start.11) | collective-permute-done | bytes 65568 | tf_op jit(solution)/shard_map/ppermute | solution.py:30
  42.8 1.9 %collective-permute-start.13 = (bf16[128,2048]{1,0:T(8,128)(2,1)S(1)}, bf16[128,2048]{1,0:T(8,128)(2,1)S(1)}, u32[]{:S(2)}, u32[]{:S(2)}) collective-permute-start(bf16[128,2048]{1,0:T(8,128)(2,1)S(1)} %up_product.4.mine.pre_mine), channel_id=1, source_target_pairs={{0,1},{1,0},{2,3},{3,2},{4,5},{5,4},{6,7},{7,6},{8,9},{9,8},{10,11... | collective-permute-start | bytes 1572872 | tf_op jit(solution)/shard_map/ppermute | solution.py:21
  44.6 2.1 %collective-permute-start.14 = (bf16[32,1024]{1,0:T(8,128)(2,1)S(1)}, bf16[32,1024]{1,0:T(8,128)(2,1)S(1)}, u32[]{:S(2)}, u32[]{:S(2)}) collective-permute-start(bf16[32,1024]{1,0:T(8,128)(2,1)S(1)} %get-tuple-element.149.refs_0_.first), channel_id=1, source_target_pairs={{0,6},{2,4},{4,2},{6,0},{1,7},{3,5},{5,3},{7,1},{8,14},{10,12},{12... | collective-permute-start | bytes 196616 | tf_op jit(solution)/shard_map/ppermute | solution.py:30
  47.5 2.6 %collective-permute-done.14.refs_1_ = bf16[32,1024]{1,0:T(8,128)(2,1)S(1)} collective-permute-done((bf16[32,1024]{1,0:T(8,128)(2,1)S(1)}, bf16[32,1024]{1,0:T(8,128)(2,1)S(1)}, u32[]{:S(2)}, u32[]{:S(2)}) %collective-permute-start.14) | collective-permute-done | bytes 65568 | tf_op jit(solution)/shard_map/ppermute | solution.py:30
  50.1 2.1 %collective-permute-start.15 = (bf16[32,1024]{1,0:T(8,128)(2,1)S(1)}, bf16[32,1024]{1,0:T(8,128)(2,1)S(1)}, u32[]{:S(2)}, u32[]{:S(2)}) collective-permute-start(bf16[32,1024]{1,0:T(8,128)(2,1)S(1)} %get-tuple-element.151), channel_id=1, source_target_pairs={{0,6},{2,4},{4,2},{6,0},{1,7},{3,5},{5,3},{7,1},{8,14},{10,12},{12... | collective-permute-start | bytes 196616 | tf_op jit(solution)/shard_map/ppermute | solution.py:30
  52.2 1.4 collective-permute-start.17
  53.9 1.2 turned_weight.3.weight
  55.2 3.4 %collective-permute-done.16.refs_2_ = bf16[32,1024]{1,0:T(8,128)(2,1)S(1)} collective-permute-done((bf16[32,1024]{1,0:T(8,128)(2,1)S(1)}, bf16[32,1024]{1,0:T(8,128)(2,1)S(1)}, u32[]{:S(2)}, u32[]{:S(2)}) %collective-permute-start.16) | collective-permute-done | bytes 65568 | tf_op jit(solution)/shard_map/ppermute | solution.py:30
  58.7 4.0 %collective-permute-start.18 = (bf16[32,1024]{1,0:T(8,128)(2,1)S(1)}, bf16[32,1024]{1,0:T(8,128)(2,1)S(1)}, u32[]{:S(2)}, u32[]{:S(2)}) collective-permute-start(bf16[32,1024]{1,0:T(8,128)(2,1)S(1)} %get-tuple-element.162), channel_id=1, source_target_pairs={{0,8},{8,16},{16,24},{1,9},{9,17},{17,25},{2,10},{10,18},{18,26},{... | collective-permute-start | bytes 196616 | tf_op jit(solution)/shard_map/ppermute | solution.py:16
  62.8 1.3 collective-permute-done.18.arrived
  64.1 2.2 %collective-permute-start.20 = (bf16[32,1024]{1,0:T(8,128)(2,1)S(1)}, bf16[32,1024]{1,0:T(8,128)(2,1)S(1)}, u32[]{:S(2)}, u32[]{:S(2)}) collective-permute-start(bf16[32,1024]{1,0:T(8,128)(2,1)S(1)} %arrive.5.refs_0_.first_out), channel_id=1, source_target_pairs={{0,6},{2,4},{4,2},{6,0},{1,7},{3,5},{5,3},{7,1},{8,14},{10,12},{12... | collective-permute-start | bytes 196616 | tf_op jit(solution)/shard_map/ppermute | solution.py:30
  66.2 1.4 collective-permute-start.22
  68.4 2.4 %collective-permute-start.19 = (bf16[128,2048]{1,0:T(8,128)(2,1)S(1)}, bf16[128,2048]{1,0:T(8,128)(2,1)S(1)}, u32[]{:S(2)}, u32[]{:S(2)}) collective-permute-start(bf16[128,2048]{1,0:T(8,128)(2,1)S(1)} %get-tuple-element.166.mine), channel_id=1, source_target_pairs={{0,1},{1,0},{2,3},{3,2},{4,5},{5,4},{6,7},{7,6},{8,9},{9,8},{10,11... | collective-permute-start | bytes 1572872 | tf_op jit(solution)/shard_map/ppermute | solution.py:21
  70.8 2.2 %collective-permute-done.21.refs_2_ = bf16[32,1024]{1,0:T(8,128)(2,1)S(1)} collective-permute-done((bf16[32,1024]{1,0:T(8,128)(2,1)S(1)}, bf16[32,1024]{1,0:T(8,128)(2,1)S(1)}, u32[]{:S(2)}, u32[]{:S(2)}) %collective-permute-start.21) | collective-permute-done | bytes 65568 | tf_op jit(solution)/shard_map/ppermute | solution.py:30
  73.7 1.1 collective-permute-start.23
  74.8 1.5 %collective-permute-done.23.pre_other.other = bf16[128,2048]{1,0:T(8,128)(2,1)S(1)} collective-permute-done((bf16[128,2048]{1,0:T(8,128)(2,1)S(1)}, bf16[128,2048]{1,0:T(8,128)(2,1)S(1)}, u32[]{:S(2)}, u32[]{:S(2)}) %collective-permute-start.23) | collective-permute-done | bytes 524320 | tf_op jit(solution)/shard_map/ppermute | solution.py:21
  76.3 1.0 in_product.3
  77.3 2.1 %collective-permute-start.24 = (bf16[32,1024]{1,0:T(8,128)(2,1)S(1)}, bf16[32,1024]{1,0:T(8,128)(2,1)S(1)}, u32[]{:S(2)}, u32[]{:S(2)}) collective-permute-start(bf16[32,1024]{1,0:T(8,128)(2,1)S(1)} %get-tuple-element.172), channel_id=1, source_target_pairs={{0,6},{2,4},{4,2},{6,0},{1,7},{3,5},{5,3},{7,1},{8,14},{10,12},{12... | collective-permute-start | bytes 196616 | tf_op jit(solution)/shard_map/ppermute | solution.py:30
  79.4 1.5 %collective-permute-start.26 = (bf16[32,1024]{1,0:T(8,128)(2,1)S(1)}, bf16[32,1024]{1,0:T(8,128)(2,1)S(1)}, u32[]{:S(2)}, u32[]{:S(2)}) collective-permute-start(bf16[32,1024]{1,0:T(8,128)(2,1)S(1)} %get-tuple-element.174), channel_id=1, source_target_pairs={{0,2},{2,0},{4,6},{6,4},{1,3},{3,1},{5,7},{7,5},{8,10},{10,8},{12,... | collective-permute-start | bytes 196616 | tf_op jit(solution)/shard_map/ppermute | solution.py:30
  81.2 1.1 collective-permute-done.24.refs_1_
  82.3 3.7 %collective-permute-done.25.refs_2_ = bf16[32,1024]{1,0:T(8,128)(2,1)S(1)} collective-permute-done((bf16[32,1024]{1,0:T(8,128)(2,1)S(1)}, bf16[32,1024]{1,0:T(8,128)(2,1)S(1)}, u32[]{:S(2)}, u32[]{:S(2)}) %collective-permute-start.25) | collective-permute-done | bytes 65568 | tf_op jit(solution)/shard_map/ppermute | solution.py:30
  86.1 2.1 %collective-permute-start.27 = (bf16[32,1024]{1,0:T(8,128)(2,1)S(1)}, bf16[32,1024]{1,0:T(8,128)(2,1)S(1)}, u32[]{:S(2)}, u32[]{:S(2)}) collective-permute-start(bf16[32,1024]{1,0:T(8,128)(2,1)S(1)} %leave_back.2.refs_11_), channel_id=1, source_target_pairs={{8,0},{16,8},{24,16},{9,1},{17,9},{25,17},{10,2},{18,10},{26,18},{... | collective-permute-start | bytes 196616 | tf_op jit(solution)/shard_map/ppermute | solution.py:16
  89.1 3.6 %collective-permute-done.27.arrived = bf16[32,1024]{1,0:T(8,128)(2,1)S(1)} collective-permute-done((bf16[32,1024]{1,0:T(8,128)(2,1)S(1)}, bf16[32,1024]{1,0:T(8,128)(2,1)S(1)}, u32[]{:S(2)}, u32[]{:S(2)}) %collective-permute-start.27) | collective-permute-done | bytes 65568 | tf_op jit(solution)/shard_map/ppermute | solution.py:16
  92.7 2.1 %collective-permute-start.28 = (bf16[32,1024]{1,0:T(8,128)(2,1)S(1)}, bf16[32,1024]{1,0:T(8,128)(2,1)S(1)}, u32[]{:S(2)}, u32[]{:S(2)}) collective-permute-start(bf16[32,1024]{1,0:T(8,128)(2,1)S(1)} %arrive.6.refs_0_.first), channel_id=1, source_target_pairs={{0,6},{2,4},{4,2},{6,0},{1,7},{3,5},{5,3},{7,1},{8,14},{10,12},{12... | collective-permute-start | bytes 196616 | tf_op jit(solution)/shard_map/ppermute | solution.py:30
  94.8 1.5 %collective-permute-start.30 = (bf16[32,1024]{1,0:T(8,128)(2,1)S(1)}, bf16[32,1024]{1,0:T(8,128)(2,1)S(1)}, u32[]{:S(2)}, u32[]{:S(2)}) collective-permute-start(bf16[32,1024]{1,0:T(8,128)(2,1)S(1)} %arrive.6.refs_0_.first), channel_id=1, source_target_pairs={{0,2},{2,0},{4,6},{6,4},{1,3},{3,1},{5,7},{7,5},{8,10},{10,8},{12,... | collective-permute-start | bytes 196616 | tf_op jit(solution)/shard_map/ppermute | solution.py:30
  96.4 1.5 %collective-permute-done.28.refs_1_ = bf16[32,1024]{1,0:T(8,128)(2,1)S(1)} collective-permute-done((bf16[32,1024]{1,0:T(8,128)(2,1)S(1)}, bf16[32,1024]{1,0:T(8,128)(2,1)S(1)}, u32[]{:S(2)}, u32[]{:S(2)}) %collective-permute-start.28) | collective-permute-done | bytes 65568 | tf_op jit(solution)/shard_map/ppermute | solution.py:30
  97.9 3.8 %collective-permute-done.29.refs_2_ = bf16[32,1024]{1,0:T(8,128)(2,1)S(1)} collective-permute-done((bf16[32,1024]{1,0:T(8,128)(2,1)S(1)}, bf16[32,1024]{1,0:T(8,128)(2,1)S(1)}, u32[]{:S(2)}, u32[]{:S(2)}) %collective-permute-start.29) | collective-permute-done | bytes 65568 | tf_op jit(solution)/shard_map/ppermute | solution.py:30
  104.6 1.0 in_product.4
  105.6 3.6 %collective-permute-done.32.refs_2_ = bf16[32,1024]{1,0:T(8,128)(2,1)S(1)} collective-permute-done((bf16[32,1024]{1,0:T(8,128)(2,1)S(1)}, bf16[32,1024]{1,0:T(8,128)(2,1)S(1)}, u32[]{:S(2)}, u32[]{:S(2)}) %collective-permute-start.32) | collective-permute-done | bytes 65568 | tf_op jit(solution)/shard_map/ppermute | solution.py:30
  109.1 2.0 %collective-permute-start.33 = (bf16[32,1024]{1,0:T(8,128)(2,1)S(1)}, bf16[32,1024]{1,0:T(8,128)(2,1)S(1)}, u32[]{:S(2)}, u32[]{:S(2)}) collective-permute-start(bf16[32,1024]{1,0:T(8,128)(2,1)S(1)} %get-tuple-element.196), channel_id=1, source_target_pairs={{0,6},{2,4},{4,2},{6,0},{1,7},{3,5},{5,3},{7,1},{8,14},{10,12},{12... | collective-permute-start | bytes 196616 | tf_op jit(solution)/shard_map/ppermute | solution.py:30
  111.1 1.5 %collective-permute-start.35 = (bf16[32,1024]{1,0:T(8,128)(2,1)S(1)}, bf16[32,1024]{1,0:T(8,128)(2,1)S(1)}, u32[]{:S(2)}, u32[]{:S(2)}) collective-permute-start(bf16[32,1024]{1,0:T(8,128)(2,1)S(1)} %get-tuple-element.198), channel_id=1, source_target_pairs={{0,2},{2,0},{4,6},{6,4},{1,3},{3,1},{5,7},{7,5},{8,10},{10,8},{12,... | collective-permute-start | bytes 196616 | tf_op jit(solution)/shard_map/ppermute | solution.py:30
  113.0 1.1 collective-permute-done.33.refs_1_
  114.1 3.7 %collective-permute-done.34.refs_2_ = bf16[32,1024]{1,0:T(8,128)(2,1)S(1)} collective-permute-done((bf16[32,1024]{1,0:T(8,128)(2,1)S(1)}, bf16[32,1024]{1,0:T(8,128)(2,1)S(1)}, u32[]{:S(2)}, u32[]{:S(2)}) %collective-permute-start.34) | collective-permute-done | bytes 65568 | tf_op jit(solution)/shard_map/ppermute | solution.py:30
  117.8 1.9 %collective-permute-start.36 = (bf16[32,1024]{1,0:T(8,128)(2,1)S(1)}, bf16[32,1024]{1,0:T(8,128)(2,1)S(1)}, u32[]{:S(2)}, u32[]{:S(2)}) collective-permute-start(bf16[32,1024]{1,0:T(8,128)(2,1)S(1)} %leave_back.3.refs_10_), channel_id=1, source_target_pairs={{8,0},{16,8},{24,16},{9,1},{17,9},{25,17},{10,2},{18,10},{26,18},{... | collective-permute-start | bytes 196616 | tf_op jit(solution)/shard_map/ppermute | solution.py:16
  119.7 4.0 %collective-permute-done.36.arrived = bf16[32,1024]{1,0:T(8,128)(2,1)S(1)} collective-permute-done((bf16[32,1024]{1,0:T(8,128)(2,1)S(1)}, bf16[32,1024]{1,0:T(8,128)(2,1)S(1)}, u32[]{:S(2)}, u32[]{:S(2)}) %collective-permute-start.36) | collective-permute-done | bytes 65568 | tf_op jit(solution)/shard_map/ppermute | solution.py:16
  123.7 2.1 %collective-permute-start.37 = (bf16[32,1024]{1,0:T(8,128)(2,1)S(1)}, bf16[32,1024]{1,0:T(8,128)(2,1)S(1)}, u32[]{:S(2)}, u32[]{:S(2)}) collective-permute-start(bf16[32,1024]{1,0:T(8,128)(2,1)S(1)} %arrive.7.refs_0_.first_grad), channel_id=1, source_target_pairs={{0,6},{2,4},{4,2},{6,0},{1,7},{3,5},{5,3},{7,1},{8,14},{10,12},{12... | collective-permute-start | bytes 196616 | tf_op jit(solution)/shard_map/ppermute | solution.py:30
  125.8 1.5 %collective-permute-start.39 = (bf16[32,1024]{1,0:T(8,128)(2,1)S(1)}, bf16[32,1024]{1,0:T(8,128)(2,1)S(1)}, u32[]{:S(2)}, u32[]{:S(2)}) collective-permute-start(bf16[32,1024]{1,0:T(8,128)(2,1)S(1)} %arrive.7.refs_0_.first_grad), channel_id=1, source_target_pairs={{0,2},{2,0},{4,6},{6,4},{1,3},{3,1},{5,7},{7,5},{8,10},{10,8},{12,... | collective-permute-start | bytes 196616 | tf_op jit(solution)/shard_map/ppermute | solution.py:30
  127.3 1.5 collective-permute-done.37.refs_1_
  128.8 3.8 %collective-permute-done.38.refs_2_ = bf16[32,1024]{1,0:T(8,128)(2,1)S(1)} collective-permute-done((bf16[32,1024]{1,0:T(8,128)(2,1)S(1)}, bf16[32,1024]{1,0:T(8,128)(2,1)S(1)}, u32[]{:S(2)}, u32[]{:S(2)}) %collective-permute-start.38) | collective-permute-done | bytes 65568 | tf_op jit(solution)/shard_map/ppermute | solution.py:30
  133.3 1.1 collective-permute-start.41
  134.4 1.7 %collective-permute-start.40 = (bf16[32,1024]{1,0:T(8,128)(2,1)S(1)}, bf16[32,1024]{1,0:T(8,128)(2,1)S(1)}, u32[]{:S(2)}, u32[]{:S(2)}) collective-permute-start(bf16[32,1024]{1,0:T(8,128)(2,1)S(1)} %get-tuple-element.206), channel_id=1, source_target_pairs={{0,6},{2,4},{4,2},{6,0},{1,7},{3,5},{5,3},{7,1},{8,14},{10,12},{12... | collective-permute-start | bytes 196616 | tf_op jit(solution)/shard_map/ppermute | solution.py:30
  136.8 1.0 in_product.5
  137.9 2.0 %collective-permute-done.40.refs_1_ = bf16[32,1024]{1,0:T(8,128)(2,1)S(1)} collective-permute-done((bf16[32,1024]{1,0:T(8,128)(2,1)S(1)}, bf16[32,1024]{1,0:T(8,128)(2,1)S(1)}, u32[]{:S(2)}, u32[]{:S(2)}) %collective-permute-start.40) | collective-permute-done | bytes 65568 | tf_op jit(solution)/shard_map/ppermute | solution.py:30
  139.9 1.7 %collective-permute-start.43 = (bf16[32,1024]{1,0:T(8,128)(2,1)S(1)}, bf16[32,1024]{1,0:T(8,128)(2,1)S(1)}, u32[]{:S(2)}, u32[]{:S(2)}) collective-permute-start(bf16[32,1024]{1,0:T(8,128)(2,1)S(1)} %get-tuple-element.212), channel_id=1, source_target_pairs={{0,6},{2,4},{4,2},{6,0},{1,7},{3,5},{5,3},{7,1},{8,14},{10,12},{12... | collective-permute-start | bytes 196616 | tf_op jit(solution)/shard_map/ppermute | solution.py:30
  141.6 1.8 %collective-permute-start.45 = (bf16[32,1024]{1,0:T(8,128)(2,1)S(1)}, bf16[32,1024]{1,0:T(8,128)(2,1)S(1)}, u32[]{:S(2)}, u32[]{:S(2)}) collective-permute-start(bf16[32,1024]{1,0:T(8,128)(2,1)S(1)} %get-tuple-element.214), channel_id=1, source_target_pairs={{0,2},{2,0},{4,6},{6,4},{1,3},{3,1},{5,7},{7,5},{8,10},{10,8},{12,... | collective-permute-start | bytes 196616 | tf_op jit(solution)/shard_map/ppermute | solution.py:30
  143.5 3.2 %weight_grad.3 = bf16[2048,1024]{1,0:T(8,128)(2,1)} custom-call(bf16[2048,128]{1,0:T(8,128)(2,1)S(1)} %turned.7.refs_0_, bf16[2048,128]{1,0:T(8,128)(2,1)S(1)} %turned.9.refs_1_, bf16[2048,128]{1,0:T(8,128)(2,1)S(1)} %turned.11.refs_2_, bf16[128,1024]{1,0:T(8,128)(2,1)S(1)} %get-tuple-element.225.refs_3_, bf16[128,1024]{1,0:T(8,128)(2,1)S(1)} %get-tuple-element.226.refs_4_, ...), custom_call_target="tpu_custom_call" | custom-call | flops 1610612736 | bytes 4194304 | tf_op jit(solution)/shard_map/weight_grad/pallas_call | solution.py:260
  146.7 3.4 %weight_grad.2 = bf16[1024,2048]{1,0:T(8,128)(2,1)} custom-call(bf16[1024,128]{1,0:T(8,128)(2,1)S(1)} %turned.6.refs_0_, bf16[1024,128]{1,0:T(8,128)(2,1)S(1)} %turned.8.refs_1_, bf16[1024,128]{1,0:T(8,128)(2,1)S(1)} %turned.10.refs_2_, bf16[128,2048]{1,0:T(8,128)(2,1)S(1)} %get-tuple-element.219.refs_3_, bf16[128,2048]{1,0:T(8,128)(2,1)S(1)} %get-tuple-element.220.refs_4_, ...), custom_call_target="tpu_custom_call" | custom-call | flops 1610612736 | bytes 4194304 | tf_op jit(solution)/shard_map/weight_grad/pallas_call | solution.py:260
  (65 shorter events, 13.6 us)
Async XLA Ops:
  1.5 9.9 %collective-permute-start.3 = (bf16[32,1024]{1,0:T(8,128)(2,1)S(1)}, bf16[32,1024]{1,0:T(8,128)(2,1)S(1)}, u32[]{:S(2)}, u32[]{:S(2)}) collective-permute-start(bf16[32,1024]{1,0:T(8,128)(2,1)S(1)} %get-tuple-element.149.refs_0_.first), channel_id=1, source_target_pairs={{0,2},{2,0},{4,6},{6,4},{1,3},{3,1},{5,7},{7,5},{8,10},{10,8},{12,... | collective-permute-start | bytes 196616 | tf_op jit(solution)/shard_map/ppermute | solution.py:30
  2.9 8.5 %collective-permute-start = (bf16[32,1024]{1,0:T(8,128)(2,1)S(1)}, bf16[32,1024]{1,0:T(8,128)(2,1)S(1)}, u32[]{:S(2)}, u32[]{:S(2)}) collective-permute-start(bf16[32,1024]{1,0:T(8,128)(2,1)S(1)} %get-tuple-element.155.refs_0_.first), channel_id=1, source_target_pairs={{0,6},{2,4},{4,2},{6,0},{1,7},{3,5},{5,3},{7,1},{8,14},{10,12},{12... | collective-permute-start | bytes 196616 | tf_op jit(solution)/shard_map/ppermute | solution.py:30
  5.1 7.2 %collective-permute-start.1 = (bf16[32,1024]{1,0:T(8,128)(2,1)S(1)}, bf16[32,1024]{1,0:T(8,128)(2,1)S(1)}, u32[]{:S(2)}, u32[]{:S(2)}) collective-permute-start(bf16[32,1024]{1,0:T(8,128)(2,1)S(1)} %get-tuple-element.155.refs_0_.first), channel_id=1, source_target_pairs={{0,4},{2,6},{4,0},{6,2},{1,5},{3,7},{5,1},{7,3},{8,12},{10,14},{12... | collective-permute-start | bytes 196616 | tf_op jit(solution)/shard_map/ppermute | solution.py:30
  5.2 7.0 %collective-permute-start.2 = (bf16[32,1024]{1,0:T(8,128)(2,1)S(1)}, bf16[32,1024]{1,0:T(8,128)(2,1)S(1)}, u32[]{:S(2)}, u32[]{:S(2)}) collective-permute-start(bf16[32,1024]{1,0:T(8,128)(2,1)S(1)} %get-tuple-element.155.refs_0_.first), channel_id=1, source_target_pairs={{0,2},{2,0},{4,6},{6,4},{1,3},{3,1},{5,7},{7,5},{8,10},{10,8},{12,... | collective-permute-start | bytes 196616 | tf_op jit(solution)/shard_map/ppermute | solution.py:30
  6.4 0.7 copy-start
  13.0 2.6 %collective-permute-start.4 = (bf16[128,2048]{1,0:T(8,128)(2,1)S(1)}, bf16[128,2048]{1,0:T(8,128)(2,1)S(1)}, u32[]{:S(2)}, u32[]{:S(2)}) collective-permute-start(bf16[128,2048]{1,0:T(8,128)(2,1)S(1)} %up_product.3.mine.pre_mine), channel_id=1, source_target_pairs={{0,1},{1,0},{2,3},{3,2},{4,5},{5,4},{6,7},{7,6},{8,9},{9,8},{10,11... | collective-permute-start | bytes 1572872 | tf_op jit(solution)/shard_map/ppermute | solution.py:21
  14.0 6.2 %collective-permute-start.5 = (bf16[32,1024]{1,0:T(8,128)(2,1)S(1)}, bf16[32,1024]{1,0:T(8,128)(2,1)S(1)}, u32[]{:S(2)}, u32[]{:S(2)}) collective-permute-start(bf16[32,1024]{1,0:T(8,128)(2,1)S(1)} %get-tuple-element.149.refs_0_.first), channel_id=1, source_target_pairs={{0,4},{2,6},{4,0},{6,2},{1,5},{3,7},{5,1},{7,3},{8,12},{10,14},{12... | collective-permute-start | bytes 196616 | tf_op jit(solution)/shard_map/ppermute | solution.py:30
  20.2 4.9 %collective-permute-start.6 = (bf16[32,1024]{1,0:T(8,128)(2,1)S(1)}, bf16[32,1024]{1,0:T(8,128)(2,1)S(1)}, u32[]{:S(2)}, u32[]{:S(2)}) collective-permute-start(bf16[32,1024]{1,0:T(8,128)(2,1)S(1)} %get-tuple-element.138), channel_id=1, source_target_pairs={{0,6},{2,4},{4,2},{6,0},{1,7},{3,5},{5,3},{7,1},{8,14},{10,12},{12... | collective-permute-start | bytes 196616 | tf_op jit(solution)/shard_map/ppermute | solution.py:30
  22.4 6.4 %collective-permute-start.7 = (bf16[32,1024]{1,0:T(8,128)(2,1)S(1)}, bf16[32,1024]{1,0:T(8,128)(2,1)S(1)}, u32[]{:S(2)}, u32[]{:S(2)}) collective-permute-start(bf16[32,1024]{1,0:T(8,128)(2,1)S(1)} %get-tuple-element.139), channel_id=1, source_target_pairs={{0,4},{2,6},{4,0},{6,2},{1,5},{3,7},{5,1},{7,3},{8,12},{10,14},{12... | collective-permute-start | bytes 196616 | tf_op jit(solution)/shard_map/ppermute | solution.py:30
  22.5 6.4 %collective-permute-start.8 = (bf16[32,1024]{1,0:T(8,128)(2,1)S(1)}, bf16[32,1024]{1,0:T(8,128)(2,1)S(1)}, u32[]{:S(2)}, u32[]{:S(2)}) collective-permute-start(bf16[32,1024]{1,0:T(8,128)(2,1)S(1)} %get-tuple-element.140), channel_id=1, source_target_pairs={{0,2},{2,0},{4,6},{6,4},{1,3},{3,1},{5,7},{7,5},{8,10},{10,8},{12,... | collective-permute-start | bytes 196616 | tf_op jit(solution)/shard_map/ppermute | solution.py:30
  28.9 5.0 %collective-permute-start.9 = (bf16[32,1024]{1,0:T(8,128)(2,1)S(1)}, bf16[32,1024]{1,0:T(8,128)(2,1)S(1)}, u32[]{:S(2)}, u32[]{:S(2)}) collective-permute-start(bf16[32,1024]{1,0:T(8,128)(2,1)S(1)} %get-tuple-element.143), channel_id=1, source_target_pairs={{0,8},{8,16},{16,24},{1,9},{9,17},{17,25},{2,10},{10,18},{18,26},{... | collective-permute-start | bytes 196616 | tf_op jit(solution)/shard_map/ppermute | solution.py:16
  34.0 5.0 %collective-permute-start.10 = (bf16[32,1024]{1,0:T(8,128)(2,1)S(1)}, bf16[32,1024]{1,0:T(8,128)(2,1)S(1)}, u32[]{:S(2)}, u32[]{:S(2)}) collective-permute-start(bf16[32,1024]{1,0:T(8,128)(2,1)S(1)} %arrive.4.refs_0_.first), channel_id=1, source_target_pairs={{0,6},{2,4},{4,2},{6,0},{1,7},{3,5},{5,3},{7,1},{8,14},{10,12},{12... | collective-permute-start | bytes 196616 | tf_op jit(solution)/shard_map/ppermute | solution.py:30
  36.2 5.8 %collective-permute-start.11 = (bf16[32,1024]{1,0:T(8,128)(2,1)S(1)}, bf16[32,1024]{1,0:T(8,128)(2,1)S(1)}, u32[]{:S(2)}, u32[]{:S(2)}) collective-permute-start(bf16[32,1024]{1,0:T(8,128)(2,1)S(1)} %arrive.4.refs_0_.first), channel_id=1, source_target_pairs={{0,4},{2,6},{4,0},{6,2},{1,5},{3,7},{5,1},{7,3},{8,12},{10,14},{12... | collective-permute-start | bytes 196616 | tf_op jit(solution)/shard_map/ppermute | solution.py:30
  36.2 5.8 %collective-permute-start.12 = (bf16[32,1024]{1,0:T(8,128)(2,1)S(1)}, bf16[32,1024]{1,0:T(8,128)(2,1)S(1)}, u32[]{:S(2)}, u32[]{:S(2)}) collective-permute-start(bf16[32,1024]{1,0:T(8,128)(2,1)S(1)} %arrive.4.refs_0_.first), channel_id=1, source_target_pairs={{0,2},{2,0},{4,6},{6,4},{1,3},{3,1},{5,7},{7,5},{8,10},{10,8},{12,... | collective-permute-start | bytes 196616 | tf_op jit(solution)/shard_map/ppermute | solution.py:30
  42.8 4.0 %collective-permute-start.13 = (bf16[128,2048]{1,0:T(8,128)(2,1)S(1)}, bf16[128,2048]{1,0:T(8,128)(2,1)S(1)}, u32[]{:S(2)}, u32[]{:S(2)}) collective-permute-start(bf16[128,2048]{1,0:T(8,128)(2,1)S(1)} %up_product.4.mine.pre_mine), channel_id=1, source_target_pairs={{0,1},{1,0},{2,3},{3,2},{4,5},{5,4},{6,7},{7,6},{8,9},{9,8},{10,11... | collective-permute-start | bytes 1572872 | tf_op jit(solution)/shard_map/ppermute | solution.py:21
  44.6 5.5 %collective-permute-start.14 = (bf16[32,1024]{1,0:T(8,128)(2,1)S(1)}, bf16[32,1024]{1,0:T(8,128)(2,1)S(1)}, u32[]{:S(2)}, u32[]{:S(2)}) collective-permute-start(bf16[32,1024]{1,0:T(8,128)(2,1)S(1)} %get-tuple-element.149.refs_0_.first), channel_id=1, source_target_pairs={{0,6},{2,4},{4,2},{6,0},{1,7},{3,5},{5,3},{7,1},{8,14},{10,12},{12... | collective-permute-start | bytes 196616 | tf_op jit(solution)/shard_map/ppermute | solution.py:30
  50.1 5.1 %collective-permute-start.15 = (bf16[32,1024]{1,0:T(8,128)(2,1)S(1)}, bf16[32,1024]{1,0:T(8,128)(2,1)S(1)}, u32[]{:S(2)}, u32[]{:S(2)}) collective-permute-start(bf16[32,1024]{1,0:T(8,128)(2,1)S(1)} %get-tuple-element.151), channel_id=1, source_target_pairs={{0,6},{2,4},{4,2},{6,0},{1,7},{3,5},{5,3},{7,1},{8,14},{10,12},{12... | collective-permute-start | bytes 196616 | tf_op jit(solution)/shard_map/ppermute | solution.py:30
  52.2 6.4 %collective-permute-start.16 = (bf16[32,1024]{1,0:T(8,128)(2,1)S(1)}, bf16[32,1024]{1,0:T(8,128)(2,1)S(1)}, u32[]{:S(2)}, u32[]{:S(2)}) collective-permute-start(bf16[32,1024]{1,0:T(8,128)(2,1)S(1)} %get-tuple-element.152), channel_id=1, source_target_pairs={{0,4},{2,6},{4,0},{6,2},{1,5},{3,7},{5,1},{7,3},{8,12},{10,14},{12... | collective-permute-start | bytes 196616 | tf_op jit(solution)/shard_map/ppermute | solution.py:30
  52.2 6.4 %collective-permute-start.17 = (bf16[32,1024]{1,0:T(8,128)(2,1)S(1)}, bf16[32,1024]{1,0:T(8,128)(2,1)S(1)}, u32[]{:S(2)}, u32[]{:S(2)}) collective-permute-start(bf16[32,1024]{1,0:T(8,128)(2,1)S(1)} %get-tuple-element.153), channel_id=1, source_target_pairs={{0,2},{2,0},{4,6},{6,4},{1,3},{3,1},{5,7},{7,5},{8,10},{10,8},{12,... | collective-permute-start | bytes 196616 | tf_op jit(solution)/shard_map/ppermute | solution.py:30
  58.7 5.4 %collective-permute-start.18 = (bf16[32,1024]{1,0:T(8,128)(2,1)S(1)}, bf16[32,1024]{1,0:T(8,128)(2,1)S(1)}, u32[]{:S(2)}, u32[]{:S(2)}) collective-permute-start(bf16[32,1024]{1,0:T(8,128)(2,1)S(1)} %get-tuple-element.162), channel_id=1, source_target_pairs={{0,8},{8,16},{16,24},{1,9},{9,17},{17,25},{2,10},{10,18},{18,26},{... | collective-permute-start | bytes 196616 | tf_op jit(solution)/shard_map/ppermute | solution.py:16
  64.1 6.7 %collective-permute-start.20 = (bf16[32,1024]{1,0:T(8,128)(2,1)S(1)}, bf16[32,1024]{1,0:T(8,128)(2,1)S(1)}, u32[]{:S(2)}, u32[]{:S(2)}) collective-permute-start(bf16[32,1024]{1,0:T(8,128)(2,1)S(1)} %arrive.5.refs_0_.first_out), channel_id=1, source_target_pairs={{0,6},{2,4},{4,2},{6,0},{1,7},{3,5},{5,3},{7,1},{8,14},{10,12},{12... | collective-permute-start | bytes 196616 | tf_op jit(solution)/shard_map/ppermute | solution.py:30
  66.2 6.7 %collective-permute-start.21 = (bf16[32,1024]{1,0:T(8,128)(2,1)S(1)}, bf16[32,1024]{1,0:T(8,128)(2,1)S(1)}, u32[]{:S(2)}, u32[]{:S(2)}) collective-permute-start(bf16[32,1024]{1,0:T(8,128)(2,1)S(1)} %arrive.5.refs_0_.first_out), channel_id=1, source_target_pairs={{0,4},{2,6},{4,0},{6,2},{1,5},{3,7},{5,1},{7,3},{8,12},{10,14},{12... | collective-permute-start | bytes 196616 | tf_op jit(solution)/shard_map/ppermute | solution.py:30
  66.2 6.7 %collective-permute-start.22 = (bf16[32,1024]{1,0:T(8,128)(2,1)S(1)}, bf16[32,1024]{1,0:T(8,128)(2,1)S(1)}, u32[]{:S(2)}, u32[]{:S(2)}) collective-permute-start(bf16[32,1024]{1,0:T(8,128)(2,1)S(1)} %arrive.5.refs_0_.first_out), channel_id=1, source_target_pairs={{0,2},{2,0},{4,6},{6,4},{1,3},{3,1},{5,7},{7,5},{8,10},{10,8},{12,... | collective-permute-start | bytes 196616 | tf_op jit(solution)/shard_map/ppermute | solution.py:30
  68.4 6.3 %collective-permute-start.19 = (bf16[128,2048]{1,0:T(8,128)(2,1)S(1)}, bf16[128,2048]{1,0:T(8,128)(2,1)S(1)}, u32[]{:S(2)}, u32[]{:S(2)}) collective-permute-start(bf16[128,2048]{1,0:T(8,128)(2,1)S(1)} %get-tuple-element.166.mine), channel_id=1, source_target_pairs={{0,1},{1,0},{2,3},{3,2},{4,5},{5,4},{6,7},{7,6},{8,9},{9,8},{10,11... | collective-permute-start | bytes 1572872 | tf_op jit(solution)/shard_map/ppermute | solution.py:21
  73.7 2.6 %collective-permute-start.23 = (bf16[128,2048]{1,0:T(8,128)(2,1)S(1)}, bf16[128,2048]{1,0:T(8,128)(2,1)S(1)}, u32[]{:S(2)}, u32[]{:S(2)}) collective-permute-start(bf16[128,2048]{1,0:T(8,128)(2,1)S(1)} %up_product.5.pre_mine.mine), channel_id=1, source_target_pairs={{0,1},{1,0},{2,3},{3,2},{4,5},{5,4},{6,7},{7,6},{8,9},{9,8},{10,11... | collective-permute-start | bytes 1572872 | tf_op jit(solution)/shard_map/ppermute | solution.py:21
  77.3 5.0 %collective-permute-start.24 = (bf16[32,1024]{1,0:T(8,128)(2,1)S(1)}, bf16[32,1024]{1,0:T(8,128)(2,1)S(1)}, u32[]{:S(2)}, u32[]{:S(2)}) collective-permute-start(bf16[32,1024]{1,0:T(8,128)(2,1)S(1)} %get-tuple-element.172), channel_id=1, source_target_pairs={{0,6},{2,4},{4,2},{6,0},{1,7},{3,5},{5,3},{7,1},{8,14},{10,12},{12... | collective-permute-start | bytes 196616 | tf_op jit(solution)/shard_map/ppermute | solution.py:30
  79.4 6.6 %collective-permute-start.25 = (bf16[32,1024]{1,0:T(8,128)(2,1)S(1)}, bf16[32,1024]{1,0:T(8,128)(2,1)S(1)}, u32[]{:S(2)}, u32[]{:S(2)}) collective-permute-start(bf16[32,1024]{1,0:T(8,128)(2,1)S(1)} %get-tuple-element.173), channel_id=1, source_target_pairs={{0,4},{2,6},{4,0},{6,2},{1,5},{3,7},{5,1},{7,3},{8,12},{10,14},{12... | collective-permute-start | bytes 196616 | tf_op jit(solution)/shard_map/ppermute | solution.py:30
  79.4 6.6 %collective-permute-start.26 = (bf16[32,1024]{1,0:T(8,128)(2,1)S(1)}, bf16[32,1024]{1,0:T(8,128)(2,1)S(1)}, u32[]{:S(2)}, u32[]{:S(2)}) collective-permute-start(bf16[32,1024]{1,0:T(8,128)(2,1)S(1)} %get-tuple-element.174), channel_id=1, source_target_pairs={{0,2},{2,0},{4,6},{6,4},{1,3},{3,1},{5,7},{7,5},{8,10},{10,8},{12,... | collective-permute-start | bytes 196616 | tf_op jit(solution)/shard_map/ppermute | solution.py:30
  86.1 6.7 %collective-permute-start.27 = (bf16[32,1024]{1,0:T(8,128)(2,1)S(1)}, bf16[32,1024]{1,0:T(8,128)(2,1)S(1)}, u32[]{:S(2)}, u32[]{:S(2)}) collective-permute-start(bf16[32,1024]{1,0:T(8,128)(2,1)S(1)} %leave_back.2.refs_11_), channel_id=1, source_target_pairs={{8,0},{16,8},{24,16},{9,1},{17,9},{25,17},{10,2},{18,10},{26,18},{... | collective-permute-start | bytes 196616 | tf_op jit(solution)/shard_map/ppermute | solution.py:16
  92.7 5.1 %collective-permute-start.28 = (bf16[32,1024]{1,0:T(8,128)(2,1)S(1)}, bf16[32,1024]{1,0:T(8,128)(2,1)S(1)}, u32[]{:S(2)}, u32[]{:S(2)}) collective-permute-start(bf16[32,1024]{1,0:T(8,128)(2,1)S(1)} %arrive.6.refs_0_.first), channel_id=1, source_target_pairs={{0,6},{2,4},{4,2},{6,0},{1,7},{3,5},{5,3},{7,1},{8,14},{10,12},{12... | collective-permute-start | bytes 196616 | tf_op jit(solution)/shard_map/ppermute | solution.py:30
  94.8 6.9 %collective-permute-start.29 = (bf16[32,1024]{1,0:T(8,128)(2,1)S(1)}, bf16[32,1024]{1,0:T(8,128)(2,1)S(1)}, u32[]{:S(2)}, u32[]{:S(2)}) collective-permute-start(bf16[32,1024]{1,0:T(8,128)(2,1)S(1)} %arrive.6.refs_0_.first), channel_id=1, source_target_pairs={{0,4},{2,6},{4,0},{6,2},{1,5},{3,7},{5,1},{7,3},{8,12},{10,14},{12... | collective-permute-start | bytes 196616 | tf_op jit(solution)/shard_map/ppermute | solution.py:30
  94.8 6.9 %collective-permute-start.30 = (bf16[32,1024]{1,0:T(8,128)(2,1)S(1)}, bf16[32,1024]{1,0:T(8,128)(2,1)S(1)}, u32[]{:S(2)}, u32[]{:S(2)}) collective-permute-start(bf16[32,1024]{1,0:T(8,128)(2,1)S(1)} %arrive.6.refs_0_.first), channel_id=1, source_target_pairs={{0,2},{2,0},{4,6},{6,4},{1,3},{3,1},{5,7},{7,5},{8,10},{10,8},{12,... | collective-permute-start | bytes 196616 | tf_op jit(solution)/shard_map/ppermute | solution.py:30
  102.4 2.1 %collective-permute-start.31 = (bf16[128,2048]{1,0:T(8,128)(2,1)S(1)}, bf16[128,2048]{1,0:T(8,128)(2,1)S(1)}, u32[]{:S(2)}, u32[]{:S(2)}) collective-permute-start(bf16[128,2048]{1,0:T(8,128)(2,1)S(1)} %get-tuple-element.189.mine), channel_id=1, source_target_pairs={{0,1},{1,0},{2,3},{3,2},{4,5},{5,4},{6,7},{7,6},{8,9},{9,8},{10,11... | collective-permute-start | bytes 1572872 | tf_op jit(solution)/shard_map/ppermute | solution.py:21
  103.0 6.1 %collective-permute-start.32 = (bf16[32,1024]{1,0:T(8,128)(2,1)S(1)}, bf16[32,1024]{1,0:T(8,128)(2,1)S(1)}, u32[]{:S(2)}, u32[]{:S(2)}) collective-permute-start(bf16[32,1024]{1,0:T(8,128)(2,1)S(1)} %get-tuple-element.194), channel_id=1, source_target_pairs={{0,4},{2,6},{4,0},{6,2},{1,5},{3,7},{5,1},{7,3},{8,12},{10,14},{12... | collective-permute-start | bytes 196616 | tf_op jit(solution)/shard_map/ppermute | solution.py:30
  109.1 5.0 %collective-permute-start.33 = (bf16[32,1024]{1,0:T(8,128)(2,1)S(1)}, bf16[32,1024]{1,0:T(8,128)(2,1)S(1)}, u32[]{:S(2)}, u32[]{:S(2)}) collective-permute-start(bf16[32,1024]{1,0:T(8,128)(2,1)S(1)} %get-tuple-element.196), channel_id=1, source_target_pairs={{0,6},{2,4},{4,2},{6,0},{1,7},{3,5},{5,3},{7,1},{8,14},{10,12},{12... | collective-permute-start | bytes 196616 | tf_op jit(solution)/shard_map/ppermute | solution.py:30
  111.1 6.6 %collective-permute-start.34 = (bf16[32,1024]{1,0:T(8,128)(2,1)S(1)}, bf16[32,1024]{1,0:T(8,128)(2,1)S(1)}, u32[]{:S(2)}, u32[]{:S(2)}) collective-permute-start(bf16[32,1024]{1,0:T(8,128)(2,1)S(1)} %get-tuple-element.197), channel_id=1, source_target_pairs={{0,4},{2,6},{4,0},{6,2},{1,5},{3,7},{5,1},{7,3},{8,12},{10,14},{12... | collective-permute-start | bytes 196616 | tf_op jit(solution)/shard_map/ppermute | solution.py:30
  111.1 6.6 %collective-permute-start.35 = (bf16[32,1024]{1,0:T(8,128)(2,1)S(1)}, bf16[32,1024]{1,0:T(8,128)(2,1)S(1)}, u32[]{:S(2)}, u32[]{:S(2)}) collective-permute-start(bf16[32,1024]{1,0:T(8,128)(2,1)S(1)} %get-tuple-element.198), channel_id=1, source_target_pairs={{0,2},{2,0},{4,6},{6,4},{1,3},{3,1},{5,7},{7,5},{8,10},{10,8},{12,... | collective-permute-start | bytes 196616 | tf_op jit(solution)/shard_map/ppermute | solution.py:30
  117.8 5.9 %collective-permute-start.36 = (bf16[32,1024]{1,0:T(8,128)(2,1)S(1)}, bf16[32,1024]{1,0:T(8,128)(2,1)S(1)}, u32[]{:S(2)}, u32[]{:S(2)}) collective-permute-start(bf16[32,1024]{1,0:T(8,128)(2,1)S(1)} %leave_back.3.refs_10_), channel_id=1, source_target_pairs={{8,0},{16,8},{24,16},{9,1},{17,9},{25,17},{10,2},{18,10},{26,18},{... | collective-permute-start | bytes 196616 | tf_op jit(solution)/shard_map/ppermute | solution.py:16
  123.7 5.1 %collective-permute-start.37 = (bf16[32,1024]{1,0:T(8,128)(2,1)S(1)}, bf16[32,1024]{1,0:T(8,128)(2,1)S(1)}, u32[]{:S(2)}, u32[]{:S(2)}) collective-permute-start(bf16[32,1024]{1,0:T(8,128)(2,1)S(1)} %arrive.7.refs_0_.first_grad), channel_id=1, source_target_pairs={{0,6},{2,4},{4,2},{6,0},{1,7},{3,5},{5,3},{7,1},{8,14},{10,12},{12... | collective-permute-start | bytes 196616 | tf_op jit(solution)/shard_map/ppermute | solution.py:30
  125.8 6.8 %collective-permute-start.38 = (bf16[32,1024]{1,0:T(8,128)(2,1)S(1)}, bf16[32,1024]{1,0:T(8,128)(2,1)S(1)}, u32[]{:S(2)}, u32[]{:S(2)}) collective-permute-start(bf16[32,1024]{1,0:T(8,128)(2,1)S(1)} %arrive.7.refs_0_.first_grad), channel_id=1, source_target_pairs={{0,4},{2,6},{4,0},{6,2},{1,5},{3,7},{5,1},{7,3},{8,12},{10,14},{12... | collective-permute-start | bytes 196616 | tf_op jit(solution)/shard_map/ppermute | solution.py:30
  125.8 6.8 %collective-permute-start.39 = (bf16[32,1024]{1,0:T(8,128)(2,1)S(1)}, bf16[32,1024]{1,0:T(8,128)(2,1)S(1)}, u32[]{:S(2)}, u32[]{:S(2)}) collective-permute-start(bf16[32,1024]{1,0:T(8,128)(2,1)S(1)} %arrive.7.refs_0_.first_grad), channel_id=1, source_target_pairs={{0,2},{2,0},{4,6},{6,4},{1,3},{3,1},{5,7},{7,5},{8,10},{10,8},{12,... | collective-permute-start | bytes 196616 | tf_op jit(solution)/shard_map/ppermute | solution.py:30
  133.3 3.5 %collective-permute-start.41 = (bf16[128,2048]{1,0:T(8,128)(2,1)S(1)}, bf16[128,2048]{1,0:T(8,128)(2,1)S(1)}, u32[]{:S(2)}, u32[]{:S(2)}) collective-permute-start(bf16[128,2048]{1,0:T(8,128)(2,1)S(1)} %get-tuple-element.205.mine), channel_id=1, source_target_pairs={{0,1},{1,0},{2,3},{3,2},{4,5},{5,4},{6,7},{7,6},{8,9},{9,8},{10,11... | collective-permute-start | bytes 1572872 | tf_op jit(solution)/shard_map/ppermute | solution.py:21
  134.4 5.5 %collective-permute-start.40 = (bf16[32,1024]{1,0:T(8,128)(2,1)S(1)}, bf16[32,1024]{1,0:T(8,128)(2,1)S(1)}, u32[]{:S(2)}, u32[]{:S(2)}) collective-permute-start(bf16[32,1024]{1,0:T(8,128)(2,1)S(1)} %get-tuple-element.206), channel_id=1, source_target_pairs={{0,6},{2,4},{4,2},{6,0},{1,7},{3,5},{5,3},{7,1},{8,14},{10,12},{12... | collective-permute-start | bytes 196616 | tf_op jit(solution)/shard_map/ppermute | solution.py:30
  139.9 10.2 %collective-permute-start.43 = (bf16[32,1024]{1,0:T(8,128)(2,1)S(1)}, bf16[32,1024]{1,0:T(8,128)(2,1)S(1)}, u32[]{:S(2)}, u32[]{:S(2)}) collective-permute-start(bf16[32,1024]{1,0:T(8,128)(2,1)S(1)} %get-tuple-element.212), channel_id=1, source_target_pairs={{0,6},{2,4},{4,2},{6,0},{1,7},{3,5},{5,3},{7,1},{8,14},{10,12},{12... | collective-permute-start | bytes 196616 | tf_op jit(solution)/shard_map/ppermute | solution.py:30
  141.6 8.5 %collective-permute-start.44 = (bf16[32,1024]{1,0:T(8,128)(2,1)S(1)}, bf16[32,1024]{1,0:T(8,128)(2,1)S(1)}, u32[]{:S(2)}, u32[]{:S(2)}) collective-permute-start(bf16[32,1024]{1,0:T(8,128)(2,1)S(1)} %get-tuple-element.213), channel_id=1, source_target_pairs={{0,4},{2,6},{4,0},{6,2},{1,5},{3,7},{5,1},{7,3},{8,12},{10,14},{12... | collective-permute-start | bytes 196616 | tf_op jit(solution)/shard_map/ppermute | solution.py:30
  141.6 8.5 %collective-permute-start.45 = (bf16[32,1024]{1,0:T(8,128)(2,1)S(1)}, bf16[32,1024]{1,0:T(8,128)(2,1)S(1)}, u32[]{:S(2)}, u32[]{:S(2)}) collective-permute-start(bf16[32,1024]{1,0:T(8,128)(2,1)S(1)} %get-tuple-element.214), channel_id=1, source_target_pairs={{0,2},{2,0},{4,6},{6,4},{1,3},{3,1},{5,7},{7,5},{8,10},{10,8},{12,... | collective-permute-start | bytes 196616 | tf_op jit(solution)/shard_map/ppermute | solution.py:30
  143.4 6.6 %collective-permute-start.42 = (bf16[32,1024]{1,0:T(8,128)(2,1)S(1)}, bf16[32,1024]{1,0:T(8,128)(2,1)S(1)}, u32[]{:S(2)}, u32[]{:S(2)}) collective-permute-start(bf16[32,1024]{1,0:T(8,128)(2,1)S(1)} %get-tuple-element.215), channel_id=1, source_target_pairs={{0,2},{2,0},{4,6},{6,4},{1,3},{3,1},{5,7},{7,5},{8,10},{10,8},{12,... | collective-permute-start | bytes 196616 | tf_op jit(solution)/shard_map/ppermute | solution.py:30

commit v9 on v8

--- a/solution.py
+++ b/solution.py
@@ -1,3 +1,5 @@
+import functools
+
 import jax
 import jax.numpy as jnp
 from jax import lax
@@ -10,10 +12,13 @@
 WEIGHT_CUTS = 8
 
 
-def from_behind(block, axis, distance):
-    devices = range(lax.axis_size(axis))
-    route = [(i - distance, i) for i in devices if i - distance in devices]
-    return lax.ppermute(block, axis, route)
+def hand_over(block):
+    count = lax.axis_size("section")
+    within = [(s, s ^ 1) for s in range(count)]
+    across = [(s, s + 1 if s % 2 else s - 1) for s in range(count)]
+    return [
+        lax.ppermute(block, "section", [(s, t) for s, t in pairs if 0 <= t < count]) for pairs in (within, across)
+    ]
 
 
 def turn(block, axis, distance):
@@ -80,7 +85,7 @@
 def fetch_kernel(sample_ids, inputs, send_base, recv_base, cotangent, *refs):
     ticks = inputs.shape[1]
     count = ticks - 1
-    weights, refs = refs[:2], refs[2:]
+    weights, refs = refs[:1], refs[1:]
     stored, bases, cots = refs[:count], refs[count : 2 * count], refs[2 * count : 3 * count]
     *kept, fresh, sems, weight_sems = refs[3 * count :]
     section, sections = lax.axis_index("section"), lax.axis_size("section")
@@ -107,25 +112,25 @@
         cots[t][...] = jnp.where(section == sections - 1, cots[t][...], jnp.zeros_like(cots[t]))
 
 
-def fetch(sample_ids, inputs, send_base, recv_base, cotangent, *weights):
+def fetch(sample_ids, inputs, send_base, recv_base, cotangent, weight):
     count = inputs.shape[1] - 1
     piece = inputs.shape[2:]
-    large = [pltpu.with_memory_space_constraint(x, pltpu.HBM) for x in (inputs, send_base, recv_base, cotangent, *weights)]
-    *outs, up_kept, down_kept = pl.pallas_call(
+    large = [pltpu.with_memory_space_constraint(x, pltpu.HBM) for x in (inputs, send_base, recv_base, cotangent, weight)]
+    *outs, kept = pl.pallas_call(
         fetch_kernel,
         in_specs=[pl.BlockSpec(memory_space=pltpu.SMEM)] + [pl.BlockSpec(memory_space=pltpu.HBM)] * len(large),
-        out_specs=vmem(3 * count + 2),
-        out_shape=[pltpu.VMEM(piece, BF)] * (3 * count) + [pltpu.VMEM(x.shape, BF) for x in weights],
+        out_specs=vmem(3 * count + 1),
+        out_shape=[pltpu.VMEM(piece, BF)] * (3 * count) + [pltpu.VMEM(weight.shape, BF)],
         scratch_shapes=[
             pltpu.VMEM((count, *piece), BF),
             pltpu.SemaphoreType.DMA((4 * count,)),
-            pltpu.SemaphoreType.DMA((2, WEIGHT_CUTS)),
+            pltpu.SemaphoreType.DMA((1, WEIGHT_CUTS)),
         ],
         compiler_params=pltpu.CompilerParams(vmem_limit_bytes=4 << 20),
-        cost_estimate=pl.CostEstimate(flops=0, bytes_accessed=10 << 20, transcendentals=0),
+        cost_estimate=pl.CostEstimate(flops=0, bytes_accessed=6 << 20, transcendentals=0),
         name="fetch",
     )(sample_ids, *large)
-    return outs[:count], outs[count : 2 * count], outs[2 * count :], up_kept, down_kept
+    return outs[:count], outs[count : 2 * count], outs[2 * count :], kept
 
 
 def first_pieces(inputs, cotangent):
@@ -149,8 +154,14 @@
     return total.astype(BF)
 
 
-def arrive(base, arrived, out):
-    out[...] = added(base, [arrived])
+def arrive(base, within, across, out):
+    odd = lax.axis_index("section") % 2 == 1
+    out[...] = added(base, [jnp.where(odd, within[...], across[...])])
+
+
+def arrive_back(base, within, across, out):
+    odd = lax.axis_index("section") % 2 == 1
+    out[...] = added(base, [jnp.where(odd, across[...], within[...])])
 
 
 def leave(first, *refs):
@@ -165,15 +176,17 @@
 
 
 def finish(first_out, first_grad, *refs):
-    *rest, outs, grads = refs
+    *rest, ins, outs, grads = refs
     count = outs.shape[1] - 1
-    terms, known = rest[: -2 * count], rest[-2 * count :]
+    terms, known = rest[: -3 * count - 1], rest[-3 * count - 1 :]
     half = len(terms) // 2
     outs[0, count] = added(first_out, terms[:half])
     grads[0, 0] = added(first_grad, terms[half:])
     for t in range(count):
         outs[0, t] = known[t][...]
         grads[0, t + 1] = known[count + t][...]
+    for t in range(count + 1):
+        ins[0, t] = known[2 * count + t][...]
 
 
 def turned(*refs):
@@ -186,9 +199,42 @@
         out[n, :] = weight[:, n].T
 
 
+def hold_kernel(weight, kept, sems):
+    step = weight.shape[0] // WEIGHT_CUTS
+    copies = []
+    for i in range(WEIGHT_CUTS):
+        part = pl.ds(i * step, step)
+        copies.append(pltpu.make_async_copy(weight.at[part], kept.at[part], sems.at[i]))
+    for copy in copies:
+        copy.start()
+    for copy in copies:
+        copy.wait()
+
+
+def hold(weight):
+    return pl.pallas_call(
+        hold_kernel,
+        in_specs=[pl.BlockSpec(memory_space=pltpu.HBM)],
+        out_specs=pl.BlockSpec(memory_space=pltpu.VMEM),
+        out_shape=pltpu.VMEM(weight.shape, BF),
+        scratch_shapes=[pltpu.SemaphoreType.DMA((WEIGHT_CUTS,))],
+        compiler_params=pltpu.CompilerParams(vmem_limit_bytes=2 << 20),
+        cost_estimate=pl.CostEstimate(flops=0, bytes_accessed=4 * weight.size, transcendentals=0),
+        name="hold",
+    )(pltpu.with_memory_space_constraint(weight, pltpu.HBM))
+
+
 def columns(width, step=256):
     step = min(width, step)
     return [slice(n, n + step) for n in range(0, width, step)]
+
+
+def up_product_after(_, *refs):
+    up_product(*refs)
+
+
+def back_product_after(_, *refs):
+    back_product(*refs)
 
 
 def up_product(*refs):
@@ -237,43 +283,52 @@
         act[:, n] = jax.nn.silu(pre).astype(BF)
 
 
-def weight_grad(*refs):
+def weight_grad(first, last, *refs):
     *blocks, out, left, right, room, sems = refs
+    if first:
+        blocks = blocks[:-1]
     count = len(blocks) // 2
     depth = blocks[-1].shape[0]
     for t in range(count):
-        left[:, t * depth : (t + 1) * depth] = blocks[t][...]
+        left[:, t * depth : (t + 1) * depth] = blocks[t][first:last, :]
         right[t * depth : (t + 1) * depth, :] = blocks[count + t][...]
     copies = []
-    for i, m in enumerate(columns(out.shape[0])):
+    for i, m in enumerate(columns(last - first)):
         for n in columns(out.shape[1]):
             room[m, n] = matmul(left[m, :], right[:, n]).astype(BF)
-        part = pl.ds(m.start, m.stop - m.start)
-        copies.append(pltpu.make_async_copy(room.at[part], out.at[part], sems.at[i]))
+        size = m.stop - m.start
+        copies.append(
+            pltpu.make_async_copy(room.at[pl.ds(m.start, size)], out.at[pl.ds(first + m.start, size)], sems.at[i])
+        )
         copies[-1].start()
     for copy in copies:
         copy.wait()
 
 
-def weight_product(lefts, rights):
+def weight_product(lefts, rights, first, last, begun=None):
     rows, width, depth = lefts[0].shape[0], rights[0].shape[1], rights[0].shape[0] * len(rights)
+    count = last - first
     return pl.pallas_call(
-        weight_grad,
-        in_specs=vmem(len(lefts) + len(rights)),
+        functools.partial(weight_grad, first, last),
+        in_specs=vmem(len(lefts) + len(rights)) + [pl.BlockSpec(memory_space=pl.ANY)] * (begun is not None),
         out_specs=pl.BlockSpec(memory_space=pl.ANY),
         out_shape=jax.ShapeDtypeStruct((rows, width), BF),
         scratch_shapes=[
-            pltpu.VMEM((rows, depth), BF),
+            pltpu.VMEM((count, depth), BF),
             pltpu.VMEM((depth, width), BF),
-            pltpu.VMEM((rows, width), BF),
-            pltpu.SemaphoreType.DMA((len(columns(rows)),)),
+            pltpu.VMEM((count, width), BF),
+            pltpu.SemaphoreType.DMA((len(columns(count)),)),
         ],
+        input_output_aliases={} if begun is None else {len(lefts) + len(rights): 0},
         compiler_params=pltpu.CompilerParams(vmem_limit_bytes=12 << 20),
         cost_estimate=pl.CostEstimate(
-            flops=2 * rows * width * depth, bytes_accessed=2 * rows * width, transcendentals=0
+            flops=2 * count * width * depth, bytes_accessed=2 * count * width, transcendentals=0
         ),
         name="weight_grad",
-    )(*[pltpu.with_memory_space_constraint(x, pltpu.VMEM) for x in (*lefts, *rights)])
+    )(
+        *[pltpu.with_memory_space_constraint(x, pltpu.VMEM) for x in (*lefts, *rights)],
+        *([] if begun is None else [begun]),
+    )
 
 
 def other_cols(partial):
@@ -312,27 +367,31 @@
     turned_ins, turned_acts = [], []
     for tick in range(ticks):
         if tick:
-            (act_in,) = run(arrive, [piece_like], bases[tick - 1], from_behind(sending, "section", 1))
+            (act_in,) = run(arrive, [piece_like], bases[tick - 1], *hand_over(sending))
+            (j,) = beside(tick)
+            cot_pieces[j] = swap_rows(after(cot_pieces[0], sending), j)
         pieces = gather_rows(act_in)
         if tick == 0:
             for j in beside(0):
                 cot_pieces[j] = swap_rows(after(cot_pieces[0], act_in), j)
-            stored, bases, cots, up_kept, down_kept = fetch(
-                after(sample_ids, act_in), inputs, send_base, recv_base, cotangent, w_up[0], w_down[0]
+            stored, bases, cots, up_kept = fetch(
+                after(sample_ids, act_in), inputs, send_base, recv_base, cotangent, w_up[0]
             )
             pieces = after(pieces, ([cot_pieces[j] for j in beside(0)], stored))
+        if tick:
+            (partial,) = run(
+                up_product_after, [hidden_like], cot_pieces[j], *pieces, up_kept, flops=flops, scratch=room
+            )
+        else:
+            (partial,) = run(up_product, [hidden_like], *pieces, up_kept, flops=flops, scratch=room)
+            down_kept = hold(after(w_down[0], partial))
+        other = other_cols(partial)
         if tick == ticks - 1:
             full_cot, first_grads = run(
-                back_product, [whole_like, hidden_like], *cot_pieces, after(down_turned, act_in), flops=flops
+                back_product, [whole_like, hidden_like], *after(cot_pieces, partial), down_turned, flops=flops
             )
-            pieces = after(pieces, first_grads)
-        (partial,) = run(up_product, [hidden_like], *pieces, up_kept, flops=flops, scratch=room)
-        other = other_cols(partial)
         if tick < ticks - 1:
-            for j in beside(tick + 1):
-                cot_pieces[j] = swap_rows(after(cot_pieces[0], partial), j)
             act, *terms = run(down_product, split_like, partial, other, down_kept, flops=flops)
-            terms = after(terms, [cot_pieces[j] for j in beside(tick + 1)])
             acts.append(act)
             terms_in = scatter_rows(terms)
             if tick == 0:
@@ -358,22 +417,26 @@
         if step == 0:
             grad_out, full_grad, partial = last_cot, full_cot, first_grads
         else:
-            arrived = from_behind(sending, "section", -1)
+            arrived = hand_over(sending)
             if step == 1:
                 (act,) = run(act_only, [hidden_like], *after(pres[-1], sending))
                 acts.append(act)
                 out_pieces = run(down_again, [piece_like] * rows, act, down_kept, flops=flops)
                 arrived = after(arrived, out_pieces)
                 out_terms = list(out_pieces)
-            (grad_out,) = run(arrive, [piece_like], cots[tick], arrived)
+            (grad_out,) = run(arrive_back, [piece_like], cots[tick], *arrived)
+            (j,) = beside(step)
+            out_terms[j] = swap_rows(after(out_pieces[j], sending), j)
             pieces = gather_rows(grad_out)
-            full_grad, partial = run(back_product, [whole_like, hidden_like], *pieces, down_turned, flops=flops)
+            full_grad, partial = run(
+                back_product_after, [whole_like, hidden_like], out_terms[j], *pieces, down_turned, flops=flops
+            )
         other = other_cols(partial)
-        for j in beside(step) if step else []:
-            out_terms[j] = swap_rows(after(out_pieces[j], partial), j)
+        if step == ticks - 1:
+            full_grads[tick] = full_grad
+            half_down = weight_product(turned_acts, full_grads, 0, hidden // 2)
+            other = after(other, half_down)
         grad_pre, *terms = run(in_product, split_like, partial, other, *pres[tick], up_turned, flops=flops)
-        if step:
-            terms = after(terms, [out_terms[j] for j in beside(step)])
         terms_in = scatter_rows(terms)
         if step < ticks - 1:
             while len(turned_ins) < min(step + 2, ticks):
@@ -387,20 +450,20 @@
     for j in beside(0):
         out_terms[j] = swap_rows(after(out_pieces[j], terms), j)
     lefts = after((turned_ins, turned_acts), terms)
-    grad_up = weight_product(lefts[0], pre_grads)
-    grad_down = weight_product(lefts[1], full_grads)
+    grad_up = weight_product(lefts[0], pre_grads, 0, width)
+    grad_down = weight_product(lefts[1], full_grads, hidden // 2, hidden, half_down)
     stack_like = jax.ShapeDtypeStruct((1, ticks, piece_rows, width), BF)
     terms_in[0] = after(terms_in[0], (grad_up, grad_down))
-    section_output, input_grad = pl.pallas_call(
+    section_input, section_output, input_grad = pl.pallas_call(
         finish,
-        in_specs=vmem(2 + 2 * rows + 2 * (ticks - 1)),
-        out_specs=vmem(2),
-        out_shape=[stack_like] * 2,
+        in_specs=vmem(2 + 2 * rows + 3 * ticks - 2),
+        out_specs=vmem(3),
+        out_shape=[stack_like] * 3,
         compiler_params=pltpu.CompilerParams(vmem_limit_bytes=6 << 20),
         name="finish",
-    )(act_in, grad_out, *out_terms, *terms_in, *seen_out, *seen_grad[1:])
+    )(act_in, grad_out, *out_terms, *terms_in, *seen_out, *seen_grad[1:], *seen_in)
     return (
-        jnp.stack(seen_in)[None],
+        section_input,
         section_output,
         input_grad,
         grad_up[None],

time: 153 us -> 148 us (0.967)
  waiting for transfers between devices: 60 us -> 48 us
  starting transfers between devices: 62.6 us -> 68.1 us
  Pallas kernels: 26 us -> 28 us
    ppermute x36, waiting for transfers between devices: 46.9 us -> 33.1 us  [swap_rows(): lax.ppermute(block, 'row', [(i, partner(i, j, size)) for i in range(size)])]
    ppermute x6, starting transfers between devices: 8.06 us -> 15.2 us  [turn(): lax.ppermute(block, axis, [(i, (i + distance) % size) for i in range(size)])]
    pallas_call x3 -> x5, Pallas kernels: 7.36 us -> 10.6 us  [the longest x3 7.52 us: weight_product(): pl.pallas_call(functools.partial(weight_grad, first, last), in_specs=vmem...]
    ppermute x36, starting transfers between devices: 43.3 us -> 40.1 us  [swap_rows(): lax.ppermute(block, 'row', [(i, partner(i, j, size)) for i in range(size)])]
    ppermute x6, waiting for transfers between devices: 2.37 us -> 4.98 us  [turn(): lax.ppermute(block, axis, [(i, (i + distance) % size) for i in range(size)])]
    ppermute x4 -> x8, starting transfers between devices: 11.2 us -> 12.8 us  [hand_over(): lax.ppermute(block, 'section', [(s, t) for s, t in pairs if 0 <= t < count])]
    ppermute x4 -> x8, waiting for transfers between devices: 10.7 us -> 9.95 us  [hand_over(): lax.ppermute(block, 'section', [(s, t) for s, t in pairs if 0 <= t < count])]
  transfers between devices with their start and end apart: 46 -> 50, of which waited for: 26 -> 29; matrix products, arithmetic and copies ran while one was open for 0% -> 0% of each run, Pallas kernels for 13% -> 12%
where the time goes in v9:
time: 148 us; the launch traced here: 146 us
  starting transfers between devices  68.1 us (46%)
  waiting for transfers between devices  48 us (32%)
  Pallas kernels  28 us (19%)
    ppermute x36, starting transfers between devices, swap_rows(): lax.ppermute(block, 'row', [(i, partner(i, j, size)) for i in range(size)])  40.1 us
    ppermute x36, waiting for transfers between devices, swap_rows(): lax.ppermute(block, 'row', [(i, partner(i, j, size)) for i in range(size)])  33.1 us
    ppermute x6, starting transfers between devices, turn(): lax.ppermute(block, axis, [(i, (i + distance) % size) for i in range(size)])  15.2 us
    pallas_call x29, Pallas kernels, run(): pl.pallas_call(kernel, in_specs=vmem(len(ins)), out_specs=vmem(len(outs))...  13.5 us
    ppermute x8, starting transfers between devices, hand_over(): lax.ppermute(block, 'section', [(s, t) for s, t in pairs if 0 <= t < count])  12.8 us
    ppermute x8, waiting for transfers between devices, hand_over(): lax.ppermute(block, 'section', [(s, t) for s, t in pairs if 0 <= t < count])  9.95 us
    pallas_call x3, Pallas kernels, weight_product(): pl.pallas_call(functools.partial(weight_grad, first, last), in_specs=vmem...  7.52 us
    ppermute x6, waiting for transfers between devices, turn(): lax.ppermute(block, axis, [(i, (i + distance) % size) for i in range(size)])  4.98 us
  transfers between devices with their start and end apart: 50, of which 29 were waited for; matrix products, arithmetic and copies ran while one was open for 0% of the time, Pallas kernels for 12%

profile of v9, /device:TPU:3, one launch (start us, length us, event | category | flops | bytes accessed | tf_op | source)
XLA Modules:
  0.0 145.8 jit_solution(10286046704338248867)
XLA Ops:
  0.6 0.9 first.1
  1.5 1.4 collective-permute-start.3
  3.1 2.3 %collective-permute-start.1 = (bf16[32,1024]{1,0:T(8,128)(2,1)S(1)}, bf16[32,1024]{1,0:T(8,128)(2,1)S(1)}, u32[]{:S(2)}, u32[]{:S(2)}) collective-permute-start(bf16[32,1024]{1,0:T(8,128)(2,1)S(1)} %get-tuple-element.132.refs_0_.first.refs_12_), channel_id=1, source_target_pairs={{0,4},{2,6},{4,0},{6,2},{1,5},{3,7},{5,1},{7,3},{8,12},{10,14},{12... | collective-permute-start | bytes 196616 | tf_op jit(solution)/shard_map/ppermute | solution.py:35
  5.4 1.1 collective-permute-start
  7.1 3.0 %fetch.1 = (bf16[32,1024]{1,0:T(8,128)(2,1)S(1)}, bf16[32,1024]{1,0:T(8,128)(2,1)S(1)}, bf16[32,1024]{1,0:T(8,128)(2,1)S(1)}, bf16[32,1024]{1,0:T(8,128)(2,1)S(1...) custom-call(s32[6]{0:T(128)S(1)} %copy-done, ...), custom_call_target="tpu_custom_call" | custom-call | bytes 6291456 | tf_op jit(solution)/shard_map/fetch/pallas_call | solution.py:119
  10.2 1.1 collective-permute-done.refs_1_
  11.9 1.9 %collective-permute-start.4 = (bf16[128,2048]{1,0:T(8,128)(2,1)S(1)}, bf16[128,2048]{1,0:T(8,128)(2,1)S(1)}, u32[]{:S(2)}, u32[]{:S(2)}) collective-permute-start(bf16[128,2048]{1,0:T(8,128)(2,1)S(1)} %up_product.1.mine.pre_mine), channel_id=1, source_target_pairs={{0,1},{1,0},{2,3},{3,2},{4,5},{5,4},{6,7},{7,6},{8,9},{9,8},{10,11... | collective-permute-start | bytes 1572872 | tf_op jit(solution)/shard_map/ppermute | solution.py:26
  13.8 2.2 %hold.1.weight = bf16[2048,1024]{1,0:T(8,128)(2,1)S(1)} custom-call(bf16[2048,1024]{1,0:T(8,128)(2,1)} %bitcast.6), custom_call_target="tpu_custom_call" | custom-call | bytes 8388608 | tf_op jit(solution)/shard_map/hold/pallas_call | solution.py:215
  16.8 2.0 %collective-permute-start.5 = (bf16[32,1024]{1,0:T(8,128)(2,1)S(1)}, bf16[32,1024]{1,0:T(8,128)(2,1)S(1)}, u32[]{:S(2)}, u32[]{:S(2)}) collective-permute-start(bf16[32,1024]{1,0:T(8,128)(2,1)S(1)} %get-tuple-element.120), channel_id=1, source_target_pairs={{0,6},{2,4},{4,2},{6,0},{1,7},{3,5},{5,3},{7,1},{8,14},{10,12},{12... | collective-permute-start | bytes 196616 | tf_op jit(solution)/shard_map/ppermute | solution.py:35
  19.0 1.4 collective-permute-start.7
  20.4 1.2 turned_weight.2.refs_4_
  22.4 3.3 %collective-permute-done.6.refs_2_ = bf16[32,1024]{1,0:T(8,128)(2,1)S(1)} collective-permute-done((bf16[32,1024]{1,0:T(8,128)(2,1)S(1)}, bf16[32,1024]{1,0:T(8,128)(2,1)S(1)}, u32[]{:S(2)}, u32[]{:S(2)}) %collective-permute-start.6) | collective-permute-done | bytes 65568 | tf_op jit(solution)/shard_map/ppermute | solution.py:35
  25.8 3.1 %collective-permute-start.9 = (bf16[32,1024]{1,0:T(8,128)(2,1)S(1)}, bf16[32,1024]{1,0:T(8,128)(2,1)S(1)}, u32[]{:S(2)}, u32[]{:S(2)}) collective-permute-start(bf16[32,1024]{1,0:T(8,128)(2,1)S(1)} %get-tuple-element.125), channel_id=1, source_target_pairs={{8,16},{16,8},{9,17},{17,9},{10,18},{18,10},{11,19},{19,11},{12,20... | collective-permute-start | bytes 196616 | tf_op jit(solution)/shard_map/ppermute | solution.py:20
  29.1 2.6 %collective-permute-done.9.across = bf16[32,1024]{1,0:T(8,128)(2,1)S(1)} collective-permute-done((bf16[32,1024]{1,0:T(8,128)(2,1)S(1)}, bf16[32,1024]{1,0:T(8,128)(2,1)S(1)}, u32[]{:S(2)}, u32[]{:S(2)}) %collective-permute-start.9) | collective-permute-done | bytes 65568 | tf_op jit(solution)/shard_map/ppermute | solution.py:20
  32.5 2.0 %collective-permute-start.12 = (bf16[32,1024]{1,0:T(8,128)(2,1)S(1)}, bf16[32,1024]{1,0:T(8,128)(2,1)S(1)}, u32[]{:S(2)}, u32[]{:S(2)}) collective-permute-start(bf16[32,1024]{1,0:T(8,128)(2,1)S(1)} %arrive.2.refs_0_.first.refs_13_), channel_id=1, source_target_pairs={{0,4},{2,6},{4,0},{6,2},{1,5},{3,7},{5,1},{7,3},{8,12},{10,14},{12... | collective-permute-start | bytes 196616 | tf_op jit(solution)/shard_map/ppermute | solution.py:35
  34.5 1.6 %collective-permute-start.11 = (bf16[32,1024]{1,0:T(8,128)(2,1)S(1)}, bf16[32,1024]{1,0:T(8,128)(2,1)S(1)}, u32[]{:S(2)}, u32[]{:S(2)}) collective-permute-start(bf16[32,1024]{1,0:T(8,128)(2,1)S(1)} %arrive.2.refs_0_.first.refs_13_), channel_id=1, source_target_pairs={{0,6},{2,4},{4,2},{6,0},{1,7},{3,5},{5,3},{7,1},{8,14},{10,12},{12... | collective-permute-start | bytes 196616 | tf_op jit(solution)/shard_map/ppermute | solution.py:35
  36.6 3.0 %collective-permute-done.11.refs_1_ = bf16[32,1024]{1,0:T(8,128)(2,1)S(1)} collective-permute-done((bf16[32,1024]{1,0:T(8,128)(2,1)S(1)}, bf16[32,1024]{1,0:T(8,128)(2,1)S(1)}, u32[]{:S(2)}, u32[]{:S(2)}) %collective-permute-start.11) | collective-permute-done | bytes 65568 | tf_op jit(solution)/shard_map/ppermute | solution.py:35
  40.3 3.8 %collective-permute-start.14 = (bf16[128,2048]{1,0:T(8,128)(2,1)S(1)}, bf16[128,2048]{1,0:T(8,128)(2,1)S(1)}, u32[]{:S(2)}, u32[]{:S(2)}) collective-permute-start(bf16[128,2048]{1,0:T(8,128)(2,1)S(1)} %up_product_after.2.mine.pre_mine), channel_id=1, source_target_pairs={{0,1},{1,0},{2,3},{3,2},{4,5},{5,4},{6,7},{7,6},{8,9},{9,8},{10,11... | collective-permute-start | bytes 1572872 | tf_op jit(solution)/shard_map/ppermute | solution.py:26
  44.1 1.5 %collective-permute-done.14.other.pre_other = bf16[128,2048]{1,0:T(8,128)(2,1)S(1)} collective-permute-done((bf16[128,2048]{1,0:T(8,128)(2,1)S(1)}, bf16[128,2048]{1,0:T(8,128)(2,1)S(1)}, u32[]{:S(2)}, u32[]{:S(2)}) %collective-permute-start.14) | collective-permute-done | bytes 524320 | tf_op jit(solution)/shard_map/ppermute | solution.py:26
  46.4 1.1 collective-permute-start.15
  47.6 2.5 %collective-permute-start.17 = (bf16[32,1024]{1,0:T(8,128)(2,1)S(1)}, bf16[32,1024]{1,0:T(8,128)(2,1)S(1)}, u32[]{:S(2)}, u32[]{:S(2)}) collective-permute-start(bf16[32,1024]{1,0:T(8,128)(2,1)S(1)} %get-tuple-element.130), channel_id=1, source_target_pairs={{0,2},{2,0},{4,6},{6,4},{1,3},{3,1},{5,7},{7,5},{8,10},{10,8},{12,... | collective-permute-start | bytes 196616 | tf_op jit(solution)/shard_map/ppermute | solution.py:35
  50.2 1.2 turned_weight.3.weight
  51.6 3.5 %collective-permute-done.16.refs_2_ = bf16[32,1024]{1,0:T(8,128)(2,1)S(1)} collective-permute-done((bf16[32,1024]{1,0:T(8,128)(2,1)S(1)}, bf16[32,1024]{1,0:T(8,128)(2,1)S(1)}, u32[]{:S(2)}, u32[]{:S(2)}) %collective-permute-start.16) | collective-permute-done | bytes 65568 | tf_op jit(solution)/shard_map/ppermute | solution.py:35
  55.2 3.1 %collective-permute-start.19 = (bf16[32,1024]{1,0:T(8,128)(2,1)S(1)}, bf16[32,1024]{1,0:T(8,128)(2,1)S(1)}, u32[]{:S(2)}, u32[]{:S(2)}) collective-permute-start(bf16[32,1024]{1,0:T(8,128)(2,1)S(1)} %get-tuple-element.139), channel_id=1, source_target_pairs={{8,16},{16,8},{9,17},{17,9},{10,18},{18,10},{11,19},{19,11},{12,20... | collective-permute-start | bytes 196616 | tf_op jit(solution)/shard_map/ppermute | solution.py:20
  58.3 1.1 collective-permute-start.20
  59.5 1.6 %collective-permute-done.19.across = bf16[32,1024]{1,0:T(8,128)(2,1)S(1)} collective-permute-done((bf16[32,1024]{1,0:T(8,128)(2,1)S(1)}, bf16[32,1024]{1,0:T(8,128)(2,1)S(1)}, u32[]{:S(2)}, u32[]{:S(2)}) %collective-permute-start.19) | collective-permute-done | bytes 65568 | tf_op jit(solution)/shard_map/ppermute | solution.py:20
  61.9 1.4 collective-permute-start.22
  63.2 2.2 %collective-permute-start.21 = (bf16[32,1024]{1,0:T(8,128)(2,1)S(1)}, bf16[32,1024]{1,0:T(8,128)(2,1)S(1)}, u32[]{:S(2)}, u32[]{:S(2)}) collective-permute-start(bf16[32,1024]{1,0:T(8,128)(2,1)S(1)} %arrive.3.refs_0_.first_out.refs_14_), channel_id=1, source_target_pairs={{0,6},{2,4},{4,2},{6,0},{1,7},{3,5},{5,3},{7,1},{8,14},{10,12},{12... | collective-permute-start | bytes 196616 | tf_op jit(solution)/shard_map/ppermute | solution.py:35
  66.2 2.3 %collective-permute-done.21.refs_1_ = bf16[32,1024]{1,0:T(8,128)(2,1)S(1)} collective-permute-done((bf16[32,1024]{1,0:T(8,128)(2,1)S(1)}, bf16[32,1024]{1,0:T(8,128)(2,1)S(1)}, u32[]{:S(2)}, u32[]{:S(2)}) %collective-permute-start.21) | collective-permute-done | bytes 65568 | tf_op jit(solution)/shard_map/ppermute | solution.py:35
  69.2 3.2 %collective-permute-start.25 = (bf16[128,2048]{1,0:T(8,128)(2,1)S(1)}, bf16[128,2048]{1,0:T(8,128)(2,1)S(1)}, u32[]{:S(2)}, u32[]{:S(2)}) collective-permute-start(bf16[128,2048]{1,0:T(8,128)(2,1)S(1)} %up_product_after.3.pre_mine.mine), channel_id=1, source_target_pairs={{0,1},{1,0},{2,3},{3,2},{4,5},{5,4},{6,7},{7,6},{8,9},{9,8},{10,11... | collective-permute-start | bytes 1572872 | tf_op jit(solution)/shard_map/ppermute | solution.py:26
  73.9 1.2 collective-permute-done.24.other
  75.1 1.0 in_product.3
  76.1 2.1 %collective-permute-start.26 = (bf16[32,1024]{1,0:T(8,128)(2,1)S(1)}, bf16[32,1024]{1,0:T(8,128)(2,1)S(1)}, u32[]{:S(2)}, u32[]{:S(2)}) collective-permute-start(bf16[32,1024]{1,0:T(8,128)(2,1)S(1)} %get-tuple-element.149), channel_id=1, source_target_pairs={{0,6},{2,4},{4,2},{6,0},{1,7},{3,5},{5,3},{7,1},{8,14},{10,12},{12... | collective-permute-start | bytes 196616 | tf_op jit(solution)/shard_map/ppermute | solution.py:35
  78.2 1.5 %collective-permute-start.28 = (bf16[32,1024]{1,0:T(8,128)(2,1)S(1)}, bf16[32,1024]{1,0:T(8,128)(2,1)S(1)}, u32[]{:S(2)}, u32[]{:S(2)}) collective-permute-start(bf16[32,1024]{1,0:T(8,128)(2,1)S(1)} %get-tuple-element.151), channel_id=1, source_target_pairs={{0,2},{2,0},{4,6},{6,4},{1,3},{3,1},{5,7},{7,5},{8,10},{10,8},{12,... | collective-permute-start | bytes 196616 | tf_op jit(solution)/shard_map/ppermute | solution.py:35
  80.0 1.5 %collective-permute-done.26.refs_1_ = bf16[32,1024]{1,0:T(8,128)(2,1)S(1)} collective-permute-done((bf16[32,1024]{1,0:T(8,128)(2,1)S(1)}, bf16[32,1024]{1,0:T(8,128)(2,1)S(1)}, u32[]{:S(2)}, u32[]{:S(2)}) %collective-permute-start.26) | collective-permute-done | bytes 65568 | tf_op jit(solution)/shard_map/ppermute | solution.py:35
  81.5 3.3 %collective-permute-done.27.refs_2_ = bf16[32,1024]{1,0:T(8,128)(2,1)S(1)} collective-permute-done((bf16[32,1024]{1,0:T(8,128)(2,1)S(1)}, bf16[32,1024]{1,0:T(8,128)(2,1)S(1)}, u32[]{:S(2)}, u32[]{:S(2)}) %collective-permute-start.27) | collective-permute-done | bytes 65568 | tf_op jit(solution)/shard_map/ppermute | solution.py:35
  84.8 3.3 %collective-permute-start.30 = (bf16[32,1024]{1,0:T(8,128)(2,1)S(1)}, bf16[32,1024]{1,0:T(8,128)(2,1)S(1)}, u32[]{:S(2)}, u32[]{:S(2)}) collective-permute-start(bf16[32,1024]{1,0:T(8,128)(2,1)S(1)} %leave_back.2.refs_11_), channel_id=1, source_target_pairs={{8,16},{16,8},{9,17},{17,9},{10,18},{18,10},{11,19},{19,11},{12,20... | collective-permute-start | bytes 196616 | tf_op jit(solution)/shard_map/ppermute | solution.py:20
  89.2 1.5 %collective-permute-done.30.across = bf16[32,1024]{1,0:T(8,128)(2,1)S(1)} collective-permute-done((bf16[32,1024]{1,0:T(8,128)(2,1)S(1)}, bf16[32,1024]{1,0:T(8,128)(2,1)S(1)}, u32[]{:S(2)}, u32[]{:S(2)}) %collective-permute-start.30) | collective-permute-done | bytes 65568 | tf_op jit(solution)/shard_map/ppermute | solution.py:20
  90.7 0.9 collective-permute-done.29.within
  91.7 2.3 %collective-permute-start.33 = (bf16[32,1024]{1,0:T(8,128)(2,1)S(1)}, bf16[32,1024]{1,0:T(8,128)(2,1)S(1)}, u32[]{:S(2)}, u32[]{:S(2)}) collective-permute-start(bf16[32,1024]{1,0:T(8,128)(2,1)S(1)} %arrive_back.2.refs_0_.first), channel_id=1, source_target_pairs={{0,4},{2,6},{4,0},{6,2},{1,5},{3,7},{5,1},{7,3},{8,12},{10,14},{12... | collective-permute-start | bytes 196616 | tf_op jit(solution)/shard_map/ppermute | solution.py:35
  94.0 1.2 collective-permute-start.32
  96.1 3.4 %collective-permute-done.32.refs_1_ = bf16[32,1024]{1,0:T(8,128)(2,1)S(1)} collective-permute-done((bf16[32,1024]{1,0:T(8,128)(2,1)S(1)}, bf16[32,1024]{1,0:T(8,128)(2,1)S(1)}, u32[]{:S(2)}, u32[]{:S(2)}) %collective-permute-start.32) | collective-permute-done | bytes 65568 | tf_op jit(solution)/shard_map/ppermute | solution.py:35
  100.2 2.9 %collective-permute-start.35 = (bf16[128,2048]{1,0:T(8,128)(2,1)S(1)}, bf16[128,2048]{1,0:T(8,128)(2,1)S(1)}, u32[]{:S(2)}, u32[]{:S(2)}) collective-permute-start(bf16[128,2048]{1,0:T(8,128)(2,1)S(1)} %get-tuple-element.168.mine), channel_id=1, source_target_pairs={{0,1},{1,0},{2,3},{3,2},{4,5},{5,4},{6,7},{7,6},{8,9},{9,8},{10,11... | collective-permute-start | bytes 1572872 | tf_op jit(solution)/shard_map/ppermute | solution.py:26
  103.1 1.5 %collective-permute-done.35.other = bf16[128,2048]{1,0:T(8,128)(2,1)S(1)} collective-permute-done((bf16[128,2048]{1,0:T(8,128)(2,1)S(1)}, bf16[128,2048]{1,0:T(8,128)(2,1)S(1)}, u32[]{:S(2)}, u32[]{:S(2)}) %collective-permute-start.35) | collective-permute-done | bytes 524320 | tf_op jit(solution)/shard_map/ppermute | solution.py:26
  104.6 1.0 in_product.4
  105.6 1.4 collective-permute-start.36
  107.0 2.2 %collective-permute-start.38 = (bf16[32,1024]{1,0:T(8,128)(2,1)S(1)}, bf16[32,1024]{1,0:T(8,128)(2,1)S(1)}, u32[]{:S(2)}, u32[]{:S(2)}) collective-permute-start(bf16[32,1024]{1,0:T(8,128)(2,1)S(1)} %get-tuple-element.172), channel_id=1, source_target_pairs={{0,2},{2,0},{4,6},{6,4},{1,3},{3,1},{5,7},{7,5},{8,10},{10,8},{12,... | collective-permute-start | bytes 196616 | tf_op jit(solution)/shard_map/ppermute | solution.py:35
  109.5 1.1 collective-permute-done.36.refs_1_
  110.7 3.6 %collective-permute-done.37.refs_2_ = bf16[32,1024]{1,0:T(8,128)(2,1)S(1)} collective-permute-done((bf16[32,1024]{1,0:T(8,128)(2,1)S(1)}, bf16[32,1024]{1,0:T(8,128)(2,1)S(1)}, u32[]{:S(2)}, u32[]{:S(2)}) %collective-permute-start.37) | collective-permute-done | bytes 65568 | tf_op jit(solution)/shard_map/ppermute | solution.py:35
  114.4 3.1 %collective-permute-start.40 = (bf16[32,1024]{1,0:T(8,128)(2,1)S(1)}, bf16[32,1024]{1,0:T(8,128)(2,1)S(1)}, u32[]{:S(2)}, u32[]{:S(2)}) collective-permute-start(bf16[32,1024]{1,0:T(8,128)(2,1)S(1)} %leave_back.3.refs_10_), channel_id=1, source_target_pairs={{8,16},{16,8},{9,17},{17,9},{10,18},{18,10},{11,19},{19,11},{12,20... | collective-permute-start | bytes 196616 | tf_op jit(solution)/shard_map/ppermute | solution.py:20
  117.5 1.4 collective-permute-start.41
  118.9 1.4 collective-permute-done.40.across
  121.0 1.6 %collective-permute-start.43 = (bf16[32,1024]{1,0:T(8,128)(2,1)S(1)}, bf16[32,1024]{1,0:T(8,128)(2,1)S(1)}, u32[]{:S(2)}, u32[]{:S(2)}) collective-permute-start(bf16[32,1024]{1,0:T(8,128)(2,1)S(1)} %arrive_back.3.refs_0_.first_grad), channel_id=1, source_target_pairs={{0,4},{2,6},{4,0},{6,2},{1,5},{3,7},{5,1},{7,3},{8,12},{10,14},{12... | collective-permute-start | bytes 196616 | tf_op jit(solution)/shard_map/ppermute | solution.py:35
  122.6 2.0 %collective-permute-start.42 = (bf16[32,1024]{1,0:T(8,128)(2,1)S(1)}, bf16[32,1024]{1,0:T(8,128)(2,1)S(1)}, u32[]{:S(2)}, u32[]{:S(2)}) collective-permute-start(bf16[32,1024]{1,0:T(8,128)(2,1)S(1)} %arrive_back.3.refs_0_.first_grad), channel_id=1, source_target_pairs={{0,6},{2,4},{4,2},{6,0},{1,7},{3,5},{5,3},{7,1},{8,14},{10,12},{12... | collective-permute-start | bytes 196616 | tf_op jit(solution)/shard_map/ppermute | solution.py:35
  125.2 2.4 %collective-permute-done.42.refs_1_ = bf16[32,1024]{1,0:T(8,128)(2,1)S(1)} collective-permute-done((bf16[32,1024]{1,0:T(8,128)(2,1)S(1)}, bf16[32,1024]{1,0:T(8,128)(2,1)S(1)}, u32[]{:S(2)}, u32[]{:S(2)}) %collective-permute-start.42) | collective-permute-done | bytes 65568 | tf_op jit(solution)/shard_map/ppermute | solution.py:35
  128.3 3.3 %collective-permute-start.45 = (bf16[128,2048]{1,0:T(8,128)(2,1)S(1)}, bf16[128,2048]{1,0:T(8,128)(2,1)S(1)}, u32[]{:S(2)}, u32[]{:S(2)}) collective-permute-start(bf16[128,2048]{1,0:T(8,128)(2,1)S(1)} %get-tuple-element.180.mine), channel_id=1, source_target_pairs={{0,1},{1,0},{2,3},{3,2},{4,5},{5,4},{6,7},{7,6},{8,9},{9,8},{10,11... | collective-permute-start | bytes 1572872 | tf_op jit(solution)/shard_map/ppermute | solution.py:26
  131.7 2.1 %weight_grad.3.refs_6_ = bf16[2048,1024]{1,0:T(8,128)(2,1)} custom-call(bf16[2048,128]{1,0:T(8,128)(2,1)S(1)} %turned.7.refs_0_, bf16[2048,128]{1,0:T(8,128)(2,1)S(1)} %turned.9.refs_1_, bf16[2048,128]{1,0:T(8,128)(2,1)S(1)} %turned.11.refs_2_, bf16[128,1024]{1,0:T(8,128)(2,1)S(1)} %get-tuple-element.181.refs_3_, ...), custom_call_target="tpu_custom_call" | custom-call | flops 805306368 | bytes 2097152 | tf_op jit(solution)/shard_map/weight_grad/pallas_call | solution.py:311
  133.8 1.0 in_product.5
  134.8 2.0 %collective-permute-start.47 = (bf16[32,1024]{1,0:T(8,128)(2,1)S(1)}, bf16[32,1024]{1,0:T(8,128)(2,1)S(1)}, u32[]{:S(2)}, u32[]{:S(2)}) collective-permute-start(bf16[32,1024]{1,0:T(8,128)(2,1)S(1)} %get-tuple-element.186), channel_id=1, source_target_pairs={{0,6},{2,4},{4,2},{6,0},{1,7},{3,5},{5,3},{7,1},{8,14},{10,12},{12... | collective-permute-start | bytes 196616 | tf_op jit(solution)/shard_map/ppermute | solution.py:35
  136.8 1.6 %collective-permute-start.49 = (bf16[32,1024]{1,0:T(8,128)(2,1)S(1)}, bf16[32,1024]{1,0:T(8,128)(2,1)S(1)}, u32[]{:S(2)}, u32[]{:S(2)}) collective-permute-start(bf16[32,1024]{1,0:T(8,128)(2,1)S(1)} %get-tuple-element.188), channel_id=1, source_target_pairs={{0,2},{2,0},{4,6},{6,4},{1,3},{3,1},{5,7},{7,5},{8,10},{10,8},{12,... | collective-permute-start | bytes 196616 | tf_op jit(solution)/shard_map/ppermute | solution.py:35
  138.4 3.3 %weight_grad.4 = bf16[1024,2048]{1,0:T(8,128)(2,1)} custom-call(bf16[1024,128]{1,0:T(8,128)(2,1)S(1)} %turned.6.refs_0_, bf16[1024,128]{1,0:T(8,128)(2,1)S(1)} %turned.8.refs_1_, bf16[1024,128]{1,0:T(8,128)(2,1)S(1)} %turned.10.refs_2_, bf16[128,2048]{1,0:T(8,128)(2,1)S(1)} %get-tuple-element.193.refs_3_, bf16[128,2048]{1,0:T(8,128)(2,1)S(1)} %get-tuple-element.194.refs_4_, ...), custom_call_target="tpu_custom_call" | custom-call | flops 1610612736 | bytes 4194304 | tf_op jit(solution)/shard_map/weight_grad/pallas_call | solution.py:311
  141.8 2.1 %weight_grad.5 = bf16[2048,1024]{1,0:T(8,128)(2,1)} custom-call(bf16[2048,128]{1,0:T(8,128)(2,1)S(1)} %turned.7.refs_0_, bf16[2048,128]{1,0:T(8,128)(2,1)S(1)} %turned.9.refs_1_, bf16[2048,128]{1,0:T(8,128)(2,1)S(1)} %turned.11.refs_2_, bf16[128,1024]{1,0:T(8,128)(2,1)S(1)} %get-tuple-element.181.refs_3_, ...), custom_call_target="tpu_custom_call", output_to_operand_aliasing={{}: (6, {})} | custom-call | flops 805306368 | bytes 2097152 | tf_op jit(solution)/shard_map/weight_grad/pallas_call | solution.py:311
  143.9 1.0 collective-permute-done.46.refs_3_
  144.9 0.9 finish.1
  (74 shorter events, 16.2 us)
Async XLA Ops:
  1.5 8.6 %collective-permute-start.3 = (bf16[32,1024]{1,0:T(8,128)(2,1)S(1)}, bf16[32,1024]{1,0:T(8,128)(2,1)S(1)}, u32[]{:S(2)}, u32[]{:S(2)}) collective-permute-start(bf16[32,1024]{1,0:T(8,128)(2,1)S(1)} %get-tuple-element.143.refs_0_.first), channel_id=1, source_target_pairs={{0,2},{2,0},{4,6},{6,4},{1,3},{3,1},{5,7},{7,5},{8,10},{10,8},{12,... | collective-permute-start | bytes 196616 | tf_op jit(solution)/shard_map/ppermute | solution.py:35
  2.9 7.2 %collective-permute-start.2 = (bf16[32,1024]{1,0:T(8,128)(2,1)S(1)}, bf16[32,1024]{1,0:T(8,128)(2,1)S(1)}, u32[]{:S(2)}, u32[]{:S(2)}) collective-permute-start(bf16[32,1024]{1,0:T(8,128)(2,1)S(1)} %get-tuple-element.132.refs_0_.first.refs_12_), channel_id=1, source_target_pairs={{0,2},{2,0},{4,6},{6,4},{1,3},{3,1},{5,7},{7,5},{8,10},{10,8},{12,... | collective-permute-start | bytes 196616 | tf_op jit(solution)/shard_map/ppermute | solution.py:35
  3.1 7.1 %collective-permute-start.1 = (bf16[32,1024]{1,0:T(8,128)(2,1)S(1)}, bf16[32,1024]{1,0:T(8,128)(2,1)S(1)}, u32[]{:S(2)}, u32[]{:S(2)}) collective-permute-start(bf16[32,1024]{1,0:T(8,128)(2,1)S(1)} %get-tuple-element.132.refs_0_.first.refs_12_), channel_id=1, source_target_pairs={{0,4},{2,6},{4,0},{6,2},{1,5},{3,7},{5,1},{7,3},{8,12},{10,14},{12... | collective-permute-start | bytes 196616 | tf_op jit(solution)/shard_map/ppermute | solution.py:35
  5.4 5.8 %collective-permute-start = (bf16[32,1024]{1,0:T(8,128)(2,1)S(1)}, bf16[32,1024]{1,0:T(8,128)(2,1)S(1)}, u32[]{:S(2)}, u32[]{:S(2)}) collective-permute-start(bf16[32,1024]{1,0:T(8,128)(2,1)S(1)} %get-tuple-element.132.refs_0_.first.refs_12_), channel_id=1, source_target_pairs={{0,6},{2,4},{4,2},{6,0},{1,7},{3,5},{5,3},{7,1},{8,14},{10,12},{12... | collective-permute-start | bytes 196616 | tf_op jit(solution)/shard_map/ppermute | solution.py:35
  6.4 0.7 copy-start
  11.9 4.1 %collective-permute-start.4 = (bf16[128,2048]{1,0:T(8,128)(2,1)S(1)}, bf16[128,2048]{1,0:T(8,128)(2,1)S(1)}, u32[]{:S(2)}, u32[]{:S(2)}) collective-permute-start(bf16[128,2048]{1,0:T(8,128)(2,1)S(1)} %up_product.1.mine.pre_mine), channel_id=1, source_target_pairs={{0,1},{1,0},{2,3},{3,2},{4,5},{5,4},{6,7},{7,6},{8,9},{9,8},{10,11... | collective-permute-start | bytes 1572872 | tf_op jit(solution)/shard_map/ppermute | solution.py:26
  16.8 5.6 %collective-permute-start.5 = (bf16[32,1024]{1,0:T(8,128)(2,1)S(1)}, bf16[32,1024]{1,0:T(8,128)(2,1)S(1)}, u32[]{:S(2)}, u32[]{:S(2)}) collective-permute-start(bf16[32,1024]{1,0:T(8,128)(2,1)S(1)} %get-tuple-element.120), channel_id=1, source_target_pairs={{0,6},{2,4},{4,2},{6,0},{1,7},{3,5},{5,3},{7,1},{8,14},{10,12},{12... | collective-permute-start | bytes 196616 | tf_op jit(solution)/shard_map/ppermute | solution.py:35
  18.8 6.9 %collective-permute-start.6 = (bf16[32,1024]{1,0:T(8,128)(2,1)S(1)}, bf16[32,1024]{1,0:T(8,128)(2,1)S(1)}, u32[]{:S(2)}, u32[]{:S(2)}) collective-permute-start(bf16[32,1024]{1,0:T(8,128)(2,1)S(1)} %get-tuple-element.121), channel_id=1, source_target_pairs={{0,4},{2,6},{4,0},{6,2},{1,5},{3,7},{5,1},{7,3},{8,12},{10,14},{12... | collective-permute-start | bytes 196616 | tf_op jit(solution)/shard_map/ppermute | solution.py:35
  19.0 6.8 %collective-permute-start.7 = (bf16[32,1024]{1,0:T(8,128)(2,1)S(1)}, bf16[32,1024]{1,0:T(8,128)(2,1)S(1)}, u32[]{:S(2)}, u32[]{:S(2)}) collective-permute-start(bf16[32,1024]{1,0:T(8,128)(2,1)S(1)} %get-tuple-element.122), channel_id=1, source_target_pairs={{0,2},{2,0},{4,6},{6,4},{1,3},{3,1},{5,7},{7,5},{8,10},{10,8},{12,... | collective-permute-start | bytes 196616 | tf_op jit(solution)/shard_map/ppermute | solution.py:35
  25.8 5.9 %collective-permute-start.9 = (bf16[32,1024]{1,0:T(8,128)(2,1)S(1)}, bf16[32,1024]{1,0:T(8,128)(2,1)S(1)}, u32[]{:S(2)}, u32[]{:S(2)}) collective-permute-start(bf16[32,1024]{1,0:T(8,128)(2,1)S(1)} %get-tuple-element.125), channel_id=1, source_target_pairs={{8,16},{16,8},{9,17},{17,9},{10,18},{18,10},{11,19},{19,11},{12,20... | collective-permute-start | bytes 196616 | tf_op jit(solution)/shard_map/ppermute | solution.py:20
  28.9 3.5 %collective-permute-start.8 = (bf16[32,1024]{1,0:T(8,128)(2,1)S(1)}, bf16[32,1024]{1,0:T(8,128)(2,1)S(1)}, u32[]{:S(2)}, u32[]{:S(2)}) collective-permute-start(bf16[32,1024]{1,0:T(8,128)(2,1)S(1)} %get-tuple-element.125), channel_id=1, source_target_pairs={{0,8},{8,0},{16,24},{24,16},{1,9},{9,1},{17,25},{25,17},{2,10},{10... | collective-permute-start | bytes 196616 | tf_op jit(solution)/shard_map/ppermute | solution.py:20
  29.0 7.0 %collective-permute-start.10 = (bf16[32,1024]{1,0:T(8,128)(2,1)S(1)}, bf16[32,1024]{1,0:T(8,128)(2,1)S(1)}, u32[]{:S(2)}, u32[]{:S(2)}) collective-permute-start(bf16[32,1024]{1,0:T(8,128)(2,1)S(1)} %get-tuple-element.143.refs_0_.first), channel_id=1, source_target_pairs={{0,4},{2,6},{4,0},{6,2},{1,5},{3,7},{5,1},{7,3},{8,12},{10,14},{12... | collective-permute-start | bytes 196616 | tf_op jit(solution)/shard_map/ppermute | solution.py:35
  32.4 3.6 %collective-permute-start.13 = (bf16[32,1024]{1,0:T(8,128)(2,1)S(1)}, bf16[32,1024]{1,0:T(8,128)(2,1)S(1)}, u32[]{:S(2)}, u32[]{:S(2)}) collective-permute-start(bf16[32,1024]{1,0:T(8,128)(2,1)S(1)} %arrive.2.refs_0_.first.refs_13_), channel_id=1, source_target_pairs={{0,2},{2,0},{4,6},{6,4},{1,3},{3,1},{5,7},{7,5},{8,10},{10,8},{12,... | collective-permute-start | bytes 196616 | tf_op jit(solution)/shard_map/ppermute | solution.py:35
  32.5 4.1 %collective-permute-start.12 = (bf16[32,1024]{1,0:T(8,128)(2,1)S(1)}, bf16[32,1024]{1,0:T(8,128)(2,1)S(1)}, u32[]{:S(2)}, u32[]{:S(2)}) collective-permute-start(bf16[32,1024]{1,0:T(8,128)(2,1)S(1)} %arrive.2.refs_0_.first.refs_13_), channel_id=1, source_target_pairs={{0,4},{2,6},{4,0},{6,2},{1,5},{3,7},{5,1},{7,3},{8,12},{10,14},{12... | collective-permute-start | bytes 196616 | tf_op jit(solution)/shard_map/ppermute | solution.py:35
  34.5 5.1 %collective-permute-start.11 = (bf16[32,1024]{1,0:T(8,128)(2,1)S(1)}, bf16[32,1024]{1,0:T(8,128)(2,1)S(1)}, u32[]{:S(2)}, u32[]{:S(2)}) collective-permute-start(bf16[32,1024]{1,0:T(8,128)(2,1)S(1)} %arrive.2.refs_0_.first.refs_13_), channel_id=1, source_target_pairs={{0,6},{2,4},{4,2},{6,0},{1,7},{3,5},{5,3},{7,1},{8,14},{10,12},{12... | collective-permute-start | bytes 196616 | tf_op jit(solution)/shard_map/ppermute | solution.py:35
  40.3 5.4 %collective-permute-start.14 = (bf16[128,2048]{1,0:T(8,128)(2,1)S(1)}, bf16[128,2048]{1,0:T(8,128)(2,1)S(1)}, u32[]{:S(2)}, u32[]{:S(2)}) collective-permute-start(bf16[128,2048]{1,0:T(8,128)(2,1)S(1)} %up_product_after.2.mine.pre_mine), channel_id=1, source_target_pairs={{0,1},{1,0},{2,3},{3,2},{4,5},{5,4},{6,7},{7,6},{8,9},{9,8},{10,11... | collective-permute-start | bytes 1572872 | tf_op jit(solution)/shard_map/ppermute | solution.py:26
  46.4 5.2 %collective-permute-start.15 = (bf16[32,1024]{1,0:T(8,128)(2,1)S(1)}, bf16[32,1024]{1,0:T(8,128)(2,1)S(1)}, u32[]{:S(2)}, u32[]{:S(2)}) collective-permute-start(bf16[32,1024]{1,0:T(8,128)(2,1)S(1)} %get-tuple-element.128), channel_id=1, source_target_pairs={{0,6},{2,4},{4,2},{6,0},{1,7},{3,5},{5,3},{7,1},{8,14},{10,12},{12... | collective-permute-start | bytes 196616 | tf_op jit(solution)/shard_map/ppermute | solution.py:35
  47.6 7.5 %collective-permute-start.16 = (bf16[32,1024]{1,0:T(8,128)(2,1)S(1)}, bf16[32,1024]{1,0:T(8,128)(2,1)S(1)}, u32[]{:S(2)}, u32[]{:S(2)}) collective-permute-start(bf16[32,1024]{1,0:T(8,128)(2,1)S(1)} %get-tuple-element.129), channel_id=1, source_target_pairs={{0,4},{2,6},{4,0},{6,2},{1,5},{3,7},{5,1},{7,3},{8,12},{10,14},{12... | collective-permute-start | bytes 196616 | tf_op jit(solution)/shard_map/ppermute | solution.py:35
  47.6 7.5 %collective-permute-start.17 = (bf16[32,1024]{1,0:T(8,128)(2,1)S(1)}, bf16[32,1024]{1,0:T(8,128)(2,1)S(1)}, u32[]{:S(2)}, u32[]{:S(2)}) collective-permute-start(bf16[32,1024]{1,0:T(8,128)(2,1)S(1)} %get-tuple-element.130), channel_id=1, source_target_pairs={{0,2},{2,0},{4,6},{6,4},{1,3},{3,1},{5,7},{7,5},{8,10},{10,8},{12,... | collective-permute-start | bytes 196616 | tf_op jit(solution)/shard_map/ppermute | solution.py:35
  55.2 5.9 %collective-permute-start.19 = (bf16[32,1024]{1,0:T(8,128)(2,1)S(1)}, bf16[32,1024]{1,0:T(8,128)(2,1)S(1)}, u32[]{:S(2)}, u32[]{:S(2)}) collective-permute-start(bf16[32,1024]{1,0:T(8,128)(2,1)S(1)} %get-tuple-element.139), channel_id=1, source_target_pairs={{8,16},{16,8},{9,17},{17,9},{10,18},{18,10},{11,19},{19,11},{12,20... | collective-permute-start | bytes 196616 | tf_op jit(solution)/shard_map/ppermute | solution.py:20
  58.3 3.5 %collective-permute-start.18 = (bf16[32,1024]{1,0:T(8,128)(2,1)S(1)}, bf16[32,1024]{1,0:T(8,128)(2,1)S(1)}, u32[]{:S(2)}, u32[]{:S(2)}) collective-permute-start(bf16[32,1024]{1,0:T(8,128)(2,1)S(1)} %get-tuple-element.139), channel_id=1, source_target_pairs={{0,8},{8,0},{16,24},{24,16},{1,9},{9,1},{17,25},{25,17},{2,10},{10... | collective-permute-start | bytes 196616 | tf_op jit(solution)/shard_map/ppermute | solution.py:20
  58.3 7.0 %collective-permute-start.20 = (bf16[32,1024]{1,0:T(8,128)(2,1)S(1)}, bf16[32,1024]{1,0:T(8,128)(2,1)S(1)}, u32[]{:S(2)}, u32[]{:S(2)}) collective-permute-start(bf16[32,1024]{1,0:T(8,128)(2,1)S(1)} %get-tuple-element.143.refs_0_.first), channel_id=1, source_target_pairs={{0,6},{2,4},{4,2},{6,0},{1,7},{3,5},{5,3},{7,1},{8,14},{10,12},{12... | collective-permute-start | bytes 196616 | tf_op jit(solution)/shard_map/ppermute | solution.py:35
  61.8 4.4 %collective-permute-start.23 = (bf16[32,1024]{1,0:T(8,128)(2,1)S(1)}, bf16[32,1024]{1,0:T(8,128)(2,1)S(1)}, u32[]{:S(2)}, u32[]{:S(2)}) collective-permute-start(bf16[32,1024]{1,0:T(8,128)(2,1)S(1)} %arrive.3.refs_0_.first_out.refs_14_), channel_id=1, source_target_pairs={{0,2},{2,0},{4,6},{6,4},{1,3},{3,1},{5,7},{7,5},{8,10},{10,8},{12,... | collective-permute-start | bytes 196616 | tf_op jit(solution)/shard_map/ppermute | solution.py:35
  61.9 4.3 %collective-permute-start.22 = (bf16[32,1024]{1,0:T(8,128)(2,1)S(1)}, bf16[32,1024]{1,0:T(8,128)(2,1)S(1)}, u32[]{:S(2)}, u32[]{:S(2)}) collective-permute-start(bf16[32,1024]{1,0:T(8,128)(2,1)S(1)} %arrive.3.refs_0_.first_out.refs_14_), channel_id=1, source_target_pairs={{0,4},{2,6},{4,0},{6,2},{1,5},{3,7},{5,1},{7,3},{8,12},{10,14},{12... | collective-permute-start | bytes 196616 | tf_op jit(solution)/shard_map/ppermute | solution.py:35
  63.2 5.2 %collective-permute-start.21 = (bf16[32,1024]{1,0:T(8,128)(2,1)S(1)}, bf16[32,1024]{1,0:T(8,128)(2,1)S(1)}, u32[]{:S(2)}, u32[]{:S(2)}) collective-permute-start(bf16[32,1024]{1,0:T(8,128)(2,1)S(1)} %arrive.3.refs_0_.first_out.refs_14_), channel_id=1, source_target_pairs={{0,6},{2,4},{4,2},{6,0},{1,7},{3,5},{5,3},{7,1},{8,14},{10,12},{12... | collective-permute-start | bytes 196616 | tf_op jit(solution)/shard_map/ppermute | solution.py:35
  69.2 4.7 %collective-permute-start.25 = (bf16[128,2048]{1,0:T(8,128)(2,1)S(1)}, bf16[128,2048]{1,0:T(8,128)(2,1)S(1)}, u32[]{:S(2)}, u32[]{:S(2)}) collective-permute-start(bf16[128,2048]{1,0:T(8,128)(2,1)S(1)} %up_product_after.3.pre_mine.mine), channel_id=1, source_target_pairs={{0,1},{1,0},{2,3},{3,2},{4,5},{5,4},{6,7},{7,6},{8,9},{9,8},{10,11... | collective-permute-start | bytes 1572872 | tf_op jit(solution)/shard_map/ppermute | solution.py:26
  73.1 2.0 %collective-permute-start.24 = (bf16[128,2048]{1,0:T(8,128)(2,1)S(1)}, bf16[128,2048]{1,0:T(8,128)(2,1)S(1)}, u32[]{:S(2)}, u32[]{:S(2)}) collective-permute-start(bf16[128,2048]{1,0:T(8,128)(2,1)S(1)} %get-tuple-element.147.mine), channel_id=1, source_target_pairs={{0,1},{1,0},{2,3},{3,2},{4,5},{5,4},{6,7},{7,6},{8,9},{9,8},{10,11... | collective-permute-start | bytes 1572872 | tf_op jit(solution)/shard_map/ppermute | solution.py:26
  76.1 5.4 %collective-permute-start.26 = (bf16[32,1024]{1,0:T(8,128)(2,1)S(1)}, bf16[32,1024]{1,0:T(8,128)(2,1)S(1)}, u32[]{:S(2)}, u32[]{:S(2)}) collective-permute-start(bf16[32,1024]{1,0:T(8,128)(2,1)S(1)} %get-tuple-element.149), channel_id=1, source_target_pairs={{0,6},{2,4},{4,2},{6,0},{1,7},{3,5},{5,3},{7,1},{8,14},{10,12},{12... | collective-permute-start | bytes 196616 | tf_op jit(solution)/shard_map/ppermute | solution.py:35
  78.2 6.6 %collective-permute-start.27 = (bf16[32,1024]{1,0:T(8,128)(2,1)S(1)}, bf16[32,1024]{1,0:T(8,128)(2,1)S(1)}, u32[]{:S(2)}, u32[]{:S(2)}) collective-permute-start(bf16[32,1024]{1,0:T(8,128)(2,1)S(1)} %get-tuple-element.150), channel_id=1, source_target_pairs={{0,4},{2,6},{4,0},{6,2},{1,5},{3,7},{5,1},{7,3},{8,12},{10,14},{12... | collective-permute-start | bytes 196616 | tf_op jit(solution)/shard_map/ppermute | solution.py:35
  78.2 6.6 %collective-permute-start.28 = (bf16[32,1024]{1,0:T(8,128)(2,1)S(1)}, bf16[32,1024]{1,0:T(8,128)(2,1)S(1)}, u32[]{:S(2)}, u32[]{:S(2)}) collective-permute-start(bf16[32,1024]{1,0:T(8,128)(2,1)S(1)} %get-tuple-element.151), channel_id=1, source_target_pairs={{0,2},{2,0},{4,6},{6,4},{1,3},{3,1},{5,7},{7,5},{8,10},{10,8},{12,... | collective-permute-start | bytes 196616 | tf_op jit(solution)/shard_map/ppermute | solution.py:35
  84.8 5.9 %collective-permute-start.30 = (bf16[32,1024]{1,0:T(8,128)(2,1)S(1)}, bf16[32,1024]{1,0:T(8,128)(2,1)S(1)}, u32[]{:S(2)}, u32[]{:S(2)}) collective-permute-start(bf16[32,1024]{1,0:T(8,128)(2,1)S(1)} %leave_back.2.refs_11_), channel_id=1, source_target_pairs={{8,16},{16,8},{9,17},{17,9},{10,18},{18,10},{11,19},{19,11},{12,20... | collective-permute-start | bytes 196616 | tf_op jit(solution)/shard_map/ppermute | solution.py:20
  88.1 3.5 %collective-permute-start.29 = (bf16[32,1024]{1,0:T(8,128)(2,1)S(1)}, bf16[32,1024]{1,0:T(8,128)(2,1)S(1)}, u32[]{:S(2)}, u32[]{:S(2)}) collective-permute-start(bf16[32,1024]{1,0:T(8,128)(2,1)S(1)} %leave_back.2.refs_11_), channel_id=1, source_target_pairs={{0,8},{8,0},{16,24},{24,16},{1,9},{9,1},{17,25},{25,17},{2,10},{10... | collective-permute-start | bytes 196616 | tf_op jit(solution)/shard_map/ppermute | solution.py:20
  89.2 6.1 %collective-permute-start.31 = (bf16[32,1024]{1,0:T(8,128)(2,1)S(1)}, bf16[32,1024]{1,0:T(8,128)(2,1)S(1)}, u32[]{:S(2)}, u32[]{:S(2)}) collective-permute-start(bf16[32,1024]{1,0:T(8,128)(2,1)S(1)} %get-tuple-element.167), channel_id=1, source_target_pairs={{0,4},{2,6},{4,0},{6,2},{1,5},{3,7},{5,1},{7,3},{8,12},{10,14},{12... | collective-permute-start | bytes 196616 | tf_op jit(solution)/shard_map/ppermute | solution.py:35
  91.6 4.5 %collective-permute-start.34 = (bf16[32,1024]{1,0:T(8,128)(2,1)S(1)}, bf16[32,1024]{1,0:T(8,128)(2,1)S(1)}, u32[]{:S(2)}, u32[]{:S(2)}) collective-permute-start(bf16[32,1024]{1,0:T(8,128)(2,1)S(1)} %arrive_back.2.refs_0_.first), channel_id=1, source_target_pairs={{0,2},{2,0},{4,6},{6,4},{1,3},{3,1},{5,7},{7,5},{8,10},{10,8},{12,... | collective-permute-start | bytes 196616 | tf_op jit(solution)/shard_map/ppermute | solution.py:35
  91.7 4.4 %collective-permute-start.33 = (bf16[32,1024]{1,0:T(8,128)(2,1)S(1)}, bf16[32,1024]{1,0:T(8,128)(2,1)S(1)}, u32[]{:S(2)}, u32[]{:S(2)}) collective-permute-start(bf16[32,1024]{1,0:T(8,128)(2,1)S(1)} %arrive_back.2.refs_0_.first), channel_id=1, source_target_pairs={{0,4},{2,6},{4,0},{6,2},{1,5},{3,7},{5,1},{7,3},{8,12},{10,14},{12... | collective-permute-start | bytes 196616 | tf_op jit(solution)/shard_map/ppermute | solution.py:35
  94.0 5.4 %collective-permute-start.32 = (bf16[32,1024]{1,0:T(8,128)(2,1)S(1)}, bf16[32,1024]{1,0:T(8,128)(2,1)S(1)}, u32[]{:S(2)}, u32[]{:S(2)}) collective-permute-start(bf16[32,1024]{1,0:T(8,128)(2,1)S(1)} %arrive_back.2.refs_0_.first), channel_id=1, source_target_pairs={{0,6},{2,4},{4,2},{6,0},{1,7},{3,5},{5,3},{7,1},{8,14},{10,12},{12... | collective-permute-start | bytes 196616 | tf_op jit(solution)/shard_map/ppermute | solution.py:35
  100.2 4.4 %collective-permute-start.35 = (bf16[128,2048]{1,0:T(8,128)(2,1)S(1)}, bf16[128,2048]{1,0:T(8,128)(2,1)S(1)}, u32[]{:S(2)}, u32[]{:S(2)}) collective-permute-start(bf16[128,2048]{1,0:T(8,128)(2,1)S(1)} %get-tuple-element.168.mine), channel_id=1, source_target_pairs={{0,1},{1,0},{2,3},{3,2},{4,5},{5,4},{6,7},{7,6},{8,9},{9,8},{10,11... | collective-permute-start | bytes 1572872 | tf_op jit(solution)/shard_map/ppermute | solution.py:26
  105.6 5.1 %collective-permute-start.36 = (bf16[32,1024]{1,0:T(8,128)(2,1)S(1)}, bf16[32,1024]{1,0:T(8,128)(2,1)S(1)}, u32[]{:S(2)}, u32[]{:S(2)}) collective-permute-start(bf16[32,1024]{1,0:T(8,128)(2,1)S(1)} %get-tuple-element.170), channel_id=1, source_target_pairs={{0,6},{2,4},{4,2},{6,0},{1,7},{3,5},{5,3},{7,1},{8,14},{10,12},{12... | collective-permute-start | bytes 196616 | tf_op jit(solution)/shard_map/ppermute | solution.py:35
  107.0 7.3 %collective-permute-start.37 = (bf16[32,1024]{1,0:T(8,128)(2,1)S(1)}, bf16[32,1024]{1,0:T(8,128)(2,1)S(1)}, u32[]{:S(2)}, u32[]{:S(2)}) collective-permute-start(bf16[32,1024]{1,0:T(8,128)(2,1)S(1)} %get-tuple-element.171), channel_id=1, source_target_pairs={{0,4},{2,6},{4,0},{6,2},{1,5},{3,7},{5,1},{7,3},{8,12},{10,14},{12... | collective-permute-start | bytes 196616 | tf_op jit(solution)/shard_map/ppermute | solution.py:35
  107.0 7.3 %collective-permute-start.38 = (bf16[32,1024]{1,0:T(8,128)(2,1)S(1)}, bf16[32,1024]{1,0:T(8,128)(2,1)S(1)}, u32[]{:S(2)}, u32[]{:S(2)}) collective-permute-start(bf16[32,1024]{1,0:T(8,128)(2,1)S(1)} %get-tuple-element.172), channel_id=1, source_target_pairs={{0,2},{2,0},{4,6},{6,4},{1,3},{3,1},{5,7},{7,5},{8,10},{10,8},{12,... | collective-permute-start | bytes 196616 | tf_op jit(solution)/shard_map/ppermute | solution.py:35
  114.4 5.9 %collective-permute-start.40 = (bf16[32,1024]{1,0:T(8,128)(2,1)S(1)}, bf16[32,1024]{1,0:T(8,128)(2,1)S(1)}, u32[]{:S(2)}, u32[]{:S(2)}) collective-permute-start(bf16[32,1024]{1,0:T(8,128)(2,1)S(1)} %leave_back.3.refs_10_), channel_id=1, source_target_pairs={{8,16},{16,8},{9,17},{17,9},{10,18},{18,10},{11,19},{19,11},{12,20... | collective-permute-start | bytes 196616 | tf_op jit(solution)/shard_map/ppermute | solution.py:20
  117.4 3.5 %collective-permute-start.39 = (bf16[32,1024]{1,0:T(8,128)(2,1)S(1)}, bf16[32,1024]{1,0:T(8,128)(2,1)S(1)}, u32[]{:S(2)}, u32[]{:S(2)}) collective-permute-start(bf16[32,1024]{1,0:T(8,128)(2,1)S(1)} %leave_back.3.refs_10_), channel_id=1, source_target_pairs={{0,8},{8,0},{16,24},{24,16},{1,9},{9,1},{17,25},{25,17},{2,10},{10... | collective-permute-start | bytes 196616 | tf_op jit(solution)/shard_map/ppermute | solution.py:20
  117.5 7.0 %collective-permute-start.41 = (bf16[32,1024]{1,0:T(8,128)(2,1)S(1)}, bf16[32,1024]{1,0:T(8,128)(2,1)S(1)}, u32[]{:S(2)}, u32[]{:S(2)}) collective-permute-start(bf16[32,1024]{1,0:T(8,128)(2,1)S(1)} %get-tuple-element.179), channel_id=1, source_target_pairs={{0,6},{2,4},{4,2},{6,0},{1,7},{3,5},{5,3},{7,1},{8,14},{10,12},{12... | collective-permute-start | bytes 196616 | tf_op jit(solution)/shard_map/ppermute | solution.py:35
  120.9 4.3 %collective-permute-start.44 = (bf16[32,1024]{1,0:T(8,128)(2,1)S(1)}, bf16[32,1024]{1,0:T(8,128)(2,1)S(1)}, u32[]{:S(2)}, u32[]{:S(2)}) collective-permute-start(bf16[32,1024]{1,0:T(8,128)(2,1)S(1)} %arrive_back.3.refs_0_.first_grad), channel_id=1, source_target_pairs={{0,2},{2,0},{4,6},{6,4},{1,3},{3,1},{5,7},{7,5},{8,10},{10,8},{12,... | collective-permute-start | bytes 196616 | tf_op jit(solution)/shard_map/ppermute | solution.py:35
  121.0 4.2 %collective-permute-start.43 = (bf16[32,1024]{1,0:T(8,128)(2,1)S(1)}, bf16[32,1024]{1,0:T(8,128)(2,1)S(1)}, u32[]{:S(2)}, u32[]{:S(2)}) collective-permute-start(bf16[32,1024]{1,0:T(8,128)(2,1)S(1)} %arrive_back.3.refs_0_.first_grad), channel_id=1, source_target_pairs={{0,4},{2,6},{4,0},{6,2},{1,5},{3,7},{5,1},{7,3},{8,12},{10,14},{12... | collective-permute-start | bytes 196616 | tf_op jit(solution)/shard_map/ppermute | solution.py:35
  122.6 5.0 %collective-permute-start.42 = (bf16[32,1024]{1,0:T(8,128)(2,1)S(1)}, bf16[32,1024]{1,0:T(8,128)(2,1)S(1)}, u32[]{:S(2)}, u32[]{:S(2)}) collective-permute-start(bf16[32,1024]{1,0:T(8,128)(2,1)S(1)} %arrive_back.3.refs_0_.first_grad), channel_id=1, source_target_pairs={{0,6},{2,4},{4,2},{6,0},{1,7},{3,5},{5,3},{7,1},{8,14},{10,12},{12... | collective-permute-start | bytes 196616 | tf_op jit(solution)/shard_map/ppermute | solution.py:35
  128.3 5.4 %collective-permute-start.45 = (bf16[128,2048]{1,0:T(8,128)(2,1)S(1)}, bf16[128,2048]{1,0:T(8,128)(2,1)S(1)}, u32[]{:S(2)}, u32[]{:S(2)}) collective-permute-start(bf16[128,2048]{1,0:T(8,128)(2,1)S(1)} %get-tuple-element.180.mine), channel_id=1, source_target_pairs={{0,1},{1,0},{2,3},{3,2},{4,5},{5,4},{6,7},{7,6},{8,9},{9,8},{10,11... | collective-permute-start | bytes 1572872 | tf_op jit(solution)/shard_map/ppermute | solution.py:26
  134.8 10.1 %collective-permute-start.47 = (bf16[32,1024]{1,0:T(8,128)(2,1)S(1)}, bf16[32,1024]{1,0:T(8,128)(2,1)S(1)}, u32[]{:S(2)}, u32[]{:S(2)}) collective-permute-start(bf16[32,1024]{1,0:T(8,128)(2,1)S(1)} %get-tuple-element.186), channel_id=1, source_target_pairs={{0,6},{2,4},{4,2},{6,0},{1,7},{3,5},{5,3},{7,1},{8,14},{10,12},{12... | collective-permute-start | bytes 196616 | tf_op jit(solution)/shard_map/ppermute | solution.py:35
  136.8 8.1 %collective-permute-start.48 = (bf16[32,1024]{1,0:T(8,128)(2,1)S(1)}, bf16[32,1024]{1,0:T(8,128)(2,1)S(1)}, u32[]{:S(2)}, u32[]{:S(2)}) collective-permute-start(bf16[32,1024]{1,0:T(8,128)(2,1)S(1)} %get-tuple-element.187), channel_id=1, source_target_pairs={{0,4},{2,6},{4,0},{6,2},{1,5},{3,7},{5,1},{7,3},{8,12},{10,14},{12... | collective-permute-start | bytes 196616 | tf_op jit(solution)/shard_map/ppermute | solution.py:35
  136.8 8.1 %collective-permute-start.49 = (bf16[32,1024]{1,0:T(8,128)(2,1)S(1)}, bf16[32,1024]{1,0:T(8,128)(2,1)S(1)}, u32[]{:S(2)}, u32[]{:S(2)}) collective-permute-start(bf16[32,1024]{1,0:T(8,128)(2,1)S(1)} %get-tuple-element.188), channel_id=1, source_target_pairs={{0,2},{2,0},{4,6},{6,4},{1,3},{3,1},{5,7},{7,5},{8,10},{10,8},{12,... | collective-permute-start | bytes 196616 | tf_op jit(solution)/shard_map/ppermute | solution.py:35
  138.4 6.5 %collective-permute-start.46 = (bf16[32,1024]{1,0:T(8,128)(2,1)S(1)}, bf16[32,1024]{1,0:T(8,128)(2,1)S(1)}, u32[]{:S(2)}, u32[]{:S(2)}) collective-permute-start(bf16[32,1024]{1,0:T(8,128)(2,1)S(1)} %get-tuple-element.189), channel_id=1, source_target_pairs={{0,2},{2,0},{4,6},{6,4},{1,3},{3,1},{5,7},{7,5},{8,10},{10,8},{12,... | collective-permute-start | bytes 196616 | tf_op jit(solution)/shard_map/ppermute | solution.py:35

commit v10 on v9

--- a/solution.py
+++ b/solution.py
@@ -12,13 +12,9 @@
 WEIGHT_CUTS = 8
 
 
-def hand_over(block):
-    count = lax.axis_size("section")
-    within = [(s, s ^ 1) for s in range(count)]
-    across = [(s, s + 1 if s % 2 else s - 1) for s in range(count)]
-    return [
-        lax.ppermute(block, "section", [(s, t) for s, t in pairs if 0 <= t < count]) for pairs in (within, across)
-    ]
+def hand_over(block, distance):
+    sections = range(lax.axis_size("section"))
+    return lax.ppermute(block, "section", [(i - distance, i) for i in sections if i - distance in sections])
 
 
 def turn(block, axis, distance):
@@ -45,7 +41,7 @@
 
 def beside(turn):
     size = lax.axis_size("row")
-    return [[size - 1], [size - 2], range(1, size - 2)][turn] if size > 2 else [[], [], [1]][turn]
+    return [[size - 1, size - 2], list(range(1, size - 2))][turn] if size > 2 else [[], [1]][turn]
 
 
 def after(block, other):
@@ -56,7 +52,7 @@
     return [pl.BlockSpec(memory_space=pltpu.VMEM)] * count
 
 
-def run(kernel, outs, *ins, flops=0, scratch=()):
+def run(kernel, outs, *ins, flops=0, scratch=(), name=None):
     ins = [pltpu.with_memory_space_constraint(block, pltpu.VMEM) for block in ins]
     size = sum(x.size * x.dtype.itemsize for x in [*ins, *outs])
     return pl.pallas_call(
@@ -67,7 +63,7 @@
         scratch_shapes=scratch,
         compiler_params=pltpu.CompilerParams(vmem_limit_bytes=6 << 20),
         cost_estimate=pl.CostEstimate(flops=flops, bytes_accessed=size, transcendentals=0),
-        name=kernel.__name__,
+        name=name or kernel.__name__,
     )(*ins)
 
 
@@ -154,14 +150,8 @@
     return total.astype(BF)
 
 
-def arrive(base, within, across, out):
-    odd = lax.axis_index("section") % 2 == 1
-    out[...] = added(base, [jnp.where(odd, within[...], across[...])])
-
-
-def arrive_back(base, within, across, out):
-    odd = lax.axis_index("section") % 2 == 1
-    out[...] = added(base, [jnp.where(odd, across[...], within[...])])
+def arrive(base, arrived, out):
+    out[...] = added(base, [arrived])
 
 
 def leave(first, *refs):
@@ -229,24 +219,31 @@
     return [slice(n, n + step) for n in range(0, width, step)]
 
 
-def up_product_after(_, *refs):
-    up_product(*refs)
-
-
-def back_product_after(_, *refs):
-    back_product(*refs)
-
-
-def up_product(*refs):
-    *pieces, weight, product, whole = refs
+def product_part(part, whole, weight, product):
+    for n in columns(product.shape[1]):
+        product[:, n] = matmul(whole[...], weight[:, n.start + part.start : n.stop + part.start]).astype(BF)
+
+
+def stack_product(part, skip, *refs):
+    *pieces, weight, whole, product = refs[skip:]
     whole[...] = jnp.concatenate([piece[...] for piece in pieces], axis=0)
-    for n in columns(product.shape[1]):
-        product[:, n] = matmul(whole[...], weight[:, n]).astype(BF)
-
-
-def back_product(*refs):
-    *ins, whole, product = refs
-    up_product(*ins, product, whole)
+    product_part(part, whole, weight, product)
+
+
+def products(parts, pieces, weight, waited=()):
+    tokens, width = len(pieces) * pieces[0].shape[0], weight.shape[0]
+    whole_like = jax.ShapeDtypeStruct((tokens, width), BF)
+    likes = [jax.ShapeDtypeStruct((tokens, part.stop - part.start), BF) for part in parts]
+    flops = 2 * tokens * width * likes[0].shape[1]
+    whole, first = run(
+        functools.partial(stack_product, parts[0], len(waited)), [whole_like, likes[0]],
+        *waited, *pieces, weight, flops=flops, name="stack_product",
+    )
+    rest = [
+        run(functools.partial(product_part, part), [like], whole, weight, flops=flops, name="product_part")[0]
+        for part, like in zip(parts[1:], likes[1:])
+    ]
+    return whole, [first, *rest]
 
 
 def put_rows(pieces, n, product):
@@ -255,78 +252,110 @@
         piece[:, n] = product[j * rows : (j + 1) * rows].astype(BF)
 
 
-def down_product(mine, other, weight, act, *pieces):
+def silu_part(mine, other, act):
     for n in columns(act.shape[1]):
         pre = mine[:, n].astype(F32) + other[:, n].astype(F32)
         act[:, n] = jax.nn.silu(pre).astype(BF)
-    for n in columns(weight.shape[1]):
-        put_rows(pieces, n, matmul(act[...], weight[:, n]))
-
-
-def down_again(act, weight, *pieces):
-    for n in columns(weight.shape[1]):
-        put_rows(pieces, n, matmul(act[...], weight[:, n]))
-
-
-def in_product(mine, other, pre_mine, pre_other, weight, grad_pre, *pieces):
+
+
+def slope_part(mine, other, pre_mine, pre_other, grad_pre):
     for n in columns(grad_pre.shape[1]):
         pre = pre_mine[:, n].astype(F32) + pre_other[:, n].astype(F32)
         grad = mine[:, n].astype(F32) + other[:, n].astype(F32)
         grad_pre[:, n] = (grad * silu_slope(pre)).astype(BF)
+
+
+def first_part(pointwise, part, *refs):
+    *ins, weight, hidden, total = refs
+    pointwise(*ins, hidden)
     for n in columns(weight.shape[1]):
-        put_rows(pieces, n, matmul(grad_pre[...], weight[:, n]))
-
-
-def act_only(mine, other, act):
-    for n in columns(act.shape[1]):
-        pre = mine[:, n].astype(F32) + other[:, n].astype(F32)
-        act[:, n] = jax.nn.silu(pre).astype(BF)
-
-
-def weight_grad(first, last, *refs):
+        total[:, n] = matmul(hidden[...], weight[part, n])
+
+
+def last_part(pointwise, part, count, *refs):
+    *ins, weight, total, hidden = refs[:-count]
+    pointwise(*ins, hidden)
+    for n in columns(weight.shape[1]):
+        put_rows(refs[-count:], n, total[:, n] + matmul(hidden[...], weight[part, n]))
+
+
+def through(pointwise, name, parts, ins, weight, piece_like, rows):
+    tokens, width = rows * piece_like.shape[0], piece_like.shape[1]
+    (first, last), done = parts, []
+    flops = 2 * tokens * width * (first.stop - first.start)
+    like = [jax.ShapeDtypeStruct((tokens, part.stop - part.start), BF) for part in parts]
+    hidden, total = run(
+        functools.partial(first_part, pointwise, first),
+        [like[0], jax.ShapeDtypeStruct((tokens, width), F32)],
+        *ins[0], weight, flops=flops, name=name,
+    )
+    rest, *pieces = run(
+        functools.partial(last_part, pointwise, last, rows),
+        [like[1]] + [piece_like] * rows,
+        *ins[1], weight, total, flops=flops, name=name,
+    )
+    return [hidden, rest], pieces
+
+
+def both_silu(*refs):
+    *ins, first, last = refs
+    silu_part(*ins[:2], first)
+    silu_part(*ins[2:], last)
+
+
+def down_again(parts, first, last, weight, *pieces):
+    for n in columns(weight.shape[1]):
+        total = matmul(first[...], weight[parts[0], n]) + matmul(last[...], weight[parts[1], n])
+        put_rows(pieces, n, total)
+
+
+def weight_grad(start, count, *refs):
     *blocks, out, left, right, room, sems = refs
-    if first:
-        blocks = blocks[:-1]
-    count = len(blocks) // 2
-    depth = blocks[-1].shape[0]
+    lefts, rights = blocks[:count], blocks[count:]
+    if start:
+        rights = rights[:-1]
+    depth = rights[0].shape[0]
     for t in range(count):
-        left[:, t * depth : (t + 1) * depth] = blocks[t][first:last, :]
-        right[t * depth : (t + 1) * depth, :] = blocks[count + t][...]
+        left[:, t * depth : (t + 1) * depth] = lefts[t][...]
+        place = 0
+        for block in rights[t * len(rights) // count : (t + 1) * len(rights) // count]:
+            right[t * depth : (t + 1) * depth, place : place + block.shape[1]] = block[...]
+            place += block.shape[1]
     copies = []
-    for i, m in enumerate(columns(last - first)):
+    for i, m in enumerate(columns(left.shape[0])):
         for n in columns(out.shape[1]):
             room[m, n] = matmul(left[m, :], right[:, n]).astype(BF)
         size = m.stop - m.start
         copies.append(
-            pltpu.make_async_copy(room.at[pl.ds(m.start, size)], out.at[pl.ds(first + m.start, size)], sems.at[i])
+            pltpu.make_async_copy(room.at[pl.ds(m.start, size)], out.at[pl.ds(start + m.start, size)], sems.at[i])
         )
         copies[-1].start()
     for copy in copies:
         copy.wait()
 
 
-def weight_product(lefts, rights, first, last, begun=None):
-    rows, width, depth = lefts[0].shape[0], rights[0].shape[1], rights[0].shape[0] * len(rights)
-    count = last - first
+def weight_product(lefts, rights, shape, start=0, begun=None):
+    count, depth = lefts[0].shape[0], rights[0].shape[0] * len(lefts)
+    ins = [*lefts, *rights]
     return pl.pallas_call(
-        functools.partial(weight_grad, first, last),
-        in_specs=vmem(len(lefts) + len(rights)) + [pl.BlockSpec(memory_space=pl.ANY)] * (begun is not None),
+        functools.partial(weight_grad, start, len(lefts)),
+        in_specs=vmem(len(ins)) + [pl.BlockSpec(memory_space=pl.ANY)] * (begun is not None),
         out_specs=pl.BlockSpec(memory_space=pl.ANY),
-        out_shape=jax.ShapeDtypeStruct((rows, width), BF),
+        out_shape=jax.ShapeDtypeStruct(shape, BF),
         scratch_shapes=[
             pltpu.VMEM((count, depth), BF),
-            pltpu.VMEM((depth, width), BF),
-            pltpu.VMEM((count, width), BF),
+            pltpu.VMEM((depth, shape[1]), BF),
+            pltpu.VMEM((count, shape[1]), BF),
             pltpu.SemaphoreType.DMA((len(columns(count)),)),
         ],
-        input_output_aliases={} if begun is None else {len(lefts) + len(rights): 0},
+        input_output_aliases={} if begun is None else {len(ins): 0},
         compiler_params=pltpu.CompilerParams(vmem_limit_bytes=12 << 20),
         cost_estimate=pl.CostEstimate(
-            flops=2 * count * width * depth, bytes_accessed=2 * count * width, transcendentals=0
+            flops=2 * count * shape[1] * depth, bytes_accessed=2 * count * shape[1], transcendentals=0
         ),
         name="weight_grad",
     )(
-        *[pltpu.with_memory_space_constraint(x, pltpu.VMEM) for x in (*lefts, *rights)],
+        *[pltpu.with_memory_space_constraint(x, pltpu.VMEM) for x in ins],
         *([] if begun is None else [begun]),
     )
 
@@ -352,46 +381,42 @@
     rows = lax.axis_size("row")
     piece_rows, width = inputs.shape[2:]
     tokens, hidden = rows * piece_rows, w_up.shape[2]
-    flops = 2 * tokens * width * hidden
+    parts = [slice(0, hidden // 2), slice(hidden // 2, hidden)]
     piece_like = jax.ShapeDtypeStruct((piece_rows, width), BF)
-    whole_like = jax.ShapeDtypeStruct((tokens, width), BF)
-    hidden_like = jax.ShapeDtypeStruct((tokens, hidden), BF)
+    part_like = jax.ShapeDtypeStruct((tokens, hidden // 2), BF)
     turned_like = jax.ShapeDtypeStruct((width, tokens), BF)
-    turned_hidden = jax.ShapeDtypeStruct((hidden, tokens), BF)
-    split_like = [hidden_like] + [piece_like] * rows
-    room = [pltpu.VMEM((tokens, width), BF)]
+    turned_part = jax.ShapeDtypeStruct((hidden // 2, tokens), BF)
+
+    def turn_blocks(tick, other):
+        turned_ins.extend(run(turned, [turned_like], after(full_ins[tick], other)))
+        for k in range(2):
+            turned_acts[k].extend(run(turned, [turned_part], after(acts[tick][k], other)))
 
     act_in, last_cot = first_pieces(inputs, cotangent)
     cot_pieces = [last_cot] + [None] * (rows - 1)
-    in_pieces, acts, pres, seen_in, seen_out = [], [], [], [], []
-    turned_ins, turned_acts = [], []
+    full_ins, acts, pres, seen_in, seen_out = [], [], [], [], []
+    turned_ins, turned_acts = [], [[], []]
     for tick in range(ticks):
+        waited = []
         if tick:
-            (act_in,) = run(arrive, [piece_like], bases[tick - 1], *hand_over(sending))
-            (j,) = beside(tick)
-            cot_pieces[j] = swap_rows(after(cot_pieces[0], sending), j)
+            act_in = run(arrive, [piece_like], bases[tick - 1], hand_over(sending, 1))[0]
+            for j in beside(tick - 1):
+                cot_pieces[j] = swap_rows(after(last_cot, sending), j)
+                waited.append(cot_pieces[j])
         pieces = gather_rows(act_in)
         if tick == 0:
-            for j in beside(0):
-                cot_pieces[j] = swap_rows(after(cot_pieces[0], act_in), j)
             stored, bases, cots, up_kept = fetch(
                 after(sample_ids, act_in), inputs, send_base, recv_base, cotangent, w_up[0]
             )
-            pieces = after(pieces, ([cot_pieces[j] for j in beside(0)], stored))
-        if tick:
-            (partial,) = run(
-                up_product_after, [hidden_like], cot_pieces[j], *pieces, up_kept, flops=flops, scratch=room
-            )
+            pieces = after(pieces, stored)
+        full_in, partial = products(parts, pieces, up_kept, waited)
+        if tick == 0:
+            down_kept = hold(after(w_down[0], partial[-1]))
+        pre = [(mine, other_cols(mine)) for mine in partial]
+        if tick == ticks - 1:
+            full_cot, first_grads = products(parts, after(cot_pieces, partial[-1]), down_turned)
         else:
-            (partial,) = run(up_product, [hidden_like], *pieces, up_kept, flops=flops, scratch=room)
-            down_kept = hold(after(w_down[0], partial))
-        other = other_cols(partial)
-        if tick == ticks - 1:
-            full_cot, first_grads = run(
-                back_product, [whole_like, hidden_like], *after(cot_pieces, partial), down_turned, flops=flops
-            )
-        if tick < ticks - 1:
-            act, *terms = run(down_product, split_like, partial, other, down_kept, flops=flops)
+            act, terms = through(silu_part, "down_part", parts, pre, down_kept, piece_like, rows)
             acts.append(act)
             terms_in = scatter_rows(terms)
             if tick == 0:
@@ -401,57 +426,50 @@
                 terms_in[0] = after(terms_in[0], down_turned)
             if tick == 1:
                 (up_turned,) = run(turned_weight, [jax.ShapeDtypeStruct((hidden, width), BF)], after(up_kept, terms))
-                turned_ins += run(turned, [turned_like], *after(in_pieces[0], terms))
-                turned_acts += run(turned, [turned_hidden], after(acts[0], terms))
+                turn_blocks(0, terms)
                 terms_in[0] = after(terms_in[0], (up_turned, turned_ins, turned_acts))
             act_out, sending = run(leave, [piece_like] * 2, act_in, *terms_in, stored[tick])
             seen_out.append(act_out)
-        in_pieces.append(pieces)
-        pres.append((partial, other))
+        full_ins.append(full_in)
+        pres.append(pre)
         seen_in.append(act_in)
-    full_grads = [None] * ticks
-    pre_grads = [None] * ticks
-    seen_grad = [None] * ticks
+    full_grads, pre_grads, seen_grad = [None] * ticks, [None] * ticks, [None] * ticks
     for step in range(ticks):
         tick = ticks - 1 - step
         if step == 0:
             grad_out, full_grad, partial = last_cot, full_cot, first_grads
         else:
-            arrived = hand_over(sending)
+            arrived = hand_over(sending, -1)
             if step == 1:
-                (act,) = run(act_only, [hidden_like], *after(pres[-1], sending))
-                acts.append(act)
-                out_pieces = run(down_again, [piece_like] * rows, act, down_kept, flops=flops)
+                acts.append(run(both_silu, [part_like] * 2, *after([*pres[-1][0], *pres[-1][1]], sending)))
+                out_pieces = run(
+                    functools.partial(down_again, parts), [piece_like] * rows, *acts[-1], down_kept,
+                    flops=2 * tokens * width * hidden, name="down_again",
+                )
                 arrived = after(arrived, out_pieces)
                 out_terms = list(out_pieces)
-            (grad_out,) = run(arrive_back, [piece_like], cots[tick], *arrived)
-            (j,) = beside(step)
-            out_terms[j] = swap_rows(after(out_pieces[j], sending), j)
-            pieces = gather_rows(grad_out)
-            full_grad, partial = run(
-                back_product_after, [whole_like, hidden_like], out_terms[j], *pieces, down_turned, flops=flops
-            )
-        other = other_cols(partial)
+            (grad_out,) = run(arrive, [piece_like], cots[tick], arrived)
+            waited = []
+            for j in beside(step - 1):
+                out_terms[j] = swap_rows(after(out_pieces[j], sending), j)
+                waited.append(out_terms[j])
+            full_grad, partial = products(parts, gather_rows(grad_out), down_turned, waited)
+        full_grads[tick] = full_grad
+        ins = [(mine, other_cols(mine), *known) for mine, known in zip(partial, pres[tick])]
         if step == ticks - 1:
-            full_grads[tick] = full_grad
-            half_down = weight_product(turned_acts, full_grads, 0, hidden // 2)
-            other = after(other, half_down)
-        grad_pre, *terms = run(in_product, split_like, partial, other, *pres[tick], up_turned, flops=flops)
+            half_down = weight_product(turned_acts[0], full_grads, (hidden, width))
+            ins[0] = after(ins[0], half_down)
+        grad_pre, terms = through(slope_part, "in_part", parts, ins, up_turned, piece_like, rows)
         terms_in = scatter_rows(terms)
         if step < ticks - 1:
-            while len(turned_ins) < min(step + 2, ticks):
-                turned_ins += run(turned, [turned_like], *after(in_pieces[len(turned_ins)], terms))
-                turned_acts += run(turned, [turned_hidden], after(acts[len(turned_acts)], terms))
+            turn_blocks(step + 1, terms)
             terms_in[0] = after(terms_in[0], (turned_ins, turned_acts))
             (sending,) = run(leave_back, [piece_like], grad_out, *terms_in)
             seen_grad[tick] = sending
-        full_grads[tick] = full_grad
         pre_grads[tick] = grad_pre
-    for j in beside(0):
-        out_terms[j] = swap_rows(after(out_pieces[j], terms), j)
-    lefts = after((turned_ins, turned_acts), terms)
-    grad_up = weight_product(lefts[0], pre_grads, 0, width)
-    grad_down = weight_product(lefts[1], full_grads, hidden // 2, hidden, half_down)
+    turned_ins, last_acts = after((turned_ins, turned_acts[1]), terms)
+    grad_up = weight_product(turned_ins, [part for grad_pre in pre_grads for part in grad_pre], (width, hidden))
+    grad_down = weight_product(last_acts, full_grads, (hidden, width), hidden // 2, half_down)
     stack_like = jax.ShapeDtypeStruct((1, ticks, piece_rows, width), BF)
     terms_in[0] = after(terms_in[0], (grad_up, grad_down))
     section_input, section_output, input_grad = pl.pallas_call(

time: 148 us -> 142 us (0.959)
  waiting for transfers between devices: 48 us -> 39.3 us
  Pallas kernels: 28 us -> 30 us
  starting transfers between devices: 68.1 us -> 69.7 us
    ppermute x8 -> x4, waiting for transfers between devices: 9.95 us -> 3.2 us  [hand_over(): lax.ppermute(block, 'section', [(i - distance, i) for i in sections if i...]
    ppermute x36, starting transfers between devices: 40.1 us -> 43.1 us  [swap_rows(): lax.ppermute(block, 'row', [(i, partner(i, j, size)) for i in range(size)])]
    ppermute x6 -> x12, waiting for transfers between devices: 4.98 us -> 2.87 us  [turn(): lax.ppermute(block, axis, [(i, (i + distance) % size) for i in range(size)])]
    pallas_call x29 -> x43, Pallas kernels: 13.5 us -> 15.5 us  [run(): pl.pallas_call(kernel, in_specs=vmem(len(ins)), out_specs=vmem(len(outs))...]
    ppermute x8 -> x4, starting transfers between devices: 12.8 us -> 11.1 us  [hand_over(): lax.ppermute(block, 'section', [(i - distance, i) for i in sections if i...]
    ppermute x6 -> x12, starting transfers between devices: 15.2 us -> 15.4 us  [turn(): lax.ppermute(block, axis, [(i, (i + distance) % size) for i in range(size)])]
  transfers between devices with their start and end apart: 50 -> 52, of which waited for: 29 -> 26; matrix products, arithmetic and copies ran while one was open for 0% -> 0% of each run, Pallas kernels for 12% -> 16%
where the time goes in v10:
time: 142 us; the launch traced here: 141 us
  starting transfers between devices  69.7 us (49%)
  waiting for transfers between devices  39.3 us (28%)
  Pallas kernels  30 us (21%)
    ppermute x36, starting transfers between devices, swap_rows(): lax.ppermute(block, 'row', [(i, partner(i, j, size)) for i in range(size)])  43.1 us
    ppermute x36, waiting for transfers between devices, swap_rows(): lax.ppermute(block, 'row', [(i, partner(i, j, size)) for i in range(size)])  33.3 us
    pallas_call x43, Pallas kernels, run(): pl.pallas_call(kernel, in_specs=vmem(len(ins)), out_specs=vmem(len(outs))...  15.5 us
    ppermute x12, starting transfers between devices, turn(): lax.ppermute(block, axis, [(i, (i + distance) % size) for i in range(size)])  15.4 us
    ppermute x4, starting transfers between devices, hand_over(): lax.ppermute(block, 'section', [(i - distance, i) for i in sections if i...  11.1 us
    pallas_call x3, Pallas kernels, weight_product(): pl.pallas_call(functools.partial(weight_grad, start, len(lefts)), in_spec...  7.52 us
    ppermute x4, waiting for transfers between devices, hand_over(): lax.ppermute(block, 'section', [(i - distance, i) for i in sections if i...  3.2 us
    pallas_call x1, Pallas kernels, fetch(): pl.pallas_call(fetch_kernel, in_specs=[pl.BlockSpec(memory_space=pltpu.SM...  3.01 us
  transfers between devices with their start and end apart: 52, of which 26 were waited for; matrix products, arithmetic and copies ran while one was open for 0% of the time, Pallas kernels for 16%

profile of v10, /device:TPU:3, one launch (start us, length us, event | category | flops | bytes accessed | tf_op | source)
XLA Modules:
  0.0 140.8 jit_solution(15531681936191989171)
XLA Ops:
  0.6 0.9 first.1
  1.5 1.4 collective-permute-start.2
  2.9 2.3 %collective-permute-start.1 = (bf16[32,1024]{1,0:T(8,128)(2,1)S(1)}, bf16[32,1024]{1,0:T(8,128)(2,1)S(1)}, u32[]{:S(2)}, u32[]{:S(2)}) collective-permute-start(bf16[32,1024]{1,0:T(8,128)(2,1)S(1)} %get-tuple-element.126.refs_0_.first.refs_12_), channel_id=1, source_target_pairs={{0,4},{2,6},{4,0},{6,2},{1,5},{3,7},{5,1},{7,3},{8,12},{10,14},{12... | collective-permute-start | bytes 196616 | tf_op jit(solution)/shard_map/ppermute | solution.py:31
  5.2 0.7 copy-done
  5.9 3.0 %fetch.1 = (bf16[32,1024]{1,0:T(8,128)(2,1)S(1)}, bf16[32,1024]{1,0:T(8,128)(2,1)S(1)}, bf16[32,1024]{1,0:T(8,128)(2,1)S(1)}, bf16[32,1024]{1,0:T(8,128)(2,1)S(1...) custom-call(s32[6]{0:T(128)S(1)} %copy-done, ...), custom_call_target="tpu_custom_call" | custom-call | bytes 6291456 | tf_op jit(solution)/shard_map/fetch/pallas_call | solution.py:115
  8.9 1.3 collective-permute-done.refs_1_
  10.7 2.4 %collective-permute-start.4 = (bf16[128,1024]{1,0:T(8,128)(2,1)S(1)}, bf16[128,1024]{1,0:T(8,128)(2,1)S(1)}, u32[]{:S(2)}, u32[]{:S(2)}) collective-permute-start(bf16[128,1024]{1,0:T(8,128)(2,1)S(1)} %get-tuple-element.210.refs_0_.refs_2_), channel_id=1, source_target_pairs={{0,1},{1,0},{2,3},{3,2},{4,5},{5,4},{6,7},{7,6},{8,9},{9,8},{10,11... | collective-permute-start | bytes 786440 | tf_op jit(solution)/shard_map/ppermute | solution.py:22
  13.6 2.2 %hold.1.refs_2_.weight = bf16[2048,1024]{1,0:T(8,128)(2,1)S(1)} custom-call(bf16[2048,1024]{1,0:T(8,128)(2,1)} %bitcast.6), custom_call_target="tpu_custom_call" | custom-call | bytes 8388608 | tf_op jit(solution)/shard_map/hold/pallas_call | solution.py:205
  16.8 1.6 %collective-permute-start.5 = (bf16[32,1024]{1,0:T(8,128)(2,1)S(1)}, bf16[32,1024]{1,0:T(8,128)(2,1)S(1)}, u32[]{:S(2)}, u32[]{:S(2)}) collective-permute-start(bf16[32,1024]{1,0:T(8,128)(2,1)S(1)} %get-tuple-element.136), channel_id=1, source_target_pairs={{0,6},{2,4},{4,2},{6,0},{1,7},{3,5},{5,3},{7,1},{8,14},{10,12},{12... | collective-permute-start | bytes 196616 | tf_op jit(solution)/shard_map/ppermute | solution.py:31
  18.3 2.0 %collective-permute-start.7 = (bf16[32,1024]{1,0:T(8,128)(2,1)S(1)}, bf16[32,1024]{1,0:T(8,128)(2,1)S(1)}, u32[]{:S(2)}, u32[]{:S(2)}) collective-permute-start(bf16[32,1024]{1,0:T(8,128)(2,1)S(1)} %get-tuple-element.138), channel_id=1, source_target_pairs={{0,2},{2,0},{4,6},{6,4},{1,3},{3,1},{5,7},{7,5},{8,10},{10,8},{12,... | collective-permute-start | bytes 196616 | tf_op jit(solution)/shard_map/ppermute | solution.py:31
  20.4 1.2 turned_weight.2.refs_4_.weight.refs_6_.refs_5_
  21.8 3.7 %collective-permute-done.6.refs_2_ = bf16[32,1024]{1,0:T(8,128)(2,1)S(1)} collective-permute-done((bf16[32,1024]{1,0:T(8,128)(2,1)S(1)}, bf16[32,1024]{1,0:T(8,128)(2,1)S(1)}, u32[]{:S(2)}, u32[]{:S(2)}) %collective-permute-start.6) | collective-permute-done | bytes 65568 | tf_op jit(solution)/shard_map/ppermute | solution.py:31
  25.5 3.1 %collective-permute-start.8 = (bf16[32,1024]{1,0:T(8,128)(2,1)S(1)}, bf16[32,1024]{1,0:T(8,128)(2,1)S(1)}, u32[]{:S(2)}, u32[]{:S(2)}) collective-permute-start(bf16[32,1024]{1,0:T(8,128)(2,1)S(1)} %get-tuple-element.141), channel_id=1, source_target_pairs={{0,8},{8,16},{16,24},{1,9},{9,17},{17,25},{2,10},{10,18},{18,26},{... | collective-permute-start | bytes 196616 | tf_op jit(solution)/shard_map/ppermute | solution.py:17
  28.7 2.0 %collective-permute-start.9 = (bf16[32,1024]{1,0:T(8,128)(2,1)S(1)}, bf16[32,1024]{1,0:T(8,128)(2,1)S(1)}, u32[]{:S(2)}, u32[]{:S(2)}) collective-permute-start(bf16[32,1024]{1,0:T(8,128)(2,1)S(1)} %get-tuple-element.163.refs_0_.first), channel_id=1, source_target_pairs={{0,2},{2,0},{4,6},{6,4},{1,3},{3,1},{5,7},{7,5},{8,10},{10,8},{12,... | collective-permute-start | bytes 196616 | tf_op jit(solution)/shard_map/ppermute | solution.py:31
  30.8 1.8 %collective-permute-start.12 = (bf16[32,1024]{1,0:T(8,128)(2,1)S(1)}, bf16[32,1024]{1,0:T(8,128)(2,1)S(1)}, u32[]{:S(2)}, u32[]{:S(2)}) collective-permute-start(bf16[32,1024]{1,0:T(8,128)(2,1)S(1)} %arrive.4.refs_2_.first.refs_13_), channel_id=1, source_target_pairs={{0,4},{2,6},{4,0},{6,2},{1,5},{3,7},{5,1},{7,3},{8,12},{10,14},{12... | collective-permute-start | bytes 196616 | tf_op jit(solution)/shard_map/ppermute | solution.py:31
  32.6 1.7 %collective-permute-start.11 = (bf16[32,1024]{1,0:T(8,128)(2,1)S(1)}, bf16[32,1024]{1,0:T(8,128)(2,1)S(1)}, u32[]{:S(2)}, u32[]{:S(2)}) collective-permute-start(bf16[32,1024]{1,0:T(8,128)(2,1)S(1)} %arrive.4.refs_2_.first.refs_13_), channel_id=1, source_target_pairs={{0,6},{2,4},{4,2},{6,0},{1,7},{3,5},{5,3},{7,1},{8,14},{10,12},{12... | collective-permute-start | bytes 196616 | tf_op jit(solution)/shard_map/ppermute | solution.py:31
  34.3 1.9 %collective-permute-done.13.refs_5_ = bf16[32,1024]{1,0:T(8,128)(2,1)S(1)} collective-permute-done((bf16[32,1024]{1,0:T(8,128)(2,1)S(1)}, bf16[32,1024]{1,0:T(8,128)(2,1)S(1)}, u32[]{:S(2)}, u32[]{:S(2)}) %collective-permute-start.13) | collective-permute-done | bytes 65568 | tf_op jit(solution)/shard_map/ppermute | solution.py:31
  36.3 1.5 %collective-permute-done.11.refs_3_ = bf16[32,1024]{1,0:T(8,128)(2,1)S(1)} collective-permute-done((bf16[32,1024]{1,0:T(8,128)(2,1)S(1)}, bf16[32,1024]{1,0:T(8,128)(2,1)S(1)}, u32[]{:S(2)}, u32[]{:S(2)}) %collective-permute-start.11) | collective-permute-done | bytes 65568 | tf_op jit(solution)/shard_map/ppermute | solution.py:31
  38.2 3.5 %collective-permute-start.15 = (bf16[128,1024]{1,0:T(8,128)(2,1)S(1)}, bf16[128,1024]{1,0:T(8,128)(2,1)S(1)}, u32[]{:S(2)}, u32[]{:S(2)}) collective-permute-start(bf16[128,1024]{1,0:T(8,128)(2,1)S(1)} %get-tuple-element.145.refs_0_.refs_2_), channel_id=1, source_target_pairs={{0,1},{1,0},{2,3},{3,2},{4,5},{5,4},{6,7},{7,6},{8,9},{9,8},{10,11... | collective-permute-start | bytes 786440 | tf_op jit(solution)/shard_map/ppermute | solution.py:22
  42.3 0.6 collective-permute-done.15.refs_1_.refs_3_
  44.3 1.5 %collective-permute-start.16 = (bf16[32,1024]{1,0:T(8,128)(2,1)S(1)}, bf16[32,1024]{1,0:T(8,128)(2,1)S(1)}, u32[]{:S(2)}, u32[]{:S(2)}) collective-permute-start(bf16[32,1024]{1,0:T(8,128)(2,1)S(1)} %get-tuple-element.148), channel_id=1, source_target_pairs={{0,6},{2,4},{4,2},{6,0},{1,7},{3,5},{5,3},{7,1},{8,14},{10,12},{12... | collective-permute-start | bytes 196616 | tf_op jit(solution)/shard_map/ppermute | solution.py:31
  45.8 2.1 %collective-permute-start.18 = (bf16[32,1024]{1,0:T(8,128)(2,1)S(1)}, bf16[32,1024]{1,0:T(8,128)(2,1)S(1)}, u32[]{:S(2)}, u32[]{:S(2)}) collective-permute-start(bf16[32,1024]{1,0:T(8,128)(2,1)S(1)} %get-tuple-element.150), channel_id=1, source_target_pairs={{0,2},{2,0},{4,6},{6,4},{1,3},{3,1},{5,7},{7,5},{8,10},{10,8},{12,... | collective-permute-start | bytes 196616 | tf_op jit(solution)/shard_map/ppermute | solution.py:31
  48.3 1.2 turned_weight.3.refs_4_
  49.7 3.3 %collective-permute-done.17.refs_2_ = bf16[32,1024]{1,0:T(8,128)(2,1)S(1)} collective-permute-done((bf16[32,1024]{1,0:T(8,128)(2,1)S(1)}, bf16[32,1024]{1,0:T(8,128)(2,1)S(1)}, u32[]{:S(2)}, u32[]{:S(2)}) %collective-permute-start.17) | collective-permute-done | bytes 65568 | tf_op jit(solution)/shard_map/ppermute | solution.py:31
  53.0 4.0 %collective-permute-start.19 = (bf16[32,1024]{1,0:T(8,128)(2,1)S(1)}, bf16[32,1024]{1,0:T(8,128)(2,1)S(1)}, u32[]{:S(2)}, u32[]{:S(2)}) collective-permute-start(bf16[32,1024]{1,0:T(8,128)(2,1)S(1)} %get-tuple-element.158), channel_id=1, source_target_pairs={{0,8},{8,16},{16,24},{1,9},{9,17},{17,25},{2,10},{10,18},{18,26},{... | collective-permute-start | bytes 196616 | tf_op jit(solution)/shard_map/ppermute | solution.py:17
  57.1 1.3 collective-permute-start.20
  58.5 2.3 %collective-permute-start.22 = (bf16[32,1024]{1,0:T(8,128)(2,1)S(1)}, bf16[32,1024]{1,0:T(8,128)(2,1)S(1)}, u32[]{:S(2)}, u32[]{:S(2)}) collective-permute-start(bf16[32,1024]{1,0:T(8,128)(2,1)S(1)} %arrive.5.refs_1_.first_out.refs_14_), channel_id=1, source_target_pairs={{0,4},{2,6},{4,0},{6,2},{1,5},{3,7},{5,1},{7,3},{8,12},{10,14},{12... | collective-permute-start | bytes 196616 | tf_op jit(solution)/shard_map/ppermute | solution.py:31
  60.8 1.2 collective-permute-start.21
  62.2 1.6 %collective-permute-done.23.refs_4_ = bf16[32,1024]{1,0:T(8,128)(2,1)S(1)} collective-permute-done((bf16[32,1024]{1,0:T(8,128)(2,1)S(1)}, bf16[32,1024]{1,0:T(8,128)(2,1)S(1)}, u32[]{:S(2)}, u32[]{:S(2)}) %collective-permute-start.23) | collective-permute-done | bytes 65568 | tf_op jit(solution)/shard_map/ppermute | solution.py:31
  63.8 2.7 %collective-permute-done.21.refs_2_ = bf16[32,1024]{1,0:T(8,128)(2,1)S(1)} collective-permute-done((bf16[32,1024]{1,0:T(8,128)(2,1)S(1)}, bf16[32,1024]{1,0:T(8,128)(2,1)S(1)}, u32[]{:S(2)}, u32[]{:S(2)}) %collective-permute-start.21) | collective-permute-done | bytes 65568 | tf_op jit(solution)/shard_map/ppermute | solution.py:31
  67.3 2.2 %collective-permute-start.25 = (bf16[128,1024]{1,0:T(8,128)(2,1)S(1)}, bf16[128,1024]{1,0:T(8,128)(2,1)S(1)}, u32[]{:S(2)}, u32[]{:S(2)}) collective-permute-start(bf16[128,1024]{1,0:T(8,128)(2,1)S(1)} %product_part.8.refs_2_), channel_id=1, source_target_pairs={{0,1},{1,0},{2,3},{3,2},{4,5},{5,4},{6,7},{7,6},{8,9},{9,8},{10,11... | collective-permute-start | bytes 786440 | tf_op jit(solution)/shard_map/ppermute | solution.py:22
  73.2 1.7 %collective-permute-start.28 = (bf16[32,1024]{1,0:T(8,128)(2,1)S(1)}, bf16[32,1024]{1,0:T(8,128)(2,1)S(1)}, u32[]{:S(2)}, u32[]{:S(2)}) collective-permute-start(bf16[32,1024]{1,0:T(8,128)(2,1)S(1)} %get-tuple-element.172), channel_id=1, source_target_pairs={{0,6},{2,4},{4,2},{6,0},{1,7},{3,5},{5,3},{7,1},{8,14},{10,12},{12... | collective-permute-start | bytes 196616 | tf_op jit(solution)/shard_map/ppermute | solution.py:31
  75.3 1.5 %collective-permute-start.30 = (bf16[32,1024]{1,0:T(8,128)(2,1)S(1)}, bf16[32,1024]{1,0:T(8,128)(2,1)S(1)}, u32[]{:S(2)}, u32[]{:S(2)}) collective-permute-start(bf16[32,1024]{1,0:T(8,128)(2,1)S(1)} %get-tuple-element.174), channel_id=1, source_target_pairs={{0,2},{2,0},{4,6},{6,4},{1,3},{3,1},{5,7},{7,5},{8,10},{10,8},{12,... | collective-permute-start | bytes 196616 | tf_op jit(solution)/shard_map/ppermute | solution.py:31
  77.2 1.4 %collective-permute-done.28.refs_1_ = bf16[32,1024]{1,0:T(8,128)(2,1)S(1)} collective-permute-done((bf16[32,1024]{1,0:T(8,128)(2,1)S(1)}, bf16[32,1024]{1,0:T(8,128)(2,1)S(1)}, u32[]{:S(2)}, u32[]{:S(2)}) %collective-permute-start.28) | collective-permute-done | bytes 65568 | tf_op jit(solution)/shard_map/ppermute | solution.py:31
  78.6 3.5 %collective-permute-done.29.refs_2_ = bf16[32,1024]{1,0:T(8,128)(2,1)S(1)} collective-permute-done((bf16[32,1024]{1,0:T(8,128)(2,1)S(1)}, bf16[32,1024]{1,0:T(8,128)(2,1)S(1)}, u32[]{:S(2)}, u32[]{:S(2)}) %collective-permute-start.29) | collective-permute-done | bytes 65568 | tf_op jit(solution)/shard_map/ppermute | solution.py:31
  82.2 2.1 %collective-permute-start.31 = (bf16[32,1024]{1,0:T(8,128)(2,1)S(1)}, bf16[32,1024]{1,0:T(8,128)(2,1)S(1)}, u32[]{:S(2)}, u32[]{:S(2)}) collective-permute-start(bf16[32,1024]{1,0:T(8,128)(2,1)S(1)} %leave_back.2.refs_11_), channel_id=1, source_target_pairs={{8,0},{16,8},{24,16},{9,1},{17,9},{25,17},{10,2},{18,10},{26,18},{... | collective-permute-start | bytes 196616 | tf_op jit(solution)/shard_map/ppermute | solution.py:17
  84.5 0.7 down_again.1
  85.3 1.9 %collective-permute-start.33 = (bf16[32,1024]{1,0:T(8,128)(2,1)S(1)}, bf16[32,1024]{1,0:T(8,128)(2,1)S(1)}, u32[]{:S(2)}, u32[]{:S(2)}) collective-permute-start(bf16[32,1024]{1,0:T(8,128)(2,1)S(1)} %get-tuple-element.193), channel_id=1, source_target_pairs={{0,4},{2,6},{4,0},{6,2},{1,5},{3,7},{5,1},{7,3},{8,12},{10,14},{12... | collective-permute-start | bytes 196616 | tf_op jit(solution)/shard_map/ppermute | solution.py:31
  87.2 0.9 collective-permute-done.31.arrived
  88.2 2.1 %collective-permute-start.35 = (bf16[32,1024]{1,0:T(8,128)(2,1)S(1)}, bf16[32,1024]{1,0:T(8,128)(2,1)S(1)}, u32[]{:S(2)}, u32[]{:S(2)}) collective-permute-start(bf16[32,1024]{1,0:T(8,128)(2,1)S(1)} %arrive.6.refs_2_.first), channel_id=1, source_target_pairs={{0,4},{2,6},{4,0},{6,2},{1,5},{3,7},{5,1},{7,3},{8,12},{10,14},{12... | collective-permute-start | bytes 196616 | tf_op jit(solution)/shard_map/ppermute | solution.py:31
  90.3 1.4 %collective-permute-start.34 = (bf16[32,1024]{1,0:T(8,128)(2,1)S(1)}, bf16[32,1024]{1,0:T(8,128)(2,1)S(1)}, u32[]{:S(2)}, u32[]{:S(2)}) collective-permute-start(bf16[32,1024]{1,0:T(8,128)(2,1)S(1)} %arrive.6.refs_2_.first), channel_id=1, source_target_pairs={{0,6},{2,4},{4,2},{6,0},{1,7},{3,5},{5,3},{7,1},{8,14},{10,12},{12... | collective-permute-start | bytes 196616 | tf_op jit(solution)/shard_map/ppermute | solution.py:31
  91.8 0.9 collective-permute-done.35.refs_4_
  92.7 2.9 %collective-permute-done.34.refs_3_ = bf16[32,1024]{1,0:T(8,128)(2,1)S(1)} collective-permute-done((bf16[32,1024]{1,0:T(8,128)(2,1)S(1)}, bf16[32,1024]{1,0:T(8,128)(2,1)S(1)}, u32[]{:S(2)}, u32[]{:S(2)}) %collective-permute-start.34) | collective-permute-done | bytes 65568 | tf_op jit(solution)/shard_map/ppermute | solution.py:31
  96.1 2.9 %collective-permute-start.38 = (bf16[128,1024]{1,0:T(8,128)(2,1)S(1)}, bf16[128,1024]{1,0:T(8,128)(2,1)S(1)}, u32[]{:S(2)}, u32[]{:S(2)}) collective-permute-start(bf16[128,1024]{1,0:T(8,128)(2,1)S(1)} %get-tuple-element.195.refs_0_), channel_id=1, source_target_pairs={{0,1},{1,0},{2,3},{3,2},{4,5},{5,4},{6,7},{7,6},{8,9},{9,8},{10,11... | collective-permute-start | bytes 786440 | tf_op jit(solution)/shard_map/ppermute | solution.py:22
  99.5 0.6 collective-permute-done.38.refs_1_
  101.6 1.7 %collective-permute-start.39 = (bf16[32,1024]{1,0:T(8,128)(2,1)S(1)}, bf16[32,1024]{1,0:T(8,128)(2,1)S(1)}, u32[]{:S(2)}, u32[]{:S(2)}) collective-permute-start(bf16[32,1024]{1,0:T(8,128)(2,1)S(1)} %get-tuple-element.198), channel_id=1, source_target_pairs={{0,6},{2,4},{4,2},{6,0},{1,7},{3,5},{5,3},{7,1},{8,14},{10,12},{12... | collective-permute-start | bytes 196616 | tf_op jit(solution)/shard_map/ppermute | solution.py:31
  103.3 1.9 %collective-permute-start.41 = (bf16[32,1024]{1,0:T(8,128)(2,1)S(1)}, bf16[32,1024]{1,0:T(8,128)(2,1)S(1)}, u32[]{:S(2)}, u32[]{:S(2)}) collective-permute-start(bf16[32,1024]{1,0:T(8,128)(2,1)S(1)} %get-tuple-element.200), channel_id=1, source_target_pairs={{0,2},{2,0},{4,6},{6,4},{1,3},{3,1},{5,7},{7,5},{8,10},{10,8},{12,... | collective-permute-start | bytes 196616 | tf_op jit(solution)/shard_map/ppermute | solution.py:31
  105.6 1.4 %collective-permute-done.39.refs_1_ = bf16[32,1024]{1,0:T(8,128)(2,1)S(1)} collective-permute-done((bf16[32,1024]{1,0:T(8,128)(2,1)S(1)}, bf16[32,1024]{1,0:T(8,128)(2,1)S(1)}, u32[]{:S(2)}, u32[]{:S(2)}) %collective-permute-start.39) | collective-permute-done | bytes 65568 | tf_op jit(solution)/shard_map/ppermute | solution.py:31
  107.0 3.3 %collective-permute-done.40.refs_2_ = bf16[32,1024]{1,0:T(8,128)(2,1)S(1)} collective-permute-done((bf16[32,1024]{1,0:T(8,128)(2,1)S(1)}, bf16[32,1024]{1,0:T(8,128)(2,1)S(1)}, u32[]{:S(2)}, u32[]{:S(2)}) %collective-permute-start.40) | collective-permute-done | bytes 65568 | tf_op jit(solution)/shard_map/ppermute | solution.py:31
  110.3 1.9 %collective-permute-start.42 = (bf16[32,1024]{1,0:T(8,128)(2,1)S(1)}, bf16[32,1024]{1,0:T(8,128)(2,1)S(1)}, u32[]{:S(2)}, u32[]{:S(2)}) collective-permute-start(bf16[32,1024]{1,0:T(8,128)(2,1)S(1)} %leave_back.3.refs_10_), channel_id=1, source_target_pairs={{8,0},{16,8},{24,16},{9,1},{17,9},{25,17},{10,2},{18,10},{26,18},{... | collective-permute-start | bytes 196616 | tf_op jit(solution)/shard_map/ppermute | solution.py:17
  112.3 1.7 %collective-permute-start.43 = (bf16[32,1024]{1,0:T(8,128)(2,1)S(1)}, bf16[32,1024]{1,0:T(8,128)(2,1)S(1)}, u32[]{:S(2)}, u32[]{:S(2)}) collective-permute-start(bf16[32,1024]{1,0:T(8,128)(2,1)S(1)} %get-tuple-element.205), channel_id=1, source_target_pairs={{0,6},{2,4},{4,2},{6,0},{1,7},{3,5},{5,3},{7,1},{8,14},{10,12},{12... | collective-permute-start | bytes 196616 | tf_op jit(solution)/shard_map/ppermute | solution.py:31
  113.9 2.3 %collective-permute-done.42.arrived = bf16[32,1024]{1,0:T(8,128)(2,1)S(1)} collective-permute-done((bf16[32,1024]{1,0:T(8,128)(2,1)S(1)}, bf16[32,1024]{1,0:T(8,128)(2,1)S(1)}, u32[]{:S(2)}, u32[]{:S(2)}) %collective-permute-start.42) | collective-permute-done | bytes 65568 | tf_op jit(solution)/shard_map/ppermute | solution.py:17
  116.3 1.9 %collective-permute-start.45 = (bf16[32,1024]{1,0:T(8,128)(2,1)S(1)}, bf16[32,1024]{1,0:T(8,128)(2,1)S(1)}, u32[]{:S(2)}, u32[]{:S(2)}) collective-permute-start(bf16[32,1024]{1,0:T(8,128)(2,1)S(1)} %arrive.7.refs_1_.first_grad), channel_id=1, source_target_pairs={{0,4},{2,6},{4,0},{6,2},{1,5},{3,7},{5,1},{7,3},{8,12},{10,14},{12... | collective-permute-start | bytes 196616 | tf_op jit(solution)/shard_map/ppermute | solution.py:31
  118.2 1.7 %collective-permute-start.44 = (bf16[32,1024]{1,0:T(8,128)(2,1)S(1)}, bf16[32,1024]{1,0:T(8,128)(2,1)S(1)}, u32[]{:S(2)}, u32[]{:S(2)}) collective-permute-start(bf16[32,1024]{1,0:T(8,128)(2,1)S(1)} %arrive.7.refs_1_.first_grad), channel_id=1, source_target_pairs={{0,6},{2,4},{4,2},{6,0},{1,7},{3,5},{5,3},{7,1},{8,14},{10,12},{12... | collective-permute-start | bytes 196616 | tf_op jit(solution)/shard_map/ppermute | solution.py:31
  120.4 2.7 %collective-permute-done.44.refs_2_ = bf16[32,1024]{1,0:T(8,128)(2,1)S(1)} collective-permute-done((bf16[32,1024]{1,0:T(8,128)(2,1)S(1)}, bf16[32,1024]{1,0:T(8,128)(2,1)S(1)}, u32[]{:S(2)}, u32[]{:S(2)}) %collective-permute-start.44) | collective-permute-done | bytes 65568 | tf_op jit(solution)/shard_map/ppermute | solution.py:31
  123.6 3.4 %collective-permute-start.48 = (bf16[128,1024]{1,0:T(8,128)(2,1)S(1)}, bf16[128,1024]{1,0:T(8,128)(2,1)S(1)}, u32[]{:S(2)}, u32[]{:S(2)}) collective-permute-start(bf16[128,1024]{1,0:T(8,128)(2,1)S(1)} %get-tuple-element.208.refs_0_), channel_id=1, source_target_pairs={{0,1},{1,0},{2,3},{3,2},{4,5},{5,4},{6,7},{7,6},{8,9},{9,8},{10,11... | collective-permute-start | bytes 786440 | tf_op jit(solution)/shard_map/ppermute | solution.py:22
  127.5 2.1 %weight_grad.3.refs_6_ = bf16[2048,1024]{1,0:T(8,128)(2,1)} custom-call(bf16[1024,128]{1,0:T(8,128)(2,1)S(1)} %turned.10.refs_0_, bf16[1024,128]{1,0:T(8,128)(2,1)S(1)} %turned.13.refs_1_, bf16[1024,128]{1,0:T(8,128)(2,1)S(1)} %turned.16.refs_2_, bf16[128,1024]{1,0:T(8,128)(2,1)S(1)} %get-tuple-element.206.whole.refs_3_, ...), custom_call_target="tpu_custom_call" | custom-call | flops 805306368 | bytes 2097152 | tf_op jit(solution)/shard_map/weight_grad/pallas_call | solution.py:340
  129.7 0.6 in_part.10
  130.3 0.6 in_part.11
  130.9 1.7 %collective-permute-start.49 = (bf16[32,1024]{1,0:T(8,128)(2,1)S(1)}, bf16[32,1024]{1,0:T(8,128)(2,1)S(1)}, u32[]{:S(2)}, u32[]{:S(2)}) collective-permute-start(bf16[32,1024]{1,0:T(8,128)(2,1)S(1)} %get-tuple-element.214), channel_id=1, source_target_pairs={{0,6},{2,4},{4,2},{6,0},{1,7},{3,5},{5,3},{7,1},{8,14},{10,12},{12... | collective-permute-start | bytes 196616 | tf_op jit(solution)/shard_map/ppermute | solution.py:31
  132.6 1.9 %collective-permute-start.51 = (bf16[32,1024]{1,0:T(8,128)(2,1)S(1)}, bf16[32,1024]{1,0:T(8,128)(2,1)S(1)}, u32[]{:S(2)}, u32[]{:S(2)}) collective-permute-start(bf16[32,1024]{1,0:T(8,128)(2,1)S(1)} %get-tuple-element.216), channel_id=1, source_target_pairs={{0,2},{2,0},{4,6},{6,4},{1,3},{3,1},{5,7},{7,5},{8,10},{10,8},{12,... | collective-permute-start | bytes 196616 | tf_op jit(solution)/shard_map/ppermute | solution.py:31
  134.5 3.3 %weight_grad.4 = bf16[1024,2048]{1,0:T(8,128)(2,1)} custom-call(bf16[1024,128]{1,0:T(8,128)(2,1)S(1)} %turned.9.refs_0_, bf16[1024,128]{1,0:T(8,128)(2,1)S(1)} %turned.12.refs_1_, bf16[1024,128]{1,0:T(8,128)(2,1)S(1)} %turned.15.refs_2_, bf16[128,1024]{1,0:T(8,128)(2,1)S(1)} %get-tuple-element.220.refs_3_, bf16[128,1024]{1,0:T(8,128)(2,1)S(1)} %get-tuple-element.221.refs_4_, ...), custom_call_target="tpu_custom_call" | custom-call | flops 1610612736 | bytes 4194304 | tf_op jit(solution)/shard_map/weight_grad/pallas_call | solution.py:340
  137.8 2.1 %weight_grad.5 = bf16[2048,1024]{1,0:T(8,128)(2,1)} custom-call(bf16[1024,128]{1,0:T(8,128)(2,1)S(1)} %turned.11.refs_0_, bf16[1024,128]{1,0:T(8,128)(2,1)S(1)} %turned.14.refs_1_, bf16[1024,128]{1,0:T(8,128)(2,1)S(1)} %turned.17.refs_2_, bf16[128,1024]{1,0:T(8,128)(2,1)S(1)} %get-tuple-element.206.whole.refs_3_, ...), custom_call_target="tpu_custom_call", output_to_operand_aliasing={{}: (6, {})} | custom-call | flops 805306368 | bytes 2097152 | tf_op jit(solution)/shard_map/weight_grad/pallas_call | solution.py:340
  139.9 0.9 finish.1
  (92 shorter events, 15.9 us)
Async XLA Ops:
  1.5 7.4 %collective-permute-start.2 = (bf16[32,1024]{1,0:T(8,128)(2,1)S(1)}, bf16[32,1024]{1,0:T(8,128)(2,1)S(1)}, u32[]{:S(2)}, u32[]{:S(2)}) collective-permute-start(bf16[32,1024]{1,0:T(8,128)(2,1)S(1)} %get-tuple-element.126.refs_0_.first.refs_12_), channel_id=1, source_target_pairs={{0,2},{2,0},{4,6},{6,4},{1,3},{3,1},{5,7},{7,5},{8,10},{10,8},{12,... | collective-permute-start | bytes 196616 | tf_op jit(solution)/shard_map/ppermute | solution.py:31
  2.9 6.0 %collective-permute-start.1 = (bf16[32,1024]{1,0:T(8,128)(2,1)S(1)}, bf16[32,1024]{1,0:T(8,128)(2,1)S(1)}, u32[]{:S(2)}, u32[]{:S(2)}) collective-permute-start(bf16[32,1024]{1,0:T(8,128)(2,1)S(1)} %get-tuple-element.126.refs_0_.first.refs_12_), channel_id=1, source_target_pairs={{0,4},{2,6},{4,0},{6,2},{1,5},{3,7},{5,1},{7,3},{8,12},{10,14},{12... | collective-permute-start | bytes 196616 | tf_op jit(solution)/shard_map/ppermute | solution.py:31
  5.2 5.0 %collective-permute-start = (bf16[32,1024]{1,0:T(8,128)(2,1)S(1)}, bf16[32,1024]{1,0:T(8,128)(2,1)S(1)}, u32[]{:S(2)}, u32[]{:S(2)}) collective-permute-start(bf16[32,1024]{1,0:T(8,128)(2,1)S(1)} %get-tuple-element.126.refs_0_.first.refs_12_), channel_id=1, source_target_pairs={{0,6},{2,4},{4,2},{6,0},{1,7},{3,5},{5,3},{7,1},{8,14},{10,12},{12... | collective-permute-start | bytes 196616 | tf_op jit(solution)/shard_map/ppermute | solution.py:31
  5.2 0.7 copy-start
  10.7 5.1 %collective-permute-start.4 = (bf16[128,1024]{1,0:T(8,128)(2,1)S(1)}, bf16[128,1024]{1,0:T(8,128)(2,1)S(1)}, u32[]{:S(2)}, u32[]{:S(2)}) collective-permute-start(bf16[128,1024]{1,0:T(8,128)(2,1)S(1)} %get-tuple-element.210.refs_0_.refs_2_), channel_id=1, source_target_pairs={{0,1},{1,0},{2,3},{3,2},{4,5},{5,4},{6,7},{7,6},{8,9},{9,8},{10,11... | collective-permute-start | bytes 786440 | tf_op jit(solution)/shard_map/ppermute | solution.py:22
  13.5 2.8 %collective-permute-start.3 = (bf16[128,1024]{1,0:T(8,128)(2,1)S(1)}, bf16[128,1024]{1,0:T(8,128)(2,1)S(1)}, u32[]{:S(2)}, u32[]{:S(2)}) collective-permute-start(bf16[128,1024]{1,0:T(8,128)(2,1)S(1)} %product_part.6.refs_0_.refs_2_), channel_id=1, source_target_pairs={{0,1},{1,0},{2,3},{3,2},{4,5},{5,4},{6,7},{7,6},{8,9},{9,8},{10,11... | collective-permute-start | bytes 786440 | tf_op jit(solution)/shard_map/ppermute | solution.py:22
  16.8 5.0 %collective-permute-start.5 = (bf16[32,1024]{1,0:T(8,128)(2,1)S(1)}, bf16[32,1024]{1,0:T(8,128)(2,1)S(1)}, u32[]{:S(2)}, u32[]{:S(2)}) collective-permute-start(bf16[32,1024]{1,0:T(8,128)(2,1)S(1)} %get-tuple-element.136), channel_id=1, source_target_pairs={{0,6},{2,4},{4,2},{6,0},{1,7},{3,5},{5,3},{7,1},{8,14},{10,12},{12... | collective-permute-start | bytes 196616 | tf_op jit(solution)/shard_map/ppermute | solution.py:31
  18.3 7.1 %collective-permute-start.6 = (bf16[32,1024]{1,0:T(8,128)(2,1)S(1)}, bf16[32,1024]{1,0:T(8,128)(2,1)S(1)}, u32[]{:S(2)}, u32[]{:S(2)}) collective-permute-start(bf16[32,1024]{1,0:T(8,128)(2,1)S(1)} %get-tuple-element.137), channel_id=1, source_target_pairs={{0,4},{2,6},{4,0},{6,2},{1,5},{3,7},{5,1},{7,3},{8,12},{10,14},{12... | collective-permute-start | bytes 196616 | tf_op jit(solution)/shard_map/ppermute | solution.py:31
  18.3 7.1 %collective-permute-start.7 = (bf16[32,1024]{1,0:T(8,128)(2,1)S(1)}, bf16[32,1024]{1,0:T(8,128)(2,1)S(1)}, u32[]{:S(2)}, u32[]{:S(2)}) collective-permute-start(bf16[32,1024]{1,0:T(8,128)(2,1)S(1)} %get-tuple-element.138), channel_id=1, source_target_pairs={{0,2},{2,0},{4,6},{6,4},{1,3},{3,1},{5,7},{7,5},{8,10},{10,8},{12,... | collective-permute-start | bytes 196616 | tf_op jit(solution)/shard_map/ppermute | solution.py:31
  25.5 5.2 %collective-permute-start.8 = (bf16[32,1024]{1,0:T(8,128)(2,1)S(1)}, bf16[32,1024]{1,0:T(8,128)(2,1)S(1)}, u32[]{:S(2)}, u32[]{:S(2)}) collective-permute-start(bf16[32,1024]{1,0:T(8,128)(2,1)S(1)} %get-tuple-element.141), channel_id=1, source_target_pairs={{0,8},{8,16},{16,24},{1,9},{9,17},{17,25},{2,10},{10,18},{18,26},{... | collective-permute-start | bytes 196616 | tf_op jit(solution)/shard_map/ppermute | solution.py:17
  28.6 5.7 %collective-permute-start.10 = (bf16[32,1024]{1,0:T(8,128)(2,1)S(1)}, bf16[32,1024]{1,0:T(8,128)(2,1)S(1)}, u32[]{:S(2)}, u32[]{:S(2)}) collective-permute-start(bf16[32,1024]{1,0:T(8,128)(2,1)S(1)} %get-tuple-element.163.refs_0_.first), channel_id=1, source_target_pairs={{0,4},{2,6},{4,0},{6,2},{1,5},{3,7},{5,1},{7,3},{8,12},{10,14},{12... | collective-permute-start | bytes 196616 | tf_op jit(solution)/shard_map/ppermute | solution.py:31
  28.7 5.6 %collective-permute-start.9 = (bf16[32,1024]{1,0:T(8,128)(2,1)S(1)}, bf16[32,1024]{1,0:T(8,128)(2,1)S(1)}, u32[]{:S(2)}, u32[]{:S(2)}) collective-permute-start(bf16[32,1024]{1,0:T(8,128)(2,1)S(1)} %get-tuple-element.163.refs_0_.first), channel_id=1, source_target_pairs={{0,2},{2,0},{4,6},{6,4},{1,3},{3,1},{5,7},{7,5},{8,10},{10,8},{12,... | collective-permute-start | bytes 196616 | tf_op jit(solution)/shard_map/ppermute | solution.py:31
  30.7 5.5 %collective-permute-start.13 = (bf16[32,1024]{1,0:T(8,128)(2,1)S(1)}, bf16[32,1024]{1,0:T(8,128)(2,1)S(1)}, u32[]{:S(2)}, u32[]{:S(2)}) collective-permute-start(bf16[32,1024]{1,0:T(8,128)(2,1)S(1)} %arrive.4.refs_2_.first.refs_13_), channel_id=1, source_target_pairs={{0,2},{2,0},{4,6},{6,4},{1,3},{3,1},{5,7},{7,5},{8,10},{10,8},{12,... | collective-permute-start | bytes 196616 | tf_op jit(solution)/shard_map/ppermute | solution.py:31
  30.8 5.5 %collective-permute-start.12 = (bf16[32,1024]{1,0:T(8,128)(2,1)S(1)}, bf16[32,1024]{1,0:T(8,128)(2,1)S(1)}, u32[]{:S(2)}, u32[]{:S(2)}) collective-permute-start(bf16[32,1024]{1,0:T(8,128)(2,1)S(1)} %arrive.4.refs_2_.first.refs_13_), channel_id=1, source_target_pairs={{0,4},{2,6},{4,0},{6,2},{1,5},{3,7},{5,1},{7,3},{8,12},{10,14},{12... | collective-permute-start | bytes 196616 | tf_op jit(solution)/shard_map/ppermute | solution.py:31
  32.6 5.1 %collective-permute-start.11 = (bf16[32,1024]{1,0:T(8,128)(2,1)S(1)}, bf16[32,1024]{1,0:T(8,128)(2,1)S(1)}, u32[]{:S(2)}, u32[]{:S(2)}) collective-permute-start(bf16[32,1024]{1,0:T(8,128)(2,1)S(1)} %arrive.4.refs_2_.first.refs_13_), channel_id=1, source_target_pairs={{0,6},{2,4},{4,2},{6,0},{1,7},{3,5},{5,3},{7,1},{8,14},{10,12},{12... | collective-permute-start | bytes 196616 | tf_op jit(solution)/shard_map/ppermute | solution.py:31
  38.2 4.7 %collective-permute-start.15 = (bf16[128,1024]{1,0:T(8,128)(2,1)S(1)}, bf16[128,1024]{1,0:T(8,128)(2,1)S(1)}, u32[]{:S(2)}, u32[]{:S(2)}) collective-permute-start(bf16[128,1024]{1,0:T(8,128)(2,1)S(1)} %get-tuple-element.145.refs_0_.refs_2_), channel_id=1, source_target_pairs={{0,1},{1,0},{2,3},{3,2},{4,5},{5,4},{6,7},{7,6},{8,9},{9,8},{10,11... | collective-permute-start | bytes 786440 | tf_op jit(solution)/shard_map/ppermute | solution.py:22
  42.2 1.6 %collective-permute-start.14 = (bf16[128,1024]{1,0:T(8,128)(2,1)S(1)}, bf16[128,1024]{1,0:T(8,128)(2,1)S(1)}, u32[]{:S(2)}, u32[]{:S(2)}) collective-permute-start(bf16[128,1024]{1,0:T(8,128)(2,1)S(1)} %product_part.7.refs_0_.refs_2_), channel_id=1, source_target_pairs={{0,1},{1,0},{2,3},{3,2},{4,5},{5,4},{6,7},{7,6},{8,9},{9,8},{10,11... | collective-permute-start | bytes 786440 | tf_op jit(solution)/shard_map/ppermute | solution.py:22
  44.3 5.4 %collective-permute-start.16 = (bf16[32,1024]{1,0:T(8,128)(2,1)S(1)}, bf16[32,1024]{1,0:T(8,128)(2,1)S(1)}, u32[]{:S(2)}, u32[]{:S(2)}) collective-permute-start(bf16[32,1024]{1,0:T(8,128)(2,1)S(1)} %get-tuple-element.148), channel_id=1, source_target_pairs={{0,6},{2,4},{4,2},{6,0},{1,7},{3,5},{5,3},{7,1},{8,14},{10,12},{12... | collective-permute-start | bytes 196616 | tf_op jit(solution)/shard_map/ppermute | solution.py:31
  45.8 7.2 %collective-permute-start.17 = (bf16[32,1024]{1,0:T(8,128)(2,1)S(1)}, bf16[32,1024]{1,0:T(8,128)(2,1)S(1)}, u32[]{:S(2)}, u32[]{:S(2)}) collective-permute-start(bf16[32,1024]{1,0:T(8,128)(2,1)S(1)} %get-tuple-element.149), channel_id=1, source_target_pairs={{0,4},{2,6},{4,0},{6,2},{1,5},{3,7},{5,1},{7,3},{8,12},{10,14},{12... | collective-permute-start | bytes 196616 | tf_op jit(solution)/shard_map/ppermute | solution.py:31
  45.8 7.2 %collective-permute-start.18 = (bf16[32,1024]{1,0:T(8,128)(2,1)S(1)}, bf16[32,1024]{1,0:T(8,128)(2,1)S(1)}, u32[]{:S(2)}, u32[]{:S(2)}) collective-permute-start(bf16[32,1024]{1,0:T(8,128)(2,1)S(1)} %get-tuple-element.150), channel_id=1, source_target_pairs={{0,2},{2,0},{4,6},{6,4},{1,3},{3,1},{5,7},{7,5},{8,10},{10,8},{12,... | collective-permute-start | bytes 196616 | tf_op jit(solution)/shard_map/ppermute | solution.py:31
  53.0 5.3 %collective-permute-start.19 = (bf16[32,1024]{1,0:T(8,128)(2,1)S(1)}, bf16[32,1024]{1,0:T(8,128)(2,1)S(1)}, u32[]{:S(2)}, u32[]{:S(2)}) collective-permute-start(bf16[32,1024]{1,0:T(8,128)(2,1)S(1)} %get-tuple-element.158), channel_id=1, source_target_pairs={{0,8},{8,16},{16,24},{1,9},{9,17},{17,25},{2,10},{10,18},{18,26},{... | collective-permute-start | bytes 196616 | tf_op jit(solution)/shard_map/ppermute | solution.py:17
  57.1 5.1 %collective-permute-start.20 = (bf16[32,1024]{1,0:T(8,128)(2,1)S(1)}, bf16[32,1024]{1,0:T(8,128)(2,1)S(1)}, u32[]{:S(2)}, u32[]{:S(2)}) collective-permute-start(bf16[32,1024]{1,0:T(8,128)(2,1)S(1)} %get-tuple-element.163.refs_0_.first), channel_id=1, source_target_pairs={{0,6},{2,4},{4,2},{6,0},{1,7},{3,5},{5,3},{7,1},{8,14},{10,12},{12... | collective-permute-start | bytes 196616 | tf_op jit(solution)/shard_map/ppermute | solution.py:31
  58.4 5.4 %collective-permute-start.23 = (bf16[32,1024]{1,0:T(8,128)(2,1)S(1)}, bf16[32,1024]{1,0:T(8,128)(2,1)S(1)}, u32[]{:S(2)}, u32[]{:S(2)}) collective-permute-start(bf16[32,1024]{1,0:T(8,128)(2,1)S(1)} %arrive.5.refs_1_.first_out.refs_14_), channel_id=1, source_target_pairs={{0,2},{2,0},{4,6},{6,4},{1,3},{3,1},{5,7},{7,5},{8,10},{10,8},{12,... | collective-permute-start | bytes 196616 | tf_op jit(solution)/shard_map/ppermute | solution.py:31
  58.5 5.3 %collective-permute-start.22 = (bf16[32,1024]{1,0:T(8,128)(2,1)S(1)}, bf16[32,1024]{1,0:T(8,128)(2,1)S(1)}, u32[]{:S(2)}, u32[]{:S(2)}) collective-permute-start(bf16[32,1024]{1,0:T(8,128)(2,1)S(1)} %arrive.5.refs_1_.first_out.refs_14_), channel_id=1, source_target_pairs={{0,4},{2,6},{4,0},{6,2},{1,5},{3,7},{5,1},{7,3},{8,12},{10,14},{12... | collective-permute-start | bytes 196616 | tf_op jit(solution)/shard_map/ppermute | solution.py:31
  60.8 5.7 %collective-permute-start.21 = (bf16[32,1024]{1,0:T(8,128)(2,1)S(1)}, bf16[32,1024]{1,0:T(8,128)(2,1)S(1)}, u32[]{:S(2)}, u32[]{:S(2)}) collective-permute-start(bf16[32,1024]{1,0:T(8,128)(2,1)S(1)} %arrive.5.refs_1_.first_out.refs_14_), channel_id=1, source_target_pairs={{0,6},{2,4},{4,2},{6,0},{1,7},{3,5},{5,3},{7,1},{8,14},{10,12},{12... | collective-permute-start | bytes 196616 | tf_op jit(solution)/shard_map/ppermute | solution.py:31
  67.3 5.0 %collective-permute-start.25 = (bf16[128,1024]{1,0:T(8,128)(2,1)S(1)}, bf16[128,1024]{1,0:T(8,128)(2,1)S(1)}, u32[]{:S(2)}, u32[]{:S(2)}) collective-permute-start(bf16[128,1024]{1,0:T(8,128)(2,1)S(1)} %product_part.8.refs_2_), channel_id=1, source_target_pairs={{0,1},{1,0},{2,3},{3,2},{4,5},{5,4},{6,7},{7,6},{8,9},{9,8},{10,11... | collective-permute-start | bytes 786440 | tf_op jit(solution)/shard_map/ppermute | solution.py:22
  69.5 1.6 %collective-permute-start.27 = (bf16[128,1024]{1,0:T(8,128)(2,1)S(1)}, bf16[128,1024]{1,0:T(8,128)(2,1)S(1)}, u32[]{:S(2)}, u32[]{:S(2)}) collective-permute-start(bf16[128,1024]{1,0:T(8,128)(2,1)S(1)} %get-tuple-element.181.refs_2_.refs_0_), channel_id=1, source_target_pairs={{0,1},{1,0},{2,3},{3,2},{4,5},{5,4},{6,7},{7,6},{8,9},{9,8},{10,11... | collective-permute-start | bytes 786440 | tf_op jit(solution)/shard_map/ppermute | solution.py:22
  70.1 1.7 %collective-permute-start.26 = (bf16[128,1024]{1,0:T(8,128)(2,1)S(1)}, bf16[128,1024]{1,0:T(8,128)(2,1)S(1)}, u32[]{:S(2)}, u32[]{:S(2)}) collective-permute-start(bf16[128,1024]{1,0:T(8,128)(2,1)S(1)} %get-tuple-element.168.refs_0_), channel_id=1, source_target_pairs={{0,1},{1,0},{2,3},{3,2},{4,5},{5,4},{6,7},{7,6},{8,9},{9,8},{10,11... | collective-permute-start | bytes 786440 | tf_op jit(solution)/shard_map/ppermute | solution.py:22
  71.0 1.6 %collective-permute-start.24 = (bf16[128,1024]{1,0:T(8,128)(2,1)S(1)}, bf16[128,1024]{1,0:T(8,128)(2,1)S(1)}, u32[]{:S(2)}, u32[]{:S(2)}) collective-permute-start(bf16[128,1024]{1,0:T(8,128)(2,1)S(1)} %product_part.9.refs_0_), channel_id=1, source_target_pairs={{0,1},{1,0},{2,3},{3,2},{4,5},{5,4},{6,7},{7,6},{8,9},{9,8},{10,11... | collective-permute-start | bytes 786440 | tf_op jit(solution)/shard_map/ppermute | solution.py:22
  73.2 5.4 %collective-permute-start.28 = (bf16[32,1024]{1,0:T(8,128)(2,1)S(1)}, bf16[32,1024]{1,0:T(8,128)(2,1)S(1)}, u32[]{:S(2)}, u32[]{:S(2)}) collective-permute-start(bf16[32,1024]{1,0:T(8,128)(2,1)S(1)} %get-tuple-element.172), channel_id=1, source_target_pairs={{0,6},{2,4},{4,2},{6,0},{1,7},{3,5},{5,3},{7,1},{8,14},{10,12},{12... | collective-permute-start | bytes 196616 | tf_op jit(solution)/shard_map/ppermute | solution.py:31
  74.9 7.2 %collective-permute-start.29 = (bf16[32,1024]{1,0:T(8,128)(2,1)S(1)}, bf16[32,1024]{1,0:T(8,128)(2,1)S(1)}, u32[]{:S(2)}, u32[]{:S(2)}) collective-permute-start(bf16[32,1024]{1,0:T(8,128)(2,1)S(1)} %get-tuple-element.173), channel_id=1, source_target_pairs={{0,4},{2,6},{4,0},{6,2},{1,5},{3,7},{5,1},{7,3},{8,12},{10,14},{12... | collective-permute-start | bytes 196616 | tf_op jit(solution)/shard_map/ppermute | solution.py:31
  75.3 6.8 %collective-permute-start.30 = (bf16[32,1024]{1,0:T(8,128)(2,1)S(1)}, bf16[32,1024]{1,0:T(8,128)(2,1)S(1)}, u32[]{:S(2)}, u32[]{:S(2)}) collective-permute-start(bf16[32,1024]{1,0:T(8,128)(2,1)S(1)} %get-tuple-element.174), channel_id=1, source_target_pairs={{0,2},{2,0},{4,6},{6,4},{1,3},{3,1},{5,7},{7,5},{8,10},{10,8},{12,... | collective-permute-start | bytes 196616 | tf_op jit(solution)/shard_map/ppermute | solution.py:31
  82.2 5.9 %collective-permute-start.31 = (bf16[32,1024]{1,0:T(8,128)(2,1)S(1)}, bf16[32,1024]{1,0:T(8,128)(2,1)S(1)}, u32[]{:S(2)}, u32[]{:S(2)}) collective-permute-start(bf16[32,1024]{1,0:T(8,128)(2,1)S(1)} %leave_back.2.refs_11_), channel_id=1, source_target_pairs={{8,0},{16,8},{24,16},{9,1},{17,9},{25,17},{10,2},{18,10},{26,18},{... | collective-permute-start | bytes 196616 | tf_op jit(solution)/shard_map/ppermute | solution.py:17
  85.3 6.5 %collective-permute-start.32 = (bf16[32,1024]{1,0:T(8,128)(2,1)S(1)}, bf16[32,1024]{1,0:T(8,128)(2,1)S(1)}, u32[]{:S(2)}, u32[]{:S(2)}) collective-permute-start(bf16[32,1024]{1,0:T(8,128)(2,1)S(1)} %get-tuple-element.192), channel_id=1, source_target_pairs={{0,2},{2,0},{4,6},{6,4},{1,3},{3,1},{5,7},{7,5},{8,10},{10,8},{12,... | collective-permute-start | bytes 196616 | tf_op jit(solution)/shard_map/ppermute | solution.py:31
  85.3 6.4 %collective-permute-start.33 = (bf16[32,1024]{1,0:T(8,128)(2,1)S(1)}, bf16[32,1024]{1,0:T(8,128)(2,1)S(1)}, u32[]{:S(2)}, u32[]{:S(2)}) collective-permute-start(bf16[32,1024]{1,0:T(8,128)(2,1)S(1)} %get-tuple-element.193), channel_id=1, source_target_pairs={{0,4},{2,6},{4,0},{6,2},{1,5},{3,7},{5,1},{7,3},{8,12},{10,14},{12... | collective-permute-start | bytes 196616 | tf_op jit(solution)/shard_map/ppermute | solution.py:31
  88.1 3.7 %collective-permute-start.36 = (bf16[32,1024]{1,0:T(8,128)(2,1)S(1)}, bf16[32,1024]{1,0:T(8,128)(2,1)S(1)}, u32[]{:S(2)}, u32[]{:S(2)}) collective-permute-start(bf16[32,1024]{1,0:T(8,128)(2,1)S(1)} %arrive.6.refs_2_.first), channel_id=1, source_target_pairs={{0,2},{2,0},{4,6},{6,4},{1,3},{3,1},{5,7},{7,5},{8,10},{10,8},{12,... | collective-permute-start | bytes 196616 | tf_op jit(solution)/shard_map/ppermute | solution.py:31
  88.2 4.5 %collective-permute-start.35 = (bf16[32,1024]{1,0:T(8,128)(2,1)S(1)}, bf16[32,1024]{1,0:T(8,128)(2,1)S(1)}, u32[]{:S(2)}, u32[]{:S(2)}) collective-permute-start(bf16[32,1024]{1,0:T(8,128)(2,1)S(1)} %arrive.6.refs_2_.first), channel_id=1, source_target_pairs={{0,4},{2,6},{4,0},{6,2},{1,5},{3,7},{5,1},{7,3},{8,12},{10,14},{12... | collective-permute-start | bytes 196616 | tf_op jit(solution)/shard_map/ppermute | solution.py:31
  90.3 5.3 %collective-permute-start.34 = (bf16[32,1024]{1,0:T(8,128)(2,1)S(1)}, bf16[32,1024]{1,0:T(8,128)(2,1)S(1)}, u32[]{:S(2)}, u32[]{:S(2)}) collective-permute-start(bf16[32,1024]{1,0:T(8,128)(2,1)S(1)} %arrive.6.refs_2_.first), channel_id=1, source_target_pairs={{0,6},{2,4},{4,2},{6,0},{1,7},{3,5},{5,3},{7,1},{8,14},{10,12},{12... | collective-permute-start | bytes 196616 | tf_op jit(solution)/shard_map/ppermute | solution.py:31
  96.1 4.0 %collective-permute-start.38 = (bf16[128,1024]{1,0:T(8,128)(2,1)S(1)}, bf16[128,1024]{1,0:T(8,128)(2,1)S(1)}, u32[]{:S(2)}, u32[]{:S(2)}) collective-permute-start(bf16[128,1024]{1,0:T(8,128)(2,1)S(1)} %get-tuple-element.195.refs_0_), channel_id=1, source_target_pairs={{0,1},{1,0},{2,3},{3,2},{4,5},{5,4},{6,7},{7,6},{8,9},{9,8},{10,11... | collective-permute-start | bytes 786440 | tf_op jit(solution)/shard_map/ppermute | solution.py:22
  99.4 1.6 %collective-permute-start.37 = (bf16[128,1024]{1,0:T(8,128)(2,1)S(1)}, bf16[128,1024]{1,0:T(8,128)(2,1)S(1)}, u32[]{:S(2)}, u32[]{:S(2)}) collective-permute-start(bf16[128,1024]{1,0:T(8,128)(2,1)S(1)} %product_part.10.refs_0_), channel_id=1, source_target_pairs={{0,1},{1,0},{2,3},{3,2},{4,5},{5,4},{6,7},{7,6},{8,9},{9,8},{10,11... | collective-permute-start | bytes 786440 | tf_op jit(solution)/shard_map/ppermute | solution.py:22
  101.6 5.4 %collective-permute-start.39 = (bf16[32,1024]{1,0:T(8,128)(2,1)S(1)}, bf16[32,1024]{1,0:T(8,128)(2,1)S(1)}, u32[]{:S(2)}, u32[]{:S(2)}) collective-permute-start(bf16[32,1024]{1,0:T(8,128)(2,1)S(1)} %get-tuple-element.198), channel_id=1, source_target_pairs={{0,6},{2,4},{4,2},{6,0},{1,7},{3,5},{5,3},{7,1},{8,14},{10,12},{12... | collective-permute-start | bytes 196616 | tf_op jit(solution)/shard_map/ppermute | solution.py:31
  103.3 7.0 %collective-permute-start.40 = (bf16[32,1024]{1,0:T(8,128)(2,1)S(1)}, bf16[32,1024]{1,0:T(8,128)(2,1)S(1)}, u32[]{:S(2)}, u32[]{:S(2)}) collective-permute-start(bf16[32,1024]{1,0:T(8,128)(2,1)S(1)} %get-tuple-element.199), channel_id=1, source_target_pairs={{0,4},{2,6},{4,0},{6,2},{1,5},{3,7},{5,1},{7,3},{8,12},{10,14},{12... | collective-permute-start | bytes 196616 | tf_op jit(solution)/shard_map/ppermute | solution.py:31
  103.3 7.0 %collective-permute-start.41 = (bf16[32,1024]{1,0:T(8,128)(2,1)S(1)}, bf16[32,1024]{1,0:T(8,128)(2,1)S(1)}, u32[]{:S(2)}, u32[]{:S(2)}) collective-permute-start(bf16[32,1024]{1,0:T(8,128)(2,1)S(1)} %get-tuple-element.200), channel_id=1, source_target_pairs={{0,2},{2,0},{4,6},{6,4},{1,3},{3,1},{5,7},{7,5},{8,10},{10,8},{12,... | collective-permute-start | bytes 196616 | tf_op jit(solution)/shard_map/ppermute | solution.py:31
  110.3 5.9 %collective-permute-start.42 = (bf16[32,1024]{1,0:T(8,128)(2,1)S(1)}, bf16[32,1024]{1,0:T(8,128)(2,1)S(1)}, u32[]{:S(2)}, u32[]{:S(2)}) collective-permute-start(bf16[32,1024]{1,0:T(8,128)(2,1)S(1)} %leave_back.3.refs_10_), channel_id=1, source_target_pairs={{8,0},{16,8},{24,16},{9,1},{17,9},{25,17},{10,2},{18,10},{26,18},{... | collective-permute-start | bytes 196616 | tf_op jit(solution)/shard_map/ppermute | solution.py:17
  112.3 7.6 %collective-permute-start.43 = (bf16[32,1024]{1,0:T(8,128)(2,1)S(1)}, bf16[32,1024]{1,0:T(8,128)(2,1)S(1)}, u32[]{:S(2)}, u32[]{:S(2)}) collective-permute-start(bf16[32,1024]{1,0:T(8,128)(2,1)S(1)} %get-tuple-element.205), channel_id=1, source_target_pairs={{0,6},{2,4},{4,2},{6,0},{1,7},{3,5},{5,3},{7,1},{8,14},{10,12},{12... | collective-permute-start | bytes 196616 | tf_op jit(solution)/shard_map/ppermute | solution.py:31
  116.3 3.6 %collective-permute-start.46 = (bf16[32,1024]{1,0:T(8,128)(2,1)S(1)}, bf16[32,1024]{1,0:T(8,128)(2,1)S(1)}, u32[]{:S(2)}, u32[]{:S(2)}) collective-permute-start(bf16[32,1024]{1,0:T(8,128)(2,1)S(1)} %arrive.7.refs_1_.first_grad), channel_id=1, source_target_pairs={{0,2},{2,0},{4,6},{6,4},{1,3},{3,1},{5,7},{7,5},{8,10},{10,8},{12,... | collective-permute-start | bytes 196616 | tf_op jit(solution)/shard_map/ppermute | solution.py:31
  116.3 4.1 %collective-permute-start.45 = (bf16[32,1024]{1,0:T(8,128)(2,1)S(1)}, bf16[32,1024]{1,0:T(8,128)(2,1)S(1)}, u32[]{:S(2)}, u32[]{:S(2)}) collective-permute-start(bf16[32,1024]{1,0:T(8,128)(2,1)S(1)} %arrive.7.refs_1_.first_grad), channel_id=1, source_target_pairs={{0,4},{2,6},{4,0},{6,2},{1,5},{3,7},{5,1},{7,3},{8,12},{10,14},{12... | collective-permute-start | bytes 196616 | tf_op jit(solution)/shard_map/ppermute | solution.py:31
  118.2 4.9 %collective-permute-start.44 = (bf16[32,1024]{1,0:T(8,128)(2,1)S(1)}, bf16[32,1024]{1,0:T(8,128)(2,1)S(1)}, u32[]{:S(2)}, u32[]{:S(2)}) collective-permute-start(bf16[32,1024]{1,0:T(8,128)(2,1)S(1)} %arrive.7.refs_1_.first_grad), channel_id=1, source_target_pairs={{0,6},{2,4},{4,2},{6,0},{1,7},{3,5},{5,3},{7,1},{8,14},{10,12},{12... | collective-permute-start | bytes 196616 | tf_op jit(solution)/shard_map/ppermute | solution.py:31
  123.6 6.0 %collective-permute-start.48 = (bf16[128,1024]{1,0:T(8,128)(2,1)S(1)}, bf16[128,1024]{1,0:T(8,128)(2,1)S(1)}, u32[]{:S(2)}, u32[]{:S(2)}) collective-permute-start(bf16[128,1024]{1,0:T(8,128)(2,1)S(1)} %get-tuple-element.208.refs_0_), channel_id=1, source_target_pairs={{0,1},{1,0},{2,3},{3,2},{4,5},{5,4},{6,7},{7,6},{8,9},{9,8},{10,11... | collective-permute-start | bytes 786440 | tf_op jit(solution)/shard_map/ppermute | solution.py:22
  127.5 2.8 %collective-permute-start.47 = (bf16[128,1024]{1,0:T(8,128)(2,1)S(1)}, bf16[128,1024]{1,0:T(8,128)(2,1)S(1)}, u32[]{:S(2)}, u32[]{:S(2)}) collective-permute-start(bf16[128,1024]{1,0:T(8,128)(2,1)S(1)} %product_part.11.refs_0_), channel_id=1, source_target_pairs={{0,1},{1,0},{2,3},{3,2},{4,5},{5,4},{6,7},{7,6},{8,9},{9,8},{10,11... | collective-permute-start | bytes 786440 | tf_op jit(solution)/shard_map/ppermute | solution.py:22
  130.9 9.1 %collective-permute-start.49 = (bf16[32,1024]{1,0:T(8,128)(2,1)S(1)}, bf16[32,1024]{1,0:T(8,128)(2,1)S(1)}, u32[]{:S(2)}, u32[]{:S(2)}) collective-permute-start(bf16[32,1024]{1,0:T(8,128)(2,1)S(1)} %get-tuple-element.214), channel_id=1, source_target_pairs={{0,6},{2,4},{4,2},{6,0},{1,7},{3,5},{5,3},{7,1},{8,14},{10,12},{12... | collective-permute-start | bytes 196616 | tf_op jit(solution)/shard_map/ppermute | solution.py:31
  132.6 7.3 %collective-permute-start.50 = (bf16[32,1024]{1,0:T(8,128)(2,1)S(1)}, bf16[32,1024]{1,0:T(8,128)(2,1)S(1)}, u32[]{:S(2)}, u32[]{:S(2)}) collective-permute-start(bf16[32,1024]{1,0:T(8,128)(2,1)S(1)} %get-tuple-element.215), channel_id=1, source_target_pairs={{0,4},{2,6},{4,0},{6,2},{1,5},{3,7},{5,1},{7,3},{8,12},{10,14},{12... | collective-permute-start | bytes 196616 | tf_op jit(solution)/shard_map/ppermute | solution.py:31
  132.6 7.4 %collective-permute-start.51 = (bf16[32,1024]{1,0:T(8,128)(2,1)S(1)}, bf16[32,1024]{1,0:T(8,128)(2,1)S(1)}, u32[]{:S(2)}, u32[]{:S(2)}) collective-permute-start(bf16[32,1024]{1,0:T(8,128)(2,1)S(1)} %get-tuple-element.216), channel_id=1, source_target_pairs={{0,2},{2,0},{4,6},{6,4},{1,3},{3,1},{5,7},{7,5},{8,10},{10,8},{12,... | collective-permute-start | bytes 196616 | tf_op jit(solution)/shard_map/ppermute | solution.py:31

commit v11 on v10

--- a/solution.py
+++ b/solution.py
@@ -81,9 +81,8 @@
 def fetch_kernel(sample_ids, inputs, send_base, recv_base, cotangent, *refs):
     ticks = inputs.shape[1]
     count = ticks - 1
-    weights, refs = refs[:1], refs[1:]
     stored, bases, cots = refs[:count], refs[count : 2 * count], refs[2 * count : 3 * count]
-    *kept, fresh, sems, weight_sems = refs[3 * count :]
+    fresh, sems = refs[3 * count :]
     section, sections = lax.axis_index("section"), lax.axis_size("section")
     samples = [sample_ids[tick - section + sections - 1] for tick in range(ticks)]
     copies = []
@@ -94,11 +93,6 @@
             pltpu.make_async_copy(inputs.at[0, t + 1], fresh.at[t], sems.at[4 * t + 2]),
             pltpu.make_async_copy(cotangent.at[0, t], cots[t], sems.at[4 * t + 3]),
         ]
-    for k, (weight, room) in enumerate(zip(weights, kept)):
-        step = weight.shape[0] // WEIGHT_CUTS
-        for i in range(WEIGHT_CUTS):
-            part = pl.ds(i * step, step)
-            copies.append(pltpu.make_async_copy(weight.at[part], room.at[part], weight_sems.at[k, i]))
     for copy in copies:
         copy.start()
     for copy in copies:
@@ -108,25 +102,21 @@
         cots[t][...] = jnp.where(section == sections - 1, cots[t][...], jnp.zeros_like(cots[t]))
 
 
-def fetch(sample_ids, inputs, send_base, recv_base, cotangent, weight):
+def fetch(sample_ids, inputs, send_base, recv_base, cotangent):
     count = inputs.shape[1] - 1
     piece = inputs.shape[2:]
-    large = [pltpu.with_memory_space_constraint(x, pltpu.HBM) for x in (inputs, send_base, recv_base, cotangent, weight)]
-    *outs, kept = pl.pallas_call(
+    large = [pltpu.with_memory_space_constraint(x, pltpu.HBM) for x in (inputs, send_base, recv_base, cotangent)]
+    outs = pl.pallas_call(
         fetch_kernel,
         in_specs=[pl.BlockSpec(memory_space=pltpu.SMEM)] + [pl.BlockSpec(memory_space=pltpu.HBM)] * len(large),
-        out_specs=vmem(3 * count + 1),
-        out_shape=[pltpu.VMEM(piece, BF)] * (3 * count) + [pltpu.VMEM(weight.shape, BF)],
-        scratch_shapes=[
-            pltpu.VMEM((count, *piece), BF),
-            pltpu.SemaphoreType.DMA((4 * count,)),
-            pltpu.SemaphoreType.DMA((1, WEIGHT_CUTS)),
-        ],
+        out_specs=vmem(3 * count),
+        out_shape=[pltpu.VMEM(piece, BF)] * (3 * count),
+        scratch_shapes=[pltpu.VMEM((count, *piece), BF), pltpu.SemaphoreType.DMA((4 * count,))],
         compiler_params=pltpu.CompilerParams(vmem_limit_bytes=4 << 20),
-        cost_estimate=pl.CostEstimate(flops=0, bytes_accessed=6 << 20, transcendentals=0),
+        cost_estimate=pl.CostEstimate(flops=0, bytes_accessed=2 << 20, transcendentals=0),
         name="fetch",
     )(sample_ids, *large)
-    return outs[:count], outs[count : 2 * count], outs[2 * count :], kept
+    return outs[:count], outs[count : 2 * count], outs[2 * count :]
 
 
 def first_pieces(inputs, cotangent):
@@ -165,18 +155,34 @@
     out[...] = added(first, terms)
 
 
-def finish(first_out, first_grad, *refs):
-    *rest, ins, outs, grads = refs
-    count = outs.shape[1] - 1
-    terms, known = rest[: -3 * count - 1], rest[-3 * count - 1 :]
-    half = len(terms) // 2
-    outs[0, count] = added(first_out, terms[:half])
-    grads[0, 0] = added(first_grad, terms[half:])
+def finish_forward(count, *refs):
+    *terms, ins, outs = refs
+    entered, left, terms = terms[:count], terms[count : 2 * count - 1], terms[2 * count - 1 :]
     for t in range(count):
-        outs[0, t] = known[t][...]
-        grads[0, t + 1] = known[count + t][...]
-    for t in range(count + 1):
-        ins[0, t] = known[2 * count + t][...]
+        ins[0, t] = entered[t][...]
+    for t in range(count - 1):
+        outs[0, t] = left[t][...]
+    outs[0, count - 1] = added(entered[-1], terms)
+
+
+def finish(first, *refs):
+    *rest, grads = refs
+    count = grads.shape[1] - 1
+    grads[0, 0] = added(first, rest[:-count])
+    for t in range(count):
+        grads[0, t + 1] = rest[t - count][...]
+
+
+def stacked(kernel, count, ins, like, name):
+    return pl.pallas_call(
+        kernel,
+        in_specs=vmem(len(ins)),
+        out_specs=vmem(count),
+        out_shape=[like] * count,
+        compiler_params=pltpu.CompilerParams(vmem_limit_bytes=6 << 20),
+        cost_estimate=pl.CostEstimate(flops=0, bytes_accessed=1 << 20, transcendentals=0),
+        name=name,
+    )(*[pltpu.with_memory_space_constraint(x, pltpu.VMEM) for x in ins])
 
 
 def turned(*refs):
@@ -189,29 +195,32 @@
         out[n, :] = weight[:, n].T
 
 
-def hold_kernel(weight, kept, sems):
-    step = weight.shape[0] // WEIGHT_CUTS
+def hold_kernel(*refs):
+    *refs, sems = refs
+    count = len(refs) // 2
     copies = []
-    for i in range(WEIGHT_CUTS):
-        part = pl.ds(i * step, step)
-        copies.append(pltpu.make_async_copy(weight.at[part], kept.at[part], sems.at[i]))
+    for k in range(count):
+        step = refs[k].shape[0] // WEIGHT_CUTS
+        for i in range(WEIGHT_CUTS):
+            part = pl.ds(i * step, step)
+            copies.append(pltpu.make_async_copy(refs[k].at[part], refs[count + k].at[part], sems.at[k, i]))
     for copy in copies:
         copy.start()
     for copy in copies:
         copy.wait()
 
 
-def hold(weight):
+def hold(weights):
     return pl.pallas_call(
         hold_kernel,
-        in_specs=[pl.BlockSpec(memory_space=pltpu.HBM)],
-        out_specs=pl.BlockSpec(memory_space=pltpu.VMEM),
-        out_shape=pltpu.VMEM(weight.shape, BF),
-        scratch_shapes=[pltpu.SemaphoreType.DMA((WEIGHT_CUTS,))],
+        in_specs=[pl.BlockSpec(memory_space=pltpu.HBM)] * len(weights),
+        out_specs=vmem(len(weights)),
+        out_shape=[pltpu.VMEM(weight.shape, BF) for weight in weights],
+        scratch_shapes=[pltpu.SemaphoreType.DMA((len(weights), WEIGHT_CUTS))],
         compiler_params=pltpu.CompilerParams(vmem_limit_bytes=2 << 20),
-        cost_estimate=pl.CostEstimate(flops=0, bytes_accessed=4 * weight.size, transcendentals=0),
+        cost_estimate=pl.CostEstimate(flops=0, bytes_accessed=16 << 20, transcendentals=0),
         name="hold",
-    )(pltpu.with_memory_space_constraint(weight, pltpu.HBM))
+    )(*[pltpu.with_memory_space_constraint(weight, pltpu.HBM) for weight in weights])
 
 
 def columns(width, step=256):
@@ -309,12 +318,8 @@
         put_rows(pieces, n, total)
 
 
-def weight_grad(start, count, *refs):
-    *blocks, out, left, right, room, sems = refs
-    lefts, rights = blocks[:count], blocks[count:]
-    if start:
-        rights = rights[:-1]
-    depth = rights[0].shape[0]
+def weight_grad(start, lefts, rights, out, left, right, room, sems):
+    count, depth = len(lefts), rights[0].shape[0]
     for t in range(count):
         left[:, t * depth : (t + 1) * depth] = lefts[t][...]
         place = 0
@@ -330,30 +335,46 @@
             pltpu.make_async_copy(room.at[pl.ds(m.start, size)], out.at[pl.ds(start + m.start, size)], sems.at[i])
         )
         copies[-1].start()
+    return copies
+
+
+def weight_grads(cuts, begun, *refs):
+    ins, refs = refs[: sum(left + right for _, left, right in cuts)], refs[sum(left + right for _, left, right in cuts) + begun :]
+    outs, rooms = refs[: len(cuts)], refs[len(cuts) :]
+    copies, place = [], 0
+    for k, (start, left, right) in enumerate(cuts):
+        lefts, rights = ins[place : place + left], ins[place + left : place + left + right]
+        copies += weight_grad(start, lefts, rights, outs[k], *rooms[4 * k : 4 * k + 4])
+        place += left + right
     for copy in copies:
         copy.wait()
 
 
-def weight_product(lefts, rights, shape, start=0, begun=None):
-    count, depth = lefts[0].shape[0], rights[0].shape[0] * len(lefts)
-    ins = [*lefts, *rights]
-    return pl.pallas_call(
-        functools.partial(weight_grad, start, len(lefts)),
-        in_specs=vmem(len(ins)) + [pl.BlockSpec(memory_space=pl.ANY)] * (begun is not None),
-        out_specs=pl.BlockSpec(memory_space=pl.ANY),
-        out_shape=jax.ShapeDtypeStruct(shape, BF),
-        scratch_shapes=[
+def weight_products(jobs, begun=None):
+    cuts, ins, scratch = [], [], []
+    flops = size = 0
+    for lefts, rights, shape, start in jobs:
+        count, depth = lefts[0].shape[0], rights[0].shape[0] * len(lefts)
+        cuts.append((start, len(lefts), len(rights)))
+        ins += [*lefts, *rights]
+        scratch += [
             pltpu.VMEM((count, depth), BF),
             pltpu.VMEM((depth, shape[1]), BF),
             pltpu.VMEM((count, shape[1]), BF),
             pltpu.SemaphoreType.DMA((len(columns(count)),)),
-        ],
-        input_output_aliases={} if begun is None else {len(ins): 0},
-        compiler_params=pltpu.CompilerParams(vmem_limit_bytes=12 << 20),
-        cost_estimate=pl.CostEstimate(
-            flops=2 * count * shape[1] * depth, bytes_accessed=2 * count * shape[1], transcendentals=0
-        ),
-        name="weight_grad",
+        ]
+        flops += 2 * count * shape[1] * depth
+        size += 2 * count * shape[1]
+    return pl.pallas_call(
+        functools.partial(weight_grads, tuple(cuts), begun is not None),
+        in_specs=vmem(len(ins)) + [pl.BlockSpec(memory_space=pl.ANY)] * (begun is not None),
+        out_specs=[pl.BlockSpec(memory_space=pl.ANY)] * len(jobs),
+        out_shape=[jax.ShapeDtypeStruct(shape, BF) for _, _, shape, _ in jobs],
+        scratch_shapes=scratch,
+        input_output_aliases={} if begun is None else {len(ins): len(jobs) - 1},
+        compiler_params=pltpu.CompilerParams(vmem_limit_bytes=18 << 20),
+        cost_estimate=pl.CostEstimate(flops=flops, bytes_accessed=size, transcendentals=0),
+        name="weight_grads",
     )(
         *[pltpu.with_memory_space_constraint(x, pltpu.VMEM) for x in ins],
         *([] if begun is None else [begun]),
@@ -381,6 +402,7 @@
     rows = lax.axis_size("row")
     piece_rows, width = inputs.shape[2:]
     tokens, hidden = rows * piece_rows, w_up.shape[2]
+    stack_like = jax.ShapeDtypeStruct((1, ticks, piece_rows, width), BF)
     parts = [slice(0, hidden // 2), slice(hidden // 2, hidden)]
     piece_like = jax.ShapeDtypeStruct((piece_rows, width), BF)
     part_like = jax.ShapeDtypeStruct((tokens, hidden // 2), BF)
@@ -405,17 +427,14 @@
                 waited.append(cot_pieces[j])
         pieces = gather_rows(act_in)
         if tick == 0:
-            stored, bases, cots, up_kept = fetch(
-                after(sample_ids, act_in), inputs, send_base, recv_base, cotangent, w_up[0]
-            )
-            pieces = after(pieces, stored)
+            up_kept, down_kept = hold(after([w_up[0], w_down[0]], act_in))
+            pieces = after(pieces, up_kept)
+        if tick == ticks - 1:
+            full_cot, first_grads = products(parts, cot_pieces, down_turned)
+            pieces, waited = after(pieces, first_grads), []
         full_in, partial = products(parts, pieces, up_kept, waited)
-        if tick == 0:
-            down_kept = hold(after(w_down[0], partial[-1]))
         pre = [(mine, other_cols(mine)) for mine in partial]
-        if tick == ticks - 1:
-            full_cot, first_grads = products(parts, after(cot_pieces, partial[-1]), down_turned)
-        else:
+        if tick < ticks - 1:
             act, terms = through(silu_part, "down_part", parts, pre, down_kept, piece_like, rows)
             acts.append(act)
             terms_in = scatter_rows(terms)
@@ -423,7 +442,8 @@
                 (down_turned,) = run(
                     turned_weight, [jax.ShapeDtypeStruct((width, hidden), BF)], after(down_kept, terms)
                 )
-                terms_in[0] = after(terms_in[0], down_turned)
+                stored, bases, cots = fetch(after(sample_ids, terms), inputs, send_base, recv_base, cotangent)
+                terms_in[0] = after(terms_in[0], (down_turned, stored))
             if tick == 1:
                 (up_turned,) = run(turned_weight, [jax.ShapeDtypeStruct((hidden, width), BF)], after(up_kept, terms))
                 turn_blocks(0, terms)
@@ -453,11 +473,18 @@
             for j in beside(step - 1):
                 out_terms[j] = swap_rows(after(out_pieces[j], sending), j)
                 waited.append(out_terms[j])
-            full_grad, partial = products(parts, gather_rows(grad_out), down_turned, waited)
+            pieces = gather_rows(grad_out)
+            if step == ticks - 1:
+                section_input, section_output = stacked(
+                    functools.partial(finish_forward, ticks), 2, [*seen_in, *seen_out, *out_terms], stack_like,
+                    "finish_forward",
+                )
+                pieces, waited = after(pieces, section_output), []
+            full_grad, partial = products(parts, pieces, down_turned, waited)
         full_grads[tick] = full_grad
         ins = [(mine, other_cols(mine), *known) for mine, known in zip(partial, pres[tick])]
         if step == ticks - 1:
-            half_down = weight_product(turned_acts[0], full_grads, (hidden, width))
+            (half_down,) = weight_products([(turned_acts[0], full_grads, (hidden, width), 0)])
             ins[0] = after(ins[0], half_down)
         grad_pre, terms = through(slope_part, "in_part", parts, ins, up_turned, piece_like, rows)
         terms_in = scatter_rows(terms)
@@ -468,18 +495,15 @@
             seen_grad[tick] = sending
         pre_grads[tick] = grad_pre
     turned_ins, last_acts = after((turned_ins, turned_acts[1]), terms)
-    grad_up = weight_product(turned_ins, [part for grad_pre in pre_grads for part in grad_pre], (width, hidden))
-    grad_down = weight_product(last_acts, full_grads, (hidden, width), hidden // 2, half_down)
-    stack_like = jax.ShapeDtypeStruct((1, ticks, piece_rows, width), BF)
+    grad_up, grad_down = weight_products(
+        [
+            (turned_ins, [part for grad_pre in pre_grads for part in grad_pre], (width, hidden), 0),
+            (last_acts, full_grads, (hidden, width), hidden // 2),
+        ],
+        half_down,
+    )
     terms_in[0] = after(terms_in[0], (grad_up, grad_down))
-    section_input, section_output, input_grad = pl.pallas_call(
-        finish,
-        in_specs=vmem(2 + 2 * rows + 3 * ticks - 2),
-        out_specs=vmem(3),
-        out_shape=[stack_like] * 3,
-        compiler_params=pltpu.CompilerParams(vmem_limit_bytes=6 << 20),
-        name="finish",
-    )(act_in, grad_out, *out_terms, *terms_in, *seen_out, *seen_grad[1:], *seen_in)
+    (input_grad,) = stacked(finish, 1, [grad_out, *terms_in, *seen_grad[1:]], stack_like, "finish")
     return (
         section_input,
         section_output,

time: 142 us -> 136 us (0.958)
  starting transfers between devices: 69.7 us -> 63.2 us
  waiting for transfers between devices: 39.3 us -> 42 us
    ppermute x12, starting transfers between devices: 15.4 us -> 8.78 us  [turn(): lax.ppermute(block, axis, [(i, (i + distance) % size) for i in range(size)])]
    ppermute x36, waiting for transfers between devices: 33.3 us -> 34.7 us  [swap_rows(): lax.ppermute(block, 'row', [(i, partner(i, j, size)) for i in range(size)])]
  transfers between devices with their start and end apart: 52 -> 52, of which waited for: 26 -> 27; matrix products, arithmetic and copies ran while one was open for 0% -> 0% of each run, Pallas kernels for 16% -> 17%
where the time goes in v11:
time: 136 us
  starting transfers between devices  63.2 us (46%)
  waiting for transfers between devices  42 us (31%)
  Pallas kernels  29.5 us (22%)
    ppermute x36, starting transfers between devices, swap_rows(): lax.ppermute(block, 'row', [(i, partner(i, j, size)) for i in range(size)])  44 us
    ppermute x36, waiting for transfers between devices, swap_rows(): lax.ppermute(block, 'row', [(i, partner(i, j, size)) for i in range(size)])  34.7 us
    pallas_call x43, Pallas kernels, run(): pl.pallas_call(kernel, in_specs=vmem(len(ins)), out_specs=vmem(len(outs))...  15.5 us
    ppermute x4, starting transfers between devices, hand_over(): lax.ppermute(block, 'section', [(i - distance, i) for i in sections if i...  10.4 us
    ppermute x12, starting transfers between devices, turn(): lax.ppermute(block, axis, [(i, (i + distance) % size) for i in range(size)])  8.78 us
    pallas_call x2, Pallas kernels, weight_products(): pl.pallas_call(functools.partial(weight_grads, tuple(cuts), begun is not...  6.4 us
    ppermute x12, waiting for transfers between devices, turn(): lax.ppermute(block, axis, [(i, (i + distance) % size) for i in range(size)])  3.98 us
    pallas_call x1, Pallas kernels, hold(): pl.pallas_call(hold_kernel, in_specs=[pl.BlockSpec(memory_space=pltpu.HBM...  3.51 us
  transfers between devices with their start and end apart: 52, of which 27 were waited for; matrix products, arithmetic and copies ran while one was open for 0% of the time, Pallas kernels for 17%

profile of v11, /device:TPU:3, one launch (start us, length us, event | category | flops | bytes accessed | tf_op | source)
XLA Modules:
  0.0 135.8 jit_solution(2432303571716706022)
XLA Ops:
  0.6 0.9 first.1
  1.5 3.4 %collective-permute-start = (bf16[32,1024]{1,0:T(8,128)(2,1)S(1)}, bf16[32,1024]{1,0:T(8,128)(2,1)S(1)}, u32[]{:S(2)}, u32[]{:S(2)}) collective-permute-start(bf16[32,1024]{1,0:T(8,128)(2,1)S(1)} %get-tuple-element.131.refs_0_.first), channel_id=1, source_target_pairs={{0,6},{2,4},{4,2},{6,0},{1,7},{3,5},{5,3},{7,1},{8,14},{10,12},{12... | collective-permute-start | bytes 196616 | tf_op jit(solution)/shard_map/ppermute | solution.py:31
  5.3 3.5 %hold.1 = (bf16[1024,2048]{1,0:T(8,128)(2,1)S(1)}, bf16[2048,1024]{1,0:T(8,128)(2,1)S(1)}) custom-call(bf16[1024,2048]{1,0:T(8,128)(2,1)} %bitcast.4, bf16[2048,1024]{1,0:T(8,128)(2,1)} %bitcast.5), custom_call_target="tpu_custom_call" | custom-call | bytes 16777216 | tf_op jit(solution)/shard_map/hold/pallas_call | solution.py:214
  8.8 2.0 %collective-permute-done.1.refs_2_ = bf16[32,1024]{1,0:T(8,128)(2,1)S(1)} collective-permute-done((bf16[32,1024]{1,0:T(8,128)(2,1)S(1)}, bf16[32,1024]{1,0:T(8,128)(2,1)S(1)}, u32[]{:S(2)}, u32[]{:S(2)}) %collective-permute-start.1) | collective-permute-done | bytes 65568 | tf_op jit(solution)/shard_map/ppermute | solution.py:31
  11.3 0.7 collective-permute-start.4
  12.5 0.6 collective-permute-done.4.refs_1_.refs_3_
  14.5 2.5 %collective-permute-start.5 = (bf16[32,1024]{1,0:T(8,128)(2,1)S(1)}, bf16[32,1024]{1,0:T(8,128)(2,1)S(1)}, u32[]{:S(2)}, u32[]{:S(2)}) collective-permute-start(bf16[32,1024]{1,0:T(8,128)(2,1)S(1)} %get-tuple-element.140), channel_id=1, source_target_pairs={{0,6},{2,4},{4,2},{6,0},{1,7},{3,5},{5,3},{7,1},{8,14},{10,12},{12... | collective-permute-start | bytes 196616 | tf_op jit(solution)/shard_map/ppermute | solution.py:31
  17.0 1.1 collective-permute-start.7
  18.1 1.2 turned_weight.2.refs_4_.weight.refs_6_
  19.4 1.7 %fetch.1 = (bf16[32,1024]{1,0:T(8,128)(2,1)S(1)}, bf16[32,1024]{1,0:T(8,128)(2,1)S(1)}, bf16[32,1024]{1,0:T(8,128)(2,1)S(1)}, bf16[32,1024]{1,0:T(8,128)(2,1)S(1...) custom-call(s32[6]{0:T(128)S(1)} %copy-done, bf16[1,3,32,1024]{3,2,1,0:T(8,128)(2,1)} %inputs.3, ...), custom_call_target="tpu_custom_call" | custom-call | bytes 2097152 | tf_op jit(solution)/shard_map/fetch/pallas_call | solution.py:109
  21.1 2.3 %collective-permute-done.6.refs_2_ = bf16[32,1024]{1,0:T(8,128)(2,1)S(1)} collective-permute-done((bf16[32,1024]{1,0:T(8,128)(2,1)S(1)}, bf16[32,1024]{1,0:T(8,128)(2,1)S(1)}, u32[]{:S(2)}, u32[]{:S(2)}) %collective-permute-start.6) | collective-permute-done | bytes 65568 | tf_op jit(solution)/shard_map/ppermute | solution.py:31
  23.5 3.1 %collective-permute-start.8 = (bf16[32,1024]{1,0:T(8,128)(2,1)S(1)}, bf16[32,1024]{1,0:T(8,128)(2,1)S(1)}, u32[]{:S(2)}, u32[]{:S(2)}) collective-permute-start(bf16[32,1024]{1,0:T(8,128)(2,1)S(1)} %get-tuple-element.149), channel_id=1, source_target_pairs={{0,8},{8,16},{16,24},{1,9},{9,17},{17,25},{2,10},{10,18},{18,26},{... | collective-permute-start | bytes 196616 | tf_op jit(solution)/shard_map/ppermute | solution.py:17
  26.7 2.4 %collective-permute-start.10 = (bf16[32,1024]{1,0:T(8,128)(2,1)S(1)}, bf16[32,1024]{1,0:T(8,128)(2,1)S(1)}, u32[]{:S(2)}, u32[]{:S(2)}) collective-permute-start(bf16[32,1024]{1,0:T(8,128)(2,1)S(1)} %get-tuple-element.170.refs_0_.first), channel_id=1, source_target_pairs={{0,4},{2,6},{4,0},{6,2},{1,5},{3,7},{5,1},{7,3},{8,12},{10,14},{12... | collective-permute-start | bytes 196616 | tf_op jit(solution)/shard_map/ppermute | solution.py:31
  29.1 1.6 %collective-permute-start.11 = (bf16[32,1024]{1,0:T(8,128)(2,1)S(1)}, bf16[32,1024]{1,0:T(8,128)(2,1)S(1)}, u32[]{:S(2)}, u32[]{:S(2)}) collective-permute-start(bf16[32,1024]{1,0:T(8,128)(2,1)S(1)} %arrive.4.refs_2_.first.refs_1_), channel_id=1, source_target_pairs={{0,6},{2,4},{4,2},{6,0},{1,7},{3,5},{5,3},{7,1},{8,14},{10,12},{12... | collective-permute-start | bytes 196616 | tf_op jit(solution)/shard_map/ppermute | solution.py:31
  30.7 2.0 %collective-permute-start.13 = (bf16[32,1024]{1,0:T(8,128)(2,1)S(1)}, bf16[32,1024]{1,0:T(8,128)(2,1)S(1)}, u32[]{:S(2)}, u32[]{:S(2)}) collective-permute-start(bf16[32,1024]{1,0:T(8,128)(2,1)S(1)} %arrive.4.refs_2_.first.refs_1_), channel_id=1, source_target_pairs={{0,2},{2,0},{4,6},{6,4},{1,3},{3,1},{5,7},{7,5},{8,10},{10,8},{12,... | collective-permute-start | bytes 196616 | tf_op jit(solution)/shard_map/ppermute | solution.py:31
  32.7 1.4 %collective-permute-done.11.refs_3_ = bf16[32,1024]{1,0:T(8,128)(2,1)S(1)} collective-permute-done((bf16[32,1024]{1,0:T(8,128)(2,1)S(1)}, bf16[32,1024]{1,0:T(8,128)(2,1)S(1)}, u32[]{:S(2)}, u32[]{:S(2)}) %collective-permute-start.11) | collective-permute-done | bytes 65568 | tf_op jit(solution)/shard_map/ppermute | solution.py:31
  34.1 3.8 %collective-permute-done.12.refs_4_ = bf16[32,1024]{1,0:T(8,128)(2,1)S(1)} collective-permute-done((bf16[32,1024]{1,0:T(8,128)(2,1)S(1)}, bf16[32,1024]{1,0:T(8,128)(2,1)S(1)}, u32[]{:S(2)}, u32[]{:S(2)}) %collective-permute-start.12) | collective-permute-done | bytes 65568 | tf_op jit(solution)/shard_map/ppermute | solution.py:31
  38.3 1.8 %collective-permute-start.15 = (bf16[128,1024]{1,0:T(8,128)(2,1)S(1)}, bf16[128,1024]{1,0:T(8,128)(2,1)S(1)}, u32[]{:S(2)}, u32[]{:S(2)}) collective-permute-start(bf16[128,1024]{1,0:T(8,128)(2,1)S(1)} %get-tuple-element.154.refs_0_.refs_2_), channel_id=1, source_target_pairs={{0,1},{1,0},{2,3},{3,2},{4,5},{5,4},{6,7},{7,6},{8,9},{9,8},{10,11... | collective-permute-start | bytes 786440 | tf_op jit(solution)/shard_map/ppermute | solution.py:22
  40.7 0.6 collective-permute-done.15.refs_1_.refs_3_
  42.7 1.7 %collective-permute-start.16 = (bf16[32,1024]{1,0:T(8,128)(2,1)S(1)}, bf16[32,1024]{1,0:T(8,128)(2,1)S(1)}, u32[]{:S(2)}, u32[]{:S(2)}) collective-permute-start(bf16[32,1024]{1,0:T(8,128)(2,1)S(1)} %get-tuple-element.157), channel_id=1, source_target_pairs={{0,6},{2,4},{4,2},{6,0},{1,7},{3,5},{5,3},{7,1},{8,14},{10,12},{12... | collective-permute-start | bytes 196616 | tf_op jit(solution)/shard_map/ppermute | solution.py:31
  44.4 1.9 %collective-permute-start.18 = (bf16[32,1024]{1,0:T(8,128)(2,1)S(1)}, bf16[32,1024]{1,0:T(8,128)(2,1)S(1)}, u32[]{:S(2)}, u32[]{:S(2)}) collective-permute-start(bf16[32,1024]{1,0:T(8,128)(2,1)S(1)} %get-tuple-element.159), channel_id=1, source_target_pairs={{0,2},{2,0},{4,6},{6,4},{1,3},{3,1},{5,7},{7,5},{8,10},{10,8},{12,... | collective-permute-start | bytes 196616 | tf_op jit(solution)/shard_map/ppermute | solution.py:31
  46.3 1.2 turned_weight.3.refs_4_
  48.1 3.3 %collective-permute-done.17.refs_2_ = bf16[32,1024]{1,0:T(8,128)(2,1)S(1)} collective-permute-done((bf16[32,1024]{1,0:T(8,128)(2,1)S(1)}, bf16[32,1024]{1,0:T(8,128)(2,1)S(1)}, u32[]{:S(2)}, u32[]{:S(2)}) %collective-permute-start.17) | collective-permute-done | bytes 65568 | tf_op jit(solution)/shard_map/ppermute | solution.py:31
  51.5 3.3 %collective-permute-start.19 = (bf16[32,1024]{1,0:T(8,128)(2,1)S(1)}, bf16[32,1024]{1,0:T(8,128)(2,1)S(1)}, u32[]{:S(2)}, u32[]{:S(2)}) collective-permute-start(bf16[32,1024]{1,0:T(8,128)(2,1)S(1)} %get-tuple-element.167), channel_id=1, source_target_pairs={{0,8},{8,16},{16,24},{1,9},{9,17},{17,25},{2,10},{10,18},{18,26},{... | collective-permute-start | bytes 196616 | tf_op jit(solution)/shard_map/ppermute | solution.py:17
  54.7 1.6 %collective-permute-start.23 = (bf16[32,1024]{1,0:T(8,128)(2,1)S(1)}, bf16[32,1024]{1,0:T(8,128)(2,1)S(1)}, u32[]{:S(2)}, u32[]{:S(2)}) collective-permute-start(bf16[32,1024]{1,0:T(8,128)(2,1)S(1)} %get-tuple-element.170.refs_0_.first), channel_id=1, source_target_pairs={{0,6},{2,4},{4,2},{6,0},{1,7},{3,5},{5,3},{7,1},{8,14},{10,12},{12... | collective-permute-start | bytes 196616 | tf_op jit(solution)/shard_map/ppermute | solution.py:31
  56.5 1.7 %collective-permute-start.20 = (bf16[32,1024]{1,0:T(8,128)(2,1)S(1)}, bf16[32,1024]{1,0:T(8,128)(2,1)S(1)}, u32[]{:S(2)}, u32[]{:S(2)}) collective-permute-start(bf16[32,1024]{1,0:T(8,128)(2,1)S(1)} %arrive.5.refs_0_.refs_2_), channel_id=1, source_target_pairs={{0,6},{2,4},{4,2},{6,0},{1,7},{3,5},{5,3},{7,1},{8,14},{10,12},{12... | collective-permute-start | bytes 196616 | tf_op jit(solution)/shard_map/ppermute | solution.py:31
  58.2 1.9 %collective-permute-start.22 = (bf16[32,1024]{1,0:T(8,128)(2,1)S(1)}, bf16[32,1024]{1,0:T(8,128)(2,1)S(1)}, u32[]{:S(2)}, u32[]{:S(2)}) collective-permute-start(bf16[32,1024]{1,0:T(8,128)(2,1)S(1)} %arrive.5.refs_0_.refs_2_), channel_id=1, source_target_pairs={{0,2},{2,0},{4,6},{6,4},{1,3},{3,1},{5,7},{7,5},{8,10},{10,8},{12,... | collective-permute-start | bytes 196616 | tf_op jit(solution)/shard_map/ppermute | solution.py:31
  61.0 2.5 %collective-permute-start.26 = (bf16[128,1024]{1,0:T(8,128)(2,1)S(1)}, bf16[128,1024]{1,0:T(8,128)(2,1)S(1)}, u32[]{:S(2)}, u32[]{:S(2)}) collective-permute-start(bf16[128,1024]{1,0:T(8,128)(2,1)S(1)} %product_part.8.refs_0_), channel_id=1, source_target_pairs={{0,1},{1,0},{2,3},{3,2},{4,5},{5,4},{6,7},{7,6},{8,9},{9,8},{10,11... | collective-permute-start | bytes 786440 | tf_op jit(solution)/shard_map/ppermute | solution.py:22
  63.6 1.8 %collective-permute-done.21.refs_2_ = bf16[32,1024]{1,0:T(8,128)(2,1)S(1)} collective-permute-done((bf16[32,1024]{1,0:T(8,128)(2,1)S(1)}, bf16[32,1024]{1,0:T(8,128)(2,1)S(1)}, u32[]{:S(2)}, u32[]{:S(2)}) %collective-permute-start.21) | collective-permute-done | bytes 65568 | tf_op jit(solution)/shard_map/ppermute | solution.py:31
  65.9 1.1 collective-permute-start.24
  67.6 0.6 collective-permute-done.24.refs_3_.refs_1_
  69.7 1.6 %collective-permute-start.28 = (bf16[32,1024]{1,0:T(8,128)(2,1)S(1)}, bf16[32,1024]{1,0:T(8,128)(2,1)S(1)}, u32[]{:S(2)}, u32[]{:S(2)}) collective-permute-start(bf16[32,1024]{1,0:T(8,128)(2,1)S(1)} %get-tuple-element.181), channel_id=1, source_target_pairs={{0,6},{2,4},{4,2},{6,0},{1,7},{3,5},{5,3},{7,1},{8,14},{10,12},{12... | collective-permute-start | bytes 196616 | tf_op jit(solution)/shard_map/ppermute | solution.py:31
  71.3 2.0 %collective-permute-start.30 = (bf16[32,1024]{1,0:T(8,128)(2,1)S(1)}, bf16[32,1024]{1,0:T(8,128)(2,1)S(1)}, u32[]{:S(2)}, u32[]{:S(2)}) collective-permute-start(bf16[32,1024]{1,0:T(8,128)(2,1)S(1)} %get-tuple-element.183), channel_id=1, source_target_pairs={{0,2},{2,0},{4,6},{6,4},{1,3},{3,1},{5,7},{7,5},{8,10},{10,8},{12,... | collective-permute-start | bytes 196616 | tf_op jit(solution)/shard_map/ppermute | solution.py:31
  73.7 1.4 %collective-permute-done.28.refs_1_ = bf16[32,1024]{1,0:T(8,128)(2,1)S(1)} collective-permute-done((bf16[32,1024]{1,0:T(8,128)(2,1)S(1)}, bf16[32,1024]{1,0:T(8,128)(2,1)S(1)}, u32[]{:S(2)}, u32[]{:S(2)}) %collective-permute-start.28) | collective-permute-done | bytes 65568 | tf_op jit(solution)/shard_map/ppermute | solution.py:31
  75.1 3.3 %collective-permute-done.29.refs_2_ = bf16[32,1024]{1,0:T(8,128)(2,1)S(1)} collective-permute-done((bf16[32,1024]{1,0:T(8,128)(2,1)S(1)}, bf16[32,1024]{1,0:T(8,128)(2,1)S(1)}, u32[]{:S(2)}, u32[]{:S(2)}) %collective-permute-start.29) | collective-permute-done | bytes 65568 | tf_op jit(solution)/shard_map/ppermute | solution.py:31
  78.5 2.1 %collective-permute-start.31 = (bf16[32,1024]{1,0:T(8,128)(2,1)S(1)}, bf16[32,1024]{1,0:T(8,128)(2,1)S(1)}, u32[]{:S(2)}, u32[]{:S(2)}) collective-permute-start(bf16[32,1024]{1,0:T(8,128)(2,1)S(1)} %leave_back.2.refs_5_), channel_id=1, source_target_pairs={{8,0},{16,8},{24,16},{9,1},{17,9},{25,17},{10,2},{18,10},{26,18},{... | collective-permute-start | bytes 196616 | tf_op jit(solution)/shard_map/ppermute | solution.py:17
  80.8 0.7 down_again.1
  81.6 1.8 %collective-permute-start.33 = (bf16[32,1024]{1,0:T(8,128)(2,1)S(1)}, bf16[32,1024]{1,0:T(8,128)(2,1)S(1)}, u32[]{:S(2)}, u32[]{:S(2)}) collective-permute-start(bf16[32,1024]{1,0:T(8,128)(2,1)S(1)} %get-tuple-element.203), channel_id=1, source_target_pairs={{0,4},{2,6},{4,0},{6,2},{1,5},{3,7},{5,1},{7,3},{8,12},{10,14},{12... | collective-permute-start | bytes 196616 | tf_op jit(solution)/shard_map/ppermute | solution.py:31
  83.4 1.0 collective-permute-done.31.arrived
  84.4 1.6 %collective-permute-start.34 = (bf16[32,1024]{1,0:T(8,128)(2,1)S(1)}, bf16[32,1024]{1,0:T(8,128)(2,1)S(1)}, u32[]{:S(2)}, u32[]{:S(2)}) collective-permute-start(bf16[32,1024]{1,0:T(8,128)(2,1)S(1)} %arrive.6.refs_2_.first), channel_id=1, source_target_pairs={{0,6},{2,4},{4,2},{6,0},{1,7},{3,5},{5,3},{7,1},{8,14},{10,12},{12... | collective-permute-start | bytes 196616 | tf_op jit(solution)/shard_map/ppermute | solution.py:31
  86.0 2.0 %collective-permute-start.36 = (bf16[32,1024]{1,0:T(8,128)(2,1)S(1)}, bf16[32,1024]{1,0:T(8,128)(2,1)S(1)}, u32[]{:S(2)}, u32[]{:S(2)}) collective-permute-start(bf16[32,1024]{1,0:T(8,128)(2,1)S(1)} %arrive.6.refs_2_.first), channel_id=1, source_target_pairs={{0,2},{2,0},{4,6},{6,4},{1,3},{3,1},{5,7},{7,5},{8,10},{10,8},{12,... | collective-permute-start | bytes 196616 | tf_op jit(solution)/shard_map/ppermute | solution.py:31
  88.0 1.5 %collective-permute-done.34.refs_3_ = bf16[32,1024]{1,0:T(8,128)(2,1)S(1)} collective-permute-done((bf16[32,1024]{1,0:T(8,128)(2,1)S(1)}, bf16[32,1024]{1,0:T(8,128)(2,1)S(1)}, u32[]{:S(2)}, u32[]{:S(2)}) %collective-permute-start.34) | collective-permute-done | bytes 65568 | tf_op jit(solution)/shard_map/ppermute | solution.py:31
  89.5 3.7 %collective-permute-done.35.refs_4_ = bf16[32,1024]{1,0:T(8,128)(2,1)S(1)} collective-permute-done((bf16[32,1024]{1,0:T(8,128)(2,1)S(1)}, bf16[32,1024]{1,0:T(8,128)(2,1)S(1)}, u32[]{:S(2)}, u32[]{:S(2)}) %collective-permute-start.35) | collective-permute-done | bytes 65568 | tf_op jit(solution)/shard_map/ppermute | solution.py:31
  93.7 1.0 collective-permute-start.38
  95.3 0.6 collective-permute-done.38.refs_1_
  97.4 1.8 %collective-permute-start.39 = (bf16[32,1024]{1,0:T(8,128)(2,1)S(1)}, bf16[32,1024]{1,0:T(8,128)(2,1)S(1)}, u32[]{:S(2)}, u32[]{:S(2)}) collective-permute-start(bf16[32,1024]{1,0:T(8,128)(2,1)S(1)} %get-tuple-element.208), channel_id=1, source_target_pairs={{0,6},{2,4},{4,2},{6,0},{1,7},{3,5},{5,3},{7,1},{8,14},{10,12},{12... | collective-permute-start | bytes 196616 | tf_op jit(solution)/shard_map/ppermute | solution.py:31
  99.3 1.8 %collective-permute-start.41 = (bf16[32,1024]{1,0:T(8,128)(2,1)S(1)}, bf16[32,1024]{1,0:T(8,128)(2,1)S(1)}, u32[]{:S(2)}, u32[]{:S(2)}) collective-permute-start(bf16[32,1024]{1,0:T(8,128)(2,1)S(1)} %get-tuple-element.210), channel_id=1, source_target_pairs={{0,2},{2,0},{4,6},{6,4},{1,3},{3,1},{5,7},{7,5},{8,10},{10,8},{12,... | collective-permute-start | bytes 196616 | tf_op jit(solution)/shard_map/ppermute | solution.py:31
  101.4 1.4 %collective-permute-done.39.refs_1_ = bf16[32,1024]{1,0:T(8,128)(2,1)S(1)} collective-permute-done((bf16[32,1024]{1,0:T(8,128)(2,1)S(1)}, bf16[32,1024]{1,0:T(8,128)(2,1)S(1)}, u32[]{:S(2)}, u32[]{:S(2)}) %collective-permute-start.39) | collective-permute-done | bytes 65568 | tf_op jit(solution)/shard_map/ppermute | solution.py:31
  102.8 3.3 %collective-permute-done.40.refs_2_ = bf16[32,1024]{1,0:T(8,128)(2,1)S(1)} collective-permute-done((bf16[32,1024]{1,0:T(8,128)(2,1)S(1)}, bf16[32,1024]{1,0:T(8,128)(2,1)S(1)}, u32[]{:S(2)}, u32[]{:S(2)}) %collective-permute-start.40) | collective-permute-done | bytes 65568 | tf_op jit(solution)/shard_map/ppermute | solution.py:31
  106.2 1.9 %collective-permute-start.43 = (bf16[32,1024]{1,0:T(8,128)(2,1)S(1)}, bf16[32,1024]{1,0:T(8,128)(2,1)S(1)}, u32[]{:S(2)}, u32[]{:S(2)}) collective-permute-start(bf16[32,1024]{1,0:T(8,128)(2,1)S(1)} %leave_back.3.refs_4_), channel_id=1, source_target_pairs={{8,0},{16,8},{24,16},{9,1},{17,9},{25,17},{10,2},{18,10},{26,18},{... | collective-permute-start | bytes 196616 | tf_op jit(solution)/shard_map/ppermute | solution.py:17
  108.1 1.8 %collective-permute-start.42 = (bf16[32,1024]{1,0:T(8,128)(2,1)S(1)}, bf16[32,1024]{1,0:T(8,128)(2,1)S(1)}, u32[]{:S(2)}, u32[]{:S(2)}) collective-permute-start(bf16[32,1024]{1,0:T(8,128)(2,1)S(1)} %get-tuple-element.215), channel_id=1, source_target_pairs={{0,6},{2,4},{4,2},{6,0},{1,7},{3,5},{5,3},{7,1},{8,14},{10,12},{12... | collective-permute-start | bytes 196616 | tf_op jit(solution)/shard_map/ppermute | solution.py:31
  109.9 2.1 %collective-permute-done.43.arrived = bf16[32,1024]{1,0:T(8,128)(2,1)S(1)} collective-permute-done((bf16[32,1024]{1,0:T(8,128)(2,1)S(1)}, bf16[32,1024]{1,0:T(8,128)(2,1)S(1)}, u32[]{:S(2)}, u32[]{:S(2)}) %collective-permute-start.43) | collective-permute-done | bytes 65568 | tf_op jit(solution)/shard_map/ppermute | solution.py:17
  112.1 1.8 %collective-permute-start.44 = (bf16[32,1024]{1,0:T(8,128)(2,1)S(1)}, bf16[32,1024]{1,0:T(8,128)(2,1)S(1)}, u32[]{:S(2)}, u32[]{:S(2)}) collective-permute-start(bf16[32,1024]{1,0:T(8,128)(2,1)S(1)} %arrive.7.refs_0_.first), channel_id=1, source_target_pairs={{0,6},{2,4},{4,2},{6,0},{1,7},{3,5},{5,3},{7,1},{8,14},{10,12},{12... | collective-permute-start | bytes 196616 | tf_op jit(solution)/shard_map/ppermute | solution.py:31
  113.9 1.8 %collective-permute-start.46 = (bf16[32,1024]{1,0:T(8,128)(2,1)S(1)}, bf16[32,1024]{1,0:T(8,128)(2,1)S(1)}, u32[]{:S(2)}, u32[]{:S(2)}) collective-permute-start(bf16[32,1024]{1,0:T(8,128)(2,1)S(1)} %arrive.7.refs_0_.first), channel_id=1, source_target_pairs={{0,2},{2,0},{4,6},{6,4},{1,3},{3,1},{5,7},{7,5},{8,10},{10,8},{12,... | collective-permute-start | bytes 196616 | tf_op jit(solution)/shard_map/ppermute | solution.py:31
  115.7 0.8 finish_forward.1
  116.5 0.7 collective-permute-done.44.refs_1_
  117.2 3.7 %collective-permute-done.45.refs_2_ = bf16[32,1024]{1,0:T(8,128)(2,1)S(1)} collective-permute-done((bf16[32,1024]{1,0:T(8,128)(2,1)S(1)}, bf16[32,1024]{1,0:T(8,128)(2,1)S(1)}, u32[]{:S(2)}, u32[]{:S(2)}) %collective-permute-start.45) | collective-permute-done | bytes 65568 | tf_op jit(solution)/shard_map/ppermute | solution.py:31
  121.4 1.1 collective-permute-start.48
  123.0 2.1 %weight_grads.2.refs_15_ = bf16[2048,1024]{1,0:T(8,128)(2,1)} custom-call(bf16[1024,128]{1,0:T(8,128)(2,1)S(1)} %turned.10.refs_0_, bf16[1024,128]{1,0:T(8,128)(2,1)S(1)} %turned.13.refs_1_, bf16[1024,128]{1,0:T(8,128)(2,1)S(1)} %turned.16.refs_2_, bf16[128,1024]{1,0:T(8,128)(2,1)S(1)} %get-tuple-element.223.whole.refs_3_.refs_12_, ...), custom_call_target="tpu_custom_call" | custom-call | flops 805306368 | bytes 2097152 | tf_op jit(solution)/shard_map/weight_grads/pallas_call | solution.py:368
  126.3 1.5 %collective-permute-start.49 = (bf16[32,1024]{1,0:T(8,128)(2,1)S(1)}, bf16[32,1024]{1,0:T(8,128)(2,1)S(1)}, u32[]{:S(2)}, u32[]{:S(2)}) collective-permute-start(bf16[32,1024]{1,0:T(8,128)(2,1)S(1)} %get-tuple-element.231), channel_id=1, source_target_pairs={{0,6},{2,4},{4,2},{6,0},{1,7},{3,5},{5,3},{7,1},{8,14},{10,12},{12... | collective-permute-start | bytes 196616 | tf_op jit(solution)/shard_map/ppermute | solution.py:31
  127.9 2.1 %collective-permute-start.51 = (bf16[32,1024]{1,0:T(8,128)(2,1)S(1)}, bf16[32,1024]{1,0:T(8,128)(2,1)S(1)}, u32[]{:S(2)}, u32[]{:S(2)}) collective-permute-start(bf16[32,1024]{1,0:T(8,128)(2,1)S(1)} %get-tuple-element.233), channel_id=1, source_target_pairs={{0,2},{2,0},{4,6},{6,4},{1,3},{3,1},{5,7},{7,5},{8,10},{10,8},{12,... | collective-permute-start | bytes 196616 | tf_op jit(solution)/shard_map/ppermute | solution.py:31
  130.0 4.3 %weight_grads.3 = (bf16[1024,2048]{1,0:T(8,128)(2,1)}, bf16[2048,1024]{1,0:T(8,128)(2,1)}) custom-call(bf16[1024,128]{1,0:T(8,128)(2,1)S(1)} %turned.9.refs_0_, bf16[1024,128]{1,0:T(8,128)(2,1)S(1)} %turned.12.refs_1_, bf16[1024,128]{1,0:T(8,128)(2,1)S(1)} %turned.15.refs_2_, ...), custom_call_target="tpu_custom_call", output_to_operand_aliasing={{1}: (15, {})} | custom-call | flops 2415919104 | bytes 6291456 | tf_op jit(solution)/shard_map/weight_grads/pallas_call | solution.py:368
  134.3 0.7 collective-permute-done.50.refs_2_
  135.0 0.7 finish.1
  (92 shorter events, 15.3 us)
Async XLA Ops:
  1.5 7.3 %collective-permute-start = (bf16[32,1024]{1,0:T(8,128)(2,1)S(1)}, bf16[32,1024]{1,0:T(8,128)(2,1)S(1)}, u32[]{:S(2)}, u32[]{:S(2)}) collective-permute-start(bf16[32,1024]{1,0:T(8,128)(2,1)S(1)} %get-tuple-element.131.refs_0_.first), channel_id=1, source_target_pairs={{0,6},{2,4},{4,2},{6,0},{1,7},{3,5},{5,3},{7,1},{8,14},{10,12},{12... | collective-permute-start | bytes 196616 | tf_op jit(solution)/shard_map/ppermute | solution.py:31
  4.9 5.9 %collective-permute-start.1 = (bf16[32,1024]{1,0:T(8,128)(2,1)S(1)}, bf16[32,1024]{1,0:T(8,128)(2,1)S(1)}, u32[]{:S(2)}, u32[]{:S(2)}) collective-permute-start(bf16[32,1024]{1,0:T(8,128)(2,1)S(1)} %get-tuple-element.131.refs_0_.first), channel_id=1, source_target_pairs={{0,4},{2,6},{4,0},{6,2},{1,5},{3,7},{5,1},{7,3},{8,12},{10,14},{12... | collective-permute-start | bytes 196616 | tf_op jit(solution)/shard_map/ppermute | solution.py:31
  4.9 5.9 %collective-permute-start.2 = (bf16[32,1024]{1,0:T(8,128)(2,1)S(1)}, bf16[32,1024]{1,0:T(8,128)(2,1)S(1)}, u32[]{:S(2)}, u32[]{:S(2)}) collective-permute-start(bf16[32,1024]{1,0:T(8,128)(2,1)S(1)} %get-tuple-element.131.refs_0_.first), channel_id=1, source_target_pairs={{0,2},{2,0},{4,6},{6,4},{1,3},{3,1},{5,7},{7,5},{8,10},{10,8},{12,... | collective-permute-start | bytes 196616 | tf_op jit(solution)/shard_map/ppermute | solution.py:31
  11.3 1.9 %collective-permute-start.4 = (bf16[128,1024]{1,0:T(8,128)(2,1)S(1)}, bf16[128,1024]{1,0:T(8,128)(2,1)S(1)}, u32[]{:S(2)}, u32[]{:S(2)}) collective-permute-start(bf16[128,1024]{1,0:T(8,128)(2,1)S(1)} %get-tuple-element.227.refs_0_.refs_2_), channel_id=1, source_target_pairs={{0,1},{1,0},{2,3},{3,2},{4,5},{5,4},{6,7},{7,6},{8,9},{9,8},{10,11... | collective-permute-start | bytes 786440 | tf_op jit(solution)/shard_map/ppermute | solution.py:22
  12.5 1.6 %collective-permute-start.3 = (bf16[128,1024]{1,0:T(8,128)(2,1)S(1)}, bf16[128,1024]{1,0:T(8,128)(2,1)S(1)}, u32[]{:S(2)}, u32[]{:S(2)}) collective-permute-start(bf16[128,1024]{1,0:T(8,128)(2,1)S(1)} %product_part.6.refs_0_.refs_2_), channel_id=1, source_target_pairs={{0,1},{1,0},{2,3},{3,2},{4,5},{5,4},{6,7},{7,6},{8,9},{9,8},{10,11... | collective-permute-start | bytes 786440 | tf_op jit(solution)/shard_map/ppermute | solution.py:22
  14.5 6.6 %collective-permute-start.5 = (bf16[32,1024]{1,0:T(8,128)(2,1)S(1)}, bf16[32,1024]{1,0:T(8,128)(2,1)S(1)}, u32[]{:S(2)}, u32[]{:S(2)}) collective-permute-start(bf16[32,1024]{1,0:T(8,128)(2,1)S(1)} %get-tuple-element.140), channel_id=1, source_target_pairs={{0,6},{2,4},{4,2},{6,0},{1,7},{3,5},{5,3},{7,1},{8,14},{10,12},{12... | collective-permute-start | bytes 196616 | tf_op jit(solution)/shard_map/ppermute | solution.py:31
  17.0 6.4 %collective-permute-start.6 = (bf16[32,1024]{1,0:T(8,128)(2,1)S(1)}, bf16[32,1024]{1,0:T(8,128)(2,1)S(1)}, u32[]{:S(2)}, u32[]{:S(2)}) collective-permute-start(bf16[32,1024]{1,0:T(8,128)(2,1)S(1)} %get-tuple-element.141), channel_id=1, source_target_pairs={{0,4},{2,6},{4,0},{6,2},{1,5},{3,7},{5,1},{7,3},{8,12},{10,14},{12... | collective-permute-start | bytes 196616 | tf_op jit(solution)/shard_map/ppermute | solution.py:31
  17.0 6.4 %collective-permute-start.7 = (bf16[32,1024]{1,0:T(8,128)(2,1)S(1)}, bf16[32,1024]{1,0:T(8,128)(2,1)S(1)}, u32[]{:S(2)}, u32[]{:S(2)}) collective-permute-start(bf16[32,1024]{1,0:T(8,128)(2,1)S(1)} %get-tuple-element.142), channel_id=1, source_target_pairs={{0,2},{2,0},{4,6},{6,4},{1,3},{3,1},{5,7},{7,5},{8,10},{10,8},{12,... | collective-permute-start | bytes 196616 | tf_op jit(solution)/shard_map/ppermute | solution.py:31
  18.1 1.2 copy-start
  23.5 5.6 %collective-permute-start.8 = (bf16[32,1024]{1,0:T(8,128)(2,1)S(1)}, bf16[32,1024]{1,0:T(8,128)(2,1)S(1)}, u32[]{:S(2)}, u32[]{:S(2)}) collective-permute-start(bf16[32,1024]{1,0:T(8,128)(2,1)S(1)} %get-tuple-element.149), channel_id=1, source_target_pairs={{0,8},{8,16},{16,24},{1,9},{9,17},{17,25},{2,10},{10,18},{18,26},{... | collective-permute-start | bytes 196616 | tf_op jit(solution)/shard_map/ppermute | solution.py:17
  26.6 6.1 %collective-permute-start.9 = (bf16[32,1024]{1,0:T(8,128)(2,1)S(1)}, bf16[32,1024]{1,0:T(8,128)(2,1)S(1)}, u32[]{:S(2)}, u32[]{:S(2)}) collective-permute-start(bf16[32,1024]{1,0:T(8,128)(2,1)S(1)} %get-tuple-element.170.refs_0_.first), channel_id=1, source_target_pairs={{0,2},{2,0},{4,6},{6,4},{1,3},{3,1},{5,7},{7,5},{8,10},{10,8},{12,... | collective-permute-start | bytes 196616 | tf_op jit(solution)/shard_map/ppermute | solution.py:31
  26.7 6.0 %collective-permute-start.10 = (bf16[32,1024]{1,0:T(8,128)(2,1)S(1)}, bf16[32,1024]{1,0:T(8,128)(2,1)S(1)}, u32[]{:S(2)}, u32[]{:S(2)}) collective-permute-start(bf16[32,1024]{1,0:T(8,128)(2,1)S(1)} %get-tuple-element.170.refs_0_.first), channel_id=1, source_target_pairs={{0,4},{2,6},{4,0},{6,2},{1,5},{3,7},{5,1},{7,3},{8,12},{10,14},{12... | collective-permute-start | bytes 196616 | tf_op jit(solution)/shard_map/ppermute | solution.py:31
  29.1 5.0 %collective-permute-start.11 = (bf16[32,1024]{1,0:T(8,128)(2,1)S(1)}, bf16[32,1024]{1,0:T(8,128)(2,1)S(1)}, u32[]{:S(2)}, u32[]{:S(2)}) collective-permute-start(bf16[32,1024]{1,0:T(8,128)(2,1)S(1)} %arrive.4.refs_2_.first.refs_1_), channel_id=1, source_target_pairs={{0,6},{2,4},{4,2},{6,0},{1,7},{3,5},{5,3},{7,1},{8,14},{10,12},{12... | collective-permute-start | bytes 196616 | tf_op jit(solution)/shard_map/ppermute | solution.py:31
  30.7 7.2 %collective-permute-start.12 = (bf16[32,1024]{1,0:T(8,128)(2,1)S(1)}, bf16[32,1024]{1,0:T(8,128)(2,1)S(1)}, u32[]{:S(2)}, u32[]{:S(2)}) collective-permute-start(bf16[32,1024]{1,0:T(8,128)(2,1)S(1)} %arrive.4.refs_2_.first.refs_1_), channel_id=1, source_target_pairs={{0,4},{2,6},{4,0},{6,2},{1,5},{3,7},{5,1},{7,3},{8,12},{10,14},{12... | collective-permute-start | bytes 196616 | tf_op jit(solution)/shard_map/ppermute | solution.py:31
  30.7 7.2 %collective-permute-start.13 = (bf16[32,1024]{1,0:T(8,128)(2,1)S(1)}, bf16[32,1024]{1,0:T(8,128)(2,1)S(1)}, u32[]{:S(2)}, u32[]{:S(2)}) collective-permute-start(bf16[32,1024]{1,0:T(8,128)(2,1)S(1)} %arrive.4.refs_2_.first.refs_1_), channel_id=1, source_target_pairs={{0,2},{2,0},{4,6},{6,4},{1,3},{3,1},{5,7},{7,5},{8,10},{10,8},{12,... | collective-permute-start | bytes 196616 | tf_op jit(solution)/shard_map/ppermute | solution.py:31
  38.3 3.0 %collective-permute-start.15 = (bf16[128,1024]{1,0:T(8,128)(2,1)S(1)}, bf16[128,1024]{1,0:T(8,128)(2,1)S(1)}, u32[]{:S(2)}, u32[]{:S(2)}) collective-permute-start(bf16[128,1024]{1,0:T(8,128)(2,1)S(1)} %get-tuple-element.154.refs_0_.refs_2_), channel_id=1, source_target_pairs={{0,1},{1,0},{2,3},{3,2},{4,5},{5,4},{6,7},{7,6},{8,9},{9,8},{10,11... | collective-permute-start | bytes 786440 | tf_op jit(solution)/shard_map/ppermute | solution.py:22
  40.6 1.6 %collective-permute-start.14 = (bf16[128,1024]{1,0:T(8,128)(2,1)S(1)}, bf16[128,1024]{1,0:T(8,128)(2,1)S(1)}, u32[]{:S(2)}, u32[]{:S(2)}) collective-permute-start(bf16[128,1024]{1,0:T(8,128)(2,1)S(1)} %product_part.7.refs_0_.refs_2_), channel_id=1, source_target_pairs={{0,1},{1,0},{2,3},{3,2},{4,5},{5,4},{6,7},{7,6},{8,9},{9,8},{10,11... | collective-permute-start | bytes 786440 | tf_op jit(solution)/shard_map/ppermute | solution.py:22
  42.7 5.4 %collective-permute-start.16 = (bf16[32,1024]{1,0:T(8,128)(2,1)S(1)}, bf16[32,1024]{1,0:T(8,128)(2,1)S(1)}, u32[]{:S(2)}, u32[]{:S(2)}) collective-permute-start(bf16[32,1024]{1,0:T(8,128)(2,1)S(1)} %get-tuple-element.157), channel_id=1, source_target_pairs={{0,6},{2,4},{4,2},{6,0},{1,7},{3,5},{5,3},{7,1},{8,14},{10,12},{12... | collective-permute-start | bytes 196616 | tf_op jit(solution)/shard_map/ppermute | solution.py:31
  44.4 7.0 %collective-permute-start.17 = (bf16[32,1024]{1,0:T(8,128)(2,1)S(1)}, bf16[32,1024]{1,0:T(8,128)(2,1)S(1)}, u32[]{:S(2)}, u32[]{:S(2)}) collective-permute-start(bf16[32,1024]{1,0:T(8,128)(2,1)S(1)} %get-tuple-element.158), channel_id=1, source_target_pairs={{0,4},{2,6},{4,0},{6,2},{1,5},{3,7},{5,1},{7,3},{8,12},{10,14},{12... | collective-permute-start | bytes 196616 | tf_op jit(solution)/shard_map/ppermute | solution.py:31
  44.4 7.0 %collective-permute-start.18 = (bf16[32,1024]{1,0:T(8,128)(2,1)S(1)}, bf16[32,1024]{1,0:T(8,128)(2,1)S(1)}, u32[]{:S(2)}, u32[]{:S(2)}) collective-permute-start(bf16[32,1024]{1,0:T(8,128)(2,1)S(1)} %get-tuple-element.159), channel_id=1, source_target_pairs={{0,2},{2,0},{4,6},{6,4},{1,3},{3,1},{5,7},{7,5},{8,10},{10,8},{12,... | collective-permute-start | bytes 196616 | tf_op jit(solution)/shard_map/ppermute | solution.py:31
  51.5 5.0 %collective-permute-start.19 = (bf16[32,1024]{1,0:T(8,128)(2,1)S(1)}, bf16[32,1024]{1,0:T(8,128)(2,1)S(1)}, u32[]{:S(2)}, u32[]{:S(2)}) collective-permute-start(bf16[32,1024]{1,0:T(8,128)(2,1)S(1)} %get-tuple-element.167), channel_id=1, source_target_pairs={{0,8},{8,16},{16,24},{1,9},{9,17},{17,25},{2,10},{10,18},{18,26},{... | collective-permute-start | bytes 196616 | tf_op jit(solution)/shard_map/ppermute | solution.py:17
  54.7 5.4 %collective-permute-start.23 = (bf16[32,1024]{1,0:T(8,128)(2,1)S(1)}, bf16[32,1024]{1,0:T(8,128)(2,1)S(1)}, u32[]{:S(2)}, u32[]{:S(2)}) collective-permute-start(bf16[32,1024]{1,0:T(8,128)(2,1)S(1)} %get-tuple-element.170.refs_0_.first), channel_id=1, source_target_pairs={{0,6},{2,4},{4,2},{6,0},{1,7},{3,5},{5,3},{7,1},{8,14},{10,12},{12... | collective-permute-start | bytes 196616 | tf_op jit(solution)/shard_map/ppermute | solution.py:31
  56.5 7.1 %collective-permute-start.20 = (bf16[32,1024]{1,0:T(8,128)(2,1)S(1)}, bf16[32,1024]{1,0:T(8,128)(2,1)S(1)}, u32[]{:S(2)}, u32[]{:S(2)}) collective-permute-start(bf16[32,1024]{1,0:T(8,128)(2,1)S(1)} %arrive.5.refs_0_.refs_2_), channel_id=1, source_target_pairs={{0,6},{2,4},{4,2},{6,0},{1,7},{3,5},{5,3},{7,1},{8,14},{10,12},{12... | collective-permute-start | bytes 196616 | tf_op jit(solution)/shard_map/ppermute | solution.py:31
  58.2 7.3 %collective-permute-start.21 = (bf16[32,1024]{1,0:T(8,128)(2,1)S(1)}, bf16[32,1024]{1,0:T(8,128)(2,1)S(1)}, u32[]{:S(2)}, u32[]{:S(2)}) collective-permute-start(bf16[32,1024]{1,0:T(8,128)(2,1)S(1)} %arrive.5.refs_0_.refs_2_), channel_id=1, source_target_pairs={{0,4},{2,6},{4,0},{6,2},{1,5},{3,7},{5,1},{7,3},{8,12},{10,14},{12... | collective-permute-start | bytes 196616 | tf_op jit(solution)/shard_map/ppermute | solution.py:31
  58.2 7.3 %collective-permute-start.22 = (bf16[32,1024]{1,0:T(8,128)(2,1)S(1)}, bf16[32,1024]{1,0:T(8,128)(2,1)S(1)}, u32[]{:S(2)}, u32[]{:S(2)}) collective-permute-start(bf16[32,1024]{1,0:T(8,128)(2,1)S(1)} %arrive.5.refs_0_.refs_2_), channel_id=1, source_target_pairs={{0,2},{2,0},{4,6},{6,4},{1,3},{3,1},{5,7},{7,5},{8,10},{10,8},{12,... | collective-permute-start | bytes 196616 | tf_op jit(solution)/shard_map/ppermute | solution.py:31
  61.0 7.8 %collective-permute-start.26 = (bf16[128,1024]{1,0:T(8,128)(2,1)S(1)}, bf16[128,1024]{1,0:T(8,128)(2,1)S(1)}, u32[]{:S(2)}, u32[]{:S(2)}) collective-permute-start(bf16[128,1024]{1,0:T(8,128)(2,1)S(1)} %product_part.8.refs_0_), channel_id=1, source_target_pairs={{0,1},{1,0},{2,3},{3,2},{4,5},{5,4},{6,7},{7,6},{8,9},{9,8},{10,11... | collective-permute-start | bytes 786440 | tf_op jit(solution)/shard_map/ppermute | solution.py:22
  63.6 4.0 %collective-permute-start.27 = (bf16[128,1024]{1,0:T(8,128)(2,1)S(1)}, bf16[128,1024]{1,0:T(8,128)(2,1)S(1)}, u32[]{:S(2)}, u32[]{:S(2)}) collective-permute-start(bf16[128,1024]{1,0:T(8,128)(2,1)S(1)} %get-tuple-element.171.refs_0_), channel_id=1, source_target_pairs={{0,1},{1,0},{2,3},{3,2},{4,5},{5,4},{6,7},{7,6},{8,9},{9,8},{10,11... | collective-permute-start | bytes 786440 | tf_op jit(solution)/shard_map/ppermute | solution.py:22
  65.9 2.3 %collective-permute-start.24 = (bf16[128,1024]{1,0:T(8,128)(2,1)S(1)}, bf16[128,1024]{1,0:T(8,128)(2,1)S(1)}, u32[]{:S(2)}, u32[]{:S(2)}) collective-permute-start(bf16[128,1024]{1,0:T(8,128)(2,1)S(1)} %get-tuple-element.190.refs_2_.refs_0_), channel_id=1, source_target_pairs={{0,1},{1,0},{2,3},{3,2},{4,5},{5,4},{6,7},{7,6},{8,9},{9,8},{10,11... | collective-permute-start | bytes 786440 | tf_op jit(solution)/shard_map/ppermute | solution.py:22
  67.5 1.6 %collective-permute-start.25 = (bf16[128,1024]{1,0:T(8,128)(2,1)S(1)}, bf16[128,1024]{1,0:T(8,128)(2,1)S(1)}, u32[]{:S(2)}, u32[]{:S(2)}) collective-permute-start(bf16[128,1024]{1,0:T(8,128)(2,1)S(1)} %product_part.9.refs_2_), channel_id=1, source_target_pairs={{0,1},{1,0},{2,3},{3,2},{4,5},{5,4},{6,7},{7,6},{8,9},{9,8},{10,11... | collective-permute-start | bytes 786440 | tf_op jit(solution)/shard_map/ppermute | solution.py:22
  69.7 5.4 %collective-permute-start.28 = (bf16[32,1024]{1,0:T(8,128)(2,1)S(1)}, bf16[32,1024]{1,0:T(8,128)(2,1)S(1)}, u32[]{:S(2)}, u32[]{:S(2)}) collective-permute-start(bf16[32,1024]{1,0:T(8,128)(2,1)S(1)} %get-tuple-element.181), channel_id=1, source_target_pairs={{0,6},{2,4},{4,2},{6,0},{1,7},{3,5},{5,3},{7,1},{8,14},{10,12},{12... | collective-permute-start | bytes 196616 | tf_op jit(solution)/shard_map/ppermute | solution.py:31
  71.3 7.1 %collective-permute-start.29 = (bf16[32,1024]{1,0:T(8,128)(2,1)S(1)}, bf16[32,1024]{1,0:T(8,128)(2,1)S(1)}, u32[]{:S(2)}, u32[]{:S(2)}) collective-permute-start(bf16[32,1024]{1,0:T(8,128)(2,1)S(1)} %get-tuple-element.182), channel_id=1, source_target_pairs={{0,4},{2,6},{4,0},{6,2},{1,5},{3,7},{5,1},{7,3},{8,12},{10,14},{12... | collective-permute-start | bytes 196616 | tf_op jit(solution)/shard_map/ppermute | solution.py:31
  71.3 7.1 %collective-permute-start.30 = (bf16[32,1024]{1,0:T(8,128)(2,1)S(1)}, bf16[32,1024]{1,0:T(8,128)(2,1)S(1)}, u32[]{:S(2)}, u32[]{:S(2)}) collective-permute-start(bf16[32,1024]{1,0:T(8,128)(2,1)S(1)} %get-tuple-element.183), channel_id=1, source_target_pairs={{0,2},{2,0},{4,6},{6,4},{1,3},{3,1},{5,7},{7,5},{8,10},{10,8},{12,... | collective-permute-start | bytes 196616 | tf_op jit(solution)/shard_map/ppermute | solution.py:31
  78.5 5.9 %collective-permute-start.31 = (bf16[32,1024]{1,0:T(8,128)(2,1)S(1)}, bf16[32,1024]{1,0:T(8,128)(2,1)S(1)}, u32[]{:S(2)}, u32[]{:S(2)}) collective-permute-start(bf16[32,1024]{1,0:T(8,128)(2,1)S(1)} %leave_back.2.refs_5_), channel_id=1, source_target_pairs={{8,0},{16,8},{24,16},{9,1},{17,9},{25,17},{10,2},{18,10},{26,18},{... | collective-permute-start | bytes 196616 | tf_op jit(solution)/shard_map/ppermute | solution.py:17
  81.5 6.5 %collective-permute-start.32 = (bf16[32,1024]{1,0:T(8,128)(2,1)S(1)}, bf16[32,1024]{1,0:T(8,128)(2,1)S(1)}, u32[]{:S(2)}, u32[]{:S(2)}) collective-permute-start(bf16[32,1024]{1,0:T(8,128)(2,1)S(1)} %get-tuple-element.202), channel_id=1, source_target_pairs={{0,2},{2,0},{4,6},{6,4},{1,3},{3,1},{5,7},{7,5},{8,10},{10,8},{12,... | collective-permute-start | bytes 196616 | tf_op jit(solution)/shard_map/ppermute | solution.py:31
  81.6 6.4 %collective-permute-start.33 = (bf16[32,1024]{1,0:T(8,128)(2,1)S(1)}, bf16[32,1024]{1,0:T(8,128)(2,1)S(1)}, u32[]{:S(2)}, u32[]{:S(2)}) collective-permute-start(bf16[32,1024]{1,0:T(8,128)(2,1)S(1)} %get-tuple-element.203), channel_id=1, source_target_pairs={{0,4},{2,6},{4,0},{6,2},{1,5},{3,7},{5,1},{7,3},{8,12},{10,14},{12... | collective-permute-start | bytes 196616 | tf_op jit(solution)/shard_map/ppermute | solution.py:31
  84.4 5.1 %collective-permute-start.34 = (bf16[32,1024]{1,0:T(8,128)(2,1)S(1)}, bf16[32,1024]{1,0:T(8,128)(2,1)S(1)}, u32[]{:S(2)}, u32[]{:S(2)}) collective-permute-start(bf16[32,1024]{1,0:T(8,128)(2,1)S(1)} %arrive.6.refs_2_.first), channel_id=1, source_target_pairs={{0,6},{2,4},{4,2},{6,0},{1,7},{3,5},{5,3},{7,1},{8,14},{10,12},{12... | collective-permute-start | bytes 196616 | tf_op jit(solution)/shard_map/ppermute | solution.py:31
  86.0 7.3 %collective-permute-start.35 = (bf16[32,1024]{1,0:T(8,128)(2,1)S(1)}, bf16[32,1024]{1,0:T(8,128)(2,1)S(1)}, u32[]{:S(2)}, u32[]{:S(2)}) collective-permute-start(bf16[32,1024]{1,0:T(8,128)(2,1)S(1)} %arrive.6.refs_2_.first), channel_id=1, source_target_pairs={{0,4},{2,6},{4,0},{6,2},{1,5},{3,7},{5,1},{7,3},{8,12},{10,14},{12... | collective-permute-start | bytes 196616 | tf_op jit(solution)/shard_map/ppermute | solution.py:31
  86.0 7.3 %collective-permute-start.36 = (bf16[32,1024]{1,0:T(8,128)(2,1)S(1)}, bf16[32,1024]{1,0:T(8,128)(2,1)S(1)}, u32[]{:S(2)}, u32[]{:S(2)}) collective-permute-start(bf16[32,1024]{1,0:T(8,128)(2,1)S(1)} %arrive.6.refs_2_.first), channel_id=1, source_target_pairs={{0,2},{2,0},{4,6},{6,4},{1,3},{3,1},{5,7},{7,5},{8,10},{10,8},{12,... | collective-permute-start | bytes 196616 | tf_op jit(solution)/shard_map/ppermute | solution.py:31
  93.7 2.2 %collective-permute-start.38 = (bf16[128,1024]{1,0:T(8,128)(2,1)S(1)}, bf16[128,1024]{1,0:T(8,128)(2,1)S(1)}, u32[]{:S(2)}, u32[]{:S(2)}) collective-permute-start(bf16[128,1024]{1,0:T(8,128)(2,1)S(1)} %get-tuple-element.205.refs_0_), channel_id=1, source_target_pairs={{0,1},{1,0},{2,3},{3,2},{4,5},{5,4},{6,7},{7,6},{8,9},{9,8},{10,11... | collective-permute-start | bytes 786440 | tf_op jit(solution)/shard_map/ppermute | solution.py:22
  95.2 1.6 %collective-permute-start.37 = (bf16[128,1024]{1,0:T(8,128)(2,1)S(1)}, bf16[128,1024]{1,0:T(8,128)(2,1)S(1)}, u32[]{:S(2)}, u32[]{:S(2)}) collective-permute-start(bf16[128,1024]{1,0:T(8,128)(2,1)S(1)} %product_part.10.refs_0_), channel_id=1, source_target_pairs={{0,1},{1,0},{2,3},{3,2},{4,5},{5,4},{6,7},{7,6},{8,9},{9,8},{10,11... | collective-permute-start | bytes 786440 | tf_op jit(solution)/shard_map/ppermute | solution.py:22
  97.4 5.4 %collective-permute-start.39 = (bf16[32,1024]{1,0:T(8,128)(2,1)S(1)}, bf16[32,1024]{1,0:T(8,128)(2,1)S(1)}, u32[]{:S(2)}, u32[]{:S(2)}) collective-permute-start(bf16[32,1024]{1,0:T(8,128)(2,1)S(1)} %get-tuple-element.208), channel_id=1, source_target_pairs={{0,6},{2,4},{4,2},{6,0},{1,7},{3,5},{5,3},{7,1},{8,14},{10,12},{12... | collective-permute-start | bytes 196616 | tf_op jit(solution)/shard_map/ppermute | solution.py:31
  99.3 6.9 %collective-permute-start.40 = (bf16[32,1024]{1,0:T(8,128)(2,1)S(1)}, bf16[32,1024]{1,0:T(8,128)(2,1)S(1)}, u32[]{:S(2)}, u32[]{:S(2)}) collective-permute-start(bf16[32,1024]{1,0:T(8,128)(2,1)S(1)} %get-tuple-element.209), channel_id=1, source_target_pairs={{0,4},{2,6},{4,0},{6,2},{1,5},{3,7},{5,1},{7,3},{8,12},{10,14},{12... | collective-permute-start | bytes 196616 | tf_op jit(solution)/shard_map/ppermute | solution.py:31
  99.3 6.9 %collective-permute-start.41 = (bf16[32,1024]{1,0:T(8,128)(2,1)S(1)}, bf16[32,1024]{1,0:T(8,128)(2,1)S(1)}, u32[]{:S(2)}, u32[]{:S(2)}) collective-permute-start(bf16[32,1024]{1,0:T(8,128)(2,1)S(1)} %get-tuple-element.210), channel_id=1, source_target_pairs={{0,2},{2,0},{4,6},{6,4},{1,3},{3,1},{5,7},{7,5},{8,10},{10,8},{12,... | collective-permute-start | bytes 196616 | tf_op jit(solution)/shard_map/ppermute | solution.py:31
  106.2 5.9 %collective-permute-start.43 = (bf16[32,1024]{1,0:T(8,128)(2,1)S(1)}, bf16[32,1024]{1,0:T(8,128)(2,1)S(1)}, u32[]{:S(2)}, u32[]{:S(2)}) collective-permute-start(bf16[32,1024]{1,0:T(8,128)(2,1)S(1)} %leave_back.3.refs_4_), channel_id=1, source_target_pairs={{8,0},{16,8},{24,16},{9,1},{17,9},{25,17},{10,2},{18,10},{26,18},{... | collective-permute-start | bytes 196616 | tf_op jit(solution)/shard_map/ppermute | solution.py:17
  108.1 7.6 %collective-permute-start.42 = (bf16[32,1024]{1,0:T(8,128)(2,1)S(1)}, bf16[32,1024]{1,0:T(8,128)(2,1)S(1)}, u32[]{:S(2)}, u32[]{:S(2)}) collective-permute-start(bf16[32,1024]{1,0:T(8,128)(2,1)S(1)} %get-tuple-element.215), channel_id=1, source_target_pairs={{0,6},{2,4},{4,2},{6,0},{1,7},{3,5},{5,3},{7,1},{8,14},{10,12},{12... | collective-permute-start | bytes 196616 | tf_op jit(solution)/shard_map/ppermute | solution.py:31
  112.1 5.1 %collective-permute-start.44 = (bf16[32,1024]{1,0:T(8,128)(2,1)S(1)}, bf16[32,1024]{1,0:T(8,128)(2,1)S(1)}, u32[]{:S(2)}, u32[]{:S(2)}) collective-permute-start(bf16[32,1024]{1,0:T(8,128)(2,1)S(1)} %arrive.7.refs_0_.first), channel_id=1, source_target_pairs={{0,6},{2,4},{4,2},{6,0},{1,7},{3,5},{5,3},{7,1},{8,14},{10,12},{12... | collective-permute-start | bytes 196616 | tf_op jit(solution)/shard_map/ppermute | solution.py:31
  113.9 7.0 %collective-permute-start.45 = (bf16[32,1024]{1,0:T(8,128)(2,1)S(1)}, bf16[32,1024]{1,0:T(8,128)(2,1)S(1)}, u32[]{:S(2)}, u32[]{:S(2)}) collective-permute-start(bf16[32,1024]{1,0:T(8,128)(2,1)S(1)} %arrive.7.refs_0_.first), channel_id=1, source_target_pairs={{0,4},{2,6},{4,0},{6,2},{1,5},{3,7},{5,1},{7,3},{8,12},{10,14},{12... | collective-permute-start | bytes 196616 | tf_op jit(solution)/shard_map/ppermute | solution.py:31
  113.9 7.0 %collective-permute-start.46 = (bf16[32,1024]{1,0:T(8,128)(2,1)S(1)}, bf16[32,1024]{1,0:T(8,128)(2,1)S(1)}, u32[]{:S(2)}, u32[]{:S(2)}) collective-permute-start(bf16[32,1024]{1,0:T(8,128)(2,1)S(1)} %arrive.7.refs_0_.first), channel_id=1, source_target_pairs={{0,2},{2,0},{4,6},{6,4},{1,3},{3,1},{5,7},{7,5},{8,10},{10,8},{12,... | collective-permute-start | bytes 196616 | tf_op jit(solution)/shard_map/ppermute | solution.py:31
  121.4 3.7 %collective-permute-start.48 = (bf16[128,1024]{1,0:T(8,128)(2,1)S(1)}, bf16[128,1024]{1,0:T(8,128)(2,1)S(1)}, u32[]{:S(2)}, u32[]{:S(2)}) collective-permute-start(bf16[128,1024]{1,0:T(8,128)(2,1)S(1)} %get-tuple-element.225.refs_0_), channel_id=1, source_target_pairs={{0,1},{1,0},{2,3},{3,2},{4,5},{5,4},{6,7},{7,6},{8,9},{9,8},{10,11... | collective-permute-start | bytes 786440 | tf_op jit(solution)/shard_map/ppermute | solution.py:22
  123.0 2.8 %collective-permute-start.47 = (bf16[128,1024]{1,0:T(8,128)(2,1)S(1)}, bf16[128,1024]{1,0:T(8,128)(2,1)S(1)}, u32[]{:S(2)}, u32[]{:S(2)}) collective-permute-start(bf16[128,1024]{1,0:T(8,128)(2,1)S(1)} %product_part.11.refs_0_), channel_id=1, source_target_pairs={{0,1},{1,0},{2,3},{3,2},{4,5},{5,4},{6,7},{7,6},{8,9},{9,8},{10,11... | collective-permute-start | bytes 786440 | tf_op jit(solution)/shard_map/ppermute | solution.py:22
  126.3 7.9 %collective-permute-start.49 = (bf16[32,1024]{1,0:T(8,128)(2,1)S(1)}, bf16[32,1024]{1,0:T(8,128)(2,1)S(1)}, u32[]{:S(2)}, u32[]{:S(2)}) collective-permute-start(bf16[32,1024]{1,0:T(8,128)(2,1)S(1)} %get-tuple-element.231), channel_id=1, source_target_pairs={{0,6},{2,4},{4,2},{6,0},{1,7},{3,5},{5,3},{7,1},{8,14},{10,12},{12... | collective-permute-start | bytes 196616 | tf_op jit(solution)/shard_map/ppermute | solution.py:31
  127.9 7.1 %collective-permute-start.50 = (bf16[32,1024]{1,0:T(8,128)(2,1)S(1)}, bf16[32,1024]{1,0:T(8,128)(2,1)S(1)}, u32[]{:S(2)}, u32[]{:S(2)}) collective-permute-start(bf16[32,1024]{1,0:T(8,128)(2,1)S(1)} %get-tuple-element.232), channel_id=1, source_target_pairs={{0,4},{2,6},{4,0},{6,2},{1,5},{3,7},{5,1},{7,3},{8,12},{10,14},{12... | collective-permute-start | bytes 196616 | tf_op jit(solution)/shard_map/ppermute | solution.py:31
  127.9 7.1 %collective-permute-start.51 = (bf16[32,1024]{1,0:T(8,128)(2,1)S(1)}, bf16[32,1024]{1,0:T(8,128)(2,1)S(1)}, u32[]{:S(2)}, u32[]{:S(2)}) collective-permute-start(bf16[32,1024]{1,0:T(8,128)(2,1)S(1)} %get-tuple-element.233), channel_id=1, source_target_pairs={{0,2},{2,0},{4,6},{6,4},{1,3},{3,1},{5,7},{7,5},{8,10},{10,8},{12,... | collective-permute-start | bytes 196616 | tf_op jit(solution)/shard_map/ppermute | solution.py:31

commit v12 on v11

--- a/solution.py
+++ b/solution.py
@@ -23,7 +23,7 @@
 
 
 def partner(row, j, size):
-    return row ^ ((size - j) % size) if size & (size - 1) == 0 else (j - row) % size
+    return row ^ j if size & (size - 1) == 0 else (j - row) % size
 
 
 def swap_rows(block, j):
@@ -41,7 +41,11 @@
 
 def beside(turn):
     size = lax.axis_size("row")
-    return [[size - 1, size - 2], list(range(1, size - 2))][turn] if size > 2 else [[], [1]][turn]
+    return [list(range(1, size - 1)), [size - 1]][turn] if size > 2 else [[], [1]][turn]
+
+
+def halves(pieces):
+    return pieces[: len(pieces) // 2], pieces[len(pieces) // 2 :]
 
 
 def after(block, other):
@@ -228,31 +232,21 @@
     return [slice(n, n + step) for n in range(0, width, step)]
 
 
-def product_part(part, whole, weight, product):
-    for n in columns(product.shape[1]):
-        product[:, n] = matmul(whole[...], weight[:, n.start + part.start : n.stop + part.start]).astype(BF)
-
-
-def stack_product(part, skip, *refs):
+def stack_product(skip, *refs):
     *pieces, weight, whole, product = refs[skip:]
     whole[...] = jnp.concatenate([piece[...] for piece in pieces], axis=0)
-    product_part(part, whole, weight, product)
-
-
-def products(parts, pieces, weight, waited=()):
-    tokens, width = len(pieces) * pieces[0].shape[0], weight.shape[0]
-    whole_like = jax.ShapeDtypeStruct((tokens, width), BF)
-    likes = [jax.ShapeDtypeStruct((tokens, part.stop - part.start), BF) for part in parts]
-    flops = 2 * tokens * width * likes[0].shape[1]
-    whole, first = run(
-        functools.partial(stack_product, parts[0], len(waited)), [whole_like, likes[0]],
-        *waited, *pieces, weight, flops=flops, name="stack_product",
+    for n in columns(product.shape[1]):
+        product[:, n] = matmul(whole[...], weight[:, n]).astype(BF)
+
+
+def stack_times(pieces, weight, waited=()):
+    tokens = len(pieces) * pieces[0].shape[0]
+    return run(
+        functools.partial(stack_product, len(waited)),
+        [jax.ShapeDtypeStruct((tokens, count), BF) for count in weight.shape],
+        *waited, *pieces, weight,
+        flops=2 * tokens * weight.size, name="stack_product",
     )
-    rest = [
-        run(functools.partial(product_part, part), [like], whole, weight, flops=flops, name="product_part")[0]
-        for part, like in zip(parts[1:], likes[1:])
-    ]
-    return whole, [first, *rest]
 
 
 def put_rows(pieces, n, product):
@@ -274,36 +268,26 @@
         grad_pre[:, n] = (grad * silu_slope(pre)).astype(BF)
 
 
-def first_part(pointwise, part, *refs):
-    *ins, weight, hidden, total = refs
+def hidden_product(pointwise, count, *refs):
+    *ins, weight, hidden = refs[:-count]
     pointwise(*ins, hidden)
     for n in columns(weight.shape[1]):
-        total[:, n] = matmul(hidden[...], weight[part, n])
-
-
-def last_part(pointwise, part, count, *refs):
-    *ins, weight, total, hidden = refs[:-count]
-    pointwise(*ins, hidden)
-    for n in columns(weight.shape[1]):
-        put_rows(refs[-count:], n, total[:, n] + matmul(hidden[...], weight[part, n]))
-
-
-def through(pointwise, name, parts, ins, weight, piece_like, rows):
-    tokens, width = rows * piece_like.shape[0], piece_like.shape[1]
-    (first, last), done = parts, []
-    flops = 2 * tokens * width * (first.stop - first.start)
-    like = [jax.ShapeDtypeStruct((tokens, part.stop - part.start), BF) for part in parts]
-    hidden, total = run(
-        functools.partial(first_part, pointwise, first),
-        [like[0], jax.ShapeDtypeStruct((tokens, width), F32)],
-        *ins[0], weight, flops=flops, name=name,
-    )
-    rest, *pieces = run(
-        functools.partial(last_part, pointwise, last, rows),
-        [like[1]] + [piece_like] * rows,
-        *ins[1], weight, total, flops=flops, name=name,
-    )
-    return [hidden, rest], pieces
+        put_rows(refs[-count:], n, matmul(hidden[...], weight[:, n]))
+
+
+def through(pointwise, name, ins, weight, piece_like):
+    hiddens, pieces = [], []
+    for half in ins:
+        tokens = half[0].shape[0]
+        count = tokens // piece_like.shape[0]
+        hidden, *done = run(
+            functools.partial(hidden_product, pointwise, count),
+            [jax.ShapeDtypeStruct((tokens, weight.shape[0]), BF)] + [piece_like] * count,
+            *half, weight, flops=2 * tokens * weight.size, name=name,
+        )
+        hiddens.append(hidden)
+        pieces += done
+    return hiddens, pieces
 
 
 def both_silu(*refs):
@@ -312,20 +296,20 @@
     silu_part(*ins[2:], last)
 
 
-def down_again(parts, first, last, weight, *pieces):
+def down_again(first, last, weight, *pieces):
     for n in columns(weight.shape[1]):
-        total = matmul(first[...], weight[parts[0], n]) + matmul(last[...], weight[parts[1], n])
-        put_rows(pieces, n, total)
+        for hidden, half in zip((first, last), halves(pieces)):
+            put_rows(half, n, matmul(hidden[...], weight[:, n]))
 
 
 def weight_grad(start, lefts, rights, out, left, right, room, sems):
-    count, depth = len(lefts), rights[0].shape[0]
-    for t in range(count):
-        left[:, t * depth : (t + 1) * depth] = lefts[t][...]
-        place = 0
-        for block in rights[t * len(rights) // count : (t + 1) * len(rights) // count]:
-            right[t * depth : (t + 1) * depth, place : place + block.shape[1]] = block[...]
-            place += block.shape[1]
+    depth = lefts[0].shape[1]
+    for t, block in enumerate(lefts):
+        left[:, t * depth : (t + 1) * depth] = block[start : start + left.shape[0], :]
+    place = 0
+    for block in rights:
+        right[place : place + block.shape[0], :] = block[...]
+        place += block.shape[0]
     copies = []
     for i, m in enumerate(columns(left.shape[0])):
         for n in columns(out.shape[1]):
@@ -353,8 +337,8 @@
 def weight_products(jobs, begun=None):
     cuts, ins, scratch = [], [], []
     flops = size = 0
-    for lefts, rights, shape, start in jobs:
-        count, depth = lefts[0].shape[0], rights[0].shape[0] * len(lefts)
+    for lefts, rights, shape, start, end in jobs:
+        count, depth = end - start, lefts[0].shape[1] * len(lefts)
         cuts.append((start, len(lefts), len(rights)))
         ins += [*lefts, *rights]
         scratch += [
@@ -369,7 +353,7 @@
         functools.partial(weight_grads, tuple(cuts), begun is not None),
         in_specs=vmem(len(ins)) + [pl.BlockSpec(memory_space=pl.ANY)] * (begun is not None),
         out_specs=[pl.BlockSpec(memory_space=pl.ANY)] * len(jobs),
-        out_shape=[jax.ShapeDtypeStruct(shape, BF) for _, _, shape, _ in jobs],
+        out_shape=[jax.ShapeDtypeStruct(shape, BF) for _, _, shape, _, _ in jobs],
         scratch_shapes=scratch,
         input_output_aliases={} if begun is None else {len(ins): len(jobs) - 1},
         compiler_params=pltpu.CompilerParams(vmem_limit_bytes=18 << 20),
@@ -403,39 +387,45 @@
     piece_rows, width = inputs.shape[2:]
     tokens, hidden = rows * piece_rows, w_up.shape[2]
     stack_like = jax.ShapeDtypeStruct((1, ticks, piece_rows, width), BF)
-    parts = [slice(0, hidden // 2), slice(hidden // 2, hidden)]
     piece_like = jax.ShapeDtypeStruct((piece_rows, width), BF)
-    part_like = jax.ShapeDtypeStruct((tokens, hidden // 2), BF)
-    turned_like = jax.ShapeDtypeStruct((width, tokens), BF)
-    turned_part = jax.ShapeDtypeStruct((hidden // 2, tokens), BF)
+    half_like = jax.ShapeDtypeStruct((tokens // 2, hidden), BF)
+
+    def products(pieces, weight, waited=()):
+        near, far = halves(pieces)
+        return zip(stack_times(near, weight, waited), stack_times(far, weight))
+
+    def gathered(block, others=()):
+        near, far = halves(gather_rows(block))
+        return [*near, *(after(far, others) if others else far)]
 
     def turn_blocks(tick, other):
-        turned_ins.extend(run(turned, [turned_like], after(full_ins[tick], other)))
-        for k in range(2):
-            turned_acts[k].extend(run(turned, [turned_part], after(acts[tick][k], other)))
+        for blocks, done in ((full_ins, turned_ins), (acts, turned_acts)):
+            like = jax.ShapeDtypeStruct((blocks[tick][0].shape[1], tokens), BF)
+            done.extend(run(turned, [like], *after(blocks[tick], other)))
 
     act_in, last_cot = first_pieces(inputs, cotangent)
     cot_pieces = [last_cot] + [None] * (rows - 1)
     full_ins, acts, pres, seen_in, seen_out = [], [], [], [], []
-    turned_ins, turned_acts = [], [[], []]
+    turned_ins, turned_acts = [], []
     for tick in range(ticks):
-        waited = []
-        if tick:
-            act_in = run(arrive, [piece_like], bases[tick - 1], hand_over(sending, 1))[0]
-            for j in beside(tick - 1):
-                cot_pieces[j] = swap_rows(after(last_cot, sending), j)
-                waited.append(cot_pieces[j])
-        pieces = gather_rows(act_in)
         if tick == 0:
             up_kept, down_kept = hold(after([w_up[0], w_down[0]], act_in))
-            pieces = after(pieces, up_kept)
-        if tick == ticks - 1:
-            full_cot, first_grads = products(parts, cot_pieces, down_turned)
-            pieces, waited = after(pieces, first_grads), []
-        full_in, partial = products(parts, pieces, up_kept, waited)
+            pieces, waited = gathered(act_in), []
+        else:
+            act_in = run(arrive, [piece_like], bases[tick - 1], hand_over(sending, 1))[0]
+            waited = beside(tick - 1)
+            for j in waited:
+                cot_pieces[j] = swap_rows(after(last_cot, sending), j)
+            waited = [cot_pieces[j] for j in waited]
+            if tick == ticks - 1:
+                full_cot, first_grads = products(cot_pieces, down_turned)
+                pieces, waited = gathered(act_in, first_grads), []
+            else:
+                pieces = gathered(act_in)
+        full_in, partial = products(pieces, up_kept, waited)
         pre = [(mine, other_cols(mine)) for mine in partial]
         if tick < ticks - 1:
-            act, terms = through(silu_part, "down_part", parts, pre, down_kept, piece_like, rows)
+            act, terms = through(silu_part, "down_part", pre, down_kept, piece_like)
             acts.append(act)
             terms_in = scatter_rows(terms)
             if tick == 0:
@@ -461,32 +451,32 @@
         else:
             arrived = hand_over(sending, -1)
             if step == 1:
-                acts.append(run(both_silu, [part_like] * 2, *after([*pres[-1][0], *pres[-1][1]], sending)))
+                acts.append(run(both_silu, [half_like] * 2, *after([*pres[-1][0], *pres[-1][1]], sending)))
                 out_pieces = run(
-                    functools.partial(down_again, parts), [piece_like] * rows, *acts[-1], down_kept,
-                    flops=2 * tokens * width * hidden, name="down_again",
+                    down_again, [piece_like] * rows, *acts[-1], down_kept, flops=2 * tokens * width * hidden
                 )
                 arrived = after(arrived, out_pieces)
                 out_terms = list(out_pieces)
             (grad_out,) = run(arrive, [piece_like], cots[tick], arrived)
-            waited = []
             for j in beside(step - 1):
                 out_terms[j] = swap_rows(after(out_pieces[j], sending), j)
-                waited.append(out_terms[j])
-            pieces = gather_rows(grad_out)
+            waited = [out_terms[j] for j in beside(step - 1)]
             if step == ticks - 1:
                 section_input, section_output = stacked(
                     functools.partial(finish_forward, ticks), 2, [*seen_in, *seen_out, *out_terms], stack_like,
                     "finish_forward",
                 )
-                pieces, waited = after(pieces, section_output), []
-            full_grad, partial = products(parts, pieces, down_turned, waited)
+                pieces, waited = gathered(grad_out, [section_output]), []
+            else:
+                pieces = gathered(grad_out)
+            full_grad, partial = products(pieces, down_turned, waited)
         full_grads[tick] = full_grad
         ins = [(mine, other_cols(mine), *known) for mine, known in zip(partial, pres[tick])]
         if step == ticks - 1:
-            (half_down,) = weight_products([(turned_acts[0], full_grads, (hidden, width), 0)])
-            ins[0] = after(ins[0], half_down)
-        grad_pre, terms = through(slope_part, "in_part", parts, ins, up_turned, piece_like, rows)
+            grad_halves = [half for blocks in full_grads for half in blocks]
+            (half_down,) = weight_products([(turned_acts, grad_halves, (hidden, width), 0, hidden // 2)])
+            ins[1] = after(ins[1], half_down)
+        grad_pre, terms = through(slope_part, "in_part", ins, up_turned, piece_like)
         terms_in = scatter_rows(terms)
         if step < ticks - 1:
             turn_blocks(step + 1, terms)
@@ -494,11 +484,11 @@
             (sending,) = run(leave_back, [piece_like], grad_out, *terms_in)
             seen_grad[tick] = sending
         pre_grads[tick] = grad_pre
-    turned_ins, last_acts = after((turned_ins, turned_acts[1]), terms)
+    turned_ins, turned_acts = after((turned_ins, turned_acts), terms)
     grad_up, grad_down = weight_products(
         [
-            (turned_ins, [part for grad_pre in pre_grads for part in grad_pre], (width, hidden), 0),
-            (last_acts, full_grads, (hidden, width), hidden // 2),
+            (turned_ins, [half for blocks in pre_grads for half in blocks], (width, hidden), 0, width),
+            (turned_acts, grad_halves, (hidden, width), hidden // 2, hidden),
         ],
         half_down,
     )

time: 136 us -> 141 us (1.037)
  waiting for transfers between devices: 42 us -> 27.7 us
  starting transfers between devices: 63.2 us -> 72.8 us
  Pallas kernels: 29.5 us -> 37.8 us
    ppermute x36, waiting for transfers between devices: 34.7 us -> 22.5 us  [swap_rows(): lax.ppermute(block, 'row', [(i, partner(i, j, size)) for i in range(size)])]
    ppermute x12, starting transfers between devices: 8.78 us -> 19.6 us  [turn(): lax.ppermute(block, axis, [(i, (i + distance) % size) for i in range(size)])]
    pallas_call x43 -> x40, Pallas kernels: 15.5 us -> 23.8 us  [run(): pl.pallas_call(kernel, in_specs=vmem(len(ins)), out_specs=vmem(len(outs))...]
    ppermute x12, waiting for transfers between devices: 3.98 us -> 1.08 us  [turn(): lax.ppermute(block, axis, [(i, (i + distance) % size) for i in range(size)])]
    ppermute x36, starting transfers between devices: 44 us -> 41.8 us  [swap_rows(): lax.ppermute(block, 'row', [(i, partner(i, j, size)) for i in range(size)])]
  transfers between devices with their start and end apart: 52 -> 52, of which waited for: 27 -> 19; matrix products, arithmetic and copies ran while one was open for 0% -> 0% of each run, Pallas kernels for 17% -> 25%
where the time goes in v12:
time: 141 us; the launch traced here: 139 us
  starting transfers between devices  72.8 us (52%)
  Pallas kernels  37.8 us (27%)
  waiting for transfers between devices  27.7 us (20%)
    ppermute x36, starting transfers between devices, swap_rows(): lax.ppermute(block, 'row', [(i, partner(i, j, size)) for i in range(size)])  41.8 us
    pallas_call x40, Pallas kernels, run(): pl.pallas_call(kernel, in_specs=vmem(len(ins)), out_specs=vmem(len(outs))...  23.8 us
    ppermute x36, waiting for transfers between devices, swap_rows(): lax.ppermute(block, 'row', [(i, partner(i, j, size)) for i in range(size)])  22.5 us
    ppermute x12, starting transfers between devices, turn(): lax.ppermute(block, axis, [(i, (i + distance) % size) for i in range(size)])  19.6 us
    ppermute x4, starting transfers between devices, hand_over(): lax.ppermute(block, 'section', [(i - distance, i) for i in sections if i...  11.4 us
    pallas_call x2, Pallas kernels, weight_products(): pl.pallas_call(functools.partial(weight_grads, tuple(cuts), begun is not...  6.4 us
    ppermute x4, waiting for transfers between devices, hand_over(): lax.ppermute(block, 'section', [(i - distance, i) for i in sections if i...  4.1 us
    pallas_call x1, Pallas kernels, hold(): pl.pallas_call(hold_kernel, in_specs=[pl.BlockSpec(memory_space=pltpu.HBM...  3.51 us
  transfers between devices with their start and end apart: 52, of which 19 were waited for; matrix products, arithmetic and copies ran while one was open for 0% of the time, Pallas kernels for 25%

profile of v12, /device:TPU:3, one launch (start us, length us, event | category | flops | bytes accessed | tf_op | source)
XLA Modules:
  0.0 139.4 jit_solution(12280587932463578558)
XLA Ops:
  0.6 0.9 first.1
  1.5 1.4 collective-permute-start
  2.9 2.2 %collective-permute-start.3 = (bf16[32,1024]{1,0:T(8,128)(2,1)S(1)}, bf16[32,1024]{1,0:T(8,128)(2,1)S(1)}, u32[]{:S(2)}, u32[]{:S(2)}) collective-permute-start(bf16[32,1024]{1,0:T(8,128)(2,1)S(1)} %get-tuple-element.129.refs_0_.first), channel_id=1, source_target_pairs={{0,6},{2,4},{4,2},{6,0},{1,7},{3,5},{5,3},{7,1},{8,14},{10,12},{12... | collective-permute-start | bytes 196616 | tf_op jit(solution)/shard_map/ppermute | solution.py:31
  5.2 3.5 %hold.1 = (bf16[1024,2048]{1,0:T(8,128)(2,1)S(1)}, bf16[2048,1024]{1,0:T(8,128)(2,1)S(1)}) custom-call(bf16[1024,2048]{1,0:T(8,128)(2,1)} %bitcast.4, bf16[2048,1024]{1,0:T(8,128)(2,1)} %bitcast.5), custom_call_target="tpu_custom_call" | custom-call | bytes 16777216 | tf_op jit(solution)/shard_map/hold/pallas_call | solution.py:218
  8.7 0.8 stack_product.12
  9.6 1.3 collective-permute-start.1
  10.9 1.4 collective-permute-done.2.refs_0_
  13.7 0.8 down_part.4
  14.8 0.8 down_part.5
  15.7 2.2 %collective-permute-start.6 = (bf16[32,1024]{1,0:T(8,128)(2,1)S(1)}, bf16[32,1024]{1,0:T(8,128)(2,1)S(1)}, u32[]{:S(2)}, u32[]{:S(2)}) collective-permute-start(bf16[32,1024]{1,0:T(8,128)(2,1)S(1)} %get-tuple-element.138), channel_id=1, source_target_pairs={{0,4},{2,6},{4,0},{6,2},{1,5},{3,7},{5,1},{7,3},{8,12},{10,14},{12... | collective-permute-start | bytes 196616 | tf_op jit(solution)/shard_map/ppermute | solution.py:31
  17.9 1.1 collective-permute-start.7
  19.1 1.2 turned_weight.2.refs_2_.refs_4_
  20.3 1.7 %fetch.1 = (bf16[32,1024]{1,0:T(8,128)(2,1)S(1)}, bf16[32,1024]{1,0:T(8,128)(2,1)S(1)}, bf16[32,1024]{1,0:T(8,128)(2,1)S(1)}, bf16[32,1024]{1,0:T(8,128)(2,1)S(1...) custom-call(s32[6]{0:T(128)S(1)} %copy-done, bf16[1,3,32,1024]{3,2,1,0:T(8,128)(2,1)} %inputs.3, ...), custom_call_target="tpu_custom_call" | custom-call | bytes 2097152 | tf_op jit(solution)/shard_map/fetch/pallas_call | solution.py:113
  22.1 0.9 collective-permute-done.7.refs_3_
  23.0 3.1 %collective-permute-start.8 = (bf16[32,1024]{1,0:T(8,128)(2,1)S(1)}, bf16[32,1024]{1,0:T(8,128)(2,1)S(1)}, u32[]{:S(2)}, u32[]{:S(2)}) collective-permute-start(bf16[32,1024]{1,0:T(8,128)(2,1)S(1)} %get-tuple-element.146), channel_id=1, source_target_pairs={{0,8},{8,16},{16,24},{1,9},{9,17},{17,25},{2,10},{10,18},{18,26},{... | collective-permute-start | bytes 196616 | tf_op jit(solution)/shard_map/ppermute | solution.py:17
  26.2 2.2 %collective-permute-start.10 = (bf16[32,1024]{1,0:T(8,128)(2,1)S(1)}, bf16[32,1024]{1,0:T(8,128)(2,1)S(1)}, u32[]{:S(2)}, u32[]{:S(2)}) collective-permute-start(bf16[32,1024]{1,0:T(8,128)(2,1)S(1)} %get-tuple-element.171.refs_0_.first), channel_id=1, source_target_pairs={{0,4},{2,6},{4,0},{6,2},{1,5},{3,7},{5,1},{7,3},{8,12},{10,14},{12... | collective-permute-start | bytes 196616 | tf_op jit(solution)/shard_map/ppermute | solution.py:31
  28.4 1.7 %collective-permute-start.11 = (bf16[32,1024]{1,0:T(8,128)(2,1)S(1)}, bf16[32,1024]{1,0:T(8,128)(2,1)S(1)}, u32[]{:S(2)}, u32[]{:S(2)}) collective-permute-start(bf16[32,1024]{1,0:T(8,128)(2,1)S(1)} %arrive.4.refs_2_.first.refs_1_), channel_id=1, source_target_pairs={{0,2},{2,0},{4,6},{6,4},{1,3},{3,1},{5,7},{7,5},{8,10},{10,8},{12,... | collective-permute-start | bytes 196616 | tf_op jit(solution)/shard_map/ppermute | solution.py:31
  30.1 1.7 %collective-permute-start.14 = (bf16[32,1024]{1,0:T(8,128)(2,1)S(1)}, bf16[32,1024]{1,0:T(8,128)(2,1)S(1)}, u32[]{:S(2)}, u32[]{:S(2)}) collective-permute-start(bf16[32,1024]{1,0:T(8,128)(2,1)S(1)} %arrive.4.refs_2_.first.refs_1_), channel_id=1, source_target_pairs={{0,6},{2,4},{4,2},{6,0},{1,7},{3,5},{5,3},{7,1},{8,14},{10,12},{12... | collective-permute-start | bytes 196616 | tf_op jit(solution)/shard_map/ppermute | solution.py:31
  31.8 1.2 collective-permute-done.11.refs_3_
  33.9 3.6 %collective-permute-start.12 = (bf16[64,2048]{1,0:T(8,128)(2,1)S(1)}, bf16[64,2048]{1,0:T(8,128)(2,1)S(1)}, u32[]{:S(2)}, u32[]{:S(2)}) collective-permute-start(bf16[64,2048]{1,0:T(8,128)(2,1)S(1)} %get-tuple-element.150.refs_0_.refs_2_), channel_id=1, source_target_pairs={{0,1},{1,0},{2,3},{3,2},{4,5},{5,4},{6,7},{7,6},{8,9},{9,8},{10,11... | collective-permute-start | bytes 786440 | tf_op jit(solution)/shard_map/ppermute | solution.py:22
  37.4 1.3 collective-permute-done.13.refs_0_
  39.6 1.7 %collective-permute-start.15 = (bf16[64,2048]{1,0:T(8,128)(2,1)S(1)}, bf16[64,2048]{1,0:T(8,128)(2,1)S(1)}, u32[]{:S(2)}, u32[]{:S(2)}) collective-permute-start(bf16[64,2048]{1,0:T(8,128)(2,1)S(1)} %get-tuple-element.153.refs_0_.refs_2_), channel_id=1, source_target_pairs={{0,1},{1,0},{2,3},{3,2},{4,5},{5,4},{6,7},{7,6},{8,9},{9,8},{10,11... | collective-permute-start | bytes 786440 | tf_op jit(solution)/shard_map/ppermute | solution.py:22
  41.2 0.8 down_part.6
  42.4 0.8 down_part.7
  43.3 1.7 %collective-permute-start.17 = (bf16[32,1024]{1,0:T(8,128)(2,1)S(1)}, bf16[32,1024]{1,0:T(8,128)(2,1)S(1)}, u32[]{:S(2)}, u32[]{:S(2)}) collective-permute-start(bf16[32,1024]{1,0:T(8,128)(2,1)S(1)} %get-tuple-element.154), channel_id=1, source_target_pairs={{0,4},{2,6},{4,0},{6,2},{1,5},{3,7},{5,1},{7,3},{8,12},{10,14},{12... | collective-permute-start | bytes 196616 | tf_op jit(solution)/shard_map/ppermute | solution.py:31
  45.0 1.6 %collective-permute-start.18 = (bf16[32,1024]{1,0:T(8,128)(2,1)S(1)}, bf16[32,1024]{1,0:T(8,128)(2,1)S(1)}, u32[]{:S(2)}, u32[]{:S(2)}) collective-permute-start(bf16[32,1024]{1,0:T(8,128)(2,1)S(1)} %get-tuple-element.155), channel_id=1, source_target_pairs={{0,6},{2,4},{4,2},{6,0},{1,7},{3,5},{5,3},{7,1},{8,14},{10,12},{12... | collective-permute-start | bytes 196616 | tf_op jit(solution)/shard_map/ppermute | solution.py:31
  46.6 1.2 turned_weight.3.refs_4_
  48.2 1.7 %collective-permute-done.18.refs_3_ = bf16[32,1024]{1,0:T(8,128)(2,1)S(1)} collective-permute-done((bf16[32,1024]{1,0:T(8,128)(2,1)S(1)}, bf16[32,1024]{1,0:T(8,128)(2,1)S(1)}, u32[]{:S(2)}, u32[]{:S(2)}) %collective-permute-start.18) | collective-permute-done | bytes 65568 | tf_op jit(solution)/shard_map/ppermute | solution.py:31
  50.0 4.2 %collective-permute-start.19 = (bf16[32,1024]{1,0:T(8,128)(2,1)S(1)}, bf16[32,1024]{1,0:T(8,128)(2,1)S(1)}, u32[]{:S(2)}, u32[]{:S(2)}) collective-permute-start(bf16[32,1024]{1,0:T(8,128)(2,1)S(1)} %get-tuple-element.166), channel_id=1, source_target_pairs={{0,8},{8,16},{16,24},{1,9},{9,17},{17,25},{2,10},{10,18},{18,26},{... | collective-permute-start | bytes 196616 | tf_op jit(solution)/shard_map/ppermute | solution.py:17
  54.2 1.5 %collective-permute-start.24 = (bf16[32,1024]{1,0:T(8,128)(2,1)S(1)}, bf16[32,1024]{1,0:T(8,128)(2,1)S(1)}, u32[]{:S(2)}, u32[]{:S(2)}) collective-permute-start(bf16[32,1024]{1,0:T(8,128)(2,1)S(1)} %get-tuple-element.171.refs_0_.first), channel_id=1, source_target_pairs={{0,6},{2,4},{4,2},{6,0},{1,7},{3,5},{5,3},{7,1},{8,14},{10,12},{12... | collective-permute-start | bytes 196616 | tf_op jit(solution)/shard_map/ppermute | solution.py:31
  55.7 1.9 %collective-permute-start.23 = (bf16[32,1024]{1,0:T(8,128)(2,1)S(1)}, bf16[32,1024]{1,0:T(8,128)(2,1)S(1)}, u32[]{:S(2)}, u32[]{:S(2)}) collective-permute-start(bf16[32,1024]{1,0:T(8,128)(2,1)S(1)} %arrive.5.refs_0_.refs_2_), channel_id=1, source_target_pairs={{0,6},{2,4},{4,2},{6,0},{1,7},{3,5},{5,3},{7,1},{8,14},{10,12},{12... | collective-permute-start | bytes 196616 | tf_op jit(solution)/shard_map/ppermute | solution.py:31
  57.6 1.1 collective-permute-start.22
  60.1 3.9 %collective-permute-start.26 = (bf16[64,2048]{1,0:T(8,128)(2,1)S(1)}, bf16[64,2048]{1,0:T(8,128)(2,1)S(1)}, u32[]{:S(2)}, u32[]{:S(2)}) collective-permute-start(bf16[64,2048]{1,0:T(8,128)(2,1)S(1)} %get-tuple-element.170.refs_0_), channel_id=1, source_target_pairs={{0,1},{1,0},{2,3},{3,2},{4,5},{5,4},{6,7},{7,6},{8,9},{9,8},{10,11... | collective-permute-start | bytes 786440 | tf_op jit(solution)/shard_map/ppermute | solution.py:22
  64.1 0.8 stack_product.18
  65.0 0.9 collective-permute-done.22.refs_0_
  65.9 0.8 stack_product.16
  66.8 1.7 %collective-permute-start.21 = (bf16[64,2048]{1,0:T(8,128)(2,1)S(1)}, bf16[64,2048]{1,0:T(8,128)(2,1)S(1)}, u32[]{:S(2)}, u32[]{:S(2)}) collective-permute-start(bf16[64,2048]{1,0:T(8,128)(2,1)S(1)} %get-tuple-element.189.refs_2_.refs_0_), channel_id=1, source_target_pairs={{0,1},{1,0},{2,3},{3,2},{4,5},{5,4},{6,7},{7,6},{8,9},{9,8},{10,11... | collective-permute-start | bytes 786440 | tf_op jit(solution)/shard_map/ppermute | solution.py:22
  71.8 1.2 collective-permute-start.29
  73.0 2.0 %collective-permute-start.30 = (bf16[32,1024]{1,0:T(8,128)(2,1)S(1)}, bf16[32,1024]{1,0:T(8,128)(2,1)S(1)}, u32[]{:S(2)}, u32[]{:S(2)}) collective-permute-start(bf16[32,1024]{1,0:T(8,128)(2,1)S(1)} %get-tuple-element.181), channel_id=1, source_target_pairs={{0,6},{2,4},{4,2},{6,0},{1,7},{3,5},{5,3},{7,1},{8,14},{10,12},{12... | collective-permute-start | bytes 196616 | tf_op jit(solution)/shard_map/ppermute | solution.py:31
  75.3 1.0 collective-permute-done.29.refs_2_
  76.3 2.2 %collective-permute-done.30.refs_3_ = bf16[32,1024]{1,0:T(8,128)(2,1)S(1)} collective-permute-done((bf16[32,1024]{1,0:T(8,128)(2,1)S(1)}, bf16[32,1024]{1,0:T(8,128)(2,1)S(1)}, u32[]{:S(2)}, u32[]{:S(2)}) %collective-permute-start.30) | collective-permute-done | bytes 65568 | tf_op jit(solution)/shard_map/ppermute | solution.py:31
  78.5 1.9 %collective-permute-start.33 = (bf16[32,1024]{1,0:T(8,128)(2,1)S(1)}, bf16[32,1024]{1,0:T(8,128)(2,1)S(1)}, u32[]{:S(2)}, u32[]{:S(2)}) collective-permute-start(bf16[32,1024]{1,0:T(8,128)(2,1)S(1)} %leave_back.2.refs_5_), channel_id=1, source_target_pairs={{8,0},{16,8},{24,16},{9,1},{17,9},{25,17},{10,2},{18,10},{26,18},{... | collective-permute-start | bytes 196616 | tf_op jit(solution)/shard_map/ppermute | solution.py:17
  80.7 1.6 %down_again.1 = (bf16[32,1024]{1,0:T(8,128)(2,1)S(1)}, bf16[32,1024]{1,0:T(8,128)(2,1)S(1)}, bf16[32,1024]{1,0:T(8,128)(2,1)S(1)}, bf16[32,1024]{1,0:T(8,128)(2,1)S(1)}) custom-call(bf16[64,2048]{1,0:T(8,128)(2,1)S(1)} %get-tuple-element.213.first.refs_0_, bf16[64,2048]{1,0:T(8,128)(2,1)S(1)} %get-tuple-element.214.last.refs_1_, ...), custom_call_target="tpu_custom_call" | custom-call | flops 536870912 | bytes 4980736 | tf_op jit(solution)/shard_map/down_again/pallas_call | solution.py:62
  82.2 2.2 %collective-permute-done.33.arrived = bf16[32,1024]{1,0:T(8,128)(2,1)S(1)} collective-permute-done((bf16[32,1024]{1,0:T(8,128)(2,1)S(1)}, bf16[32,1024]{1,0:T(8,128)(2,1)S(1)}, u32[]{:S(2)}, u32[]{:S(2)}) %collective-permute-start.33) | collective-permute-done | bytes 65568 | tf_op jit(solution)/shard_map/ppermute | solution.py:17
  84.4 1.5 %collective-permute-start.37 = (bf16[32,1024]{1,0:T(8,128)(2,1)S(1)}, bf16[32,1024]{1,0:T(8,128)(2,1)S(1)}, u32[]{:S(2)}, u32[]{:S(2)}) collective-permute-start(bf16[32,1024]{1,0:T(8,128)(2,1)S(1)} %arrive.6.refs_2_.first), channel_id=1, source_target_pairs={{0,6},{2,4},{4,2},{6,0},{1,7},{3,5},{5,3},{7,1},{8,14},{10,12},{12... | collective-permute-start | bytes 196616 | tf_op jit(solution)/shard_map/ppermute | solution.py:31
  86.0 2.1 %collective-permute-start.36 = (bf16[32,1024]{1,0:T(8,128)(2,1)S(1)}, bf16[32,1024]{1,0:T(8,128)(2,1)S(1)}, u32[]{:S(2)}, u32[]{:S(2)}) collective-permute-start(bf16[32,1024]{1,0:T(8,128)(2,1)S(1)} %arrive.6.refs_2_.first), channel_id=1, source_target_pairs={{0,4},{2,6},{4,0},{6,2},{1,5},{3,7},{5,1},{7,3},{8,12},{10,14},{12... | collective-permute-start | bytes 196616 | tf_op jit(solution)/shard_map/ppermute | solution.py:31
  88.3 1.3 collective-permute-start.31
  89.8 3.3 %collective-permute-done.36.refs_0_ = bf16[32,1024]{1,0:T(8,128)(2,1)S(1)} collective-permute-done((bf16[32,1024]{1,0:T(8,128)(2,1)S(1)}, bf16[32,1024]{1,0:T(8,128)(2,1)S(1)}, u32[]{:S(2)}, u32[]{:S(2)}) %collective-permute-start.36) | collective-permute-done | bytes 65568 | tf_op jit(solution)/shard_map/ppermute | solution.py:31
  93.9 4.2 %collective-permute-start.38 = (bf16[64,2048]{1,0:T(8,128)(2,1)S(1)}, bf16[64,2048]{1,0:T(8,128)(2,1)S(1)}, u32[]{:S(2)}, u32[]{:S(2)}) collective-permute-start(bf16[64,2048]{1,0:T(8,128)(2,1)S(1)} %get-tuple-element.208.refs_0_), channel_id=1, source_target_pairs={{0,1},{1,0},{2,3},{3,2},{4,5},{5,4},{6,7},{7,6},{8,9},{9,8},{10,11... | collective-permute-start | bytes 786440 | tf_op jit(solution)/shard_map/ppermute | solution.py:22
  98.2 0.8 stack_product.20
  100.9 1.5 %collective-permute-start.41 = (bf16[32,1024]{1,0:T(8,128)(2,1)S(1)}, bf16[32,1024]{1,0:T(8,128)(2,1)S(1)}, u32[]{:S(2)}, u32[]{:S(2)}) collective-permute-start(bf16[32,1024]{1,0:T(8,128)(2,1)S(1)} %get-tuple-element.210), channel_id=1, source_target_pairs={{0,6},{2,4},{4,2},{6,0},{1,7},{3,5},{5,3},{7,1},{8,14},{10,12},{12... | collective-permute-start | bytes 196616 | tf_op jit(solution)/shard_map/ppermute | solution.py:31
  104.2 3.6 %collective-permute-done.40.refs_2_ = bf16[32,1024]{1,0:T(8,128)(2,1)S(1)} collective-permute-done((bf16[32,1024]{1,0:T(8,128)(2,1)S(1)}, bf16[32,1024]{1,0:T(8,128)(2,1)S(1)}, u32[]{:S(2)}, u32[]{:S(2)}) %collective-permute-start.40) | collective-permute-done | bytes 65568 | tf_op jit(solution)/shard_map/ppermute | solution.py:31
  107.8 1.3 collective-permute-done.39.refs_1_
  109.2 2.1 %collective-permute-start.43 = (bf16[32,1024]{1,0:T(8,128)(2,1)S(1)}, bf16[32,1024]{1,0:T(8,128)(2,1)S(1)}, u32[]{:S(2)}, u32[]{:S(2)}) collective-permute-start(bf16[32,1024]{1,0:T(8,128)(2,1)S(1)} %leave_back.3.refs_4_), channel_id=1, source_target_pairs={{8,0},{16,8},{24,16},{9,1},{17,9},{25,17},{10,2},{18,10},{26,18},{... | collective-permute-start | bytes 196616 | tf_op jit(solution)/shard_map/ppermute | solution.py:17
  111.4 1.8 %collective-permute-start.42 = (bf16[32,1024]{1,0:T(8,128)(2,1)S(1)}, bf16[32,1024]{1,0:T(8,128)(2,1)S(1)}, u32[]{:S(2)}, u32[]{:S(2)}) collective-permute-start(bf16[32,1024]{1,0:T(8,128)(2,1)S(1)} %get-tuple-element.216), channel_id=1, source_target_pairs={{0,6},{2,4},{4,2},{6,0},{1,7},{3,5},{5,3},{7,1},{8,14},{10,12},{12... | collective-permute-start | bytes 196616 | tf_op jit(solution)/shard_map/ppermute | solution.py:31
  113.2 1.9 %collective-permute-done.43.arrived = bf16[32,1024]{1,0:T(8,128)(2,1)S(1)} collective-permute-done((bf16[32,1024]{1,0:T(8,128)(2,1)S(1)}, bf16[32,1024]{1,0:T(8,128)(2,1)S(1)}, u32[]{:S(2)}, u32[]{:S(2)}) %collective-permute-start.43) | collective-permute-done | bytes 65568 | tf_op jit(solution)/shard_map/ppermute | solution.py:17
  115.1 1.8 %collective-permute-start.47 = (bf16[32,1024]{1,0:T(8,128)(2,1)S(1)}, bf16[32,1024]{1,0:T(8,128)(2,1)S(1)}, u32[]{:S(2)}, u32[]{:S(2)}) collective-permute-start(bf16[32,1024]{1,0:T(8,128)(2,1)S(1)} %arrive.7.refs_0_.first), channel_id=1, source_target_pairs={{0,6},{2,4},{4,2},{6,0},{1,7},{3,5},{5,3},{7,1},{8,14},{10,12},{12... | collective-permute-start | bytes 196616 | tf_op jit(solution)/shard_map/ppermute | solution.py:31
  117.0 1.8 %collective-permute-start.44 = (bf16[32,1024]{1,0:T(8,128)(2,1)S(1)}, bf16[32,1024]{1,0:T(8,128)(2,1)S(1)}, u32[]{:S(2)}, u32[]{:S(2)}) collective-permute-start(bf16[32,1024]{1,0:T(8,128)(2,1)S(1)} %arrive.7.refs_0_.first), channel_id=1, source_target_pairs={{0,2},{2,0},{4,6},{6,4},{1,3},{3,1},{5,7},{7,5},{8,10},{10,8},{12,... | collective-permute-start | bytes 196616 | tf_op jit(solution)/shard_map/ppermute | solution.py:31
  120.2 3.1 %collective-permute-done.46.refs_0_ = bf16[32,1024]{1,0:T(8,128)(2,1)S(1)} collective-permute-done((bf16[32,1024]{1,0:T(8,128)(2,1)S(1)}, bf16[32,1024]{1,0:T(8,128)(2,1)S(1)}, u32[]{:S(2)}, u32[]{:S(2)}) %collective-permute-start.46) | collective-permute-done | bytes 65568 | tf_op jit(solution)/shard_map/ppermute | solution.py:31
  124.1 1.9 %collective-permute-start.45 = (bf16[64,2048]{1,0:T(8,128)(2,1)S(1)}, bf16[64,2048]{1,0:T(8,128)(2,1)S(1)}, u32[]{:S(2)}, u32[]{:S(2)}) collective-permute-start(bf16[64,2048]{1,0:T(8,128)(2,1)S(1)} %get-tuple-element.220.refs_0_), channel_id=1, source_target_pairs={{0,1},{1,0},{2,3},{3,2},{4,5},{5,4},{6,7},{7,6},{8,9},{9,8},{10,11... | collective-permute-start | bytes 786440 | tf_op jit(solution)/shard_map/ppermute | solution.py:22
  126.9 2.1 %weight_grads.2.refs_18_ = bf16[2048,1024]{1,0:T(8,128)(2,1)} custom-call(bf16[2048,128]{1,0:T(8,128)(2,1)S(1)} %turned.7.refs_0_.refs_9_, bf16[2048,128]{1,0:T(8,128)(2,1)S(1)} %turned.9.refs_1_.refs_10_, bf16[2048,128]{1,0:T(8,128)(2,1)S(1)} %turned.11.refs_2_.refs_11_, bf16[64,1024]{1,0:T(8,128)(2,1)S(1)} %get-tuple-element.226.refs_3_.refs_12_, ...), custom_call_target="tpu_custom_call" | custom-call | flops 805306368 | bytes 2097152 | tf_op jit(solution)/shard_map/weight_grads/pallas_call | solution.py:352
  130.9 1.9 %collective-permute-start.50 = (bf16[32,1024]{1,0:T(8,128)(2,1)S(1)}, bf16[32,1024]{1,0:T(8,128)(2,1)S(1)}, u32[]{:S(2)}, u32[]{:S(2)}) collective-permute-start(bf16[32,1024]{1,0:T(8,128)(2,1)S(1)} %get-tuple-element.236), channel_id=1, source_target_pairs={{0,4},{2,6},{4,0},{6,2},{1,5},{3,7},{5,1},{7,3},{8,12},{10,14},{12... | collective-permute-start | bytes 196616 | tf_op jit(solution)/shard_map/ppermute | solution.py:31
  132.8 1.5 %collective-permute-start.51 = (bf16[32,1024]{1,0:T(8,128)(2,1)S(1)}, bf16[32,1024]{1,0:T(8,128)(2,1)S(1)}, u32[]{:S(2)}, u32[]{:S(2)}) collective-permute-start(bf16[32,1024]{1,0:T(8,128)(2,1)S(1)} %get-tuple-element.237), channel_id=1, source_target_pairs={{0,6},{2,4},{4,2},{6,0},{1,7},{3,5},{5,3},{7,1},{8,14},{10,12},{12... | collective-permute-start | bytes 196616 | tf_op jit(solution)/shard_map/ppermute | solution.py:31
  134.3 4.3 %weight_grads.3 = (bf16[1024,2048]{1,0:T(8,128)(2,1)}, bf16[2048,1024]{1,0:T(8,128)(2,1)}) custom-call(bf16[1024,128]{1,0:T(8,128)(2,1)S(1)} %turned.6.refs_0_, bf16[1024,128]{1,0:T(8,128)(2,1)S(1)} %turned.8.refs_1_, bf16[1024,128]{1,0:T(8,128)(2,1)S(1)} %turned.10.refs_2_, ...), custom_call_target="tpu_custom_call", output_to_operand_aliasing={{1}: (18, {})} | custom-call | flops 2415919104 | bytes 6291456 | tf_op jit(solution)/shard_map/weight_grads/pallas_call | solution.py:352
  (89 shorter events, 20.6 us)
Async XLA Ops:
  1.5 7.2 %collective-permute-start = (bf16[32,1024]{1,0:T(8,128)(2,1)S(1)}, bf16[32,1024]{1,0:T(8,128)(2,1)S(1)}, u32[]{:S(2)}, u32[]{:S(2)}) collective-permute-start(bf16[32,1024]{1,0:T(8,128)(2,1)S(1)} %get-tuple-element.129.refs_0_.first), channel_id=1, source_target_pairs={{0,2},{2,0},{4,6},{6,4},{1,3},{3,1},{5,7},{7,5},{8,10},{10,8},{12,... | collective-permute-start | bytes 196616 | tf_op jit(solution)/shard_map/ppermute | solution.py:31
  2.9 8.0 %collective-permute-start.3 = (bf16[32,1024]{1,0:T(8,128)(2,1)S(1)}, bf16[32,1024]{1,0:T(8,128)(2,1)S(1)}, u32[]{:S(2)}, u32[]{:S(2)}) collective-permute-start(bf16[32,1024]{1,0:T(8,128)(2,1)S(1)} %get-tuple-element.129.refs_0_.first), channel_id=1, source_target_pairs={{0,6},{2,4},{4,2},{6,0},{1,7},{3,5},{5,3},{7,1},{8,14},{10,12},{12... | collective-permute-start | bytes 196616 | tf_op jit(solution)/shard_map/ppermute | solution.py:31
  5.1 7.2 %collective-permute-start.2 = (bf16[32,1024]{1,0:T(8,128)(2,1)S(1)}, bf16[32,1024]{1,0:T(8,128)(2,1)S(1)}, u32[]{:S(2)}, u32[]{:S(2)}) collective-permute-start(bf16[32,1024]{1,0:T(8,128)(2,1)S(1)} %get-tuple-element.129.refs_0_.first), channel_id=1, source_target_pairs={{0,4},{2,6},{4,0},{6,2},{1,5},{3,7},{5,1},{7,3},{8,12},{10,14},{12... | collective-permute-start | bytes 196616 | tf_op jit(solution)/shard_map/ppermute | solution.py:31
  9.6 4.1 %collective-permute-start.1 = (bf16[64,2048]{1,0:T(8,128)(2,1)S(1)}, bf16[64,2048]{1,0:T(8,128)(2,1)S(1)}, u32[]{:S(2)}, u32[]{:S(2)}) collective-permute-start(bf16[64,2048]{1,0:T(8,128)(2,1)S(1)} %get-tuple-element.133.refs_0_.refs_2_), channel_id=1, source_target_pairs={{0,1},{1,0},{2,3},{3,2},{4,5},{5,4},{6,7},{7,6},{8,9},{9,8},{10,11... | collective-permute-start | bytes 786440 | tf_op jit(solution)/shard_map/ppermute | solution.py:22
  13.1 1.8 %collective-permute-start.4 = (bf16[64,2048]{1,0:T(8,128)(2,1)S(1)}, bf16[64,2048]{1,0:T(8,128)(2,1)S(1)}, u32[]{:S(2)}, u32[]{:S(2)}) collective-permute-start(bf16[64,2048]{1,0:T(8,128)(2,1)S(1)} %get-tuple-element.234.refs_0_.refs_2_), channel_id=1, source_target_pairs={{0,1},{1,0},{2,3},{3,2},{4,5},{5,4},{6,7},{7,6},{8,9},{9,8},{10,11... | collective-permute-start | bytes 786440 | tf_op jit(solution)/shard_map/ppermute | solution.py:22
  14.5 7.5 %collective-permute-start.5 = (bf16[32,1024]{1,0:T(8,128)(2,1)S(1)}, bf16[32,1024]{1,0:T(8,128)(2,1)S(1)}, u32[]{:S(2)}, u32[]{:S(2)}) collective-permute-start(bf16[32,1024]{1,0:T(8,128)(2,1)S(1)} %get-tuple-element.136), channel_id=1, source_target_pairs={{0,2},{2,0},{4,6},{6,4},{1,3},{3,1},{5,7},{7,5},{8,10},{10,8},{12,... | collective-permute-start | bytes 196616 | tf_op jit(solution)/shard_map/ppermute | solution.py:31
  15.7 6.4 %collective-permute-start.6 = (bf16[32,1024]{1,0:T(8,128)(2,1)S(1)}, bf16[32,1024]{1,0:T(8,128)(2,1)S(1)}, u32[]{:S(2)}, u32[]{:S(2)}) collective-permute-start(bf16[32,1024]{1,0:T(8,128)(2,1)S(1)} %get-tuple-element.138), channel_id=1, source_target_pairs={{0,4},{2,6},{4,0},{6,2},{1,5},{3,7},{5,1},{7,3},{8,12},{10,14},{12... | collective-permute-start | bytes 196616 | tf_op jit(solution)/shard_map/ppermute | solution.py:31
  17.9 5.0 %collective-permute-start.7 = (bf16[32,1024]{1,0:T(8,128)(2,1)S(1)}, bf16[32,1024]{1,0:T(8,128)(2,1)S(1)}, u32[]{:S(2)}, u32[]{:S(2)}) collective-permute-start(bf16[32,1024]{1,0:T(8,128)(2,1)S(1)} %get-tuple-element.139), channel_id=1, source_target_pairs={{0,6},{2,4},{4,2},{6,0},{1,7},{3,5},{5,3},{7,1},{8,14},{10,12},{12... | collective-permute-start | bytes 196616 | tf_op jit(solution)/shard_map/ppermute | solution.py:31
  19.1 1.2 copy-start
  23.0 5.4 %collective-permute-start.8 = (bf16[32,1024]{1,0:T(8,128)(2,1)S(1)}, bf16[32,1024]{1,0:T(8,128)(2,1)S(1)}, u32[]{:S(2)}, u32[]{:S(2)}) collective-permute-start(bf16[32,1024]{1,0:T(8,128)(2,1)S(1)} %get-tuple-element.146), channel_id=1, source_target_pairs={{0,8},{8,16},{16,24},{1,9},{9,17},{17,25},{2,10},{10,18},{18,26},{... | collective-permute-start | bytes 196616 | tf_op jit(solution)/shard_map/ppermute | solution.py:17
  26.2 5.7 %collective-permute-start.10 = (bf16[32,1024]{1,0:T(8,128)(2,1)S(1)}, bf16[32,1024]{1,0:T(8,128)(2,1)S(1)}, u32[]{:S(2)}, u32[]{:S(2)}) collective-permute-start(bf16[32,1024]{1,0:T(8,128)(2,1)S(1)} %get-tuple-element.171.refs_0_.first), channel_id=1, source_target_pairs={{0,4},{2,6},{4,0},{6,2},{1,5},{3,7},{5,1},{7,3},{8,12},{10,14},{12... | collective-permute-start | bytes 196616 | tf_op jit(solution)/shard_map/ppermute | solution.py:31
  28.4 3.4 %collective-permute-start.9 = (bf16[32,1024]{1,0:T(8,128)(2,1)S(1)}, bf16[32,1024]{1,0:T(8,128)(2,1)S(1)}, u32[]{:S(2)}, u32[]{:S(2)}) collective-permute-start(bf16[32,1024]{1,0:T(8,128)(2,1)S(1)} %get-tuple-element.171.refs_0_.first), channel_id=1, source_target_pairs={{0,2},{2,0},{4,6},{6,4},{1,3},{3,1},{5,7},{7,5},{8,10},{10,8},{12,... | collective-permute-start | bytes 196616 | tf_op jit(solution)/shard_map/ppermute | solution.py:31
  28.4 4.6 %collective-permute-start.11 = (bf16[32,1024]{1,0:T(8,128)(2,1)S(1)}, bf16[32,1024]{1,0:T(8,128)(2,1)S(1)}, u32[]{:S(2)}, u32[]{:S(2)}) collective-permute-start(bf16[32,1024]{1,0:T(8,128)(2,1)S(1)} %arrive.4.refs_2_.first.refs_1_), channel_id=1, source_target_pairs={{0,2},{2,0},{4,6},{6,4},{1,3},{3,1},{5,7},{7,5},{8,10},{10,8},{12,... | collective-permute-start | bytes 196616 | tf_op jit(solution)/shard_map/ppermute | solution.py:31
  30.1 7.4 %collective-permute-start.14 = (bf16[32,1024]{1,0:T(8,128)(2,1)S(1)}, bf16[32,1024]{1,0:T(8,128)(2,1)S(1)}, u32[]{:S(2)}, u32[]{:S(2)}) collective-permute-start(bf16[32,1024]{1,0:T(8,128)(2,1)S(1)} %arrive.4.refs_2_.first.refs_1_), channel_id=1, source_target_pairs={{0,6},{2,4},{4,2},{6,0},{1,7},{3,5},{5,3},{7,1},{8,14},{10,12},{12... | collective-permute-start | bytes 196616 | tf_op jit(solution)/shard_map/ppermute | solution.py:31
  31.8 6.9 %collective-permute-start.13 = (bf16[32,1024]{1,0:T(8,128)(2,1)S(1)}, bf16[32,1024]{1,0:T(8,128)(2,1)S(1)}, u32[]{:S(2)}, u32[]{:S(2)}) collective-permute-start(bf16[32,1024]{1,0:T(8,128)(2,1)S(1)} %arrive.4.refs_2_.first.refs_1_), channel_id=1, source_target_pairs={{0,4},{2,6},{4,0},{6,2},{1,5},{3,7},{5,1},{7,3},{8,12},{10,14},{12... | collective-permute-start | bytes 196616 | tf_op jit(solution)/shard_map/ppermute | solution.py:31
  33.9 7.4 %collective-permute-start.12 = (bf16[64,2048]{1,0:T(8,128)(2,1)S(1)}, bf16[64,2048]{1,0:T(8,128)(2,1)S(1)}, u32[]{:S(2)}, u32[]{:S(2)}) collective-permute-start(bf16[64,2048]{1,0:T(8,128)(2,1)S(1)} %get-tuple-element.150.refs_0_.refs_2_), channel_id=1, source_target_pairs={{0,1},{1,0},{2,3},{3,2},{4,5},{5,4},{6,7},{7,6},{8,9},{9,8},{10,11... | collective-permute-start | bytes 786440 | tf_op jit(solution)/shard_map/ppermute | solution.py:22
  39.6 2.8 %collective-permute-start.15 = (bf16[64,2048]{1,0:T(8,128)(2,1)S(1)}, bf16[64,2048]{1,0:T(8,128)(2,1)S(1)}, u32[]{:S(2)}, u32[]{:S(2)}) collective-permute-start(bf16[64,2048]{1,0:T(8,128)(2,1)S(1)} %get-tuple-element.153.refs_0_.refs_2_), channel_id=1, source_target_pairs={{0,1},{1,0},{2,3},{3,2},{4,5},{5,4},{6,7},{7,6},{8,9},{9,8},{10,11... | collective-permute-start | bytes 786440 | tf_op jit(solution)/shard_map/ppermute | solution.py:22
  42.1 6.1 %collective-permute-start.16 = (bf16[32,1024]{1,0:T(8,128)(2,1)S(1)}, bf16[32,1024]{1,0:T(8,128)(2,1)S(1)}, u32[]{:S(2)}, u32[]{:S(2)}) collective-permute-start(bf16[32,1024]{1,0:T(8,128)(2,1)S(1)} %get-tuple-element.152), channel_id=1, source_target_pairs={{0,2},{2,0},{4,6},{6,4},{1,3},{3,1},{5,7},{7,5},{8,10},{10,8},{12,... | collective-permute-start | bytes 196616 | tf_op jit(solution)/shard_map/ppermute | solution.py:31
  43.3 4.9 %collective-permute-start.17 = (bf16[32,1024]{1,0:T(8,128)(2,1)S(1)}, bf16[32,1024]{1,0:T(8,128)(2,1)S(1)}, u32[]{:S(2)}, u32[]{:S(2)}) collective-permute-start(bf16[32,1024]{1,0:T(8,128)(2,1)S(1)} %get-tuple-element.154), channel_id=1, source_target_pairs={{0,4},{2,6},{4,0},{6,2},{1,5},{3,7},{5,1},{7,3},{8,12},{10,14},{12... | collective-permute-start | bytes 196616 | tf_op jit(solution)/shard_map/ppermute | solution.py:31
  45.0 4.9 %collective-permute-start.18 = (bf16[32,1024]{1,0:T(8,128)(2,1)S(1)}, bf16[32,1024]{1,0:T(8,128)(2,1)S(1)}, u32[]{:S(2)}, u32[]{:S(2)}) collective-permute-start(bf16[32,1024]{1,0:T(8,128)(2,1)S(1)} %get-tuple-element.155), channel_id=1, source_target_pairs={{0,6},{2,4},{4,2},{6,0},{1,7},{3,5},{5,3},{7,1},{8,14},{10,12},{12... | collective-permute-start | bytes 196616 | tf_op jit(solution)/shard_map/ppermute | solution.py:31
  50.0 5.7 %collective-permute-start.19 = (bf16[32,1024]{1,0:T(8,128)(2,1)S(1)}, bf16[32,1024]{1,0:T(8,128)(2,1)S(1)}, u32[]{:S(2)}, u32[]{:S(2)}) collective-permute-start(bf16[32,1024]{1,0:T(8,128)(2,1)S(1)} %get-tuple-element.166), channel_id=1, source_target_pairs={{0,8},{8,16},{16,24},{1,9},{9,17},{17,25},{2,10},{10,18},{18,26},{... | collective-permute-start | bytes 196616 | tf_op jit(solution)/shard_map/ppermute | solution.py:17
  54.2 9.9 %collective-permute-start.24 = (bf16[32,1024]{1,0:T(8,128)(2,1)S(1)}, bf16[32,1024]{1,0:T(8,128)(2,1)S(1)}, u32[]{:S(2)}, u32[]{:S(2)}) collective-permute-start(bf16[32,1024]{1,0:T(8,128)(2,1)S(1)} %get-tuple-element.171.refs_0_.first), channel_id=1, source_target_pairs={{0,6},{2,4},{4,2},{6,0},{1,7},{3,5},{5,3},{7,1},{8,14},{10,12},{12... | collective-permute-start | bytes 196616 | tf_op jit(solution)/shard_map/ppermute | solution.py:31
  55.7 9.3 %collective-permute-start.23 = (bf16[32,1024]{1,0:T(8,128)(2,1)S(1)}, bf16[32,1024]{1,0:T(8,128)(2,1)S(1)}, u32[]{:S(2)}, u32[]{:S(2)}) collective-permute-start(bf16[32,1024]{1,0:T(8,128)(2,1)S(1)} %arrive.5.refs_0_.refs_2_), channel_id=1, source_target_pairs={{0,6},{2,4},{4,2},{6,0},{1,7},{3,5},{5,3},{7,1},{8,14},{10,12},{12... | collective-permute-start | bytes 196616 | tf_op jit(solution)/shard_map/ppermute | solution.py:31
  57.6 8.3 %collective-permute-start.22 = (bf16[32,1024]{1,0:T(8,128)(2,1)S(1)}, bf16[32,1024]{1,0:T(8,128)(2,1)S(1)}, u32[]{:S(2)}, u32[]{:S(2)}) collective-permute-start(bf16[32,1024]{1,0:T(8,128)(2,1)S(1)} %arrive.5.refs_0_.refs_2_), channel_id=1, source_target_pairs={{0,4},{2,6},{4,0},{6,2},{1,5},{3,7},{5,1},{7,3},{8,12},{10,14},{12... | collective-permute-start | bytes 196616 | tf_op jit(solution)/shard_map/ppermute | solution.py:31
  58.7 7.2 %collective-permute-start.20 = (bf16[32,1024]{1,0:T(8,128)(2,1)S(1)}, bf16[32,1024]{1,0:T(8,128)(2,1)S(1)}, u32[]{:S(2)}, u32[]{:S(2)}) collective-permute-start(bf16[32,1024]{1,0:T(8,128)(2,1)S(1)} %arrive.5.refs_0_.refs_2_), channel_id=1, source_target_pairs={{0,2},{2,0},{4,6},{6,4},{1,3},{3,1},{5,7},{7,5},{8,10},{10,8},{12,... | collective-permute-start | bytes 196616 | tf_op jit(solution)/shard_map/ppermute | solution.py:31
  60.1 9.3 %collective-permute-start.26 = (bf16[64,2048]{1,0:T(8,128)(2,1)S(1)}, bf16[64,2048]{1,0:T(8,128)(2,1)S(1)}, u32[]{:S(2)}, u32[]{:S(2)}) collective-permute-start(bf16[64,2048]{1,0:T(8,128)(2,1)S(1)} %get-tuple-element.170.refs_0_), channel_id=1, source_target_pairs={{0,1},{1,0},{2,3},{3,2},{4,5},{5,4},{6,7},{7,6},{8,9},{9,8},{10,11... | collective-permute-start | bytes 786440 | tf_op jit(solution)/shard_map/ppermute | solution.py:22
  64.9 5.7 %collective-permute-start.27 = (bf16[64,2048]{1,0:T(8,128)(2,1)S(1)}, bf16[64,2048]{1,0:T(8,128)(2,1)S(1)}, u32[]{:S(2)}, u32[]{:S(2)}) collective-permute-start(bf16[64,2048]{1,0:T(8,128)(2,1)S(1)} %get-tuple-element.172.refs_0_), channel_id=1, source_target_pairs={{0,1},{1,0},{2,3},{3,2},{4,5},{5,4},{6,7},{7,6},{8,9},{9,8},{10,11... | collective-permute-start | bytes 786440 | tf_op jit(solution)/shard_map/ppermute | solution.py:22
  66.8 2.9 %collective-permute-start.21 = (bf16[64,2048]{1,0:T(8,128)(2,1)S(1)}, bf16[64,2048]{1,0:T(8,128)(2,1)S(1)}, u32[]{:S(2)}, u32[]{:S(2)}) collective-permute-start(bf16[64,2048]{1,0:T(8,128)(2,1)S(1)} %get-tuple-element.189.refs_2_.refs_0_), channel_id=1, source_target_pairs={{0,1},{1,0},{2,3},{3,2},{4,5},{5,4},{6,7},{7,6},{8,9},{9,8},{10,11... | collective-permute-start | bytes 786440 | tf_op jit(solution)/shard_map/ppermute | solution.py:22
  69.3 1.6 %collective-permute-start.25 = (bf16[64,2048]{1,0:T(8,128)(2,1)S(1)}, bf16[64,2048]{1,0:T(8,128)(2,1)S(1)}, u32[]{:S(2)}, u32[]{:S(2)}) collective-permute-start(bf16[64,2048]{1,0:T(8,128)(2,1)S(1)} %get-tuple-element.191.refs_2_), channel_id=1, source_target_pairs={{0,1},{1,0},{2,3},{3,2},{4,5},{5,4},{6,7},{7,6},{8,9},{9,8},{10,11... | collective-permute-start | bytes 786440 | tf_op jit(solution)/shard_map/ppermute | solution.py:22
  70.5 4.8 %collective-permute-start.28 = (bf16[32,1024]{1,0:T(8,128)(2,1)S(1)}, bf16[32,1024]{1,0:T(8,128)(2,1)S(1)}, u32[]{:S(2)}, u32[]{:S(2)}) collective-permute-start(bf16[32,1024]{1,0:T(8,128)(2,1)S(1)} %get-tuple-element.179), channel_id=1, source_target_pairs={{0,2},{2,0},{4,6},{6,4},{1,3},{3,1},{5,7},{7,5},{8,10},{10,8},{12,... | collective-permute-start | bytes 196616 | tf_op jit(solution)/shard_map/ppermute | solution.py:31
  71.8 4.5 %collective-permute-start.29 = (bf16[32,1024]{1,0:T(8,128)(2,1)S(1)}, bf16[32,1024]{1,0:T(8,128)(2,1)S(1)}, u32[]{:S(2)}, u32[]{:S(2)}) collective-permute-start(bf16[32,1024]{1,0:T(8,128)(2,1)S(1)} %get-tuple-element.180), channel_id=1, source_target_pairs={{0,4},{2,6},{4,0},{6,2},{1,5},{3,7},{5,1},{7,3},{8,12},{10,14},{12... | collective-permute-start | bytes 196616 | tf_op jit(solution)/shard_map/ppermute | solution.py:31
  73.0 5.5 %collective-permute-start.30 = (bf16[32,1024]{1,0:T(8,128)(2,1)S(1)}, bf16[32,1024]{1,0:T(8,128)(2,1)S(1)}, u32[]{:S(2)}, u32[]{:S(2)}) collective-permute-start(bf16[32,1024]{1,0:T(8,128)(2,1)S(1)} %get-tuple-element.181), channel_id=1, source_target_pairs={{0,6},{2,4},{4,2},{6,0},{1,7},{3,5},{5,3},{7,1},{8,14},{10,12},{12... | collective-permute-start | bytes 196616 | tf_op jit(solution)/shard_map/ppermute | solution.py:31
  78.5 5.9 %collective-permute-start.33 = (bf16[32,1024]{1,0:T(8,128)(2,1)S(1)}, bf16[32,1024]{1,0:T(8,128)(2,1)S(1)}, u32[]{:S(2)}, u32[]{:S(2)}) collective-permute-start(bf16[32,1024]{1,0:T(8,128)(2,1)S(1)} %leave_back.2.refs_5_), channel_id=1, source_target_pairs={{8,0},{16,8},{24,16},{9,1},{17,9},{25,17},{10,2},{18,10},{26,18},{... | collective-permute-start | bytes 196616 | tf_op jit(solution)/shard_map/ppermute | solution.py:17
  84.4 5.4 %collective-permute-start.37 = (bf16[32,1024]{1,0:T(8,128)(2,1)S(1)}, bf16[32,1024]{1,0:T(8,128)(2,1)S(1)}, u32[]{:S(2)}, u32[]{:S(2)}) collective-permute-start(bf16[32,1024]{1,0:T(8,128)(2,1)S(1)} %arrive.6.refs_2_.first), channel_id=1, source_target_pairs={{0,6},{2,4},{4,2},{6,0},{1,7},{3,5},{5,3},{7,1},{8,14},{10,12},{12... | collective-permute-start | bytes 196616 | tf_op jit(solution)/shard_map/ppermute | solution.py:31
  86.0 7.1 %collective-permute-start.36 = (bf16[32,1024]{1,0:T(8,128)(2,1)S(1)}, bf16[32,1024]{1,0:T(8,128)(2,1)S(1)}, u32[]{:S(2)}, u32[]{:S(2)}) collective-permute-start(bf16[32,1024]{1,0:T(8,128)(2,1)S(1)} %arrive.6.refs_2_.first), channel_id=1, source_target_pairs={{0,4},{2,6},{4,0},{6,2},{1,5},{3,7},{5,1},{7,3},{8,12},{10,14},{12... | collective-permute-start | bytes 196616 | tf_op jit(solution)/shard_map/ppermute | solution.py:31
  88.0 10.1 %collective-permute-start.32 = (bf16[32,1024]{1,0:T(8,128)(2,1)S(1)}, bf16[32,1024]{1,0:T(8,128)(2,1)S(1)}, u32[]{:S(2)}, u32[]{:S(2)}) collective-permute-start(bf16[32,1024]{1,0:T(8,128)(2,1)S(1)} %get-tuple-element.199), channel_id=1, source_target_pairs={{0,4},{2,6},{4,0},{6,2},{1,5},{3,7},{5,1},{7,3},{8,12},{10,14},{12... | collective-permute-start | bytes 196616 | tf_op jit(solution)/shard_map/ppermute | solution.py:31
  88.3 9.8 %collective-permute-start.31 = (bf16[32,1024]{1,0:T(8,128)(2,1)S(1)}, bf16[32,1024]{1,0:T(8,128)(2,1)S(1)}, u32[]{:S(2)}, u32[]{:S(2)}) collective-permute-start(bf16[32,1024]{1,0:T(8,128)(2,1)S(1)} %get-tuple-element.197), channel_id=1, source_target_pairs={{0,2},{2,0},{4,6},{6,4},{1,3},{3,1},{5,7},{7,5},{8,10},{10,8},{12,... | collective-permute-start | bytes 196616 | tf_op jit(solution)/shard_map/ppermute | solution.py:31
  89.6 8.6 %collective-permute-start.34 = (bf16[32,1024]{1,0:T(8,128)(2,1)S(1)}, bf16[32,1024]{1,0:T(8,128)(2,1)S(1)}, u32[]{:S(2)}, u32[]{:S(2)}) collective-permute-start(bf16[32,1024]{1,0:T(8,128)(2,1)S(1)} %arrive.6.refs_2_.first), channel_id=1, source_target_pairs={{0,2},{2,0},{4,6},{6,4},{1,3},{3,1},{5,7},{7,5},{8,10},{10,8},{12,... | collective-permute-start | bytes 196616 | tf_op jit(solution)/shard_map/ppermute | solution.py:31
  93.9 5.5 %collective-permute-start.38 = (bf16[64,2048]{1,0:T(8,128)(2,1)S(1)}, bf16[64,2048]{1,0:T(8,128)(2,1)S(1)}, u32[]{:S(2)}, u32[]{:S(2)}) collective-permute-start(bf16[64,2048]{1,0:T(8,128)(2,1)S(1)} %get-tuple-element.208.refs_0_), channel_id=1, source_target_pairs={{0,1},{1,0},{2,3},{3,2},{4,5},{5,4},{6,7},{7,6},{8,9},{9,8},{10,11... | collective-permute-start | bytes 786440 | tf_op jit(solution)/shard_map/ppermute | solution.py:22
  99.0 3.4 %collective-permute-start.35 = (bf16[64,2048]{1,0:T(8,128)(2,1)S(1)}, bf16[64,2048]{1,0:T(8,128)(2,1)S(1)}, u32[]{:S(2)}, u32[]{:S(2)}) collective-permute-start(bf16[64,2048]{1,0:T(8,128)(2,1)S(1)} %get-tuple-element.203.refs_0_), channel_id=1, source_target_pairs={{0,1},{1,0},{2,3},{3,2},{4,5},{5,4},{6,7},{7,6},{8,9},{9,8},{10,11... | collective-permute-start | bytes 786440 | tf_op jit(solution)/shard_map/ppermute | solution.py:22
  100.3 7.5 %collective-permute-start.40 = (bf16[32,1024]{1,0:T(8,128)(2,1)S(1)}, bf16[32,1024]{1,0:T(8,128)(2,1)S(1)}, u32[]{:S(2)}, u32[]{:S(2)}) collective-permute-start(bf16[32,1024]{1,0:T(8,128)(2,1)S(1)} %get-tuple-element.209), channel_id=1, source_target_pairs={{0,4},{2,6},{4,0},{6,2},{1,5},{3,7},{5,1},{7,3},{8,12},{10,14},{12... | collective-permute-start | bytes 196616 | tf_op jit(solution)/shard_map/ppermute | solution.py:31
  100.9 6.9 %collective-permute-start.41 = (bf16[32,1024]{1,0:T(8,128)(2,1)S(1)}, bf16[32,1024]{1,0:T(8,128)(2,1)S(1)}, u32[]{:S(2)}, u32[]{:S(2)}) collective-permute-start(bf16[32,1024]{1,0:T(8,128)(2,1)S(1)} %get-tuple-element.210), channel_id=1, source_target_pairs={{0,6},{2,4},{4,2},{6,0},{1,7},{3,5},{5,3},{7,1},{8,14},{10,12},{12... | collective-permute-start | bytes 196616 | tf_op jit(solution)/shard_map/ppermute | solution.py:31
  103.2 5.9 %collective-permute-start.39 = (bf16[32,1024]{1,0:T(8,128)(2,1)S(1)}, bf16[32,1024]{1,0:T(8,128)(2,1)S(1)}, u32[]{:S(2)}, u32[]{:S(2)}) collective-permute-start(bf16[32,1024]{1,0:T(8,128)(2,1)S(1)} %get-tuple-element.207), channel_id=1, source_target_pairs={{0,2},{2,0},{4,6},{6,4},{1,3},{3,1},{5,7},{7,5},{8,10},{10,8},{12,... | collective-permute-start | bytes 196616 | tf_op jit(solution)/shard_map/ppermute | solution.py:31
  109.2 5.9 %collective-permute-start.43 = (bf16[32,1024]{1,0:T(8,128)(2,1)S(1)}, bf16[32,1024]{1,0:T(8,128)(2,1)S(1)}, u32[]{:S(2)}, u32[]{:S(2)}) collective-permute-start(bf16[32,1024]{1,0:T(8,128)(2,1)S(1)} %leave_back.3.refs_4_), channel_id=1, source_target_pairs={{8,0},{16,8},{24,16},{9,1},{17,9},{25,17},{10,2},{18,10},{26,18},{... | collective-permute-start | bytes 196616 | tf_op jit(solution)/shard_map/ppermute | solution.py:17
  111.4 7.4 %collective-permute-start.42 = (bf16[32,1024]{1,0:T(8,128)(2,1)S(1)}, bf16[32,1024]{1,0:T(8,128)(2,1)S(1)}, u32[]{:S(2)}, u32[]{:S(2)}) collective-permute-start(bf16[32,1024]{1,0:T(8,128)(2,1)S(1)} %get-tuple-element.216), channel_id=1, source_target_pairs={{0,6},{2,4},{4,2},{6,0},{1,7},{3,5},{5,3},{7,1},{8,14},{10,12},{12... | collective-permute-start | bytes 196616 | tf_op jit(solution)/shard_map/ppermute | solution.py:31
  115.1 5.0 %collective-permute-start.47 = (bf16[32,1024]{1,0:T(8,128)(2,1)S(1)}, bf16[32,1024]{1,0:T(8,128)(2,1)S(1)}, u32[]{:S(2)}, u32[]{:S(2)}) collective-permute-start(bf16[32,1024]{1,0:T(8,128)(2,1)S(1)} %arrive.7.refs_0_.first), channel_id=1, source_target_pairs={{0,6},{2,4},{4,2},{6,0},{1,7},{3,5},{5,3},{7,1},{8,14},{10,12},{12... | collective-permute-start | bytes 196616 | tf_op jit(solution)/shard_map/ppermute | solution.py:31
  117.0 6.3 %collective-permute-start.46 = (bf16[32,1024]{1,0:T(8,128)(2,1)S(1)}, bf16[32,1024]{1,0:T(8,128)(2,1)S(1)}, u32[]{:S(2)}, u32[]{:S(2)}) collective-permute-start(bf16[32,1024]{1,0:T(8,128)(2,1)S(1)} %arrive.7.refs_0_.first), channel_id=1, source_target_pairs={{0,4},{2,6},{4,0},{6,2},{1,5},{3,7},{5,1},{7,3},{8,12},{10,14},{12... | collective-permute-start | bytes 196616 | tf_op jit(solution)/shard_map/ppermute | solution.py:31
  117.0 6.3 %collective-permute-start.44 = (bf16[32,1024]{1,0:T(8,128)(2,1)S(1)}, bf16[32,1024]{1,0:T(8,128)(2,1)S(1)}, u32[]{:S(2)}, u32[]{:S(2)}) collective-permute-start(bf16[32,1024]{1,0:T(8,128)(2,1)S(1)} %arrive.7.refs_0_.first), channel_id=1, source_target_pairs={{0,2},{2,0},{4,6},{6,4},{1,3},{3,1},{5,7},{7,5},{8,10},{10,8},{12,... | collective-permute-start | bytes 196616 | tf_op jit(solution)/shard_map/ppermute | solution.py:31
  124.1 4.9 %collective-permute-start.45 = (bf16[64,2048]{1,0:T(8,128)(2,1)S(1)}, bf16[64,2048]{1,0:T(8,128)(2,1)S(1)}, u32[]{:S(2)}, u32[]{:S(2)}) collective-permute-start(bf16[64,2048]{1,0:T(8,128)(2,1)S(1)} %get-tuple-element.220.refs_0_), channel_id=1, source_target_pairs={{0,1},{1,0},{2,3},{3,2},{4,5},{5,4},{6,7},{7,6},{8,9},{9,8},{10,11... | collective-permute-start | bytes 786440 | tf_op jit(solution)/shard_map/ppermute | solution.py:22
  126.8 3.3 %collective-permute-start.48 = (bf16[64,2048]{1,0:T(8,128)(2,1)S(1)}, bf16[64,2048]{1,0:T(8,128)(2,1)S(1)}, u32[]{:S(2)}, u32[]{:S(2)}) collective-permute-start(bf16[64,2048]{1,0:T(8,128)(2,1)S(1)} %get-tuple-element.232.refs_0_), channel_id=1, source_target_pairs={{0,1},{1,0},{2,3},{3,2},{4,5},{5,4},{6,7},{7,6},{8,9},{9,8},{10,11... | collective-permute-start | bytes 786440 | tf_op jit(solution)/shard_map/ppermute | solution.py:22
  129.8 8.8 %collective-permute-start.49 = (bf16[32,1024]{1,0:T(8,128)(2,1)S(1)}, bf16[32,1024]{1,0:T(8,128)(2,1)S(1)}, u32[]{:S(2)}, u32[]{:S(2)}) collective-permute-start(bf16[32,1024]{1,0:T(8,128)(2,1)S(1)} %get-tuple-element.222), channel_id=1, source_target_pairs={{0,2},{2,0},{4,6},{6,4},{1,3},{3,1},{5,7},{7,5},{8,10},{10,8},{12,... | collective-permute-start | bytes 196616 | tf_op jit(solution)/shard_map/ppermute | solution.py:31
  130.9 7.8 %collective-permute-start.50 = (bf16[32,1024]{1,0:T(8,128)(2,1)S(1)}, bf16[32,1024]{1,0:T(8,128)(2,1)S(1)}, u32[]{:S(2)}, u32[]{:S(2)}) collective-permute-start(bf16[32,1024]{1,0:T(8,128)(2,1)S(1)} %get-tuple-element.236), channel_id=1, source_target_pairs={{0,4},{2,6},{4,0},{6,2},{1,5},{3,7},{5,1},{7,3},{8,12},{10,14},{12... | collective-permute-start | bytes 196616 | tf_op jit(solution)/shard_map/ppermute | solution.py:31
  132.8 5.8 %collective-permute-start.51 = (bf16[32,1024]{1,0:T(8,128)(2,1)S(1)}, bf16[32,1024]{1,0:T(8,128)(2,1)S(1)}, u32[]{:S(2)}, u32[]{:S(2)}) collective-permute-start(bf16[32,1024]{1,0:T(8,128)(2,1)S(1)} %get-tuple-element.237), channel_id=1, source_target_pairs={{0,6},{2,4},{4,2},{6,0},{1,7},{3,5},{5,3},{7,1},{8,14},{10,12},{12... | collective-permute-start | bytes 196616 | tf_op jit(solution)/shard_map/ppermute | solution.py:31

commit v13 on v11

--- a/solution.py
+++ b/solution.py
@@ -318,67 +318,82 @@
         put_rows(pieces, n, total)
 
 
-def weight_grad(start, lefts, rights, out, left, right, room, sems):
-    count, depth = len(lefts), rights[0].shape[0]
-    for t in range(count):
-        left[:, t * depth : (t + 1) * depth] = lefts[t][...]
-        place = 0
-        for block in rights[t * len(rights) // count : (t + 1) * len(rights) // count]:
-            right[t * depth : (t + 1) * depth, place : place + block.shape[1]] = block[...]
-            place += block.shape[1]
-    copies = []
-    for i, m in enumerate(columns(left.shape[0])):
-        for n in columns(out.shape[1]):
-            room[m, n] = matmul(left[m, :], right[:, n]).astype(BF)
-        size = m.stop - m.start
-        copies.append(
-            pltpu.make_async_copy(room.at[pl.ds(m.start, size)], out.at[pl.ds(start + m.start, size)], sems.at[i])
-        )
-        copies[-1].start()
-    return copies
-
-
-def weight_grads(cuts, begun, *refs):
-    ins, refs = refs[: sum(left + right for _, left, right in cuts)], refs[sum(left + right for _, left, right in cuts) + begun :]
-    outs, rooms = refs[: len(cuts)], refs[len(cuts) :]
-    copies, place = [], 0
-    for k, (start, left, right) in enumerate(cuts):
-        lefts, rights = ins[place : place + left], ins[place + left : place + left + right]
-        copies += weight_grad(start, lefts, rights, outs[k], *rooms[4 * k : 4 * k + 4])
-        place += left + right
+def grad_begun(row_parts, col_parts, *refs):
+    *blocks, total, left, right = refs
+    depth = blocks[0].shape[1]
+    count = left.shape[1] // depth
+    lefts, rights = blocks[: row_parts * count], blocks[row_parts * count :]
+    for i, block in enumerate(lefts):
+        size, part, t = block.shape[0], i // count, i % count
+        left[part * size : (part + 1) * size, t * depth : (t + 1) * depth] = block[...]
+    for i, block in enumerate(rights):
+        size, t, part = block.shape[1], i // col_parts, i % col_parts
+        right[t * depth : (t + 1) * depth, part * size : (part + 1) * size] = block[...]
+    for m in columns(total.shape[0]):
+        for n in columns(total.shape[1]):
+            total[m, n] = matmul(left[m, :], right[:, n])
+
+
+def begin_grad(lefts, rights):
+    ins = [block for part in lefts for block in part] + [block for tick in rights for block in tick]
+    rows = sum(part[0].shape[0] for part in lefts)
+    width = sum(block.shape[1] for block in rights[0])
+    depth = lefts[0][0].shape[1] * len(rights)
+    return run(
+        functools.partial(grad_begun, len(lefts), len(rights[0])),
+        [jax.ShapeDtypeStruct((rows, width), F32)], *ins,
+        flops=2 * rows * width * depth, name="grad_begun",
+        scratch=[pltpu.VMEM((rows, depth), BF), pltpu.VMEM((depth, width), BF)],
+    )[0]
+
+
+def grads_ended(cuts, *refs):
+    place, copies = 0, []
+    ends = sum(left + right + 1 for left, right in cuts)
+    outs, rooms = refs[ends : ends + len(cuts)], refs[ends + len(cuts) :]
+    for k, (left, right) in enumerate(cuts):
+        lefts, rights = refs[place : place + left], refs[place + left : place + left + right]
+        total = refs[place + left + right]
+        place += left + right + 1
+        room, sems = rooms[2 * k : 2 * k + 2]
+        row = chunk = 0
+        for block in lefts:
+            for m in columns(block.shape[0]):
+                size, col = m.stop - m.start, 0
+                here = slice(row, row + size)
+                for part in rights:
+                    for n in columns(part.shape[1]):
+                        there = slice(col + n.start, col + n.stop)
+                        room[here, there] = (total[here, there] + matmul(block[m, :], part[:, n])).astype(BF)
+                    col += part.shape[1]
+                copies.append(
+                    pltpu.make_async_copy(room.at[pl.ds(row, size)], outs[k].at[pl.ds(row, size)], sems.at[chunk])
+                )
+                copies[-1].start()
+                row, chunk = row + size, chunk + 1
     for copy in copies:
         copy.wait()
 
 
-def weight_products(jobs, begun=None):
-    cuts, ins, scratch = [], [], []
-    flops = size = 0
-    for lefts, rights, shape, start in jobs:
-        count, depth = lefts[0].shape[0], rights[0].shape[0] * len(lefts)
-        cuts.append((start, len(lefts), len(rights)))
-        ins += [*lefts, *rights]
-        scratch += [
-            pltpu.VMEM((count, depth), BF),
-            pltpu.VMEM((depth, shape[1]), BF),
-            pltpu.VMEM((count, shape[1]), BF),
-            pltpu.SemaphoreType.DMA((len(columns(count)),)),
-        ]
-        flops += 2 * count * shape[1] * depth
-        size += 2 * count * shape[1]
+def end_grads(jobs):
+    ins = [block for lefts, rights, total in jobs for block in (*lefts, *rights, total)]
+    shapes = [total.shape for _, _, total in jobs]
+    scratch = []
+    for shape in shapes:
+        scratch += [pltpu.VMEM(shape, BF), pltpu.SemaphoreType.DMA((len(columns(shape[0])),))]
+    size = sum(rows * width for rows, width in shapes)
     return pl.pallas_call(
-        functools.partial(weight_grads, tuple(cuts), begun is not None),
-        in_specs=vmem(len(ins)) + [pl.BlockSpec(memory_space=pl.ANY)] * (begun is not None),
+        functools.partial(grads_ended, tuple((len(lefts), len(rights)) for lefts, rights, _ in jobs)),
+        in_specs=vmem(len(ins)),
         out_specs=[pl.BlockSpec(memory_space=pl.ANY)] * len(jobs),
-        out_shape=[jax.ShapeDtypeStruct(shape, BF) for _, _, shape, _ in jobs],
+        out_shape=[jax.ShapeDtypeStruct(shape, BF) for shape in shapes],
         scratch_shapes=scratch,
-        input_output_aliases={} if begun is None else {len(ins): len(jobs) - 1},
-        compiler_params=pltpu.CompilerParams(vmem_limit_bytes=18 << 20),
-        cost_estimate=pl.CostEstimate(flops=flops, bytes_accessed=size, transcendentals=0),
-        name="weight_grads",
-    )(
-        *[pltpu.with_memory_space_constraint(x, pltpu.VMEM) for x in ins],
-        *([] if begun is None else [begun]),
-    )
+        compiler_params=pltpu.CompilerParams(vmem_limit_bytes=12 << 20),
+        cost_estimate=pl.CostEstimate(
+            flops=2 * size * jobs[0][0][0].shape[1], bytes_accessed=2 * size, transcendentals=0
+        ),
+        name="grads_ended",
+    )(*[pltpu.with_memory_space_constraint(x, pltpu.VMEM) for x in ins])
 
 
 def other_cols(partial):
@@ -386,6 +401,13 @@
     if size == 2:
         return turn(partial, "col", 1)
     return (lax.psum(partial.astype(F32), "col") - partial.astype(F32)).astype(BF)
+
+
+def swapped(parts):
+    pairs = []
+    for mine in parts:
+        pairs.append((mine, other_cols(after(mine, pairs[-1][1]) if pairs else mine)))
+    return pairs
 
 
 def silu_slope(value):
@@ -433,7 +455,7 @@
             full_cot, first_grads = products(parts, cot_pieces, down_turned)
             pieces, waited = after(pieces, first_grads), []
         full_in, partial = products(parts, pieces, up_kept, waited)
-        pre = [(mine, other_cols(mine)) for mine in partial]
+        pre = swapped(partial)
         if tick < ticks - 1:
             act, terms = through(silu_part, "down_part", parts, pre, down_kept, piece_like, rows)
             acts.append(act)
@@ -479,28 +501,27 @@
                     functools.partial(finish_forward, ticks), 2, [*seen_in, *seen_out, *out_terms], stack_like,
                     "finish_forward",
                 )
-                pieces, waited = after(pieces, section_output), []
+                begun_down = begin_grad([part[1:] for part in turned_acts], [[block] for block in after(full_grads[1:], grad_out)])
+                pieces, waited = after(pieces, (section_output, begun_down)), []
             full_grad, partial = products(parts, pieces, down_turned, waited)
         full_grads[tick] = full_grad
-        ins = [(mine, other_cols(mine), *known) for mine, known in zip(partial, pres[tick])]
-        if step == ticks - 1:
-            (half_down,) = weight_products([(turned_acts[0], full_grads, (hidden, width), 0)])
-            ins[0] = after(ins[0], half_down)
+        ins = [(*pair, *known) for pair, known in zip(swapped(partial), pres[tick])]
         grad_pre, terms = through(slope_part, "in_part", parts, ins, up_turned, piece_like, rows)
         terms_in = scatter_rows(terms)
         if step < ticks - 1:
             turn_blocks(step + 1, terms)
             terms_in[0] = after(terms_in[0], (turned_ins, turned_acts))
+            if step == ticks - 2:
+                begun_up = begin_grad([turned_ins[1:]], [*pre_grads[1:tick], grad_pre, *pre_grads[tick + 1 :]])
+                terms_in[0] = after(terms_in[0], begun_up)
             (sending,) = run(leave_back, [piece_like], grad_out, *terms_in)
             seen_grad[tick] = sending
         pre_grads[tick] = grad_pre
-    turned_ins, last_acts = after((turned_ins, turned_acts[1]), terms)
-    grad_up, grad_down = weight_products(
+    grad_up, grad_down = end_grads(
         [
-            (turned_ins, [part for grad_pre in pre_grads for part in grad_pre], (width, hidden), 0),
-            (last_acts, full_grads, (hidden, width), hidden // 2),
-        ],
-        half_down,
+            ([turned_ins[0]], grad_pre, after(begun_up, terms)),
+            ([part[0] for part in turned_acts], [full_grad], begun_down),
+        ]
     )
     terms_in[0] = after(terms_in[0], (grad_up, grad_down))
     (input_grad,) = stacked(finish, 1, [grad_out, *terms_in, *seen_grad[1:]], stack_like, "finish")

time: 136 us -> 140 us (1.029)
  starting transfers between devices: 63.2 us -> 73.4 us
  waiting for transfers between devices: 42 us -> 35.6 us
    ppermute x12, starting transfers between devices: 8.78 us -> 19.1 us  [turn(): lax.ppermute(block, axis, [(i, (i + distance) % size) for i in range(size)])]
    ppermute x36, waiting for transfers between devices: 34.7 us -> 25.7 us  [swap_rows(): lax.ppermute(block, 'row', [(i, partner(i, j, size)) for i in range(size)])]
    pallas_call x2 -> x1, Pallas kernels: 6.4 us -> 3.8 us  [end_grads(): pl.pallas_call(functools.partial(grads_ended, tuple(((len(lefts), len(rig...]
    ppermute x12, waiting for transfers between devices: 3.98 us -> 6.57 us  [turn(): lax.ppermute(block, axis, [(i, (i + distance) % size) for i in range(size)])]
    pallas_call x43 -> x45, Pallas kernels: 15.5 us -> 18 us  [run(): pl.pallas_call(kernel, in_specs=vmem(len(ins)), out_specs=vmem(len(outs))...]
where the time goes in v13:
time: 140 us
  starting transfers between devices  73.4 us (52%)
  waiting for transfers between devices  35.6 us (25%)
  Pallas kernels  29.4 us (21%)
    ppermute x36, starting transfers between devices, swap_rows(): lax.ppermute(block, 'row', [(i, partner(i, j, size)) for i in range(size)])  43.1 us
    ppermute x36, waiting for transfers between devices, swap_rows(): lax.ppermute(block, 'row', [(i, partner(i, j, size)) for i in range(size)])  25.7 us
    ppermute x12, starting transfers between devices, turn(): lax.ppermute(block, axis, [(i, (i + distance) % size) for i in range(size)])  19.1 us
    pallas_call x45, Pallas kernels, run(): pl.pallas_call(kernel, in_specs=vmem(len(ins)), out_specs=vmem(len(outs))...  18 us
    ppermute x4, starting transfers between devices, hand_over(): lax.ppermute(block, 'section', [(i - distance, i) for i in sections if i...  11.2 us
    ppermute x12, waiting for transfers between devices, turn(): lax.ppermute(block, axis, [(i, (i + distance) % size) for i in range(size)])  6.57 us
    pallas_call x1, Pallas kernels, end_grads(): pl.pallas_call(functools.partial(grads_ended, tuple(((len(lefts), len(rig...  3.8 us
    pallas_call x1, Pallas kernels, hold(): pl.pallas_call(hold_kernel, in_specs=[pl.BlockSpec(memory_space=pltpu.HBM...  3.51 us
  transfers between devices with their start and end apart: 52, of which 27 were waited for; matrix products, arithmetic and copies ran while one was open for 0% of the time, Pallas kernels for 17%

profile of v13, /device:TPU:3, one launch (start us, length us, event | category | flops | bytes accessed | tf_op | source)
XLA Modules:
  0.0 139.5 jit_solution(9640347190895697792)
XLA Ops:
  0.6 0.9 first.1
  1.5 1.4 collective-permute-start.2
  2.9 2.3 %collective-permute-start.1 = (bf16[32,1024]{1,0:T(8,128)(2,1)S(1)}, bf16[32,1024]{1,0:T(8,128)(2,1)S(1)}, u32[]{:S(2)}, u32[]{:S(2)}) collective-permute-start(bf16[32,1024]{1,0:T(8,128)(2,1)S(1)} %get-tuple-element.131.refs_0_.first), channel_id=1, source_target_pairs={{0,4},{2,6},{4,0},{6,2},{1,5},{3,7},{5,1},{7,3},{8,12},{10,14},{12... | collective-permute-start | bytes 196616 | tf_op jit(solution)/shard_map/ppermute | solution.py:31
  5.2 3.5 %hold.1 = (bf16[1024,2048]{1,0:T(8,128)(2,1)S(1)}, bf16[2048,1024]{1,0:T(8,128)(2,1)S(1)}) custom-call(bf16[1024,2048]{1,0:T(8,128)(2,1)} %bitcast.4, bf16[2048,1024]{1,0:T(8,128)(2,1)} %bitcast.5), custom_call_target="tpu_custom_call" | custom-call | bytes 16777216 | tf_op jit(solution)/shard_map/hold/pallas_call | solution.py:214
  8.7 1.5 %collective-permute-done.refs_1_ = bf16[32,1024]{1,0:T(8,128)(2,1)S(1)} collective-permute-done((bf16[32,1024]{1,0:T(8,128)(2,1)S(1)}, bf16[32,1024]{1,0:T(8,128)(2,1)S(1)}, u32[]{:S(2)}, u32[]{:S(2)}) %collective-permute-start) | collective-permute-done | bytes 65568 | tf_op jit(solution)/shard_map/ppermute | solution.py:31
  10.7 2.4 %collective-permute-start.3 = (bf16[128,1024]{1,0:T(8,128)(2,1)S(1)}, bf16[128,1024]{1,0:T(8,128)(2,1)S(1)}, u32[]{:S(2)}, u32[]{:S(2)}) collective-permute-start(bf16[128,1024]{1,0:T(8,128)(2,1)S(1)} %get-tuple-element.136.refs_0_.refs_2_), channel_id=1, source_target_pairs={{0,1},{1,0},{2,3},{3,2},{4,5},{5,4},{6,7},{7,6},{8,9},{9,8},{10,11... | collective-permute-start | bytes 786440 | tf_op jit(solution)/shard_map/ppermute | solution.py:22
  13.5 0.7 collective-permute-done.3.refs_1_.refs_3_
  16.2 1.6 %collective-permute-start.5 = (bf16[32,1024]{1,0:T(8,128)(2,1)S(1)}, bf16[32,1024]{1,0:T(8,128)(2,1)S(1)}, u32[]{:S(2)}, u32[]{:S(2)}) collective-permute-start(bf16[32,1024]{1,0:T(8,128)(2,1)S(1)} %get-tuple-element.141), channel_id=1, source_target_pairs={{0,6},{2,4},{4,2},{6,0},{1,7},{3,5},{5,3},{7,1},{8,14},{10,12},{12... | collective-permute-start | bytes 196616 | tf_op jit(solution)/shard_map/ppermute | solution.py:31
  17.8 2.0 %collective-permute-start.7 = (bf16[32,1024]{1,0:T(8,128)(2,1)S(1)}, bf16[32,1024]{1,0:T(8,128)(2,1)S(1)}, u32[]{:S(2)}, u32[]{:S(2)}) collective-permute-start(bf16[32,1024]{1,0:T(8,128)(2,1)S(1)} %get-tuple-element.143), channel_id=1, source_target_pairs={{0,2},{2,0},{4,6},{6,4},{1,3},{3,1},{5,7},{7,5},{8,10},{10,8},{12,... | collective-permute-start | bytes 196616 | tf_op jit(solution)/shard_map/ppermute | solution.py:31
  19.8 1.2 turned_weight.2.refs_4_.weight.refs_6_
  21.1 1.7 %fetch.1 = (bf16[32,1024]{1,0:T(8,128)(2,1)S(1)}, bf16[32,1024]{1,0:T(8,128)(2,1)S(1)}, bf16[32,1024]{1,0:T(8,128)(2,1)S(1)}, bf16[32,1024]{1,0:T(8,128)(2,1)S(1...) custom-call(s32[6]{0:T(128)S(1)} %copy-done, bf16[1,3,32,1024]{3,2,1,0:T(8,128)(2,1)} %inputs.3, ...), custom_call_target="tpu_custom_call" | custom-call | bytes 2097152 | tf_op jit(solution)/shard_map/fetch/pallas_call | solution.py:109
  22.8 2.1 %collective-permute-done.6.refs_2_ = bf16[32,1024]{1,0:T(8,128)(2,1)S(1)} collective-permute-done((bf16[32,1024]{1,0:T(8,128)(2,1)S(1)}, bf16[32,1024]{1,0:T(8,128)(2,1)S(1)}, u32[]{:S(2)}, u32[]{:S(2)}) %collective-permute-start.6) | collective-permute-done | bytes 65568 | tf_op jit(solution)/shard_map/ppermute | solution.py:31
  25.0 3.1 %collective-permute-start.8 = (bf16[32,1024]{1,0:T(8,128)(2,1)S(1)}, bf16[32,1024]{1,0:T(8,128)(2,1)S(1)}, u32[]{:S(2)}, u32[]{:S(2)}) collective-permute-start(bf16[32,1024]{1,0:T(8,128)(2,1)S(1)} %get-tuple-element.150), channel_id=1, source_target_pairs={{0,8},{8,16},{16,24},{1,9},{9,17},{17,25},{2,10},{10,18},{18,26},{... | collective-permute-start | bytes 196616 | tf_op jit(solution)/shard_map/ppermute | solution.py:17
  28.2 2.0 %collective-permute-start.9 = (bf16[32,1024]{1,0:T(8,128)(2,1)S(1)}, bf16[32,1024]{1,0:T(8,128)(2,1)S(1)}, u32[]{:S(2)}, u32[]{:S(2)}) collective-permute-start(bf16[32,1024]{1,0:T(8,128)(2,1)S(1)} %get-tuple-element.172.refs_0_.first), channel_id=1, source_target_pairs={{0,2},{2,0},{4,6},{6,4},{1,3},{3,1},{5,7},{7,5},{8,10},{10,8},{12,... | collective-permute-start | bytes 196616 | tf_op jit(solution)/shard_map/ppermute | solution.py:31
  30.3 1.8 %collective-permute-start.12 = (bf16[32,1024]{1,0:T(8,128)(2,1)S(1)}, bf16[32,1024]{1,0:T(8,128)(2,1)S(1)}, u32[]{:S(2)}, u32[]{:S(2)}) collective-permute-start(bf16[32,1024]{1,0:T(8,128)(2,1)S(1)} %arrive.4.refs_2_.first.refs_1_), channel_id=1, source_target_pairs={{0,4},{2,6},{4,0},{6,2},{1,5},{3,7},{5,1},{7,3},{8,12},{10,14},{12... | collective-permute-start | bytes 196616 | tf_op jit(solution)/shard_map/ppermute | solution.py:31
  32.1 1.7 %collective-permute-start.11 = (bf16[32,1024]{1,0:T(8,128)(2,1)S(1)}, bf16[32,1024]{1,0:T(8,128)(2,1)S(1)}, u32[]{:S(2)}, u32[]{:S(2)}) collective-permute-start(bf16[32,1024]{1,0:T(8,128)(2,1)S(1)} %arrive.4.refs_2_.first.refs_1_), channel_id=1, source_target_pairs={{0,6},{2,4},{4,2},{6,0},{1,7},{3,5},{5,3},{7,1},{8,14},{10,12},{12... | collective-permute-start | bytes 196616 | tf_op jit(solution)/shard_map/ppermute | solution.py:31
  33.8 2.0 %collective-permute-done.13.refs_5_ = bf16[32,1024]{1,0:T(8,128)(2,1)S(1)} collective-permute-done((bf16[32,1024]{1,0:T(8,128)(2,1)S(1)}, bf16[32,1024]{1,0:T(8,128)(2,1)S(1)}, u32[]{:S(2)}, u32[]{:S(2)}) %collective-permute-start.13) | collective-permute-done | bytes 65568 | tf_op jit(solution)/shard_map/ppermute | solution.py:31
  35.8 1.4 %collective-permute-done.11.refs_3_ = bf16[32,1024]{1,0:T(8,128)(2,1)S(1)} collective-permute-done((bf16[32,1024]{1,0:T(8,128)(2,1)S(1)}, bf16[32,1024]{1,0:T(8,128)(2,1)S(1)}, u32[]{:S(2)}, u32[]{:S(2)}) %collective-permute-start.11) | collective-permute-done | bytes 65568 | tf_op jit(solution)/shard_map/ppermute | solution.py:31
  37.6 3.4 %collective-permute-start.14 = (bf16[128,1024]{1,0:T(8,128)(2,1)S(1)}, bf16[128,1024]{1,0:T(8,128)(2,1)S(1)}, u32[]{:S(2)}, u32[]{:S(2)}) collective-permute-start(bf16[128,1024]{1,0:T(8,128)(2,1)S(1)} %get-tuple-element.155.refs_0_.refs_2_), channel_id=1, source_target_pairs={{0,1},{1,0},{2,3},{3,2},{4,5},{5,4},{6,7},{7,6},{8,9},{9,8},{10,11... | collective-permute-start | bytes 786440 | tf_op jit(solution)/shard_map/ppermute | solution.py:22
  41.5 0.7 collective-permute-done.14.refs_1_.refs_3_
  44.2 1.5 %collective-permute-start.16 = (bf16[32,1024]{1,0:T(8,128)(2,1)S(1)}, bf16[32,1024]{1,0:T(8,128)(2,1)S(1)}, u32[]{:S(2)}, u32[]{:S(2)}) collective-permute-start(bf16[32,1024]{1,0:T(8,128)(2,1)S(1)} %get-tuple-element.159), channel_id=1, source_target_pairs={{0,6},{2,4},{4,2},{6,0},{1,7},{3,5},{5,3},{7,1},{8,14},{10,12},{12... | collective-permute-start | bytes 196616 | tf_op jit(solution)/shard_map/ppermute | solution.py:31
  45.7 2.1 %collective-permute-start.18 = (bf16[32,1024]{1,0:T(8,128)(2,1)S(1)}, bf16[32,1024]{1,0:T(8,128)(2,1)S(1)}, u32[]{:S(2)}, u32[]{:S(2)}) collective-permute-start(bf16[32,1024]{1,0:T(8,128)(2,1)S(1)} %get-tuple-element.161), channel_id=1, source_target_pairs={{0,2},{2,0},{4,6},{6,4},{1,3},{3,1},{5,7},{7,5},{8,10},{10,8},{12,... | collective-permute-start | bytes 196616 | tf_op jit(solution)/shard_map/ppermute | solution.py:31
  48.2 1.2 turned_weight.3.refs_4_
  49.5 3.4 %collective-permute-done.17.refs_2_ = bf16[32,1024]{1,0:T(8,128)(2,1)S(1)} collective-permute-done((bf16[32,1024]{1,0:T(8,128)(2,1)S(1)}, bf16[32,1024]{1,0:T(8,128)(2,1)S(1)}, u32[]{:S(2)}, u32[]{:S(2)}) %collective-permute-start.17) | collective-permute-done | bytes 65568 | tf_op jit(solution)/shard_map/ppermute | solution.py:31
  53.0 4.0 %collective-permute-start.19 = (bf16[32,1024]{1,0:T(8,128)(2,1)S(1)}, bf16[32,1024]{1,0:T(8,128)(2,1)S(1)}, u32[]{:S(2)}, u32[]{:S(2)}) collective-permute-start(bf16[32,1024]{1,0:T(8,128)(2,1)S(1)} %get-tuple-element.169), channel_id=1, source_target_pairs={{0,8},{8,16},{16,24},{1,9},{9,17},{17,25},{2,10},{10,18},{18,26},{... | collective-permute-start | bytes 196616 | tf_op jit(solution)/shard_map/ppermute | solution.py:17
  57.0 1.4 collective-permute-start.23
  58.5 2.2 %collective-permute-start.21 = (bf16[32,1024]{1,0:T(8,128)(2,1)S(1)}, bf16[32,1024]{1,0:T(8,128)(2,1)S(1)}, u32[]{:S(2)}, u32[]{:S(2)}) collective-permute-start(bf16[32,1024]{1,0:T(8,128)(2,1)S(1)} %arrive.5.refs_0_.refs_2_), channel_id=1, source_target_pairs={{0,4},{2,6},{4,0},{6,2},{1,5},{3,7},{5,1},{7,3},{8,12},{10,14},{12... | collective-permute-start | bytes 196616 | tf_op jit(solution)/shard_map/ppermute | solution.py:31
  60.7 1.3 collective-permute-start.20
  62.6 2.6 %collective-permute-start.26 = (bf16[128,1024]{1,0:T(8,128)(2,1)S(1)}, bf16[128,1024]{1,0:T(8,128)(2,1)S(1)}, u32[]{:S(2)}, u32[]{:S(2)}) collective-permute-start(bf16[128,1024]{1,0:T(8,128)(2,1)S(1)} %get-tuple-element.173.refs_0_), channel_id=1, source_target_pairs={{0,1},{1,0},{2,3},{3,2},{4,5},{5,4},{6,7},{7,6},{8,9},{9,8},{10,11... | collective-permute-start | bytes 786440 | tf_op jit(solution)/shard_map/ppermute | solution.py:22
  65.6 0.8 collective-permute-done.20.refs_1_
  66.8 2.2 %collective-permute-start.24 = (bf16[128,1024]{1,0:T(8,128)(2,1)S(1)}, bf16[128,1024]{1,0:T(8,128)(2,1)S(1)}, u32[]{:S(2)}, u32[]{:S(2)}) collective-permute-start(bf16[128,1024]{1,0:T(8,128)(2,1)S(1)} %get-tuple-element.194.refs_2_.refs_0_), channel_id=1, source_target_pairs={{0,1},{1,0},{2,3},{3,2},{4,5},{5,4},{6,7},{7,6},{8,9},{9,8},{10,11... | collective-permute-start | bytes 786440 | tf_op jit(solution)/shard_map/ppermute | solution.py:22
  72.3 1.7 %collective-permute-start.28 = (bf16[32,1024]{1,0:T(8,128)(2,1)S(1)}, bf16[32,1024]{1,0:T(8,128)(2,1)S(1)}, u32[]{:S(2)}, u32[]{:S(2)}) collective-permute-start(bf16[32,1024]{1,0:T(8,128)(2,1)S(1)} %get-tuple-element.185), channel_id=1, source_target_pairs={{0,6},{2,4},{4,2},{6,0},{1,7},{3,5},{5,3},{7,1},{8,14},{10,12},{12... | collective-permute-start | bytes 196616 | tf_op jit(solution)/shard_map/ppermute | solution.py:31
  74.4 1.5 %collective-permute-start.30 = (bf16[32,1024]{1,0:T(8,128)(2,1)S(1)}, bf16[32,1024]{1,0:T(8,128)(2,1)S(1)}, u32[]{:S(2)}, u32[]{:S(2)}) collective-permute-start(bf16[32,1024]{1,0:T(8,128)(2,1)S(1)} %get-tuple-element.187), channel_id=1, source_target_pairs={{0,2},{2,0},{4,6},{6,4},{1,3},{3,1},{5,7},{7,5},{8,10},{10,8},{12,... | collective-permute-start | bytes 196616 | tf_op jit(solution)/shard_map/ppermute | solution.py:31
  76.3 1.1 collective-permute-done.28.refs_1_
  77.5 3.8 %collective-permute-done.29.refs_2_ = bf16[32,1024]{1,0:T(8,128)(2,1)S(1)} collective-permute-done((bf16[32,1024]{1,0:T(8,128)(2,1)S(1)}, bf16[32,1024]{1,0:T(8,128)(2,1)S(1)}, u32[]{:S(2)}, u32[]{:S(2)}) %collective-permute-start.29) | collective-permute-done | bytes 65568 | tf_op jit(solution)/shard_map/ppermute | solution.py:31
  81.3 2.1 %collective-permute-start.31 = (bf16[32,1024]{1,0:T(8,128)(2,1)S(1)}, bf16[32,1024]{1,0:T(8,128)(2,1)S(1)}, u32[]{:S(2)}, u32[]{:S(2)}) collective-permute-start(bf16[32,1024]{1,0:T(8,128)(2,1)S(1)} %leave_back.2.refs_5_), channel_id=1, source_target_pairs={{8,0},{16,8},{24,16},{9,1},{17,9},{25,17},{10,2},{18,10},{26,18},{... | collective-permute-start | bytes 196616 | tf_op jit(solution)/shard_map/ppermute | solution.py:17
  83.6 0.7 down_again.1
  84.4 1.9 %collective-permute-start.33 = (bf16[32,1024]{1,0:T(8,128)(2,1)S(1)}, bf16[32,1024]{1,0:T(8,128)(2,1)S(1)}, u32[]{:S(2)}, u32[]{:S(2)}) collective-permute-start(bf16[32,1024]{1,0:T(8,128)(2,1)S(1)} %get-tuple-element.207), channel_id=1, source_target_pairs={{0,4},{2,6},{4,0},{6,2},{1,5},{3,7},{5,1},{7,3},{8,12},{10,14},{12... | collective-permute-start | bytes 196616 | tf_op jit(solution)/shard_map/ppermute | solution.py:31
  86.3 0.9 collective-permute-done.31.arrived
  87.3 2.1 %collective-permute-start.35 = (bf16[32,1024]{1,0:T(8,128)(2,1)S(1)}, bf16[32,1024]{1,0:T(8,128)(2,1)S(1)}, u32[]{:S(2)}, u32[]{:S(2)}) collective-permute-start(bf16[32,1024]{1,0:T(8,128)(2,1)S(1)} %arrive.6.refs_2_.first), channel_id=1, source_target_pairs={{0,4},{2,6},{4,0},{6,2},{1,5},{3,7},{5,1},{7,3},{8,12},{10,14},{12... | collective-permute-start | bytes 196616 | tf_op jit(solution)/shard_map/ppermute | solution.py:31
  89.4 1.4 %collective-permute-start.34 = (bf16[32,1024]{1,0:T(8,128)(2,1)S(1)}, bf16[32,1024]{1,0:T(8,128)(2,1)S(1)}, u32[]{:S(2)}, u32[]{:S(2)}) collective-permute-start(bf16[32,1024]{1,0:T(8,128)(2,1)S(1)} %arrive.6.refs_2_.first), channel_id=1, source_target_pairs={{0,6},{2,4},{4,2},{6,0},{1,7},{3,5},{5,3},{7,1},{8,14},{10,12},{12... | collective-permute-start | bytes 196616 | tf_op jit(solution)/shard_map/ppermute | solution.py:31
  91.2 0.9 collective-permute-done.35.refs_4_
  92.1 2.5 %collective-permute-done.34.refs_3_ = bf16[32,1024]{1,0:T(8,128)(2,1)S(1)} collective-permute-done((bf16[32,1024]{1,0:T(8,128)(2,1)S(1)}, bf16[32,1024]{1,0:T(8,128)(2,1)S(1)}, u32[]{:S(2)}, u32[]{:S(2)}) %collective-permute-start.34) | collective-permute-done | bytes 65568 | tf_op jit(solution)/shard_map/ppermute | solution.py:31
  95.0 3.2 %collective-permute-start.37 = (bf16[128,1024]{1,0:T(8,128)(2,1)S(1)}, bf16[128,1024]{1,0:T(8,128)(2,1)S(1)}, u32[]{:S(2)}, u32[]{:S(2)}) collective-permute-start(bf16[128,1024]{1,0:T(8,128)(2,1)S(1)} %get-tuple-element.209.refs_0_), channel_id=1, source_target_pairs={{0,1},{1,0},{2,3},{3,2},{4,5},{5,4},{6,7},{7,6},{8,9},{9,8},{10,11... | collective-permute-start | bytes 786440 | tf_op jit(solution)/shard_map/ppermute | solution.py:22
  98.7 0.7 collective-permute-done.37.refs_1_
  101.5 1.5 %collective-permute-start.39 = (bf16[32,1024]{1,0:T(8,128)(2,1)S(1)}, bf16[32,1024]{1,0:T(8,128)(2,1)S(1)}, u32[]{:S(2)}, u32[]{:S(2)}) collective-permute-start(bf16[32,1024]{1,0:T(8,128)(2,1)S(1)} %get-tuple-element.213), channel_id=1, source_target_pairs={{0,6},{2,4},{4,2},{6,0},{1,7},{3,5},{5,3},{7,1},{8,14},{10,12},{12... | collective-permute-start | bytes 196616 | tf_op jit(solution)/shard_map/ppermute | solution.py:31
  103.1 2.1 %collective-permute-start.41 = (bf16[32,1024]{1,0:T(8,128)(2,1)S(1)}, bf16[32,1024]{1,0:T(8,128)(2,1)S(1)}, u32[]{:S(2)}, u32[]{:S(2)}) collective-permute-start(bf16[32,1024]{1,0:T(8,128)(2,1)S(1)} %get-tuple-element.215), channel_id=1, source_target_pairs={{0,2},{2,0},{4,6},{6,4},{1,3},{3,1},{5,7},{7,5},{8,10},{10,8},{12,... | collective-permute-start | bytes 196616 | tf_op jit(solution)/shard_map/ppermute | solution.py:31
  105.5 1.3 grad_begun.2.refs_3_
  106.8 3.4 %collective-permute-done.40.refs_2_ = bf16[32,1024]{1,0:T(8,128)(2,1)S(1)} collective-permute-done((bf16[32,1024]{1,0:T(8,128)(2,1)S(1)}, bf16[32,1024]{1,0:T(8,128)(2,1)S(1)}, u32[]{:S(2)}, u32[]{:S(2)}) %collective-permute-start.40) | collective-permute-done | bytes 65568 | tf_op jit(solution)/shard_map/ppermute | solution.py:31
  110.3 1.9 %collective-permute-start.43 = (bf16[32,1024]{1,0:T(8,128)(2,1)S(1)}, bf16[32,1024]{1,0:T(8,128)(2,1)S(1)}, u32[]{:S(2)}, u32[]{:S(2)}) collective-permute-start(bf16[32,1024]{1,0:T(8,128)(2,1)S(1)} %leave_back.3.refs_4_), channel_id=1, source_target_pairs={{8,0},{16,8},{24,16},{9,1},{17,9},{25,17},{10,2},{18,10},{26,18},{... | collective-permute-start | bytes 196616 | tf_op jit(solution)/shard_map/ppermute | solution.py:17
  112.2 1.5 %collective-permute-start.42 = (bf16[32,1024]{1,0:T(8,128)(2,1)S(1)}, bf16[32,1024]{1,0:T(8,128)(2,1)S(1)}, u32[]{:S(2)}, u32[]{:S(2)}) collective-permute-start(bf16[32,1024]{1,0:T(8,128)(2,1)S(1)} %get-tuple-element.225), channel_id=1, source_target_pairs={{0,6},{2,4},{4,2},{6,0},{1,7},{3,5},{5,3},{7,1},{8,14},{10,12},{12... | collective-permute-start | bytes 196616 | tf_op jit(solution)/shard_map/ppermute | solution.py:31
  113.7 2.4 %collective-permute-done.43.arrived = bf16[32,1024]{1,0:T(8,128)(2,1)S(1)} collective-permute-done((bf16[32,1024]{1,0:T(8,128)(2,1)S(1)}, bf16[32,1024]{1,0:T(8,128)(2,1)S(1)}, u32[]{:S(2)}, u32[]{:S(2)}) %collective-permute-start.43) | collective-permute-done | bytes 65568 | tf_op jit(solution)/shard_map/ppermute | solution.py:17
  116.3 1.8 %collective-permute-start.45 = (bf16[32,1024]{1,0:T(8,128)(2,1)S(1)}, bf16[32,1024]{1,0:T(8,128)(2,1)S(1)}, u32[]{:S(2)}, u32[]{:S(2)}) collective-permute-start(bf16[32,1024]{1,0:T(8,128)(2,1)S(1)} %arrive.7.refs_0_.first), channel_id=1, source_target_pairs={{0,4},{2,6},{4,0},{6,2},{1,5},{3,7},{5,1},{7,3},{8,12},{10,14},{12... | collective-permute-start | bytes 196616 | tf_op jit(solution)/shard_map/ppermute | solution.py:31
  118.0 1.8 %collective-permute-start.44 = (bf16[32,1024]{1,0:T(8,128)(2,1)S(1)}, bf16[32,1024]{1,0:T(8,128)(2,1)S(1)}, u32[]{:S(2)}, u32[]{:S(2)}) collective-permute-start(bf16[32,1024]{1,0:T(8,128)(2,1)S(1)} %arrive.7.refs_0_.first), channel_id=1, source_target_pairs={{0,6},{2,4},{4,2},{6,0},{1,7},{3,5},{5,3},{7,1},{8,14},{10,12},{12... | collective-permute-start | bytes 196616 | tf_op jit(solution)/shard_map/ppermute | solution.py:31
  119.8 0.8 finish_forward.1
  120.6 1.3 grad_begun.3.refs_7_
  121.9 1.1 collective-permute-done.44.refs_1_
  123.4 3.4 %collective-permute-start.47 = (bf16[128,1024]{1,0:T(8,128)(2,1)S(1)}, bf16[128,1024]{1,0:T(8,128)(2,1)S(1)}, u32[]{:S(2)}, u32[]{:S(2)}) collective-permute-start(bf16[128,1024]{1,0:T(8,128)(2,1)S(1)} %get-tuple-element.236.refs_0_), channel_id=1, source_target_pairs={{0,1},{1,0},{2,3},{3,2},{4,5},{5,4},{6,7},{7,6},{8,9},{9,8},{10,11... | collective-permute-start | bytes 786440 | tf_op jit(solution)/shard_map/ppermute | solution.py:22
  127.3 0.7 collective-permute-done.47.refs_1_
  130.1 1.8 %collective-permute-start.49 = (bf16[32,1024]{1,0:T(8,128)(2,1)S(1)}, bf16[32,1024]{1,0:T(8,128)(2,1)S(1)}, u32[]{:S(2)}, u32[]{:S(2)}) collective-permute-start(bf16[32,1024]{1,0:T(8,128)(2,1)S(1)} %get-tuple-element.242), channel_id=1, source_target_pairs={{0,6},{2,4},{4,2},{6,0},{1,7},{3,5},{5,3},{7,1},{8,14},{10,12},{12... | collective-permute-start | bytes 196616 | tf_op jit(solution)/shard_map/ppermute | solution.py:31
  132.0 1.8 %collective-permute-start.51 = (bf16[32,1024]{1,0:T(8,128)(2,1)S(1)}, bf16[32,1024]{1,0:T(8,128)(2,1)S(1)}, u32[]{:S(2)}, u32[]{:S(2)}) collective-permute-start(bf16[32,1024]{1,0:T(8,128)(2,1)S(1)} %get-tuple-element.244), channel_id=1, source_target_pairs={{0,2},{2,0},{4,6},{6,4},{1,3},{3,1},{5,7},{7,5},{8,10},{10,8},{12,... | collective-permute-start | bytes 196616 | tf_op jit(solution)/shard_map/ppermute | solution.py:31
  133.7 3.8 %grads_ended.1 = (bf16[1024,2048]{1,0:T(8,128)(2,1)}, bf16[2048,1024]{1,0:T(8,128)(2,1)}) custom-call(bf16[1024,128]{1,0:T(8,128)(2,1)S(1)} %turned.9.refs_0_, bf16[128,1024]{1,0:T(8,128)(2,1)S(1)} %get-tuple-element.240.refs_1_, bf16[128,1024]{1,0:T(8,128)(2,1)S(1)} %get-tuple-element.241.refs_2_, f32[1024,2048]{1,0:T(8,128)S(1)} %grad_begun.2.refs_3_, ...), custom_call_target="tpu_custom_call" | custom-call | flops 1073741824 | bytes 8388608 | tf_op jit(solution)/shard_map/grads_ended/pallas_call | solution.py:385
  137.6 1.3 collective-permute-done.50.refs_2_
  138.8 0.7 finish.1
  (93 shorter events, 19.3 us)
Async XLA Ops:
  1.5 7.2 %collective-permute-start.2 = (bf16[32,1024]{1,0:T(8,128)(2,1)S(1)}, bf16[32,1024]{1,0:T(8,128)(2,1)S(1)}, u32[]{:S(2)}, u32[]{:S(2)}) collective-permute-start(bf16[32,1024]{1,0:T(8,128)(2,1)S(1)} %get-tuple-element.131.refs_0_.first), channel_id=1, source_target_pairs={{0,2},{2,0},{4,6},{6,4},{1,3},{3,1},{5,7},{7,5},{8,10},{10,8},{12,... | collective-permute-start | bytes 196616 | tf_op jit(solution)/shard_map/ppermute | solution.py:31
  2.9 5.8 %collective-permute-start.1 = (bf16[32,1024]{1,0:T(8,128)(2,1)S(1)}, bf16[32,1024]{1,0:T(8,128)(2,1)S(1)}, u32[]{:S(2)}, u32[]{:S(2)}) collective-permute-start(bf16[32,1024]{1,0:T(8,128)(2,1)S(1)} %get-tuple-element.131.refs_0_.first), channel_id=1, source_target_pairs={{0,4},{2,6},{4,0},{6,2},{1,5},{3,7},{5,1},{7,3},{8,12},{10,14},{12... | collective-permute-start | bytes 196616 | tf_op jit(solution)/shard_map/ppermute | solution.py:31
  5.2 5.0 %collective-permute-start = (bf16[32,1024]{1,0:T(8,128)(2,1)S(1)}, bf16[32,1024]{1,0:T(8,128)(2,1)S(1)}, u32[]{:S(2)}, u32[]{:S(2)}) collective-permute-start(bf16[32,1024]{1,0:T(8,128)(2,1)S(1)} %get-tuple-element.131.refs_0_.first), channel_id=1, source_target_pairs={{0,6},{2,4},{4,2},{6,0},{1,7},{3,5},{5,3},{7,1},{8,14},{10,12},{12... | collective-permute-start | bytes 196616 | tf_op jit(solution)/shard_map/ppermute | solution.py:31
  10.7 3.5 %collective-permute-start.3 = (bf16[128,1024]{1,0:T(8,128)(2,1)S(1)}, bf16[128,1024]{1,0:T(8,128)(2,1)S(1)}, u32[]{:S(2)}, u32[]{:S(2)}) collective-permute-start(bf16[128,1024]{1,0:T(8,128)(2,1)S(1)} %get-tuple-element.136.refs_0_.refs_2_), channel_id=1, source_target_pairs={{0,1},{1,0},{2,3},{3,2},{4,5},{5,4},{6,7},{7,6},{8,9},{9,8},{10,11... | collective-permute-start | bytes 786440 | tf_op jit(solution)/shard_map/ppermute | solution.py:22
  14.2 1.5 %collective-permute-start.4 = (bf16[128,1024]{1,0:T(8,128)(2,1)S(1)}, bf16[128,1024]{1,0:T(8,128)(2,1)S(1)}, u32[]{:S(2)}, u32[]{:S(2)}) collective-permute-start(bf16[128,1024]{1,0:T(8,128)(2,1)S(1)} %product_part.6.refs_0_.refs_2_), channel_id=1, source_target_pairs={{0,1},{1,0},{2,3},{3,2},{4,5},{5,4},{6,7},{7,6},{8,9},{9,8},{10,11... | collective-permute-start | bytes 786440 | tf_op jit(solution)/shard_map/ppermute | solution.py:22
  16.2 6.6 %collective-permute-start.5 = (bf16[32,1024]{1,0:T(8,128)(2,1)S(1)}, bf16[32,1024]{1,0:T(8,128)(2,1)S(1)}, u32[]{:S(2)}, u32[]{:S(2)}) collective-permute-start(bf16[32,1024]{1,0:T(8,128)(2,1)S(1)} %get-tuple-element.141), channel_id=1, source_target_pairs={{0,6},{2,4},{4,2},{6,0},{1,7},{3,5},{5,3},{7,1},{8,14},{10,12},{12... | collective-permute-start | bytes 196616 | tf_op jit(solution)/shard_map/ppermute | solution.py:31
  17.8 7.1 %collective-permute-start.6 = (bf16[32,1024]{1,0:T(8,128)(2,1)S(1)}, bf16[32,1024]{1,0:T(8,128)(2,1)S(1)}, u32[]{:S(2)}, u32[]{:S(2)}) collective-permute-start(bf16[32,1024]{1,0:T(8,128)(2,1)S(1)} %get-tuple-element.142), channel_id=1, source_target_pairs={{0,4},{2,6},{4,0},{6,2},{1,5},{3,7},{5,1},{7,3},{8,12},{10,14},{12... | collective-permute-start | bytes 196616 | tf_op jit(solution)/shard_map/ppermute | solution.py:31
  17.8 7.1 %collective-permute-start.7 = (bf16[32,1024]{1,0:T(8,128)(2,1)S(1)}, bf16[32,1024]{1,0:T(8,128)(2,1)S(1)}, u32[]{:S(2)}, u32[]{:S(2)}) collective-permute-start(bf16[32,1024]{1,0:T(8,128)(2,1)S(1)} %get-tuple-element.143), channel_id=1, source_target_pairs={{0,2},{2,0},{4,6},{6,4},{1,3},{3,1},{5,7},{7,5},{8,10},{10,8},{12,... | collective-permute-start | bytes 196616 | tf_op jit(solution)/shard_map/ppermute | solution.py:31
  19.8 1.2 copy-start
  25.0 5.2 %collective-permute-start.8 = (bf16[32,1024]{1,0:T(8,128)(2,1)S(1)}, bf16[32,1024]{1,0:T(8,128)(2,1)S(1)}, u32[]{:S(2)}, u32[]{:S(2)}) collective-permute-start(bf16[32,1024]{1,0:T(8,128)(2,1)S(1)} %get-tuple-element.150), channel_id=1, source_target_pairs={{0,8},{8,16},{16,24},{1,9},{9,17},{17,25},{2,10},{10,18},{18,26},{... | collective-permute-start | bytes 196616 | tf_op jit(solution)/shard_map/ppermute | solution.py:17
  28.1 5.7 %collective-permute-start.10 = (bf16[32,1024]{1,0:T(8,128)(2,1)S(1)}, bf16[32,1024]{1,0:T(8,128)(2,1)S(1)}, u32[]{:S(2)}, u32[]{:S(2)}) collective-permute-start(bf16[32,1024]{1,0:T(8,128)(2,1)S(1)} %get-tuple-element.172.refs_0_.first), channel_id=1, source_target_pairs={{0,4},{2,6},{4,0},{6,2},{1,5},{3,7},{5,1},{7,3},{8,12},{10,14},{12... | collective-permute-start | bytes 196616 | tf_op jit(solution)/shard_map/ppermute | solution.py:31
  28.2 5.6 %collective-permute-start.9 = (bf16[32,1024]{1,0:T(8,128)(2,1)S(1)}, bf16[32,1024]{1,0:T(8,128)(2,1)S(1)}, u32[]{:S(2)}, u32[]{:S(2)}) collective-permute-start(bf16[32,1024]{1,0:T(8,128)(2,1)S(1)} %get-tuple-element.172.refs_0_.first), channel_id=1, source_target_pairs={{0,2},{2,0},{4,6},{6,4},{1,3},{3,1},{5,7},{7,5},{8,10},{10,8},{12,... | collective-permute-start | bytes 196616 | tf_op jit(solution)/shard_map/ppermute | solution.py:31
  30.2 5.6 %collective-permute-start.13 = (bf16[32,1024]{1,0:T(8,128)(2,1)S(1)}, bf16[32,1024]{1,0:T(8,128)(2,1)S(1)}, u32[]{:S(2)}, u32[]{:S(2)}) collective-permute-start(bf16[32,1024]{1,0:T(8,128)(2,1)S(1)} %arrive.4.refs_2_.first.refs_1_), channel_id=1, source_target_pairs={{0,2},{2,0},{4,6},{6,4},{1,3},{3,1},{5,7},{7,5},{8,10},{10,8},{12,... | collective-permute-start | bytes 196616 | tf_op jit(solution)/shard_map/ppermute | solution.py:31
  30.3 5.5 %collective-permute-start.12 = (bf16[32,1024]{1,0:T(8,128)(2,1)S(1)}, bf16[32,1024]{1,0:T(8,128)(2,1)S(1)}, u32[]{:S(2)}, u32[]{:S(2)}) collective-permute-start(bf16[32,1024]{1,0:T(8,128)(2,1)S(1)} %arrive.4.refs_2_.first.refs_1_), channel_id=1, source_target_pairs={{0,4},{2,6},{4,0},{6,2},{1,5},{3,7},{5,1},{7,3},{8,12},{10,14},{12... | collective-permute-start | bytes 196616 | tf_op jit(solution)/shard_map/ppermute | solution.py:31
  32.1 5.1 %collective-permute-start.11 = (bf16[32,1024]{1,0:T(8,128)(2,1)S(1)}, bf16[32,1024]{1,0:T(8,128)(2,1)S(1)}, u32[]{:S(2)}, u32[]{:S(2)}) collective-permute-start(bf16[32,1024]{1,0:T(8,128)(2,1)S(1)} %arrive.4.refs_2_.first.refs_1_), channel_id=1, source_target_pairs={{0,6},{2,4},{4,2},{6,0},{1,7},{3,5},{5,3},{7,1},{8,14},{10,12},{12... | collective-permute-start | bytes 196616 | tf_op jit(solution)/shard_map/ppermute | solution.py:31
  37.6 4.6 %collective-permute-start.14 = (bf16[128,1024]{1,0:T(8,128)(2,1)S(1)}, bf16[128,1024]{1,0:T(8,128)(2,1)S(1)}, u32[]{:S(2)}, u32[]{:S(2)}) collective-permute-start(bf16[128,1024]{1,0:T(8,128)(2,1)S(1)} %get-tuple-element.155.refs_0_.refs_2_), channel_id=1, source_target_pairs={{0,1},{1,0},{2,3},{3,2},{4,5},{5,4},{6,7},{7,6},{8,9},{9,8},{10,11... | collective-permute-start | bytes 786440 | tf_op jit(solution)/shard_map/ppermute | solution.py:22
  42.2 1.5 %collective-permute-start.15 = (bf16[128,1024]{1,0:T(8,128)(2,1)S(1)}, bf16[128,1024]{1,0:T(8,128)(2,1)S(1)}, u32[]{:S(2)}, u32[]{:S(2)}) collective-permute-start(bf16[128,1024]{1,0:T(8,128)(2,1)S(1)} %product_part.7.refs_0_.refs_2_), channel_id=1, source_target_pairs={{0,1},{1,0},{2,3},{3,2},{4,5},{5,4},{6,7},{7,6},{8,9},{9,8},{10,11... | collective-permute-start | bytes 786440 | tf_op jit(solution)/shard_map/ppermute | solution.py:22
  44.2 5.2 %collective-permute-start.16 = (bf16[32,1024]{1,0:T(8,128)(2,1)S(1)}, bf16[32,1024]{1,0:T(8,128)(2,1)S(1)}, u32[]{:S(2)}, u32[]{:S(2)}) collective-permute-start(bf16[32,1024]{1,0:T(8,128)(2,1)S(1)} %get-tuple-element.159), channel_id=1, source_target_pairs={{0,6},{2,4},{4,2},{6,0},{1,7},{3,5},{5,3},{7,1},{8,14},{10,12},{12... | collective-permute-start | bytes 196616 | tf_op jit(solution)/shard_map/ppermute | solution.py:31
  45.7 7.2 %collective-permute-start.17 = (bf16[32,1024]{1,0:T(8,128)(2,1)S(1)}, bf16[32,1024]{1,0:T(8,128)(2,1)S(1)}, u32[]{:S(2)}, u32[]{:S(2)}) collective-permute-start(bf16[32,1024]{1,0:T(8,128)(2,1)S(1)} %get-tuple-element.160), channel_id=1, source_target_pairs={{0,4},{2,6},{4,0},{6,2},{1,5},{3,7},{5,1},{7,3},{8,12},{10,14},{12... | collective-permute-start | bytes 196616 | tf_op jit(solution)/shard_map/ppermute | solution.py:31
  45.7 7.2 %collective-permute-start.18 = (bf16[32,1024]{1,0:T(8,128)(2,1)S(1)}, bf16[32,1024]{1,0:T(8,128)(2,1)S(1)}, u32[]{:S(2)}, u32[]{:S(2)}) collective-permute-start(bf16[32,1024]{1,0:T(8,128)(2,1)S(1)} %get-tuple-element.161), channel_id=1, source_target_pairs={{0,2},{2,0},{4,6},{6,4},{1,3},{3,1},{5,7},{7,5},{8,10},{10,8},{12,... | collective-permute-start | bytes 196616 | tf_op jit(solution)/shard_map/ppermute | solution.py:31
  53.0 5.4 %collective-permute-start.19 = (bf16[32,1024]{1,0:T(8,128)(2,1)S(1)}, bf16[32,1024]{1,0:T(8,128)(2,1)S(1)}, u32[]{:S(2)}, u32[]{:S(2)}) collective-permute-start(bf16[32,1024]{1,0:T(8,128)(2,1)S(1)} %get-tuple-element.169), channel_id=1, source_target_pairs={{0,8},{8,16},{16,24},{1,9},{9,17},{17,25},{2,10},{10,18},{18,26},{... | collective-permute-start | bytes 196616 | tf_op jit(solution)/shard_map/ppermute | solution.py:17
  57.0 5.1 %collective-permute-start.23 = (bf16[32,1024]{1,0:T(8,128)(2,1)S(1)}, bf16[32,1024]{1,0:T(8,128)(2,1)S(1)}, u32[]{:S(2)}, u32[]{:S(2)}) collective-permute-start(bf16[32,1024]{1,0:T(8,128)(2,1)S(1)} %get-tuple-element.172.refs_0_.first), channel_id=1, source_target_pairs={{0,6},{2,4},{4,2},{6,0},{1,7},{3,5},{5,3},{7,1},{8,14},{10,12},{12... | collective-permute-start | bytes 196616 | tf_op jit(solution)/shard_map/ppermute | solution.py:31
  58.4 7.1 %collective-permute-start.22 = (bf16[32,1024]{1,0:T(8,128)(2,1)S(1)}, bf16[32,1024]{1,0:T(8,128)(2,1)S(1)}, u32[]{:S(2)}, u32[]{:S(2)}) collective-permute-start(bf16[32,1024]{1,0:T(8,128)(2,1)S(1)} %arrive.5.refs_0_.refs_2_), channel_id=1, source_target_pairs={{0,2},{2,0},{4,6},{6,4},{1,3},{3,1},{5,7},{7,5},{8,10},{10,8},{12,... | collective-permute-start | bytes 196616 | tf_op jit(solution)/shard_map/ppermute | solution.py:31
  58.5 7.1 %collective-permute-start.21 = (bf16[32,1024]{1,0:T(8,128)(2,1)S(1)}, bf16[32,1024]{1,0:T(8,128)(2,1)S(1)}, u32[]{:S(2)}, u32[]{:S(2)}) collective-permute-start(bf16[32,1024]{1,0:T(8,128)(2,1)S(1)} %arrive.5.refs_0_.refs_2_), channel_id=1, source_target_pairs={{0,4},{2,6},{4,0},{6,2},{1,5},{3,7},{5,1},{7,3},{8,12},{10,14},{12... | collective-permute-start | bytes 196616 | tf_op jit(solution)/shard_map/ppermute | solution.py:31
  60.7 5.7 %collective-permute-start.20 = (bf16[32,1024]{1,0:T(8,128)(2,1)S(1)}, bf16[32,1024]{1,0:T(8,128)(2,1)S(1)}, u32[]{:S(2)}, u32[]{:S(2)}) collective-permute-start(bf16[32,1024]{1,0:T(8,128)(2,1)S(1)} %arrive.5.refs_0_.refs_2_), channel_id=1, source_target_pairs={{0,6},{2,4},{4,2},{6,0},{1,7},{3,5},{5,3},{7,1},{8,14},{10,12},{12... | collective-permute-start | bytes 196616 | tf_op jit(solution)/shard_map/ppermute | solution.py:31
  62.6 6.9 %collective-permute-start.26 = (bf16[128,1024]{1,0:T(8,128)(2,1)S(1)}, bf16[128,1024]{1,0:T(8,128)(2,1)S(1)}, u32[]{:S(2)}, u32[]{:S(2)}) collective-permute-start(bf16[128,1024]{1,0:T(8,128)(2,1)S(1)} %get-tuple-element.173.refs_0_), channel_id=1, source_target_pairs={{0,1},{1,0},{2,3},{3,2},{4,5},{5,4},{6,7},{7,6},{8,9},{9,8},{10,11... | collective-permute-start | bytes 786440 | tf_op jit(solution)/shard_map/ppermute | solution.py:22
  66.8 3.4 %collective-permute-start.24 = (bf16[128,1024]{1,0:T(8,128)(2,1)S(1)}, bf16[128,1024]{1,0:T(8,128)(2,1)S(1)}, u32[]{:S(2)}, u32[]{:S(2)}) collective-permute-start(bf16[128,1024]{1,0:T(8,128)(2,1)S(1)} %get-tuple-element.194.refs_2_.refs_0_), channel_id=1, source_target_pairs={{0,1},{1,0},{2,3},{3,2},{4,5},{5,4},{6,7},{7,6},{8,9},{9,8},{10,11... | collective-permute-start | bytes 786440 | tf_op jit(solution)/shard_map/ppermute | solution.py:22
  69.5 1.7 %collective-permute-start.27 = (bf16[128,1024]{1,0:T(8,128)(2,1)S(1)}, bf16[128,1024]{1,0:T(8,128)(2,1)S(1)}, u32[]{:S(2)}, u32[]{:S(2)}) collective-permute-start(bf16[128,1024]{1,0:T(8,128)(2,1)S(1)} %product_part.8.refs_0_), channel_id=1, source_target_pairs={{0,1},{1,0},{2,3},{3,2},{4,5},{5,4},{6,7},{7,6},{8,9},{9,8},{10,11... | collective-permute-start | bytes 786440 | tf_op jit(solution)/shard_map/ppermute | solution.py:22
  70.2 1.5 %collective-permute-start.25 = (bf16[128,1024]{1,0:T(8,128)(2,1)S(1)}, bf16[128,1024]{1,0:T(8,128)(2,1)S(1)}, u32[]{:S(2)}, u32[]{:S(2)}) collective-permute-start(bf16[128,1024]{1,0:T(8,128)(2,1)S(1)} %product_part.9.refs_2_), channel_id=1, source_target_pairs={{0,1},{1,0},{2,3},{3,2},{4,5},{5,4},{6,7},{7,6},{8,9},{9,8},{10,11... | collective-permute-start | bytes 786440 | tf_op jit(solution)/shard_map/ppermute | solution.py:22
  72.3 5.1 %collective-permute-start.28 = (bf16[32,1024]{1,0:T(8,128)(2,1)S(1)}, bf16[32,1024]{1,0:T(8,128)(2,1)S(1)}, u32[]{:S(2)}, u32[]{:S(2)}) collective-permute-start(bf16[32,1024]{1,0:T(8,128)(2,1)S(1)} %get-tuple-element.185), channel_id=1, source_target_pairs={{0,6},{2,4},{4,2},{6,0},{1,7},{3,5},{5,3},{7,1},{8,14},{10,12},{12... | collective-permute-start | bytes 196616 | tf_op jit(solution)/shard_map/ppermute | solution.py:31
  74.0 7.2 %collective-permute-start.29 = (bf16[32,1024]{1,0:T(8,128)(2,1)S(1)}, bf16[32,1024]{1,0:T(8,128)(2,1)S(1)}, u32[]{:S(2)}, u32[]{:S(2)}) collective-permute-start(bf16[32,1024]{1,0:T(8,128)(2,1)S(1)} %get-tuple-element.186), channel_id=1, source_target_pairs={{0,4},{2,6},{4,0},{6,2},{1,5},{3,7},{5,1},{7,3},{8,12},{10,14},{12... | collective-permute-start | bytes 196616 | tf_op jit(solution)/shard_map/ppermute | solution.py:31
  74.4 6.8 %collective-permute-start.30 = (bf16[32,1024]{1,0:T(8,128)(2,1)S(1)}, bf16[32,1024]{1,0:T(8,128)(2,1)S(1)}, u32[]{:S(2)}, u32[]{:S(2)}) collective-permute-start(bf16[32,1024]{1,0:T(8,128)(2,1)S(1)} %get-tuple-element.187), channel_id=1, source_target_pairs={{0,2},{2,0},{4,6},{6,4},{1,3},{3,1},{5,7},{7,5},{8,10},{10,8},{12,... | collective-permute-start | bytes 196616 | tf_op jit(solution)/shard_map/ppermute | solution.py:31
  81.3 5.9 %collective-permute-start.31 = (bf16[32,1024]{1,0:T(8,128)(2,1)S(1)}, bf16[32,1024]{1,0:T(8,128)(2,1)S(1)}, u32[]{:S(2)}, u32[]{:S(2)}) collective-permute-start(bf16[32,1024]{1,0:T(8,128)(2,1)S(1)} %leave_back.2.refs_5_), channel_id=1, source_target_pairs={{8,0},{16,8},{24,16},{9,1},{17,9},{25,17},{10,2},{18,10},{26,18},{... | collective-permute-start | bytes 196616 | tf_op jit(solution)/shard_map/ppermute | solution.py:17
  84.3 6.5 %collective-permute-start.32 = (bf16[32,1024]{1,0:T(8,128)(2,1)S(1)}, bf16[32,1024]{1,0:T(8,128)(2,1)S(1)}, u32[]{:S(2)}, u32[]{:S(2)}) collective-permute-start(bf16[32,1024]{1,0:T(8,128)(2,1)S(1)} %get-tuple-element.206), channel_id=1, source_target_pairs={{0,2},{2,0},{4,6},{6,4},{1,3},{3,1},{5,7},{7,5},{8,10},{10,8},{12,... | collective-permute-start | bytes 196616 | tf_op jit(solution)/shard_map/ppermute | solution.py:31
  84.4 6.4 %collective-permute-start.33 = (bf16[32,1024]{1,0:T(8,128)(2,1)S(1)}, bf16[32,1024]{1,0:T(8,128)(2,1)S(1)}, u32[]{:S(2)}, u32[]{:S(2)}) collective-permute-start(bf16[32,1024]{1,0:T(8,128)(2,1)S(1)} %get-tuple-element.207), channel_id=1, source_target_pairs={{0,4},{2,6},{4,0},{6,2},{1,5},{3,7},{5,1},{7,3},{8,12},{10,14},{12... | collective-permute-start | bytes 196616 | tf_op jit(solution)/shard_map/ppermute | solution.py:31
  87.2 3.9 %collective-permute-start.36 = (bf16[32,1024]{1,0:T(8,128)(2,1)S(1)}, bf16[32,1024]{1,0:T(8,128)(2,1)S(1)}, u32[]{:S(2)}, u32[]{:S(2)}) collective-permute-start(bf16[32,1024]{1,0:T(8,128)(2,1)S(1)} %arrive.6.refs_2_.first), channel_id=1, source_target_pairs={{0,2},{2,0},{4,6},{6,4},{1,3},{3,1},{5,7},{7,5},{8,10},{10,8},{12,... | collective-permute-start | bytes 196616 | tf_op jit(solution)/shard_map/ppermute | solution.py:31
  87.3 4.8 %collective-permute-start.35 = (bf16[32,1024]{1,0:T(8,128)(2,1)S(1)}, bf16[32,1024]{1,0:T(8,128)(2,1)S(1)}, u32[]{:S(2)}, u32[]{:S(2)}) collective-permute-start(bf16[32,1024]{1,0:T(8,128)(2,1)S(1)} %arrive.6.refs_2_.first), channel_id=1, source_target_pairs={{0,4},{2,6},{4,0},{6,2},{1,5},{3,7},{5,1},{7,3},{8,12},{10,14},{12... | collective-permute-start | bytes 196616 | tf_op jit(solution)/shard_map/ppermute | solution.py:31
  89.4 5.2 %collective-permute-start.34 = (bf16[32,1024]{1,0:T(8,128)(2,1)S(1)}, bf16[32,1024]{1,0:T(8,128)(2,1)S(1)}, u32[]{:S(2)}, u32[]{:S(2)}) collective-permute-start(bf16[32,1024]{1,0:T(8,128)(2,1)S(1)} %arrive.6.refs_2_.first), channel_id=1, source_target_pairs={{0,6},{2,4},{4,2},{6,0},{1,7},{3,5},{5,3},{7,1},{8,14},{10,12},{12... | collective-permute-start | bytes 196616 | tf_op jit(solution)/shard_map/ppermute | solution.py:31
  95.0 4.4 %collective-permute-start.37 = (bf16[128,1024]{1,0:T(8,128)(2,1)S(1)}, bf16[128,1024]{1,0:T(8,128)(2,1)S(1)}, u32[]{:S(2)}, u32[]{:S(2)}) collective-permute-start(bf16[128,1024]{1,0:T(8,128)(2,1)S(1)} %get-tuple-element.209.refs_0_), channel_id=1, source_target_pairs={{0,1},{1,0},{2,3},{3,2},{4,5},{5,4},{6,7},{7,6},{8,9},{9,8},{10,11... | collective-permute-start | bytes 786440 | tf_op jit(solution)/shard_map/ppermute | solution.py:22
  99.4 1.5 %collective-permute-start.38 = (bf16[128,1024]{1,0:T(8,128)(2,1)S(1)}, bf16[128,1024]{1,0:T(8,128)(2,1)S(1)}, u32[]{:S(2)}, u32[]{:S(2)}) collective-permute-start(bf16[128,1024]{1,0:T(8,128)(2,1)S(1)} %product_part.10.refs_0_), channel_id=1, source_target_pairs={{0,1},{1,0},{2,3},{3,2},{4,5},{5,4},{6,7},{7,6},{8,9},{9,8},{10,11... | collective-permute-start | bytes 786440 | tf_op jit(solution)/shard_map/ppermute | solution.py:22
  101.5 5.3 %collective-permute-start.39 = (bf16[32,1024]{1,0:T(8,128)(2,1)S(1)}, bf16[32,1024]{1,0:T(8,128)(2,1)S(1)}, u32[]{:S(2)}, u32[]{:S(2)}) collective-permute-start(bf16[32,1024]{1,0:T(8,128)(2,1)S(1)} %get-tuple-element.213), channel_id=1, source_target_pairs={{0,6},{2,4},{4,2},{6,0},{1,7},{3,5},{5,3},{7,1},{8,14},{10,12},{12... | collective-permute-start | bytes 196616 | tf_op jit(solution)/shard_map/ppermute | solution.py:31
  103.1 7.1 %collective-permute-start.40 = (bf16[32,1024]{1,0:T(8,128)(2,1)S(1)}, bf16[32,1024]{1,0:T(8,128)(2,1)S(1)}, u32[]{:S(2)}, u32[]{:S(2)}) collective-permute-start(bf16[32,1024]{1,0:T(8,128)(2,1)S(1)} %get-tuple-element.214), channel_id=1, source_target_pairs={{0,4},{2,6},{4,0},{6,2},{1,5},{3,7},{5,1},{7,3},{8,12},{10,14},{12... | collective-permute-start | bytes 196616 | tf_op jit(solution)/shard_map/ppermute | solution.py:31
  103.1 7.1 %collective-permute-start.41 = (bf16[32,1024]{1,0:T(8,128)(2,1)S(1)}, bf16[32,1024]{1,0:T(8,128)(2,1)S(1)}, u32[]{:S(2)}, u32[]{:S(2)}) collective-permute-start(bf16[32,1024]{1,0:T(8,128)(2,1)S(1)} %get-tuple-element.215), channel_id=1, source_target_pairs={{0,2},{2,0},{4,6},{6,4},{1,3},{3,1},{5,7},{7,5},{8,10},{10,8},{12,... | collective-permute-start | bytes 196616 | tf_op jit(solution)/shard_map/ppermute | solution.py:31
  110.3 5.9 %collective-permute-start.43 = (bf16[32,1024]{1,0:T(8,128)(2,1)S(1)}, bf16[32,1024]{1,0:T(8,128)(2,1)S(1)}, u32[]{:S(2)}, u32[]{:S(2)}) collective-permute-start(bf16[32,1024]{1,0:T(8,128)(2,1)S(1)} %leave_back.3.refs_4_), channel_id=1, source_target_pairs={{8,0},{16,8},{24,16},{9,1},{17,9},{25,17},{10,2},{18,10},{26,18},{... | collective-permute-start | bytes 196616 | tf_op jit(solution)/shard_map/ppermute | solution.py:17
  112.2 7.6 %collective-permute-start.42 = (bf16[32,1024]{1,0:T(8,128)(2,1)S(1)}, bf16[32,1024]{1,0:T(8,128)(2,1)S(1)}, u32[]{:S(2)}, u32[]{:S(2)}) collective-permute-start(bf16[32,1024]{1,0:T(8,128)(2,1)S(1)} %get-tuple-element.225), channel_id=1, source_target_pairs={{0,6},{2,4},{4,2},{6,0},{1,7},{3,5},{5,3},{7,1},{8,14},{10,12},{12... | collective-permute-start | bytes 196616 | tf_op jit(solution)/shard_map/ppermute | solution.py:31
  116.2 5.7 %collective-permute-start.46 = (bf16[32,1024]{1,0:T(8,128)(2,1)S(1)}, bf16[32,1024]{1,0:T(8,128)(2,1)S(1)}, u32[]{:S(2)}, u32[]{:S(2)}) collective-permute-start(bf16[32,1024]{1,0:T(8,128)(2,1)S(1)} %arrive.7.refs_0_.first), channel_id=1, source_target_pairs={{0,2},{2,0},{4,6},{6,4},{1,3},{3,1},{5,7},{7,5},{8,10},{10,8},{12,... | collective-permute-start | bytes 196616 | tf_op jit(solution)/shard_map/ppermute | solution.py:31
  116.3 5.6 %collective-permute-start.45 = (bf16[32,1024]{1,0:T(8,128)(2,1)S(1)}, bf16[32,1024]{1,0:T(8,128)(2,1)S(1)}, u32[]{:S(2)}, u32[]{:S(2)}) collective-permute-start(bf16[32,1024]{1,0:T(8,128)(2,1)S(1)} %arrive.7.refs_0_.first), channel_id=1, source_target_pairs={{0,4},{2,6},{4,0},{6,2},{1,5},{3,7},{5,1},{7,3},{8,12},{10,14},{12... | collective-permute-start | bytes 196616 | tf_op jit(solution)/shard_map/ppermute | solution.py:31
  118.0 4.9 %collective-permute-start.44 = (bf16[32,1024]{1,0:T(8,128)(2,1)S(1)}, bf16[32,1024]{1,0:T(8,128)(2,1)S(1)}, u32[]{:S(2)}, u32[]{:S(2)}) collective-permute-start(bf16[32,1024]{1,0:T(8,128)(2,1)S(1)} %arrive.7.refs_0_.first), channel_id=1, source_target_pairs={{0,6},{2,4},{4,2},{6,0},{1,7},{3,5},{5,3},{7,1},{8,14},{10,12},{12... | collective-permute-start | bytes 196616 | tf_op jit(solution)/shard_map/ppermute | solution.py:31
  123.4 4.6 %collective-permute-start.47 = (bf16[128,1024]{1,0:T(8,128)(2,1)S(1)}, bf16[128,1024]{1,0:T(8,128)(2,1)S(1)}, u32[]{:S(2)}, u32[]{:S(2)}) collective-permute-start(bf16[128,1024]{1,0:T(8,128)(2,1)S(1)} %get-tuple-element.236.refs_0_), channel_id=1, source_target_pairs={{0,1},{1,0},{2,3},{3,2},{4,5},{5,4},{6,7},{7,6},{8,9},{9,8},{10,11... | collective-permute-start | bytes 786440 | tf_op jit(solution)/shard_map/ppermute | solution.py:22
  128.0 1.5 %collective-permute-start.48 = (bf16[128,1024]{1,0:T(8,128)(2,1)S(1)}, bf16[128,1024]{1,0:T(8,128)(2,1)S(1)}, u32[]{:S(2)}, u32[]{:S(2)}) collective-permute-start(bf16[128,1024]{1,0:T(8,128)(2,1)S(1)} %product_part.11.refs_0_), channel_id=1, source_target_pairs={{0,1},{1,0},{2,3},{3,2},{4,5},{5,4},{6,7},{7,6},{8,9},{9,8},{10,11... | collective-permute-start | bytes 786440 | tf_op jit(solution)/shard_map/ppermute | solution.py:22
  130.1 7.4 %collective-permute-start.49 = (bf16[32,1024]{1,0:T(8,128)(2,1)S(1)}, bf16[32,1024]{1,0:T(8,128)(2,1)S(1)}, u32[]{:S(2)}, u32[]{:S(2)}) collective-permute-start(bf16[32,1024]{1,0:T(8,128)(2,1)S(1)} %get-tuple-element.242), channel_id=1, source_target_pairs={{0,6},{2,4},{4,2},{6,0},{1,7},{3,5},{5,3},{7,1},{8,14},{10,12},{12... | collective-permute-start | bytes 196616 | tf_op jit(solution)/shard_map/ppermute | solution.py:31
  131.9 6.9 %collective-permute-start.50 = (bf16[32,1024]{1,0:T(8,128)(2,1)S(1)}, bf16[32,1024]{1,0:T(8,128)(2,1)S(1)}, u32[]{:S(2)}, u32[]{:S(2)}) collective-permute-start(bf16[32,1024]{1,0:T(8,128)(2,1)S(1)} %get-tuple-element.243), channel_id=1, source_target_pairs={{0,4},{2,6},{4,0},{6,2},{1,5},{3,7},{5,1},{7,3},{8,12},{10,14},{12... | collective-permute-start | bytes 196616 | tf_op jit(solution)/shard_map/ppermute | solution.py:31
  132.0 6.9 %collective-permute-start.51 = (bf16[32,1024]{1,0:T(8,128)(2,1)S(1)}, bf16[32,1024]{1,0:T(8,128)(2,1)S(1)}, u32[]{:S(2)}, u32[]{:S(2)}) collective-permute-start(bf16[32,1024]{1,0:T(8,128)(2,1)S(1)} %get-tuple-element.244), channel_id=1, source_target_pairs={{0,2},{2,0},{4,6},{6,4},{1,3},{3,1},{5,7},{7,5},{8,10},{10,8},{12,... | collective-permute-start | bytes 196616 | tf_op jit(solution)/shard_map/ppermute | solution.py:31

commit v14 on v13

--- a/solution.py
+++ b/solution.py
@@ -403,13 +403,6 @@
     return (lax.psum(partial.astype(F32), "col") - partial.astype(F32)).astype(BF)
 
 
-def swapped(parts):
-    pairs = []
-    for mine in parts:
-        pairs.append((mine, other_cols(after(mine, pairs[-1][1]) if pairs else mine)))
-    return pairs
-
-
 def silu_slope(value):
     sig = jax.nn.sigmoid(value)
     return sig * (1.0 + value * (1.0 - sig))
@@ -455,7 +448,7 @@
             full_cot, first_grads = products(parts, cot_pieces, down_turned)
             pieces, waited = after(pieces, first_grads), []
         full_in, partial = products(parts, pieces, up_kept, waited)
-        pre = swapped(partial)
+        pre = [(mine, other_cols(mine)) for mine in partial]
         if tick < ticks - 1:
             act, terms = through(silu_part, "down_part", parts, pre, down_kept, piece_like, rows)
             acts.append(act)
@@ -505,7 +498,7 @@
                 pieces, waited = after(pieces, (section_output, begun_down)), []
             full_grad, partial = products(parts, pieces, down_turned, waited)
         full_grads[tick] = full_grad
-        ins = [(*pair, *known) for pair, known in zip(swapped(partial), pres[tick])]
+        ins = [(mine, other_cols(mine), *known) for mine, known in zip(partial, pres[tick])]
         grad_pre, terms = through(slope_part, "in_part", parts, ins, up_turned, piece_like, rows)
         terms_in = scatter_rows(terms)
         if step < ticks - 1:

time: 140 us -> 136 us (0.971)
  starting transfers between devices: 73.4 us -> 71.6 us
  waiting for transfers between devices: 35.6 us -> 34 us
    ppermute x12, starting transfers between devices: 19.1 us -> 17.1 us  [turn(): lax.ppermute(block, axis, [(i, (i + distance) % size) for i in range(size)])]
    ppermute x12, waiting for transfers between devices: 6.57 us -> 4.9 us  [turn(): lax.ppermute(block, axis, [(i, (i + distance) % size) for i in range(size)])]
where the time goes in v14:
time: 136 us
  starting transfers between devices  71.6 us (53%)
  waiting for transfers between devices  34 us (25%)
  Pallas kernels  29.4 us (22%)
    ppermute x36, starting transfers between devices, swap_rows(): lax.ppermute(block, 'row', [(i, partner(i, j, size)) for i in range(size)])  43.4 us
    ppermute x36, waiting for transfers between devices, swap_rows(): lax.ppermute(block, 'row', [(i, partner(i, j, size)) for i in range(size)])  25.9 us
    pallas_call x45, Pallas kernels, run(): pl.pallas_call(kernel, in_specs=vmem(len(ins)), out_specs=vmem(len(outs))...  18 us
    ppermute x12, starting transfers between devices, turn(): lax.ppermute(block, axis, [(i, (i + distance) % size) for i in range(size)])  17.1 us
    ppermute x4, starting transfers between devices, hand_over(): lax.ppermute(block, 'section', [(i - distance, i) for i in sections if i...  11.2 us
    ppermute x12, waiting for transfers between devices, turn(): lax.ppermute(block, axis, [(i, (i + distance) % size) for i in range(size)])  4.9 us
    pallas_call x1, Pallas kernels, end_grads(): pl.pallas_call(functools.partial(grads_ended, tuple(((len(lefts), len(rig...  3.8 us
    pallas_call x1, Pallas kernels, hold(): pl.pallas_call(hold_kernel, in_specs=[pl.BlockSpec(memory_space=pltpu.HBM...  3.51 us
  transfers between devices with their start and end apart: 52, of which 27 were waited for; matrix products, arithmetic and copies ran while one was open for 0% of the time, Pallas kernels for 17%

profile of v14, /device:TPU:3, one launch (start us, length us, event | category | flops | bytes accessed | tf_op | source)
XLA Modules:
  0.0 136.2 jit_solution(2118740941226231974)
XLA Ops:
  0.6 0.9 first.1
  1.5 1.4 collective-permute-start.2
  2.9 2.3 %collective-permute-start.1 = (bf16[32,1024]{1,0:T(8,128)(2,1)S(1)}, bf16[32,1024]{1,0:T(8,128)(2,1)S(1)}, u32[]{:S(2)}, u32[]{:S(2)}) collective-permute-start(bf16[32,1024]{1,0:T(8,128)(2,1)S(1)} %get-tuple-element.125.refs_0_.first), channel_id=1, source_target_pairs={{0,4},{2,6},{4,0},{6,2},{1,5},{3,7},{5,1},{7,3},{8,12},{10,14},{12... | collective-permute-start | bytes 196616 | tf_op jit(solution)/shard_map/ppermute | solution.py:31
  5.2 3.5 %hold.1 = (bf16[1024,2048]{1,0:T(8,128)(2,1)S(1)}, bf16[2048,1024]{1,0:T(8,128)(2,1)S(1)}) custom-call(bf16[1024,2048]{1,0:T(8,128)(2,1)} %bitcast.4, bf16[2048,1024]{1,0:T(8,128)(2,1)} %bitcast.5), custom_call_target="tpu_custom_call" | custom-call | bytes 16777216 | tf_op jit(solution)/shard_map/hold/pallas_call | solution.py:214
  8.7 1.5 %collective-permute-done.refs_1_ = bf16[32,1024]{1,0:T(8,128)(2,1)S(1)} collective-permute-done((bf16[32,1024]{1,0:T(8,128)(2,1)S(1)}, bf16[32,1024]{1,0:T(8,128)(2,1)S(1)}, u32[]{:S(2)}, u32[]{:S(2)}) %collective-permute-start) | collective-permute-done | bytes 65568 | tf_op jit(solution)/shard_map/ppermute | solution.py:31
  10.7 2.4 %collective-permute-start.4 = (bf16[128,1024]{1,0:T(8,128)(2,1)S(1)}, bf16[128,1024]{1,0:T(8,128)(2,1)S(1)}, u32[]{:S(2)}, u32[]{:S(2)}) collective-permute-start(bf16[128,1024]{1,0:T(8,128)(2,1)S(1)} %get-tuple-element.131.refs_0_.refs_2_), channel_id=1, source_target_pairs={{0,1},{1,0},{2,3},{3,2},{4,5},{5,4},{6,7},{7,6},{8,9},{9,8},{10,11... | collective-permute-start | bytes 786440 | tf_op jit(solution)/shard_map/ppermute | solution.py:22
  15.6 1.6 %collective-permute-start.5 = (bf16[32,1024]{1,0:T(8,128)(2,1)S(1)}, bf16[32,1024]{1,0:T(8,128)(2,1)S(1)}, u32[]{:S(2)}, u32[]{:S(2)}) collective-permute-start(bf16[32,1024]{1,0:T(8,128)(2,1)S(1)} %get-tuple-element.134), channel_id=1, source_target_pairs={{0,6},{2,4},{4,2},{6,0},{1,7},{3,5},{5,3},{7,1},{8,14},{10,12},{12... | collective-permute-start | bytes 196616 | tf_op jit(solution)/shard_map/ppermute | solution.py:31
  17.1 2.0 %collective-permute-start.7 = (bf16[32,1024]{1,0:T(8,128)(2,1)S(1)}, bf16[32,1024]{1,0:T(8,128)(2,1)S(1)}, u32[]{:S(2)}, u32[]{:S(2)}) collective-permute-start(bf16[32,1024]{1,0:T(8,128)(2,1)S(1)} %get-tuple-element.136), channel_id=1, source_target_pairs={{0,2},{2,0},{4,6},{6,4},{1,3},{3,1},{5,7},{7,5},{8,10},{10,8},{12,... | collective-permute-start | bytes 196616 | tf_op jit(solution)/shard_map/ppermute | solution.py:31
  19.2 1.2 turned_weight.2.refs_4_.weight.refs_6_
  20.4 1.7 %fetch.1 = (bf16[32,1024]{1,0:T(8,128)(2,1)S(1)}, bf16[32,1024]{1,0:T(8,128)(2,1)S(1)}, bf16[32,1024]{1,0:T(8,128)(2,1)S(1)}, bf16[32,1024]{1,0:T(8,128)(2,1)S(1...) custom-call(s32[6]{0:T(128)S(1)} %copy-done, bf16[1,3,32,1024]{3,2,1,0:T(8,128)(2,1)} %inputs.3, ...), custom_call_target="tpu_custom_call" | custom-call | bytes 2097152 | tf_op jit(solution)/shard_map/fetch/pallas_call | solution.py:109
  22.2 2.1 %collective-permute-done.6.refs_2_ = bf16[32,1024]{1,0:T(8,128)(2,1)S(1)} collective-permute-done((bf16[32,1024]{1,0:T(8,128)(2,1)S(1)}, bf16[32,1024]{1,0:T(8,128)(2,1)S(1)}, u32[]{:S(2)}, u32[]{:S(2)}) %collective-permute-start.6) | collective-permute-done | bytes 65568 | tf_op jit(solution)/shard_map/ppermute | solution.py:31
  24.3 3.1 %collective-permute-start.8 = (bf16[32,1024]{1,0:T(8,128)(2,1)S(1)}, bf16[32,1024]{1,0:T(8,128)(2,1)S(1)}, u32[]{:S(2)}, u32[]{:S(2)}) collective-permute-start(bf16[32,1024]{1,0:T(8,128)(2,1)S(1)} %get-tuple-element.143), channel_id=1, source_target_pairs={{0,8},{8,16},{16,24},{1,9},{9,17},{17,25},{2,10},{10,18},{18,26},{... | collective-permute-start | bytes 196616 | tf_op jit(solution)/shard_map/ppermute | solution.py:17
  27.5 2.0 %collective-permute-start.9 = (bf16[32,1024]{1,0:T(8,128)(2,1)S(1)}, bf16[32,1024]{1,0:T(8,128)(2,1)S(1)}, u32[]{:S(2)}, u32[]{:S(2)}) collective-permute-start(bf16[32,1024]{1,0:T(8,128)(2,1)S(1)} %get-tuple-element.164.refs_0_.first), channel_id=1, source_target_pairs={{0,2},{2,0},{4,6},{6,4},{1,3},{3,1},{5,7},{7,5},{8,10},{10,8},{12,... | collective-permute-start | bytes 196616 | tf_op jit(solution)/shard_map/ppermute | solution.py:31
  29.6 1.8 %collective-permute-start.12 = (bf16[32,1024]{1,0:T(8,128)(2,1)S(1)}, bf16[32,1024]{1,0:T(8,128)(2,1)S(1)}, u32[]{:S(2)}, u32[]{:S(2)}) collective-permute-start(bf16[32,1024]{1,0:T(8,128)(2,1)S(1)} %arrive.4.refs_2_.first.refs_1_), channel_id=1, source_target_pairs={{0,4},{2,6},{4,0},{6,2},{1,5},{3,7},{5,1},{7,3},{8,12},{10,14},{12... | collective-permute-start | bytes 196616 | tf_op jit(solution)/shard_map/ppermute | solution.py:31
  31.4 1.7 %collective-permute-start.11 = (bf16[32,1024]{1,0:T(8,128)(2,1)S(1)}, bf16[32,1024]{1,0:T(8,128)(2,1)S(1)}, u32[]{:S(2)}, u32[]{:S(2)}) collective-permute-start(bf16[32,1024]{1,0:T(8,128)(2,1)S(1)} %arrive.4.refs_2_.first.refs_1_), channel_id=1, source_target_pairs={{0,6},{2,4},{4,2},{6,0},{1,7},{3,5},{5,3},{7,1},{8,14},{10,12},{12... | collective-permute-start | bytes 196616 | tf_op jit(solution)/shard_map/ppermute | solution.py:31
  33.2 2.0 %collective-permute-done.13.refs_5_ = bf16[32,1024]{1,0:T(8,128)(2,1)S(1)} collective-permute-done((bf16[32,1024]{1,0:T(8,128)(2,1)S(1)}, bf16[32,1024]{1,0:T(8,128)(2,1)S(1)}, u32[]{:S(2)}, u32[]{:S(2)}) %collective-permute-start.13) | collective-permute-done | bytes 65568 | tf_op jit(solution)/shard_map/ppermute | solution.py:31
  35.2 1.5 %collective-permute-done.11.refs_3_ = bf16[32,1024]{1,0:T(8,128)(2,1)S(1)} collective-permute-done((bf16[32,1024]{1,0:T(8,128)(2,1)S(1)}, bf16[32,1024]{1,0:T(8,128)(2,1)S(1)}, u32[]{:S(2)}, u32[]{:S(2)}) %collective-permute-start.11) | collective-permute-done | bytes 65568 | tf_op jit(solution)/shard_map/ppermute | solution.py:31
  37.1 3.2 %collective-permute-start.15 = (bf16[128,1024]{1,0:T(8,128)(2,1)S(1)}, bf16[128,1024]{1,0:T(8,128)(2,1)S(1)}, u32[]{:S(2)}, u32[]{:S(2)}) collective-permute-start(bf16[128,1024]{1,0:T(8,128)(2,1)S(1)} %get-tuple-element.148.refs_0_.refs_2_), channel_id=1, source_target_pairs={{0,1},{1,0},{2,3},{3,2},{4,5},{5,4},{6,7},{7,6},{8,9},{9,8},{10,11... | collective-permute-start | bytes 786440 | tf_op jit(solution)/shard_map/ppermute | solution.py:22
  40.8 0.6 collective-permute-done.15.refs_1_.refs_3_
  42.8 1.5 %collective-permute-start.16 = (bf16[32,1024]{1,0:T(8,128)(2,1)S(1)}, bf16[32,1024]{1,0:T(8,128)(2,1)S(1)}, u32[]{:S(2)}, u32[]{:S(2)}) collective-permute-start(bf16[32,1024]{1,0:T(8,128)(2,1)S(1)} %get-tuple-element.151), channel_id=1, source_target_pairs={{0,6},{2,4},{4,2},{6,0},{1,7},{3,5},{5,3},{7,1},{8,14},{10,12},{12... | collective-permute-start | bytes 196616 | tf_op jit(solution)/shard_map/ppermute | solution.py:31
  44.4 2.1 %collective-permute-start.18 = (bf16[32,1024]{1,0:T(8,128)(2,1)S(1)}, bf16[32,1024]{1,0:T(8,128)(2,1)S(1)}, u32[]{:S(2)}, u32[]{:S(2)}) collective-permute-start(bf16[32,1024]{1,0:T(8,128)(2,1)S(1)} %get-tuple-element.153), channel_id=1, source_target_pairs={{0,2},{2,0},{4,6},{6,4},{1,3},{3,1},{5,7},{7,5},{8,10},{10,8},{12,... | collective-permute-start | bytes 196616 | tf_op jit(solution)/shard_map/ppermute | solution.py:31
  46.8 1.2 turned_weight.3.refs_4_
  48.2 3.3 %collective-permute-done.17.refs_2_ = bf16[32,1024]{1,0:T(8,128)(2,1)S(1)} collective-permute-done((bf16[32,1024]{1,0:T(8,128)(2,1)S(1)}, bf16[32,1024]{1,0:T(8,128)(2,1)S(1)}, u32[]{:S(2)}, u32[]{:S(2)}) %collective-permute-start.17) | collective-permute-done | bytes 65568 | tf_op jit(solution)/shard_map/ppermute | solution.py:31
  51.6 4.0 %collective-permute-start.19 = (bf16[32,1024]{1,0:T(8,128)(2,1)S(1)}, bf16[32,1024]{1,0:T(8,128)(2,1)S(1)}, u32[]{:S(2)}, u32[]{:S(2)}) collective-permute-start(bf16[32,1024]{1,0:T(8,128)(2,1)S(1)} %get-tuple-element.161), channel_id=1, source_target_pairs={{0,8},{8,16},{16,24},{1,9},{9,17},{17,25},{2,10},{10,18},{18,26},{... | collective-permute-start | bytes 196616 | tf_op jit(solution)/shard_map/ppermute | solution.py:17
  55.6 1.5 %collective-permute-start.23 = (bf16[32,1024]{1,0:T(8,128)(2,1)S(1)}, bf16[32,1024]{1,0:T(8,128)(2,1)S(1)}, u32[]{:S(2)}, u32[]{:S(2)}) collective-permute-start(bf16[32,1024]{1,0:T(8,128)(2,1)S(1)} %get-tuple-element.164.refs_0_.first), channel_id=1, source_target_pairs={{0,6},{2,4},{4,2},{6,0},{1,7},{3,5},{5,3},{7,1},{8,14},{10,12},{12... | collective-permute-start | bytes 196616 | tf_op jit(solution)/shard_map/ppermute | solution.py:31
  57.3 2.1 %collective-permute-start.21 = (bf16[32,1024]{1,0:T(8,128)(2,1)S(1)}, bf16[32,1024]{1,0:T(8,128)(2,1)S(1)}, u32[]{:S(2)}, u32[]{:S(2)}) collective-permute-start(bf16[32,1024]{1,0:T(8,128)(2,1)S(1)} %arrive.5.refs_0_.refs_2_), channel_id=1, source_target_pairs={{0,4},{2,6},{4,0},{6,2},{1,5},{3,7},{5,1},{7,3},{8,12},{10,14},{12... | collective-permute-start | bytes 196616 | tf_op jit(solution)/shard_map/ppermute | solution.py:31
  59.3 1.5 %collective-permute-start.20 = (bf16[32,1024]{1,0:T(8,128)(2,1)S(1)}, bf16[32,1024]{1,0:T(8,128)(2,1)S(1)}, u32[]{:S(2)}, u32[]{:S(2)}) collective-permute-start(bf16[32,1024]{1,0:T(8,128)(2,1)S(1)} %arrive.5.refs_0_.refs_2_), channel_id=1, source_target_pairs={{0,6},{2,4},{4,2},{6,0},{1,7},{3,5},{5,3},{7,1},{8,14},{10,12},{12... | collective-permute-start | bytes 196616 | tf_op jit(solution)/shard_map/ppermute | solution.py:31
  61.7 2.4 %collective-permute-start.26 = (bf16[128,1024]{1,0:T(8,128)(2,1)S(1)}, bf16[128,1024]{1,0:T(8,128)(2,1)S(1)}, u32[]{:S(2)}, u32[]{:S(2)}) collective-permute-start(bf16[128,1024]{1,0:T(8,128)(2,1)S(1)} %product_part.8.refs_0_), channel_id=1, source_target_pairs={{0,1},{1,0},{2,3},{3,2},{4,5},{5,4},{6,7},{7,6},{8,9},{9,8},{10,11... | collective-permute-start | bytes 786440 | tf_op jit(solution)/shard_map/ppermute | solution.py:22
  64.2 0.8 collective-permute-done.20.refs_1_
  65.4 2.2 %collective-permute-start.24 = (bf16[128,1024]{1,0:T(8,128)(2,1)S(1)}, bf16[128,1024]{1,0:T(8,128)(2,1)S(1)}, u32[]{:S(2)}, u32[]{:S(2)}) collective-permute-start(bf16[128,1024]{1,0:T(8,128)(2,1)S(1)} %get-tuple-element.184.refs_2_.refs_0_), channel_id=1, source_target_pairs={{0,1},{1,0},{2,3},{3,2},{4,5},{5,4},{6,7},{7,6},{8,9},{9,8},{10,11... | collective-permute-start | bytes 786440 | tf_op jit(solution)/shard_map/ppermute | solution.py:22
  68.2 0.6 collective-permute-done.24.refs_3_.refs_1_
  70.3 1.7 %collective-permute-start.28 = (bf16[32,1024]{1,0:T(8,128)(2,1)S(1)}, bf16[32,1024]{1,0:T(8,128)(2,1)S(1)}, u32[]{:S(2)}, u32[]{:S(2)}) collective-permute-start(bf16[32,1024]{1,0:T(8,128)(2,1)S(1)} %get-tuple-element.175), channel_id=1, source_target_pairs={{0,6},{2,4},{4,2},{6,0},{1,7},{3,5},{5,3},{7,1},{8,14},{10,12},{12... | collective-permute-start | bytes 196616 | tf_op jit(solution)/shard_map/ppermute | solution.py:31
  72.4 1.5 %collective-permute-start.30 = (bf16[32,1024]{1,0:T(8,128)(2,1)S(1)}, bf16[32,1024]{1,0:T(8,128)(2,1)S(1)}, u32[]{:S(2)}, u32[]{:S(2)}) collective-permute-start(bf16[32,1024]{1,0:T(8,128)(2,1)S(1)} %get-tuple-element.177), channel_id=1, source_target_pairs={{0,2},{2,0},{4,6},{6,4},{1,3},{3,1},{5,7},{7,5},{8,10},{10,8},{12,... | collective-permute-start | bytes 196616 | tf_op jit(solution)/shard_map/ppermute | solution.py:31
  74.3 1.4 %collective-permute-done.28.refs_1_ = bf16[32,1024]{1,0:T(8,128)(2,1)S(1)} collective-permute-done((bf16[32,1024]{1,0:T(8,128)(2,1)S(1)}, bf16[32,1024]{1,0:T(8,128)(2,1)S(1)}, u32[]{:S(2)}, u32[]{:S(2)}) %collective-permute-start.28) | collective-permute-done | bytes 65568 | tf_op jit(solution)/shard_map/ppermute | solution.py:31
  75.7 3.5 %collective-permute-done.29.refs_2_ = bf16[32,1024]{1,0:T(8,128)(2,1)S(1)} collective-permute-done((bf16[32,1024]{1,0:T(8,128)(2,1)S(1)}, bf16[32,1024]{1,0:T(8,128)(2,1)S(1)}, u32[]{:S(2)}, u32[]{:S(2)}) %collective-permute-start.29) | collective-permute-done | bytes 65568 | tf_op jit(solution)/shard_map/ppermute | solution.py:31
  79.3 2.1 %collective-permute-start.31 = (bf16[32,1024]{1,0:T(8,128)(2,1)S(1)}, bf16[32,1024]{1,0:T(8,128)(2,1)S(1)}, u32[]{:S(2)}, u32[]{:S(2)}) collective-permute-start(bf16[32,1024]{1,0:T(8,128)(2,1)S(1)} %leave_back.2.refs_5_), channel_id=1, source_target_pairs={{8,0},{16,8},{24,16},{9,1},{17,9},{25,17},{10,2},{18,10},{26,18},{... | collective-permute-start | bytes 196616 | tf_op jit(solution)/shard_map/ppermute | solution.py:17
  81.6 0.7 down_again.1
  82.4 1.9 %collective-permute-start.33 = (bf16[32,1024]{1,0:T(8,128)(2,1)S(1)}, bf16[32,1024]{1,0:T(8,128)(2,1)S(1)}, u32[]{:S(2)}, u32[]{:S(2)}) collective-permute-start(bf16[32,1024]{1,0:T(8,128)(2,1)S(1)} %get-tuple-element.197), channel_id=1, source_target_pairs={{0,4},{2,6},{4,0},{6,2},{1,5},{3,7},{5,1},{7,3},{8,12},{10,14},{12... | collective-permute-start | bytes 196616 | tf_op jit(solution)/shard_map/ppermute | solution.py:31
  84.3 0.9 collective-permute-done.31.arrived
  85.3 2.1 %collective-permute-start.35 = (bf16[32,1024]{1,0:T(8,128)(2,1)S(1)}, bf16[32,1024]{1,0:T(8,128)(2,1)S(1)}, u32[]{:S(2)}, u32[]{:S(2)}) collective-permute-start(bf16[32,1024]{1,0:T(8,128)(2,1)S(1)} %arrive.6.refs_2_.first), channel_id=1, source_target_pairs={{0,4},{2,6},{4,0},{6,2},{1,5},{3,7},{5,1},{7,3},{8,12},{10,14},{12... | collective-permute-start | bytes 196616 | tf_op jit(solution)/shard_map/ppermute | solution.py:31
  87.3 1.5 %collective-permute-start.34 = (bf16[32,1024]{1,0:T(8,128)(2,1)S(1)}, bf16[32,1024]{1,0:T(8,128)(2,1)S(1)}, u32[]{:S(2)}, u32[]{:S(2)}) collective-permute-start(bf16[32,1024]{1,0:T(8,128)(2,1)S(1)} %arrive.6.refs_2_.first), channel_id=1, source_target_pairs={{0,6},{2,4},{4,2},{6,0},{1,7},{3,5},{5,3},{7,1},{8,14},{10,12},{12... | collective-permute-start | bytes 196616 | tf_op jit(solution)/shard_map/ppermute | solution.py:31
  88.9 0.9 collective-permute-done.35.refs_4_
  89.8 2.8 %collective-permute-done.34.refs_3_ = bf16[32,1024]{1,0:T(8,128)(2,1)S(1)} collective-permute-done((bf16[32,1024]{1,0:T(8,128)(2,1)S(1)}, bf16[32,1024]{1,0:T(8,128)(2,1)S(1)}, u32[]{:S(2)}, u32[]{:S(2)}) %collective-permute-start.34) | collective-permute-done | bytes 65568 | tf_op jit(solution)/shard_map/ppermute | solution.py:31
  93.0 3.0 %collective-permute-start.38 = (bf16[128,1024]{1,0:T(8,128)(2,1)S(1)}, bf16[128,1024]{1,0:T(8,128)(2,1)S(1)}, u32[]{:S(2)}, u32[]{:S(2)}) collective-permute-start(bf16[128,1024]{1,0:T(8,128)(2,1)S(1)} %get-tuple-element.199.refs_0_), channel_id=1, source_target_pairs={{0,1},{1,0},{2,3},{3,2},{4,5},{5,4},{6,7},{7,6},{8,9},{9,8},{10,11... | collective-permute-start | bytes 786440 | tf_op jit(solution)/shard_map/ppermute | solution.py:22
  96.6 0.6 collective-permute-done.38.refs_1_
  98.7 1.7 %collective-permute-start.39 = (bf16[32,1024]{1,0:T(8,128)(2,1)S(1)}, bf16[32,1024]{1,0:T(8,128)(2,1)S(1)}, u32[]{:S(2)}, u32[]{:S(2)}) collective-permute-start(bf16[32,1024]{1,0:T(8,128)(2,1)S(1)} %get-tuple-element.202), channel_id=1, source_target_pairs={{0,6},{2,4},{4,2},{6,0},{1,7},{3,5},{5,3},{7,1},{8,14},{10,12},{12... | collective-permute-start | bytes 196616 | tf_op jit(solution)/shard_map/ppermute | solution.py:31
  100.4 1.9 %collective-permute-start.41 = (bf16[32,1024]{1,0:T(8,128)(2,1)S(1)}, bf16[32,1024]{1,0:T(8,128)(2,1)S(1)}, u32[]{:S(2)}, u32[]{:S(2)}) collective-permute-start(bf16[32,1024]{1,0:T(8,128)(2,1)S(1)} %get-tuple-element.204), channel_id=1, source_target_pairs={{0,2},{2,0},{4,6},{6,4},{1,3},{3,1},{5,7},{7,5},{8,10},{10,8},{12,... | collective-permute-start | bytes 196616 | tf_op jit(solution)/shard_map/ppermute | solution.py:31
  102.7 1.3 grad_begun.2.refs_3_
  104.1 3.3 %collective-permute-done.40.refs_2_ = bf16[32,1024]{1,0:T(8,128)(2,1)S(1)} collective-permute-done((bf16[32,1024]{1,0:T(8,128)(2,1)S(1)}, bf16[32,1024]{1,0:T(8,128)(2,1)S(1)}, u32[]{:S(2)}, u32[]{:S(2)}) %collective-permute-start.40) | collective-permute-done | bytes 65568 | tf_op jit(solution)/shard_map/ppermute | solution.py:31
  107.4 1.9 %collective-permute-start.43 = (bf16[32,1024]{1,0:T(8,128)(2,1)S(1)}, bf16[32,1024]{1,0:T(8,128)(2,1)S(1)}, u32[]{:S(2)}, u32[]{:S(2)}) collective-permute-start(bf16[32,1024]{1,0:T(8,128)(2,1)S(1)} %leave_back.3.refs_4_), channel_id=1, source_target_pairs={{8,0},{16,8},{24,16},{9,1},{17,9},{25,17},{10,2},{18,10},{26,18},{... | collective-permute-start | bytes 196616 | tf_op jit(solution)/shard_map/ppermute | solution.py:17
  109.4 1.7 %collective-permute-start.42 = (bf16[32,1024]{1,0:T(8,128)(2,1)S(1)}, bf16[32,1024]{1,0:T(8,128)(2,1)S(1)}, u32[]{:S(2)}, u32[]{:S(2)}) collective-permute-start(bf16[32,1024]{1,0:T(8,128)(2,1)S(1)} %get-tuple-element.214), channel_id=1, source_target_pairs={{0,6},{2,4},{4,2},{6,0},{1,7},{3,5},{5,3},{7,1},{8,14},{10,12},{12... | collective-permute-start | bytes 196616 | tf_op jit(solution)/shard_map/ppermute | solution.py:31
  111.0 2.3 %collective-permute-done.43.arrived = bf16[32,1024]{1,0:T(8,128)(2,1)S(1)} collective-permute-done((bf16[32,1024]{1,0:T(8,128)(2,1)S(1)}, bf16[32,1024]{1,0:T(8,128)(2,1)S(1)}, u32[]{:S(2)}, u32[]{:S(2)}) %collective-permute-start.43) | collective-permute-done | bytes 65568 | tf_op jit(solution)/shard_map/ppermute | solution.py:17
  113.4 1.9 %collective-permute-start.45 = (bf16[32,1024]{1,0:T(8,128)(2,1)S(1)}, bf16[32,1024]{1,0:T(8,128)(2,1)S(1)}, u32[]{:S(2)}, u32[]{:S(2)}) collective-permute-start(bf16[32,1024]{1,0:T(8,128)(2,1)S(1)} %arrive.7.refs_0_.first), channel_id=1, source_target_pairs={{0,4},{2,6},{4,0},{6,2},{1,5},{3,7},{5,1},{7,3},{8,12},{10,14},{12... | collective-permute-start | bytes 196616 | tf_op jit(solution)/shard_map/ppermute | solution.py:31
  115.3 1.7 %collective-permute-start.44 = (bf16[32,1024]{1,0:T(8,128)(2,1)S(1)}, bf16[32,1024]{1,0:T(8,128)(2,1)S(1)}, u32[]{:S(2)}, u32[]{:S(2)}) collective-permute-start(bf16[32,1024]{1,0:T(8,128)(2,1)S(1)} %arrive.7.refs_0_.first), channel_id=1, source_target_pairs={{0,6},{2,4},{4,2},{6,0},{1,7},{3,5},{5,3},{7,1},{8,14},{10,12},{12... | collective-permute-start | bytes 196616 | tf_op jit(solution)/shard_map/ppermute | solution.py:31
  117.0 0.8 finish_forward.1
  117.7 1.3 grad_begun.3.refs_7_
  119.0 1.2 collective-permute-done.44.refs_1_
  120.7 3.4 %collective-permute-start.48 = (bf16[128,1024]{1,0:T(8,128)(2,1)S(1)}, bf16[128,1024]{1,0:T(8,128)(2,1)S(1)}, u32[]{:S(2)}, u32[]{:S(2)}) collective-permute-start(bf16[128,1024]{1,0:T(8,128)(2,1)S(1)} %get-tuple-element.225.refs_0_), channel_id=1, source_target_pairs={{0,1},{1,0},{2,3},{3,2},{4,5},{5,4},{6,7},{7,6},{8,9},{9,8},{10,11... | collective-permute-start | bytes 786440 | tf_op jit(solution)/shard_map/ppermute | solution.py:22
  124.6 0.6 collective-permute-done.48.refs_1_
  126.7 1.7 %collective-permute-start.49 = (bf16[32,1024]{1,0:T(8,128)(2,1)S(1)}, bf16[32,1024]{1,0:T(8,128)(2,1)S(1)}, u32[]{:S(2)}, u32[]{:S(2)}) collective-permute-start(bf16[32,1024]{1,0:T(8,128)(2,1)S(1)} %get-tuple-element.230), channel_id=1, source_target_pairs={{0,6},{2,4},{4,2},{6,0},{1,7},{3,5},{5,3},{7,1},{8,14},{10,12},{12... | collective-permute-start | bytes 196616 | tf_op jit(solution)/shard_map/ppermute | solution.py:31
  128.5 1.9 %collective-permute-start.51 = (bf16[32,1024]{1,0:T(8,128)(2,1)S(1)}, bf16[32,1024]{1,0:T(8,128)(2,1)S(1)}, u32[]{:S(2)}, u32[]{:S(2)}) collective-permute-start(bf16[32,1024]{1,0:T(8,128)(2,1)S(1)} %get-tuple-element.232), channel_id=1, source_target_pairs={{0,2},{2,0},{4,6},{6,4},{1,3},{3,1},{5,7},{7,5},{8,10},{10,8},{12,... | collective-permute-start | bytes 196616 | tf_op jit(solution)/shard_map/ppermute | solution.py:31
  130.4 3.8 %grads_ended.1 = (bf16[1024,2048]{1,0:T(8,128)(2,1)}, bf16[2048,1024]{1,0:T(8,128)(2,1)}) custom-call(bf16[1024,128]{1,0:T(8,128)(2,1)S(1)} %turned.9.refs_0_, bf16[128,1024]{1,0:T(8,128)(2,1)S(1)} %get-tuple-element.228.refs_1_, bf16[128,1024]{1,0:T(8,128)(2,1)S(1)} %get-tuple-element.229.refs_2_, f32[1024,2048]{1,0:T(8,128)S(1)} %grad_begun.2.refs_3_, ...), custom_call_target="tpu_custom_call" | custom-call | flops 1073741824 | bytes 8388608 | tf_op jit(solution)/shard_map/grads_ended/pallas_call | solution.py:385
  134.2 1.3 collective-permute-done.50.refs_2_
  135.4 0.7 finish.1
  (93 shorter events, 16.6 us)
Async XLA Ops:
  1.5 7.2 %collective-permute-start.2 = (bf16[32,1024]{1,0:T(8,128)(2,1)S(1)}, bf16[32,1024]{1,0:T(8,128)(2,1)S(1)}, u32[]{:S(2)}, u32[]{:S(2)}) collective-permute-start(bf16[32,1024]{1,0:T(8,128)(2,1)S(1)} %get-tuple-element.125.refs_0_.first), channel_id=1, source_target_pairs={{0,2},{2,0},{4,6},{6,4},{1,3},{3,1},{5,7},{7,5},{8,10},{10,8},{12,... | collective-permute-start | bytes 196616 | tf_op jit(solution)/shard_map/ppermute | solution.py:31
  2.9 5.8 %collective-permute-start.1 = (bf16[32,1024]{1,0:T(8,128)(2,1)S(1)}, bf16[32,1024]{1,0:T(8,128)(2,1)S(1)}, u32[]{:S(2)}, u32[]{:S(2)}) collective-permute-start(bf16[32,1024]{1,0:T(8,128)(2,1)S(1)} %get-tuple-element.125.refs_0_.first), channel_id=1, source_target_pairs={{0,4},{2,6},{4,0},{6,2},{1,5},{3,7},{5,1},{7,3},{8,12},{10,14},{12... | collective-permute-start | bytes 196616 | tf_op jit(solution)/shard_map/ppermute | solution.py:31
  5.2 5.0 %collective-permute-start = (bf16[32,1024]{1,0:T(8,128)(2,1)S(1)}, bf16[32,1024]{1,0:T(8,128)(2,1)S(1)}, u32[]{:S(2)}, u32[]{:S(2)}) collective-permute-start(bf16[32,1024]{1,0:T(8,128)(2,1)S(1)} %get-tuple-element.125.refs_0_.first), channel_id=1, source_target_pairs={{0,6},{2,4},{4,2},{6,0},{1,7},{3,5},{5,3},{7,1},{8,14},{10,12},{12... | collective-permute-start | bytes 196616 | tf_op jit(solution)/shard_map/ppermute | solution.py:31
  10.7 3.5 %collective-permute-start.4 = (bf16[128,1024]{1,0:T(8,128)(2,1)S(1)}, bf16[128,1024]{1,0:T(8,128)(2,1)S(1)}, u32[]{:S(2)}, u32[]{:S(2)}) collective-permute-start(bf16[128,1024]{1,0:T(8,128)(2,1)S(1)} %get-tuple-element.131.refs_0_.refs_2_), channel_id=1, source_target_pairs={{0,1},{1,0},{2,3},{3,2},{4,5},{5,4},{6,7},{7,6},{8,9},{9,8},{10,11... | collective-permute-start | bytes 786440 | tf_op jit(solution)/shard_map/ppermute | solution.py:22
  13.5 1.6 %collective-permute-start.3 = (bf16[128,1024]{1,0:T(8,128)(2,1)S(1)}, bf16[128,1024]{1,0:T(8,128)(2,1)S(1)}, u32[]{:S(2)}, u32[]{:S(2)}) collective-permute-start(bf16[128,1024]{1,0:T(8,128)(2,1)S(1)} %product_part.6.refs_0_.refs_2_), channel_id=1, source_target_pairs={{0,1},{1,0},{2,3},{3,2},{4,5},{5,4},{6,7},{7,6},{8,9},{9,8},{10,11... | collective-permute-start | bytes 786440 | tf_op jit(solution)/shard_map/ppermute | solution.py:22
  15.6 6.6 %collective-permute-start.5 = (bf16[32,1024]{1,0:T(8,128)(2,1)S(1)}, bf16[32,1024]{1,0:T(8,128)(2,1)S(1)}, u32[]{:S(2)}, u32[]{:S(2)}) collective-permute-start(bf16[32,1024]{1,0:T(8,128)(2,1)S(1)} %get-tuple-element.134), channel_id=1, source_target_pairs={{0,6},{2,4},{4,2},{6,0},{1,7},{3,5},{5,3},{7,1},{8,14},{10,12},{12... | collective-permute-start | bytes 196616 | tf_op jit(solution)/shard_map/ppermute | solution.py:31
  17.1 7.1 %collective-permute-start.6 = (bf16[32,1024]{1,0:T(8,128)(2,1)S(1)}, bf16[32,1024]{1,0:T(8,128)(2,1)S(1)}, u32[]{:S(2)}, u32[]{:S(2)}) collective-permute-start(bf16[32,1024]{1,0:T(8,128)(2,1)S(1)} %get-tuple-element.135), channel_id=1, source_target_pairs={{0,4},{2,6},{4,0},{6,2},{1,5},{3,7},{5,1},{7,3},{8,12},{10,14},{12... | collective-permute-start | bytes 196616 | tf_op jit(solution)/shard_map/ppermute | solution.py:31
  17.1 7.1 %collective-permute-start.7 = (bf16[32,1024]{1,0:T(8,128)(2,1)S(1)}, bf16[32,1024]{1,0:T(8,128)(2,1)S(1)}, u32[]{:S(2)}, u32[]{:S(2)}) collective-permute-start(bf16[32,1024]{1,0:T(8,128)(2,1)S(1)} %get-tuple-element.136), channel_id=1, source_target_pairs={{0,2},{2,0},{4,6},{6,4},{1,3},{3,1},{5,7},{7,5},{8,10},{10,8},{12,... | collective-permute-start | bytes 196616 | tf_op jit(solution)/shard_map/ppermute | solution.py:31
  19.2 1.2 copy-start
  24.3 5.2 %collective-permute-start.8 = (bf16[32,1024]{1,0:T(8,128)(2,1)S(1)}, bf16[32,1024]{1,0:T(8,128)(2,1)S(1)}, u32[]{:S(2)}, u32[]{:S(2)}) collective-permute-start(bf16[32,1024]{1,0:T(8,128)(2,1)S(1)} %get-tuple-element.143), channel_id=1, source_target_pairs={{0,8},{8,16},{16,24},{1,9},{9,17},{17,25},{2,10},{10,18},{18,26},{... | collective-permute-start | bytes 196616 | tf_op jit(solution)/shard_map/ppermute | solution.py:17
  27.5 5.7 %collective-permute-start.10 = (bf16[32,1024]{1,0:T(8,128)(2,1)S(1)}, bf16[32,1024]{1,0:T(8,128)(2,1)S(1)}, u32[]{:S(2)}, u32[]{:S(2)}) collective-permute-start(bf16[32,1024]{1,0:T(8,128)(2,1)S(1)} %get-tuple-element.164.refs_0_.first), channel_id=1, source_target_pairs={{0,4},{2,6},{4,0},{6,2},{1,5},{3,7},{5,1},{7,3},{8,12},{10,14},{12... | collective-permute-start | bytes 196616 | tf_op jit(solution)/shard_map/ppermute | solution.py:31
  27.5 5.6 %collective-permute-start.9 = (bf16[32,1024]{1,0:T(8,128)(2,1)S(1)}, bf16[32,1024]{1,0:T(8,128)(2,1)S(1)}, u32[]{:S(2)}, u32[]{:S(2)}) collective-permute-start(bf16[32,1024]{1,0:T(8,128)(2,1)S(1)} %get-tuple-element.164.refs_0_.first), channel_id=1, source_target_pairs={{0,2},{2,0},{4,6},{6,4},{1,3},{3,1},{5,7},{7,5},{8,10},{10,8},{12,... | collective-permute-start | bytes 196616 | tf_op jit(solution)/shard_map/ppermute | solution.py:31
  29.6 5.6 %collective-permute-start.13 = (bf16[32,1024]{1,0:T(8,128)(2,1)S(1)}, bf16[32,1024]{1,0:T(8,128)(2,1)S(1)}, u32[]{:S(2)}, u32[]{:S(2)}) collective-permute-start(bf16[32,1024]{1,0:T(8,128)(2,1)S(1)} %arrive.4.refs_2_.first.refs_1_), channel_id=1, source_target_pairs={{0,2},{2,0},{4,6},{6,4},{1,3},{3,1},{5,7},{7,5},{8,10},{10,8},{12,... | collective-permute-start | bytes 196616 | tf_op jit(solution)/shard_map/ppermute | solution.py:31
  29.6 5.5 %collective-permute-start.12 = (bf16[32,1024]{1,0:T(8,128)(2,1)S(1)}, bf16[32,1024]{1,0:T(8,128)(2,1)S(1)}, u32[]{:S(2)}, u32[]{:S(2)}) collective-permute-start(bf16[32,1024]{1,0:T(8,128)(2,1)S(1)} %arrive.4.refs_2_.first.refs_1_), channel_id=1, source_target_pairs={{0,4},{2,6},{4,0},{6,2},{1,5},{3,7},{5,1},{7,3},{8,12},{10,14},{12... | collective-permute-start | bytes 196616 | tf_op jit(solution)/shard_map/ppermute | solution.py:31
  31.4 5.2 %collective-permute-start.11 = (bf16[32,1024]{1,0:T(8,128)(2,1)S(1)}, bf16[32,1024]{1,0:T(8,128)(2,1)S(1)}, u32[]{:S(2)}, u32[]{:S(2)}) collective-permute-start(bf16[32,1024]{1,0:T(8,128)(2,1)S(1)} %arrive.4.refs_2_.first.refs_1_), channel_id=1, source_target_pairs={{0,6},{2,4},{4,2},{6,0},{1,7},{3,5},{5,3},{7,1},{8,14},{10,12},{12... | collective-permute-start | bytes 196616 | tf_op jit(solution)/shard_map/ppermute | solution.py:31
  37.1 4.4 %collective-permute-start.15 = (bf16[128,1024]{1,0:T(8,128)(2,1)S(1)}, bf16[128,1024]{1,0:T(8,128)(2,1)S(1)}, u32[]{:S(2)}, u32[]{:S(2)}) collective-permute-start(bf16[128,1024]{1,0:T(8,128)(2,1)S(1)} %get-tuple-element.148.refs_0_.refs_2_), channel_id=1, source_target_pairs={{0,1},{1,0},{2,3},{3,2},{4,5},{5,4},{6,7},{7,6},{8,9},{9,8},{10,11... | collective-permute-start | bytes 786440 | tf_op jit(solution)/shard_map/ppermute | solution.py:22
  40.7 1.6 %collective-permute-start.14 = (bf16[128,1024]{1,0:T(8,128)(2,1)S(1)}, bf16[128,1024]{1,0:T(8,128)(2,1)S(1)}, u32[]{:S(2)}, u32[]{:S(2)}) collective-permute-start(bf16[128,1024]{1,0:T(8,128)(2,1)S(1)} %product_part.7.refs_0_.refs_2_), channel_id=1, source_target_pairs={{0,1},{1,0},{2,3},{3,2},{4,5},{5,4},{6,7},{7,6},{8,9},{9,8},{10,11... | collective-permute-start | bytes 786440 | tf_op jit(solution)/shard_map/ppermute | solution.py:22
  42.8 5.4 %collective-permute-start.16 = (bf16[32,1024]{1,0:T(8,128)(2,1)S(1)}, bf16[32,1024]{1,0:T(8,128)(2,1)S(1)}, u32[]{:S(2)}, u32[]{:S(2)}) collective-permute-start(bf16[32,1024]{1,0:T(8,128)(2,1)S(1)} %get-tuple-element.151), channel_id=1, source_target_pairs={{0,6},{2,4},{4,2},{6,0},{1,7},{3,5},{5,3},{7,1},{8,14},{10,12},{12... | collective-permute-start | bytes 196616 | tf_op jit(solution)/shard_map/ppermute | solution.py:31
  44.4 7.2 %collective-permute-start.17 = (bf16[32,1024]{1,0:T(8,128)(2,1)S(1)}, bf16[32,1024]{1,0:T(8,128)(2,1)S(1)}, u32[]{:S(2)}, u32[]{:S(2)}) collective-permute-start(bf16[32,1024]{1,0:T(8,128)(2,1)S(1)} %get-tuple-element.152), channel_id=1, source_target_pairs={{0,4},{2,6},{4,0},{6,2},{1,5},{3,7},{5,1},{7,3},{8,12},{10,14},{12... | collective-permute-start | bytes 196616 | tf_op jit(solution)/shard_map/ppermute | solution.py:31
  44.4 7.2 %collective-permute-start.18 = (bf16[32,1024]{1,0:T(8,128)(2,1)S(1)}, bf16[32,1024]{1,0:T(8,128)(2,1)S(1)}, u32[]{:S(2)}, u32[]{:S(2)}) collective-permute-start(bf16[32,1024]{1,0:T(8,128)(2,1)S(1)} %get-tuple-element.153), channel_id=1, source_target_pairs={{0,2},{2,0},{4,6},{6,4},{1,3},{3,1},{5,7},{7,5},{8,10},{10,8},{12,... | collective-permute-start | bytes 196616 | tf_op jit(solution)/shard_map/ppermute | solution.py:31
  51.6 5.6 %collective-permute-start.19 = (bf16[32,1024]{1,0:T(8,128)(2,1)S(1)}, bf16[32,1024]{1,0:T(8,128)(2,1)S(1)}, u32[]{:S(2)}, u32[]{:S(2)}) collective-permute-start(bf16[32,1024]{1,0:T(8,128)(2,1)S(1)} %get-tuple-element.161), channel_id=1, source_target_pairs={{0,8},{8,16},{16,24},{1,9},{9,17},{17,25},{2,10},{10,18},{18,26},{... | collective-permute-start | bytes 196616 | tf_op jit(solution)/shard_map/ppermute | solution.py:17
  55.6 5.2 %collective-permute-start.23 = (bf16[32,1024]{1,0:T(8,128)(2,1)S(1)}, bf16[32,1024]{1,0:T(8,128)(2,1)S(1)}, u32[]{:S(2)}, u32[]{:S(2)}) collective-permute-start(bf16[32,1024]{1,0:T(8,128)(2,1)S(1)} %get-tuple-element.164.refs_0_.first), channel_id=1, source_target_pairs={{0,6},{2,4},{4,2},{6,0},{1,7},{3,5},{5,3},{7,1},{8,14},{10,12},{12... | collective-permute-start | bytes 196616 | tf_op jit(solution)/shard_map/ppermute | solution.py:31
  57.2 7.0 %collective-permute-start.22 = (bf16[32,1024]{1,0:T(8,128)(2,1)S(1)}, bf16[32,1024]{1,0:T(8,128)(2,1)S(1)}, u32[]{:S(2)}, u32[]{:S(2)}) collective-permute-start(bf16[32,1024]{1,0:T(8,128)(2,1)S(1)} %arrive.5.refs_0_.refs_2_), channel_id=1, source_target_pairs={{0,2},{2,0},{4,6},{6,4},{1,3},{3,1},{5,7},{7,5},{8,10},{10,8},{12,... | collective-permute-start | bytes 196616 | tf_op jit(solution)/shard_map/ppermute | solution.py:31
  57.3 6.9 %collective-permute-start.21 = (bf16[32,1024]{1,0:T(8,128)(2,1)S(1)}, bf16[32,1024]{1,0:T(8,128)(2,1)S(1)}, u32[]{:S(2)}, u32[]{:S(2)}) collective-permute-start(bf16[32,1024]{1,0:T(8,128)(2,1)S(1)} %arrive.5.refs_0_.refs_2_), channel_id=1, source_target_pairs={{0,4},{2,6},{4,0},{6,2},{1,5},{3,7},{5,1},{7,3},{8,12},{10,14},{12... | collective-permute-start | bytes 196616 | tf_op jit(solution)/shard_map/ppermute | solution.py:31
  59.3 5.7 %collective-permute-start.20 = (bf16[32,1024]{1,0:T(8,128)(2,1)S(1)}, bf16[32,1024]{1,0:T(8,128)(2,1)S(1)}, u32[]{:S(2)}, u32[]{:S(2)}) collective-permute-start(bf16[32,1024]{1,0:T(8,128)(2,1)S(1)} %arrive.5.refs_0_.refs_2_), channel_id=1, source_target_pairs={{0,6},{2,4},{4,2},{6,0},{1,7},{3,5},{5,3},{7,1},{8,14},{10,12},{12... | collective-permute-start | bytes 196616 | tf_op jit(solution)/shard_map/ppermute | solution.py:31
  61.7 7.6 %collective-permute-start.26 = (bf16[128,1024]{1,0:T(8,128)(2,1)S(1)}, bf16[128,1024]{1,0:T(8,128)(2,1)S(1)}, u32[]{:S(2)}, u32[]{:S(2)}) collective-permute-start(bf16[128,1024]{1,0:T(8,128)(2,1)S(1)} %product_part.8.refs_0_), channel_id=1, source_target_pairs={{0,1},{1,0},{2,3},{3,2},{4,5},{5,4},{6,7},{7,6},{8,9},{9,8},{10,11... | collective-permute-start | bytes 786440 | tf_op jit(solution)/shard_map/ppermute | solution.py:22
  64.1 4.1 %collective-permute-start.27 = (bf16[128,1024]{1,0:T(8,128)(2,1)S(1)}, bf16[128,1024]{1,0:T(8,128)(2,1)S(1)}, u32[]{:S(2)}, u32[]{:S(2)}) collective-permute-start(bf16[128,1024]{1,0:T(8,128)(2,1)S(1)} %get-tuple-element.165.refs_0_), channel_id=1, source_target_pairs={{0,1},{1,0},{2,3},{3,2},{4,5},{5,4},{6,7},{7,6},{8,9},{9,8},{10,11... | collective-permute-start | bytes 786440 | tf_op jit(solution)/shard_map/ppermute | solution.py:22
  65.4 3.3 %collective-permute-start.24 = (bf16[128,1024]{1,0:T(8,128)(2,1)S(1)}, bf16[128,1024]{1,0:T(8,128)(2,1)S(1)}, u32[]{:S(2)}, u32[]{:S(2)}) collective-permute-start(bf16[128,1024]{1,0:T(8,128)(2,1)S(1)} %get-tuple-element.184.refs_2_.refs_0_), channel_id=1, source_target_pairs={{0,1},{1,0},{2,3},{3,2},{4,5},{5,4},{6,7},{7,6},{8,9},{9,8},{10,11... | collective-permute-start | bytes 786440 | tf_op jit(solution)/shard_map/ppermute | solution.py:22
  68.1 1.6 %collective-permute-start.25 = (bf16[128,1024]{1,0:T(8,128)(2,1)S(1)}, bf16[128,1024]{1,0:T(8,128)(2,1)S(1)}, u32[]{:S(2)}, u32[]{:S(2)}) collective-permute-start(bf16[128,1024]{1,0:T(8,128)(2,1)S(1)} %product_part.9.refs_2_), channel_id=1, source_target_pairs={{0,1},{1,0},{2,3},{3,2},{4,5},{5,4},{6,7},{7,6},{8,9},{9,8},{10,11... | collective-permute-start | bytes 786440 | tf_op jit(solution)/shard_map/ppermute | solution.py:22
  70.3 5.4 %collective-permute-start.28 = (bf16[32,1024]{1,0:T(8,128)(2,1)S(1)}, bf16[32,1024]{1,0:T(8,128)(2,1)S(1)}, u32[]{:S(2)}, u32[]{:S(2)}) collective-permute-start(bf16[32,1024]{1,0:T(8,128)(2,1)S(1)} %get-tuple-element.175), channel_id=1, source_target_pairs={{0,6},{2,4},{4,2},{6,0},{1,7},{3,5},{5,3},{7,1},{8,14},{10,12},{12... | collective-permute-start | bytes 196616 | tf_op jit(solution)/shard_map/ppermute | solution.py:31
  71.9 7.3 %collective-permute-start.29 = (bf16[32,1024]{1,0:T(8,128)(2,1)S(1)}, bf16[32,1024]{1,0:T(8,128)(2,1)S(1)}, u32[]{:S(2)}, u32[]{:S(2)}) collective-permute-start(bf16[32,1024]{1,0:T(8,128)(2,1)S(1)} %get-tuple-element.176), channel_id=1, source_target_pairs={{0,4},{2,6},{4,0},{6,2},{1,5},{3,7},{5,1},{7,3},{8,12},{10,14},{12... | collective-permute-start | bytes 196616 | tf_op jit(solution)/shard_map/ppermute | solution.py:31
  72.4 6.8 %collective-permute-start.30 = (bf16[32,1024]{1,0:T(8,128)(2,1)S(1)}, bf16[32,1024]{1,0:T(8,128)(2,1)S(1)}, u32[]{:S(2)}, u32[]{:S(2)}) collective-permute-start(bf16[32,1024]{1,0:T(8,128)(2,1)S(1)} %get-tuple-element.177), channel_id=1, source_target_pairs={{0,2},{2,0},{4,6},{6,4},{1,3},{3,1},{5,7},{7,5},{8,10},{10,8},{12,... | collective-permute-start | bytes 196616 | tf_op jit(solution)/shard_map/ppermute | solution.py:31
  79.3 5.9 %collective-permute-start.31 = (bf16[32,1024]{1,0:T(8,128)(2,1)S(1)}, bf16[32,1024]{1,0:T(8,128)(2,1)S(1)}, u32[]{:S(2)}, u32[]{:S(2)}) collective-permute-start(bf16[32,1024]{1,0:T(8,128)(2,1)S(1)} %leave_back.2.refs_5_), channel_id=1, source_target_pairs={{8,0},{16,8},{24,16},{9,1},{17,9},{25,17},{10,2},{18,10},{26,18},{... | collective-permute-start | bytes 196616 | tf_op jit(solution)/shard_map/ppermute | solution.py:17
  82.3 6.5 %collective-permute-start.32 = (bf16[32,1024]{1,0:T(8,128)(2,1)S(1)}, bf16[32,1024]{1,0:T(8,128)(2,1)S(1)}, u32[]{:S(2)}, u32[]{:S(2)}) collective-permute-start(bf16[32,1024]{1,0:T(8,128)(2,1)S(1)} %get-tuple-element.196), channel_id=1, source_target_pairs={{0,2},{2,0},{4,6},{6,4},{1,3},{3,1},{5,7},{7,5},{8,10},{10,8},{12,... | collective-permute-start | bytes 196616 | tf_op jit(solution)/shard_map/ppermute | solution.py:31
  82.4 6.4 %collective-permute-start.33 = (bf16[32,1024]{1,0:T(8,128)(2,1)S(1)}, bf16[32,1024]{1,0:T(8,128)(2,1)S(1)}, u32[]{:S(2)}, u32[]{:S(2)}) collective-permute-start(bf16[32,1024]{1,0:T(8,128)(2,1)S(1)} %get-tuple-element.197), channel_id=1, source_target_pairs={{0,4},{2,6},{4,0},{6,2},{1,5},{3,7},{5,1},{7,3},{8,12},{10,14},{12... | collective-permute-start | bytes 196616 | tf_op jit(solution)/shard_map/ppermute | solution.py:31
  85.2 3.7 %collective-permute-start.36 = (bf16[32,1024]{1,0:T(8,128)(2,1)S(1)}, bf16[32,1024]{1,0:T(8,128)(2,1)S(1)}, u32[]{:S(2)}, u32[]{:S(2)}) collective-permute-start(bf16[32,1024]{1,0:T(8,128)(2,1)S(1)} %arrive.6.refs_2_.first), channel_id=1, source_target_pairs={{0,2},{2,0},{4,6},{6,4},{1,3},{3,1},{5,7},{7,5},{8,10},{10,8},{12,... | collective-permute-start | bytes 196616 | tf_op jit(solution)/shard_map/ppermute | solution.py:31
  85.3 4.5 %collective-permute-start.35 = (bf16[32,1024]{1,0:T(8,128)(2,1)S(1)}, bf16[32,1024]{1,0:T(8,128)(2,1)S(1)}, u32[]{:S(2)}, u32[]{:S(2)}) collective-permute-start(bf16[32,1024]{1,0:T(8,128)(2,1)S(1)} %arrive.6.refs_2_.first), channel_id=1, source_target_pairs={{0,4},{2,6},{4,0},{6,2},{1,5},{3,7},{5,1},{7,3},{8,12},{10,14},{12... | collective-permute-start | bytes 196616 | tf_op jit(solution)/shard_map/ppermute | solution.py:31
  87.3 5.2 %collective-permute-start.34 = (bf16[32,1024]{1,0:T(8,128)(2,1)S(1)}, bf16[32,1024]{1,0:T(8,128)(2,1)S(1)}, u32[]{:S(2)}, u32[]{:S(2)}) collective-permute-start(bf16[32,1024]{1,0:T(8,128)(2,1)S(1)} %arrive.6.refs_2_.first), channel_id=1, source_target_pairs={{0,6},{2,4},{4,2},{6,0},{1,7},{3,5},{5,3},{7,1},{8,14},{10,12},{12... | collective-permute-start | bytes 196616 | tf_op jit(solution)/shard_map/ppermute | solution.py:31
  93.0 4.2 %collective-permute-start.38 = (bf16[128,1024]{1,0:T(8,128)(2,1)S(1)}, bf16[128,1024]{1,0:T(8,128)(2,1)S(1)}, u32[]{:S(2)}, u32[]{:S(2)}) collective-permute-start(bf16[128,1024]{1,0:T(8,128)(2,1)S(1)} %get-tuple-element.199.refs_0_), channel_id=1, source_target_pairs={{0,1},{1,0},{2,3},{3,2},{4,5},{5,4},{6,7},{7,6},{8,9},{9,8},{10,11... | collective-permute-start | bytes 786440 | tf_op jit(solution)/shard_map/ppermute | solution.py:22
  96.5 1.6 %collective-permute-start.37 = (bf16[128,1024]{1,0:T(8,128)(2,1)S(1)}, bf16[128,1024]{1,0:T(8,128)(2,1)S(1)}, u32[]{:S(2)}, u32[]{:S(2)}) collective-permute-start(bf16[128,1024]{1,0:T(8,128)(2,1)S(1)} %product_part.10.refs_0_), channel_id=1, source_target_pairs={{0,1},{1,0},{2,3},{3,2},{4,5},{5,4},{6,7},{7,6},{8,9},{9,8},{10,11... | collective-permute-start | bytes 786440 | tf_op jit(solution)/shard_map/ppermute | solution.py:22
  98.7 5.4 %collective-permute-start.39 = (bf16[32,1024]{1,0:T(8,128)(2,1)S(1)}, bf16[32,1024]{1,0:T(8,128)(2,1)S(1)}, u32[]{:S(2)}, u32[]{:S(2)}) collective-permute-start(bf16[32,1024]{1,0:T(8,128)(2,1)S(1)} %get-tuple-element.202), channel_id=1, source_target_pairs={{0,6},{2,4},{4,2},{6,0},{1,7},{3,5},{5,3},{7,1},{8,14},{10,12},{12... | collective-permute-start | bytes 196616 | tf_op jit(solution)/shard_map/ppermute | solution.py:31
  100.3 7.0 %collective-permute-start.40 = (bf16[32,1024]{1,0:T(8,128)(2,1)S(1)}, bf16[32,1024]{1,0:T(8,128)(2,1)S(1)}, u32[]{:S(2)}, u32[]{:S(2)}) collective-permute-start(bf16[32,1024]{1,0:T(8,128)(2,1)S(1)} %get-tuple-element.203), channel_id=1, source_target_pairs={{0,4},{2,6},{4,0},{6,2},{1,5},{3,7},{5,1},{7,3},{8,12},{10,14},{12... | collective-permute-start | bytes 196616 | tf_op jit(solution)/shard_map/ppermute | solution.py:31
  100.4 7.0 %collective-permute-start.41 = (bf16[32,1024]{1,0:T(8,128)(2,1)S(1)}, bf16[32,1024]{1,0:T(8,128)(2,1)S(1)}, u32[]{:S(2)}, u32[]{:S(2)}) collective-permute-start(bf16[32,1024]{1,0:T(8,128)(2,1)S(1)} %get-tuple-element.204), channel_id=1, source_target_pairs={{0,2},{2,0},{4,6},{6,4},{1,3},{3,1},{5,7},{7,5},{8,10},{10,8},{12,... | collective-permute-start | bytes 196616 | tf_op jit(solution)/shard_map/ppermute | solution.py:31
  107.4 5.9 %collective-permute-start.43 = (bf16[32,1024]{1,0:T(8,128)(2,1)S(1)}, bf16[32,1024]{1,0:T(8,128)(2,1)S(1)}, u32[]{:S(2)}, u32[]{:S(2)}) collective-permute-start(bf16[32,1024]{1,0:T(8,128)(2,1)S(1)} %leave_back.3.refs_4_), channel_id=1, source_target_pairs={{8,0},{16,8},{24,16},{9,1},{17,9},{25,17},{10,2},{18,10},{26,18},{... | collective-permute-start | bytes 196616 | tf_op jit(solution)/shard_map/ppermute | solution.py:17
  109.4 7.6 %collective-permute-start.42 = (bf16[32,1024]{1,0:T(8,128)(2,1)S(1)}, bf16[32,1024]{1,0:T(8,128)(2,1)S(1)}, u32[]{:S(2)}, u32[]{:S(2)}) collective-permute-start(bf16[32,1024]{1,0:T(8,128)(2,1)S(1)} %get-tuple-element.214), channel_id=1, source_target_pairs={{0,6},{2,4},{4,2},{6,0},{1,7},{3,5},{5,3},{7,1},{8,14},{10,12},{12... | collective-permute-start | bytes 196616 | tf_op jit(solution)/shard_map/ppermute | solution.py:31
  113.4 5.7 %collective-permute-start.46 = (bf16[32,1024]{1,0:T(8,128)(2,1)S(1)}, bf16[32,1024]{1,0:T(8,128)(2,1)S(1)}, u32[]{:S(2)}, u32[]{:S(2)}) collective-permute-start(bf16[32,1024]{1,0:T(8,128)(2,1)S(1)} %arrive.7.refs_0_.first), channel_id=1, source_target_pairs={{0,2},{2,0},{4,6},{6,4},{1,3},{3,1},{5,7},{7,5},{8,10},{10,8},{12,... | collective-permute-start | bytes 196616 | tf_op jit(solution)/shard_map/ppermute | solution.py:31
  113.4 5.6 %collective-permute-start.45 = (bf16[32,1024]{1,0:T(8,128)(2,1)S(1)}, bf16[32,1024]{1,0:T(8,128)(2,1)S(1)}, u32[]{:S(2)}, u32[]{:S(2)}) collective-permute-start(bf16[32,1024]{1,0:T(8,128)(2,1)S(1)} %arrive.7.refs_0_.first), channel_id=1, source_target_pairs={{0,4},{2,6},{4,0},{6,2},{1,5},{3,7},{5,1},{7,3},{8,12},{10,14},{12... | collective-permute-start | bytes 196616 | tf_op jit(solution)/shard_map/ppermute | solution.py:31
  115.3 4.9 %collective-permute-start.44 = (bf16[32,1024]{1,0:T(8,128)(2,1)S(1)}, bf16[32,1024]{1,0:T(8,128)(2,1)S(1)}, u32[]{:S(2)}, u32[]{:S(2)}) collective-permute-start(bf16[32,1024]{1,0:T(8,128)(2,1)S(1)} %arrive.7.refs_0_.first), channel_id=1, source_target_pairs={{0,6},{2,4},{4,2},{6,0},{1,7},{3,5},{5,3},{7,1},{8,14},{10,12},{12... | collective-permute-start | bytes 196616 | tf_op jit(solution)/shard_map/ppermute | solution.py:31
  120.7 4.6 %collective-permute-start.48 = (bf16[128,1024]{1,0:T(8,128)(2,1)S(1)}, bf16[128,1024]{1,0:T(8,128)(2,1)S(1)}, u32[]{:S(2)}, u32[]{:S(2)}) collective-permute-start(bf16[128,1024]{1,0:T(8,128)(2,1)S(1)} %get-tuple-element.225.refs_0_), channel_id=1, source_target_pairs={{0,1},{1,0},{2,3},{3,2},{4,5},{5,4},{6,7},{7,6},{8,9},{9,8},{10,11... | collective-permute-start | bytes 786440 | tf_op jit(solution)/shard_map/ppermute | solution.py:22
  124.5 1.6 %collective-permute-start.47 = (bf16[128,1024]{1,0:T(8,128)(2,1)S(1)}, bf16[128,1024]{1,0:T(8,128)(2,1)S(1)}, u32[]{:S(2)}, u32[]{:S(2)}) collective-permute-start(bf16[128,1024]{1,0:T(8,128)(2,1)S(1)} %product_part.11.refs_0_), channel_id=1, source_target_pairs={{0,1},{1,0},{2,3},{3,2},{4,5},{5,4},{6,7},{7,6},{8,9},{9,8},{10,11... | collective-permute-start | bytes 786440 | tf_op jit(solution)/shard_map/ppermute | solution.py:22
  126.7 7.4 %collective-permute-start.49 = (bf16[32,1024]{1,0:T(8,128)(2,1)S(1)}, bf16[32,1024]{1,0:T(8,128)(2,1)S(1)}, u32[]{:S(2)}, u32[]{:S(2)}) collective-permute-start(bf16[32,1024]{1,0:T(8,128)(2,1)S(1)} %get-tuple-element.230), channel_id=1, source_target_pairs={{0,6},{2,4},{4,2},{6,0},{1,7},{3,5},{5,3},{7,1},{8,14},{10,12},{12... | collective-permute-start | bytes 196616 | tf_op jit(solution)/shard_map/ppermute | solution.py:31
  128.5 7.0 %collective-permute-start.50 = (bf16[32,1024]{1,0:T(8,128)(2,1)S(1)}, bf16[32,1024]{1,0:T(8,128)(2,1)S(1)}, u32[]{:S(2)}, u32[]{:S(2)}) collective-permute-start(bf16[32,1024]{1,0:T(8,128)(2,1)S(1)} %get-tuple-element.231), channel_id=1, source_target_pairs={{0,4},{2,6},{4,0},{6,2},{1,5},{3,7},{5,1},{7,3},{8,12},{10,14},{12... | collective-permute-start | bytes 196616 | tf_op jit(solution)/shard_map/ppermute | solution.py:31
  128.5 7.0 %collective-permute-start.51 = (bf16[32,1024]{1,0:T(8,128)(2,1)S(1)}, bf16[32,1024]{1,0:T(8,128)(2,1)S(1)}, u32[]{:S(2)}, u32[]{:S(2)}) collective-permute-start(bf16[32,1024]{1,0:T(8,128)(2,1)S(1)} %get-tuple-element.232), channel_id=1, source_target_pairs={{0,2},{2,0},{4,6},{6,4},{1,3},{3,1},{5,7},{7,5},{8,10},{10,8},{12,... | collective-permute-start | bytes 196616 | tf_op jit(solution)/shard_map/ppermute | solution.py:31

commit v15 on v14

--- a/solution.py
+++ b/solution.py
@@ -235,7 +235,7 @@
 
 def stack_product(part, skip, *refs):
     *pieces, weight, whole, product = refs[skip:]
-    whole[...] = jnp.concatenate([piece[...] for piece in pieces], axis=0)
+    whole[...] = jnp.concatenate([piece[...] for piece in reversed(pieces)], axis=0)
     product_part(part, whole, weight, product)
 
 
@@ -246,7 +246,7 @@
     flops = 2 * tokens * width * likes[0].shape[1]
     whole, first = run(
         functools.partial(stack_product, parts[0], len(waited)), [whole_like, likes[0]],
-        *waited, *pieces, weight, flops=flops, name="stack_product",
+        *waited, *reversed(pieces), weight, flops=flops, name="stack_product",
     )
     rest = [
         run(functools.partial(product_part, part), [like], whole, weight, flops=flops, name="product_part")[0]
@@ -443,10 +443,10 @@
         pieces = gather_rows(act_in)
         if tick == 0:
             up_kept, down_kept = hold(after([w_up[0], w_down[0]], act_in))
-            pieces = after(pieces, up_kept)
+            pieces = after(pieces[::-1], up_kept)[::-1]
         if tick == ticks - 1:
             full_cot, first_grads = products(parts, cot_pieces, down_turned)
-            pieces, waited = after(pieces, first_grads), []
+            pieces, waited = after(pieces[::-1], first_grads)[::-1], []
         full_in, partial = products(parts, pieces, up_kept, waited)
         pre = [(mine, other_cols(mine)) for mine in partial]
         if tick < ticks - 1:
@@ -495,7 +495,7 @@
                     "finish_forward",
                 )
                 begun_down = begin_grad([part[1:] for part in turned_acts], [[block] for block in after(full_grads[1:], grad_out)])
-                pieces, waited = after(pieces, (section_output, begun_down)), []
+                pieces, waited = after(pieces[::-1], (section_output, begun_down))[::-1], []
             full_grad, partial = products(parts, pieces, down_turned, waited)
         full_grads[tick] = full_grad
         ins = [(mine, other_cols(mine), *known) for mine, known in zip(partial, pres[tick])]

time: 136 us -> 134 us (0.985)
  starting transfers between devices: 71.6 us -> 64 us
  waiting for transfers between devices: 34 us -> 39.5 us
    ppermute x12, starting transfers between devices: 17.1 us -> 9.19 us  [turn(): lax.ppermute(block, axis, [(i, (i + distance) % size) for i in range(size)])]
    ppermute x36, waiting for transfers between devices: 25.9 us -> 31.4 us  [swap_rows(): lax.ppermute(block, 'row', [(i, partner(i, j, size)) for i in range(size)])]
where the time goes in v15:
time: 134 us
  starting transfers between devices  64 us (48%)
  waiting for transfers between devices  39.5 us (29%)
  Pallas kernels  29.5 us (22%)
    ppermute x36, starting transfers between devices, swap_rows(): lax.ppermute(block, 'row', [(i, partner(i, j, size)) for i in range(size)])  44.2 us
    ppermute x36, waiting for transfers between devices, swap_rows(): lax.ppermute(block, 'row', [(i, partner(i, j, size)) for i in range(size)])  31.4 us
    pallas_call x45, Pallas kernels, run(): pl.pallas_call(kernel, in_specs=vmem(len(ins)), out_specs=vmem(len(outs))...  18 us
    ppermute x4, starting transfers between devices, hand_over(): lax.ppermute(block, 'section', [(i - distance, i) for i in sections if i...  10.6 us
    ppermute x12, starting transfers between devices, turn(): lax.ppermute(block, axis, [(i, (i + distance) % size) for i in range(size)])  9.19 us
    ppermute x12, waiting for transfers between devices, turn(): lax.ppermute(block, axis, [(i, (i + distance) % size) for i in range(size)])  4.88 us
    pallas_call x1, Pallas kernels, end_grads(): pl.pallas_call(functools.partial(grads_ended, tuple(((len(lefts), len(rig...  3.8 us
    pallas_call x1, Pallas kernels, hold(): pl.pallas_call(hold_kernel, in_specs=[pl.BlockSpec(memory_space=pltpu.HBM...  3.51 us
  transfers between devices with their start and end apart: 52, of which 27 were waited for; matrix products, arithmetic and copies ran while one was open for 0% of the time, Pallas kernels for 17%

profile of v15, /device:TPU:3, one launch (start us, length us, event | category | flops | bytes accessed | tf_op | source)
XLA Modules:
  0.0 134.0 jit_solution(4806912301258334332)
XLA Ops:
  0.6 0.9 first.1
  1.5 3.4 %collective-permute-start.2 = (bf16[32,1024]{1,0:T(8,128)(2,1)S(1)}, bf16[32,1024]{1,0:T(8,128)(2,1)S(1)}, u32[]{:S(2)}, u32[]{:S(2)}) collective-permute-start(bf16[32,1024]{1,0:T(8,128)(2,1)S(1)} %get-tuple-element.128.refs_3_.first.refs_0_), channel_id=1, source_target_pairs={{0,6},{2,4},{4,2},{6,0},{1,7},{3,5},{5,3},{7,1},{8,14},{10,12},{12... | collective-permute-start | bytes 196616 | tf_op jit(solution)/shard_map/ppermute | solution.py:31
  5.3 3.5 %hold.1 = (bf16[1024,2048]{1,0:T(8,128)(2,1)S(1)}, bf16[2048,1024]{1,0:T(8,128)(2,1)S(1)}) custom-call(bf16[1024,2048]{1,0:T(8,128)(2,1)} %bitcast.4, bf16[2048,1024]{1,0:T(8,128)(2,1)} %bitcast.5), custom_call_target="tpu_custom_call" | custom-call | bytes 16777216 | tf_op jit(solution)/shard_map/hold/pallas_call | solution.py:214
  8.8 2.0 %collective-permute-done.1.refs_1_ = bf16[32,1024]{1,0:T(8,128)(2,1)S(1)} collective-permute-done((bf16[32,1024]{1,0:T(8,128)(2,1)S(1)}, bf16[32,1024]{1,0:T(8,128)(2,1)S(1)}, u32[]{:S(2)}, u32[]{:S(2)}) %collective-permute-start.1) | collective-permute-done | bytes 65568 | tf_op jit(solution)/shard_map/ppermute | solution.py:31
  11.3 0.7 collective-permute-start.4
  12.5 0.6 collective-permute-done.4.refs_1_.refs_3_
  14.5 2.5 %collective-permute-start.5 = (bf16[32,1024]{1,0:T(8,128)(2,1)S(1)}, bf16[32,1024]{1,0:T(8,128)(2,1)S(1)}, u32[]{:S(2)}, u32[]{:S(2)}) collective-permute-start(bf16[32,1024]{1,0:T(8,128)(2,1)S(1)} %get-tuple-element.134), channel_id=1, source_target_pairs={{0,6},{2,4},{4,2},{6,0},{1,7},{3,5},{5,3},{7,1},{8,14},{10,12},{12... | collective-permute-start | bytes 196616 | tf_op jit(solution)/shard_map/ppermute | solution.py:31
  17.0 1.1 collective-permute-start.7
  18.1 1.2 turned_weight.2.refs_4_.weight.refs_6_
  19.4 1.7 %fetch.1 = (bf16[32,1024]{1,0:T(8,128)(2,1)S(1)}, bf16[32,1024]{1,0:T(8,128)(2,1)S(1)}, bf16[32,1024]{1,0:T(8,128)(2,1)S(1)}, bf16[32,1024]{1,0:T(8,128)(2,1)S(1...) custom-call(s32[6]{0:T(128)S(1)} %copy-done, bf16[1,3,32,1024]{3,2,1,0:T(8,128)(2,1)} %inputs.3, ...), custom_call_target="tpu_custom_call" | custom-call | bytes 2097152 | tf_op jit(solution)/shard_map/fetch/pallas_call | solution.py:109
  21.1 2.3 %collective-permute-done.6.refs_2_ = bf16[32,1024]{1,0:T(8,128)(2,1)S(1)} collective-permute-done((bf16[32,1024]{1,0:T(8,128)(2,1)S(1)}, bf16[32,1024]{1,0:T(8,128)(2,1)S(1)}, u32[]{:S(2)}, u32[]{:S(2)}) %collective-permute-start.6) | collective-permute-done | bytes 65568 | tf_op jit(solution)/shard_map/ppermute | solution.py:31
  23.5 3.1 %collective-permute-start.8 = (bf16[32,1024]{1,0:T(8,128)(2,1)S(1)}, bf16[32,1024]{1,0:T(8,128)(2,1)S(1)}, u32[]{:S(2)}, u32[]{:S(2)}) collective-permute-start(bf16[32,1024]{1,0:T(8,128)(2,1)S(1)} %get-tuple-element.143), channel_id=1, source_target_pairs={{0,8},{8,16},{16,24},{1,9},{9,17},{17,25},{2,10},{10,18},{18,26},{... | collective-permute-start | bytes 196616 | tf_op jit(solution)/shard_map/ppermute | solution.py:17
  26.7 2.4 %collective-permute-start.9 = (bf16[32,1024]{1,0:T(8,128)(2,1)S(1)}, bf16[32,1024]{1,0:T(8,128)(2,1)S(1)}, u32[]{:S(2)}, u32[]{:S(2)}) collective-permute-start(bf16[32,1024]{1,0:T(8,128)(2,1)S(1)} %get-tuple-element.164.refs_3_.first), channel_id=1, source_target_pairs={{0,2},{2,0},{4,6},{6,4},{1,3},{3,1},{5,7},{7,5},{8,10},{10,8},{12,... | collective-permute-start | bytes 196616 | tf_op jit(solution)/shard_map/ppermute | solution.py:31
  29.1 1.6 %collective-permute-start.13 = (bf16[32,1024]{1,0:T(8,128)(2,1)S(1)}, bf16[32,1024]{1,0:T(8,128)(2,1)S(1)}, u32[]{:S(2)}, u32[]{:S(2)}) collective-permute-start(bf16[32,1024]{1,0:T(8,128)(2,1)S(1)} %arrive.4.refs_5_.first.refs_1_), channel_id=1, source_target_pairs={{0,6},{2,4},{4,2},{6,0},{1,7},{3,5},{5,3},{7,1},{8,14},{10,12},{12... | collective-permute-start | bytes 196616 | tf_op jit(solution)/shard_map/ppermute | solution.py:31
  30.7 2.0 %collective-permute-start.11 = (bf16[32,1024]{1,0:T(8,128)(2,1)S(1)}, bf16[32,1024]{1,0:T(8,128)(2,1)S(1)}, u32[]{:S(2)}, u32[]{:S(2)}) collective-permute-start(bf16[32,1024]{1,0:T(8,128)(2,1)S(1)} %arrive.4.refs_5_.first.refs_1_), channel_id=1, source_target_pairs={{0,2},{2,0},{4,6},{6,4},{1,3},{3,1},{5,7},{7,5},{8,10},{10,8},{12,... | collective-permute-start | bytes 196616 | tf_op jit(solution)/shard_map/ppermute | solution.py:31
  32.7 1.5 %collective-permute-done.13.refs_4_ = bf16[32,1024]{1,0:T(8,128)(2,1)S(1)} collective-permute-done((bf16[32,1024]{1,0:T(8,128)(2,1)S(1)}, bf16[32,1024]{1,0:T(8,128)(2,1)S(1)}, u32[]{:S(2)}, u32[]{:S(2)}) %collective-permute-start.13) | collective-permute-done | bytes 65568 | tf_op jit(solution)/shard_map/ppermute | solution.py:31
  34.2 3.7 %collective-permute-done.12.refs_3_ = bf16[32,1024]{1,0:T(8,128)(2,1)S(1)} collective-permute-done((bf16[32,1024]{1,0:T(8,128)(2,1)S(1)}, bf16[32,1024]{1,0:T(8,128)(2,1)S(1)}, u32[]{:S(2)}, u32[]{:S(2)}) %collective-permute-start.12) | collective-permute-done | bytes 65568 | tf_op jit(solution)/shard_map/ppermute | solution.py:31
  38.4 1.0 collective-permute-start.15
  40.0 0.6 collective-permute-done.15.refs_1_.refs_3_
  42.0 1.7 %collective-permute-start.16 = (bf16[32,1024]{1,0:T(8,128)(2,1)S(1)}, bf16[32,1024]{1,0:T(8,128)(2,1)S(1)}, u32[]{:S(2)}, u32[]{:S(2)}) collective-permute-start(bf16[32,1024]{1,0:T(8,128)(2,1)S(1)} %get-tuple-element.151), channel_id=1, source_target_pairs={{0,6},{2,4},{4,2},{6,0},{1,7},{3,5},{5,3},{7,1},{8,14},{10,12},{12... | collective-permute-start | bytes 196616 | tf_op jit(solution)/shard_map/ppermute | solution.py:31
  43.6 1.9 %collective-permute-start.18 = (bf16[32,1024]{1,0:T(8,128)(2,1)S(1)}, bf16[32,1024]{1,0:T(8,128)(2,1)S(1)}, u32[]{:S(2)}, u32[]{:S(2)}) collective-permute-start(bf16[32,1024]{1,0:T(8,128)(2,1)S(1)} %get-tuple-element.153), channel_id=1, source_target_pairs={{0,2},{2,0},{4,6},{6,4},{1,3},{3,1},{5,7},{7,5},{8,10},{10,8},{12,... | collective-permute-start | bytes 196616 | tf_op jit(solution)/shard_map/ppermute | solution.py:31
  45.9 1.2 turned_weight.3.refs_4_
  47.4 3.3 %collective-permute-done.17.refs_2_ = bf16[32,1024]{1,0:T(8,128)(2,1)S(1)} collective-permute-done((bf16[32,1024]{1,0:T(8,128)(2,1)S(1)}, bf16[32,1024]{1,0:T(8,128)(2,1)S(1)}, u32[]{:S(2)}, u32[]{:S(2)}) %collective-permute-start.17) | collective-permute-done | bytes 65568 | tf_op jit(solution)/shard_map/ppermute | solution.py:31
  50.7 3.5 %collective-permute-start.19 = (bf16[32,1024]{1,0:T(8,128)(2,1)S(1)}, bf16[32,1024]{1,0:T(8,128)(2,1)S(1)}, u32[]{:S(2)}, u32[]{:S(2)}) collective-permute-start(bf16[32,1024]{1,0:T(8,128)(2,1)S(1)} %get-tuple-element.161), channel_id=1, source_target_pairs={{0,8},{8,16},{16,24},{1,9},{9,17},{17,25},{2,10},{10,18},{18,26},{... | collective-permute-start | bytes 196616 | tf_op jit(solution)/shard_map/ppermute | solution.py:17
  54.2 1.8 %collective-permute-start.23 = (bf16[32,1024]{1,0:T(8,128)(2,1)S(1)}, bf16[32,1024]{1,0:T(8,128)(2,1)S(1)}, u32[]{:S(2)}, u32[]{:S(2)}) collective-permute-start(bf16[32,1024]{1,0:T(8,128)(2,1)S(1)} %get-tuple-element.164.refs_3_.first), channel_id=1, source_target_pairs={{0,6},{2,4},{4,2},{6,0},{1,7},{3,5},{5,3},{7,1},{8,14},{10,12},{12... | collective-permute-start | bytes 196616 | tf_op jit(solution)/shard_map/ppermute | solution.py:31
  56.1 1.6 %collective-permute-start.22 = (bf16[32,1024]{1,0:T(8,128)(2,1)S(1)}, bf16[32,1024]{1,0:T(8,128)(2,1)S(1)}, u32[]{:S(2)}, u32[]{:S(2)}) collective-permute-start(bf16[32,1024]{1,0:T(8,128)(2,1)S(1)} %arrive.5.refs_3_.refs_2_), channel_id=1, source_target_pairs={{0,6},{2,4},{4,2},{6,0},{1,7},{3,5},{5,3},{7,1},{8,14},{10,12},{12... | collective-permute-start | bytes 196616 | tf_op jit(solution)/shard_map/ppermute | solution.py:31
  57.7 2.0 %collective-permute-start.20 = (bf16[32,1024]{1,0:T(8,128)(2,1)S(1)}, bf16[32,1024]{1,0:T(8,128)(2,1)S(1)}, u32[]{:S(2)}, u32[]{:S(2)}) collective-permute-start(bf16[32,1024]{1,0:T(8,128)(2,1)S(1)} %arrive.5.refs_3_.refs_2_), channel_id=1, source_target_pairs={{0,2},{2,0},{4,6},{6,4},{1,3},{3,1},{5,7},{7,5},{8,10},{10,8},{12,... | collective-permute-start | bytes 196616 | tf_op jit(solution)/shard_map/ppermute | solution.py:31
  60.6 2.2 %collective-permute-start.26 = (bf16[128,1024]{1,0:T(8,128)(2,1)S(1)}, bf16[128,1024]{1,0:T(8,128)(2,1)S(1)}, u32[]{:S(2)}, u32[]{:S(2)}) collective-permute-start(bf16[128,1024]{1,0:T(8,128)(2,1)S(1)} %product_part.8.refs_0_), channel_id=1, source_target_pairs={{0,1},{1,0},{2,3},{3,2},{4,5},{5,4},{6,7},{7,6},{8,9},{9,8},{10,11... | collective-permute-start | bytes 786440 | tf_op jit(solution)/shard_map/ppermute | solution.py:22
  62.9 2.1 %collective-permute-done.21.refs_1_ = bf16[32,1024]{1,0:T(8,128)(2,1)S(1)} collective-permute-done((bf16[32,1024]{1,0:T(8,128)(2,1)S(1)}, bf16[32,1024]{1,0:T(8,128)(2,1)S(1)}, u32[]{:S(2)}, u32[]{:S(2)}) %collective-permute-start.21) | collective-permute-done | bytes 65568 | tf_op jit(solution)/shard_map/ppermute | solution.py:31
  65.5 1.1 collective-permute-start.24
  67.1 0.6 collective-permute-done.24.refs_3_.refs_1_
  69.2 1.8 %collective-permute-start.28 = (bf16[32,1024]{1,0:T(8,128)(2,1)S(1)}, bf16[32,1024]{1,0:T(8,128)(2,1)S(1)}, u32[]{:S(2)}, u32[]{:S(2)}) collective-permute-start(bf16[32,1024]{1,0:T(8,128)(2,1)S(1)} %get-tuple-element.175), channel_id=1, source_target_pairs={{0,6},{2,4},{4,2},{6,0},{1,7},{3,5},{5,3},{7,1},{8,14},{10,12},{12... | collective-permute-start | bytes 196616 | tf_op jit(solution)/shard_map/ppermute | solution.py:31
  71.1 1.8 %collective-permute-start.30 = (bf16[32,1024]{1,0:T(8,128)(2,1)S(1)}, bf16[32,1024]{1,0:T(8,128)(2,1)S(1)}, u32[]{:S(2)}, u32[]{:S(2)}) collective-permute-start(bf16[32,1024]{1,0:T(8,128)(2,1)S(1)} %get-tuple-element.177), channel_id=1, source_target_pairs={{0,2},{2,0},{4,6},{6,4},{1,3},{3,1},{5,7},{7,5},{8,10},{10,8},{12,... | collective-permute-start | bytes 196616 | tf_op jit(solution)/shard_map/ppermute | solution.py:31
  73.2 1.4 %collective-permute-done.28.refs_1_ = bf16[32,1024]{1,0:T(8,128)(2,1)S(1)} collective-permute-done((bf16[32,1024]{1,0:T(8,128)(2,1)S(1)}, bf16[32,1024]{1,0:T(8,128)(2,1)S(1)}, u32[]{:S(2)}, u32[]{:S(2)}) %collective-permute-start.28) | collective-permute-done | bytes 65568 | tf_op jit(solution)/shard_map/ppermute | solution.py:31
  74.6 3.3 %collective-permute-done.29.refs_2_ = bf16[32,1024]{1,0:T(8,128)(2,1)S(1)} collective-permute-done((bf16[32,1024]{1,0:T(8,128)(2,1)S(1)}, bf16[32,1024]{1,0:T(8,128)(2,1)S(1)}, u32[]{:S(2)}, u32[]{:S(2)}) %collective-permute-start.29) | collective-permute-done | bytes 65568 | tf_op jit(solution)/shard_map/ppermute | solution.py:31
  78.0 2.1 %collective-permute-start.31 = (bf16[32,1024]{1,0:T(8,128)(2,1)S(1)}, bf16[32,1024]{1,0:T(8,128)(2,1)S(1)}, u32[]{:S(2)}, u32[]{:S(2)}) collective-permute-start(bf16[32,1024]{1,0:T(8,128)(2,1)S(1)} %leave_back.2.refs_5_), channel_id=1, source_target_pairs={{8,0},{16,8},{24,16},{9,1},{17,9},{25,17},{10,2},{18,10},{26,18},{... | collective-permute-start | bytes 196616 | tf_op jit(solution)/shard_map/ppermute | solution.py:17
  80.3 0.7 down_again.1
  81.1 2.0 %collective-permute-start.33 = (bf16[32,1024]{1,0:T(8,128)(2,1)S(1)}, bf16[32,1024]{1,0:T(8,128)(2,1)S(1)}, u32[]{:S(2)}, u32[]{:S(2)}) collective-permute-start(bf16[32,1024]{1,0:T(8,128)(2,1)S(1)} %get-tuple-element.197), channel_id=1, source_target_pairs={{0,4},{2,6},{4,0},{6,2},{1,5},{3,7},{5,1},{7,3},{8,12},{10,14},{12... | collective-permute-start | bytes 196616 | tf_op jit(solution)/shard_map/ppermute | solution.py:31
  83.2 0.7 collective-permute-done.31.arrived
  83.9 1.8 %collective-permute-start.36 = (bf16[32,1024]{1,0:T(8,128)(2,1)S(1)}, bf16[32,1024]{1,0:T(8,128)(2,1)S(1)}, u32[]{:S(2)}, u32[]{:S(2)}) collective-permute-start(bf16[32,1024]{1,0:T(8,128)(2,1)S(1)} %arrive.6.refs_5_.first), channel_id=1, source_target_pairs={{0,6},{2,4},{4,2},{6,0},{1,7},{3,5},{5,3},{7,1},{8,14},{10,12},{12... | collective-permute-start | bytes 196616 | tf_op jit(solution)/shard_map/ppermute | solution.py:31
  85.7 1.8 %collective-permute-start.34 = (bf16[32,1024]{1,0:T(8,128)(2,1)S(1)}, bf16[32,1024]{1,0:T(8,128)(2,1)S(1)}, u32[]{:S(2)}, u32[]{:S(2)}) collective-permute-start(bf16[32,1024]{1,0:T(8,128)(2,1)S(1)} %arrive.6.refs_5_.first), channel_id=1, source_target_pairs={{0,2},{2,0},{4,6},{6,4},{1,3},{3,1},{5,7},{7,5},{8,10},{10,8},{12,... | collective-permute-start | bytes 196616 | tf_op jit(solution)/shard_map/ppermute | solution.py:31
  87.5 1.5 %collective-permute-done.36.refs_4_ = bf16[32,1024]{1,0:T(8,128)(2,1)S(1)} collective-permute-done((bf16[32,1024]{1,0:T(8,128)(2,1)S(1)}, bf16[32,1024]{1,0:T(8,128)(2,1)S(1)}, u32[]{:S(2)}, u32[]{:S(2)}) %collective-permute-start.36) | collective-permute-done | bytes 65568 | tf_op jit(solution)/shard_map/ppermute | solution.py:31
  89.0 3.6 %collective-permute-done.35.refs_3_ = bf16[32,1024]{1,0:T(8,128)(2,1)S(1)} collective-permute-done((bf16[32,1024]{1,0:T(8,128)(2,1)S(1)}, bf16[32,1024]{1,0:T(8,128)(2,1)S(1)}, u32[]{:S(2)}, u32[]{:S(2)}) %collective-permute-start.35) | collective-permute-done | bytes 65568 | tf_op jit(solution)/shard_map/ppermute | solution.py:31
  93.1 1.5 %collective-permute-start.38 = (bf16[128,1024]{1,0:T(8,128)(2,1)S(1)}, bf16[128,1024]{1,0:T(8,128)(2,1)S(1)}, u32[]{:S(2)}, u32[]{:S(2)}) collective-permute-start(bf16[128,1024]{1,0:T(8,128)(2,1)S(1)} %get-tuple-element.199.refs_0_), channel_id=1, source_target_pairs={{0,1},{1,0},{2,3},{3,2},{4,5},{5,4},{6,7},{7,6},{8,9},{9,8},{10,11... | collective-permute-start | bytes 786440 | tf_op jit(solution)/shard_map/ppermute | solution.py:22
  95.1 0.6 collective-permute-done.38.refs_1_
  97.2 1.5 %collective-permute-start.39 = (bf16[32,1024]{1,0:T(8,128)(2,1)S(1)}, bf16[32,1024]{1,0:T(8,128)(2,1)S(1)}, u32[]{:S(2)}, u32[]{:S(2)}) collective-permute-start(bf16[32,1024]{1,0:T(8,128)(2,1)S(1)} %get-tuple-element.202), channel_id=1, source_target_pairs={{0,6},{2,4},{4,2},{6,0},{1,7},{3,5},{5,3},{7,1},{8,14},{10,12},{12... | collective-permute-start | bytes 196616 | tf_op jit(solution)/shard_map/ppermute | solution.py:31
  98.7 2.1 %collective-permute-start.41 = (bf16[32,1024]{1,0:T(8,128)(2,1)S(1)}, bf16[32,1024]{1,0:T(8,128)(2,1)S(1)}, u32[]{:S(2)}, u32[]{:S(2)}) collective-permute-start(bf16[32,1024]{1,0:T(8,128)(2,1)S(1)} %get-tuple-element.204), channel_id=1, source_target_pairs={{0,2},{2,0},{4,6},{6,4},{1,3},{3,1},{5,7},{7,5},{8,10},{10,8},{12,... | collective-permute-start | bytes 196616 | tf_op jit(solution)/shard_map/ppermute | solution.py:31
  101.2 1.3 grad_begun.2.refs_3_
  102.6 3.3 %collective-permute-done.40.refs_2_ = bf16[32,1024]{1,0:T(8,128)(2,1)S(1)} collective-permute-done((bf16[32,1024]{1,0:T(8,128)(2,1)S(1)}, bf16[32,1024]{1,0:T(8,128)(2,1)S(1)}, u32[]{:S(2)}, u32[]{:S(2)}) %collective-permute-start.40) | collective-permute-done | bytes 65568 | tf_op jit(solution)/shard_map/ppermute | solution.py:31
  105.9 1.9 %collective-permute-start.43 = (bf16[32,1024]{1,0:T(8,128)(2,1)S(1)}, bf16[32,1024]{1,0:T(8,128)(2,1)S(1)}, u32[]{:S(2)}, u32[]{:S(2)}) collective-permute-start(bf16[32,1024]{1,0:T(8,128)(2,1)S(1)} %leave_back.3.refs_4_), channel_id=1, source_target_pairs={{8,0},{16,8},{24,16},{9,1},{17,9},{25,17},{10,2},{18,10},{26,18},{... | collective-permute-start | bytes 196616 | tf_op jit(solution)/shard_map/ppermute | solution.py:17
  107.9 1.5 %collective-permute-start.42 = (bf16[32,1024]{1,0:T(8,128)(2,1)S(1)}, bf16[32,1024]{1,0:T(8,128)(2,1)S(1)}, u32[]{:S(2)}, u32[]{:S(2)}) collective-permute-start(bf16[32,1024]{1,0:T(8,128)(2,1)S(1)} %get-tuple-element.214), channel_id=1, source_target_pairs={{0,6},{2,4},{4,2},{6,0},{1,7},{3,5},{5,3},{7,1},{8,14},{10,12},{12... | collective-permute-start | bytes 196616 | tf_op jit(solution)/shard_map/ppermute | solution.py:31
  109.4 2.4 %collective-permute-done.43.arrived = bf16[32,1024]{1,0:T(8,128)(2,1)S(1)} collective-permute-done((bf16[32,1024]{1,0:T(8,128)(2,1)S(1)}, bf16[32,1024]{1,0:T(8,128)(2,1)S(1)}, u32[]{:S(2)}, u32[]{:S(2)}) %collective-permute-start.43) | collective-permute-done | bytes 65568 | tf_op jit(solution)/shard_map/ppermute | solution.py:17
  111.9 1.5 %collective-permute-start.46 = (bf16[32,1024]{1,0:T(8,128)(2,1)S(1)}, bf16[32,1024]{1,0:T(8,128)(2,1)S(1)}, u32[]{:S(2)}, u32[]{:S(2)}) collective-permute-start(bf16[32,1024]{1,0:T(8,128)(2,1)S(1)} %arrive.7.refs_3_.first), channel_id=1, source_target_pairs={{0,6},{2,4},{4,2},{6,0},{1,7},{3,5},{5,3},{7,1},{8,14},{10,12},{12... | collective-permute-start | bytes 196616 | tf_op jit(solution)/shard_map/ppermute | solution.py:31
  113.4 2.1 %collective-permute-start.44 = (bf16[32,1024]{1,0:T(8,128)(2,1)S(1)}, bf16[32,1024]{1,0:T(8,128)(2,1)S(1)}, u32[]{:S(2)}, u32[]{:S(2)}) collective-permute-start(bf16[32,1024]{1,0:T(8,128)(2,1)S(1)} %arrive.7.refs_3_.first), channel_id=1, source_target_pairs={{0,2},{2,0},{4,6},{6,4},{1,3},{3,1},{5,7},{7,5},{8,10},{10,8},{12,... | collective-permute-start | bytes 196616 | tf_op jit(solution)/shard_map/ppermute | solution.py:31
  115.5 0.8 finish_forward.1
  116.2 1.3 grad_begun.3.refs_7_
  117.5 1.8 %collective-permute-done.45.refs_1_ = bf16[32,1024]{1,0:T(8,128)(2,1)S(1)} collective-permute-done((bf16[32,1024]{1,0:T(8,128)(2,1)S(1)}, bf16[32,1024]{1,0:T(8,128)(2,1)S(1)}, u32[]{:S(2)}, u32[]{:S(2)}) %collective-permute-start.45) | collective-permute-done | bytes 65568 | tf_op jit(solution)/shard_map/ppermute | solution.py:31
  119.8 2.2 %collective-permute-start.48 = (bf16[128,1024]{1,0:T(8,128)(2,1)S(1)}, bf16[128,1024]{1,0:T(8,128)(2,1)S(1)}, u32[]{:S(2)}, u32[]{:S(2)}) collective-permute-start(bf16[128,1024]{1,0:T(8,128)(2,1)S(1)} %get-tuple-element.225.refs_0_), channel_id=1, source_target_pairs={{0,1},{1,0},{2,3},{3,2},{4,5},{5,4},{6,7},{7,6},{8,9},{9,8},{10,11... | collective-permute-start | bytes 786440 | tf_op jit(solution)/shard_map/ppermute | solution.py:22
  122.5 0.6 collective-permute-done.48.refs_1_
  124.6 1.9 %collective-permute-start.49 = (bf16[32,1024]{1,0:T(8,128)(2,1)S(1)}, bf16[32,1024]{1,0:T(8,128)(2,1)S(1)}, u32[]{:S(2)}, u32[]{:S(2)}) collective-permute-start(bf16[32,1024]{1,0:T(8,128)(2,1)S(1)} %get-tuple-element.230), channel_id=1, source_target_pairs={{0,6},{2,4},{4,2},{6,0},{1,7},{3,5},{5,3},{7,1},{8,14},{10,12},{12... | collective-permute-start | bytes 196616 | tf_op jit(solution)/shard_map/ppermute | solution.py:31
  126.5 1.8 %collective-permute-start.51 = (bf16[32,1024]{1,0:T(8,128)(2,1)S(1)}, bf16[32,1024]{1,0:T(8,128)(2,1)S(1)}, u32[]{:S(2)}, u32[]{:S(2)}) collective-permute-start(bf16[32,1024]{1,0:T(8,128)(2,1)S(1)} %get-tuple-element.232), channel_id=1, source_target_pairs={{0,2},{2,0},{4,6},{6,4},{1,3},{3,1},{5,7},{7,5},{8,10},{10,8},{12,... | collective-permute-start | bytes 196616 | tf_op jit(solution)/shard_map/ppermute | solution.py:31
  128.2 3.8 %grads_ended.1 = (bf16[1024,2048]{1,0:T(8,128)(2,1)}, bf16[2048,1024]{1,0:T(8,128)(2,1)}) custom-call(bf16[1024,128]{1,0:T(8,128)(2,1)S(1)} %turned.9.refs_0_, bf16[128,1024]{1,0:T(8,128)(2,1)S(1)} %get-tuple-element.228.refs_1_, bf16[128,1024]{1,0:T(8,128)(2,1)S(1)} %get-tuple-element.229.refs_2_, f32[1024,2048]{1,0:T(8,128)S(1)} %grad_begun.2.refs_3_, ...), custom_call_target="tpu_custom_call" | custom-call | flops 1073741824 | bytes 8388608 | tf_op jit(solution)/shard_map/grads_ended/pallas_call | solution.py:385
  132.1 1.3 collective-permute-done.50.refs_2_
  133.3 0.7 finish.1
  (93 shorter events, 15.5 us)
Async XLA Ops:
  1.5 7.3 %collective-permute-start.2 = (bf16[32,1024]{1,0:T(8,128)(2,1)S(1)}, bf16[32,1024]{1,0:T(8,128)(2,1)S(1)}, u32[]{:S(2)}, u32[]{:S(2)}) collective-permute-start(bf16[32,1024]{1,0:T(8,128)(2,1)S(1)} %get-tuple-element.128.refs_3_.first.refs_0_), channel_id=1, source_target_pairs={{0,6},{2,4},{4,2},{6,0},{1,7},{3,5},{5,3},{7,1},{8,14},{10,12},{12... | collective-permute-start | bytes 196616 | tf_op jit(solution)/shard_map/ppermute | solution.py:31
  4.9 5.9 %collective-permute-start.1 = (bf16[32,1024]{1,0:T(8,128)(2,1)S(1)}, bf16[32,1024]{1,0:T(8,128)(2,1)S(1)}, u32[]{:S(2)}, u32[]{:S(2)}) collective-permute-start(bf16[32,1024]{1,0:T(8,128)(2,1)S(1)} %get-tuple-element.128.refs_3_.first.refs_0_), channel_id=1, source_target_pairs={{0,4},{2,6},{4,0},{6,2},{1,5},{3,7},{5,1},{7,3},{8,12},{10,14},{12... | collective-permute-start | bytes 196616 | tf_op jit(solution)/shard_map/ppermute | solution.py:31
  4.9 5.9 %collective-permute-start = (bf16[32,1024]{1,0:T(8,128)(2,1)S(1)}, bf16[32,1024]{1,0:T(8,128)(2,1)S(1)}, u32[]{:S(2)}, u32[]{:S(2)}) collective-permute-start(bf16[32,1024]{1,0:T(8,128)(2,1)S(1)} %get-tuple-element.128.refs_3_.first.refs_0_), channel_id=1, source_target_pairs={{0,2},{2,0},{4,6},{6,4},{1,3},{3,1},{5,7},{7,5},{8,10},{10,8},{12,... | collective-permute-start | bytes 196616 | tf_op jit(solution)/shard_map/ppermute | solution.py:31
  11.3 1.9 %collective-permute-start.4 = (bf16[128,1024]{1,0:T(8,128)(2,1)S(1)}, bf16[128,1024]{1,0:T(8,128)(2,1)S(1)}, u32[]{:S(2)}, u32[]{:S(2)}) collective-permute-start(bf16[128,1024]{1,0:T(8,128)(2,1)S(1)} %get-tuple-element.131.refs_0_.refs_2_), channel_id=1, source_target_pairs={{0,1},{1,0},{2,3},{3,2},{4,5},{5,4},{6,7},{7,6},{8,9},{9,8},{10,11... | collective-permute-start | bytes 786440 | tf_op jit(solution)/shard_map/ppermute | solution.py:22
  12.5 1.6 %collective-permute-start.3 = (bf16[128,1024]{1,0:T(8,128)(2,1)S(1)}, bf16[128,1024]{1,0:T(8,128)(2,1)S(1)}, u32[]{:S(2)}, u32[]{:S(2)}) collective-permute-start(bf16[128,1024]{1,0:T(8,128)(2,1)S(1)} %product_part.6.refs_0_.refs_2_), channel_id=1, source_target_pairs={{0,1},{1,0},{2,3},{3,2},{4,5},{5,4},{6,7},{7,6},{8,9},{9,8},{10,11... | collective-permute-start | bytes 786440 | tf_op jit(solution)/shard_map/ppermute | solution.py:22
  14.5 6.6 %collective-permute-start.5 = (bf16[32,1024]{1,0:T(8,128)(2,1)S(1)}, bf16[32,1024]{1,0:T(8,128)(2,1)S(1)}, u32[]{:S(2)}, u32[]{:S(2)}) collective-permute-start(bf16[32,1024]{1,0:T(8,128)(2,1)S(1)} %get-tuple-element.134), channel_id=1, source_target_pairs={{0,6},{2,4},{4,2},{6,0},{1,7},{3,5},{5,3},{7,1},{8,14},{10,12},{12... | collective-permute-start | bytes 196616 | tf_op jit(solution)/shard_map/ppermute | solution.py:31
  17.0 6.4 %collective-permute-start.6 = (bf16[32,1024]{1,0:T(8,128)(2,1)S(1)}, bf16[32,1024]{1,0:T(8,128)(2,1)S(1)}, u32[]{:S(2)}, u32[]{:S(2)}) collective-permute-start(bf16[32,1024]{1,0:T(8,128)(2,1)S(1)} %get-tuple-element.135), channel_id=1, source_target_pairs={{0,4},{2,6},{4,0},{6,2},{1,5},{3,7},{5,1},{7,3},{8,12},{10,14},{12... | collective-permute-start | bytes 196616 | tf_op jit(solution)/shard_map/ppermute | solution.py:31
  17.0 6.4 %collective-permute-start.7 = (bf16[32,1024]{1,0:T(8,128)(2,1)S(1)}, bf16[32,1024]{1,0:T(8,128)(2,1)S(1)}, u32[]{:S(2)}, u32[]{:S(2)}) collective-permute-start(bf16[32,1024]{1,0:T(8,128)(2,1)S(1)} %get-tuple-element.136), channel_id=1, source_target_pairs={{0,2},{2,0},{4,6},{6,4},{1,3},{3,1},{5,7},{7,5},{8,10},{10,8},{12,... | collective-permute-start | bytes 196616 | tf_op jit(solution)/shard_map/ppermute | solution.py:31
  18.1 1.2 copy-start
  23.5 5.6 %collective-permute-start.8 = (bf16[32,1024]{1,0:T(8,128)(2,1)S(1)}, bf16[32,1024]{1,0:T(8,128)(2,1)S(1)}, u32[]{:S(2)}, u32[]{:S(2)}) collective-permute-start(bf16[32,1024]{1,0:T(8,128)(2,1)S(1)} %get-tuple-element.143), channel_id=1, source_target_pairs={{0,8},{8,16},{16,24},{1,9},{9,17},{17,25},{2,10},{10,18},{18,26},{... | collective-permute-start | bytes 196616 | tf_op jit(solution)/shard_map/ppermute | solution.py:17
  26.6 6.1 %collective-permute-start.10 = (bf16[32,1024]{1,0:T(8,128)(2,1)S(1)}, bf16[32,1024]{1,0:T(8,128)(2,1)S(1)}, u32[]{:S(2)}, u32[]{:S(2)}) collective-permute-start(bf16[32,1024]{1,0:T(8,128)(2,1)S(1)} %get-tuple-element.164.refs_3_.first), channel_id=1, source_target_pairs={{0,4},{2,6},{4,0},{6,2},{1,5},{3,7},{5,1},{7,3},{8,12},{10,14},{12... | collective-permute-start | bytes 196616 | tf_op jit(solution)/shard_map/ppermute | solution.py:31
  26.7 6.0 %collective-permute-start.9 = (bf16[32,1024]{1,0:T(8,128)(2,1)S(1)}, bf16[32,1024]{1,0:T(8,128)(2,1)S(1)}, u32[]{:S(2)}, u32[]{:S(2)}) collective-permute-start(bf16[32,1024]{1,0:T(8,128)(2,1)S(1)} %get-tuple-element.164.refs_3_.first), channel_id=1, source_target_pairs={{0,2},{2,0},{4,6},{6,4},{1,3},{3,1},{5,7},{7,5},{8,10},{10,8},{12,... | collective-permute-start | bytes 196616 | tf_op jit(solution)/shard_map/ppermute | solution.py:31
  29.1 5.1 %collective-permute-start.13 = (bf16[32,1024]{1,0:T(8,128)(2,1)S(1)}, bf16[32,1024]{1,0:T(8,128)(2,1)S(1)}, u32[]{:S(2)}, u32[]{:S(2)}) collective-permute-start(bf16[32,1024]{1,0:T(8,128)(2,1)S(1)} %arrive.4.refs_5_.first.refs_1_), channel_id=1, source_target_pairs={{0,6},{2,4},{4,2},{6,0},{1,7},{3,5},{5,3},{7,1},{8,14},{10,12},{12... | collective-permute-start | bytes 196616 | tf_op jit(solution)/shard_map/ppermute | solution.py:31
  30.7 7.3 %collective-permute-start.12 = (bf16[32,1024]{1,0:T(8,128)(2,1)S(1)}, bf16[32,1024]{1,0:T(8,128)(2,1)S(1)}, u32[]{:S(2)}, u32[]{:S(2)}) collective-permute-start(bf16[32,1024]{1,0:T(8,128)(2,1)S(1)} %arrive.4.refs_5_.first.refs_1_), channel_id=1, source_target_pairs={{0,4},{2,6},{4,0},{6,2},{1,5},{3,7},{5,1},{7,3},{8,12},{10,14},{12... | collective-permute-start | bytes 196616 | tf_op jit(solution)/shard_map/ppermute | solution.py:31
  30.7 7.3 %collective-permute-start.11 = (bf16[32,1024]{1,0:T(8,128)(2,1)S(1)}, bf16[32,1024]{1,0:T(8,128)(2,1)S(1)}, u32[]{:S(2)}, u32[]{:S(2)}) collective-permute-start(bf16[32,1024]{1,0:T(8,128)(2,1)S(1)} %arrive.4.refs_5_.first.refs_1_), channel_id=1, source_target_pairs={{0,2},{2,0},{4,6},{6,4},{1,3},{3,1},{5,7},{7,5},{8,10},{10,8},{12,... | collective-permute-start | bytes 196616 | tf_op jit(solution)/shard_map/ppermute | solution.py:31
  38.4 2.2 %collective-permute-start.15 = (bf16[128,1024]{1,0:T(8,128)(2,1)S(1)}, bf16[128,1024]{1,0:T(8,128)(2,1)S(1)}, u32[]{:S(2)}, u32[]{:S(2)}) collective-permute-start(bf16[128,1024]{1,0:T(8,128)(2,1)S(1)} %get-tuple-element.148.refs_0_.refs_2_), channel_id=1, source_target_pairs={{0,1},{1,0},{2,3},{3,2},{4,5},{5,4},{6,7},{7,6},{8,9},{9,8},{10,11... | collective-permute-start | bytes 786440 | tf_op jit(solution)/shard_map/ppermute | solution.py:22
  39.9 1.6 %collective-permute-start.14 = (bf16[128,1024]{1,0:T(8,128)(2,1)S(1)}, bf16[128,1024]{1,0:T(8,128)(2,1)S(1)}, u32[]{:S(2)}, u32[]{:S(2)}) collective-permute-start(bf16[128,1024]{1,0:T(8,128)(2,1)S(1)} %product_part.7.refs_0_.refs_2_), channel_id=1, source_target_pairs={{0,1},{1,0},{2,3},{3,2},{4,5},{5,4},{6,7},{7,6},{8,9},{9,8},{10,11... | collective-permute-start | bytes 786440 | tf_op jit(solution)/shard_map/ppermute | solution.py:22
  42.0 5.4 %collective-permute-start.16 = (bf16[32,1024]{1,0:T(8,128)(2,1)S(1)}, bf16[32,1024]{1,0:T(8,128)(2,1)S(1)}, u32[]{:S(2)}, u32[]{:S(2)}) collective-permute-start(bf16[32,1024]{1,0:T(8,128)(2,1)S(1)} %get-tuple-element.151), channel_id=1, source_target_pairs={{0,6},{2,4},{4,2},{6,0},{1,7},{3,5},{5,3},{7,1},{8,14},{10,12},{12... | collective-permute-start | bytes 196616 | tf_op jit(solution)/shard_map/ppermute | solution.py:31
  43.6 7.0 %collective-permute-start.17 = (bf16[32,1024]{1,0:T(8,128)(2,1)S(1)}, bf16[32,1024]{1,0:T(8,128)(2,1)S(1)}, u32[]{:S(2)}, u32[]{:S(2)}) collective-permute-start(bf16[32,1024]{1,0:T(8,128)(2,1)S(1)} %get-tuple-element.152), channel_id=1, source_target_pairs={{0,4},{2,6},{4,0},{6,2},{1,5},{3,7},{5,1},{7,3},{8,12},{10,14},{12... | collective-permute-start | bytes 196616 | tf_op jit(solution)/shard_map/ppermute | solution.py:31
  43.6 7.0 %collective-permute-start.18 = (bf16[32,1024]{1,0:T(8,128)(2,1)S(1)}, bf16[32,1024]{1,0:T(8,128)(2,1)S(1)}, u32[]{:S(2)}, u32[]{:S(2)}) collective-permute-start(bf16[32,1024]{1,0:T(8,128)(2,1)S(1)} %get-tuple-element.153), channel_id=1, source_target_pairs={{0,2},{2,0},{4,6},{6,4},{1,3},{3,1},{5,7},{7,5},{8,10},{10,8},{12,... | collective-permute-start | bytes 196616 | tf_op jit(solution)/shard_map/ppermute | solution.py:31
  50.7 5.3 %collective-permute-start.19 = (bf16[32,1024]{1,0:T(8,128)(2,1)S(1)}, bf16[32,1024]{1,0:T(8,128)(2,1)S(1)}, u32[]{:S(2)}, u32[]{:S(2)}) collective-permute-start(bf16[32,1024]{1,0:T(8,128)(2,1)S(1)} %get-tuple-element.161), channel_id=1, source_target_pairs={{0,8},{8,16},{16,24},{1,9},{9,17},{17,25},{2,10},{10,18},{18,26},{... | collective-permute-start | bytes 196616 | tf_op jit(solution)/shard_map/ppermute | solution.py:17
  54.2 5.5 %collective-permute-start.23 = (bf16[32,1024]{1,0:T(8,128)(2,1)S(1)}, bf16[32,1024]{1,0:T(8,128)(2,1)S(1)}, u32[]{:S(2)}, u32[]{:S(2)}) collective-permute-start(bf16[32,1024]{1,0:T(8,128)(2,1)S(1)} %get-tuple-element.164.refs_3_.first), channel_id=1, source_target_pairs={{0,6},{2,4},{4,2},{6,0},{1,7},{3,5},{5,3},{7,1},{8,14},{10,12},{12... | collective-permute-start | bytes 196616 | tf_op jit(solution)/shard_map/ppermute | solution.py:31
  56.1 6.8 %collective-permute-start.22 = (bf16[32,1024]{1,0:T(8,128)(2,1)S(1)}, bf16[32,1024]{1,0:T(8,128)(2,1)S(1)}, u32[]{:S(2)}, u32[]{:S(2)}) collective-permute-start(bf16[32,1024]{1,0:T(8,128)(2,1)S(1)} %arrive.5.refs_3_.refs_2_), channel_id=1, source_target_pairs={{0,6},{2,4},{4,2},{6,0},{1,7},{3,5},{5,3},{7,1},{8,14},{10,12},{12... | collective-permute-start | bytes 196616 | tf_op jit(solution)/shard_map/ppermute | solution.py:31
  57.7 7.3 %collective-permute-start.21 = (bf16[32,1024]{1,0:T(8,128)(2,1)S(1)}, bf16[32,1024]{1,0:T(8,128)(2,1)S(1)}, u32[]{:S(2)}, u32[]{:S(2)}) collective-permute-start(bf16[32,1024]{1,0:T(8,128)(2,1)S(1)} %arrive.5.refs_3_.refs_2_), channel_id=1, source_target_pairs={{0,4},{2,6},{4,0},{6,2},{1,5},{3,7},{5,1},{7,3},{8,12},{10,14},{12... | collective-permute-start | bytes 196616 | tf_op jit(solution)/shard_map/ppermute | solution.py:31
  57.7 7.3 %collective-permute-start.20 = (bf16[32,1024]{1,0:T(8,128)(2,1)S(1)}, bf16[32,1024]{1,0:T(8,128)(2,1)S(1)}, u32[]{:S(2)}, u32[]{:S(2)}) collective-permute-start(bf16[32,1024]{1,0:T(8,128)(2,1)S(1)} %arrive.5.refs_3_.refs_2_), channel_id=1, source_target_pairs={{0,2},{2,0},{4,6},{6,4},{1,3},{3,1},{5,7},{7,5},{8,10},{10,8},{12,... | collective-permute-start | bytes 196616 | tf_op jit(solution)/shard_map/ppermute | solution.py:31
  60.6 7.7 %collective-permute-start.26 = (bf16[128,1024]{1,0:T(8,128)(2,1)S(1)}, bf16[128,1024]{1,0:T(8,128)(2,1)S(1)}, u32[]{:S(2)}, u32[]{:S(2)}) collective-permute-start(bf16[128,1024]{1,0:T(8,128)(2,1)S(1)} %product_part.8.refs_0_), channel_id=1, source_target_pairs={{0,1},{1,0},{2,3},{3,2},{4,5},{5,4},{6,7},{7,6},{8,9},{9,8},{10,11... | collective-permute-start | bytes 786440 | tf_op jit(solution)/shard_map/ppermute | solution.py:22
  62.8 4.3 %collective-permute-start.27 = (bf16[128,1024]{1,0:T(8,128)(2,1)S(1)}, bf16[128,1024]{1,0:T(8,128)(2,1)S(1)}, u32[]{:S(2)}, u32[]{:S(2)}) collective-permute-start(bf16[128,1024]{1,0:T(8,128)(2,1)S(1)} %get-tuple-element.165.refs_0_), channel_id=1, source_target_pairs={{0,1},{1,0},{2,3},{3,2},{4,5},{5,4},{6,7},{7,6},{8,9},{9,8},{10,11... | collective-permute-start | bytes 786440 | tf_op jit(solution)/shard_map/ppermute | solution.py:22
  65.5 2.3 %collective-permute-start.24 = (bf16[128,1024]{1,0:T(8,128)(2,1)S(1)}, bf16[128,1024]{1,0:T(8,128)(2,1)S(1)}, u32[]{:S(2)}, u32[]{:S(2)}) collective-permute-start(bf16[128,1024]{1,0:T(8,128)(2,1)S(1)} %get-tuple-element.184.refs_2_.refs_0_), channel_id=1, source_target_pairs={{0,1},{1,0},{2,3},{3,2},{4,5},{5,4},{6,7},{7,6},{8,9},{9,8},{10,11... | collective-permute-start | bytes 786440 | tf_op jit(solution)/shard_map/ppermute | solution.py:22
  67.0 1.6 %collective-permute-start.25 = (bf16[128,1024]{1,0:T(8,128)(2,1)S(1)}, bf16[128,1024]{1,0:T(8,128)(2,1)S(1)}, u32[]{:S(2)}, u32[]{:S(2)}) collective-permute-start(bf16[128,1024]{1,0:T(8,128)(2,1)S(1)} %product_part.9.refs_2_), channel_id=1, source_target_pairs={{0,1},{1,0},{2,3},{3,2},{4,5},{5,4},{6,7},{7,6},{8,9},{9,8},{10,11... | collective-permute-start | bytes 786440 | tf_op jit(solution)/shard_map/ppermute | solution.py:22
  69.2 5.4 %collective-permute-start.28 = (bf16[32,1024]{1,0:T(8,128)(2,1)S(1)}, bf16[32,1024]{1,0:T(8,128)(2,1)S(1)}, u32[]{:S(2)}, u32[]{:S(2)}) collective-permute-start(bf16[32,1024]{1,0:T(8,128)(2,1)S(1)} %get-tuple-element.175), channel_id=1, source_target_pairs={{0,6},{2,4},{4,2},{6,0},{1,7},{3,5},{5,3},{7,1},{8,14},{10,12},{12... | collective-permute-start | bytes 196616 | tf_op jit(solution)/shard_map/ppermute | solution.py:31
  71.0 6.9 %collective-permute-start.29 = (bf16[32,1024]{1,0:T(8,128)(2,1)S(1)}, bf16[32,1024]{1,0:T(8,128)(2,1)S(1)}, u32[]{:S(2)}, u32[]{:S(2)}) collective-permute-start(bf16[32,1024]{1,0:T(8,128)(2,1)S(1)} %get-tuple-element.176), channel_id=1, source_target_pairs={{0,4},{2,6},{4,0},{6,2},{1,5},{3,7},{5,1},{7,3},{8,12},{10,14},{12... | collective-permute-start | bytes 196616 | tf_op jit(solution)/shard_map/ppermute | solution.py:31
  71.1 6.9 %collective-permute-start.30 = (bf16[32,1024]{1,0:T(8,128)(2,1)S(1)}, bf16[32,1024]{1,0:T(8,128)(2,1)S(1)}, u32[]{:S(2)}, u32[]{:S(2)}) collective-permute-start(bf16[32,1024]{1,0:T(8,128)(2,1)S(1)} %get-tuple-element.177), channel_id=1, source_target_pairs={{0,2},{2,0},{4,6},{6,4},{1,3},{3,1},{5,7},{7,5},{8,10},{10,8},{12,... | collective-permute-start | bytes 196616 | tf_op jit(solution)/shard_map/ppermute | solution.py:31
  78.0 5.9 %collective-permute-start.31 = (bf16[32,1024]{1,0:T(8,128)(2,1)S(1)}, bf16[32,1024]{1,0:T(8,128)(2,1)S(1)}, u32[]{:S(2)}, u32[]{:S(2)}) collective-permute-start(bf16[32,1024]{1,0:T(8,128)(2,1)S(1)} %leave_back.2.refs_5_), channel_id=1, source_target_pairs={{8,0},{16,8},{24,16},{9,1},{17,9},{25,17},{10,2},{18,10},{26,18},{... | collective-permute-start | bytes 196616 | tf_op jit(solution)/shard_map/ppermute | solution.py:17
  81.0 6.5 %collective-permute-start.32 = (bf16[32,1024]{1,0:T(8,128)(2,1)S(1)}, bf16[32,1024]{1,0:T(8,128)(2,1)S(1)}, u32[]{:S(2)}, u32[]{:S(2)}) collective-permute-start(bf16[32,1024]{1,0:T(8,128)(2,1)S(1)} %get-tuple-element.196), channel_id=1, source_target_pairs={{0,2},{2,0},{4,6},{6,4},{1,3},{3,1},{5,7},{7,5},{8,10},{10,8},{12,... | collective-permute-start | bytes 196616 | tf_op jit(solution)/shard_map/ppermute | solution.py:31
  81.1 6.4 %collective-permute-start.33 = (bf16[32,1024]{1,0:T(8,128)(2,1)S(1)}, bf16[32,1024]{1,0:T(8,128)(2,1)S(1)}, u32[]{:S(2)}, u32[]{:S(2)}) collective-permute-start(bf16[32,1024]{1,0:T(8,128)(2,1)S(1)} %get-tuple-element.197), channel_id=1, source_target_pairs={{0,4},{2,6},{4,0},{6,2},{1,5},{3,7},{5,1},{7,3},{8,12},{10,14},{12... | collective-permute-start | bytes 196616 | tf_op jit(solution)/shard_map/ppermute | solution.py:31
  83.9 5.1 %collective-permute-start.36 = (bf16[32,1024]{1,0:T(8,128)(2,1)S(1)}, bf16[32,1024]{1,0:T(8,128)(2,1)S(1)}, u32[]{:S(2)}, u32[]{:S(2)}) collective-permute-start(bf16[32,1024]{1,0:T(8,128)(2,1)S(1)} %arrive.6.refs_5_.first), channel_id=1, source_target_pairs={{0,6},{2,4},{4,2},{6,0},{1,7},{3,5},{5,3},{7,1},{8,14},{10,12},{12... | collective-permute-start | bytes 196616 | tf_op jit(solution)/shard_map/ppermute | solution.py:31
  85.7 6.9 %collective-permute-start.35 = (bf16[32,1024]{1,0:T(8,128)(2,1)S(1)}, bf16[32,1024]{1,0:T(8,128)(2,1)S(1)}, u32[]{:S(2)}, u32[]{:S(2)}) collective-permute-start(bf16[32,1024]{1,0:T(8,128)(2,1)S(1)} %arrive.6.refs_5_.first), channel_id=1, source_target_pairs={{0,4},{2,6},{4,0},{6,2},{1,5},{3,7},{5,1},{7,3},{8,12},{10,14},{12... | collective-permute-start | bytes 196616 | tf_op jit(solution)/shard_map/ppermute | solution.py:31
  85.7 6.9 %collective-permute-start.34 = (bf16[32,1024]{1,0:T(8,128)(2,1)S(1)}, bf16[32,1024]{1,0:T(8,128)(2,1)S(1)}, u32[]{:S(2)}, u32[]{:S(2)}) collective-permute-start(bf16[32,1024]{1,0:T(8,128)(2,1)S(1)} %arrive.6.refs_5_.first), channel_id=1, source_target_pairs={{0,2},{2,0},{4,6},{6,4},{1,3},{3,1},{5,7},{7,5},{8,10},{10,8},{12,... | collective-permute-start | bytes 196616 | tf_op jit(solution)/shard_map/ppermute | solution.py:31
  93.1 2.6 %collective-permute-start.38 = (bf16[128,1024]{1,0:T(8,128)(2,1)S(1)}, bf16[128,1024]{1,0:T(8,128)(2,1)S(1)}, u32[]{:S(2)}, u32[]{:S(2)}) collective-permute-start(bf16[128,1024]{1,0:T(8,128)(2,1)S(1)} %get-tuple-element.199.refs_0_), channel_id=1, source_target_pairs={{0,1},{1,0},{2,3},{3,2},{4,5},{5,4},{6,7},{7,6},{8,9},{9,8},{10,11... | collective-permute-start | bytes 786440 | tf_op jit(solution)/shard_map/ppermute | solution.py:22
  95.0 1.6 %collective-permute-start.37 = (bf16[128,1024]{1,0:T(8,128)(2,1)S(1)}, bf16[128,1024]{1,0:T(8,128)(2,1)S(1)}, u32[]{:S(2)}, u32[]{:S(2)}) collective-permute-start(bf16[128,1024]{1,0:T(8,128)(2,1)S(1)} %product_part.10.refs_0_), channel_id=1, source_target_pairs={{0,1},{1,0},{2,3},{3,2},{4,5},{5,4},{6,7},{7,6},{8,9},{9,8},{10,11... | collective-permute-start | bytes 786440 | tf_op jit(solution)/shard_map/ppermute | solution.py:22
  97.2 5.4 %collective-permute-start.39 = (bf16[32,1024]{1,0:T(8,128)(2,1)S(1)}, bf16[32,1024]{1,0:T(8,128)(2,1)S(1)}, u32[]{:S(2)}, u32[]{:S(2)}) collective-permute-start(bf16[32,1024]{1,0:T(8,128)(2,1)S(1)} %get-tuple-element.202), channel_id=1, source_target_pairs={{0,6},{2,4},{4,2},{6,0},{1,7},{3,5},{5,3},{7,1},{8,14},{10,12},{12... | collective-permute-start | bytes 196616 | tf_op jit(solution)/shard_map/ppermute | solution.py:31
  98.7 7.1 %collective-permute-start.40 = (bf16[32,1024]{1,0:T(8,128)(2,1)S(1)}, bf16[32,1024]{1,0:T(8,128)(2,1)S(1)}, u32[]{:S(2)}, u32[]{:S(2)}) collective-permute-start(bf16[32,1024]{1,0:T(8,128)(2,1)S(1)} %get-tuple-element.203), channel_id=1, source_target_pairs={{0,4},{2,6},{4,0},{6,2},{1,5},{3,7},{5,1},{7,3},{8,12},{10,14},{12... | collective-permute-start | bytes 196616 | tf_op jit(solution)/shard_map/ppermute | solution.py:31
  98.7 7.1 %collective-permute-start.41 = (bf16[32,1024]{1,0:T(8,128)(2,1)S(1)}, bf16[32,1024]{1,0:T(8,128)(2,1)S(1)}, u32[]{:S(2)}, u32[]{:S(2)}) collective-permute-start(bf16[32,1024]{1,0:T(8,128)(2,1)S(1)} %get-tuple-element.204), channel_id=1, source_target_pairs={{0,2},{2,0},{4,6},{6,4},{1,3},{3,1},{5,7},{7,5},{8,10},{10,8},{12,... | collective-permute-start | bytes 196616 | tf_op jit(solution)/shard_map/ppermute | solution.py:31
  105.9 5.9 %collective-permute-start.43 = (bf16[32,1024]{1,0:T(8,128)(2,1)S(1)}, bf16[32,1024]{1,0:T(8,128)(2,1)S(1)}, u32[]{:S(2)}, u32[]{:S(2)}) collective-permute-start(bf16[32,1024]{1,0:T(8,128)(2,1)S(1)} %leave_back.3.refs_4_), channel_id=1, source_target_pairs={{8,0},{16,8},{24,16},{9,1},{17,9},{25,17},{10,2},{18,10},{26,18},{... | collective-permute-start | bytes 196616 | tf_op jit(solution)/shard_map/ppermute | solution.py:17
  107.9 7.6 %collective-permute-start.42 = (bf16[32,1024]{1,0:T(8,128)(2,1)S(1)}, bf16[32,1024]{1,0:T(8,128)(2,1)S(1)}, u32[]{:S(2)}, u32[]{:S(2)}) collective-permute-start(bf16[32,1024]{1,0:T(8,128)(2,1)S(1)} %get-tuple-element.214), channel_id=1, source_target_pairs={{0,6},{2,4},{4,2},{6,0},{1,7},{3,5},{5,3},{7,1},{8,14},{10,12},{12... | collective-permute-start | bytes 196616 | tf_op jit(solution)/shard_map/ppermute | solution.py:31
  111.9 5.7 %collective-permute-start.46 = (bf16[32,1024]{1,0:T(8,128)(2,1)S(1)}, bf16[32,1024]{1,0:T(8,128)(2,1)S(1)}, u32[]{:S(2)}, u32[]{:S(2)}) collective-permute-start(bf16[32,1024]{1,0:T(8,128)(2,1)S(1)} %arrive.7.refs_3_.first), channel_id=1, source_target_pairs={{0,6},{2,4},{4,2},{6,0},{1,7},{3,5},{5,3},{7,1},{8,14},{10,12},{12... | collective-permute-start | bytes 196616 | tf_op jit(solution)/shard_map/ppermute | solution.py:31
  113.4 5.9 %collective-permute-start.45 = (bf16[32,1024]{1,0:T(8,128)(2,1)S(1)}, bf16[32,1024]{1,0:T(8,128)(2,1)S(1)}, u32[]{:S(2)}, u32[]{:S(2)}) collective-permute-start(bf16[32,1024]{1,0:T(8,128)(2,1)S(1)} %arrive.7.refs_3_.first), channel_id=1, source_target_pairs={{0,4},{2,6},{4,0},{6,2},{1,5},{3,7},{5,1},{7,3},{8,12},{10,14},{12... | collective-permute-start | bytes 196616 | tf_op jit(solution)/shard_map/ppermute | solution.py:31
  113.4 5.9 %collective-permute-start.44 = (bf16[32,1024]{1,0:T(8,128)(2,1)S(1)}, bf16[32,1024]{1,0:T(8,128)(2,1)S(1)}, u32[]{:S(2)}, u32[]{:S(2)}) collective-permute-start(bf16[32,1024]{1,0:T(8,128)(2,1)S(1)} %arrive.7.refs_3_.first), channel_id=1, source_target_pairs={{0,2},{2,0},{4,6},{6,4},{1,3},{3,1},{5,7},{7,5},{8,10},{10,8},{12,... | collective-permute-start | bytes 196616 | tf_op jit(solution)/shard_map/ppermute | solution.py:31
  119.8 3.3 %collective-permute-start.48 = (bf16[128,1024]{1,0:T(8,128)(2,1)S(1)}, bf16[128,1024]{1,0:T(8,128)(2,1)S(1)}, u32[]{:S(2)}, u32[]{:S(2)}) collective-permute-start(bf16[128,1024]{1,0:T(8,128)(2,1)S(1)} %get-tuple-element.225.refs_0_), channel_id=1, source_target_pairs={{0,1},{1,0},{2,3},{3,2},{4,5},{5,4},{6,7},{7,6},{8,9},{9,8},{10,11... | collective-permute-start | bytes 786440 | tf_op jit(solution)/shard_map/ppermute | solution.py:22
  122.4 1.6 %collective-permute-start.47 = (bf16[128,1024]{1,0:T(8,128)(2,1)S(1)}, bf16[128,1024]{1,0:T(8,128)(2,1)S(1)}, u32[]{:S(2)}, u32[]{:S(2)}) collective-permute-start(bf16[128,1024]{1,0:T(8,128)(2,1)S(1)} %product_part.11.refs_0_), channel_id=1, source_target_pairs={{0,1},{1,0},{2,3},{3,2},{4,5},{5,4},{6,7},{7,6},{8,9},{9,8},{10,11... | collective-permute-start | bytes 786440 | tf_op jit(solution)/shard_map/ppermute | solution.py:22
  124.6 7.4 %collective-permute-start.49 = (bf16[32,1024]{1,0:T(8,128)(2,1)S(1)}, bf16[32,1024]{1,0:T(8,128)(2,1)S(1)}, u32[]{:S(2)}, u32[]{:S(2)}) collective-permute-start(bf16[32,1024]{1,0:T(8,128)(2,1)S(1)} %get-tuple-element.230), channel_id=1, source_target_pairs={{0,6},{2,4},{4,2},{6,0},{1,7},{3,5},{5,3},{7,1},{8,14},{10,12},{12... | collective-permute-start | bytes 196616 | tf_op jit(solution)/shard_map/ppermute | solution.py:31
  126.5 6.8 %collective-permute-start.50 = (bf16[32,1024]{1,0:T(8,128)(2,1)S(1)}, bf16[32,1024]{1,0:T(8,128)(2,1)S(1)}, u32[]{:S(2)}, u32[]{:S(2)}) collective-permute-start(bf16[32,1024]{1,0:T(8,128)(2,1)S(1)} %get-tuple-element.231), channel_id=1, source_target_pairs={{0,4},{2,6},{4,0},{6,2},{1,5},{3,7},{5,1},{7,3},{8,12},{10,14},{12... | collective-permute-start | bytes 196616 | tf_op jit(solution)/shard_map/ppermute | solution.py:31
  126.5 6.8 %collective-permute-start.51 = (bf16[32,1024]{1,0:T(8,128)(2,1)S(1)}, bf16[32,1024]{1,0:T(8,128)(2,1)S(1)}, u32[]{:S(2)}, u32[]{:S(2)}) collective-permute-start(bf16[32,1024]{1,0:T(8,128)(2,1)S(1)} %get-tuple-element.232), channel_id=1, source_target_pairs={{0,2},{2,0},{4,6},{6,4},{1,3},{3,1},{5,7},{7,5},{8,10},{10,8},{12,... | collective-permute-start | bytes 196616 | tf_op jit(solution)/shard_map/ppermute | solution.py:31

commit v16 on v15

--- a/solution.py
+++ b/solution.py
@@ -23,7 +23,8 @@
 
 
 def partner(row, j, size):
-    return row ^ ((size - j) % size) if size & (size - 1) == 0 else (j - row) % size
+    away = (size - j) % size
+    return row ^ away ^ (away >> 1) if size & (size - 1) == 0 else (j - row) % size
 
 
 def swap_rows(block, j):

time: 134 us -> 136 us (1.015)
  waiting for transfers between devices: 39.5 us -> 42.3 us
  starting transfers between devices: 64 us -> 62.3 us
    ppermute x36, starting transfers between devices: 44.2 us -> 36.3 us  [swap_rows(): lax.ppermute(block, 'row', [(i, partner(i, j, size)) for i in range(size)])]
    ppermute x12, starting transfers between devices: 9.19 us -> 15.9 us  [turn(): lax.ppermute(block, axis, [(i, (i + distance) % size) for i in range(size)])]
    ppermute x4, waiting for transfers between devices: 3.14 us -> 4.68 us  [hand_over(): lax.ppermute(block, 'section', [(i - distance, i) for i in sections if i...]
  transfers between devices with their start and end apart: 52 -> 52, of which waited for: 27 -> 36; matrix products, arithmetic and copies ran while one was open for 0% -> 0% of each run, Pallas kernels for 17% -> 17%
where the time goes in v16:
time: 136 us; the launch traced here: 135 us
  starting transfers between devices  62.3 us (46%)
  waiting for transfers between devices  42.3 us (31%)
  Pallas kernels  29.4 us (22%)
    ppermute x36, starting transfers between devices, swap_rows(): lax.ppermute(block, 'row', [(i, partner(i, j, size)) for i in range(size)])  36.3 us
    ppermute x36, waiting for transfers between devices, swap_rows(): lax.ppermute(block, 'row', [(i, partner(i, j, size)) for i in range(size)])  32.7 us
    pallas_call x45, Pallas kernels, run(): pl.pallas_call(kernel, in_specs=vmem(len(ins)), out_specs=vmem(len(outs))...  18 us
    ppermute x12, starting transfers between devices, turn(): lax.ppermute(block, axis, [(i, (i + distance) % size) for i in range(size)])  15.9 us
    ppermute x4, starting transfers between devices, hand_over(): lax.ppermute(block, 'section', [(i - distance, i) for i in sections if i...  10.1 us
    ppermute x12, waiting for transfers between devices, turn(): lax.ppermute(block, axis, [(i, (i + distance) % size) for i in range(size)])  4.92 us
    ppermute x4, waiting for transfers between devices, hand_over(): lax.ppermute(block, 'section', [(i - distance, i) for i in sections if i...  4.68 us
    pallas_call x1, Pallas kernels, end_grads(): pl.pallas_call(functools.partial(grads_ended, tuple(((len(lefts), len(rig...  3.8 us
  transfers between devices with their start and end apart: 52, of which 36 were waited for; matrix products, arithmetic and copies ran while one was open for 0% of the time, Pallas kernels for 17%

profile of v16, /device:TPU:3, one launch (start us, length us, event | category | flops | bytes accessed | tf_op | source)
XLA Modules:
  0.0 135.2 jit_solution(16970299106167326580)
XLA Ops:
  0.6 0.9 first.1
  1.5 2.4 %collective-permute-start.2 = (bf16[32,1024]{1,0:T(8,128)(2,1)S(1)}, bf16[32,1024]{1,0:T(8,128)(2,1)S(1)}, u32[]{:S(2)}, u32[]{:S(2)}) collective-permute-start(bf16[32,1024]{1,0:T(8,128)(2,1)S(1)} %get-tuple-element.128.refs_3_.first.refs_0_), channel_id=1, source_target_pairs={{0,4},{2,6},{4,0},{6,2},{1,5},{3,7},{5,1},{7,3},{8,12},{10,14},{12... | collective-permute-start | bytes 196616 | tf_op jit(solution)/shard_map/ppermute | solution.py:32
  3.9 1.1 collective-permute-start.1
  5.2 3.5 %hold.1 = (bf16[1024,2048]{1,0:T(8,128)(2,1)S(1)}, bf16[2048,1024]{1,0:T(8,128)(2,1)S(1)}) custom-call(bf16[1024,2048]{1,0:T(8,128)(2,1)} %bitcast.4, bf16[2048,1024]{1,0:T(8,128)(2,1)} %bitcast.5), custom_call_target="tpu_custom_call" | custom-call | bytes 16777216 | tf_op jit(solution)/shard_map/hold/pallas_call | solution.py:215
  9.7 2.0 %collective-permute-start.4 = (bf16[128,1024]{1,0:T(8,128)(2,1)S(1)}, bf16[128,1024]{1,0:T(8,128)(2,1)S(1)}, u32[]{:S(2)}, u32[]{:S(2)}) collective-permute-start(bf16[128,1024]{1,0:T(8,128)(2,1)S(1)} %get-tuple-element.131.refs_0_.refs_2_), channel_id=1, source_target_pairs={{0,1},{1,0},{2,3},{3,2},{4,5},{5,4},{6,7},{7,6},{8,9},{9,8},{10,11... | collective-permute-start | bytes 786440 | tf_op jit(solution)/shard_map/ppermute | solution.py:22
  12.2 0.6 collective-permute-done.4.refs_1_.refs_3_
  14.2 2.5 %collective-permute-start.5 = (bf16[32,1024]{1,0:T(8,128)(2,1)S(1)}, bf16[32,1024]{1,0:T(8,128)(2,1)S(1)}, u32[]{:S(2)}, u32[]{:S(2)}) collective-permute-start(bf16[32,1024]{1,0:T(8,128)(2,1)S(1)} %get-tuple-element.134), channel_id=1, source_target_pairs={{0,4},{2,6},{4,0},{6,2},{1,5},{3,7},{5,1},{7,3},{8,12},{10,14},{12... | collective-permute-start | bytes 196616 | tf_op jit(solution)/shard_map/ppermute | solution.py:32
  17.3 1.2 turned_weight.2.refs_4_.weight.refs_6_
  18.5 1.7 %fetch.1 = (bf16[32,1024]{1,0:T(8,128)(2,1)S(1)}, bf16[32,1024]{1,0:T(8,128)(2,1)S(1)}, bf16[32,1024]{1,0:T(8,128)(2,1)S(1)}, bf16[32,1024]{1,0:T(8,128)(2,1)S(1...) custom-call(s32[6]{0:T(128)S(1)} %copy-done, bf16[1,3,32,1024]{3,2,1,0:T(8,128)(2,1)} %inputs.3, ...), custom_call_target="tpu_custom_call" | custom-call | bytes 2097152 | tf_op jit(solution)/shard_map/fetch/pallas_call | solution.py:110
  20.4 1.4 %collective-permute-done.6.refs_2_ = bf16[32,1024]{1,0:T(8,128)(2,1)S(1)} collective-permute-done((bf16[32,1024]{1,0:T(8,128)(2,1)S(1)}, bf16[32,1024]{1,0:T(8,128)(2,1)S(1)}, u32[]{:S(2)}, u32[]{:S(2)}) %collective-permute-start.6) | collective-permute-done | bytes 65568 | tf_op jit(solution)/shard_map/ppermute | solution.py:32
  21.8 1.4 %collective-permute-done.7.refs_3_ = bf16[32,1024]{1,0:T(8,128)(2,1)S(1)} collective-permute-done((bf16[32,1024]{1,0:T(8,128)(2,1)S(1)}, bf16[32,1024]{1,0:T(8,128)(2,1)S(1)}, u32[]{:S(2)}, u32[]{:S(2)}) %collective-permute-start.7) | collective-permute-done | bytes 65568 | tf_op jit(solution)/shard_map/ppermute | solution.py:32
  23.3 3.1 %collective-permute-start.8 = (bf16[32,1024]{1,0:T(8,128)(2,1)S(1)}, bf16[32,1024]{1,0:T(8,128)(2,1)S(1)}, u32[]{:S(2)}, u32[]{:S(2)}) collective-permute-start(bf16[32,1024]{1,0:T(8,128)(2,1)S(1)} %get-tuple-element.143), channel_id=1, source_target_pairs={{0,8},{8,16},{16,24},{1,9},{9,17},{17,25},{2,10},{10,18},{18,26},{... | collective-permute-start | bytes 196616 | tf_op jit(solution)/shard_map/ppermute | solution.py:17
  26.3 2.5 %collective-permute-start.10 = (bf16[32,1024]{1,0:T(8,128)(2,1)S(1)}, bf16[32,1024]{1,0:T(8,128)(2,1)S(1)}, u32[]{:S(2)}, u32[]{:S(2)}) collective-permute-start(bf16[32,1024]{1,0:T(8,128)(2,1)S(1)} %get-tuple-element.164.refs_3_.first), channel_id=1, source_target_pairs={{0,6},{2,4},{4,2},{6,0},{1,7},{3,5},{5,3},{7,1},{8,14},{10,12},{12... | collective-permute-start | bytes 196616 | tf_op jit(solution)/shard_map/ppermute | solution.py:32
  28.8 1.2 collective-permute-start.13
  30.0 2.4 %collective-permute-start.12 = (bf16[32,1024]{1,0:T(8,128)(2,1)S(1)}, bf16[32,1024]{1,0:T(8,128)(2,1)S(1)}, u32[]{:S(2)}, u32[]{:S(2)}) collective-permute-start(bf16[32,1024]{1,0:T(8,128)(2,1)S(1)} %arrive.4.refs_5_.first.refs_1_), channel_id=1, source_target_pairs={{0,6},{2,4},{4,2},{6,0},{1,7},{3,5},{5,3},{7,1},{8,14},{10,12},{12... | collective-permute-start | bytes 196616 | tf_op jit(solution)/shard_map/ppermute | solution.py:32
  32.4 1.3 collective-permute-done.13.refs_4_
  33.7 1.3 collective-permute-done.12.refs_3_
  35.1 1.3 collective-permute-done.11.refs_2_
  36.9 2.9 %collective-permute-start.15 = (bf16[128,1024]{1,0:T(8,128)(2,1)S(1)}, bf16[128,1024]{1,0:T(8,128)(2,1)S(1)}, u32[]{:S(2)}, u32[]{:S(2)}) collective-permute-start(bf16[128,1024]{1,0:T(8,128)(2,1)S(1)} %get-tuple-element.148.refs_0_.refs_2_), channel_id=1, source_target_pairs={{0,1},{1,0},{2,3},{3,2},{4,5},{5,4},{6,7},{7,6},{8,9},{9,8},{10,11... | collective-permute-start | bytes 786440 | tf_op jit(solution)/shard_map/ppermute | solution.py:22
  40.3 0.6 collective-permute-done.15.refs_1_.refs_3_
  42.2 1.4 %collective-permute-start.16 = (bf16[32,1024]{1,0:T(8,128)(2,1)S(1)}, bf16[32,1024]{1,0:T(8,128)(2,1)S(1)}, u32[]{:S(2)}, u32[]{:S(2)}) collective-permute-start(bf16[32,1024]{1,0:T(8,128)(2,1)S(1)} %get-tuple-element.151), channel_id=1, source_target_pairs={{0,4},{2,6},{4,0},{6,2},{1,5},{3,7},{5,1},{7,3},{8,12},{10,14},{12... | collective-permute-start | bytes 196616 | tf_op jit(solution)/shard_map/ppermute | solution.py:32
  43.6 1.0 collective-permute-start.17
  45.3 1.2 turned_weight.3.refs_4_
  46.6 3.2 %collective-permute-done.16.refs_1_ = bf16[32,1024]{1,0:T(8,128)(2,1)S(1)} collective-permute-done((bf16[32,1024]{1,0:T(8,128)(2,1)S(1)}, bf16[32,1024]{1,0:T(8,128)(2,1)S(1)}, u32[]{:S(2)}, u32[]{:S(2)}) %collective-permute-start.16) | collective-permute-done | bytes 65568 | tf_op jit(solution)/shard_map/ppermute | solution.py:32
  49.8 1.6 %collective-permute-done.18.refs_3_ = bf16[32,1024]{1,0:T(8,128)(2,1)S(1)} collective-permute-done((bf16[32,1024]{1,0:T(8,128)(2,1)S(1)}, bf16[32,1024]{1,0:T(8,128)(2,1)S(1)}, u32[]{:S(2)}, u32[]{:S(2)}) %collective-permute-start.18) | collective-permute-done | bytes 65568 | tf_op jit(solution)/shard_map/ppermute | solution.py:32
  51.4 3.0 %collective-permute-start.19 = (bf16[32,1024]{1,0:T(8,128)(2,1)S(1)}, bf16[32,1024]{1,0:T(8,128)(2,1)S(1)}, u32[]{:S(2)}, u32[]{:S(2)}) collective-permute-start(bf16[32,1024]{1,0:T(8,128)(2,1)S(1)} %get-tuple-element.161), channel_id=1, source_target_pairs={{0,8},{8,16},{16,24},{1,9},{9,17},{17,25},{2,10},{10,18},{18,26},{... | collective-permute-start | bytes 196616 | tf_op jit(solution)/shard_map/ppermute | solution.py:17
  54.5 1.4 %collective-permute-start.23 = (bf16[32,1024]{1,0:T(8,128)(2,1)S(1)}, bf16[32,1024]{1,0:T(8,128)(2,1)S(1)}, u32[]{:S(2)}, u32[]{:S(2)}) collective-permute-start(bf16[32,1024]{1,0:T(8,128)(2,1)S(1)} %get-tuple-element.164.refs_3_.first), channel_id=1, source_target_pairs={{0,4},{2,6},{4,0},{6,2},{1,5},{3,7},{5,1},{7,3},{8,12},{10,14},{12... | collective-permute-start | bytes 196616 | tf_op jit(solution)/shard_map/ppermute | solution.py:32
  56.4 1.0 collective-permute-start.22
  57.4 1.6 %collective-permute-start.21 = (bf16[32,1024]{1,0:T(8,128)(2,1)S(1)}, bf16[32,1024]{1,0:T(8,128)(2,1)S(1)}, u32[]{:S(2)}, u32[]{:S(2)}) collective-permute-start(bf16[32,1024]{1,0:T(8,128)(2,1)S(1)} %arrive.5.refs_3_.refs_2_), channel_id=1, source_target_pairs={{0,6},{2,4},{4,2},{6,0},{1,7},{3,5},{5,3},{7,1},{8,14},{10,12},{12... | collective-permute-start | bytes 196616 | tf_op jit(solution)/shard_map/ppermute | solution.py:32
  59.2 1.9 %collective-permute-done.23.refs_2_ = bf16[32,1024]{1,0:T(8,128)(2,1)S(1)} collective-permute-done((bf16[32,1024]{1,0:T(8,128)(2,1)S(1)}, bf16[32,1024]{1,0:T(8,128)(2,1)S(1)}, u32[]{:S(2)}, u32[]{:S(2)}) %collective-permute-start.23) | collective-permute-done | bytes 65568 | tf_op jit(solution)/shard_map/ppermute | solution.py:32
  62.0 2.9 %collective-permute-start.26 = (bf16[128,1024]{1,0:T(8,128)(2,1)S(1)}, bf16[128,1024]{1,0:T(8,128)(2,1)S(1)}, u32[]{:S(2)}, u32[]{:S(2)}) collective-permute-start(bf16[128,1024]{1,0:T(8,128)(2,1)S(1)} %product_part.8.refs_0_), channel_id=1, source_target_pairs={{0,1},{1,0},{2,3},{3,2},{4,5},{5,4},{6,7},{7,6},{8,9},{9,8},{10,11... | collective-permute-start | bytes 786440 | tf_op jit(solution)/shard_map/ppermute | solution.py:22
  65.5 1.6 %collective-permute-start.24 = (bf16[128,1024]{1,0:T(8,128)(2,1)S(1)}, bf16[128,1024]{1,0:T(8,128)(2,1)S(1)}, u32[]{:S(2)}, u32[]{:S(2)}) collective-permute-start(bf16[128,1024]{1,0:T(8,128)(2,1)S(1)} %get-tuple-element.184.refs_2_.refs_0_), channel_id=1, source_target_pairs={{0,1},{1,0},{2,3},{3,2},{4,5},{5,4},{6,7},{7,6},{8,9},{9,8},{10,11... | collective-permute-start | bytes 786440 | tf_op jit(solution)/shard_map/ppermute | solution.py:22
  69.7 1.5 %collective-permute-start.28 = (bf16[32,1024]{1,0:T(8,128)(2,1)S(1)}, bf16[32,1024]{1,0:T(8,128)(2,1)S(1)}, u32[]{:S(2)}, u32[]{:S(2)}) collective-permute-start(bf16[32,1024]{1,0:T(8,128)(2,1)S(1)} %get-tuple-element.175), channel_id=1, source_target_pairs={{0,4},{2,6},{4,0},{6,2},{1,5},{3,7},{5,1},{7,3},{8,12},{10,14},{12... | collective-permute-start | bytes 196616 | tf_op jit(solution)/shard_map/ppermute | solution.py:32
  71.2 1.3 collective-permute-start.29
  72.9 2.7 %collective-permute-done.28.refs_1_ = bf16[32,1024]{1,0:T(8,128)(2,1)S(1)} collective-permute-done((bf16[32,1024]{1,0:T(8,128)(2,1)S(1)}, bf16[32,1024]{1,0:T(8,128)(2,1)S(1)}, u32[]{:S(2)}, u32[]{:S(2)}) %collective-permute-start.28) | collective-permute-done | bytes 65568 | tf_op jit(solution)/shard_map/ppermute | solution.py:32
  76.2 2.6 %collective-permute-done.30.refs_3_ = bf16[32,1024]{1,0:T(8,128)(2,1)S(1)} collective-permute-done((bf16[32,1024]{1,0:T(8,128)(2,1)S(1)}, bf16[32,1024]{1,0:T(8,128)(2,1)S(1)}, u32[]{:S(2)}, u32[]{:S(2)}) %collective-permute-start.30) | collective-permute-done | bytes 65568 | tf_op jit(solution)/shard_map/ppermute | solution.py:32
  78.8 2.1 %collective-permute-start.31 = (bf16[32,1024]{1,0:T(8,128)(2,1)S(1)}, bf16[32,1024]{1,0:T(8,128)(2,1)S(1)}, u32[]{:S(2)}, u32[]{:S(2)}) collective-permute-start(bf16[32,1024]{1,0:T(8,128)(2,1)S(1)} %leave_back.2.refs_5_), channel_id=1, source_target_pairs={{8,0},{16,8},{24,16},{9,1},{17,9},{25,17},{10,2},{18,10},{26,18},{... | collective-permute-start | bytes 196616 | tf_op jit(solution)/shard_map/ppermute | solution.py:17
  81.2 0.7 down_again.1
  82.0 1.9 %collective-permute-start.33 = (bf16[32,1024]{1,0:T(8,128)(2,1)S(1)}, bf16[32,1024]{1,0:T(8,128)(2,1)S(1)}, u32[]{:S(2)}, u32[]{:S(2)}) collective-permute-start(bf16[32,1024]{1,0:T(8,128)(2,1)S(1)} %get-tuple-element.197), channel_id=1, source_target_pairs={{0,6},{2,4},{4,2},{6,0},{1,7},{3,5},{5,3},{7,1},{8,14},{10,12},{12... | collective-permute-start | bytes 196616 | tf_op jit(solution)/shard_map/ppermute | solution.py:32
  83.9 0.9 collective-permute-done.31.arrived
  85.2 1.7 %collective-permute-start.35 = (bf16[32,1024]{1,0:T(8,128)(2,1)S(1)}, bf16[32,1024]{1,0:T(8,128)(2,1)S(1)}, u32[]{:S(2)}, u32[]{:S(2)}) collective-permute-start(bf16[32,1024]{1,0:T(8,128)(2,1)S(1)} %arrive.6.refs_5_.first), channel_id=1, source_target_pairs={{0,6},{2,4},{4,2},{6,0},{1,7},{3,5},{5,3},{7,1},{8,14},{10,12},{12... | collective-permute-start | bytes 196616 | tf_op jit(solution)/shard_map/ppermute | solution.py:32
  87.6 4.8 %collective-permute-done.36.refs_4_ = bf16[32,1024]{1,0:T(8,128)(2,1)S(1)} collective-permute-done((bf16[32,1024]{1,0:T(8,128)(2,1)S(1)}, bf16[32,1024]{1,0:T(8,128)(2,1)S(1)}, u32[]{:S(2)}, u32[]{:S(2)}) %collective-permute-start.36) | collective-permute-done | bytes 65568 | tf_op jit(solution)/shard_map/ppermute | solution.py:32
  92.8 2.2 %collective-permute-start.38 = (bf16[128,1024]{1,0:T(8,128)(2,1)S(1)}, bf16[128,1024]{1,0:T(8,128)(2,1)S(1)}, u32[]{:S(2)}, u32[]{:S(2)}) collective-permute-start(bf16[128,1024]{1,0:T(8,128)(2,1)S(1)} %get-tuple-element.199.refs_0_), channel_id=1, source_target_pairs={{0,1},{1,0},{2,3},{3,2},{4,5},{5,4},{6,7},{7,6},{8,9},{9,8},{10,11... | collective-permute-start | bytes 786440 | tf_op jit(solution)/shard_map/ppermute | solution.py:22
  97.7 1.6 %collective-permute-start.39 = (bf16[32,1024]{1,0:T(8,128)(2,1)S(1)}, bf16[32,1024]{1,0:T(8,128)(2,1)S(1)}, u32[]{:S(2)}, u32[]{:S(2)}) collective-permute-start(bf16[32,1024]{1,0:T(8,128)(2,1)S(1)} %get-tuple-element.202), channel_id=1, source_target_pairs={{0,4},{2,6},{4,0},{6,2},{1,5},{3,7},{5,1},{7,3},{8,12},{10,14},{12... | collective-permute-start | bytes 196616 | tf_op jit(solution)/shard_map/ppermute | solution.py:32
  99.3 1.4 %collective-permute-start.40 = (bf16[32,1024]{1,0:T(8,128)(2,1)S(1)}, bf16[32,1024]{1,0:T(8,128)(2,1)S(1)}, u32[]{:S(2)}, u32[]{:S(2)}) collective-permute-start(bf16[32,1024]{1,0:T(8,128)(2,1)S(1)} %get-tuple-element.203), channel_id=1, source_target_pairs={{0,6},{2,4},{4,2},{6,0},{1,7},{3,5},{5,3},{7,1},{8,14},{10,12},{12... | collective-permute-start | bytes 196616 | tf_op jit(solution)/shard_map/ppermute | solution.py:32
  101.1 1.3 grad_begun.2.refs_3_
  102.4 1.3 collective-permute-done.39.refs_1_
  104.3 2.5 %collective-permute-done.41.refs_3_ = bf16[32,1024]{1,0:T(8,128)(2,1)S(1)} collective-permute-done((bf16[32,1024]{1,0:T(8,128)(2,1)S(1)}, bf16[32,1024]{1,0:T(8,128)(2,1)S(1)}, u32[]{:S(2)}, u32[]{:S(2)}) %collective-permute-start.41) | collective-permute-done | bytes 65568 | tf_op jit(solution)/shard_map/ppermute | solution.py:32
  106.9 1.9 %collective-permute-start.43 = (bf16[32,1024]{1,0:T(8,128)(2,1)S(1)}, bf16[32,1024]{1,0:T(8,128)(2,1)S(1)}, u32[]{:S(2)}, u32[]{:S(2)}) collective-permute-start(bf16[32,1024]{1,0:T(8,128)(2,1)S(1)} %leave_back.3.refs_4_), channel_id=1, source_target_pairs={{8,0},{16,8},{24,16},{9,1},{17,9},{25,17},{10,2},{18,10},{26,18},{... | collective-permute-start | bytes 196616 | tf_op jit(solution)/shard_map/ppermute | solution.py:17
  108.8 0.7 collective-permute-start.42
  109.5 3.3 %collective-permute-done.43.arrived = bf16[32,1024]{1,0:T(8,128)(2,1)S(1)} collective-permute-done((bf16[32,1024]{1,0:T(8,128)(2,1)S(1)}, bf16[32,1024]{1,0:T(8,128)(2,1)S(1)}, u32[]{:S(2)}, u32[]{:S(2)}) %collective-permute-start.43) | collective-permute-done | bytes 65568 | tf_op jit(solution)/shard_map/ppermute | solution.py:17
  112.8 0.7 collective-permute-start.46
  113.5 1.4 %collective-permute-start.45 = (bf16[32,1024]{1,0:T(8,128)(2,1)S(1)}, bf16[32,1024]{1,0:T(8,128)(2,1)S(1)}, u32[]{:S(2)}, u32[]{:S(2)}) collective-permute-start(bf16[32,1024]{1,0:T(8,128)(2,1)S(1)} %arrive.7.refs_3_.first), channel_id=1, source_target_pairs={{0,6},{2,4},{4,2},{6,0},{1,7},{3,5},{5,3},{7,1},{8,14},{10,12},{12... | collective-permute-start | bytes 196616 | tf_op jit(solution)/shard_map/ppermute | solution.py:32
  115.5 0.8 finish_forward.1
  116.3 1.3 grad_begun.3.refs_7_
  117.5 1.0 collective-permute-done.45.refs_1_
  119.2 3.9 %collective-permute-start.48 = (bf16[128,1024]{1,0:T(8,128)(2,1)S(1)}, bf16[128,1024]{1,0:T(8,128)(2,1)S(1)}, u32[]{:S(2)}, u32[]{:S(2)}) collective-permute-start(bf16[128,1024]{1,0:T(8,128)(2,1)S(1)} %get-tuple-element.225.refs_0_), channel_id=1, source_target_pairs={{0,1},{1,0},{2,3},{3,2},{4,5},{5,4},{6,7},{7,6},{8,9},{9,8},{10,11... | collective-permute-start | bytes 786440 | tf_op jit(solution)/shard_map/ppermute | solution.py:22
  125.7 0.7 collective-permute-start.49
  126.3 1.4 %collective-permute-start.50 = (bf16[32,1024]{1,0:T(8,128)(2,1)S(1)}, bf16[32,1024]{1,0:T(8,128)(2,1)S(1)}, u32[]{:S(2)}, u32[]{:S(2)}) collective-permute-start(bf16[32,1024]{1,0:T(8,128)(2,1)S(1)} %get-tuple-element.231), channel_id=1, source_target_pairs={{0,6},{2,4},{4,2},{6,0},{1,7},{3,5},{5,3},{7,1},{8,14},{10,12},{12... | collective-permute-start | bytes 196616 | tf_op jit(solution)/shard_map/ppermute | solution.py:32
  127.8 0.6 collective-permute-start.51
  128.4 3.8 %grads_ended.1 = (bf16[1024,2048]{1,0:T(8,128)(2,1)}, bf16[2048,1024]{1,0:T(8,128)(2,1)}) custom-call(bf16[1024,128]{1,0:T(8,128)(2,1)S(1)} %turned.9.refs_0_, bf16[128,1024]{1,0:T(8,128)(2,1)S(1)} %get-tuple-element.228.refs_1_, bf16[128,1024]{1,0:T(8,128)(2,1)S(1)} %get-tuple-element.229.refs_2_, f32[1024,2048]{1,0:T(8,128)S(1)} %grad_begun.2.refs_3_, ...), custom_call_target="tpu_custom_call" | custom-call | flops 1073741824 | bytes 8388608 | tf_op jit(solution)/shard_map/grads_ended/pallas_call | solution.py:386
  132.2 1.0 collective-permute-done.49.refs_1_
  133.2 1.2 collective-permute-done.51.refs_3_
  134.4 0.7 finish.1
  (93 shorter events, 22.0 us)
Async XLA Ops:
  1.5 7.2 %collective-permute-start.2 = (bf16[32,1024]{1,0:T(8,128)(2,1)S(1)}, bf16[32,1024]{1,0:T(8,128)(2,1)S(1)}, u32[]{:S(2)}, u32[]{:S(2)}) collective-permute-start(bf16[32,1024]{1,0:T(8,128)(2,1)S(1)} %get-tuple-element.128.refs_3_.first.refs_0_), channel_id=1, source_target_pairs={{0,4},{2,6},{4,0},{6,2},{1,5},{3,7},{5,1},{7,3},{8,12},{10,14},{12... | collective-permute-start | bytes 196616 | tf_op jit(solution)/shard_map/ppermute | solution.py:32
  3.9 5.0 %collective-permute-start.1 = (bf16[32,1024]{1,0:T(8,128)(2,1)S(1)}, bf16[32,1024]{1,0:T(8,128)(2,1)S(1)}, u32[]{:S(2)}, u32[]{:S(2)}) collective-permute-start(bf16[32,1024]{1,0:T(8,128)(2,1)S(1)} %get-tuple-element.128.refs_3_.first.refs_0_), channel_id=1, source_target_pairs={{0,6},{2,4},{4,2},{6,0},{1,7},{3,5},{5,3},{7,1},{8,14},{10,12},{12... | collective-permute-start | bytes 196616 | tf_op jit(solution)/shard_map/ppermute | solution.py:32
  5.0 4.3 %collective-permute-start = (bf16[32,1024]{1,0:T(8,128)(2,1)S(1)}, bf16[32,1024]{1,0:T(8,128)(2,1)S(1)}, u32[]{:S(2)}, u32[]{:S(2)}) collective-permute-start(bf16[32,1024]{1,0:T(8,128)(2,1)S(1)} %get-tuple-element.128.refs_3_.first.refs_0_), channel_id=1, source_target_pairs={{0,2},{2,0},{4,6},{6,4},{1,3},{3,1},{5,7},{7,5},{8,10},{10,8},{12,... | collective-permute-start | bytes 196616 | tf_op jit(solution)/shard_map/ppermute | solution.py:32
  9.7 3.2 %collective-permute-start.4 = (bf16[128,1024]{1,0:T(8,128)(2,1)S(1)}, bf16[128,1024]{1,0:T(8,128)(2,1)S(1)}, u32[]{:S(2)}, u32[]{:S(2)}) collective-permute-start(bf16[128,1024]{1,0:T(8,128)(2,1)S(1)} %get-tuple-element.131.refs_0_.refs_2_), channel_id=1, source_target_pairs={{0,1},{1,0},{2,3},{3,2},{4,5},{5,4},{6,7},{7,6},{8,9},{9,8},{10,11... | collective-permute-start | bytes 786440 | tf_op jit(solution)/shard_map/ppermute | solution.py:22
  12.2 1.6 %collective-permute-start.3 = (bf16[128,1024]{1,0:T(8,128)(2,1)S(1)}, bf16[128,1024]{1,0:T(8,128)(2,1)S(1)}, u32[]{:S(2)}, u32[]{:S(2)}) collective-permute-start(bf16[128,1024]{1,0:T(8,128)(2,1)S(1)} %product_part.6.refs_0_.refs_2_), channel_id=1, source_target_pairs={{0,1},{1,0},{2,3},{3,2},{4,5},{5,4},{6,7},{7,6},{8,9},{9,8},{10,11... | collective-permute-start | bytes 786440 | tf_op jit(solution)/shard_map/ppermute | solution.py:22
  14.2 6.2 %collective-permute-start.5 = (bf16[32,1024]{1,0:T(8,128)(2,1)S(1)}, bf16[32,1024]{1,0:T(8,128)(2,1)S(1)}, u32[]{:S(2)}, u32[]{:S(2)}) collective-permute-start(bf16[32,1024]{1,0:T(8,128)(2,1)S(1)} %get-tuple-element.134), channel_id=1, source_target_pairs={{0,4},{2,6},{4,0},{6,2},{1,5},{3,7},{5,1},{7,3},{8,12},{10,14},{12... | collective-permute-start | bytes 196616 | tf_op jit(solution)/shard_map/ppermute | solution.py:32
  16.7 5.1 %collective-permute-start.6 = (bf16[32,1024]{1,0:T(8,128)(2,1)S(1)}, bf16[32,1024]{1,0:T(8,128)(2,1)S(1)}, u32[]{:S(2)}, u32[]{:S(2)}) collective-permute-start(bf16[32,1024]{1,0:T(8,128)(2,1)S(1)} %get-tuple-element.135), channel_id=1, source_target_pairs={{0,6},{2,4},{4,2},{6,0},{1,7},{3,5},{5,3},{7,1},{8,14},{10,12},{12... | collective-permute-start | bytes 196616 | tf_op jit(solution)/shard_map/ppermute | solution.py:32
  17.1 6.1 %collective-permute-start.7 = (bf16[32,1024]{1,0:T(8,128)(2,1)S(1)}, bf16[32,1024]{1,0:T(8,128)(2,1)S(1)}, u32[]{:S(2)}, u32[]{:S(2)}) collective-permute-start(bf16[32,1024]{1,0:T(8,128)(2,1)S(1)} %get-tuple-element.136), channel_id=1, source_target_pairs={{0,2},{2,0},{4,6},{6,4},{1,3},{3,1},{5,7},{7,5},{8,10},{10,8},{12,... | collective-permute-start | bytes 196616 | tf_op jit(solution)/shard_map/ppermute | solution.py:32
  17.3 1.2 copy-start
  23.3 5.5 %collective-permute-start.8 = (bf16[32,1024]{1,0:T(8,128)(2,1)S(1)}, bf16[32,1024]{1,0:T(8,128)(2,1)S(1)}, u32[]{:S(2)}, u32[]{:S(2)}) collective-permute-start(bf16[32,1024]{1,0:T(8,128)(2,1)S(1)} %get-tuple-element.143), channel_id=1, source_target_pairs={{0,8},{8,16},{16,24},{1,9},{9,17},{17,25},{2,10},{10,18},{18,26},{... | collective-permute-start | bytes 196616 | tf_op jit(solution)/shard_map/ppermute | solution.py:17
  26.3 6.1 %collective-permute-start.10 = (bf16[32,1024]{1,0:T(8,128)(2,1)S(1)}, bf16[32,1024]{1,0:T(8,128)(2,1)S(1)}, u32[]{:S(2)}, u32[]{:S(2)}) collective-permute-start(bf16[32,1024]{1,0:T(8,128)(2,1)S(1)} %get-tuple-element.164.refs_3_.first), channel_id=1, source_target_pairs={{0,6},{2,4},{4,2},{6,0},{1,7},{3,5},{5,3},{7,1},{8,14},{10,12},{12... | collective-permute-start | bytes 196616 | tf_op jit(solution)/shard_map/ppermute | solution.py:32
  28.8 3.6 %collective-permute-start.9 = (bf16[32,1024]{1,0:T(8,128)(2,1)S(1)}, bf16[32,1024]{1,0:T(8,128)(2,1)S(1)}, u32[]{:S(2)}, u32[]{:S(2)}) collective-permute-start(bf16[32,1024]{1,0:T(8,128)(2,1)S(1)} %get-tuple-element.164.refs_3_.first), channel_id=1, source_target_pairs={{0,2},{2,0},{4,6},{6,4},{1,3},{3,1},{5,7},{7,5},{8,10},{10,8},{12,... | collective-permute-start | bytes 196616 | tf_op jit(solution)/shard_map/ppermute | solution.py:32
  28.8 4.9 %collective-permute-start.13 = (bf16[32,1024]{1,0:T(8,128)(2,1)S(1)}, bf16[32,1024]{1,0:T(8,128)(2,1)S(1)}, u32[]{:S(2)}, u32[]{:S(2)}) collective-permute-start(bf16[32,1024]{1,0:T(8,128)(2,1)S(1)} %arrive.4.refs_5_.first.refs_1_), channel_id=1, source_target_pairs={{0,4},{2,6},{4,0},{6,2},{1,5},{3,7},{5,1},{7,3},{8,12},{10,14},{12... | collective-permute-start | bytes 196616 | tf_op jit(solution)/shard_map/ppermute | solution.py:32
  30.0 5.1 %collective-permute-start.12 = (bf16[32,1024]{1,0:T(8,128)(2,1)S(1)}, bf16[32,1024]{1,0:T(8,128)(2,1)S(1)}, u32[]{:S(2)}, u32[]{:S(2)}) collective-permute-start(bf16[32,1024]{1,0:T(8,128)(2,1)S(1)} %arrive.4.refs_5_.first.refs_1_), channel_id=1, source_target_pairs={{0,6},{2,4},{4,2},{6,0},{1,7},{3,5},{5,3},{7,1},{8,14},{10,12},{12... | collective-permute-start | bytes 196616 | tf_op jit(solution)/shard_map/ppermute | solution.py:32
  32.4 4.0 %collective-permute-start.11 = (bf16[32,1024]{1,0:T(8,128)(2,1)S(1)}, bf16[32,1024]{1,0:T(8,128)(2,1)S(1)}, u32[]{:S(2)}, u32[]{:S(2)}) collective-permute-start(bf16[32,1024]{1,0:T(8,128)(2,1)S(1)} %arrive.4.refs_5_.first.refs_1_), channel_id=1, source_target_pairs={{0,2},{2,0},{4,6},{6,4},{1,3},{3,1},{5,7},{7,5},{8,10},{10,8},{12,... | collective-permute-start | bytes 196616 | tf_op jit(solution)/shard_map/ppermute | solution.py:32
  36.9 4.0 %collective-permute-start.15 = (bf16[128,1024]{1,0:T(8,128)(2,1)S(1)}, bf16[128,1024]{1,0:T(8,128)(2,1)S(1)}, u32[]{:S(2)}, u32[]{:S(2)}) collective-permute-start(bf16[128,1024]{1,0:T(8,128)(2,1)S(1)} %get-tuple-element.148.refs_0_.refs_2_), channel_id=1, source_target_pairs={{0,1},{1,0},{2,3},{3,2},{4,5},{5,4},{6,7},{7,6},{8,9},{9,8},{10,11... | collective-permute-start | bytes 786440 | tf_op jit(solution)/shard_map/ppermute | solution.py:22
  40.2 1.6 %collective-permute-start.14 = (bf16[128,1024]{1,0:T(8,128)(2,1)S(1)}, bf16[128,1024]{1,0:T(8,128)(2,1)S(1)}, u32[]{:S(2)}, u32[]{:S(2)}) collective-permute-start(bf16[128,1024]{1,0:T(8,128)(2,1)S(1)} %product_part.7.refs_0_.refs_2_), channel_id=1, source_target_pairs={{0,1},{1,0},{2,3},{3,2},{4,5},{5,4},{6,7},{7,6},{8,9},{9,8},{10,11... | collective-permute-start | bytes 786440 | tf_op jit(solution)/shard_map/ppermute | solution.py:22
  42.2 7.5 %collective-permute-start.16 = (bf16[32,1024]{1,0:T(8,128)(2,1)S(1)}, bf16[32,1024]{1,0:T(8,128)(2,1)S(1)}, u32[]{:S(2)}, u32[]{:S(2)}) collective-permute-start(bf16[32,1024]{1,0:T(8,128)(2,1)S(1)} %get-tuple-element.151), channel_id=1, source_target_pairs={{0,4},{2,6},{4,0},{6,2},{1,5},{3,7},{5,1},{7,3},{8,12},{10,14},{12... | collective-permute-start | bytes 196616 | tf_op jit(solution)/shard_map/ppermute | solution.py:32
  43.6 6.2 %collective-permute-start.17 = (bf16[32,1024]{1,0:T(8,128)(2,1)S(1)}, bf16[32,1024]{1,0:T(8,128)(2,1)S(1)}, u32[]{:S(2)}, u32[]{:S(2)}) collective-permute-start(bf16[32,1024]{1,0:T(8,128)(2,1)S(1)} %get-tuple-element.152), channel_id=1, source_target_pairs={{0,6},{2,4},{4,2},{6,0},{1,7},{3,5},{5,3},{7,1},{8,14},{10,12},{12... | collective-permute-start | bytes 196616 | tf_op jit(solution)/shard_map/ppermute | solution.py:32
  44.7 6.7 %collective-permute-start.18 = (bf16[32,1024]{1,0:T(8,128)(2,1)S(1)}, bf16[32,1024]{1,0:T(8,128)(2,1)S(1)}, u32[]{:S(2)}, u32[]{:S(2)}) collective-permute-start(bf16[32,1024]{1,0:T(8,128)(2,1)S(1)} %get-tuple-element.153), channel_id=1, source_target_pairs={{0,2},{2,0},{4,6},{6,4},{1,3},{3,1},{5,7},{7,5},{8,10},{10,8},{12,... | collective-permute-start | bytes 196616 | tf_op jit(solution)/shard_map/ppermute | solution.py:32
  51.4 5.0 %collective-permute-start.19 = (bf16[32,1024]{1,0:T(8,128)(2,1)S(1)}, bf16[32,1024]{1,0:T(8,128)(2,1)S(1)}, u32[]{:S(2)}, u32[]{:S(2)}) collective-permute-start(bf16[32,1024]{1,0:T(8,128)(2,1)S(1)} %get-tuple-element.161), channel_id=1, source_target_pairs={{0,8},{8,16},{16,24},{1,9},{9,17},{17,25},{2,10},{10,18},{18,26},{... | collective-permute-start | bytes 196616 | tf_op jit(solution)/shard_map/ppermute | solution.py:17
  54.5 6.6 %collective-permute-start.23 = (bf16[32,1024]{1,0:T(8,128)(2,1)S(1)}, bf16[32,1024]{1,0:T(8,128)(2,1)S(1)}, u32[]{:S(2)}, u32[]{:S(2)}) collective-permute-start(bf16[32,1024]{1,0:T(8,128)(2,1)S(1)} %get-tuple-element.164.refs_3_.first), channel_id=1, source_target_pairs={{0,4},{2,6},{4,0},{6,2},{1,5},{3,7},{5,1},{7,3},{8,12},{10,14},{12... | collective-permute-start | bytes 196616 | tf_op jit(solution)/shard_map/ppermute | solution.py:32
  56.4 8.5 %collective-permute-start.22 = (bf16[32,1024]{1,0:T(8,128)(2,1)S(1)}, bf16[32,1024]{1,0:T(8,128)(2,1)S(1)}, u32[]{:S(2)}, u32[]{:S(2)}) collective-permute-start(bf16[32,1024]{1,0:T(8,128)(2,1)S(1)} %arrive.5.refs_3_.refs_2_), channel_id=1, source_target_pairs={{0,4},{2,6},{4,0},{6,2},{1,5},{3,7},{5,1},{7,3},{8,12},{10,14},{12... | collective-permute-start | bytes 196616 | tf_op jit(solution)/shard_map/ppermute | solution.py:32
  57.4 7.6 %collective-permute-start.21 = (bf16[32,1024]{1,0:T(8,128)(2,1)S(1)}, bf16[32,1024]{1,0:T(8,128)(2,1)S(1)}, u32[]{:S(2)}, u32[]{:S(2)}) collective-permute-start(bf16[32,1024]{1,0:T(8,128)(2,1)S(1)} %arrive.5.refs_3_.refs_2_), channel_id=1, source_target_pairs={{0,6},{2,4},{4,2},{6,0},{1,7},{3,5},{5,3},{7,1},{8,14},{10,12},{12... | collective-permute-start | bytes 196616 | tf_op jit(solution)/shard_map/ppermute | solution.py:32
  59.0 5.9 %collective-permute-start.20 = (bf16[32,1024]{1,0:T(8,128)(2,1)S(1)}, bf16[32,1024]{1,0:T(8,128)(2,1)S(1)}, u32[]{:S(2)}, u32[]{:S(2)}) collective-permute-start(bf16[32,1024]{1,0:T(8,128)(2,1)S(1)} %arrive.5.refs_3_.refs_2_), channel_id=1, source_target_pairs={{0,2},{2,0},{4,6},{6,4},{1,3},{3,1},{5,7},{7,5},{8,10},{10,8},{12,... | collective-permute-start | bytes 196616 | tf_op jit(solution)/shard_map/ppermute | solution.py:32
  62.0 6.8 %collective-permute-start.26 = (bf16[128,1024]{1,0:T(8,128)(2,1)S(1)}, bf16[128,1024]{1,0:T(8,128)(2,1)S(1)}, u32[]{:S(2)}, u32[]{:S(2)}) collective-permute-start(bf16[128,1024]{1,0:T(8,128)(2,1)S(1)} %product_part.8.refs_0_), channel_id=1, source_target_pairs={{0,1},{1,0},{2,3},{3,2},{4,5},{5,4},{6,7},{7,6},{8,9},{9,8},{10,11... | collective-permute-start | bytes 786440 | tf_op jit(solution)/shard_map/ppermute | solution.py:22
  64.9 2.7 %collective-permute-start.27 = (bf16[128,1024]{1,0:T(8,128)(2,1)S(1)}, bf16[128,1024]{1,0:T(8,128)(2,1)S(1)}, u32[]{:S(2)}, u32[]{:S(2)}) collective-permute-start(bf16[128,1024]{1,0:T(8,128)(2,1)S(1)} %get-tuple-element.165.refs_0_), channel_id=1, source_target_pairs={{0,1},{1,0},{2,3},{3,2},{4,5},{5,4},{6,7},{7,6},{8,9},{9,8},{10,11... | collective-permute-start | bytes 786440 | tf_op jit(solution)/shard_map/ppermute | solution.py:22
  65.5 2.7 %collective-permute-start.24 = (bf16[128,1024]{1,0:T(8,128)(2,1)S(1)}, bf16[128,1024]{1,0:T(8,128)(2,1)S(1)}, u32[]{:S(2)}, u32[]{:S(2)}) collective-permute-start(bf16[128,1024]{1,0:T(8,128)(2,1)S(1)} %get-tuple-element.184.refs_2_.refs_0_), channel_id=1, source_target_pairs={{0,1},{1,0},{2,3},{3,2},{4,5},{5,4},{6,7},{7,6},{8,9},{9,8},{10,11... | collective-permute-start | bytes 786440 | tf_op jit(solution)/shard_map/ppermute | solution.py:22
  67.5 1.6 %collective-permute-start.25 = (bf16[128,1024]{1,0:T(8,128)(2,1)S(1)}, bf16[128,1024]{1,0:T(8,128)(2,1)S(1)}, u32[]{:S(2)}, u32[]{:S(2)}) collective-permute-start(bf16[128,1024]{1,0:T(8,128)(2,1)S(1)} %product_part.9.refs_2_), channel_id=1, source_target_pairs={{0,1},{1,0},{2,3},{3,2},{4,5},{5,4},{6,7},{7,6},{8,9},{9,8},{10,11... | collective-permute-start | bytes 786440 | tf_op jit(solution)/shard_map/ppermute | solution.py:22
  69.7 6.0 %collective-permute-start.28 = (bf16[32,1024]{1,0:T(8,128)(2,1)S(1)}, bf16[32,1024]{1,0:T(8,128)(2,1)S(1)}, u32[]{:S(2)}, u32[]{:S(2)}) collective-permute-start(bf16[32,1024]{1,0:T(8,128)(2,1)S(1)} %get-tuple-element.175), channel_id=1, source_target_pairs={{0,4},{2,6},{4,0},{6,2},{1,5},{3,7},{5,1},{7,3},{8,12},{10,14},{12... | collective-permute-start | bytes 196616 | tf_op jit(solution)/shard_map/ppermute | solution.py:32
  71.2 5.0 %collective-permute-start.29 = (bf16[32,1024]{1,0:T(8,128)(2,1)S(1)}, bf16[32,1024]{1,0:T(8,128)(2,1)S(1)}, u32[]{:S(2)}, u32[]{:S(2)}) collective-permute-start(bf16[32,1024]{1,0:T(8,128)(2,1)S(1)} %get-tuple-element.176), channel_id=1, source_target_pairs={{0,6},{2,4},{4,2},{6,0},{1,7},{3,5},{5,3},{7,1},{8,14},{10,12},{12... | collective-permute-start | bytes 196616 | tf_op jit(solution)/shard_map/ppermute | solution.py:32
  72.6 6.2 %collective-permute-start.30 = (bf16[32,1024]{1,0:T(8,128)(2,1)S(1)}, bf16[32,1024]{1,0:T(8,128)(2,1)S(1)}, u32[]{:S(2)}, u32[]{:S(2)}) collective-permute-start(bf16[32,1024]{1,0:T(8,128)(2,1)S(1)} %get-tuple-element.177), channel_id=1, source_target_pairs={{0,2},{2,0},{4,6},{6,4},{1,3},{3,1},{5,7},{7,5},{8,10},{10,8},{12,... | collective-permute-start | bytes 196616 | tf_op jit(solution)/shard_map/ppermute | solution.py:32
  78.8 5.9 %collective-permute-start.31 = (bf16[32,1024]{1,0:T(8,128)(2,1)S(1)}, bf16[32,1024]{1,0:T(8,128)(2,1)S(1)}, u32[]{:S(2)}, u32[]{:S(2)}) collective-permute-start(bf16[32,1024]{1,0:T(8,128)(2,1)S(1)} %leave_back.2.refs_5_), channel_id=1, source_target_pairs={{8,0},{16,8},{24,16},{9,1},{17,9},{25,17},{10,2},{18,10},{26,18},{... | collective-permute-start | bytes 196616 | tf_op jit(solution)/shard_map/ppermute | solution.py:17
  81.9 5.6 %collective-permute-start.32 = (bf16[32,1024]{1,0:T(8,128)(2,1)S(1)}, bf16[32,1024]{1,0:T(8,128)(2,1)S(1)}, u32[]{:S(2)}, u32[]{:S(2)}) collective-permute-start(bf16[32,1024]{1,0:T(8,128)(2,1)S(1)} %get-tuple-element.196), channel_id=1, source_target_pairs={{0,2},{2,0},{4,6},{6,4},{1,3},{3,1},{5,7},{7,5},{8,10},{10,8},{12,... | collective-permute-start | bytes 196616 | tf_op jit(solution)/shard_map/ppermute | solution.py:32
  82.0 5.6 %collective-permute-start.33 = (bf16[32,1024]{1,0:T(8,128)(2,1)S(1)}, bf16[32,1024]{1,0:T(8,128)(2,1)S(1)}, u32[]{:S(2)}, u32[]{:S(2)}) collective-permute-start(bf16[32,1024]{1,0:T(8,128)(2,1)S(1)} %get-tuple-element.197), channel_id=1, source_target_pairs={{0,6},{2,4},{4,2},{6,0},{1,7},{3,5},{5,3},{7,1},{8,14},{10,12},{12... | collective-permute-start | bytes 196616 | tf_op jit(solution)/shard_map/ppermute | solution.py:32
  84.8 7.6 %collective-permute-start.36 = (bf16[32,1024]{1,0:T(8,128)(2,1)S(1)}, bf16[32,1024]{1,0:T(8,128)(2,1)S(1)}, u32[]{:S(2)}, u32[]{:S(2)}) collective-permute-start(bf16[32,1024]{1,0:T(8,128)(2,1)S(1)} %arrive.6.refs_5_.first), channel_id=1, source_target_pairs={{0,4},{2,6},{4,0},{6,2},{1,5},{3,7},{5,1},{7,3},{8,12},{10,14},{12... | collective-permute-start | bytes 196616 | tf_op jit(solution)/shard_map/ppermute | solution.py:32
  85.2 7.2 %collective-permute-start.35 = (bf16[32,1024]{1,0:T(8,128)(2,1)S(1)}, bf16[32,1024]{1,0:T(8,128)(2,1)S(1)}, u32[]{:S(2)}, u32[]{:S(2)}) collective-permute-start(bf16[32,1024]{1,0:T(8,128)(2,1)S(1)} %arrive.6.refs_5_.first), channel_id=1, source_target_pairs={{0,6},{2,4},{4,2},{6,0},{1,7},{3,5},{5,3},{7,1},{8,14},{10,12},{12... | collective-permute-start | bytes 196616 | tf_op jit(solution)/shard_map/ppermute | solution.py:32
  86.9 5.5 %collective-permute-start.34 = (bf16[32,1024]{1,0:T(8,128)(2,1)S(1)}, bf16[32,1024]{1,0:T(8,128)(2,1)S(1)}, u32[]{:S(2)}, u32[]{:S(2)}) collective-permute-start(bf16[32,1024]{1,0:T(8,128)(2,1)S(1)} %arrive.6.refs_5_.first), channel_id=1, source_target_pairs={{0,2},{2,0},{4,6},{6,4},{1,3},{3,1},{5,7},{7,5},{8,10},{10,8},{12,... | collective-permute-start | bytes 196616 | tf_op jit(solution)/shard_map/ppermute | solution.py:32
  92.8 3.4 %collective-permute-start.38 = (bf16[128,1024]{1,0:T(8,128)(2,1)S(1)}, bf16[128,1024]{1,0:T(8,128)(2,1)S(1)}, u32[]{:S(2)}, u32[]{:S(2)}) collective-permute-start(bf16[128,1024]{1,0:T(8,128)(2,1)S(1)} %get-tuple-element.199.refs_0_), channel_id=1, source_target_pairs={{0,1},{1,0},{2,3},{3,2},{4,5},{5,4},{6,7},{7,6},{8,9},{9,8},{10,11... | collective-permute-start | bytes 786440 | tf_op jit(solution)/shard_map/ppermute | solution.py:22
  95.5 1.6 %collective-permute-start.37 = (bf16[128,1024]{1,0:T(8,128)(2,1)S(1)}, bf16[128,1024]{1,0:T(8,128)(2,1)S(1)}, u32[]{:S(2)}, u32[]{:S(2)}) collective-permute-start(bf16[128,1024]{1,0:T(8,128)(2,1)S(1)} %product_part.10.refs_0_), channel_id=1, source_target_pairs={{0,1},{1,0},{2,3},{3,2},{4,5},{5,4},{6,7},{7,6},{8,9},{9,8},{10,11... | collective-permute-start | bytes 786440 | tf_op jit(solution)/shard_map/ppermute | solution.py:22
  97.7 5.9 %collective-permute-start.39 = (bf16[32,1024]{1,0:T(8,128)(2,1)S(1)}, bf16[32,1024]{1,0:T(8,128)(2,1)S(1)}, u32[]{:S(2)}, u32[]{:S(2)}) collective-permute-start(bf16[32,1024]{1,0:T(8,128)(2,1)S(1)} %get-tuple-element.202), channel_id=1, source_target_pairs={{0,4},{2,6},{4,0},{6,2},{1,5},{3,7},{5,1},{7,3},{8,12},{10,14},{12... | collective-permute-start | bytes 196616 | tf_op jit(solution)/shard_map/ppermute | solution.py:32
  99.3 5.0 %collective-permute-start.40 = (bf16[32,1024]{1,0:T(8,128)(2,1)S(1)}, bf16[32,1024]{1,0:T(8,128)(2,1)S(1)}, u32[]{:S(2)}, u32[]{:S(2)}) collective-permute-start(bf16[32,1024]{1,0:T(8,128)(2,1)S(1)} %get-tuple-element.203), channel_id=1, source_target_pairs={{0,6},{2,4},{4,2},{6,0},{1,7},{3,5},{5,3},{7,1},{8,14},{10,12},{12... | collective-permute-start | bytes 196616 | tf_op jit(solution)/shard_map/ppermute | solution.py:32
  100.7 6.1 %collective-permute-start.41 = (bf16[32,1024]{1,0:T(8,128)(2,1)S(1)}, bf16[32,1024]{1,0:T(8,128)(2,1)S(1)}, u32[]{:S(2)}, u32[]{:S(2)}) collective-permute-start(bf16[32,1024]{1,0:T(8,128)(2,1)S(1)} %get-tuple-element.204), channel_id=1, source_target_pairs={{0,2},{2,0},{4,6},{6,4},{1,3},{3,1},{5,7},{7,5},{8,10},{10,8},{12,... | collective-permute-start | bytes 196616 | tf_op jit(solution)/shard_map/ppermute | solution.py:32
  106.9 5.9 %collective-permute-start.43 = (bf16[32,1024]{1,0:T(8,128)(2,1)S(1)}, bf16[32,1024]{1,0:T(8,128)(2,1)S(1)}, u32[]{:S(2)}, u32[]{:S(2)}) collective-permute-start(bf16[32,1024]{1,0:T(8,128)(2,1)S(1)} %leave_back.3.refs_4_), channel_id=1, source_target_pairs={{8,0},{16,8},{24,16},{9,1},{17,9},{25,17},{10,2},{18,10},{26,18},{... | collective-permute-start | bytes 196616 | tf_op jit(solution)/shard_map/ppermute | solution.py:17
  108.8 6.7 %collective-permute-start.42 = (bf16[32,1024]{1,0:T(8,128)(2,1)S(1)}, bf16[32,1024]{1,0:T(8,128)(2,1)S(1)}, u32[]{:S(2)}, u32[]{:S(2)}) collective-permute-start(bf16[32,1024]{1,0:T(8,128)(2,1)S(1)} %get-tuple-element.214), channel_id=1, source_target_pairs={{0,4},{2,6},{4,0},{6,2},{1,5},{3,7},{5,1},{7,3},{8,12},{10,14},{12... | collective-permute-start | bytes 196616 | tf_op jit(solution)/shard_map/ppermute | solution.py:32
  112.8 4.8 %collective-permute-start.46 = (bf16[32,1024]{1,0:T(8,128)(2,1)S(1)}, bf16[32,1024]{1,0:T(8,128)(2,1)S(1)}, u32[]{:S(2)}, u32[]{:S(2)}) collective-permute-start(bf16[32,1024]{1,0:T(8,128)(2,1)S(1)} %arrive.7.refs_3_.first), channel_id=1, source_target_pairs={{0,4},{2,6},{4,0},{6,2},{1,5},{3,7},{5,1},{7,3},{8,12},{10,14},{12... | collective-permute-start | bytes 196616 | tf_op jit(solution)/shard_map/ppermute | solution.py:32
  113.5 5.1 %collective-permute-start.45 = (bf16[32,1024]{1,0:T(8,128)(2,1)S(1)}, bf16[32,1024]{1,0:T(8,128)(2,1)S(1)}, u32[]{:S(2)}, u32[]{:S(2)}) collective-permute-start(bf16[32,1024]{1,0:T(8,128)(2,1)S(1)} %arrive.7.refs_3_.first), channel_id=1, source_target_pairs={{0,6},{2,4},{4,2},{6,0},{1,7},{3,5},{5,3},{7,1},{8,14},{10,12},{12... | collective-permute-start | bytes 196616 | tf_op jit(solution)/shard_map/ppermute | solution.py:32
  114.9 3.8 %collective-permute-start.44 = (bf16[32,1024]{1,0:T(8,128)(2,1)S(1)}, bf16[32,1024]{1,0:T(8,128)(2,1)S(1)}, u32[]{:S(2)}, u32[]{:S(2)}) collective-permute-start(bf16[32,1024]{1,0:T(8,128)(2,1)S(1)} %arrive.7.refs_3_.first), channel_id=1, source_target_pairs={{0,2},{2,0},{4,6},{6,4},{1,3},{3,1},{5,7},{7,5},{8,10},{10,8},{12,... | collective-permute-start | bytes 196616 | tf_op jit(solution)/shard_map/ppermute | solution.py:32
  119.2 5.0 %collective-permute-start.48 = (bf16[128,1024]{1,0:T(8,128)(2,1)S(1)}, bf16[128,1024]{1,0:T(8,128)(2,1)S(1)}, u32[]{:S(2)}, u32[]{:S(2)}) collective-permute-start(bf16[128,1024]{1,0:T(8,128)(2,1)S(1)} %get-tuple-element.225.refs_0_), channel_id=1, source_target_pairs={{0,1},{1,0},{2,3},{3,2},{4,5},{5,4},{6,7},{7,6},{8,9},{9,8},{10,11... | collective-permute-start | bytes 786440 | tf_op jit(solution)/shard_map/ppermute | solution.py:22
  123.5 1.6 %collective-permute-start.47 = (bf16[128,1024]{1,0:T(8,128)(2,1)S(1)}, bf16[128,1024]{1,0:T(8,128)(2,1)S(1)}, u32[]{:S(2)}, u32[]{:S(2)}) collective-permute-start(bf16[128,1024]{1,0:T(8,128)(2,1)S(1)} %product_part.11.refs_0_), channel_id=1, source_target_pairs={{0,1},{1,0},{2,3},{3,2},{4,5},{5,4},{6,7},{7,6},{8,9},{9,8},{10,11... | collective-permute-start | bytes 786440 | tf_op jit(solution)/shard_map/ppermute | solution.py:22
  125.7 7.5 %collective-permute-start.49 = (bf16[32,1024]{1,0:T(8,128)(2,1)S(1)}, bf16[32,1024]{1,0:T(8,128)(2,1)S(1)}, u32[]{:S(2)}, u32[]{:S(2)}) collective-permute-start(bf16[32,1024]{1,0:T(8,128)(2,1)S(1)} %get-tuple-element.230), channel_id=1, source_target_pairs={{0,4},{2,6},{4,0},{6,2},{1,5},{3,7},{5,1},{7,3},{8,12},{10,14},{12... | collective-permute-start | bytes 196616 | tf_op jit(solution)/shard_map/ppermute | solution.py:32
  126.3 6.9 %collective-permute-start.50 = (bf16[32,1024]{1,0:T(8,128)(2,1)S(1)}, bf16[32,1024]{1,0:T(8,128)(2,1)S(1)}, u32[]{:S(2)}, u32[]{:S(2)}) collective-permute-start(bf16[32,1024]{1,0:T(8,128)(2,1)S(1)} %get-tuple-element.231), channel_id=1, source_target_pairs={{0,6},{2,4},{4,2},{6,0},{1,7},{3,5},{5,3},{7,1},{8,14},{10,12},{12... | collective-permute-start | bytes 196616 | tf_op jit(solution)/shard_map/ppermute | solution.py:32
  127.8 6.7 %collective-permute-start.51 = (bf16[32,1024]{1,0:T(8,128)(2,1)S(1)}, bf16[32,1024]{1,0:T(8,128)(2,1)S(1)}, u32[]{:S(2)}, u32[]{:S(2)}) collective-permute-start(bf16[32,1024]{1,0:T(8,128)(2,1)S(1)} %get-tuple-element.232), channel_id=1, source_target_pairs={{0,2},{2,0},{4,6},{6,4},{1,3},{3,1},{5,7},{7,5},{8,10},{10,8},{12,... | collective-permute-start | bytes 196616 | tf_op jit(solution)/shard_map/ppermute | solution.py:32

commit v17 on v15

--- a/solution.py
+++ b/solution.py
@@ -41,7 +41,7 @@
 
 def beside(turn):
     size = lax.axis_size("row")
-    return [[size - 1, size - 2], list(range(1, size - 2))][turn] if size > 2 else [[], [1]][turn]
+    return [list(range(2, size - 1)), [1], [size - 1]][turn] if size > 2 else [[], [1], []][turn]
 
 
 def after(block, other):
@@ -458,7 +458,9 @@
                     turned_weight, [jax.ShapeDtypeStruct((width, hidden), BF)], after(down_kept, terms)
                 )
                 stored, bases, cots = fetch(after(sample_ids, terms), inputs, send_base, recv_base, cotangent)
-                terms_in[0] = after(terms_in[0], (down_turned, stored))
+                for j in beside(2):
+                    cot_pieces[j] = swap_rows(after(last_cot, down_turned), j)
+                terms_in[0] = after(terms_in[0], (down_turned, stored, [cot_pieces[j] for j in beside(2)]))
             if tick == 1:
                 (up_turned,) = run(turned_weight, [jax.ShapeDtypeStruct((hidden, width), BF)], after(up_kept, terms))
                 turn_blocks(0, terms)
@@ -506,7 +508,9 @@
             terms_in[0] = after(terms_in[0], (turned_ins, turned_acts))
             if step == ticks - 2:
                 begun_up = begin_grad([turned_ins[1:]], [*pre_grads[1:tick], grad_pre, *pre_grads[tick + 1 :]])
-                terms_in[0] = after(terms_in[0], begun_up)
+                for j in beside(2):
+                    out_terms[j] = swap_rows(after(out_pieces[j], begun_up), j)
+                terms_in[0] = after(terms_in[0], (begun_up, [out_terms[j] for j in beside(2)]))
             (sending,) = run(leave_back, [piece_like], grad_out, *terms_in)
             seen_grad[tick] = sending
         pre_grads[tick] = grad_pre

time: 134 us -> 138 us (1.030)
  waiting for transfers between devices: 39.5 us -> 45.3 us
  starting transfers between devices: 64 us -> 61.9 us
    ppermute x4, waiting for transfers between devices: 3.14 us -> 6.93 us  [hand_over(): lax.ppermute(block, 'section', [(i - distance, i) for i in sections if i...]
    ppermute x36, starting transfers between devices: 44.2 us -> 41.3 us  [swap_rows(): lax.ppermute(block, 'row', [(i, partner(i, j, size)) for i in range(size)])]
    ppermute x36, waiting for transfers between devices: 31.4 us -> 33.4 us  [swap_rows(): lax.ppermute(block, 'row', [(i, partner(i, j, size)) for i in range(size)])]
  transfers between devices with their start and end apart: 52 -> 52, of which waited for: 27 -> 28; matrix products, arithmetic and copies ran while one was open for 0% -> 0% of each run, Pallas kernels for 17% -> 15%
where the time goes in v17:
time: 138 us
  starting transfers between devices  61.9 us (45%)
  waiting for transfers between devices  45.3 us (33%)
  Pallas kernels  29.4 us (21%)
    ppermute x36, starting transfers between devices, swap_rows(): lax.ppermute(block, 'row', [(i, partner(i, j, size)) for i in range(size)])  41.3 us
    ppermute x36, waiting for transfers between devices, swap_rows(): lax.ppermute(block, 'row', [(i, partner(i, j, size)) for i in range(size)])  33.4 us
    pallas_call x45, Pallas kernels, run(): pl.pallas_call(kernel, in_specs=vmem(len(ins)), out_specs=vmem(len(outs))...  18 us
    ppermute x4, starting transfers between devices, hand_over(): lax.ppermute(block, 'section', [(i - distance, i) for i in sections if i...  10.9 us
    ppermute x12, starting transfers between devices, turn(): lax.ppermute(block, axis, [(i, (i + distance) % size) for i in range(size)])  9.8 us
    ppermute x4, waiting for transfers between devices, hand_over(): lax.ppermute(block, 'section', [(i - distance, i) for i in sections if i...  6.93 us
    ppermute x12, waiting for transfers between devices, turn(): lax.ppermute(block, axis, [(i, (i + distance) % size) for i in range(size)])  4.91 us
    pallas_call x1, Pallas kernels, end_grads(): pl.pallas_call(functools.partial(grads_ended, tuple(((len(lefts), len(rig...  3.8 us
  transfers between devices with their start and end apart: 52, of which 28 were waited for; matrix products, arithmetic and copies ran while one was open for 0% of the time, Pallas kernels for 15%

profile of v17, /device:TPU:3, one launch (start us, length us, event | category | flops | bytes accessed | tf_op | source)
XLA Modules:
  0.0 137.8 jit_solution(2957340276467913884)
XLA Ops:
  0.6 0.9 first.1
  1.5 3.4 %collective-permute-start.2 = (bf16[32,1024]{1,0:T(8,128)(2,1)S(1)}, bf16[32,1024]{1,0:T(8,128)(2,1)S(1)}, u32[]{:S(2)}, u32[]{:S(2)}) collective-permute-start(bf16[32,1024]{1,0:T(8,128)(2,1)S(1)} %get-tuple-element.129.refs_3_.first.refs_0_), channel_id=1, source_target_pairs={{0,6},{2,4},{4,2},{6,0},{1,7},{3,5},{5,3},{7,1},{8,14},{10,12},{12... | collective-permute-start | bytes 196616 | tf_op jit(solution)/shard_map/ppermute | solution.py:31
  5.3 3.5 %hold.1 = (bf16[1024,2048]{1,0:T(8,128)(2,1)S(1)}, bf16[2048,1024]{1,0:T(8,128)(2,1)S(1)}) custom-call(bf16[1024,2048]{1,0:T(8,128)(2,1)} %bitcast.4, bf16[2048,1024]{1,0:T(8,128)(2,1)} %bitcast.5), custom_call_target="tpu_custom_call" | custom-call | bytes 16777216 | tf_op jit(solution)/shard_map/hold/pallas_call | solution.py:214
  8.8 2.0 %collective-permute-done.1.refs_1_ = bf16[32,1024]{1,0:T(8,128)(2,1)S(1)} collective-permute-done((bf16[32,1024]{1,0:T(8,128)(2,1)S(1)}, bf16[32,1024]{1,0:T(8,128)(2,1)S(1)}, u32[]{:S(2)}, u32[]{:S(2)}) %collective-permute-start.1) | collective-permute-done | bytes 65568 | tf_op jit(solution)/shard_map/ppermute | solution.py:31
  11.3 0.7 collective-permute-start.4
  12.5 0.6 collective-permute-done.4.refs_1_.refs_3_
  14.5 1.2 turned_weight.2.refs_4_.weight.refs_5_
  15.8 0.9 collective-permute-start.5
  16.6 1.7 %collective-permute-start.6 = (bf16[32,1024]{1,0:T(8,128)(2,1)S(1)}, bf16[32,1024]{1,0:T(8,128)(2,1)S(1)}, u32[]{:S(2)}, u32[]{:S(2)}) collective-permute-start(bf16[32,1024]{1,0:T(8,128)(2,1)S(1)} %get-tuple-element.135), channel_id=1, source_target_pairs={{0,6},{2,4},{4,2},{6,0},{1,7},{3,5},{5,3},{7,1},{8,14},{10,12},{12... | collective-permute-start | bytes 196616 | tf_op jit(solution)/shard_map/ppermute | solution.py:31
  18.6 1.6 %collective-permute-start.8 = (bf16[32,1024]{1,0:T(8,128)(2,1)S(1)}, bf16[32,1024]{1,0:T(8,128)(2,1)S(1)}, u32[]{:S(2)}, u32[]{:S(2)}) collective-permute-start(bf16[32,1024]{1,0:T(8,128)(2,1)S(1)} %get-tuple-element.137), channel_id=1, source_target_pairs={{0,2},{2,0},{4,6},{6,4},{1,3},{3,1},{5,7},{7,5},{8,10},{10,8},{12,... | collective-permute-start | bytes 196616 | tf_op jit(solution)/shard_map/ppermute | solution.py:31
  20.2 1.7 %fetch.1 = (bf16[32,1024]{1,0:T(8,128)(2,1)S(1)}, bf16[32,1024]{1,0:T(8,128)(2,1)S(1)}, bf16[32,1024]{1,0:T(8,128)(2,1)S(1)}, bf16[32,1024]{1,0:T(8,128)(2,1)S(1...) custom-call(s32[6]{0:T(128)S(1)} %copy-done, bf16[1,3,32,1024]{3,2,1,0:T(8,128)(2,1)} %inputs.3, ...), custom_call_target="tpu_custom_call" | custom-call | bytes 2097152 | tf_op jit(solution)/shard_map/fetch/pallas_call | solution.py:109
  21.9 3.6 %collective-permute-done.7.refs_2_ = bf16[32,1024]{1,0:T(8,128)(2,1)S(1)} collective-permute-done((bf16[32,1024]{1,0:T(8,128)(2,1)S(1)}, bf16[32,1024]{1,0:T(8,128)(2,1)S(1)}, u32[]{:S(2)}, u32[]{:S(2)}) %collective-permute-start.7) | collective-permute-done | bytes 65568 | tf_op jit(solution)/shard_map/ppermute | solution.py:31
  25.6 3.1 %collective-permute-start.9 = (bf16[32,1024]{1,0:T(8,128)(2,1)S(1)}, bf16[32,1024]{1,0:T(8,128)(2,1)S(1)}, u32[]{:S(2)}, u32[]{:S(2)}) collective-permute-start(bf16[32,1024]{1,0:T(8,128)(2,1)S(1)} %get-tuple-element.146), channel_id=1, source_target_pairs={{0,8},{8,16},{16,24},{1,9},{9,17},{17,25},{2,10},{10,18},{18,26},{... | collective-permute-start | bytes 196616 | tf_op jit(solution)/shard_map/ppermute | solution.py:17
  28.8 1.8 %collective-permute-done.9.arrived = bf16[32,1024]{1,0:T(8,128)(2,1)S(1)} collective-permute-done((bf16[32,1024]{1,0:T(8,128)(2,1)S(1)}, bf16[32,1024]{1,0:T(8,128)(2,1)S(1)}, u32[]{:S(2)}, u32[]{:S(2)}) %collective-permute-start.9) | collective-permute-done | bytes 65568 | tf_op jit(solution)/shard_map/ppermute | solution.py:17
  30.6 1.7 %collective-permute-start.13 = (bf16[32,1024]{1,0:T(8,128)(2,1)S(1)}, bf16[32,1024]{1,0:T(8,128)(2,1)S(1)}, u32[]{:S(2)}, u32[]{:S(2)}) collective-permute-start(bf16[32,1024]{1,0:T(8,128)(2,1)S(1)} %arrive.4.refs_4_.first.refs_1_), channel_id=1, source_target_pairs={{0,6},{2,4},{4,2},{6,0},{1,7},{3,5},{5,3},{7,1},{8,14},{10,12},{12... | collective-permute-start | bytes 196616 | tf_op jit(solution)/shard_map/ppermute | solution.py:31
  32.3 1.9 %collective-permute-start.11 = (bf16[32,1024]{1,0:T(8,128)(2,1)S(1)}, bf16[32,1024]{1,0:T(8,128)(2,1)S(1)}, u32[]{:S(2)}, u32[]{:S(2)}) collective-permute-start(bf16[32,1024]{1,0:T(8,128)(2,1)S(1)} %arrive.4.refs_4_.first.refs_1_), channel_id=1, source_target_pairs={{0,2},{2,0},{4,6},{6,4},{1,3},{3,1},{5,7},{7,5},{8,10},{10,8},{12,... | collective-permute-start | bytes 196616 | tf_op jit(solution)/shard_map/ppermute | solution.py:31
  34.2 1.5 %collective-permute-done.13.refs_3_ = bf16[32,1024]{1,0:T(8,128)(2,1)S(1)} collective-permute-done((bf16[32,1024]{1,0:T(8,128)(2,1)S(1)}, bf16[32,1024]{1,0:T(8,128)(2,1)S(1)}, u32[]{:S(2)}, u32[]{:S(2)}) %collective-permute-start.13) | collective-permute-done | bytes 65568 | tf_op jit(solution)/shard_map/ppermute | solution.py:31
  35.8 3.8 %collective-permute-done.12.refs_2_ = bf16[32,1024]{1,0:T(8,128)(2,1)S(1)} collective-permute-done((bf16[32,1024]{1,0:T(8,128)(2,1)S(1)}, bf16[32,1024]{1,0:T(8,128)(2,1)S(1)}, u32[]{:S(2)}, u32[]{:S(2)}) %collective-permute-start.12) | collective-permute-done | bytes 65568 | tf_op jit(solution)/shard_map/ppermute | solution.py:31
  40.0 1.1 collective-permute-start.15
  41.6 0.6 collective-permute-done.15.refs_1_.refs_3_
  43.6 1.8 %collective-permute-start.16 = (bf16[32,1024]{1,0:T(8,128)(2,1)S(1)}, bf16[32,1024]{1,0:T(8,128)(2,1)S(1)}, u32[]{:S(2)}, u32[]{:S(2)}) collective-permute-start(bf16[32,1024]{1,0:T(8,128)(2,1)S(1)} %get-tuple-element.153), channel_id=1, source_target_pairs={{0,6},{2,4},{4,2},{6,0},{1,7},{3,5},{5,3},{7,1},{8,14},{10,12},{12... | collective-permute-start | bytes 196616 | tf_op jit(solution)/shard_map/ppermute | solution.py:31
  45.4 1.9 %collective-permute-start.18 = (bf16[32,1024]{1,0:T(8,128)(2,1)S(1)}, bf16[32,1024]{1,0:T(8,128)(2,1)S(1)}, u32[]{:S(2)}, u32[]{:S(2)}) collective-permute-start(bf16[32,1024]{1,0:T(8,128)(2,1)S(1)} %get-tuple-element.155), channel_id=1, source_target_pairs={{0,2},{2,0},{4,6},{6,4},{1,3},{3,1},{5,7},{7,5},{8,10},{10,8},{12,... | collective-permute-start | bytes 196616 | tf_op jit(solution)/shard_map/ppermute | solution.py:31
  47.6 1.2 turned_weight.3.refs_4_
  49.0 3.3 %collective-permute-done.17.refs_2_ = bf16[32,1024]{1,0:T(8,128)(2,1)S(1)} collective-permute-done((bf16[32,1024]{1,0:T(8,128)(2,1)S(1)}, bf16[32,1024]{1,0:T(8,128)(2,1)S(1)}, u32[]{:S(2)}, u32[]{:S(2)}) %collective-permute-start.17) | collective-permute-done | bytes 65568 | tf_op jit(solution)/shard_map/ppermute | solution.py:31
  52.4 3.7 %collective-permute-start.19 = (bf16[32,1024]{1,0:T(8,128)(2,1)S(1)}, bf16[32,1024]{1,0:T(8,128)(2,1)S(1)}, u32[]{:S(2)}, u32[]{:S(2)}) collective-permute-start(bf16[32,1024]{1,0:T(8,128)(2,1)S(1)} %get-tuple-element.163), channel_id=1, source_target_pairs={{0,8},{8,16},{16,24},{1,9},{9,17},{17,25},{2,10},{10,18},{18,26},{... | collective-permute-start | bytes 196616 | tf_op jit(solution)/shard_map/ppermute | solution.py:17
  56.1 2.0 %collective-permute-start.23 = (bf16[32,1024]{1,0:T(8,128)(2,1)S(1)}, bf16[32,1024]{1,0:T(8,128)(2,1)S(1)}, u32[]{:S(2)}, u32[]{:S(2)}) collective-permute-start(bf16[32,1024]{1,0:T(8,128)(2,1)S(1)} %get-tuple-element.166.refs_3_.first), channel_id=1, source_target_pairs={{0,6},{2,4},{4,2},{6,0},{1,7},{3,5},{5,3},{7,1},{8,14},{10,12},{12... | collective-permute-start | bytes 196616 | tf_op jit(solution)/shard_map/ppermute | solution.py:31
  58.2 1.4 collective-permute-start.22
  59.6 2.3 %collective-permute-start.20 = (bf16[32,1024]{1,0:T(8,128)(2,1)S(1)}, bf16[32,1024]{1,0:T(8,128)(2,1)S(1)}, u32[]{:S(2)}, u32[]{:S(2)}) collective-permute-start(bf16[32,1024]{1,0:T(8,128)(2,1)S(1)} %arrive.5.refs_3_.refs_2_), channel_id=1, source_target_pairs={{0,2},{2,0},{4,6},{6,4},{1,3},{3,1},{5,7},{7,5},{8,10},{10,8},{12,... | collective-permute-start | bytes 196616 | tf_op jit(solution)/shard_map/ppermute | solution.py:31
  62.7 1.9 %collective-permute-start.26 = (bf16[128,1024]{1,0:T(8,128)(2,1)S(1)}, bf16[128,1024]{1,0:T(8,128)(2,1)S(1)}, u32[]{:S(2)}, u32[]{:S(2)}) collective-permute-start(bf16[128,1024]{1,0:T(8,128)(2,1)S(1)} %product_part.8.refs_0_), channel_id=1, source_target_pairs={{0,1},{1,0},{2,3},{3,2},{4,5},{5,4},{6,7},{7,6},{8,9},{9,8},{10,11... | collective-permute-start | bytes 786440 | tf_op jit(solution)/shard_map/ppermute | solution.py:22
  64.7 2.3 %collective-permute-done.21.refs_1_ = bf16[32,1024]{1,0:T(8,128)(2,1)S(1)} collective-permute-done((bf16[32,1024]{1,0:T(8,128)(2,1)S(1)}, bf16[32,1024]{1,0:T(8,128)(2,1)S(1)}, u32[]{:S(2)}, u32[]{:S(2)}) %collective-permute-start.21) | collective-permute-done | bytes 65568 | tf_op jit(solution)/shard_map/ppermute | solution.py:31
  67.5 1.0 collective-permute-start.24
  71.1 1.6 %collective-permute-start.28 = (bf16[32,1024]{1,0:T(8,128)(2,1)S(1)}, bf16[32,1024]{1,0:T(8,128)(2,1)S(1)}, u32[]{:S(2)}, u32[]{:S(2)}) collective-permute-start(bf16[32,1024]{1,0:T(8,128)(2,1)S(1)} %get-tuple-element.177), channel_id=1, source_target_pairs={{0,6},{2,4},{4,2},{6,0},{1,7},{3,5},{5,3},{7,1},{8,14},{10,12},{12... | collective-permute-start | bytes 196616 | tf_op jit(solution)/shard_map/ppermute | solution.py:31
  72.7 2.0 %collective-permute-start.30 = (bf16[32,1024]{1,0:T(8,128)(2,1)S(1)}, bf16[32,1024]{1,0:T(8,128)(2,1)S(1)}, u32[]{:S(2)}, u32[]{:S(2)}) collective-permute-start(bf16[32,1024]{1,0:T(8,128)(2,1)S(1)} %get-tuple-element.179), channel_id=1, source_target_pairs={{0,2},{2,0},{4,6},{6,4},{1,3},{3,1},{5,7},{7,5},{8,10},{10,8},{12,... | collective-permute-start | bytes 196616 | tf_op jit(solution)/shard_map/ppermute | solution.py:31
  75.1 1.4 %collective-permute-done.28.refs_1_ = bf16[32,1024]{1,0:T(8,128)(2,1)S(1)} collective-permute-done((bf16[32,1024]{1,0:T(8,128)(2,1)S(1)}, bf16[32,1024]{1,0:T(8,128)(2,1)S(1)}, u32[]{:S(2)}, u32[]{:S(2)}) %collective-permute-start.28) | collective-permute-done | bytes 65568 | tf_op jit(solution)/shard_map/ppermute | solution.py:31
  76.5 3.3 %collective-permute-done.29.refs_2_ = bf16[32,1024]{1,0:T(8,128)(2,1)S(1)} collective-permute-done((bf16[32,1024]{1,0:T(8,128)(2,1)S(1)}, bf16[32,1024]{1,0:T(8,128)(2,1)S(1)}, u32[]{:S(2)}, u32[]{:S(2)}) %collective-permute-start.29) | collective-permute-done | bytes 65568 | tf_op jit(solution)/shard_map/ppermute | solution.py:31
  79.9 2.1 %collective-permute-start.31 = (bf16[32,1024]{1,0:T(8,128)(2,1)S(1)}, bf16[32,1024]{1,0:T(8,128)(2,1)S(1)}, u32[]{:S(2)}, u32[]{:S(2)}) collective-permute-start(bf16[32,1024]{1,0:T(8,128)(2,1)S(1)} %leave_back.2.refs_5_), channel_id=1, source_target_pairs={{8,0},{16,8},{24,16},{9,1},{17,9},{25,17},{10,2},{18,10},{26,18},{... | collective-permute-start | bytes 196616 | tf_op jit(solution)/shard_map/ppermute | solution.py:17
  82.2 0.7 down_again.1
  83.0 2.8 %collective-permute-done.31.arrived = bf16[32,1024]{1,0:T(8,128)(2,1)S(1)} collective-permute-done((bf16[32,1024]{1,0:T(8,128)(2,1)S(1)}, bf16[32,1024]{1,0:T(8,128)(2,1)S(1)}, u32[]{:S(2)}, u32[]{:S(2)}) %collective-permute-start.31) | collective-permute-done | bytes 65568 | tf_op jit(solution)/shard_map/ppermute | solution.py:17
  85.8 1.6 %collective-permute-start.35 = (bf16[32,1024]{1,0:T(8,128)(2,1)S(1)}, bf16[32,1024]{1,0:T(8,128)(2,1)S(1)}, u32[]{:S(2)}, u32[]{:S(2)}) collective-permute-start(bf16[32,1024]{1,0:T(8,128)(2,1)S(1)} %arrive.6.refs_4_.first), channel_id=1, source_target_pairs={{0,6},{2,4},{4,2},{6,0},{1,7},{3,5},{5,3},{7,1},{8,14},{10,12},{12... | collective-permute-start | bytes 196616 | tf_op jit(solution)/shard_map/ppermute | solution.py:31
  87.4 2.0 %collective-permute-start.33 = (bf16[32,1024]{1,0:T(8,128)(2,1)S(1)}, bf16[32,1024]{1,0:T(8,128)(2,1)S(1)}, u32[]{:S(2)}, u32[]{:S(2)}) collective-permute-start(bf16[32,1024]{1,0:T(8,128)(2,1)S(1)} %arrive.6.refs_4_.first), channel_id=1, source_target_pairs={{0,2},{2,0},{4,6},{6,4},{1,3},{3,1},{5,7},{7,5},{8,10},{10,8},{12,... | collective-permute-start | bytes 196616 | tf_op jit(solution)/shard_map/ppermute | solution.py:31
  89.4 1.5 %collective-permute-done.35.refs_3_ = bf16[32,1024]{1,0:T(8,128)(2,1)S(1)} collective-permute-done((bf16[32,1024]{1,0:T(8,128)(2,1)S(1)}, bf16[32,1024]{1,0:T(8,128)(2,1)S(1)}, u32[]{:S(2)}, u32[]{:S(2)}) %collective-permute-start.35) | collective-permute-done | bytes 65568 | tf_op jit(solution)/shard_map/ppermute | solution.py:31
  90.9 2.5 %collective-permute-done.34.refs_2_ = bf16[32,1024]{1,0:T(8,128)(2,1)S(1)} collective-permute-done((bf16[32,1024]{1,0:T(8,128)(2,1)S(1)}, bf16[32,1024]{1,0:T(8,128)(2,1)S(1)}, u32[]{:S(2)}, u32[]{:S(2)}) %collective-permute-start.34) | collective-permute-done | bytes 65568 | tf_op jit(solution)/shard_map/ppermute | solution.py:31
  93.9 2.1 %collective-permute-start.37 = (bf16[128,1024]{1,0:T(8,128)(2,1)S(1)}, bf16[128,1024]{1,0:T(8,128)(2,1)S(1)}, u32[]{:S(2)}, u32[]{:S(2)}) collective-permute-start(bf16[128,1024]{1,0:T(8,128)(2,1)S(1)} %get-tuple-element.200.refs_0_), channel_id=1, source_target_pairs={{0,1},{1,0},{2,3},{3,2},{4,5},{5,4},{6,7},{7,6},{8,9},{9,8},{10,11... | collective-permute-start | bytes 786440 | tf_op jit(solution)/shard_map/ppermute | solution.py:22
  98.8 1.3 grad_begun.2.refs_3_
  100.5 1.6 %collective-permute-start.39 = (bf16[32,1024]{1,0:T(8,128)(2,1)S(1)}, bf16[32,1024]{1,0:T(8,128)(2,1)S(1)}, u32[]{:S(2)}, u32[]{:S(2)}) collective-permute-start(bf16[32,1024]{1,0:T(8,128)(2,1)S(1)} %get-tuple-element.203), channel_id=1, source_target_pairs={{0,6},{2,4},{4,2},{6,0},{1,7},{3,5},{5,3},{7,1},{8,14},{10,12},{12... | collective-permute-start | bytes 196616 | tf_op jit(solution)/shard_map/ppermute | solution.py:31
  102.1 0.7 collective-permute-start.40
  102.7 1.3 collective-permute-start.41
  104.3 1.2 collective-permute-done.39.refs_1_
  105.6 3.8 %collective-permute-done.40.refs_2_ = bf16[32,1024]{1,0:T(8,128)(2,1)S(1)} collective-permute-done((bf16[32,1024]{1,0:T(8,128)(2,1)S(1)}, bf16[32,1024]{1,0:T(8,128)(2,1)S(1)}, u32[]{:S(2)}, u32[]{:S(2)}) %collective-permute-start.40) | collective-permute-done | bytes 65568 | tf_op jit(solution)/shard_map/ppermute | solution.py:31
  109.4 1.9 %collective-permute-start.43 = (bf16[32,1024]{1,0:T(8,128)(2,1)S(1)}, bf16[32,1024]{1,0:T(8,128)(2,1)S(1)}, u32[]{:S(2)}, u32[]{:S(2)}) collective-permute-start(bf16[32,1024]{1,0:T(8,128)(2,1)S(1)} %leave_back.3.refs_4_), channel_id=1, source_target_pairs={{8,0},{16,8},{24,16},{9,1},{17,9},{25,17},{10,2},{18,10},{26,18},{... | collective-permute-start | bytes 196616 | tf_op jit(solution)/shard_map/ppermute | solution.py:17
  111.3 1.6 %collective-permute-start.42 = (bf16[32,1024]{1,0:T(8,128)(2,1)S(1)}, bf16[32,1024]{1,0:T(8,128)(2,1)S(1)}, u32[]{:S(2)}, u32[]{:S(2)}) collective-permute-start(bf16[32,1024]{1,0:T(8,128)(2,1)S(1)} %get-tuple-element.216), channel_id=1, source_target_pairs={{0,6},{2,4},{4,2},{6,0},{1,7},{3,5},{5,3},{7,1},{8,14},{10,12},{12... | collective-permute-start | bytes 196616 | tf_op jit(solution)/shard_map/ppermute | solution.py:31
  112.9 2.4 %collective-permute-done.43.arrived = bf16[32,1024]{1,0:T(8,128)(2,1)S(1)} collective-permute-done((bf16[32,1024]{1,0:T(8,128)(2,1)S(1)}, bf16[32,1024]{1,0:T(8,128)(2,1)S(1)}, u32[]{:S(2)}, u32[]{:S(2)}) %collective-permute-start.43) | collective-permute-done | bytes 65568 | tf_op jit(solution)/shard_map/ppermute | solution.py:17
  115.3 1.6 %collective-permute-start.46 = (bf16[32,1024]{1,0:T(8,128)(2,1)S(1)}, bf16[32,1024]{1,0:T(8,128)(2,1)S(1)}, u32[]{:S(2)}, u32[]{:S(2)}) collective-permute-start(bf16[32,1024]{1,0:T(8,128)(2,1)S(1)} %arrive.7.refs_3_.first), channel_id=1, source_target_pairs={{0,6},{2,4},{4,2},{6,0},{1,7},{3,5},{5,3},{7,1},{8,14},{10,12},{12... | collective-permute-start | bytes 196616 | tf_op jit(solution)/shard_map/ppermute | solution.py:31
  116.9 2.0 %collective-permute-start.44 = (bf16[32,1024]{1,0:T(8,128)(2,1)S(1)}, bf16[32,1024]{1,0:T(8,128)(2,1)S(1)}, u32[]{:S(2)}, u32[]{:S(2)}) collective-permute-start(bf16[32,1024]{1,0:T(8,128)(2,1)S(1)} %arrive.7.refs_3_.first), channel_id=1, source_target_pairs={{0,2},{2,0},{4,6},{6,4},{1,3},{3,1},{5,7},{7,5},{8,10},{10,8},{12,... | collective-permute-start | bytes 196616 | tf_op jit(solution)/shard_map/ppermute | solution.py:31
  118.9 0.8 finish_forward.1
  119.7 1.3 grad_begun.3.refs_7_
  121.0 1.5 %collective-permute-done.45.refs_1_ = bf16[32,1024]{1,0:T(8,128)(2,1)S(1)} collective-permute-done((bf16[32,1024]{1,0:T(8,128)(2,1)S(1)}, bf16[32,1024]{1,0:T(8,128)(2,1)S(1)}, u32[]{:S(2)}, u32[]{:S(2)}) %collective-permute-start.45) | collective-permute-done | bytes 65568 | tf_op jit(solution)/shard_map/ppermute | solution.py:31
  122.9 2.6 %collective-permute-start.48 = (bf16[128,1024]{1,0:T(8,128)(2,1)S(1)}, bf16[128,1024]{1,0:T(8,128)(2,1)S(1)}, u32[]{:S(2)}, u32[]{:S(2)}) collective-permute-start(bf16[128,1024]{1,0:T(8,128)(2,1)S(1)} %get-tuple-element.227.refs_0_), channel_id=1, source_target_pairs={{0,1},{1,0},{2,3},{3,2},{4,5},{5,4},{6,7},{7,6},{8,9},{9,8},{10,11... | collective-permute-start | bytes 786440 | tf_op jit(solution)/shard_map/ppermute | solution.py:22
  126.0 0.6 collective-permute-done.48.refs_1_
  128.1 1.9 %collective-permute-start.49 = (bf16[32,1024]{1,0:T(8,128)(2,1)S(1)}, bf16[32,1024]{1,0:T(8,128)(2,1)S(1)}, u32[]{:S(2)}, u32[]{:S(2)}) collective-permute-start(bf16[32,1024]{1,0:T(8,128)(2,1)S(1)} %get-tuple-element.232), channel_id=1, source_target_pairs={{0,6},{2,4},{4,2},{6,0},{1,7},{3,5},{5,3},{7,1},{8,14},{10,12},{12... | collective-permute-start | bytes 196616 | tf_op jit(solution)/shard_map/ppermute | solution.py:31
  130.2 1.5 %collective-permute-start.51 = (bf16[32,1024]{1,0:T(8,128)(2,1)S(1)}, bf16[32,1024]{1,0:T(8,128)(2,1)S(1)}, u32[]{:S(2)}, u32[]{:S(2)}) collective-permute-start(bf16[32,1024]{1,0:T(8,128)(2,1)S(1)} %get-tuple-element.234), channel_id=1, source_target_pairs={{0,2},{2,0},{4,6},{6,4},{1,3},{3,1},{5,7},{7,5},{8,10},{10,8},{12,... | collective-permute-start | bytes 196616 | tf_op jit(solution)/shard_map/ppermute | solution.py:31
  131.7 3.8 %grads_ended.1 = (bf16[1024,2048]{1,0:T(8,128)(2,1)}, bf16[2048,1024]{1,0:T(8,128)(2,1)}) custom-call(bf16[1024,128]{1,0:T(8,128)(2,1)S(1)} %turned.9.refs_0_, bf16[128,1024]{1,0:T(8,128)(2,1)S(1)} %get-tuple-element.230.refs_1_, bf16[128,1024]{1,0:T(8,128)(2,1)S(1)} %get-tuple-element.231.refs_2_, f32[1024,2048]{1,0:T(8,128)S(1)} %grad_begun.2.refs_3_, ...), custom_call_target="tpu_custom_call" | custom-call | flops 1073741824 | bytes 8388608 | tf_op jit(solution)/shard_map/grads_ended/pallas_call | solution.py:385
  135.5 1.5 %collective-permute-done.50.refs_2_ = bf16[32,1024]{1,0:T(8,128)(2,1)S(1)} collective-permute-done((bf16[32,1024]{1,0:T(8,128)(2,1)S(1)}, bf16[32,1024]{1,0:T(8,128)(2,1)S(1)}, u32[]{:S(2)}, u32[]{:S(2)}) %collective-permute-start.50) | collective-permute-done | bytes 65568 | tf_op jit(solution)/shard_map/ppermute | solution.py:31
  137.0 0.7 finish.1
  (93 shorter events, 17.6 us)
Async XLA Ops:
  1.5 7.3 %collective-permute-start.2 = (bf16[32,1024]{1,0:T(8,128)(2,1)S(1)}, bf16[32,1024]{1,0:T(8,128)(2,1)S(1)}, u32[]{:S(2)}, u32[]{:S(2)}) collective-permute-start(bf16[32,1024]{1,0:T(8,128)(2,1)S(1)} %get-tuple-element.129.refs_3_.first.refs_0_), channel_id=1, source_target_pairs={{0,6},{2,4},{4,2},{6,0},{1,7},{3,5},{5,3},{7,1},{8,14},{10,12},{12... | collective-permute-start | bytes 196616 | tf_op jit(solution)/shard_map/ppermute | solution.py:31
  4.9 5.9 %collective-permute-start.1 = (bf16[32,1024]{1,0:T(8,128)(2,1)S(1)}, bf16[32,1024]{1,0:T(8,128)(2,1)S(1)}, u32[]{:S(2)}, u32[]{:S(2)}) collective-permute-start(bf16[32,1024]{1,0:T(8,128)(2,1)S(1)} %get-tuple-element.129.refs_3_.first.refs_0_), channel_id=1, source_target_pairs={{0,4},{2,6},{4,0},{6,2},{1,5},{3,7},{5,1},{7,3},{8,12},{10,14},{12... | collective-permute-start | bytes 196616 | tf_op jit(solution)/shard_map/ppermute | solution.py:31
  4.9 5.9 %collective-permute-start = (bf16[32,1024]{1,0:T(8,128)(2,1)S(1)}, bf16[32,1024]{1,0:T(8,128)(2,1)S(1)}, u32[]{:S(2)}, u32[]{:S(2)}) collective-permute-start(bf16[32,1024]{1,0:T(8,128)(2,1)S(1)} %get-tuple-element.129.refs_3_.first.refs_0_), channel_id=1, source_target_pairs={{0,2},{2,0},{4,6},{6,4},{1,3},{3,1},{5,7},{7,5},{8,10},{10,8},{12,... | collective-permute-start | bytes 196616 | tf_op jit(solution)/shard_map/ppermute | solution.py:31
  11.3 1.9 %collective-permute-start.4 = (bf16[128,1024]{1,0:T(8,128)(2,1)S(1)}, bf16[128,1024]{1,0:T(8,128)(2,1)S(1)}, u32[]{:S(2)}, u32[]{:S(2)}) collective-permute-start(bf16[128,1024]{1,0:T(8,128)(2,1)S(1)} %get-tuple-element.132.refs_0_.refs_2_), channel_id=1, source_target_pairs={{0,1},{1,0},{2,3},{3,2},{4,5},{5,4},{6,7},{7,6},{8,9},{9,8},{10,11... | collective-permute-start | bytes 786440 | tf_op jit(solution)/shard_map/ppermute | solution.py:22
  12.5 1.6 %collective-permute-start.3 = (bf16[128,1024]{1,0:T(8,128)(2,1)S(1)}, bf16[128,1024]{1,0:T(8,128)(2,1)S(1)}, u32[]{:S(2)}, u32[]{:S(2)}) collective-permute-start(bf16[128,1024]{1,0:T(8,128)(2,1)S(1)} %product_part.6.refs_0_.refs_2_), channel_id=1, source_target_pairs={{0,1},{1,0},{2,3},{3,2},{4,5},{5,4},{6,7},{7,6},{8,9},{9,8},{10,11... | collective-permute-start | bytes 786440 | tf_op jit(solution)/shard_map/ppermute | solution.py:22
  14.5 5.7 %copy-start = (s32[6]{0:T(128)S(1)}, s32[6]{0:T(128)}, u32[]{:S(2)}) copy-start(s32[6]{0:T(128)} %sample_ids) | copy-start | bytes 76
  15.8 6.1 %collective-permute-start.5 = (bf16[32,1024]{1,0:T(8,128)(2,1)S(1)}, bf16[32,1024]{1,0:T(8,128)(2,1)S(1)}, u32[]{:S(2)}, u32[]{:S(2)}) collective-permute-start(bf16[32,1024]{1,0:T(8,128)(2,1)S(1)} %get-tuple-element.166.refs_3_.first), channel_id=1, source_target_pairs={{0,2},{2,0},{4,6},{6,4},{1,3},{3,1},{5,7},{7,5},{8,10},{10,8},{12,... | collective-permute-start | bytes 196616 | tf_op jit(solution)/shard_map/ppermute | solution.py:31
  16.6 5.3 %collective-permute-start.6 = (bf16[32,1024]{1,0:T(8,128)(2,1)S(1)}, bf16[32,1024]{1,0:T(8,128)(2,1)S(1)}, u32[]{:S(2)}, u32[]{:S(2)}) collective-permute-start(bf16[32,1024]{1,0:T(8,128)(2,1)S(1)} %get-tuple-element.135), channel_id=1, source_target_pairs={{0,6},{2,4},{4,2},{6,0},{1,7},{3,5},{5,3},{7,1},{8,14},{10,12},{12... | collective-permute-start | bytes 196616 | tf_op jit(solution)/shard_map/ppermute | solution.py:31
  18.4 7.2 %collective-permute-start.7 = (bf16[32,1024]{1,0:T(8,128)(2,1)S(1)}, bf16[32,1024]{1,0:T(8,128)(2,1)S(1)}, u32[]{:S(2)}, u32[]{:S(2)}) collective-permute-start(bf16[32,1024]{1,0:T(8,128)(2,1)S(1)} %get-tuple-element.136), channel_id=1, source_target_pairs={{0,4},{2,6},{4,0},{6,2},{1,5},{3,7},{5,1},{7,3},{8,12},{10,14},{12... | collective-permute-start | bytes 196616 | tf_op jit(solution)/shard_map/ppermute | solution.py:31
  18.6 7.0 %collective-permute-start.8 = (bf16[32,1024]{1,0:T(8,128)(2,1)S(1)}, bf16[32,1024]{1,0:T(8,128)(2,1)S(1)}, u32[]{:S(2)}, u32[]{:S(2)}) collective-permute-start(bf16[32,1024]{1,0:T(8,128)(2,1)S(1)} %get-tuple-element.137), channel_id=1, source_target_pairs={{0,2},{2,0},{4,6},{6,4},{1,3},{3,1},{5,7},{7,5},{8,10},{10,8},{12,... | collective-permute-start | bytes 196616 | tf_op jit(solution)/shard_map/ppermute | solution.py:31
  25.6 5.0 %collective-permute-start.9 = (bf16[32,1024]{1,0:T(8,128)(2,1)S(1)}, bf16[32,1024]{1,0:T(8,128)(2,1)S(1)}, u32[]{:S(2)}, u32[]{:S(2)}) collective-permute-start(bf16[32,1024]{1,0:T(8,128)(2,1)S(1)} %get-tuple-element.146), channel_id=1, source_target_pairs={{0,8},{8,16},{16,24},{1,9},{9,17},{17,25},{2,10},{10,18},{18,26},{... | collective-permute-start | bytes 196616 | tf_op jit(solution)/shard_map/ppermute | solution.py:17
  28.7 5.5 %collective-permute-start.10 = (bf16[32,1024]{1,0:T(8,128)(2,1)S(1)}, bf16[32,1024]{1,0:T(8,128)(2,1)S(1)}, u32[]{:S(2)}, u32[]{:S(2)}) collective-permute-start(bf16[32,1024]{1,0:T(8,128)(2,1)S(1)} %get-tuple-element.166.refs_3_.first), channel_id=1, source_target_pairs={{0,4},{2,6},{4,0},{6,2},{1,5},{3,7},{5,1},{7,3},{8,12},{10,14},{12... | collective-permute-start | bytes 196616 | tf_op jit(solution)/shard_map/ppermute | solution.py:31
  30.6 5.1 %collective-permute-start.13 = (bf16[32,1024]{1,0:T(8,128)(2,1)S(1)}, bf16[32,1024]{1,0:T(8,128)(2,1)S(1)}, u32[]{:S(2)}, u32[]{:S(2)}) collective-permute-start(bf16[32,1024]{1,0:T(8,128)(2,1)S(1)} %arrive.4.refs_4_.first.refs_1_), channel_id=1, source_target_pairs={{0,6},{2,4},{4,2},{6,0},{1,7},{3,5},{5,3},{7,1},{8,14},{10,12},{12... | collective-permute-start | bytes 196616 | tf_op jit(solution)/shard_map/ppermute | solution.py:31
  32.3 7.3 %collective-permute-start.12 = (bf16[32,1024]{1,0:T(8,128)(2,1)S(1)}, bf16[32,1024]{1,0:T(8,128)(2,1)S(1)}, u32[]{:S(2)}, u32[]{:S(2)}) collective-permute-start(bf16[32,1024]{1,0:T(8,128)(2,1)S(1)} %arrive.4.refs_4_.first.refs_1_), channel_id=1, source_target_pairs={{0,4},{2,6},{4,0},{6,2},{1,5},{3,7},{5,1},{7,3},{8,12},{10,14},{12... | collective-permute-start | bytes 196616 | tf_op jit(solution)/shard_map/ppermute | solution.py:31
  32.3 7.3 %collective-permute-start.11 = (bf16[32,1024]{1,0:T(8,128)(2,1)S(1)}, bf16[32,1024]{1,0:T(8,128)(2,1)S(1)}, u32[]{:S(2)}, u32[]{:S(2)}) collective-permute-start(bf16[32,1024]{1,0:T(8,128)(2,1)S(1)} %arrive.4.refs_4_.first.refs_1_), channel_id=1, source_target_pairs={{0,2},{2,0},{4,6},{6,4},{1,3},{3,1},{5,7},{7,5},{8,10},{10,8},{12,... | collective-permute-start | bytes 196616 | tf_op jit(solution)/shard_map/ppermute | solution.py:31
  40.0 2.2 %collective-permute-start.15 = (bf16[128,1024]{1,0:T(8,128)(2,1)S(1)}, bf16[128,1024]{1,0:T(8,128)(2,1)S(1)}, u32[]{:S(2)}, u32[]{:S(2)}) collective-permute-start(bf16[128,1024]{1,0:T(8,128)(2,1)S(1)} %get-tuple-element.150.refs_0_.refs_2_), channel_id=1, source_target_pairs={{0,1},{1,0},{2,3},{3,2},{4,5},{5,4},{6,7},{7,6},{8,9},{9,8},{10,11... | collective-permute-start | bytes 786440 | tf_op jit(solution)/shard_map/ppermute | solution.py:22
  41.6 1.6 %collective-permute-start.14 = (bf16[128,1024]{1,0:T(8,128)(2,1)S(1)}, bf16[128,1024]{1,0:T(8,128)(2,1)S(1)}, u32[]{:S(2)}, u32[]{:S(2)}) collective-permute-start(bf16[128,1024]{1,0:T(8,128)(2,1)S(1)} %product_part.7.refs_0_.refs_2_), channel_id=1, source_target_pairs={{0,1},{1,0},{2,3},{3,2},{4,5},{5,4},{6,7},{7,6},{8,9},{9,8},{10,11... | collective-permute-start | bytes 786440 | tf_op jit(solution)/shard_map/ppermute | solution.py:22
  43.6 5.4 %collective-permute-start.16 = (bf16[32,1024]{1,0:T(8,128)(2,1)S(1)}, bf16[32,1024]{1,0:T(8,128)(2,1)S(1)}, u32[]{:S(2)}, u32[]{:S(2)}) collective-permute-start(bf16[32,1024]{1,0:T(8,128)(2,1)S(1)} %get-tuple-element.153), channel_id=1, source_target_pairs={{0,6},{2,4},{4,2},{6,0},{1,7},{3,5},{5,3},{7,1},{8,14},{10,12},{12... | collective-permute-start | bytes 196616 | tf_op jit(solution)/shard_map/ppermute | solution.py:31
  45.4 6.9 %collective-permute-start.17 = (bf16[32,1024]{1,0:T(8,128)(2,1)S(1)}, bf16[32,1024]{1,0:T(8,128)(2,1)S(1)}, u32[]{:S(2)}, u32[]{:S(2)}) collective-permute-start(bf16[32,1024]{1,0:T(8,128)(2,1)S(1)} %get-tuple-element.154), channel_id=1, source_target_pairs={{0,4},{2,6},{4,0},{6,2},{1,5},{3,7},{5,1},{7,3},{8,12},{10,14},{12... | collective-permute-start | bytes 196616 | tf_op jit(solution)/shard_map/ppermute | solution.py:31
  45.4 6.9 %collective-permute-start.18 = (bf16[32,1024]{1,0:T(8,128)(2,1)S(1)}, bf16[32,1024]{1,0:T(8,128)(2,1)S(1)}, u32[]{:S(2)}, u32[]{:S(2)}) collective-permute-start(bf16[32,1024]{1,0:T(8,128)(2,1)S(1)} %get-tuple-element.155), channel_id=1, source_target_pairs={{0,2},{2,0},{4,6},{6,4},{1,3},{3,1},{5,7},{7,5},{8,10},{10,8},{12,... | collective-permute-start | bytes 196616 | tf_op jit(solution)/shard_map/ppermute | solution.py:31
  52.4 5.8 %collective-permute-start.19 = (bf16[32,1024]{1,0:T(8,128)(2,1)S(1)}, bf16[32,1024]{1,0:T(8,128)(2,1)S(1)}, u32[]{:S(2)}, u32[]{:S(2)}) collective-permute-start(bf16[32,1024]{1,0:T(8,128)(2,1)S(1)} %get-tuple-element.163), channel_id=1, source_target_pairs={{0,8},{8,16},{16,24},{1,9},{9,17},{17,25},{2,10},{10,18},{18,26},{... | collective-permute-start | bytes 196616 | tf_op jit(solution)/shard_map/ppermute | solution.py:17
  56.1 5.7 %collective-permute-start.23 = (bf16[32,1024]{1,0:T(8,128)(2,1)S(1)}, bf16[32,1024]{1,0:T(8,128)(2,1)S(1)}, u32[]{:S(2)}, u32[]{:S(2)}) collective-permute-start(bf16[32,1024]{1,0:T(8,128)(2,1)S(1)} %get-tuple-element.166.refs_3_.first), channel_id=1, source_target_pairs={{0,6},{2,4},{4,2},{6,0},{1,7},{3,5},{5,3},{7,1},{8,14},{10,12},{12... | collective-permute-start | bytes 196616 | tf_op jit(solution)/shard_map/ppermute | solution.py:31
  58.2 6.5 %collective-permute-start.22 = (bf16[32,1024]{1,0:T(8,128)(2,1)S(1)}, bf16[32,1024]{1,0:T(8,128)(2,1)S(1)}, u32[]{:S(2)}, u32[]{:S(2)}) collective-permute-start(bf16[32,1024]{1,0:T(8,128)(2,1)S(1)} %arrive.5.refs_3_.refs_2_), channel_id=1, source_target_pairs={{0,6},{2,4},{4,2},{6,0},{1,7},{3,5},{5,3},{7,1},{8,14},{10,12},{12... | collective-permute-start | bytes 196616 | tf_op jit(solution)/shard_map/ppermute | solution.py:31
  59.6 7.5 %collective-permute-start.21 = (bf16[32,1024]{1,0:T(8,128)(2,1)S(1)}, bf16[32,1024]{1,0:T(8,128)(2,1)S(1)}, u32[]{:S(2)}, u32[]{:S(2)}) collective-permute-start(bf16[32,1024]{1,0:T(8,128)(2,1)S(1)} %arrive.5.refs_3_.refs_2_), channel_id=1, source_target_pairs={{0,4},{2,6},{4,0},{6,2},{1,5},{3,7},{5,1},{7,3},{8,12},{10,14},{12... | collective-permute-start | bytes 196616 | tf_op jit(solution)/shard_map/ppermute | solution.py:31
  59.6 7.5 %collective-permute-start.20 = (bf16[32,1024]{1,0:T(8,128)(2,1)S(1)}, bf16[32,1024]{1,0:T(8,128)(2,1)S(1)}, u32[]{:S(2)}, u32[]{:S(2)}) collective-permute-start(bf16[32,1024]{1,0:T(8,128)(2,1)S(1)} %arrive.5.refs_3_.refs_2_), channel_id=1, source_target_pairs={{0,2},{2,0},{4,6},{6,4},{1,3},{3,1},{5,7},{7,5},{8,10},{10,8},{12,... | collective-permute-start | bytes 196616 | tf_op jit(solution)/shard_map/ppermute | solution.py:31
  62.7 7.4 %collective-permute-start.26 = (bf16[128,1024]{1,0:T(8,128)(2,1)S(1)}, bf16[128,1024]{1,0:T(8,128)(2,1)S(1)}, u32[]{:S(2)}, u32[]{:S(2)}) collective-permute-start(bf16[128,1024]{1,0:T(8,128)(2,1)S(1)} %product_part.8.refs_0_), channel_id=1, source_target_pairs={{0,1},{1,0},{2,3},{3,2},{4,5},{5,4},{6,7},{7,6},{8,9},{9,8},{10,11... | collective-permute-start | bytes 786440 | tf_op jit(solution)/shard_map/ppermute | solution.py:22
  64.6 4.4 %collective-permute-start.27 = (bf16[128,1024]{1,0:T(8,128)(2,1)S(1)}, bf16[128,1024]{1,0:T(8,128)(2,1)S(1)}, u32[]{:S(2)}, u32[]{:S(2)}) collective-permute-start(bf16[128,1024]{1,0:T(8,128)(2,1)S(1)} %get-tuple-element.167.refs_0_), channel_id=1, source_target_pairs={{0,1},{1,0},{2,3},{3,2},{4,5},{5,4},{6,7},{7,6},{8,9},{9,8},{10,11... | collective-permute-start | bytes 786440 | tf_op jit(solution)/shard_map/ppermute | solution.py:22
  67.5 2.1 %collective-permute-start.24 = (bf16[128,1024]{1,0:T(8,128)(2,1)S(1)}, bf16[128,1024]{1,0:T(8,128)(2,1)S(1)}, u32[]{:S(2)}, u32[]{:S(2)}) collective-permute-start(bf16[128,1024]{1,0:T(8,128)(2,1)S(1)} %get-tuple-element.186.refs_2_.refs_0_), channel_id=1, source_target_pairs={{0,1},{1,0},{2,3},{3,2},{4,5},{5,4},{6,7},{7,6},{8,9},{9,8},{10,11... | collective-permute-start | bytes 786440 | tf_op jit(solution)/shard_map/ppermute | solution.py:22
  68.9 1.6 %collective-permute-start.25 = (bf16[128,1024]{1,0:T(8,128)(2,1)S(1)}, bf16[128,1024]{1,0:T(8,128)(2,1)S(1)}, u32[]{:S(2)}, u32[]{:S(2)}) collective-permute-start(bf16[128,1024]{1,0:T(8,128)(2,1)S(1)} %product_part.9.refs_2_), channel_id=1, source_target_pairs={{0,1},{1,0},{2,3},{3,2},{4,5},{5,4},{6,7},{7,6},{8,9},{9,8},{10,11... | collective-permute-start | bytes 786440 | tf_op jit(solution)/shard_map/ppermute | solution.py:22
  71.1 5.4 %collective-permute-start.28 = (bf16[32,1024]{1,0:T(8,128)(2,1)S(1)}, bf16[32,1024]{1,0:T(8,128)(2,1)S(1)}, u32[]{:S(2)}, u32[]{:S(2)}) collective-permute-start(bf16[32,1024]{1,0:T(8,128)(2,1)S(1)} %get-tuple-element.177), channel_id=1, source_target_pairs={{0,6},{2,4},{4,2},{6,0},{1,7},{3,5},{5,3},{7,1},{8,14},{10,12},{12... | collective-permute-start | bytes 196616 | tf_op jit(solution)/shard_map/ppermute | solution.py:31
  72.7 7.1 %collective-permute-start.29 = (bf16[32,1024]{1,0:T(8,128)(2,1)S(1)}, bf16[32,1024]{1,0:T(8,128)(2,1)S(1)}, u32[]{:S(2)}, u32[]{:S(2)}) collective-permute-start(bf16[32,1024]{1,0:T(8,128)(2,1)S(1)} %get-tuple-element.178), channel_id=1, source_target_pairs={{0,4},{2,6},{4,0},{6,2},{1,5},{3,7},{5,1},{7,3},{8,12},{10,14},{12... | collective-permute-start | bytes 196616 | tf_op jit(solution)/shard_map/ppermute | solution.py:31
  72.7 7.1 %collective-permute-start.30 = (bf16[32,1024]{1,0:T(8,128)(2,1)S(1)}, bf16[32,1024]{1,0:T(8,128)(2,1)S(1)}, u32[]{:S(2)}, u32[]{:S(2)}) collective-permute-start(bf16[32,1024]{1,0:T(8,128)(2,1)S(1)} %get-tuple-element.179), channel_id=1, source_target_pairs={{0,2},{2,0},{4,6},{6,4},{1,3},{3,1},{5,7},{7,5},{8,10},{10,8},{12,... | collective-permute-start | bytes 196616 | tf_op jit(solution)/shard_map/ppermute | solution.py:31
  79.9 5.9 %collective-permute-start.31 = (bf16[32,1024]{1,0:T(8,128)(2,1)S(1)}, bf16[32,1024]{1,0:T(8,128)(2,1)S(1)}, u32[]{:S(2)}, u32[]{:S(2)}) collective-permute-start(bf16[32,1024]{1,0:T(8,128)(2,1)S(1)} %leave_back.2.refs_5_), channel_id=1, source_target_pairs={{8,0},{16,8},{24,16},{9,1},{17,9},{25,17},{10,2},{18,10},{26,18},{... | collective-permute-start | bytes 196616 | tf_op jit(solution)/shard_map/ppermute | solution.py:17
  82.9 6.5 %collective-permute-start.32 = (bf16[32,1024]{1,0:T(8,128)(2,1)S(1)}, bf16[32,1024]{1,0:T(8,128)(2,1)S(1)}, u32[]{:S(2)}, u32[]{:S(2)}) collective-permute-start(bf16[32,1024]{1,0:T(8,128)(2,1)S(1)} %get-tuple-element.198), channel_id=1, source_target_pairs={{0,4},{2,6},{4,0},{6,2},{1,5},{3,7},{5,1},{7,3},{8,12},{10,14},{12... | collective-permute-start | bytes 196616 | tf_op jit(solution)/shard_map/ppermute | solution.py:31
  85.8 5.1 %collective-permute-start.35 = (bf16[32,1024]{1,0:T(8,128)(2,1)S(1)}, bf16[32,1024]{1,0:T(8,128)(2,1)S(1)}, u32[]{:S(2)}, u32[]{:S(2)}) collective-permute-start(bf16[32,1024]{1,0:T(8,128)(2,1)S(1)} %arrive.6.refs_4_.first), channel_id=1, source_target_pairs={{0,6},{2,4},{4,2},{6,0},{1,7},{3,5},{5,3},{7,1},{8,14},{10,12},{12... | collective-permute-start | bytes 196616 | tf_op jit(solution)/shard_map/ppermute | solution.py:31
  87.4 6.0 %collective-permute-start.34 = (bf16[32,1024]{1,0:T(8,128)(2,1)S(1)}, bf16[32,1024]{1,0:T(8,128)(2,1)S(1)}, u32[]{:S(2)}, u32[]{:S(2)}) collective-permute-start(bf16[32,1024]{1,0:T(8,128)(2,1)S(1)} %arrive.6.refs_4_.first), channel_id=1, source_target_pairs={{0,4},{2,6},{4,0},{6,2},{1,5},{3,7},{5,1},{7,3},{8,12},{10,14},{12... | collective-permute-start | bytes 196616 | tf_op jit(solution)/shard_map/ppermute | solution.py:31
  87.4 6.0 %collective-permute-start.33 = (bf16[32,1024]{1,0:T(8,128)(2,1)S(1)}, bf16[32,1024]{1,0:T(8,128)(2,1)S(1)}, u32[]{:S(2)}, u32[]{:S(2)}) collective-permute-start(bf16[32,1024]{1,0:T(8,128)(2,1)S(1)} %arrive.6.refs_4_.first), channel_id=1, source_target_pairs={{0,2},{2,0},{4,6},{6,4},{1,3},{3,1},{5,7},{7,5},{8,10},{10,8},{12,... | collective-permute-start | bytes 196616 | tf_op jit(solution)/shard_map/ppermute | solution.py:31
  93.9 3.3 %collective-permute-start.37 = (bf16[128,1024]{1,0:T(8,128)(2,1)S(1)}, bf16[128,1024]{1,0:T(8,128)(2,1)S(1)}, u32[]{:S(2)}, u32[]{:S(2)}) collective-permute-start(bf16[128,1024]{1,0:T(8,128)(2,1)S(1)} %get-tuple-element.200.refs_0_), channel_id=1, source_target_pairs={{0,1},{1,0},{2,3},{3,2},{4,5},{5,4},{6,7},{7,6},{8,9},{9,8},{10,11... | collective-permute-start | bytes 786440 | tf_op jit(solution)/shard_map/ppermute | solution.py:22
  96.4 1.6 %collective-permute-start.36 = (bf16[128,1024]{1,0:T(8,128)(2,1)S(1)}, bf16[128,1024]{1,0:T(8,128)(2,1)S(1)}, u32[]{:S(2)}, u32[]{:S(2)}) collective-permute-start(bf16[128,1024]{1,0:T(8,128)(2,1)S(1)} %product_part.10.refs_0_), channel_id=1, source_target_pairs={{0,1},{1,0},{2,3},{3,2},{4,5},{5,4},{6,7},{7,6},{8,9},{9,8},{10,11... | collective-permute-start | bytes 786440 | tf_op jit(solution)/shard_map/ppermute | solution.py:22
  100.0 4.3 %collective-permute-start.38 = (bf16[32,1024]{1,0:T(8,128)(2,1)S(1)}, bf16[32,1024]{1,0:T(8,128)(2,1)S(1)}, u32[]{:S(2)}, u32[]{:S(2)}) collective-permute-start(bf16[32,1024]{1,0:T(8,128)(2,1)S(1)} %get-tuple-element.214), channel_id=1, source_target_pairs={{0,2},{2,0},{4,6},{6,4},{1,3},{3,1},{5,7},{7,5},{8,10},{10,8},{12,... | collective-permute-start | bytes 196616 | tf_op jit(solution)/shard_map/ppermute | solution.py:31
  100.5 5.1 %collective-permute-start.39 = (bf16[32,1024]{1,0:T(8,128)(2,1)S(1)}, bf16[32,1024]{1,0:T(8,128)(2,1)S(1)}, u32[]{:S(2)}, u32[]{:S(2)}) collective-permute-start(bf16[32,1024]{1,0:T(8,128)(2,1)S(1)} %get-tuple-element.203), channel_id=1, source_target_pairs={{0,6},{2,4},{4,2},{6,0},{1,7},{3,5},{5,3},{7,1},{8,14},{10,12},{12... | collective-permute-start | bytes 196616 | tf_op jit(solution)/shard_map/ppermute | solution.py:31
  102.1 7.2 %collective-permute-start.40 = (bf16[32,1024]{1,0:T(8,128)(2,1)S(1)}, bf16[32,1024]{1,0:T(8,128)(2,1)S(1)}, u32[]{:S(2)}, u32[]{:S(2)}) collective-permute-start(bf16[32,1024]{1,0:T(8,128)(2,1)S(1)} %get-tuple-element.204), channel_id=1, source_target_pairs={{0,4},{2,6},{4,0},{6,2},{1,5},{3,7},{5,1},{7,3},{8,12},{10,14},{12... | collective-permute-start | bytes 196616 | tf_op jit(solution)/shard_map/ppermute | solution.py:31
  102.7 6.6 %collective-permute-start.41 = (bf16[32,1024]{1,0:T(8,128)(2,1)S(1)}, bf16[32,1024]{1,0:T(8,128)(2,1)S(1)}, u32[]{:S(2)}, u32[]{:S(2)}) collective-permute-start(bf16[32,1024]{1,0:T(8,128)(2,1)S(1)} %get-tuple-element.205), channel_id=1, source_target_pairs={{0,2},{2,0},{4,6},{6,4},{1,3},{3,1},{5,7},{7,5},{8,10},{10,8},{12,... | collective-permute-start | bytes 196616 | tf_op jit(solution)/shard_map/ppermute | solution.py:31
  109.4 5.9 %collective-permute-start.43 = (bf16[32,1024]{1,0:T(8,128)(2,1)S(1)}, bf16[32,1024]{1,0:T(8,128)(2,1)S(1)}, u32[]{:S(2)}, u32[]{:S(2)}) collective-permute-start(bf16[32,1024]{1,0:T(8,128)(2,1)S(1)} %leave_back.3.refs_4_), channel_id=1, source_target_pairs={{8,0},{16,8},{24,16},{9,1},{17,9},{25,17},{10,2},{18,10},{26,18},{... | collective-permute-start | bytes 196616 | tf_op jit(solution)/shard_map/ppermute | solution.py:17
  111.3 7.6 %collective-permute-start.42 = (bf16[32,1024]{1,0:T(8,128)(2,1)S(1)}, bf16[32,1024]{1,0:T(8,128)(2,1)S(1)}, u32[]{:S(2)}, u32[]{:S(2)}) collective-permute-start(bf16[32,1024]{1,0:T(8,128)(2,1)S(1)} %get-tuple-element.216), channel_id=1, source_target_pairs={{0,6},{2,4},{4,2},{6,0},{1,7},{3,5},{5,3},{7,1},{8,14},{10,12},{12... | collective-permute-start | bytes 196616 | tf_op jit(solution)/shard_map/ppermute | solution.py:31
  115.3 5.7 %collective-permute-start.46 = (bf16[32,1024]{1,0:T(8,128)(2,1)S(1)}, bf16[32,1024]{1,0:T(8,128)(2,1)S(1)}, u32[]{:S(2)}, u32[]{:S(2)}) collective-permute-start(bf16[32,1024]{1,0:T(8,128)(2,1)S(1)} %arrive.7.refs_3_.first), channel_id=1, source_target_pairs={{0,6},{2,4},{4,2},{6,0},{1,7},{3,5},{5,3},{7,1},{8,14},{10,12},{12... | collective-permute-start | bytes 196616 | tf_op jit(solution)/shard_map/ppermute | solution.py:31
  116.9 5.5 %collective-permute-start.45 = (bf16[32,1024]{1,0:T(8,128)(2,1)S(1)}, bf16[32,1024]{1,0:T(8,128)(2,1)S(1)}, u32[]{:S(2)}, u32[]{:S(2)}) collective-permute-start(bf16[32,1024]{1,0:T(8,128)(2,1)S(1)} %arrive.7.refs_3_.first), channel_id=1, source_target_pairs={{0,4},{2,6},{4,0},{6,2},{1,5},{3,7},{5,1},{7,3},{8,12},{10,14},{12... | collective-permute-start | bytes 196616 | tf_op jit(solution)/shard_map/ppermute | solution.py:31
  116.9 5.5 %collective-permute-start.44 = (bf16[32,1024]{1,0:T(8,128)(2,1)S(1)}, bf16[32,1024]{1,0:T(8,128)(2,1)S(1)}, u32[]{:S(2)}, u32[]{:S(2)}) collective-permute-start(bf16[32,1024]{1,0:T(8,128)(2,1)S(1)} %arrive.7.refs_3_.first), channel_id=1, source_target_pairs={{0,2},{2,0},{4,6},{6,4},{1,3},{3,1},{5,7},{7,5},{8,10},{10,8},{12,... | collective-permute-start | bytes 196616 | tf_op jit(solution)/shard_map/ppermute | solution.py:31
  122.9 3.7 %collective-permute-start.48 = (bf16[128,1024]{1,0:T(8,128)(2,1)S(1)}, bf16[128,1024]{1,0:T(8,128)(2,1)S(1)}, u32[]{:S(2)}, u32[]{:S(2)}) collective-permute-start(bf16[128,1024]{1,0:T(8,128)(2,1)S(1)} %get-tuple-element.227.refs_0_), channel_id=1, source_target_pairs={{0,1},{1,0},{2,3},{3,2},{4,5},{5,4},{6,7},{7,6},{8,9},{9,8},{10,11... | collective-permute-start | bytes 786440 | tf_op jit(solution)/shard_map/ppermute | solution.py:22
  125.9 1.6 %collective-permute-start.47 = (bf16[128,1024]{1,0:T(8,128)(2,1)S(1)}, bf16[128,1024]{1,0:T(8,128)(2,1)S(1)}, u32[]{:S(2)}, u32[]{:S(2)}) collective-permute-start(bf16[128,1024]{1,0:T(8,128)(2,1)S(1)} %product_part.11.refs_0_), channel_id=1, source_target_pairs={{0,1},{1,0},{2,3},{3,2},{4,5},{5,4},{6,7},{7,6},{8,9},{9,8},{10,11... | collective-permute-start | bytes 786440 | tf_op jit(solution)/shard_map/ppermute | solution.py:22
  128.1 7.4 %collective-permute-start.49 = (bf16[32,1024]{1,0:T(8,128)(2,1)S(1)}, bf16[32,1024]{1,0:T(8,128)(2,1)S(1)}, u32[]{:S(2)}, u32[]{:S(2)}) collective-permute-start(bf16[32,1024]{1,0:T(8,128)(2,1)S(1)} %get-tuple-element.232), channel_id=1, source_target_pairs={{0,6},{2,4},{4,2},{6,0},{1,7},{3,5},{5,3},{7,1},{8,14},{10,12},{12... | collective-permute-start | bytes 196616 | tf_op jit(solution)/shard_map/ppermute | solution.py:31
  130.0 7.1 %collective-permute-start.50 = (bf16[32,1024]{1,0:T(8,128)(2,1)S(1)}, bf16[32,1024]{1,0:T(8,128)(2,1)S(1)}, u32[]{:S(2)}, u32[]{:S(2)}) collective-permute-start(bf16[32,1024]{1,0:T(8,128)(2,1)S(1)} %get-tuple-element.233), channel_id=1, source_target_pairs={{0,4},{2,6},{4,0},{6,2},{1,5},{3,7},{5,1},{7,3},{8,12},{10,14},{12... | collective-permute-start | bytes 196616 | tf_op jit(solution)/shard_map/ppermute | solution.py:31
  130.2 6.8 %collective-permute-start.51 = (bf16[32,1024]{1,0:T(8,128)(2,1)S(1)}, bf16[32,1024]{1,0:T(8,128)(2,1)S(1)}, u32[]{:S(2)}, u32[]{:S(2)}) collective-permute-start(bf16[32,1024]{1,0:T(8,128)(2,1)S(1)} %get-tuple-element.234), channel_id=1, source_target_pairs={{0,2},{2,0},{4,6},{6,4},{1,3},{3,1},{5,7},{7,5},{8,10},{10,8},{12,... | collective-permute-start | bytes 196616 | tf_op jit(solution)/shard_map/ppermute | solution.py:31
